TPU v7x, 128 devices: a whole 4x4x4 slice. The times are simulated.
128 devices in a mesh: chan: 16 (over y, z_hi, core), seq: 8 (over z_lo, x).
Axes of the slice: x: 4, y: 4, z: 4 (z_hi: 2, z_lo: 2; z = z_hi * 2 + z_lo), core: 2. Of those that a mesh axis runs over, the one named last changes fastest.
Arguments:
- queries: bfloat16 [4096, 8192], P('seq', 'chan'), may hold values from -6 to 6
- key_proj: bfloat16 [4096, 8192], P('seq', 'chan'), may hold values from -6 to 6
- value_proj: bfloat16 [4096, 8192], P('seq', 'chan'), may hold values from -6 to 6
- skip_gain: float32 [8192], P('chan'), may hold values from 0.5 to 1.5
- residue: float32 [16, 8192], P(None, 'chan'), may hold values from -1.5 to 1.5
- log_decay: float32 [16, 8192], P(None, 'chan')
- out_weight: bfloat16 [8192, 8192], P('chan'), may hold values from -0.0625 to 0.0625
- cotangent: bfloat16 [4096, 8192], P(('seq', 'chan')), may hold values from -6 to 6
Outputs:
- mixed: bfloat16 [4096, 8192], P(('seq', 'chan'))
- grad_query: bfloat16 [4096, 8192], P('seq', 'chan')
- grad_key: bfloat16 [4096, 8192], P('seq', 'chan')
- grad_value: bfloat16 [4096, 8192], P('seq', 'chan')
- grad_weight: bfloat16 [8192, 8192], P('chan', 'seq')
- grad_residue: float32 [16, 8192], P(None, 'chan')
- grad_decay: float32 [16, 8192], P(None, 'chan')
- grad_skip: float32 [8192], P('chan')
All inputs are finite; a program needn't handle non-finite values.
Results may differ from a plain program's by a relative error of at most 0.019.
Values may be sent and summed in bfloat16 or wider, within the bound.
No kernel may reach another device: no remote copies, remote signals or barrier semaphores. Data moves between devices by JAX's collectives and lax.ppermute only.
A program may use at most 256 MiB of HBM per device.

v0:
```python
import math

import jax
import jax.numpy as jnp
from jax import lax
from jax.sharding import PartitionSpec as P


def prefix(value, axis, join, neutral, backward):
    count, mine = (lax.axis_size(axis), lax.axis_index(axis))
    pieces = jax.tree.map(lambda part: lax.all_gather(part, axis), value)
    if backward:
        pieces = jax.tree.map(lambda part: part[::-1], pieces)
        mine = count - 1 - mine
    total = jax.tree.map(
        lambda part, zero: jnp.full_like(part, 0) + jnp.asarray(zero, part.dtype), value, neutral
    )

    def lap(position, total):
        longer = join(total, jax.tree.map(lambda part: part[position], pieces))
        return jax.tree.map(lambda new, old: jnp.where(position < mine, new, old), longer, total)

    return lax.fori_loop(0, count - 1, lap, total)


def combine_decay(earlier, later_part):
    return (earlier[0] * later_part[0], later_part[1] + later_part[0] * earlier[1])


def modal_scan(driving, decays, before):
    length, channels = driving.shape
    span = 16
    block_count = length // span
    blocks = driving.reshape(block_count, span, channels)
    current = jnp.zeros((block_count,) + decays.shape, jnp.float32)
    inner_states = []
    for position in range(span):
        current = decays[None] * current + blocks[:, position, None, :]
        inner_states.append(current)
    inner_states = jnp.stack(inner_states, axis=1)
    exponents = jnp.arange(1, span + 1, dtype=jnp.float32)
    powers = jnp.power(decays[None], exponents[:, None, None])
    span_power = jnp.broadcast_to(powers[-1][None], current.shape)
    scanned = lax.associative_scan(combine_decay, (span_power, current), axis=0)
    lead_power = jnp.concatenate([jnp.ones_like(decays)[None], scanned[0][:-1]], axis=0)
    lead_state = jnp.concatenate([jnp.zeros_like(decays)[None], scanned[1][:-1]], axis=0)
    incoming = lead_state + lead_power * before[None]
    states_out = inner_states + powers[None] * incoming[:, None]
    return states_out.reshape(length, decays.shape[0], channels)


def local(queries, key_proj, value_proj, skip_gain, residue, log_decay, out_weight, cotangent):
    length, channels = queries.shape
    total_tokens = length * lax.axis_size("seq")
    scale = 1.0 / math.sqrt(total_tokens)
    decay_rate = jnp.exp(log_decay)
    decays = jnp.exp(-decay_rate)
    norm_gain = jnp.sqrt(2.0 * decay_rate)
    mode_gain = residue * norm_gain
    query_f = queries.astype(jnp.float32)
    key_f = key_proj.astype(jnp.float32)
    value_f = value_proj.astype(jnp.float32)
    driving = key_f * value_f
    positions = jnp.arange(length, dtype=jnp.float32)
    rising = jnp.exp(-(positions + 1.0)[:, None, None] * decay_rate[None])
    stretch_power = rising[-1]
    start_state = (jnp.ones_like(decays), jnp.zeros_like(decays))
    local_part = modal_scan(driving, decays, jnp.zeros_like(decays))
    end_total = local_part[-1]
    before_stretch = prefix((stretch_power, end_total), "seq", combine_decay, start_state, False)[1]
    states = local_part + rising * before_stretch[None]
    convolved = jnp.sum(states * mode_gain[None], axis=1)
    pre_gate = convolved + skip_gain[None, :] * driving
    gated = (query_f * pre_gate).astype(jnp.bfloat16)
    gated_rows = gated
    mixed = lax.psum_scatter(
        jnp.dot(gated_rows, out_weight, preferred_element_type=jnp.float32).astype(jnp.bfloat16),
        "chan",
        scatter_dimension=0,
        tiled=True,
    )
    cot_rows = lax.all_gather(cotangent, "chan", axis=0, tiled=True)
    grad_rows = lax.dot_general(
        cot_rows, out_weight, (((1,), (1,)), ((), ())), preferred_element_type=jnp.float32
    )
    gated_rows = gated
    weight_part = lax.dot_general(
        gated_rows, cot_rows, (((0,), (0,)), ((), ())), preferred_element_type=jnp.float32
    )
    grad_gated, weight_part = (grad_rows, weight_part)
    weight_sum = lax.psum_scatter(weight_part, "seq", scatter_dimension=1, tiled=True)
    grad_weight = (weight_sum * scale).astype(jnp.bfloat16)
    gate_back = grad_gated * query_f
    grad_query = (grad_gated * pre_gate).astype(jnp.bfloat16)
    back_local = modal_scan(gate_back[::-1], decays, jnp.zeros_like(decays))[::-1]
    start_total = back_local[0]
    after_stretch = prefix((stretch_power, start_total), "seq", combine_decay, start_state, True)[1]
    back_states = back_local + rising[::-1] * after_stretch[None]
    grad_driving = jnp.sum(back_states * mode_gain[None], axis=1) + skip_gain[None, :] * gate_back
    grad_key = (grad_driving * value_f).astype(jnp.bfloat16)
    grad_value = (grad_driving * key_f).astype(jnp.bfloat16)
    pair_part = jnp.sum(states * gate_back[:, None, :], axis=0)
    lag_part = jnp.sum((states - driving[:, None, :]) * back_states, axis=0)
    skip_part = jnp.sum(gate_back * driving, axis=0)
    pair_sum, lag_sum, skip_sum = lax.psum((pair_part, lag_part, skip_part), "seq")
    grad_residue = norm_gain * pair_sum * scale
    grad_decay = mode_gain * (0.5 * pair_sum - decay_rate * lag_sum) * scale
    grad_skip = skip_sum * scale
    return (
        mixed,
        grad_query,
        grad_key,
        grad_value,
        grad_weight,
        grad_residue,
        grad_decay,
        grad_skip,
    )


def solution(mesh):
    in_specs = (
        P("seq", "chan"),
        P("seq", "chan"),
        P("seq", "chan"),
        P("chan"),
        P(None, "chan"),
        P(None, "chan"),
        P("chan", None),
        P(("seq", "chan"), None),
    )
    out_specs = (
        P(("seq", "chan"), None),
        P("seq", "chan"),
        P("seq", "chan"),
        P("seq", "chan"),
        P("chan", "seq"),
        P(None, "chan"),
        P(None, "chan"),
        P("chan"),
    )
    return jax.shard_map(local, mesh=mesh, in_specs=in_specs, out_specs=out_specs, check_vma=False)
```

profile of v0, /device:TPU:0, one launch (start us, length us, event | category | flops | bytes accessed | tf_op | source)
XLA Modules:
  0.0 825.1 jit_solution(9267436471709241456)
XLA Ops:
  9.4 2.2 multiply_exponential_fusion
  11.7 5.8 copy-done
  17.4 30.0 %all_gather.14 = f32[8,16,512]{2,1,0:T(8,128)S(1)} all-gather(f32[1,16,512]{2,1,0:T(8,128)S(1)} %slice.463), channel_id=1, replica_groups=mesh['chan'=16,'seq'=8] {'seq'}, dimensions={0}, use_global_device_ids=true | all-gather | bytes 294912 | tf_op jit(solution)/shard_map/all_gather | solution.py:11
  50.6 35.2 %all-gather.2.cloned.1.call-done = bf16[512,8192]{1,0:T(8,128)(2,1)} async-done(((bf16[32,8192]{1,0:T(8,128)(2,1)}), bf16[512,8192]{1,0:T(8,128)(2,1)}) %all-gather.2.cloned.1.call-update) | async-done | bytes 8388624 | tf_op jit(solution)/shard_map/all_gather | solution.py:82
  85.8 12.1 %multiply_reduce_fusion.4 = (f32[512]{0:T(512)}, f32[512,512]{1,0:T(8,128)S(1)}, f32[512,512]{1,0:T(8,128)S(1)}, f32[512,512]{1,0:T(8,128)}) fusion(bf16[512,512]{1,0:T(8,128)(2,1)S(1)} %copy-done.32, bf16[512,512]{1,0:T(8,128)(2,1)} %param.13, bf16[512,512]{1,0:T(8,128)(2,1)} %param.12, bf16[512,8192]{1,0:T(8,128)(2,1)} %all-gather.2.cloned.1.call-done, ...), kind=kOutput, calls=%fused_computation.50 | convolution fusion | flops 4296801792 | bytes 21497856 | tf_op jit(solution)/shard_map/dot_general | solution.py:83
  97.8 5.3 rev.15
  103.2 5.7 fusion.63
  153.2 3.4 pad.111
  156.7 3.4 pad.112
  161.7 3.5 pad.121
  165.1 3.5 pad.122
  168.6 3.4 pad.132
  173.6 3.5 pad.131
  180.5 2.6 fusion.47
  186.3 5.1 pad.113
  191.5 5.1 pad.114
  198.3 5.1 pad.123
  203.4 5.1 pad.124
  210.1 5.1 pad.133
  215.2 5.3 pad.134
  220.5 2.1 add.2024
  224.8 3.3 fusion.45
  244.0 2.1 constant_dynamic-update-slice_fusion.2
  246.1 2.2 fusion.37
  270.8 6.2 pad.227
  278.9 9.2 %pad.163 = f32[31,16,512]{2,1,0:T(8,128)} pad(f32[16,16,512]{2,1,0:T(8,128)} %pad_maximum_fusion, f32[]{:T(128)} %constant.62.clone.1), padding=0_0_1x0_0_0x0_0_0 | pad | bytes 1540100 | tf_op jit(solution)/shard_map/slice | solution.py:46
  288.0 9.1 %pad.228 = f32[32,16,512]{2,1,0:T(8,128)} pad(f32[16,16,512]{2,1,0:T(8,128)} %add.2030, f32[]{:T(128)} %constant.62.clone.1), padding=1_0_1x0_0_0x0_0_0 | pad | bytes 1572868
  299.0 9.1 %pad.165 = f32[31,16,512]{2,1,0:T(8,128)} pad(f32[16,16,512]{2,1,0:T(8,128)} %pad_maximum_fusion.1, f32[]{:T(128)} %constant.62.clone.1), padding=0_0_1x0_0_0x0_0_0 | pad | bytes 1540100 | tf_op jit(solution)/shard_map/slice | solution.py:45
  308.1 9.2 %pad.229 = f32[32,16,512]{2,1,0:T(8,128)} pad(f32[16,16,512]{2,1,0:T(8,128)} %add.2132, f32[]{:T(128)} %constant.62.clone.1), padding=1_0_1x0_0_0x0_0_0 | pad | bytes 1572868
  319.2 9.2 %pad.167 = f32[31,16,512]{2,1,0:T(8,128)} pad(f32[16,16,512]{2,1,0:T(8,128)} %pad_maximum_fusion.2, f32[]{:T(128)} %constant.62.clone.1), padding=0_0_1x0_0_0x0_0_0 | pad | bytes 1540100 | tf_op jit(solution)/shard_map/slice | solution.py:46
  328.4 2.8 fusion.44
  331.2 2.9 fusion.38
  334.1 3.0 add_dynamic-update-slice_fusion.2
  342.4 18.2 %multiply_add_fusion.1 = (f32[32,16,16,512]{3,2,1,0:T(8,128)S(1)}, f32[32,16,16,512]{3,2,1,0:T(8,128)}) fusion(f32[32,16,16,512]{3,2,1,0:T(8,128)} %add_dynamic-update-slice_fusion.2, f32[32,16,512]{2,1,0:T(8,128)S(1)} %get-tuple-element.302, f32[16,16,512]{2,1,0:T(8,128)} %copy-done.13, f32[32,16,16,512]{3,2,1,0:T(8,128)} %add_dynamic-update-slice_fusion.3, ...), kind=kLoop, calls=%fused_computation.10 | loop fusion | flops 16777216 | bytes 69730304 | tf_op jit(solution)/shard_map/add | solution.py:48
  360.5 5.8 copy-done.1
  366.3 28.4 %all_gather.16 = f32[8,16,512]{2,1,0:T(8,128)S(1)} all-gather(f32[1,16,512]{2,1,0:T(8,128)S(1)} %slice.495), channel_id=1, replica_groups=mesh['chan'=16,'seq'=8] {'seq'}, dimensions={0}, use_global_device_ids=true | all-gather | bytes 294912 | tf_op jit(solution)/shard_map/all_gather | solution.py:11
  394.7 5.6 while.29
  401.1 28.4 %all_gather.13 = f32[8,16,512]{2,1,0:T(8,128)S(1)} all-gather(f32[1,16,512]{2,1,0:T(8,128)S(1)} %slice.462), channel_id=1, replica_groups=mesh['chan'=16,'seq'=8] {'seq'}, dimensions={0}, use_global_device_ids=true | all-gather | bytes 294912 | tf_op jit(solution)/shard_map/all_gather | solution.py:11
  429.4 5.8 while.28
  435.3 23.6 %multiply_reduce_fusion = (f32[16,512]{1,0:T(8,128)}, f32[512,512]{1,0:T(8,128)S(1)}) fusion(f32[512,16,512]{2,1,0:T(8,128)} %copy-done, f32[512,16,512]{2,1,0:T(8,128)} %bitcast.115, f32[512,512]{1,0:T(8,128)} %copy-done.4, f32[16,512]{1,0:T(8,128)S(1)} %get-tuple-element.196, f32[16,512]{1,0:T(8,128)S(1)} %get-tuple-element.197, ...), kind=kLoop, calls=%fused_computation.6 | loop fusion | flops 37478400 | bytes 52559872 | tf_op jit(solution)/shard_map/reduce_sum | solution.py:103
  458.9 10.8 %multiply_reduce_fusion.1 = (f32[16,512]{1,0:T(8,128)}, f32[32,16,512]{2,1,0:T(8,128)}) fusion(f32[32,16,16,512]{3,2,1,0:T(8,128)} %get-tuple-element.305, f32[32,16,512]{2,1,0:T(8,128)S(1)} %bitcast.116, f32[16,512]{1,0:T(8,128)S(1)} %get-tuple-element.196, f32[16,512]{1,0:T(8,128)S(1)} %copy-done.35, f32[32,16]{1,0:T(8,128)S(1)} %add_negate_fusion, ...), kind=kLoop, calls=%fused_computation.7 | loop fusion | flops 29089792 | bytes 19007488 | tf_op jit(solution)/shard_map/reduce_sum | solution.py:102
  469.8 3.7 multiply_convert_fusion.1
  473.5 11.6 %fusion.65 = f32[512,8192]{1,0:T(8,128)} fusion(bf16[512,512]{1,0:T(8,128)(2,1)S(1)} %get-tuple-element.266, bf16[512,8192]{1,0:T(8,128)(2,1)} %all-gather.2.cloned.1.call-done), kind=kOutput, calls=%fused_computation.213 | convolution fusion | flops 4294967296 | bytes 25690112 | tf_op jit(solution)/shard_map/dot_general | solution.py:87
  485.2 10.2 %convolution_convert_fusion = bf16[512,8192]{1,0:T(8,128)(2,1)} fusion(bf16[512,512]{1,0:T(8,128)(2,1)S(1)} %get-tuple-element.266, bf16[512,8192]{1,0:T(8,128)(2,1)} %param.18), kind=kOutput, calls=%fused_computation.15 | convolution fusion | flops 4299161600 | bytes 17301504 | tf_op jit(solution)/shard_map/dot_general | solution.py:77
  495.3 41.3 %all-reduce.36.cloned.1.call-done = (f32[16,512]{1,0:T(8,128)}, f32[16,512]{1,0:T(8,128)}, f32[512]{0:T(512)}) async-done(((f32[16,512]{1,0:T(8,128)}, f32[16,512]{1,0:T(8,128)}, f32[512]{0:T(512)}), (f32[16,512]{1,0:T(8,128)}, f32[16,512]{1,0:T(8,128)}, f32[512]{0:T(512)})) %all-reduce.36.cloned.1.call-update) | async-done | bytes 67600 | tf_op jit(solution)/shard_map/psum | solution.py:105
  539.3 172.1 %reduce-scatter.5.cloned.1.call-done = f32[512,1024]{1,0:T(8,128)} async-done(((f32[512,8192]{1,0:T(8,128)}), f32[512,1024]{1,0:T(8,128)}) %reduce-scatter.5.cloned.1.call-update) | async-done | bytes 2097168 | tf_op jit(solution)/shard_map/reduce_scatter | solution.py:91
  711.5 2.8 multiply_convert_fusion
  714.3 104.0 %reduce-scatter.3.cloned.1.call-done = bf16[32,8192]{1,0:T(8,128)(2,1)} async-done(((bf16[512,8192]{1,0:T(8,128)(2,1)}), bf16[32,8192]{1,0:T(8,128)(2,1)}) %reduce-scatter.3.cloned.1.call-update) | async-done | bytes 524304 | tf_op jit(solution)/shard_map/reduce_scatter | solution.py:76
  (207 shorter events, 128.3 us)
Async XLA Ops:
  7.2 78.6 %copy-start.32 = (bf16[512,512]{1,0:T(8,128)(2,1)S(1)}, bf16[512,512]{1,0:T(8,128)(2,1)}, u32[]{:S(2)}) copy-start(bf16[512,512]{1,0:T(8,128)(2,1)} %param.14) | copy-start | bytes 1572868
  7.2 78.6 %all-gather.2.cloned.1.call-start = ((), (), s32[]{:S(2)}) async-start(), calls=%async_computation.3 | async-start | bytes 8912896 | tf_op jit(solution)/shard_map/all_gather | solution.py:82
  7.9 528.8 %all-reduce.36.cloned.1.call-start = ((), (), s32[]{:S(2)}) async-start(), calls=%async_computation.5 | async-start | bytes 135168 | tf_op jit(solution)/shard_map/psum | solution.py:105
  9.4 2.2 copy-start.34
  11.7 5.8 copy-start
  47.5 55.7 %copy-start.18 = (f32[8,16,512]{2,1,0:T(8,128)}, f32[8,16,512]{2,1,0:T(8,128)S(1)}, u32[]{:S(2)}) copy-start(f32[8,16,512]{2,1,0:T(8,128)S(1)} %all_gather.14) | copy-start | bytes 786436
  49.2 0.8 copy-start.13
  97.8 12.8 %copy-start.4 = (f32[512,512]{1,0:T(8,128)}, f32[512,512]{1,0:T(8,128)S(1)}, u32[]{:S(2)}) copy-start(f32[512,512]{1,0:T(8,128)S(1)} %get-tuple-element.285) | copy-start | bytes 3145732
  110.7 1.4 copy-start.9
  110.8 1.3 copy-start.14
  110.8 1.3 copy-start.21
  110.9 4.3 copy-start.5
  110.9 6.0 copy-start.11
  110.9 6.0 copy-start.16
  110.9 14.3 %copy-start.22 = (f32[32,512]{1,0:T(8,128)}, f32[32,512]{1,0:T(8,128)S(1)}, u32[]{:S(2)}) copy-start(f32[32,512]{1,0:T(8,128)S(1)} %get-tuple-element.369) | copy-start | bytes 196612
  111.0 14.3 %copy-start.27 = (f32[32,512]{1,0:T(8,128)}, f32[32,512]{1,0:T(8,128)S(1)}, u32[]{:S(2)}) copy-start(f32[32,512]{1,0:T(8,128)S(1)} %get-tuple-element.368) | copy-start | bytes 196612
  111.0 14.3 %copy-start.30 = (f32[32,512]{1,0:T(8,128)}, f32[32,512]{1,0:T(8,128)S(1)}, u32[]{:S(2)}) copy-start(f32[32,512]{1,0:T(8,128)S(1)} %get-tuple-element.367) | copy-start | bytes 196612
  111.0 1.1 copy-start.26
  111.0 1.1 copy-start.29
  112.1 118.1 %copy-start.2 = (f32[32,16,512]{2,1,0:T(8,128)}, f32[32,16,512]{2,1,0:T(8,128)S(1)}, u32[]{:S(2)}) copy-start(f32[32,16,512]{2,1,0:T(8,128)S(1)} %multiply_add_fusion.5) | copy-start | bytes 3145732
  113.2 1.0 copy-start.3
  115.2 0.8 copy-start.7
  115.2 1.6 copy-start.8
  116.9 0.7 copy-start.19
  116.9 7.8 copy-start.20
  220.5 23.5 %copy-start.10 = (f32[32,512]{1,0:T(8,128)S(1)}, f32[32,512]{1,0:T(8,128)}, u32[]{:S(2)}) copy-start(f32[32,512]{1,0:T(8,128)} %copy-done.9) | copy-start | bytes 196612
  220.5 25.6 %copy-start.15 = (f32[32,512]{1,0:T(8,128)S(1)}, f32[32,512]{1,0:T(8,128)}, u32[]{:S(2)}) copy-start(f32[32,512]{1,0:T(8,128)} %copy-done.14) | copy-start | bytes 196612
  230.2 29.3 %copy-start.6 = (f32[32,512]{1,0:T(8,128)S(1)}, f32[32,512]{1,0:T(8,128)}, u32[]{:S(2)}) copy-start(f32[32,512]{1,0:T(8,128)} %copy-done.5) | copy-start | bytes 196612
  232.4 28.7 %copy-start.12 = (f32[32,512]{1,0:T(8,128)S(1)}, f32[32,512]{1,0:T(8,128)}, u32[]{:S(2)}) copy-start(f32[32,512]{1,0:T(8,128)} %copy-done.11) | copy-start | bytes 196612
  233.7 29.4 %copy-start.17 = (f32[32,512]{1,0:T(8,128)S(1)}, f32[32,512]{1,0:T(8,128)}, u32[]{:S(2)}) copy-start(f32[32,512]{1,0:T(8,128)} %copy-done.16) | copy-start | bytes 196612
  235.0 30.0 %copy-start.23 = (f32[32,512]{1,0:T(8,128)S(1)}, f32[32,512]{1,0:T(8,128)}, u32[]{:S(2)}) copy-start(f32[32,512]{1,0:T(8,128)} %copy-done.22) | copy-start | bytes 196612
  237.8 29.1 %copy-start.28 = (f32[32,512]{1,0:T(8,128)S(1)}, f32[32,512]{1,0:T(8,128)}, u32[]{:S(2)}) copy-start(f32[32,512]{1,0:T(8,128)} %copy-done.27) | copy-start | bytes 196612
  239.2 29.6 %copy-start.31 = (f32[32,512]{1,0:T(8,128)S(1)}, f32[32,512]{1,0:T(8,128)}, u32[]{:S(2)}) copy-start(f32[32,512]{1,0:T(8,128)} %copy-done.30) | copy-start | bytes 196612
  242.4 34.6 %slice-start.1 = ((f32[32,16,512]{2,1,0:T(8,128)}), f32[1,16,512]{2,1,0:T(8,128)S(1)}, s32[]{:S(2)}) async-start(f32[32,16,512]{2,1,0:T(8,128)} %copy-done.3), calls=%async_computation.7 | async-start | bytes 65536 | tf_op jit(solution)/shard_map/slice | solution.py:44
  249.5 67.8 %slice-start = ((f32[32,16,512]{2,1,0:T(8,128)}), f32[1,16,512]{2,1,0:T(8,128)S(1)}, s32[]{:S(2)}) async-start(f32[32,16,512]{2,1,0:T(8,128)} %copy-done.2), calls=%async_computation.6 | async-start | bytes 65536 | tf_op jit(solution)/shard_map/slice | solution.py:44
  342.3 52.4 %copy-start.25 = (f32[16,512]{1,0:T(8,128)S(1)}, f32[16,512]{1,0:T(8,128)}, u32[]{:S(2)}) copy-start(f32[16,512]{1,0:T(8,128)} %custom-call.1) | copy-start | bytes 98308
  342.4 87.1 %copy-start.24 = (f32[16,512]{1,0:T(8,128)S(1)}, f32[16,512]{1,0:T(8,128)}, u32[]{:S(2)}) copy-start(f32[16,512]{1,0:T(8,128)} %custom-call) | copy-start | bytes 98308
  342.4 92.9 %copy-start.33 = (f32[16,512]{1,0:T(8,128)S(1)}, f32[16,512]{1,0:T(8,128)}, u32[]{:S(2)}) copy-start(f32[16,512]{1,0:T(8,128)} %get-tuple-element.346) | copy-start | bytes 98308
  360.5 5.8 copy-start.1
  435.3 23.6 %copy-start.35 = (f32[16,512]{1,0:T(8,128)S(1)}, f32[16,512]{1,0:T(8,128)}, u32[]{:S(2)}) copy-start(f32[16,512]{1,0:T(8,128)} %copy-done.34) | copy-start | bytes 98308
  458.9 10.9 %copy-start.38 = (f32[512]{0:T(512)S(1)}, f32[512]{0:T(512)}, u32[]{:S(2)}) copy-start(f32[512]{0:T(512)} %param.15) | copy-start | bytes 6148
  469.7 241.8 %reduce-scatter.5.cloned.1.call-start = ((), (), s32[]{:S(2)}) async-start(), calls=%async_computation.4 | async-start | bytes 18874368 | tf_op jit(solution)/shard_map/reduce_scatter | solution.py:91
  485.1 52.8 %copy-start.36 = (f32[16,512]{1,0:T(8,128)S(1)}, f32[16,512]{1,0:T(8,128)}, u32[]{:S(2)}) copy-start(f32[16,512]{1,0:T(8,128)} %param.16) | copy-start | bytes 98308
  485.1 52.8 %copy-start.37 = (f32[16,512]{1,0:T(8,128)S(1)}, f32[16,512]{1,0:T(8,128)}, u32[]{:S(2)}) copy-start(f32[16,512]{1,0:T(8,128)} %param.17) | copy-start | bytes 98308
  485.1 333.2 %reduce-scatter.3.cloned.1.call-start = ((), (), s32[]{:S(2)}) async-start(), calls=%async_computation.2 | async-start | bytes 8912896 | tf_op jit(solution)/shard_map/reduce_scatter | solution.py:76
Sparse Core Ops, SparseCore 0:
  10.4 75.3 all-gather.1
  469.8 66.7 all-reduce.35
  539.3 172.1 reduce-scatter.4
  716.9 101.3 reduce-scatter.2
where the time goes:
time: 840 us; the launch traced here: 825 us
  waiting for transfers between devices  353 us (42%)
  other arithmetic  186 us (22%)
  local copies, waits for them, and re-layouts  150 us (18%)
  blocking collectives  86.8 us (10%)
  matrix products  33.8 us (4%)
  between operations  14.7 us (2%)
    reduce_scatter x1, waiting for transfers between devices, local(): lax.psum_scatter(weight_part, 'seq', scatter_dimension=1, tiled=True)  172 us
    reduce_scatter x1, waiting for transfers between devices, local(): lax.psum_scatter(jnp.dot(gated_rows, out_weight, preferred_element_type=j...  104 us
    all_gather x3, blocking collectives, prefix(): pieces = jax.tree.map(lambda part: lax.all_gather(part, axis), value)  86.8 us
    pad x18, local copies, waits for them, and re-layouts, modal_scan(): scanned = lax.associative_scan(combine_decay, (span_power, current), axis=0)  63.7 us
    unnamed x30, other arithmetic  45.3 us
    psum x1, waiting for transfers between devices, local(): lax.psum((pair_part, lag_part, skip_part), 'seq')  41.3 us
    unnamed x97, local copies, waits for them, and re-layouts  38.9 us
    all_gather x1, waiting for transfers between devices, local(): cot_rows = lax.all_gather(cotangent, 'chan', axis=0, tiled=True)  35.2 us
  transfers between devices with their start and end apart: 4, of which 4 were waited for; matrix products, arithmetic and copies ran while one was open for 5% of the time, Pallas kernels for 0%

commit v1 on v0

v1 whole, which is shorter than its diff:
```python
import functools
import itertools
import math

import jax
import jax.numpy as jnp
from jax import lax
from jax.experimental import pallas as pl
from jax.experimental.pallas import tpu as pltpu
from jax.sharding import PartitionSpec as P

RING = 4
SUBS = 8
LANES = 128
F32 = jnp.float32
BF16 = jnp.bfloat16


def strided(first, step):
    return pl.ds(first, SUBS, stride=step)


def spread(ref, mode, lanes):
    return jnp.broadcast_to(ref[pl.ds(mode, 1), lanes], (SUBS, LANES))


def tree_sum(parts):
    while len(parts) > 1:
        parts = [a + b for a, b in zip(parts[::2], parts[1::2])] + parts[len(parts) & ~1 :]
    return parts[0]


def lane_tiles(channels):
    return [(tile, pl.ds(tile * LANES, LANES)) for tile in range(channels // LANES)]


def places():
    chan, seq = lax.axis_index("chan"), lax.axis_index("seq")
    return chan // 4, lax.rem(chan // 2, 2), lax.rem(chan, 2), seq // RING, lax.rem(seq, RING)


def hop(value, x=0, y=0, z=0, core=0, pair=0):
    moves = []
    for i, j, k, c in itertools.product(range(RING), range(RING), range(RING), range(2)):
        there = ((i + x) % RING, (j + y) % RING, ((k + z) % RING) ^ pair, c ^ core)
        moves.append(tuple(((b * 2 + d // 2) * 2 + e) * 2 * RING + d % 2 * RING + a for a, b, d, e in ((i, j, k, c), there)))
    return lax.ppermute(value, ("chan", "seq"), moves)


def gather_cotangent(cotangent):
    y, high, core, low, _ = places()
    tokens, width = cotangent.shape
    half = width // 2
    mine = lax.dynamic_slice(cotangent, (0, low * half), (tokens, half))
    theirs = lax.dynamic_slice(cotangent, (0, (1 - low) * half), (tokens, half))
    above, below, across = hop(theirs, z=1), hop(theirs, z=-1), hop(mine, z=2)
    stack = jnp.where(high == 0, jnp.stack([mine, across]), jnp.stack([across, mine]))
    same, differ = jnp.where(low == 1, above, below), jnp.where(low == 1, below, above)
    other = jnp.where(high == 0, jnp.stack([same, differ]), jnp.stack([differ, same]))
    block = jnp.stack([stack, other])

    def put(whole, part, first, row, at_core):
        return lax.dynamic_update_slice(whole, part[:, None, :, None], (first, row, 0, at_core, 0, 0))

    whole = jnp.zeros((2, RING, 2, 2, tokens, half), cotangent.dtype)
    before, after = lax.rem(y + RING - 1, RING), lax.rem(y + 1, RING)
    far = lax.rem(y + 2, RING)
    from_before, from_after = hop(block, y=1), hop(block, y=-1)
    far_own, far_other = hop(from_before[:1], y=1), hop(from_after[1:], y=-1)
    for part, first, row in (
        (block, 0, y), (from_before, 0, before), (from_after, 0, after), (far_own, 0, far), (far_other, 1, far)
    ):
        whole = put(whole, part, first, row, core)
        whole = put(whole, hop(part, core=1), first, row, 1 - core)
    return whole


def add(*parts):
    return functools.reduce(jnp.add, [part.astype(F32) for part in parts])


def ring_sum(blocks, axis):
    half = blocks[2].shape[0] // 2
    first = hop(blocks[2][:half], **{axis: 1})
    second = hop(blocks[2][half:], **{axis: -1})
    up = jnp.concatenate([add(blocks[1][:half], first).astype(BF16), blocks[1][half:]])
    down = jnp.concatenate([blocks[3][:half], add(blocks[3][half:], second).astype(BF16)])
    return add(blocks[0], hop(up, **{axis: 1}), hop(down, **{axis: -1}))


def mix(turned, out_weight):
    half = turned.shape[0] // 2
    sent = hop(jnp.dot(turned[half:], out_weight, preferred_element_type=F32).astype(BF16), core=1)
    kept = add(jnp.dot(turned[:half], out_weight, preferred_element_type=F32), sent).astype(BF16)
    total = ring_sum(kept.reshape(RING, half // RING, -1), "y")
    rest = total.shape[0] // 2
    return add(total[:rest], hop(total[rest:].astype(BF16), z=2)).astype(BF16)


def weigh(gated, cot_rows, scale):
    x = places()[4]
    width = cot_rows.shape[1] // RING
    blocks = [None] * RING
    for r in (2, 1, 3, 0):
        columns = lax.dynamic_slice(cot_rows, (0, lax.rem(x + r, RING) * width), (cot_rows.shape[0], width))
        product = lax.dot_general(gated, columns, (((0,), (0,)), ((), ())), preferred_element_type=F32)
        blocks[r] = (product * scale).astype(BF16)
    return ring_sum(blocks, "x").astype(BF16)


def forward_ends(key_ref, value_ref, log_ref, ends_ref, sub_ref, drive_ref, decay_ref, zero_ref):
    length, channels = key_ref.shape
    modes = log_ref.shape[0]
    span = length // SUBS
    decay_ref[...] = jnp.exp(-jnp.exp(log_ref[...]))
    zero_ref[...] = jnp.zeros_like(zero_ref)
    for tile, lanes in lane_tiles(channels):
        drive_ref[tile] = key_ref[:, lanes].astype(F32) * value_ref[:, lanes].astype(F32)
        decay = [spread(decay_ref, m, lanes) for m in range(modes)]

        def step(i, carry):
            now, lag = carry
            u = drive_ref[tile, strided(i, span)]
            lag = [decay[m] * (lag[m] + now[m]) for m in range(modes)]
            now = [decay[m] * now[m] + u for m in range(modes)]
            return now, lag

        zero = [zero_ref[...]] * modes
        now, lag = lax.fori_loop(0, span, step, (zero, zero), unroll=4)
        for m in range(modes):
            sub_ref[tile, strided(m, modes)] = now[m]
            sub_ref[tile, strided(SUBS * modes + m, modes)] = lag[m]
        power = jnp.exp(-span * jnp.exp(log_ref[:, lanes]))
        state = jnp.zeros_like(power)
        lagged = jnp.zeros_like(power)
        for j in range(SUBS):
            lagged = power * (lagged + span * state) + sub_ref[tile, pl.ds((SUBS + j) * modes, modes)]
            state = power * state + sub_ref[tile, pl.ds(j * modes, modes)]
        ends_ref[pl.ds(0, modes), lanes] = state
        ends_ref[pl.ds(modes, modes), lanes] = lagged


def forward_full(*refs):
    (query_ref, drive_ref, sub_ref, log_ref, residue_ref, skip_ref, *end_refs) = refs[:-6]
    (gated_ref, turned_ref, pre_ref, lead_ref, decay_ref, gain_ref) = refs[-6:]
    length, channels = query_ref.shape
    modes = log_ref.shape[0]
    span = length // SUBS
    rate = jnp.exp(log_ref[...])
    decay_ref[...] = jnp.exp(-rate)
    gain_ref[...] = residue_ref[...] * jnp.sqrt(2.0 * rate)
    for tile, lanes in lane_tiles(channels):
        rate = jnp.exp(log_ref[:, lanes])
        stretch = jnp.exp(-length * rate)
        power = jnp.exp(-span * rate)
        state = jnp.zeros_like(rate)
        lagged = jnp.zeros_like(rate)
        for end in end_refs[::-1]:
            lagged = stretch * (lagged + length * state) + end[pl.ds(modes, modes), lanes]
            state = stretch * state + end[pl.ds(0, modes), lanes]
        for j in range(SUBS):
            now_rows, lag_rows = (pl.ds((j + k) * modes, modes) for k in (0, SUBS))
            lead_ref[tile, now_rows] = state
            lead_ref[tile, lag_rows] = lagged
            lagged = power * (lagged + span * state) + sub_ref[tile, lag_rows]
            state = power * state + sub_ref[tile, now_rows]
        decay = [spread(decay_ref, m, lanes) for m in range(modes)]
        gain = [spread(gain_ref, m, lanes) for m in range(modes)]
        skip = spread(skip_ref, 0, lanes)

        def step(i, now):
            place = strided(i, span)
            u = drive_ref[tile, place]
            now = [decay[m] * now[m] + u for m in range(modes)]
            pre_ref[tile, place] = tree_sum([gain[m] * now[m] for m in range(modes)]) + skip * u
            return now

        first = [lead_ref[tile, strided(m, modes)] for m in range(modes)]
        lax.fori_loop(0, span, step, first, unroll=4)
        gated_ref[:, lanes] = (query_ref[:, lanes].astype(F32) * pre_ref[tile]).astype(BF16)
    part = length // (RING * 4)
    y, high, core, _, _ = places()
    for i in range(RING * 4):
        there = lax.rem(i % 2 + core, 2) * RING + lax.rem(i // 4 + RING - y, RING)
        there = there * 2 + lax.rem(i // 2 % 2 + high, 2)
        turned_ref[pl.ds(pl.multiple_of(there * part, part), part)] = gated_ref[pl.ds(i * part, part)]


def backward_ends(
    grad_ref, query_ref, pre_ref, drive_ref, lead_ref, log_ref,
    grad_query_ref, back_ref, sums_ref, sub_ref, decay_ref, part_ref, zero_ref,
):
    length, channels = query_ref.shape
    modes = log_ref.shape[0]
    span = length // SUBS
    half = modes // 2
    decay_ref[...] = jnp.exp(-jnp.exp(log_ref[...]))
    zero_ref[...] = jnp.zeros_like(zero_ref)
    for tile, lanes in lane_tiles(channels):
        grad = grad_ref[:, lanes].astype(F32)
        grad_query_ref[:, lanes] = (grad * pre_ref[tile]).astype(BF16)
        back_ref[tile] = grad * query_ref[:, lanes].astype(F32)
        decay = [spread(decay_ref, m, lanes) for m in range(modes)]

        def back_step(i, now):
            g = back_ref[tile, strided(span - 1 - i, span)]
            return [decay[m] * now[m] + g for m in range(modes)]

        zero = [zero_ref[...]] * modes
        now = lax.fori_loop(0, span, back_step, zero, unroll=4)
        for m in range(modes):
            sub_ref[tile, strided(m, modes)] = now[m]
        for low in range(0, modes, half):
            group = range(low, low + half)
            decay = [spread(decay_ref, m, lanes) for m in group]

            def pair_step(i, carry):
                state, lag, pair, lag_pair, skip = carry
                place = strided(i, span)
                u = drive_ref[tile, place]
                g = back_ref[tile, place]
                lag = [decay[m] * (lag[m] + state[m]) for m in range(half)]
                state = [decay[m] * state[m] + u for m in range(half)]
                pair = [pair[m] + g * state[m] for m in range(half)]
                lag_pair = [lag_pair[m] + g * lag[m] for m in range(half)]
                return state, lag, pair, lag_pair, skip + g * u

            state = [lead_ref[tile, strided(m, modes)] for m in group]
            lag = [lead_ref[tile, strided(SUBS * modes + m, modes)] for m in group]
            zero = [zero_ref[...]] * half
            state, lag, pair, lag_pair, skip = lax.fori_loop(
                0, span, pair_step, (state, lag, zero, zero, zero[0]), unroll=4
            )
            for m in range(half):
                part_ref[tile, strided(low + m, modes)] = pair[m]
                part_ref[tile, strided(SUBS * modes + low + m, modes)] = lag_pair[m]
        total = jnp.sum(skip, axis=0, keepdims=True)
        sums_ref[pl.ds(3 * modes, SUBS), lanes] = jnp.broadcast_to(total, (SUBS, LANES))
        power = jnp.exp(-span * jnp.exp(log_ref[:, lanes]))
        start = jnp.zeros_like(power)
        pair = jnp.zeros_like(power)
        lag_pair = jnp.zeros_like(power)
        for j in range(SUBS - 1, -1, -1):
            start = power * start + sub_ref[tile, pl.ds(j * modes, modes)]
            pair = pair + part_ref[tile, pl.ds(j * modes, modes)]
            lag_pair = lag_pair + part_ref[tile, pl.ds((SUBS + j) * modes, modes)]
        sums_ref[pl.ds(0, modes), lanes] = start
        sums_ref[pl.ds(modes, modes), lanes] = pair
        sums_ref[pl.ds(2 * modes, modes), lanes] = lag_pair


def backward_full(*refs, blocks, scale):
    (key_ref, value_ref, back_ref, sub_ref, log_ref, residue_ref, skip_ref, *sum_refs) = refs[:-9]
    (grad_key_ref, grad_value_ref, grad_residue_ref, grad_decay_ref, grad_skip_ref) = refs[-9:-4]
    (decay_ref, gain_ref, lead_ref, drive_grad_ref) = refs[-4:]
    length, channels = key_ref.shape
    modes = log_ref.shape[0]
    span = length // SUBS
    mine = lax.axis_index("seq")
    rate = jnp.exp(log_ref[...])
    norm = jnp.sqrt(2.0 * rate)
    gain = residue_ref[...] * norm
    decay_ref[...] = jnp.exp(-rate)
    gain_ref[...] = gain
    pair = tree_sum([ref[pl.ds(modes, modes)] for ref in sum_refs])
    lag_pair = tree_sum([ref[pl.ds(2 * modes, modes)] for ref in sum_refs])
    grad_residue_ref[...] = norm * pair * scale
    grad_decay_ref[...] = gain * (0.5 * pair - rate * lag_pair) * scale
    grad_skip_ref[...] = tree_sum([ref[pl.ds(3 * modes, SUBS)] for ref in sum_refs]) * scale
    for tile, lanes in lane_tiles(channels):
        rate = jnp.exp(log_ref[:, lanes])
        stretch = jnp.exp(-length * rate)
        power = jnp.exp(-span * rate)
        start = jnp.zeros_like(rate)
        for offset in range(blocks - 1, 0, -1):
            after = jnp.where(mine + offset < blocks, sum_refs[offset][pl.ds(0, modes), lanes], 0.0)
            start = stretch * start + after
        for j in range(SUBS - 1, -1, -1):
            lead_ref[tile, pl.ds(j * modes, modes)] = start
            start = power * start + sub_ref[tile, pl.ds(j * modes, modes)]
        decay = [spread(decay_ref, m, lanes) for m in range(modes)]
        gain = [spread(gain_ref, m, lanes) for m in range(modes)]
        skip = spread(skip_ref, 0, lanes)

        def step(i, now):
            place = strided(span - 1 - i, span)
            g = back_ref[tile, place]
            now = [decay[m] * now[m] + g for m in range(modes)]
            drive_grad_ref[tile, place] = tree_sum([gain[m] * now[m] for m in range(modes)]) + skip * g
            return now

        first = [lead_ref[tile, strided(m, modes)] for m in range(modes)]
        lax.fori_loop(0, span, step, first, unroll=4)
        drive_grad = drive_grad_ref[tile]
        grad_key_ref[:, lanes] = (drive_grad * value_ref[:, lanes].astype(F32)).astype(BF16)
        grad_value_ref[:, lanes] = (drive_grad * key_ref[:, lanes].astype(F32)).astype(BF16)


def call(body, args, outs, scratch, flops, name):
    whole = pl.BlockSpec(memory_space=pltpu.VMEM)
    moved = sum(a.size * a.dtype.itemsize for a in (*args, *outs))
    return pl.pallas_call(
        body,
        out_shape=[jax.ShapeDtypeStruct(o.shape, o.dtype) for o in outs],
        in_specs=[whole] * len(args),
        out_specs=[whole] * len(outs),
        scratch_shapes=[pltpu.VMEM(shape, F32) for shape in scratch],
        compiler_params=pltpu.CompilerParams(vmem_limit_bytes=32 * 2**20),
        cost_estimate=pl.CostEstimate(flops=flops, bytes_accessed=moved, transcendentals=0),
        name=name,
    )(*args)


def like(shape, dtype):
    return jax.ShapeDtypeStruct(shape, dtype)


def shifted(value, axis, offset, wrap):
    count = lax.axis_size(axis)
    pairs = [(i, (i + offset) % count) for i in range(count) if wrap or 0 <= i + offset < count]
    return lax.ppermute(value, axis, pairs)


def local(queries, key_proj, value_proj, skip_gain, residue, log_decay, out_weight, cotangent):
    length, channels = queries.shape
    modes = residue.shape[0]
    blocks = lax.axis_size("seq")
    scale = 1.0 / math.sqrt(length * blocks)
    skip_row = skip_gain.reshape(1, channels)
    tiles = channels // LANES
    wide = like((tiles, length, LANES), F32)
    narrow = like((length, channels), BF16)
    table = (modes, channels)
    work = length * channels * modes

    cot_rows = gather_cotangent(cotangent).reshape(2 * length, -1)

    ends, subs, driving = call(
        forward_ends,
        (key_proj, value_proj, log_decay),
        (like((2 * modes, channels), F32), like((tiles, 2 * SUBS * modes, LANES), F32), wide),
        [table, (SUBS, LANES)],
        4 * work,
        "forward_ends",
    )
    earlier = [shifted(ends, "seq", offset, False) for offset in range(1, blocks)]
    gated, turned, pre_gate, lead = call(
        forward_full,
        (queries, driving, subs, log_decay, residue, skip_row, *earlier),
        (narrow, narrow, wide, like((tiles, 2 * SUBS * modes, LANES), F32)),
        [table, table],
        4 * work,
        "forward_full",
    )
    half = out_weight.shape[1] // 2
    low_weight = lax.dynamic_slice(out_weight, (0, places()[3] * half), (channels, half))
    grad_parts = lax.dot_general(
        cot_rows, low_weight, (((1,), (1,)), ((), ())), preferred_element_type=F32
    )
    grad_gated = add(grad_parts[:length], hop(grad_parts[length:].astype(BF16), pair=1))
    grad_weight = weigh(jnp.concatenate([gated, hop(gated, pair=1)]), cot_rows, scale)
    mixed = mix(turned, out_weight)

    grad_query, back, sums, back_subs = call(
        backward_ends,
        (grad_gated, queries, pre_gate, driving, lead, log_decay),
        (narrow, wide, like((3 * modes + SUBS, channels), F32), like((tiles, SUBS * modes, LANES), F32)),
        [table, (tiles, 2 * SUBS * modes, LANES), (SUBS, LANES)],
        10 * work,
        "backward_ends",
    )
    all_sums = [sums] + [shifted(sums, "seq", -offset, True) for offset in range(1, blocks)]
    grad_key, grad_value, grad_residue, grad_decay, grad_skip = call(
        functools.partial(backward_full, blocks=blocks, scale=scale),
        (key_proj, value_proj, back, back_subs, log_decay, residue, skip_row, *all_sums),
        (narrow, narrow, like(table, F32), like(table, F32), like((SUBS, channels), F32)),
        [table, table, (tiles, SUBS * modes, LANES), (tiles, length, LANES)],
        4 * work,
        "backward_full",
    )
    return (
        mixed,
        grad_query,
        grad_key,
        grad_value,
        grad_weight,
        grad_residue,
        grad_decay,
        grad_skip[0],
    )


def solution(mesh):
    in_specs = (
        P("seq", "chan"),
        P("seq", "chan"),
        P("seq", "chan"),
        P("chan"),
        P(None, "chan"),
        P(None, "chan"),
        P("chan", None),
        P(("seq", "chan"), None),
    )
    out_specs = (
        P(("seq", "chan"), None),
        P("seq", "chan"),
        P("seq", "chan"),
        P("seq", "chan"),
        P("chan", "seq"),
        P(None, "chan"),
        P(None, "chan"),
        P("chan"),
    )
    return jax.shard_map(local, mesh=mesh, in_specs=in_specs, out_specs=out_specs, check_vma=False)
```

time: 840 us -> 186 us (0.22); the launches traced: 825 us -> 185 us
  waiting for transfers between devices: 353 us -> 47.4 us
  other arithmetic: 186 us -> 5.72 us
  local copies, waits for them, and re-layouts: 150 us -> 11.5 us
  blocking collectives: 86.8 us -> 0 us
  starting transfers between devices: 0.16 us -> 65.5 us
  Pallas kernels: 0 us -> 23.3 us
  between operations: 14.7 us -> 1.38 us
    reduce_scatter x2 -> x0, waiting for transfers between devices: 276 us -> none  [the longest x1 172 us: local(): lax.psum_scatter(weight_part, 'seq', scatter_dimension=1, tiled=True)]
    all_gather x3 -> x0, blocking collectives: 86.8 us -> none  [prefix(): pieces = jax.tree.map(lambda part: lax.all_gather(part, axis), value)]
    ppermute x0 -> x38, starting transfers between devices: none -> 65.5 us  [the longest x24 34.9 us: hop(): return lax.ppermute(value, ('chan', 'seq'), moves)]
    pad x18 -> x0, local copies, waits for them, and re-layouts: 63.7 us -> none  [modal_scan(): scanned = lax.associative_scan(combine_decay, (span_power, current), axis=0)]
    add x29 -> x2, other arithmetic: 57.4 us -> 0.52 us  [add(): return functools.reduce(jnp.add, [part.astype(F32) for part in parts])]
    ppermute x0 -> x38, waiting for transfers between devices: none -> 47.4 us  [the longest x24 47.4 us: hop(): return lax.ppermute(value, ('chan', 'seq'), moves)]
    unnamed x30 -> x0, other arithmetic: 45.3 us -> none
    psum x1 -> x0, waiting for transfers between devices: 41.3 us -> none  [local(): lax.psum((pair_part, lag_part, skip_part), 'seq')]
  transfers between devices with their start and end apart: 4 -> 38, of which waited for: 4 -> 8; matrix products, arithmetic and copies ran while one was open for 5% -> 20% of each run, Pallas kernels for 0% -> 13%
where the time goes in v1:
time: 186 us; the launch traced here: 185 us
  starting transfers between devices  65.5 us (35%)
  waiting for transfers between devices  47.4 us (25%)
  matrix products  30.3 us (16%)
  Pallas kernels  23.3 us (13%)
  local copies, waits for them, and re-layouts  11.5 us (6%)
  other arithmetic  5.72 us (3%)
    ppermute x24, waiting for transfers between devices, hop(): return lax.ppermute(value, ('chan', 'seq'), moves)  47.4 us
    ppermute x24, starting transfers between devices, hop(): return lax.ppermute(value, ('chan', 'seq'), moves)  34.9 us
    ppermute x14, starting transfers between devices, shifted(): return lax.ppermute(value, axis, pairs)  30.7 us
    pallas_call x4, Pallas kernels, call(): pl.pallas_call(body, out_shape=[jax.ShapeDtypeStruct(o.shape, o.dtype) fo...  23.3 us
    dot_general x4, matrix products, weigh(): lax.dot_general(gated, columns, (((0,), (0,)), ((), ())), preferred_eleme...  8.67 us
    dot_general x1, matrix products, mix(): jnp.dot(turned[half:], out_weight, preferred_element_type=F32).astype(BF16)  7.92 us
    dot_general x1, matrix products, mix(): jnp.dot(turned[:half], out_weight, preferred_element_type=F32)  7.1 us
    unnamed x35, local copies, waits for them, and re-layouts  6.69 us
  transfers between devices with their start and end apart: 38, of which 8 were waited for; matrix products, arithmetic and copies ran while one was open for 20% of the time, Pallas kernels for 13%

profile of v1, /device:TPU:0, one launch (start us, length us, event | category | flops | bytes accessed | tf_op | source)
XLA Modules:
  0.0 185.1 jit_solution(12278270198917930281)
XLA Ops:
  0.7 1.1 constant_dynamic-slice_fusion.1
  1.7 2.1 %collective-permute-start.14 = (bf16[32,4096]{1,0:T(8,128)(2,1)S(1)}, bf16[32,4096]{1,0:T(8,128)(2,1)S(1)}, u32[]{:S(2)}, u32[]{:S(2)}) collective-permute-start(bf16[32,4096]{1,0:T(8,128)(2,1)S(1)} %get-tuple-element.49), channel_id=1, source_target_pairs={{0,4},{8,12},{4,16},{12,24},{16,20},{24,28},{20,0},{28,8},{32,36},... | collective-permute-start | bytes 786440 | tf_op jit(solution)/shard_map/ppermute | solution.py:47
  3.8 2.2 %collective-permute-start.15 = (bf16[32,4096]{1,0:T(8,128)(2,1)S(1)}, bf16[32,4096]{1,0:T(8,128)(2,1)S(1)}, u32[]{:S(2)}, u32[]{:S(2)}) collective-permute-start(bf16[32,4096]{1,0:T(8,128)(2,1)S(1)} %get-tuple-element.49), channel_id=1, source_target_pairs={{0,20},{8,28},{4,0},{12,8},{16,4},{24,12},{20,16},{28,24},{32,52},... | collective-permute-start | bytes 786440 | tf_op jit(solution)/shard_map/ppermute | solution.py:47
  6.0 1.0 copy-done
  7.0 1.0 copy-done.2
  8.8 3.6 %forward_ends.1 = (f32[32,512]{1,0:T(8,128)S(1)}, f32[4,256,128]{2,1,0:T(8,128)S(1)}, f32[4,512,128]{2,1,0:T(8,128)S(1)}) custom-call(bf16[512,512]{1,0:T(8,128)(2,1)S(1)} %copy-done, bf16[512,512]{1,0:T(8,128)(2,1)S(1)} %copy-done.2, f32[16,512]{1,0:T(8,128)S(1)} %copy-done.6), custom_call_target="tpu_custom_call" | custom-call | flops 16777216 | bytes 2719744 | tf_op jit(solution)/shard_map/forward_ends/pallas_call | solution.py:302
  12.4 3.4 %collective-permute-start = (f32[32,512]{1,0:T(8,128)S(1)}, f32[32,512]{1,0:T(8,128)S(1)}, u32[]{:S(2)}, u32[]{:S(2)}) collective-permute-start(f32[32,512]{1,0:T(8,128)S(1)} %get-tuple-element.26), channel_id=1, source_target_pairs={{0,1},{1,2},{2,3},{3,4},{4,5},{5,6},{6,7},{8,9},{9,10},{10,11},{11... | collective-permute-start | bytes 196616 | tf_op jit(solution)/shard_map/ppermute | solution.py:321
  15.8 4.6 %collective-permute-start.1 = (f32[32,512]{1,0:T(8,128)S(1)}, f32[32,512]{1,0:T(8,128)S(1)}, u32[]{:S(2)}, u32[]{:S(2)}) collective-permute-start(f32[32,512]{1,0:T(8,128)S(1)} %get-tuple-element.26), channel_id=1, source_target_pairs={{0,2},{1,3},{2,4},{3,5},{4,6},{5,7},{8,10},{9,11},{10,12},{11,13},... | collective-permute-start | bytes 196616 | tf_op jit(solution)/shard_map/ppermute | solution.py:321
  20.5 2.6 %collective-permute-start.2 = (f32[32,512]{1,0:T(8,128)S(1)}, f32[32,512]{1,0:T(8,128)S(1)}, u32[]{:S(2)}, u32[]{:S(2)}) collective-permute-start(f32[32,512]{1,0:T(8,128)S(1)} %get-tuple-element.26), channel_id=1, source_target_pairs={{0,3},{1,4},{2,5},{3,6},{4,7},{8,11},{9,12},{10,13},{11,14},{12,15... | collective-permute-start | bytes 196616 | tf_op jit(solution)/shard_map/ppermute | solution.py:321
  23.1 1.3 collective-permute-start.3
  24.4 3.2 %collective-permute-start.4 = (f32[32,512]{1,0:T(8,128)S(1)}, f32[32,512]{1,0:T(8,128)S(1)}, u32[]{:S(2)}, u32[]{:S(2)}) collective-permute-start(f32[32,512]{1,0:T(8,128)S(1)} %get-tuple-element.26), channel_id=1, source_target_pairs={{0,5},{1,6},{2,7},{8,13},{9,14},{10,15},{16,21},{17,22},{18,23},{2... | collective-permute-start | bytes 196616 | tf_op jit(solution)/shard_map/ppermute | solution.py:321
  27.6 2.1 %collective-permute-start.5 = (f32[32,512]{1,0:T(8,128)S(1)}, f32[32,512]{1,0:T(8,128)S(1)}, u32[]{:S(2)}, u32[]{:S(2)}) collective-permute-start(f32[32,512]{1,0:T(8,128)S(1)} %get-tuple-element.26), channel_id=1, source_target_pairs={{0,6},{1,7},{8,14},{9,15},{16,22},{17,23},{24,30},{25,31},{32,38},... | collective-permute-start | bytes 196616 | tf_op jit(solution)/shard_map/ppermute | solution.py:321
  29.7 1.3 collective-permute-start.6
  31.1 3.7 %collective-permute-start.13 = (bf16[32,4096]{1,0:T(8,128)(2,1)S(1)}, bf16[32,4096]{1,0:T(8,128)(2,1)S(1)}, u32[]{:S(2)}, u32[]{:S(2)}) collective-permute-start(bf16[32,4096]{1,0:T(8,128)(2,1)S(1)} %get-tuple-element.48), channel_id=1, source_target_pairs={{0,16},{8,24},{4,20},{12,28},{16,0},{24,8},{20,4},{28,12},{32,48},... | collective-permute-start | bytes 786440 | tf_op jit(solution)/shard_map/ppermute | solution.py:47
  34.8 1.0 copy-done.4
  38.1 4.0 %forward_full.1 = (bf16[512,512]{1,0:T(8,128)(2,1)S(1)}, bf16[512,512]{1,0:T(8,128)(2,1)S(1)}, f32[4,512,128]{2,1,0:T(8,128)S(1)}, f32[4,256,128]{2,1,0:T(8,128)S(1)}) custom-call(bf16[512,512]{1,0:T(8,128)(2,1)S(1)} %copy-done.4, f32[4,512,128]{2,1,0:T(8,128)S(1)} %get-tuple-element.24.refs_1_.drive_ref, f32[4,256,128]{2,1,0:T(8,128)S(1)} %get-tuple-element.25.refs_2_, ...), custom_call_target="tpu_custom_call" | custom-call | flops 16777216 | bytes 5244928 | tf_op jit(solution)/shard_map/forward_full/pallas_call | solution.py:302
  42.6 1.6 collective-permute-start.17
  44.3 1.7 collective-permute-start.19
  46.0 7.9 %convolution_convert_fusion = bf16[256,8192]{1,0:T(8,128)(2,1)} fusion(bf16[512,8192]{1,0:T(8,128)(2,1)} %param.14, bf16[512,512]{1,0:T(8,128)(2,1)S(1)} %get-tuple-element.27), kind=kOutput, calls=%fused_computation.2 | convolution fusion | flops 2149580800 | bytes 12845056 | tf_op jit(solution)/shard_map/dot_general | solution.py:93
  54.0 1.0 broadcast_in_dim.33
  55.2 14.2 %collective-permute-done.17 = bf16[2,2,32,4096]{3,2,1,0:T(8,128)(2,1)S(1)} collective-permute-done((bf16[2,2,32,4096]{3,2,1,0:T(8,128)(2,1)S(1)}, bf16[2,2,32,4096]{3,2,1,0:T(8,128)(2,1)S(1)}, u32[]{:S(2)}, u32[]{:S(2)}) %collective-permute-start.17) | collective-permute-done | bytes 1048608 | tf_op jit(solution)/shard_map/ppermute | solution.py:47
  70.0 3.0 %collective-permute-start.23 = (bf16[1,2,32,4096]{3,2,1,0:T(8,128)(2,1)S(1)}, bf16[1,2,32,4096]{3,2,1,0:T(8,128)(2,1)S(1)}, u32[]{:S(2)}, u32[]{:S(2)}) collective-permute-start(bf16[1,2,32,4096]{3,2,1,0:T(8,128)(2,1)S(1)} %slice.119), channel_id=1, source_target_pairs={{0,96},{8,104},{4,100},{12,108},{16,112},{24,120},{20,116},{28,124... | collective-permute-start | bytes 1572872 | tf_op jit(solution)/shard_map/ppermute | solution.py:47
  73.7 10.7 %collective-permute-done.21 = bf16[1,2,32,4096]{3,2,1,0:T(8,128)(2,1)S(1)} collective-permute-done((bf16[1,2,32,4096]{3,2,1,0:T(8,128)(2,1)S(1)}, bf16[1,2,32,4096]{3,2,1,0:T(8,128)(2,1)S(1)}, u32[]{:S(2)}, u32[]{:S(2)}) %collective-permute-start.21) | collective-permute-done | bytes 524320 | tf_op jit(solution)/shard_map/ppermute | solution.py:47
  85.3 1.0 collective-permute-done.22
  87.1 1.3 multiply_convert_fusion.1
  88.4 2.0 %collective-permute-start.34 = (bf16[256,1024]{1,0:T(8,128)(2,1)S(1)}, bf16[256,1024]{1,0:T(8,128)(2,1)S(1)}, u32[]{:S(2)}, u32[]{:S(2)}) collective-permute-start(bf16[256,1024]{1,0:T(8,128)(2,1)S(1)} %get-tuple-element.46), channel_id=1, source_target_pairs={{0,1},{8,9},{4,5},{12,13},{16,17},{24,25},{20,21},{28,29},{32,33},... | collective-permute-start | bytes 1572872 | tf_op jit(solution)/shard_map/ppermute | solution.py:47
  90.4 6.6 %fusion.1 = f32[1024,512]{1,0:T(8,128)S(1)} fusion(bf16[1024,4096]{1,0:T(8,128)(2,1)S(1)} %bitcast.57, bf16[512,8192]{1,0:T(8,128)(2,1)} %param.14, s32[]{:T(128)S(6)} %select_n.104), kind=kOutput, calls=%fused_computation.3 | convolution fusion | flops 4294967296 | bytes 14680068 | tf_op jit(solution)/shard_map/dot_general | solution.py:357
  97.0 7.1 %fusion = bf16[256,8192]{1,0:T(8,128)(2,1)S(1)} fusion(bf16[512,8192]{1,0:T(8,128)(2,1)} %param.14, bf16[256,8192]{1,0:T(8,128)(2,1)} %collective-permute-done.7, bf16[512,512]{1,0:T(8,128)(2,1)S(1)} %get-tuple-element.27), kind=kOutput, calls=%fused_computation.1 | convolution fusion | flops 2153775104 | bytes 17039360 | tf_op jit(solution)/shard_map/dot_general | solution.py:94
  104.3 2.4 %collective-permute-start.10 = (bf16[32,8192]{1,0:T(8,128)(2,1)S(1)}, bf16[32,8192]{1,0:T(8,128)(2,1)S(1)}, u32[]{:S(2)}, u32[]{:S(2)}) collective-permute-start(bf16[32,8192]{1,0:T(8,128)(2,1)S(1)} %get-tuple-element.43), channel_id=1, source_target_pairs={{0,96},{8,104},{4,100},{12,108},{16,112},{24,120},{20,116},{28,124... | collective-permute-start | bytes 1572872 | tf_op jit(solution)/shard_map/ppermute | solution.py:47
  106.7 1.3 multiply_convert_fusion.2
  108.0 2.8 %collective-permute-start.36 = (bf16[256,1024]{1,0:T(8,128)(2,1)S(1)}, bf16[256,1024]{1,0:T(8,128)(2,1)S(1)}, u32[]{:S(2)}, u32[]{:S(2)}) collective-permute-start(bf16[256,1024]{1,0:T(8,128)(2,1)S(1)} %get-tuple-element.47), channel_id=1, source_target_pairs={{0,3},{8,11},{4,7},{12,15},{16,19},{24,27},{20,23},{28,31},{32,35}... | collective-permute-start | bytes 1572872 | tf_op jit(solution)/shard_map/ppermute | solution.py:47
  110.8 1.3 multiply_convert_fusion
  113.0 5.0 %collective-permute-done.10 = bf16[32,8192]{1,0:T(8,128)(2,1)S(1)} collective-permute-done((bf16[32,8192]{1,0:T(8,128)(2,1)S(1)}, bf16[32,8192]{1,0:T(8,128)(2,1)S(1)}, u32[]{:S(2)}, u32[]{:S(2)}) %collective-permute-start.10) | collective-permute-done | bytes 524320 | tf_op jit(solution)/shard_map/ppermute | solution.py:47
  118.0 3.3 %collective-permute-done.8 = bf16[32,8192]{1,0:T(8,128)(2,1)S(1)} collective-permute-done((bf16[32,8192]{1,0:T(8,128)(2,1)S(1)}, bf16[32,8192]{1,0:T(8,128)(2,1)S(1)}, u32[]{:S(2)}, u32[]{:S(2)}) %collective-permute-start.8) | collective-permute-done | bytes 524320 | tf_op jit(solution)/shard_map/ppermute | solution.py:47
  121.8 3.3 %collective-permute-start.11 = (bf16[64,8192]{1,0:T(8,128)(2,1)S(1)}, bf16[64,8192]{1,0:T(8,128)(2,1)S(1)}, u32[]{:S(2)}, u32[]{:S(2)}) collective-permute-start(bf16[64,8192]{1,0:T(8,128)(2,1)S(1)} %pad_maximum_fusion.1), channel_id=1, source_target_pairs={{0,96},{8,104},{4,100},{12,108},{16,112},{24,120},{20,116},{28,124... | collective-permute-start | bytes 3145736 | tf_op jit(solution)/shard_map/ppermute | solution.py:47
  125.8 10.5 %backward_ends.1 = (bf16[512,512]{1,0:T(8,128)(2,1)}, f32[4,512,128]{2,1,0:T(8,128)S(1)}, f32[56,512]{1,0:T(8,128)S(1)}, f32[4,128,128]{2,1,0:T(8,128)S(1)}) custom-call(f32[512,512]{1,0:T(8,128)S(1)} %slice_add_fusion.grad_ref, bf16[512,512]{1,0:T(8,128)(2,1)S(1)} %copy-done.5, f32[4,512,128]{2,1,0:T(8,128)S(1)} %get-tuple-element.28.pre_ref, ...), custom_call_target="tpu_custom_call" | custom-call | flops 41943040 | bytes 6176768 | tf_op jit(solution)/shard_map/backward_ends/pallas_call | solution.py:302
  136.3 2.3 %collective-permute-start.26 = (f32[56,512]{1,0:T(8,128)S(1)}, f32[56,512]{1,0:T(8,128)S(1)}, u32[]{:S(2)}, u32[]{:S(2)}) collective-permute-start(f32[56,512]{1,0:T(8,128)S(1)} %get-tuple-element.33.refs_7_), channel_id=1, source_target_pairs={{0,7},{1,0},{2,1},{3,2},{4,3},{5,4},{6,5},{7,6},{8,15},{9,8},{10,9... | collective-permute-start | bytes 344072 | tf_op jit(solution)/shard_map/ppermute | solution.py:321
  139.1 2.4 %collective-permute-start.28 = (f32[56,512]{1,0:T(8,128)S(1)}, f32[56,512]{1,0:T(8,128)S(1)}, u32[]{:S(2)}, u32[]{:S(2)}) collective-permute-start(f32[56,512]{1,0:T(8,128)S(1)} %get-tuple-element.33.refs_7_), channel_id=1, source_target_pairs={{0,5},{1,6},{2,7},{3,0},{4,1},{5,2},{6,3},{7,4},{8,13},{9,14},{10,... | collective-permute-start | bytes 344072 | tf_op jit(solution)/shard_map/ppermute | solution.py:321
  141.7 1.0 pad_maximum_fusion.3
  142.7 1.7 collective-permute-start.29
  144.5 1.0 pad_maximum_fusion.4
  145.5 4.6 %collective-permute-start.30 = (f32[56,512]{1,0:T(8,128)S(1)}, f32[56,512]{1,0:T(8,128)S(1)}, u32[]{:S(2)}, u32[]{:S(2)}) collective-permute-start(f32[56,512]{1,0:T(8,128)S(1)} %get-tuple-element.33.refs_7_), channel_id=1, source_target_pairs={{0,3},{1,4},{2,5},{3,6},{4,7},{5,0},{6,1},{7,2},{8,11},{9,12},{10,... | collective-permute-start | bytes 344072 | tf_op jit(solution)/shard_map/ppermute | solution.py:321
  151.0 4.0 %collective-permute-start.35 = (bf16[512,1024]{1,0:T(8,128)(2,1)}, bf16[512,1024]{1,0:T(8,128)(2,1)}, u32[]{:S(2)}, u32[]{:S(2)}) collective-permute-start(bf16[512,1024]{1,0:T(8,128)(2,1)} %pad_maximum_fusion.3), channel_id=1, source_target_pairs={{0,1},{8,9},{4,5},{12,13},{16,17},{24,25},{20,21},{28,29},{32,33},... | collective-permute-start | bytes 3145736 | tf_op jit(solution)/shard_map/ppermute | solution.py:47
  156.9 3.6 %collective-permute-start.12 = (bf16[32,8192]{1,0:T(8,128)(2,1)}, bf16[32,8192]{1,0:T(8,128)(2,1)}, u32[]{:S(2)}, u32[]{:S(2)}) collective-permute-start(bf16[32,8192]{1,0:T(8,128)(2,1)} %slice.144), channel_id=1, source_target_pairs={{0,16},{8,24},{4,20},{12,28},{16,0},{24,8},{20,4},{28,12},{32,48},... | collective-permute-start | bytes 1572872 | tf_op jit(solution)/shard_map/ppermute | solution.py:47
  160.5 5.2 %backward_full.1 = (bf16[512,512]{1,0:T(8,128)(2,1)}, bf16[512,512]{1,0:T(8,128)(2,1)}, f32[16,512]{1,0:T(8,128)}, f32[16,512]{1,0:T(8,128)}, f32[8,512]{1,0:T(8,128)S(1)}) custom-call(bf16[512,512]{1,0:T(8,128)(2,1)S(1)} %copy-done.1, bf16[512,512]{1,0:T(8,128)(2,1)S(1)} %copy-done.3, f32[4,512,128]{2,1,0:T(8,128)S(1)} %get-tuple-element.31.refs_2_, ...), custom_call_target="tpu_custom_call" | custom-call | flops 16777216 | bytes 4474880 | tf_op jit(solution)/shard_map/backward_full/pallas_call | solution.py:302
  166.3 12.0 %collective-permute-done.35 = bf16[512,1024]{1,0:T(8,128)(2,1)} collective-permute-done((bf16[512,1024]{1,0:T(8,128)(2,1)}, bf16[512,1024]{1,0:T(8,128)(2,1)}, u32[]{:S(2)}, u32[]{:S(2)}) %collective-permute-start.35) | collective-permute-done | bytes 1048608 | tf_op jit(solution)/shard_map/ppermute | solution.py:47
  178.3 4.8 %add_convert_fusion = bf16[512,1024]{1,0:T(8,128)(2,1)} fusion(bf16[512,1024]{1,0:T(8,128)(2,1)} %collective-permute-done.37, bf16[512,1024]{1,0:T(8,128)(2,1)} %collective-permute-done.35, bf16[1024,512]{1,0:T(8,128)(2,1)} %copy-done.16, bf16[1024,4096]{1,0:T(8,128)(2,1)} %bitcast.60, s32[]{:T(128)S(6)} %select_n.118), kind=kOutput, calls=%fused_computation.5 | convolution fusion | flops 1077936128 | bytes 6291460 | tf_op jit(solution)/shard_map/dot_general | solution.py:106
  183.2 1.9 %fusion.21 = bf16[32,8192]{1,0:T(8,128)(2,1)} fusion(f32[64,8192]{1,0:T(8,128)S(1)} %copy-done.15, bf16[32,8192]{1,0:T(8,128)(2,1)} %collective-permute-done.12), kind=kLoop, calls=%fused_computation.23 | loop fusion | flops 786432 | bytes 2097152 | tf_op jit(solution)/shard_map/convert_element_type | solution.py:97
  (110 shorter events, 12.9 us)
Async XLA Ops:
  1.7 40.5 %collective-permute-start.14 = (bf16[32,4096]{1,0:T(8,128)(2,1)S(1)}, bf16[32,4096]{1,0:T(8,128)(2,1)S(1)}, u32[]{:S(2)}, u32[]{:S(2)}) collective-permute-start(bf16[32,4096]{1,0:T(8,128)(2,1)S(1)} %get-tuple-element.49), channel_id=1, source_target_pairs={{0,4},{8,12},{4,16},{12,24},{16,20},{24,28},{20,0},{28,8},{32,36},... | collective-permute-start | bytes 786440 | tf_op jit(solution)/shard_map/ppermute | solution.py:47
  3.8 38.4 %collective-permute-start.15 = (bf16[32,4096]{1,0:T(8,128)(2,1)S(1)}, bf16[32,4096]{1,0:T(8,128)(2,1)S(1)}, u32[]{:S(2)}, u32[]{:S(2)}) collective-permute-start(bf16[32,4096]{1,0:T(8,128)(2,1)S(1)} %get-tuple-element.49), channel_id=1, source_target_pairs={{0,20},{8,28},{4,0},{12,8},{16,4},{24,12},{20,16},{28,24},{32,52},... | collective-permute-start | bytes 786440 | tf_op jit(solution)/shard_map/ppermute | solution.py:47
  12.4 10.7 %collective-permute-start = (f32[32,512]{1,0:T(8,128)S(1)}, f32[32,512]{1,0:T(8,128)S(1)}, u32[]{:S(2)}, u32[]{:S(2)}) collective-permute-start(f32[32,512]{1,0:T(8,128)S(1)} %get-tuple-element.26), channel_id=1, source_target_pairs={{0,1},{1,2},{2,3},{3,4},{4,5},{5,6},{6,7},{8,9},{9,10},{10,11},{11... | collective-permute-start | bytes 196616 | tf_op jit(solution)/shard_map/ppermute | solution.py:321
  15.8 8.6 %collective-permute-start.1 = (f32[32,512]{1,0:T(8,128)S(1)}, f32[32,512]{1,0:T(8,128)S(1)}, u32[]{:S(2)}, u32[]{:S(2)}) collective-permute-start(f32[32,512]{1,0:T(8,128)S(1)} %get-tuple-element.26), channel_id=1, source_target_pairs={{0,2},{1,3},{2,4},{3,5},{4,6},{5,7},{8,10},{9,11},{10,12},{11,13},... | collective-permute-start | bytes 196616 | tf_op jit(solution)/shard_map/ppermute | solution.py:321
  20.5 7.1 %collective-permute-start.2 = (f32[32,512]{1,0:T(8,128)S(1)}, f32[32,512]{1,0:T(8,128)S(1)}, u32[]{:S(2)}, u32[]{:S(2)}) collective-permute-start(f32[32,512]{1,0:T(8,128)S(1)} %get-tuple-element.26), channel_id=1, source_target_pairs={{0,3},{1,4},{2,5},{3,6},{4,7},{8,11},{9,12},{10,13},{11,14},{12,15... | collective-permute-start | bytes 196616 | tf_op jit(solution)/shard_map/ppermute | solution.py:321
  23.1 6.6 %collective-permute-start.3 = (f32[32,512]{1,0:T(8,128)S(1)}, f32[32,512]{1,0:T(8,128)S(1)}, u32[]{:S(2)}, u32[]{:S(2)}) collective-permute-start(f32[32,512]{1,0:T(8,128)S(1)} %get-tuple-element.26), channel_id=1, source_target_pairs={{0,4},{1,5},{2,6},{3,7},{8,12},{9,13},{10,14},{11,15},{16,20},{17,... | collective-permute-start | bytes 196616 | tf_op jit(solution)/shard_map/ppermute | solution.py:321
  24.4 6.7 %collective-permute-start.4 = (f32[32,512]{1,0:T(8,128)S(1)}, f32[32,512]{1,0:T(8,128)S(1)}, u32[]{:S(2)}, u32[]{:S(2)}) collective-permute-start(f32[32,512]{1,0:T(8,128)S(1)} %get-tuple-element.26), channel_id=1, source_target_pairs={{0,5},{1,6},{2,7},{8,13},{9,14},{10,15},{16,21},{17,22},{18,23},{2... | collective-permute-start | bytes 196616 | tf_op jit(solution)/shard_map/ppermute | solution.py:321
  27.6 7.2 %collective-permute-start.5 = (f32[32,512]{1,0:T(8,128)S(1)}, f32[32,512]{1,0:T(8,128)S(1)}, u32[]{:S(2)}, u32[]{:S(2)}) collective-permute-start(f32[32,512]{1,0:T(8,128)S(1)} %get-tuple-element.26), channel_id=1, source_target_pairs={{0,6},{1,7},{8,14},{9,15},{16,22},{17,23},{24,30},{25,31},{32,38},... | collective-permute-start | bytes 196616 | tf_op jit(solution)/shard_map/ppermute | solution.py:321
  29.7 5.1 %collective-permute-start.6 = (f32[32,512]{1,0:T(8,128)S(1)}, f32[32,512]{1,0:T(8,128)S(1)}, u32[]{:S(2)}, u32[]{:S(2)}) collective-permute-start(f32[32,512]{1,0:T(8,128)S(1)} %get-tuple-element.26), channel_id=1, source_target_pairs={{0,7},{8,15},{16,23},{24,31},{32,39},{40,47},{48,55},{56,63},{64,7... | collective-permute-start | bytes 196616 | tf_op jit(solution)/shard_map/ppermute | solution.py:321
  31.1 11.2 %collective-permute-start.13 = (bf16[32,4096]{1,0:T(8,128)(2,1)S(1)}, bf16[32,4096]{1,0:T(8,128)(2,1)S(1)}, u32[]{:S(2)}, u32[]{:S(2)}) collective-permute-start(bf16[32,4096]{1,0:T(8,128)(2,1)S(1)} %get-tuple-element.48), channel_id=1, source_target_pairs={{0,16},{8,24},{4,20},{12,28},{16,0},{24,8},{20,4},{28,12},{32,48},... | collective-permute-start | bytes 786440 | tf_op jit(solution)/shard_map/ppermute | solution.py:47
  42.1 13.1 %collective-permute-start.33 = (bf16[512,512]{1,0:T(8,128)(2,1)S(1)}, bf16[512,512]{1,0:T(8,128)(2,1)S(1)}, u32[]{:S(2)}, u32[]{:S(2)}) collective-permute-start(bf16[512,512]{1,0:T(8,128)(2,1)S(1)} %get-tuple-element.36), channel_id=1, source_target_pairs={{0,4},{8,12},{4,0},{12,8},{16,20},{24,28},{20,16},{28,24},{32,36},... | collective-permute-start | bytes 1572872 | tf_op jit(solution)/shard_map/ppermute | solution.py:47
  42.6 30.4 %collective-permute-start.16 = (bf16[2,2,32,4096]{3,2,1,0:T(8,128)(2,1)S(1)}, bf16[2,2,32,4096]{3,2,1,0:T(8,128)(2,1)S(1)}, u32[]{:S(2)}, u32[]{:S(2)}) collective-permute-start(bf16[2,2,32,4096]{3,2,1,0:T(8,128)(2,1)S(1)} %pad_maximum_fusion.2), channel_id=1, source_target_pairs={{0,8},{8,0},{4,12},{12,4},{16,24},{24,16},{20,28},{28,20},{32,40},... | collective-permute-start | bytes 3145736 | tf_op jit(solution)/shard_map/ppermute | solution.py:47
  42.6 26.8 %collective-permute-start.17 = (bf16[2,2,32,4096]{3,2,1,0:T(8,128)(2,1)S(1)}, bf16[2,2,32,4096]{3,2,1,0:T(8,128)(2,1)S(1)}, u32[]{:S(2)}, u32[]{:S(2)}) collective-permute-start(bf16[2,2,32,4096]{3,2,1,0:T(8,128)(2,1)S(1)} %pad_maximum_fusion.2), channel_id=1, source_target_pairs={{0,32},{8,40},{4,36},{12,44},{16,48},{24,56},{20,52},{28,60},{32,6... | collective-permute-start | bytes 3145736 | tf_op jit(solution)/shard_map/ppermute | solution.py:47
  44.3 25.6 %collective-permute-start.19 = (bf16[2,2,32,4096]{3,2,1,0:T(8,128)(2,1)S(1)}, bf16[2,2,32,4096]{3,2,1,0:T(8,128)(2,1)S(1)}, u32[]{:S(2)}, u32[]{:S(2)}) collective-permute-start(bf16[2,2,32,4096]{3,2,1,0:T(8,128)(2,1)S(1)} %pad_maximum_fusion.2), channel_id=1, source_target_pairs={{0,96},{8,104},{4,100},{12,108},{16,112},{24,120},{20,116},{28,124... | collective-permute-start | bytes 3145736 | tf_op jit(solution)/shard_map/ppermute | solution.py:47
  53.9 43.1 %collective-permute-start.7 = (bf16[256,8192]{1,0:T(8,128)(2,1)}, bf16[256,8192]{1,0:T(8,128)(2,1)}, u32[]{:S(2)}, u32[]{:S(2)}) collective-permute-start(bf16[256,8192]{1,0:T(8,128)(2,1)} %convolution_convert_fusion), channel_id=1, source_target_pairs={{0,8},{8,0},{4,12},{12,4},{16,24},{24,16},{20,28},{28,20},{32,40},... | collective-permute-start | bytes 12582920 | tf_op jit(solution)/shard_map/ppermute | solution.py:47
  55.2 55.5 %copy-start.16 = (bf16[1024,512]{1,0:T(8,128)(2,1)}, bf16[1024,512]{1,0:T(8,128)(2,1)S(1)}, u32[]{:S(2)}) copy-start(bf16[1024,512]{1,0:T(8,128)(2,1)S(1)} %constant_dynamic-update-slice_fusion) | copy-start | bytes 3145732
  69.5 14.8 %collective-permute-start.21 = (bf16[1,2,32,4096]{3,2,1,0:T(8,128)(2,1)S(1)}, bf16[1,2,32,4096]{3,2,1,0:T(8,128)(2,1)S(1)}, u32[]{:S(2)}, u32[]{:S(2)}) collective-permute-start(bf16[1,2,32,4096]{3,2,1,0:T(8,128)(2,1)S(1)} %slice.118), channel_id=1, source_target_pairs={{0,32},{8,40},{4,36},{12,44},{16,48},{24,56},{20,52},{28,60},{32,6... | collective-permute-start | bytes 1572872 | tf_op jit(solution)/shard_map/ppermute | solution.py:47
  70.0 14.4 %collective-permute-start.23 = (bf16[1,2,32,4096]{3,2,1,0:T(8,128)(2,1)S(1)}, bf16[1,2,32,4096]{3,2,1,0:T(8,128)(2,1)S(1)}, u32[]{:S(2)}, u32[]{:S(2)}) collective-permute-start(bf16[1,2,32,4096]{3,2,1,0:T(8,128)(2,1)S(1)} %slice.119), channel_id=1, source_target_pairs={{0,96},{8,104},{4,100},{12,108},{16,112},{24,120},{20,116},{28,124... | collective-permute-start | bytes 1572872 | tf_op jit(solution)/shard_map/ppermute | solution.py:47
  72.9 11.9 %collective-permute-start.18 = (bf16[2,2,32,4096]{3,2,1,0:T(8,128)(2,1)S(1)}, bf16[2,2,32,4096]{3,2,1,0:T(8,128)(2,1)S(1)}, u32[]{:S(2)}, u32[]{:S(2)}) collective-permute-start(bf16[2,2,32,4096]{3,2,1,0:T(8,128)(2,1)S(1)} %collective-permute-done.17), channel_id=1, source_target_pairs={{0,8},{8,0},{4,12},{12,4},{16,24},{24,16},{20,28},{28,20},{32,40},... | collective-permute-start | bytes 3145736 | tf_op jit(solution)/shard_map/ppermute | solution.py:47
  72.9 12.1 %collective-permute-start.20 = (bf16[2,2,32,4096]{3,2,1,0:T(8,128)(2,1)S(1)}, bf16[2,2,32,4096]{3,2,1,0:T(8,128)(2,1)S(1)}, u32[]{:S(2)}, u32[]{:S(2)}) collective-permute-start(bf16[2,2,32,4096]{3,2,1,0:T(8,128)(2,1)S(1)} %collective-permute-done.19), channel_id=1, source_target_pairs={{0,8},{8,0},{4,12},{12,4},{16,24},{24,16},{20,28},{28,20},{32,40},... | collective-permute-start | bytes 3145736 | tf_op jit(solution)/shard_map/ppermute | solution.py:47
  84.3 1.9 %collective-permute-start.22 = (bf16[1,2,32,4096]{3,2,1,0:T(8,128)(2,1)S(1)}, bf16[1,2,32,4096]{3,2,1,0:T(8,128)(2,1)S(1)}, u32[]{:S(2)}, u32[]{:S(2)}) collective-permute-start(bf16[1,2,32,4096]{3,2,1,0:T(8,128)(2,1)S(1)} %collective-permute-done.21), channel_id=1, source_target_pairs={{0,8},{8,0},{4,12},{12,4},{16,24},{24,16},{20,28},{28,20},{32,40},... | collective-permute-start | bytes 1572872 | tf_op jit(solution)/shard_map/ppermute | solution.py:47
  84.3 2.7 %collective-permute-start.24 = (bf16[1,2,32,4096]{3,2,1,0:T(8,128)(2,1)S(1)}, bf16[1,2,32,4096]{3,2,1,0:T(8,128)(2,1)S(1)}, u32[]{:S(2)}, u32[]{:S(2)}) collective-permute-start(bf16[1,2,32,4096]{3,2,1,0:T(8,128)(2,1)S(1)} %collective-permute-done.23), channel_id=1, source_target_pairs={{0,8},{8,0},{4,12},{12,4},{16,24},{24,16},{20,28},{28,20},{32,40},... | collective-permute-start | bytes 1572872 | tf_op jit(solution)/shard_map/ppermute | solution.py:47
  87.0 23.7 %copy-start.13 = (bf16[2,4,2,2,32,4096]{5,4,3,2,1,0:T(8,128)(2,1)}, bf16[2,4,2,2,32,4096]{5,4,3,2,1,0:T(8,128)(2,1)S(1)}, u32[]{:S(2)}) copy-start(bf16[2,4,2,2,32,4096]{5,4,3,2,1,0:T(8,128)(2,1)S(1)} %bitcast_dynamic-update-slice_fusion.9) | copy-start | bytes 25165828
  88.4 50.2 %collective-permute-start.34 = (bf16[256,1024]{1,0:T(8,128)(2,1)S(1)}, bf16[256,1024]{1,0:T(8,128)(2,1)S(1)}, u32[]{:S(2)}, u32[]{:S(2)}) collective-permute-start(bf16[256,1024]{1,0:T(8,128)(2,1)S(1)} %get-tuple-element.46), channel_id=1, source_target_pairs={{0,1},{8,9},{4,5},{12,13},{16,17},{24,25},{20,21},{28,29},{32,33},... | collective-permute-start | bytes 1572872 | tf_op jit(solution)/shard_map/ppermute | solution.py:47
  104.3 13.7 %collective-permute-start.10 = (bf16[32,8192]{1,0:T(8,128)(2,1)S(1)}, bf16[32,8192]{1,0:T(8,128)(2,1)S(1)}, u32[]{:S(2)}, u32[]{:S(2)}) collective-permute-start(bf16[32,8192]{1,0:T(8,128)(2,1)S(1)} %get-tuple-element.43), channel_id=1, source_target_pairs={{0,96},{8,104},{4,100},{12,108},{16,112},{24,120},{20,116},{28,124... | collective-permute-start | bytes 1572872 | tf_op jit(solution)/shard_map/ppermute | solution.py:47
  106.7 14.6 %collective-permute-start.8 = (bf16[32,8192]{1,0:T(8,128)(2,1)S(1)}, bf16[32,8192]{1,0:T(8,128)(2,1)S(1)}, u32[]{:S(2)}, u32[]{:S(2)}) collective-permute-start(bf16[32,8192]{1,0:T(8,128)(2,1)S(1)} %get-tuple-element.42), channel_id=1, source_target_pairs={{0,32},{8,40},{4,36},{12,44},{16,48},{24,56},{20,52},{28,60},{32,6... | collective-permute-start | bytes 1572872 | tf_op jit(solution)/shard_map/ppermute | solution.py:47
  108.0 31.1 %collective-permute-start.36 = (bf16[256,1024]{1,0:T(8,128)(2,1)S(1)}, bf16[256,1024]{1,0:T(8,128)(2,1)S(1)}, u32[]{:S(2)}, u32[]{:S(2)}) collective-permute-start(bf16[256,1024]{1,0:T(8,128)(2,1)S(1)} %get-tuple-element.47), channel_id=1, source_target_pairs={{0,3},{8,11},{4,7},{12,15},{16,19},{24,27},{20,23},{28,31},{32,35}... | collective-permute-start | bytes 1572872 | tf_op jit(solution)/shard_map/ppermute | solution.py:47
  112.2 13.5 %collective-permute-start.25 = (bf16[512,512]{1,0:T(8,128)(2,1)S(1)}, bf16[512,512]{1,0:T(8,128)(2,1)S(1)}, u32[]{:S(2)}, u32[]{:S(2)}) collective-permute-start(bf16[512,512]{1,0:T(8,128)(2,1)S(1)} %slice.143), channel_id=1, source_target_pairs={{0,4},{8,12},{4,0},{12,8},{16,20},{24,28},{20,16},{28,24},{32,36},... | collective-permute-start | bytes 1572872 | tf_op jit(solution)/shard_map/ppermute | solution.py:47
  121.6 4.3 %copy-start.5 = (bf16[512,512]{1,0:T(8,128)(2,1)S(1)}, bf16[512,512]{1,0:T(8,128)(2,1)}, u32[]{:S(2)}) copy-start(bf16[512,512]{1,0:T(8,128)(2,1)} %query_ref.1) | copy-start | bytes 1572868
  121.6 4.3 %copy-start.8 = (f32[16,512]{1,0:T(8,128)S(1)}, f32[16,512]{1,0:T(8,128)}, u32[]{:S(2)}) copy-start(f32[16,512]{1,0:T(8,128)} %refs_4_.3) | copy-start | bytes 98308
  121.7 29.4 %collective-permute-start.9 = (bf16[64,8192]{1,0:T(8,128)(2,1)S(1)}, bf16[64,8192]{1,0:T(8,128)(2,1)S(1)}, u32[]{:S(2)}, u32[]{:S(2)}) collective-permute-start(bf16[64,8192]{1,0:T(8,128)(2,1)S(1)} %pad_maximum_fusion), channel_id=1, source_target_pairs={{0,32},{8,40},{4,36},{12,44},{16,48},{24,56},{20,52},{28,60},{32,6... | collective-permute-start | bytes 3145736 | tf_op jit(solution)/shard_map/ppermute | solution.py:47
  121.8 33.2 %collective-permute-start.11 = (bf16[64,8192]{1,0:T(8,128)(2,1)S(1)}, bf16[64,8192]{1,0:T(8,128)(2,1)S(1)}, u32[]{:S(2)}, u32[]{:S(2)}) collective-permute-start(bf16[64,8192]{1,0:T(8,128)(2,1)S(1)} %pad_maximum_fusion.1), channel_id=1, source_target_pairs={{0,96},{8,104},{4,100},{12,108},{16,112},{24,120},{20,116},{28,124... | collective-permute-start | bytes 3145736 | tf_op jit(solution)/shard_map/ppermute | solution.py:47
  136.3 6.4 %collective-permute-start.26 = (f32[56,512]{1,0:T(8,128)S(1)}, f32[56,512]{1,0:T(8,128)S(1)}, u32[]{:S(2)}, u32[]{:S(2)}) collective-permute-start(f32[56,512]{1,0:T(8,128)S(1)} %get-tuple-element.33.refs_7_), channel_id=1, source_target_pairs={{0,7},{1,0},{2,1},{3,2},{4,3},{5,4},{6,5},{7,6},{8,15},{9,8},{10,9... | collective-permute-start | bytes 344072 | tf_op jit(solution)/shard_map/ppermute | solution.py:321
  138.7 6.8 %collective-permute-start.27 = (f32[56,512]{1,0:T(8,128)S(1)}, f32[56,512]{1,0:T(8,128)S(1)}, u32[]{:S(2)}, u32[]{:S(2)}) collective-permute-start(f32[56,512]{1,0:T(8,128)S(1)} %get-tuple-element.33.refs_7_), channel_id=1, source_target_pairs={{0,6},{1,7},{2,0},{3,1},{4,2},{5,3},{6,4},{7,5},{8,14},{9,15},{10,... | collective-permute-start | bytes 344072 | tf_op jit(solution)/shard_map/ppermute | solution.py:321
  139.1 11.0 %collective-permute-start.28 = (f32[56,512]{1,0:T(8,128)S(1)}, f32[56,512]{1,0:T(8,128)S(1)}, u32[]{:S(2)}, u32[]{:S(2)}) collective-permute-start(f32[56,512]{1,0:T(8,128)S(1)} %get-tuple-element.33.refs_7_), channel_id=1, source_target_pairs={{0,5},{1,6},{2,7},{3,0},{4,1},{5,2},{6,3},{7,4},{8,13},{9,14},{10,... | collective-permute-start | bytes 344072 | tf_op jit(solution)/shard_map/ppermute | solution.py:321
  142.7 17.8 %copy-start.1 = (bf16[512,512]{1,0:T(8,128)(2,1)S(1)}, bf16[512,512]{1,0:T(8,128)(2,1)}, u32[]{:S(2)}) copy-start(bf16[512,512]{1,0:T(8,128)(2,1)} %refs_0_.3) | copy-start | bytes 1572868
  142.7 17.8 %copy-start.3 = (bf16[512,512]{1,0:T(8,128)(2,1)S(1)}, bf16[512,512]{1,0:T(8,128)(2,1)}, u32[]{:S(2)}) copy-start(bf16[512,512]{1,0:T(8,128)(2,1)} %refs_1_.1) | copy-start | bytes 1572868
  142.7 17.8 %copy-start.10 = (f32[16,512]{1,0:T(8,128)S(1)}, f32[16,512]{1,0:T(8,128)}, u32[]{:S(2)}) copy-start(f32[16,512]{1,0:T(8,128)} %refs_5_.1) | copy-start | bytes 98308
  142.7 17.8 %copy-start.12 = (f32[512]{0:T(512)S(1)}, f32[512]{0:T(512)}, u32[]{:S(2)}) copy-start(f32[512]{0:T(512)} %param.11) | copy-start | bytes 6148
  142.7 7.4 %collective-permute-start.29 = (f32[56,512]{1,0:T(8,128)S(1)}, f32[56,512]{1,0:T(8,128)S(1)}, u32[]{:S(2)}, u32[]{:S(2)}) collective-permute-start(f32[56,512]{1,0:T(8,128)S(1)} %get-tuple-element.33.refs_7_), channel_id=1, source_target_pairs={{0,4},{1,5},{2,6},{3,7},{4,0},{5,1},{6,2},{7,3},{8,12},{9,13},{10,... | collective-permute-start | bytes 344072 | tf_op jit(solution)/shard_map/ppermute | solution.py:321
  145.5 10.8 %collective-permute-start.30 = (f32[56,512]{1,0:T(8,128)S(1)}, f32[56,512]{1,0:T(8,128)S(1)}, u32[]{:S(2)}, u32[]{:S(2)}) collective-permute-start(f32[56,512]{1,0:T(8,128)S(1)} %get-tuple-element.33.refs_7_), channel_id=1, source_target_pairs={{0,3},{1,4},{2,5},{3,6},{4,7},{5,0},{6,1},{7,2},{8,11},{9,12},{10,... | collective-permute-start | bytes 344072 | tf_op jit(solution)/shard_map/ppermute | solution.py:321
  150.1 10.4 %collective-permute-start.31 = (f32[56,512]{1,0:T(8,128)S(1)}, f32[56,512]{1,0:T(8,128)S(1)}, u32[]{:S(2)}, u32[]{:S(2)}) collective-permute-start(f32[56,512]{1,0:T(8,128)S(1)} %get-tuple-element.33.refs_7_), channel_id=1, source_target_pairs={{0,2},{1,3},{2,4},{3,5},{4,6},{5,7},{6,0},{7,1},{8,10},{9,11},{10,... | collective-permute-start | bytes 344072 | tf_op jit(solution)/shard_map/ppermute | solution.py:321
  150.1 10.4 %collective-permute-start.32 = (f32[56,512]{1,0:T(8,128)S(1)}, f32[56,512]{1,0:T(8,128)S(1)}, u32[]{:S(2)}, u32[]{:S(2)}) collective-permute-start(f32[56,512]{1,0:T(8,128)S(1)} %get-tuple-element.33.refs_7_), channel_id=1, source_target_pairs={{0,1},{1,2},{2,3},{3,4},{4,5},{5,6},{6,7},{7,0},{8,9},{9,10},{10,1... | collective-permute-start | bytes 344072 | tf_op jit(solution)/shard_map/ppermute | solution.py:321
  151.0 27.3 %collective-permute-start.35 = (bf16[512,1024]{1,0:T(8,128)(2,1)}, bf16[512,1024]{1,0:T(8,128)(2,1)}, u32[]{:S(2)}, u32[]{:S(2)}) collective-permute-start(bf16[512,1024]{1,0:T(8,128)(2,1)} %pad_maximum_fusion.3), channel_id=1, source_target_pairs={{0,1},{8,9},{4,5},{12,13},{16,17},{24,25},{20,21},{28,29},{32,33},... | collective-permute-start | bytes 3145736 | tf_op jit(solution)/shard_map/ppermute | solution.py:47
  155.0 23.3 %collective-permute-start.37 = (bf16[512,1024]{1,0:T(8,128)(2,1)}, bf16[512,1024]{1,0:T(8,128)(2,1)}, u32[]{:S(2)}, u32[]{:S(2)}) collective-permute-start(bf16[512,1024]{1,0:T(8,128)(2,1)} %pad_maximum_fusion.4), channel_id=1, source_target_pairs={{0,3},{8,11},{4,7},{12,15},{16,19},{24,27},{20,23},{28,31},{32,35}... | collective-permute-start | bytes 3145736 | tf_op jit(solution)/shard_map/ppermute | solution.py:47
  155.4 1.5 copy-start.14
  156.9 26.3 %collective-permute-start.12 = (bf16[32,8192]{1,0:T(8,128)(2,1)}, bf16[32,8192]{1,0:T(8,128)(2,1)}, u32[]{:S(2)}, u32[]{:S(2)}) collective-permute-start(bf16[32,8192]{1,0:T(8,128)(2,1)} %slice.144), channel_id=1, source_target_pairs={{0,16},{8,24},{4,20},{12,28},{16,0},{24,8},{20,4},{28,12},{32,48},... | collective-permute-start | bytes 1572872 | tf_op jit(solution)/shard_map/ppermute | solution.py:47
  160.5 22.6 %copy-start.15 = (f32[64,8192]{1,0:T(8,128)S(1)}, f32[64,8192]{1,0:T(8,128)}, u32[]{:S(2)}) copy-start(f32[64,8192]{1,0:T(8,128)} %copy-done.14) | copy-start | bytes 6291460
  (7 other events, 6.1 us)

commit v2 on v1

--- a/solution.py
+++ b/solution.py
@@ -47,8 +47,8 @@
     return lax.ppermute(value, ("chan", "seq"), moves)
 
 
-def gather_cotangent(cotangent):
-    y, high, core, low, _ = places()
+def gather_z(cotangent):
+    _, high, _, low, _ = places()
     tokens, width = cotangent.shape
     half = width // 2
     mine = lax.dynamic_slice(cotangent, (0, low * half), (tokens, half))
@@ -57,55 +57,81 @@
     stack = jnp.where(high == 0, jnp.stack([mine, across]), jnp.stack([across, mine]))
     same, differ = jnp.where(low == 1, above, below), jnp.where(low == 1, below, above)
     other = jnp.where(high == 0, jnp.stack([same, differ]), jnp.stack([differ, same]))
-    block = jnp.stack([stack, other])
+    return jnp.stack([stack, other])
+
+
+def gather_y(block, near_blocks, kept):
+    y, _, core, _, _ = places()
+    _, _, tokens, half = block.shape
 
     def put(whole, part, first, row, at_core):
         return lax.dynamic_update_slice(whole, part[:, None, :, None], (first, row, 0, at_core, 0, 0))
 
-    whole = jnp.zeros((2, RING, 2, 2, tokens, half), cotangent.dtype)
+    whole = jnp.zeros((2, RING, 2, 2, tokens, half), block.dtype)
     before, after = lax.rem(y + RING - 1, RING), lax.rem(y + 1, RING)
     far = lax.rem(y + 2, RING)
-    from_before, from_after = hop(block, y=1), hop(block, y=-1)
+    from_before, from_after = near_blocks
     far_own, far_other = hop(from_before[:1], y=1), hop(from_after[1:], y=-1)
+    far_own, far_other, kept = together(far_own, far_other, kept)
     for part, first, row in (
         (block, 0, y), (from_before, 0, before), (from_after, 0, after), (far_own, 0, far), (far_other, 1, far)
     ):
         whole = put(whole, part, first, row, core)
         whole = put(whole, hop(part, core=1), first, row, 1 - core)
-    return whole
+    return whole, kept
 
 
 def add(*parts):
     return functools.reduce(jnp.add, [part.astype(F32) for part in parts])
 
 
-def ring_sum(blocks, axis):
-    half = blocks[2].shape[0] // 2
-    first = hop(blocks[2][:half], **{axis: 1})
-    second = hop(blocks[2][half:], **{axis: -1})
-    up = jnp.concatenate([add(blocks[1][:half], first).astype(BF16), blocks[1][half:]])
-    down = jnp.concatenate([blocks[3][:half], add(blocks[3][half:], second).astype(BF16)])
-    return add(blocks[0], hop(up, **{axis: 1}), hop(down, **{axis: -1}))
-
-
-def mix(turned, out_weight):
-    half = turned.shape[0] // 2
-    sent = hop(jnp.dot(turned[half:], out_weight, preferred_element_type=F32).astype(BF16), core=1)
-    kept = add(jnp.dot(turned[:half], out_weight, preferred_element_type=F32), sent).astype(BF16)
-    total = ring_sum(kept.reshape(RING, half // RING, -1), "y")
-    rest = total.shape[0] // 2
-    return add(total[:rest], hop(total[rest:].astype(BF16), z=2)).astype(BF16)
-
-
-def weigh(gated, cot_rows, scale):
-    x = places()[4]
+def project_tile(rows_ref, weight_ref, *out_refs):
+    product = jnp.dot(rows_ref[...], weight_ref[...], preferred_element_type=F32).astype(BF16)
+    first = 0
+    for ref in out_refs:
+        ref[...] = product[first : first + ref.shape[0]]
+        first += ref.shape[0]
+
+
+def project(turned, out_weight):
+    rows, depth = turned.shape
+    width = out_weight.shape[1]
+    tile = 1024
+    sizes = [rows // 8, 3 * rows // 8] * 2
+    return pl.pallas_call(
+        project_tile,
+        grid=(width // tile,),
+        out_shape=[jax.ShapeDtypeStruct((size, width), BF16) for size in sizes],
+        in_specs=[pl.BlockSpec((rows, depth), lambda i: (0, 0)), pl.BlockSpec((depth, tile), lambda i: (0, i))],
+        out_specs=[pl.BlockSpec((size, tile), lambda i: (0, i)) for size in sizes],
+        compiler_params=pltpu.CompilerParams(vmem_limit_bytes=32 * 2**20),
+        cost_estimate=pl.CostEstimate(
+            flops=2 * rows * depth * width, bytes_accessed=2 * width * (rows + depth), transcendentals=0
+        ),
+        name="project",
+    )(turned, out_weight)
+
+
+def weigh(gated, cot_rows, scale, r):
     width = cot_rows.shape[1] // RING
-    blocks = [None] * RING
-    for r in (2, 1, 3, 0):
-        columns = lax.dynamic_slice(cot_rows, (0, lax.rem(x + r, RING) * width), (cot_rows.shape[0], width))
-        product = lax.dot_general(gated, columns, (((0,), (0,)), ((), ())), preferred_element_type=F32)
-        blocks[r] = (product * scale).astype(BF16)
-    return ring_sum(blocks, "x").astype(BF16)
+    first = lax.rem(places()[4] + r, RING) * width
+    columns = lax.dynamic_slice(cot_rows, (0, first), (cot_rows.shape[0], width))
+    product = lax.dot_general(gated, columns, (((0,), (0,)), ((), ())), preferred_element_type=F32)
+    return (product * scale).astype(BF16)
+
+
+def nearby(refs, distance, way, first, modes, lanes):
+    _, _, _, low, x = places()
+    before = x if way == 1 else RING - 1 - x
+    other_counts = low == (way + 1) // 2
+    other = refs[0].shape[0] // 2 if way == 1 else modes
+    step = distance % RING
+    ref = refs[way * step % RING]
+    mine = ref[pl.ds(first, modes), lanes]
+    theirs = jnp.where(other_counts, ref[pl.ds(other + first, modes), lanes], 0.0)
+    if distance < RING:
+        return jnp.where(step <= before, mine, theirs)
+    return jnp.where(step <= before, theirs, 0.0)
 
 
 def forward_ends(key_ref, value_ref, log_ref, ends_ref, sub_ref, drive_ref, decay_ref, zero_ref):
@@ -155,9 +181,9 @@
         power = jnp.exp(-span * rate)
         state = jnp.zeros_like(rate)
         lagged = jnp.zeros_like(rate)
-        for end in end_refs[::-1]:
-            lagged = stretch * (lagged + length * state) + end[pl.ds(modes, modes), lanes]
-            state = stretch * state + end[pl.ds(0, modes), lanes]
+        for distance in range(2 * RING - 1, 0, -1):
+            lagged = stretch * (lagged + length * state) + nearby(end_refs, distance, 1, modes, modes, lanes)
+            state = stretch * state + nearby(end_refs, distance, 1, 0, modes, lanes)
         for j in range(SUBS):
             now_rows, lag_rows = (pl.ds((j + k) * modes, modes) for k in (0, SUBS))
             lead_ref[tile, now_rows] = state
@@ -181,7 +207,8 @@
     part = length // (RING * 4)
     y, high, core, _, _ = places()
     for i in range(RING * 4):
-        there = lax.rem(i % 2 + core, 2) * RING + lax.rem(i // 4 + RING - y, RING)
+        on = lax.rem(i // 4 + RING - y, RING)
+        there = lax.rem(i % 2 + core, 2) * RING + jnp.where(on == 0, 3, jnp.where(on == 2, 0, (on + 1) // 2))
         there = there * 2 + lax.rem(i // 2 % 2 + high, 2)
         turned_ref[pl.ds(pl.multiple_of(there * part, part), part)] = gated_ref[pl.ds(i * part, part)]
 
@@ -249,32 +276,30 @@
         sums_ref[pl.ds(2 * modes, modes), lanes] = lag_pair
 
 
-def backward_full(*refs, blocks, scale):
+def backward_full(*refs, scale):
     (key_ref, value_ref, back_ref, sub_ref, log_ref, residue_ref, skip_ref, *sum_refs) = refs[:-9]
     (grad_key_ref, grad_value_ref, grad_residue_ref, grad_decay_ref, grad_skip_ref) = refs[-9:-4]
     (decay_ref, gain_ref, lead_ref, drive_grad_ref) = refs[-4:]
     length, channels = key_ref.shape
     modes = log_ref.shape[0]
     span = length // SUBS
-    mine = lax.axis_index("seq")
     rate = jnp.exp(log_ref[...])
     norm = jnp.sqrt(2.0 * rate)
     gain = residue_ref[...] * norm
     decay_ref[...] = jnp.exp(-rate)
     gain_ref[...] = gain
-    pair = tree_sum([ref[pl.ds(modes, modes)] for ref in sum_refs])
-    lag_pair = tree_sum([ref[pl.ds(2 * modes, modes)] for ref in sum_refs])
+    pair = tree_sum([ref[pl.ds(2 * modes, modes)] for ref in sum_refs])
+    lag_pair = tree_sum([ref[pl.ds(3 * modes, modes)] for ref in sum_refs])
     grad_residue_ref[...] = norm * pair * scale
     grad_decay_ref[...] = gain * (0.5 * pair - rate * lag_pair) * scale
-    grad_skip_ref[...] = tree_sum([ref[pl.ds(3 * modes, SUBS)] for ref in sum_refs]) * scale
+    grad_skip_ref[...] = tree_sum([ref[pl.ds(4 * modes, SUBS)] for ref in sum_refs]) * scale
     for tile, lanes in lane_tiles(channels):
         rate = jnp.exp(log_ref[:, lanes])
         stretch = jnp.exp(-length * rate)
         power = jnp.exp(-span * rate)
         start = jnp.zeros_like(rate)
-        for offset in range(blocks - 1, 0, -1):
-            after = jnp.where(mine + offset < blocks, sum_refs[offset][pl.ds(0, modes), lanes], 0.0)
-            start = stretch * start + after
+        for distance in range(2 * RING - 1, 0, -1):
+            start = stretch * start + nearby(sum_refs, distance, -1, 0, modes, lanes)
         for j in range(SUBS - 1, -1, -1):
             lead_ref[tile, pl.ds(j * modes, modes)] = start
             start = power * start + sub_ref[tile, pl.ds(j * modes, modes)]
@@ -296,9 +321,8 @@
         grad_value_ref[:, lanes] = (drive_grad * key_ref[:, lanes].astype(F32)).astype(BF16)
 
 
-def call(body, args, outs, scratch, flops, name):
+def call(body, args, outs, scratch, micros, name):
     whole = pl.BlockSpec(memory_space=pltpu.VMEM)
-    moved = sum(a.size * a.dtype.itemsize for a in (*args, *outs))
     return pl.pallas_call(
         body,
         out_shape=[jax.ShapeDtypeStruct(o.shape, o.dtype) for o in outs],
@@ -306,7 +330,7 @@
         out_specs=[whole] * len(outs),
         scratch_shapes=[pltpu.VMEM(shape, F32) for shape in scratch],
         compiler_params=pltpu.CompilerParams(vmem_limit_bytes=32 * 2**20),
-        cost_estimate=pl.CostEstimate(flops=flops, bytes_accessed=moved, transcendentals=0),
+        cost_estimate=pl.CostEstimate(flops=int(micros * 1.15e9), bytes_accessed=0, transcendentals=0),
         name=name,
     )(*args)
 
@@ -315,10 +339,12 @@
     return jax.ShapeDtypeStruct(shape, dtype)
 
 
-def shifted(value, axis, offset, wrap):
-    count = lax.axis_size(axis)
-    pairs = [(i, (i + offset) % count) for i in range(count) if wrap or 0 <= i + offset < count]
-    return lax.ppermute(value, axis, pairs)
+def spread_over_x(value):
+    return [value] + [hop(value, x=offset) for offset in range(1, RING)]
+
+
+def together(*values):
+    return lax.optimization_barrier(values)
 
 
 def local(queries, key_proj, value_proj, skip_gain, residue, log_decay, out_weight, cotangent):
@@ -331,51 +357,84 @@
     wide = like((tiles, length, LANES), F32)
     narrow = like((length, channels), BF16)
     table = (modes, channels)
-    work = length * channels * modes
-
-    cot_rows = gather_cotangent(cotangent).reshape(2 * length, -1)
-
+
+    block = gather_z(cotangent)
     ends, subs, driving = call(
         forward_ends,
         (key_proj, value_proj, log_decay),
         (like((2 * modes, channels), F32), like((tiles, 2 * SUBS * modes, LANES), F32), wide),
         [table, (SUBS, LANES)],
-        4 * work,
+        0.1,
         "forward_ends",
     )
-    earlier = [shifted(ends, "seq", offset, False) for offset in range(1, blocks)]
+    ends_pair = jnp.concatenate([ends, hop(ends, pair=1)])
+    block, ends_pair = together(block, ends_pair)
+    near_blocks = [hop(block, y=1), hop(block, y=-1)]
+    earlier = spread_over_x(ends_pair)
     gated, turned, pre_gate, lead = call(
         forward_full,
         (queries, driving, subs, log_decay, residue, skip_row, *earlier),
         (narrow, narrow, wide, like((tiles, 2 * SUBS * modes, LANES), F32)),
         [table, table],
-        4 * work,
+        0.1,
         "forward_full",
     )
+    turned, *near_blocks = together(turned, *near_blocks)
+    near_first, near_rest, far_first, far_rest = project(turned, out_weight)
+    got_first, got_rest = hop(far_first, core=1), hop(far_rest, core=1)
+    gated_pair = jnp.concatenate([gated, hop(gated, pair=1)])
+    opposite = add(near_first, got_first).astype(BF16)
+    cot_rows, opposite = gather_y(block, near_blocks, opposite)
+    cot_rows, got_rest = together(cot_rows.reshape(2 * length, -1), got_rest)
+
     half = out_weight.shape[1] // 2
     low_weight = lax.dynamic_slice(out_weight, (0, places()[3] * half), (channels, half))
-    grad_parts = lax.dot_general(
-        cot_rows, low_weight, (((1,), (1,)), ((), ())), preferred_element_type=F32
-    )
-    grad_gated = add(grad_parts[:length], hop(grad_parts[length:].astype(BF16), pair=1))
-    grad_weight = weigh(jnp.concatenate([gated, hop(gated, pair=1)]), cot_rows, scale)
-    mixed = mix(turned, out_weight)
+    weights = {2: weigh(gated_pair, cot_rows, scale, 2)}
+    cot_rows, weights[2] = together(cot_rows, weights[2])
+    grad_parts = lax.dot_general(cot_rows, low_weight, (((1,), (1,)), ((), ())), preferred_element_type=F32)
+    cot_rows, grad_parts = together(cot_rows, grad_parts)
+    theirs = hop(grad_parts[length:].astype(BF16), pair=1)
+    part = opposite.shape[0] // 2
+    low_sum, high_sum = hop(opposite[:part], y=1), hop(opposite[part:], y=-1)
+    up_low, up_high, down_low, down_high, own_low, own_high = (
+        add(near_rest[i * part : (i + 1) * part], got_rest[i * part : (i + 1) * part]) for i in range(6)
+    )
+    up_low = add(up_low, low_sum).astype(BF16)
+    down_high = add(down_high, high_sum).astype(BF16)
+    for r in (1, 3, 0):
+        weights[r] = weigh(gated_pair, cot_rows, scale, r)
+    cut = channels // 2
+    upper, lower = hop(weights[2][:cut], x=1), hop(weights[2][cut:], x=-1)
+    weights_up = jnp.concatenate([add(weights[1][:cut], upper).astype(BF16), weights[1][cut:]])
+    weights_down = jnp.concatenate([weights[3][:cut], add(weights[3][cut:], lower).astype(BF16)])
+    theirs, up_low, down_high, weights_up, weights_down, own_weights = together(
+        theirs, up_low, down_high, weights_up, weights_down, weights[0]
+    )
+    grad_weight = add(own_weights, hop(weights_up, x=1), hop(weights_down, x=-1)).astype(BF16)
+    grad_gated = add(grad_parts[:length], theirs)
+    other_high = add(own_high, hop(up_high.astype(BF16), y=1), hop(down_high, y=-1)).astype(BF16)
+    width = other_high.shape[1] // 2
+    crossed = [hop(hop(other_high[:, :width], z=1), z=1), hop(hop(other_high[:, width:], z=-1), z=-1)]
+    mixed = add(own_low, hop(up_low, y=1), hop(down_low.astype(BF16), y=-1), jnp.concatenate(crossed, axis=1)).astype(BF16)
 
     grad_query, back, sums, back_subs = call(
         backward_ends,
         (grad_gated, queries, pre_gate, driving, lead, log_decay),
         (narrow, wide, like((3 * modes + SUBS, channels), F32), like((tiles, SUBS * modes, LANES), F32)),
         [table, (tiles, 2 * SUBS * modes, LANES), (SUBS, LANES)],
-        10 * work,
+        0.1,
         "backward_ends",
     )
-    all_sums = [sums] + [shifted(sums, "seq", -offset, True) for offset in range(1, blocks)]
+    others = hop(sums, pair=1)
+    all_sums = spread_over_x(
+        jnp.concatenate([sums[:modes], others[:modes], sums[modes:] + others[modes:]])
+    )
     grad_key, grad_value, grad_residue, grad_decay, grad_skip = call(
-        functools.partial(backward_full, blocks=blocks, scale=scale),
+        functools.partial(backward_full, scale=scale),
         (key_proj, value_proj, back, back_subs, log_decay, residue, skip_row, *all_sums),
         (narrow, narrow, like(table, F32), like(table, F32), like((SUBS, channels), F32)),
         [table, table, (tiles, SUBS * modes, LANES), (tiles, length, LANES)],
-        4 * work,
+        0.1,
         "backward_full",
     )
     return (

time: 186 us -> 181 us (0.973)
  matrix products: 30.3 us -> 10.9 us
  starting transfers between devices: 65.5 us -> 50.6 us
  waiting for transfers between devices: 47.4 us -> 60.6 us
  local copies, waits for them, and re-layouts: 11.5 us -> 19.1 us
  Pallas kernels: 23.3 us -> 30.1 us
  other arithmetic: 5.72 us -> 8.19 us
    ppermute x14 -> x0, starting transfers between devices: 30.7 us -> none  [shifted(): return lax.ppermute(value, axis, pairs)]
    ppermute x24 -> x38, starting transfers between devices: 34.9 us -> 50.6 us  [hop(): return lax.ppermute(value, ('chan', 'seq'), moves)]
    dot_general x2 -> x0, matrix products: 15 us -> none  [the longest x1 7.92 us: mix(): jnp.dot(turned[half:], out_weight, preferred_element_type=F32).astype(BF16)]
    ppermute x24 -> x38, waiting for transfers between devices: 47.4 us -> 60.6 us  [hop(): return lax.ppermute(value, ('chan', 'seq'), moves)]
    pallas_call x0 -> x1, Pallas kernels: none -> 6.86 us  [project(): pl.pallas_call(project_tile, grid=(width // tile,), out_shape=[jax.ShapeD...]
    dynamic_update_slice x9 -> x10, local copies, waits for them, and re-layouts: 0.71 us -> 5.67 us  [put(): lax.dynamic_update_slice(whole, part[:, None, :, None], (first, row, 0, a...]
    slice x8 -> x10, local copies, waits for them, and re-layouts: 1.35 us -> 5.02 us  [the longest x2 3.74 us: gather_y(): far_own, far_other = (hop(from_before[:1], y=1), hop(from_after[1:], y=-1))]
    convert_element_type x4 -> x7, other arithmetic: 2.55 us -> 5.55 us  [the longest x1 1.78 us: local(): up_high.astype(BF16)]
  transfers between devices with their start and end apart: 38 -> 38, of which waited for: 8 -> 12; matrix products, arithmetic and copies ran while one was open for 20% -> 16% of each run, Pallas kernels for 13% -> 17%
where the time goes in v2:
time: 181 us
  waiting for transfers between devices  60.6 us (33%)
  starting transfers between devices  50.6 us (28%)
  Pallas kernels  30.1 us (17%)
  local copies, waits for them, and re-layouts  19.1 us (11%)
  matrix products  10.9 us (6%)
  other arithmetic  8.19 us (5%)
    ppermute x38, waiting for transfers between devices, hop(): return lax.ppermute(value, ('chan', 'seq'), moves)  60.6 us
    ppermute x38, starting transfers between devices, hop(): return lax.ppermute(value, ('chan', 'seq'), moves)  50.6 us
    pallas_call x4, Pallas kernels, call(): pl.pallas_call(body, out_shape=[jax.ShapeDtypeStruct(o.shape, o.dtype) fo...  23.2 us
    pallas_call x1, Pallas kernels, project(): pl.pallas_call(project_tile, grid=(width // tile,), out_shape=[jax.ShapeD...  6.86 us
    dot_general x4, matrix products, weigh(): lax.dot_general(gated, columns, (((0,), (0,)), ((), ())), preferred_eleme...  6.33 us
    dynamic_update_slice x10, local copies, waits for them, and re-layouts, put(): lax.dynamic_update_slice(whole, part[:, None, :, None], (first, row, 0, a...  5.67 us
    unnamed x35, local copies, waits for them, and re-layouts  4.56 us
    dot_general x1, matrix products, local(): lax.dot_general(cot_rows, low_weight, (((1,), (1,)), ((), ())), preferred...  4.53 us
  transfers between devices with their start and end apart: 38, of which 12 were waited for; matrix products, arithmetic and copies ran while one was open for 16% of the time, Pallas kernels for 17%

profile of v2, /device:TPU:0, one launch (start us, length us, event | category | flops | bytes accessed | tf_op | source)
XLA Modules:
  0.0 180.7 jit_solution(3525690898888023047)
XLA Ops:
  1.8 2.1 %collective-permute-start.1 = (bf16[32,4096]{1,0:T(8,128)(2,1)S(1)}, bf16[32,4096]{1,0:T(8,128)(2,1)S(1)}, u32[]{:S(2)}, u32[]{:S(2)}) collective-permute-start(bf16[32,4096]{1,0:T(8,128)(2,1)S(1)} %get-tuple-element.100), channel_id=1, source_target_pairs={{0,4},{8,12},{4,16},{12,24},{16,20},{24,28},{20,0},{28,8},{32,36},... | collective-permute-start | bytes 786440 | tf_op jit(solution)/shard_map/ppermute | solution.py:47
  3.9 2.2 %collective-permute-start.2 = (bf16[32,4096]{1,0:T(8,128)(2,1)S(1)}, bf16[32,4096]{1,0:T(8,128)(2,1)S(1)}, u32[]{:S(2)}, u32[]{:S(2)}) collective-permute-start(bf16[32,4096]{1,0:T(8,128)(2,1)S(1)} %get-tuple-element.100), channel_id=1, source_target_pairs={{0,20},{8,28},{4,0},{12,8},{16,4},{24,12},{20,16},{28,24},{32,52},... | collective-permute-start | bytes 786440 | tf_op jit(solution)/shard_map/ppermute | solution.py:47
  8.9 3.6 %forward_ends.1 = (f32[32,512]{1,0:T(8,128)S(1)}, f32[4,256,128]{2,1,0:T(8,128)S(1)}, f32[4,512,128]{2,1,0:T(8,128)S(1)}) custom-call(bf16[512,512]{1,0:T(8,128)(2,1)S(1)} %copy-done, bf16[512,512]{1,0:T(8,128)(2,1)S(1)} %copy-done.2, f32[16,512]{1,0:T(8,128)S(1)} %copy-done.5), custom_call_target="tpu_custom_call" | custom-call | flops 115000000 | tf_op jit(solution)/shard_map/forward_ends/pallas_call | solution.py:326
  12.6 3.4 %collective-permute-start = (bf16[32,4096]{1,0:T(8,128)(2,1)S(1)}, bf16[32,4096]{1,0:T(8,128)(2,1)}, u32[]{:S(2)}, u32[]{:S(2)}) collective-permute-start(bf16[32,4096]{1,0:T(8,128)(2,1)S(1)} %get-tuple-element.99), channel_id=1, source_target_pairs={{0,16},{8,24},{4,20},{12,28},{16,0},{24,8},{20,4},{28,12},{32,48},... | collective-permute-start | bytes 786440 | tf_op jit(solution)/shard_map/ppermute | solution.py:47
  16.0 1.6 collective-permute-done.3
  17.8 5.2 %collective-permute-done = bf16[32,4096]{1,0:T(8,128)(2,1)} collective-permute-done((bf16[32,4096]{1,0:T(8,128)(2,1)S(1)}, bf16[32,4096]{1,0:T(8,128)(2,1)}, u32[]{:S(2)}, u32[]{:S(2)}) %collective-permute-start) | collective-permute-done | bytes 262176 | tf_op jit(solution)/shard_map/ppermute | solution.py:47
  23.0 1.1 maximum_select_fusion
  25.2 1.5 collective-permute-start.4
  26.7 2.7 %collective-permute-start.5 = (f32[64,512]{1,0:T(8,128)S(1)}, f32[64,512]{1,0:T(8,128)S(1)}, u32[]{:S(2)}, u32[]{:S(2)}) collective-permute-start(f32[64,512]{1,0:T(8,128)S(1)} %pad_maximum_fusion.4.refs_6_), channel_id=1, source_target_pairs={{0,2},{8,10},{4,6},{12,14},{16,18},{24,26},{20,22},{28,30},{32,34}... | collective-permute-start | bytes 393224 | tf_op jit(solution)/shard_map/ppermute | solution.py:47
  29.4 1.4 collective-permute-start.6
  30.9 1.6 collective-permute-start.7
  32.5 3.0 %collective-permute-start.8 = (bf16[2,2,32,4096]{3,2,1,0:T(8,128)(2,1)}, bf16[2,2,32,4096]{3,2,1,0:T(8,128)(2,1)}, u32[]{:S(2)}, u32[]{:S(2)}) collective-permute-start(bf16[2,2,32,4096]{3,2,1,0:T(8,128)(2,1)} %pad_maximum_fusion), channel_id=1, source_target_pairs={{0,96},{8,104},{4,100},{12,108},{16,112},{24,120},{20,116},{28,124... | collective-permute-start | bytes 3145736 | tf_op jit(solution)/shard_map/ppermute | solution.py:47
  35.6 4.1 %forward_full.1 = (bf16[512,512]{1,0:T(8,128)(2,1)S(1)}, bf16[512,512]{1,0:T(8,128)(2,1)S(1)}, f32[4,512,128]{2,1,0:T(8,128)S(1)}, f32[4,256,128]{2,1,0:T(8,128)S(1)}) custom-call(bf16[512,512]{1,0:T(8,128)(2,1)S(1)} %copy-done.4, f32[4,512,128]{2,1,0:T(8,128)S(1)} %get-tuple-element.48.refs_1_.drive_ref, f32[4,256,128]{2,1,0:T(8,128)S(1)} %get-tuple-element.49.refs_2_, ...), custom_call_target="tpu_custom_call" | custom-call | flops 115000000 | tf_op jit(solution)/shard_map/forward_full/pallas_call | solution.py:326
  41.9 10.4 %collective-permute-done.18 = bf16[512,512]{1,0:T(8,128)(2,1)} collective-permute-done((bf16[512,512]{1,0:T(8,128)(2,1)S(1)}, bf16[512,512]{1,0:T(8,128)(2,1)}, u32[]{:S(2)}, u32[]{:S(2)}) %collective-permute-start.18) | collective-permute-done | bytes 524320 | tf_op jit(solution)/shard_map/ppermute | solution.py:47
  53.4 4.6 %collective-permute-done.7 = bf16[2,2,32,4096]{3,2,1,0:T(8,128)(2,1)} collective-permute-done((bf16[2,2,32,4096]{3,2,1,0:T(8,128)(2,1)}, bf16[2,2,32,4096]{3,2,1,0:T(8,128)(2,1)}, u32[]{:S(2)}, u32[]{:S(2)}) %collective-permute-start.7) | collective-permute-done | bytes 1048608 | tf_op jit(solution)/shard_map/ppermute | solution.py:47
  58.0 1.9 %slice.95 = bf16[1,2,32,4096]{3,2,1,0:T(8,128)(2,1)} slice(bf16[2,2,32,4096]{3,2,1,0:T(8,128)(2,1)} %collective-permute-done.7), slice={[0:1], [0:2], [0:32], [0:4096]} | slice | bytes 1048576 | tf_op jit(solution)/shard_map/slice | solution.py:74
  60.4 1.9 %slice.96 = bf16[1,2,32,4096]{3,2,1,0:T(8,128)(2,1)} slice(bf16[2,2,32,4096]{3,2,1,0:T(8,128)(2,1)} %collective-permute-done.8), slice={[1:2], [0:2], [0:32], [0:4096]} | slice | bytes 1048576 | tf_op jit(solution)/shard_map/slice | solution.py:74
  62.3 1.6 collective-permute-start.12
  63.9 1.7 collective-permute-start.13
  65.5 6.9 %project.1 = (bf16[64,8192]{1,0:T(8,128)(2,1)S(1)}, bf16[192,8192]{1,0:T(8,128)(2,1)S(1)}, bf16[64,8192]{1,0:T(8,128)(2,1)S(1)}, bf16[192,8192]{1,0:T(8,128)(2,1)S(1)}) custom-call(bf16[512,512]{1,0:T(8,128)(2,1)S(1)} %get-tuple-element.54.rows_ref, bf16[512,8192]{1,0:T(8,128)(2,1)S(1)} %bitcast.55), custom_call_target="tpu_custom_call" | custom-call | flops 4294967296 | bytes 16777216 | tf_op jit(solution)/shard_map/project/pallas_call | solution.py:101
  72.5 1.3 bitcast_dynamic-update-slice_fusion.4
  73.9 1.3 bitcast_dynamic-update-slice_fusion.3
  76.1 1.6 collective-permute-done.12
  79.2 2.9 %collective-permute-start.21 = (bf16[32,8192]{1,0:T(8,128)(2,1)}, bf16[32,8192]{1,0:T(8,128)(2,1)}, u32[]{:S(2)}, u32[]{:S(2)}) collective-permute-start(bf16[32,8192]{1,0:T(8,128)(2,1)} %get-tuple-element.95), channel_id=1, source_target_pairs={{0,96},{8,104},{4,100},{12,108},{16,112},{24,120},{20,116},{28,124... | collective-permute-start | bytes 1572872 | tf_op jit(solution)/shard_map/ppermute | solution.py:47
  82.2 1.4 bitcast_dynamic-update-slice_fusion.1
  85.3 1.6 copy-done.10
  86.9 1.3 multiply_convert_fusion.3
  88.2 4.5 %fusion = f32[1024,512]{1,0:T(8,128)S(1)} fusion(bf16[1024,4096]{1,0:T(8,128)(2,1)S(1)} %bitcast.57, bf16[512,8192]{1,0:T(8,128)(2,1)S(1)} %bitcast.55, s32[]{:T(128)S(6)} %select_n.104), kind=kOutput, calls=%fused_computation | convolution fusion | flops 4294967296 | bytes 14680068 | tf_op jit(solution)/shard_map/dot_general | solution.py:394
  94.4 2.6 %collective-permute-start.23 = (bf16[256,1024]{1,0:T(8,128)(2,1)S(1)}, bf16[256,1024]{1,0:T(8,128)(2,1)S(1)}, u32[]{:S(2)}, u32[]{:S(2)}) collective-permute-start(bf16[256,1024]{1,0:T(8,128)(2,1)S(1)} %get-tuple-element.93), channel_id=1, source_target_pairs={{0,3},{8,11},{4,7},{12,15},{16,19},{24,27},{20,23},{28,31},{32,35}... | collective-permute-start | bytes 1572872 | tf_op jit(solution)/shard_map/ppermute | solution.py:47
  97.1 2.5 %multiply_convert_fusion.2 = bf16[512,1024]{1,0:T(8,128)(2,1)S(1)} fusion(bf16[1024,512]{1,0:T(8,128)(2,1)} %copy-done.12, bf16[1024,4096]{1,0:T(8,128)(2,1)S(1)} %bitcast.58, s32[]{:T(128)S(6)} %select_n.119), kind=kOutput, calls=%fused_computation.9 | convolution fusion | flops 1074790400 | bytes 4194308 | tf_op jit(solution)/shard_map/dot_general | solution.py:119
  99.6 1.8 add_convert_fusion.4
  101.4 1.3 multiply_convert_fusion.1
  102.7 1.3 multiply_convert_fusion
  104.5 3.8 %collective-permute-done.22 = bf16[256,1024]{1,0:T(8,128)(2,1)S(1)} collective-permute-done((bf16[256,1024]{1,0:T(8,128)(2,1)S(1)}, bf16[256,1024]{1,0:T(8,128)(2,1)S(1)}, u32[]{:S(2)}, u32[]{:S(2)}) %collective-permute-start.22) | collective-permute-done | bytes 524320 | tf_op jit(solution)/shard_map/ppermute | solution.py:47
  108.9 3.2 %collective-permute-start.27 = (bf16[32,8192]{1,0:T(8,128)(2,1)S(1)}, bf16[32,8192]{1,0:T(8,128)(2,1)S(1)}, u32[]{:S(2)}, u32[]{:S(2)}) collective-permute-start(bf16[32,8192]{1,0:T(8,128)(2,1)S(1)} %get-tuple-element.72), channel_id=1, source_target_pairs={{0,96},{8,104},{4,100},{12,108},{16,112},{24,120},{20,116},{28,124... | collective-permute-start | bytes 1572872 | tf_op jit(solution)/shard_map/ppermute | solution.py:47
  112.3 10.5 %backward_ends.1 = (bf16[512,512]{1,0:T(8,128)(2,1)}, f32[4,512,128]{2,1,0:T(8,128)S(1)}, f32[56,512]{1,0:T(8,128)S(1)}, f32[4,128,128]{2,1,0:T(8,128)S(1)}) custom-call(f32[512,512]{1,0:T(8,128)S(1)} %convert_add_fusion.grad_ref, bf16[512,512]{1,0:T(8,128)(2,1)S(1)} %copy-done.4, f32[4,512,128]{2,1,0:T(8,128)S(1)} %get-tuple-element.74.pre_ref, ...), custom_call_target="tpu_custom_call" | custom-call | flops 115000000 | tf_op jit(solution)/shard_map/backward_ends/pallas_call | solution.py:326
  122.8 1.2 collective-permute-start.32
  124.0 2.7 %collective-permute-start.37 = (bf16[512,1024]{1,0:T(8,128)(2,1)S(1)}, bf16[512,1024]{1,0:T(8,128)(2,1)S(1)}, u32[]{:S(2)}, u32[]{:S(2)}) collective-permute-start(bf16[512,1024]{1,0:T(8,128)(2,1)S(1)} %pad_maximum_fusion.2), channel_id=1, source_target_pairs={{0,3},{8,11},{4,7},{12,15},{16,19},{24,27},{20,23},{28,31},{32,35}... | collective-permute-start | bytes 3145736 | tf_op jit(solution)/shard_map/ppermute | solution.py:47
  128.2 1.7 collective-permute-start.30
  129.8 4.1 %collective-permute-start.34 = (f32[72,512]{1,0:T(8,128)S(1)}, f32[72,512]{1,0:T(8,128)S(1)}, u32[]{:S(2)}, u32[]{:S(2)}) collective-permute-start(f32[72,512]{1,0:T(8,128)S(1)} %pad_maximum_fusion.3.refs_7_), channel_id=1, source_target_pairs={{0,2},{8,10},{4,6},{12,14},{16,18},{24,26},{20,22},{28,30},{32,34}... | collective-permute-start | bytes 442376 | tf_op jit(solution)/shard_map/ppermute | solution.py:47
  134.0 22.5 %collective-permute-done.33.refs_8_ = f32[72,512]{1,0:T(8,128)S(1)} collective-permute-done((f32[72,512]{1,0:T(8,128)S(1)}, f32[72,512]{1,0:T(8,128)S(1)}, u32[]{:S(2)}, u32[]{:S(2)}) %collective-permute-start.33) | collective-permute-done | bytes 147488 | tf_op jit(solution)/shard_map/ppermute | solution.py:47
  157.2 4.3 %collective-permute-done.35.refs_10_ = f32[72,512]{1,0:T(8,128)S(1)} collective-permute-done((f32[72,512]{1,0:T(8,128)S(1)}, f32[72,512]{1,0:T(8,128)S(1)}, u32[]{:S(2)}, u32[]{:S(2)}) %collective-permute-start.35) | collective-permute-done | bytes 147488 | tf_op jit(solution)/shard_map/ppermute | solution.py:47
  161.6 3.2 %collective-permute-start.25 = (bf16[32,8192]{1,0:T(8,128)(2,1)S(1)}, bf16[32,8192]{1,0:T(8,128)(2,1)S(1)}, u32[]{:S(2)}, u32[]{:S(2)}) collective-permute-start(bf16[32,8192]{1,0:T(8,128)(2,1)S(1)} %get-tuple-element.89), channel_id=1, source_target_pairs={{0,96},{8,104},{4,100},{12,108},{16,112},{24,120},{20,116},{28,124... | collective-permute-start | bytes 1572872 | tf_op jit(solution)/shard_map/ppermute | solution.py:47
  164.8 5.1 %backward_full.1 = (bf16[512,512]{1,0:T(8,128)(2,1)}, bf16[512,512]{1,0:T(8,128)(2,1)}, f32[16,512]{1,0:T(8,128)}, f32[16,512]{1,0:T(8,128)}, f32[8,512]{1,0:T(8,128)S(1)}) custom-call(bf16[512,512]{1,0:T(8,128)(2,1)S(1)} %copy-done.1, bf16[512,512]{1,0:T(8,128)(2,1)S(1)} %copy-done.3, f32[4,512,128]{2,1,0:T(8,128)S(1)} %get-tuple-element.77.refs_2_, ...), custom_call_target="tpu_custom_call" | custom-call | flops 115000000 | tf_op jit(solution)/shard_map/backward_full/pallas_call | solution.py:326
  170.4 1.6 collective-permute-start.31
  172.5 1.6 add_convert_fusion
  174.1 2.7 %collective-permute-done.31 = bf16[32,4096]{1,0:T(8,128)(2,1)S(1)} collective-permute-done((bf16[32,4096]{1,0:T(8,128)(2,1)S(1)}, bf16[32,4096]{1,0:T(8,128)(2,1)S(1)}, u32[]{:S(2)}, u32[]{:S(2)}) %collective-permute-start.31) | collective-permute-done | bytes 262176 | tf_op jit(solution)/shard_map/ppermute | solution.py:47
  176.8 2.8 %collective-permute-done.29 = bf16[32,4096]{1,0:T(8,128)(2,1)S(1)} collective-permute-done((bf16[32,4096]{1,0:T(8,128)(2,1)S(1)}, bf16[32,4096]{1,0:T(8,128)(2,1)S(1)}, u32[]{:S(2)}, u32[]{:S(2)}) %collective-permute-start.29) | collective-permute-done | bytes 262176 | tf_op jit(solution)/shard_map/ppermute | solution.py:47
  (115 shorter events, 20.6 us)
Async XLA Ops:
  0.6 34.9 %copy-start.6 = (f32[16,512]{1,0:T(8,128)S(1)}, f32[16,512]{1,0:T(8,128)}, u32[]{:S(2)}) copy-start(f32[16,512]{1,0:T(8,128)} %refs_4_.3) | copy-start | bytes 98308
  0.6 34.9 %copy-start.4 = (bf16[512,512]{1,0:T(8,128)(2,1)S(1)}, bf16[512,512]{1,0:T(8,128)(2,1)}, u32[]{:S(2)}) copy-start(bf16[512,512]{1,0:T(8,128)(2,1)} %query_ref.1) | copy-start | bytes 1572868
  0.7 34.9 %copy-start.7 = (f32[16,512]{1,0:T(8,128)S(1)}, f32[16,512]{1,0:T(8,128)}, u32[]{:S(2)}) copy-start(f32[16,512]{1,0:T(8,128)} %refs_5_.1) | copy-start | bytes 98308
  0.7 34.9 %copy-start.8 = (f32[512]{0:T(512)S(1)}, f32[512]{0:T(512)}, u32[]{:S(2)}) copy-start(f32[512]{0:T(512)} %param.11) | copy-start | bytes 6148
  1.8 15.8 %collective-permute-start.1 = (bf16[32,4096]{1,0:T(8,128)(2,1)S(1)}, bf16[32,4096]{1,0:T(8,128)(2,1)S(1)}, u32[]{:S(2)}, u32[]{:S(2)}) collective-permute-start(bf16[32,4096]{1,0:T(8,128)(2,1)S(1)} %get-tuple-element.100), channel_id=1, source_target_pairs={{0,4},{8,12},{4,16},{12,24},{16,20},{24,28},{20,0},{28,8},{32,36},... | collective-permute-start | bytes 786440 | tf_op jit(solution)/shard_map/ppermute | solution.py:47
  3.9 13.8 %collective-permute-start.2 = (bf16[32,4096]{1,0:T(8,128)(2,1)S(1)}, bf16[32,4096]{1,0:T(8,128)(2,1)S(1)}, u32[]{:S(2)}, u32[]{:S(2)}) collective-permute-start(bf16[32,4096]{1,0:T(8,128)(2,1)S(1)} %get-tuple-element.100), channel_id=1, source_target_pairs={{0,20},{8,28},{4,0},{12,8},{16,4},{24,12},{20,16},{28,24},{32,52},... | collective-permute-start | bytes 786440 | tf_op jit(solution)/shard_map/ppermute | solution.py:47
  12.5 5.1 %collective-permute-start.3 = (f32[32,512]{1,0:T(8,128)S(1)}, f32[32,512]{1,0:T(8,128)S(1)}, u32[]{:S(2)}, u32[]{:S(2)}) collective-permute-start(f32[32,512]{1,0:T(8,128)S(1)} %get-tuple-element.50), channel_id=1, source_target_pairs={{0,4},{8,12},{4,0},{12,8},{16,20},{24,28},{20,16},{28,24},{32,36},... | collective-permute-start | bytes 196616 | tf_op jit(solution)/shard_map/ppermute | solution.py:47
  12.6 10.4 %collective-permute-start = (bf16[32,4096]{1,0:T(8,128)(2,1)S(1)}, bf16[32,4096]{1,0:T(8,128)(2,1)}, u32[]{:S(2)}, u32[]{:S(2)}) collective-permute-start(bf16[32,4096]{1,0:T(8,128)(2,1)S(1)} %get-tuple-element.99), channel_id=1, source_target_pairs={{0,16},{8,24},{4,20},{12,28},{16,0},{24,8},{20,4},{28,12},{32,48},... | collective-permute-start | bytes 786440 | tf_op jit(solution)/shard_map/ppermute | solution.py:47
  25.2 7.4 %collective-permute-start.4 = (f32[64,512]{1,0:T(8,128)S(1)}, f32[64,512]{1,0:T(8,128)S(1)}, u32[]{:S(2)}, u32[]{:S(2)}) collective-permute-start(f32[64,512]{1,0:T(8,128)S(1)} %pad_maximum_fusion.4.refs_6_), channel_id=1, source_target_pairs={{0,1},{8,9},{4,5},{12,13},{16,17},{24,25},{20,21},{28,29},{32,33},... | collective-permute-start | bytes 393224 | tf_op jit(solution)/shard_map/ppermute | solution.py:47
  26.7 8.9 %collective-permute-start.5 = (f32[64,512]{1,0:T(8,128)S(1)}, f32[64,512]{1,0:T(8,128)S(1)}, u32[]{:S(2)}, u32[]{:S(2)}) collective-permute-start(f32[64,512]{1,0:T(8,128)S(1)} %pad_maximum_fusion.4.refs_6_), channel_id=1, source_target_pairs={{0,2},{8,10},{4,6},{12,14},{16,18},{24,26},{20,22},{28,30},{32,34}... | collective-permute-start | bytes 393224 | tf_op jit(solution)/shard_map/ppermute | solution.py:47
  29.4 6.1 %collective-permute-start.6 = (f32[64,512]{1,0:T(8,128)S(1)}, f32[64,512]{1,0:T(8,128)S(1)}, u32[]{:S(2)}, u32[]{:S(2)}) collective-permute-start(f32[64,512]{1,0:T(8,128)S(1)} %pad_maximum_fusion.4.refs_6_), channel_id=1, source_target_pairs={{0,3},{8,11},{4,7},{12,15},{16,19},{24,27},{20,23},{28,31},{32,35}... | collective-permute-start | bytes 393224 | tf_op jit(solution)/shard_map/ppermute | solution.py:47
  30.8 41.6 %collective-permute-start.9 = (bf16[2,2,32,4096]{3,2,1,0:T(8,128)(2,1)}, bf16[2,2,32,4096]{3,2,1,0:T(8,128)(2,1)}, u32[]{:S(2)}, u32[]{:S(2)}) collective-permute-start(bf16[2,2,32,4096]{3,2,1,0:T(8,128)(2,1)} %pad_maximum_fusion), channel_id=1, source_target_pairs={{0,8},{8,0},{4,12},{12,4},{16,24},{24,16},{20,28},{28,20},{32,40},... | collective-permute-start | bytes 3145736 | tf_op jit(solution)/shard_map/ppermute | solution.py:47
  30.9 27.2 %collective-permute-start.7 = (bf16[2,2,32,4096]{3,2,1,0:T(8,128)(2,1)}, bf16[2,2,32,4096]{3,2,1,0:T(8,128)(2,1)}, u32[]{:S(2)}, u32[]{:S(2)}) collective-permute-start(bf16[2,2,32,4096]{3,2,1,0:T(8,128)(2,1)} %pad_maximum_fusion), channel_id=1, source_target_pairs={{0,32},{8,40},{4,36},{12,44},{16,48},{24,56},{20,52},{28,60},{32,6... | collective-permute-start | bytes 3145736 | tf_op jit(solution)/shard_map/ppermute | solution.py:47
  32.5 25.5 %collective-permute-start.8 = (bf16[2,2,32,4096]{3,2,1,0:T(8,128)(2,1)}, bf16[2,2,32,4096]{3,2,1,0:T(8,128)(2,1)}, u32[]{:S(2)}, u32[]{:S(2)}) collective-permute-start(bf16[2,2,32,4096]{3,2,1,0:T(8,128)(2,1)} %pad_maximum_fusion), channel_id=1, source_target_pairs={{0,96},{8,104},{4,100},{12,108},{16,112},{24,120},{20,116},{28,124... | collective-permute-start | bytes 3145736 | tf_op jit(solution)/shard_map/ppermute | solution.py:47
  35.6 29.9 %slice-start = ((s8[8388608]{0:T(1024)(128)(4,1)}), s8[4194304]{0:T(1024)(128)(4,1)S(1)}, s32[]{:S(2)}) async-start(s8[8388608]{0:T(1024)(128)(4,1)} %bitcast.54), calls=%async_computation | async-start | bytes 8388608
  39.7 25.8 %slice-start.1 = ((s8[8388608]{0:T(1024)(128)(4,1)}), s8[4194304]{0:T(1024)(128)(4,1)S(1)}, s32[]{:S(2)}) async-start(s8[8388608]{0:T(1024)(128)(4,1)} %bitcast.54), calls=%async_computation.1 | async-start | bytes 8388608
  39.7 12.6 %collective-permute-start.18 = (bf16[512,512]{1,0:T(8,128)(2,1)S(1)}, bf16[512,512]{1,0:T(8,128)(2,1)}, u32[]{:S(2)}, u32[]{:S(2)}) collective-permute-start(bf16[512,512]{1,0:T(8,128)(2,1)S(1)} %get-tuple-element.65), channel_id=1, source_target_pairs={{0,4},{8,12},{4,0},{12,8},{16,20},{24,28},{20,16},{28,24},{32,36},... | collective-permute-start | bytes 1572872 | tf_op jit(solution)/shard_map/ppermute | solution.py:47
  53.4 10.5 %copy-start.12 = (bf16[1024,512]{1,0:T(8,128)(2,1)}, bf16[1024,512]{1,0:T(8,128)(2,1)S(1)}, u32[]{:S(2)}) copy-start(bf16[1024,512]{1,0:T(8,128)(2,1)S(1)} %constant_dynamic-update-slice_fusion) | copy-start | bytes 3145732
  58.0 21.2 %collective-permute-start.10 = (bf16[2,2,32,4096]{3,2,1,0:T(8,128)(2,1)}, bf16[2,2,32,4096]{3,2,1,0:T(8,128)(2,1)S(1)}, u32[]{:S(2)}, u32[]{:S(2)}) collective-permute-start(bf16[2,2,32,4096]{3,2,1,0:T(8,128)(2,1)} %collective-permute-done.7), channel_id=1, source_target_pairs={{0,8},{8,0},{4,12},{12,4},{16,24},{24,16},{20,28},{28,20},{32,40},... | collective-permute-start | bytes 3145736 | tf_op jit(solution)/shard_map/ppermute | solution.py:47
  59.9 23.7 %collective-permute-start.11 = (bf16[2,2,32,4096]{3,2,1,0:T(8,128)(2,1)}, bf16[2,2,32,4096]{3,2,1,0:T(8,128)(2,1)S(1)}, u32[]{:S(2)}, u32[]{:S(2)}) collective-permute-start(bf16[2,2,32,4096]{3,2,1,0:T(8,128)(2,1)} %collective-permute-done.8), channel_id=1, source_target_pairs={{0,8},{8,0},{4,12},{12,4},{16,24},{24,16},{20,28},{28,20},{32,40},... | collective-permute-start | bytes 3145736 | tf_op jit(solution)/shard_map/ppermute | solution.py:47
  62.3 15.4 %collective-permute-start.12 = (bf16[1,2,32,4096]{3,2,1,0:T(8,128)(2,1)}, bf16[1,2,32,4096]{3,2,1,0:T(8,128)(2,1)}, u32[]{:S(2)}, u32[]{:S(2)}) collective-permute-start(bf16[1,2,32,4096]{3,2,1,0:T(8,128)(2,1)} %slice.95), channel_id=1, source_target_pairs={{0,32},{8,40},{4,36},{12,44},{16,48},{24,56},{20,52},{28,60},{32,6... | collective-permute-start | bytes 1572872 | tf_op jit(solution)/shard_map/ppermute | solution.py:47
  63.9 13.8 %collective-permute-start.13 = (bf16[1,2,32,4096]{3,2,1,0:T(8,128)(2,1)}, bf16[1,2,32,4096]{3,2,1,0:T(8,128)(2,1)S(1)}, u32[]{:S(2)}, u32[]{:S(2)}) collective-permute-start(bf16[1,2,32,4096]{3,2,1,0:T(8,128)(2,1)} %slice.96), channel_id=1, source_target_pairs={{0,96},{8,104},{4,100},{12,108},{16,112},{24,120},{20,116},{28,124... | collective-permute-start | bytes 1572872 | tf_op jit(solution)/shard_map/ppermute | solution.py:47
  72.4 2.8 %collective-permute-start.14 = (bf16[64,8192]{1,0:T(8,128)(2,1)S(1)}, bf16[64,8192]{1,0:T(8,128)(2,1)S(1)}, u32[]{:S(2)}, u32[]{:S(2)}) collective-permute-start(bf16[64,8192]{1,0:T(8,128)(2,1)S(1)} %get-tuple-element.59), channel_id=1, source_target_pairs={{0,8},{8,0},{4,12},{12,4},{16,24},{24,16},{20,28},{28,20},{32,40},... | collective-permute-start | bytes 3145736 | tf_op jit(solution)/shard_map/ppermute | solution.py:47
  75.2 10.1 %collective-permute-start.17 = (bf16[192,8192]{1,0:T(8,128)(2,1)S(1)}, bf16[192,8192]{1,0:T(8,128)(2,1)S(1)}, u32[]{:S(2)}, u32[]{:S(2)}) collective-permute-start(bf16[192,8192]{1,0:T(8,128)(2,1)S(1)} %get-tuple-element.62), channel_id=1, source_target_pairs={{0,8},{8,0},{4,12},{12,4},{16,24},{24,16},{20,28},{28,20},{32,40},... | collective-permute-start | bytes 9437192 | tf_op jit(solution)/shard_map/ppermute | solution.py:47
  77.6 7.5 %collective-permute-start.15 = (bf16[1,2,32,4096]{3,2,1,0:T(8,128)(2,1)}, bf16[1,2,32,4096]{3,2,1,0:T(8,128)(2,1)S(1)}, u32[]{:S(2)}, u32[]{:S(2)}) collective-permute-start(bf16[1,2,32,4096]{3,2,1,0:T(8,128)(2,1)} %collective-permute-done.12), channel_id=1, source_target_pairs={{0,8},{8,0},{4,12},{12,4},{16,24},{24,16},{20,28},{28,20},{32,40},... | collective-permute-start | bytes 1572872 | tf_op jit(solution)/shard_map/ppermute | solution.py:47
  77.7 7.6 %collective-permute-start.16 = (bf16[1,2,32,4096]{3,2,1,0:T(8,128)(2,1)S(1)}, bf16[1,2,32,4096]{3,2,1,0:T(8,128)(2,1)S(1)}, u32[]{:S(2)}, u32[]{:S(2)}) collective-permute-start(bf16[1,2,32,4096]{3,2,1,0:T(8,128)(2,1)S(1)} %collective-permute-done.13), channel_id=1, source_target_pairs={{0,8},{8,0},{4,12},{12,4},{16,24},{24,16},{20,28},{28,20},{32,40},... | collective-permute-start | bytes 1572872 | tf_op jit(solution)/shard_map/ppermute | solution.py:47
  79.2 20.4 %collective-permute-start.21 = (bf16[32,8192]{1,0:T(8,128)(2,1)}, bf16[32,8192]{1,0:T(8,128)(2,1)}, u32[]{:S(2)}, u32[]{:S(2)}) collective-permute-start(bf16[32,8192]{1,0:T(8,128)(2,1)} %get-tuple-element.95), channel_id=1, source_target_pairs={{0,96},{8,104},{4,100},{12,108},{16,112},{24,120},{20,116},{28,124... | collective-permute-start | bytes 1572872 | tf_op jit(solution)/shard_map/ppermute | solution.py:47
  83.6 16.0 %collective-permute-start.20 = (bf16[32,8192]{1,0:T(8,128)(2,1)}, bf16[32,8192]{1,0:T(8,128)(2,1)}, u32[]{:S(2)}, u32[]{:S(2)}) collective-permute-start(bf16[32,8192]{1,0:T(8,128)(2,1)} %get-tuple-element.96), channel_id=1, source_target_pairs={{0,32},{8,40},{4,36},{12,44},{16,48},{24,56},{20,52},{28,60},{32,6... | collective-permute-start | bytes 1572872 | tf_op jit(solution)/shard_map/ppermute | solution.py:47
  92.8 6.8 %copy-start.11 = (bf16[192,8192]{1,0:T(8,128)(2,1)S(1)}, bf16[192,8192]{1,0:T(8,128)(2,1)}, u32[]{:S(2)}) copy-start(bf16[192,8192]{1,0:T(8,128)(2,1)} %copy-done.10) | copy-start | bytes 9437188
  92.8 16.1 %collective-permute-start.19 = (bf16[512,512]{1,0:T(8,128)(2,1)S(1)}, bf16[512,512]{1,0:T(8,128)(2,1)S(1)}, u32[]{:S(2)}, u32[]{:S(2)}) collective-permute-start(bf16[512,512]{1,0:T(8,128)(2,1)S(1)} %slice.152), channel_id=1, source_target_pairs={{0,4},{8,12},{4,0},{12,8},{16,20},{24,28},{20,16},{28,24},{32,36},... | collective-permute-start | bytes 1572872 | tf_op jit(solution)/shard_map/ppermute | solution.py:47
  93.8 14.6 %collective-permute-start.22 = (bf16[256,1024]{1,0:T(8,128)(2,1)S(1)}, bf16[256,1024]{1,0:T(8,128)(2,1)S(1)}, u32[]{:S(2)}, u32[]{:S(2)}) collective-permute-start(bf16[256,1024]{1,0:T(8,128)(2,1)S(1)} %get-tuple-element.94), channel_id=1, source_target_pairs={{0,1},{8,9},{4,5},{12,13},{16,17},{24,25},{20,21},{28,29},{32,33},... | collective-permute-start | bytes 1572872 | tf_op jit(solution)/shard_map/ppermute | solution.py:47
  94.4 14.2 %collective-permute-start.23 = (bf16[256,1024]{1,0:T(8,128)(2,1)S(1)}, bf16[256,1024]{1,0:T(8,128)(2,1)S(1)}, u32[]{:S(2)}, u32[]{:S(2)}) collective-permute-start(bf16[256,1024]{1,0:T(8,128)(2,1)S(1)} %get-tuple-element.93), channel_id=1, source_target_pairs={{0,3},{8,11},{4,7},{12,15},{16,19},{24,27},{20,23},{28,31},{32,35}... | collective-permute-start | bytes 1572872 | tf_op jit(solution)/shard_map/ppermute | solution.py:47
  104.1 23.6 %collective-permute-start.26 = (bf16[32,8192]{1,0:T(8,128)(2,1)S(1)}, bf16[32,8192]{1,0:T(8,128)(2,1)S(1)}, u32[]{:S(2)}, u32[]{:S(2)}) collective-permute-start(bf16[32,8192]{1,0:T(8,128)(2,1)S(1)} %get-tuple-element.90), channel_id=1, source_target_pairs={{0,32},{8,40},{4,36},{12,44},{16,48},{24,56},{20,52},{28,60},{32,6... | collective-permute-start | bytes 1572872 | tf_op jit(solution)/shard_map/ppermute | solution.py:47
  108.9 18.8 %collective-permute-start.27 = (bf16[32,8192]{1,0:T(8,128)(2,1)S(1)}, bf16[32,8192]{1,0:T(8,128)(2,1)S(1)}, u32[]{:S(2)}, u32[]{:S(2)}) collective-permute-start(bf16[32,8192]{1,0:T(8,128)(2,1)S(1)} %get-tuple-element.72), channel_id=1, source_target_pairs={{0,96},{8,104},{4,100},{12,108},{16,112},{24,120},{20,116},{28,124... | collective-permute-start | bytes 1572872 | tf_op jit(solution)/shard_map/ppermute | solution.py:47
  112.3 52.5 %copy-start.1 = (bf16[512,512]{1,0:T(8,128)(2,1)S(1)}, bf16[512,512]{1,0:T(8,128)(2,1)}, u32[]{:S(2)}) copy-start(bf16[512,512]{1,0:T(8,128)(2,1)} %refs_0_.3) | copy-start | bytes 1572868
  112.3 52.5 %copy-start.3 = (bf16[512,512]{1,0:T(8,128)(2,1)S(1)}, bf16[512,512]{1,0:T(8,128)(2,1)}, u32[]{:S(2)}) copy-start(bf16[512,512]{1,0:T(8,128)(2,1)} %refs_1_.1) | copy-start | bytes 1572868
  122.8 4.8 %collective-permute-start.32 = (f32[56,512]{1,0:T(8,128)S(1)}, f32[56,512]{1,0:T(8,128)S(1)}, u32[]{:S(2)}, u32[]{:S(2)}) collective-permute-start(f32[56,512]{1,0:T(8,128)S(1)} %get-tuple-element.79), channel_id=1, source_target_pairs={{0,4},{8,12},{4,0},{12,8},{16,20},{24,28},{20,16},{28,24},{32,36},... | collective-permute-start | bytes 344072 | tf_op jit(solution)/shard_map/ppermute | solution.py:47
  124.0 48.0 %collective-permute-start.37 = (bf16[512,1024]{1,0:T(8,128)(2,1)S(1)}, bf16[512,1024]{1,0:T(8,128)(2,1)S(1)}, u32[]{:S(2)}, u32[]{:S(2)}) collective-permute-start(bf16[512,1024]{1,0:T(8,128)(2,1)S(1)} %pad_maximum_fusion.2), channel_id=1, source_target_pairs={{0,3},{8,11},{4,7},{12,15},{16,19},{24,27},{20,23},{28,31},{32,35}... | collective-permute-start | bytes 3145736 | tf_op jit(solution)/shard_map/ppermute | solution.py:47
  126.7 45.8 %collective-permute-start.36 = (bf16[512,1024]{1,0:T(8,128)(2,1)S(1)}, bf16[512,1024]{1,0:T(8,128)(2,1)S(1)}, u32[]{:S(2)}, u32[]{:S(2)}) collective-permute-start(bf16[512,1024]{1,0:T(8,128)(2,1)S(1)} %pad_maximum_fusion.1), channel_id=1, source_target_pairs={{0,1},{8,9},{4,5},{12,13},{16,17},{24,25},{20,21},{28,29},{32,33},... | collective-permute-start | bytes 3145736 | tf_op jit(solution)/shard_map/ppermute | solution.py:47
  127.6 28.8 %collective-permute-start.33 = (f32[72,512]{1,0:T(8,128)S(1)}, f32[72,512]{1,0:T(8,128)S(1)}, u32[]{:S(2)}, u32[]{:S(2)}) collective-permute-start(f32[72,512]{1,0:T(8,128)S(1)} %pad_maximum_fusion.3.refs_7_), channel_id=1, source_target_pairs={{0,1},{8,9},{4,5},{12,13},{16,17},{24,25},{20,21},{28,29},{32,33},... | collective-permute-start | bytes 442376 | tf_op jit(solution)/shard_map/ppermute | solution.py:47
  128.2 33.4 %collective-permute-start.30 = (bf16[32,4096]{1,0:T(8,128)(2,1)S(1)}, bf16[32,4096]{1,0:T(8,128)(2,1)S(1)}, u32[]{:S(2)}, u32[]{:S(2)}) collective-permute-start(bf16[32,4096]{1,0:T(8,128)(2,1)S(1)} %get-tuple-element.98), channel_id=1, source_target_pairs={{0,20},{8,28},{4,0},{12,8},{16,4},{24,12},{20,16},{28,24},{32,52},... | collective-permute-start | bytes 786440 | tf_op jit(solution)/shard_map/ppermute | solution.py:47
  129.8 26.6 %collective-permute-start.34 = (f32[72,512]{1,0:T(8,128)S(1)}, f32[72,512]{1,0:T(8,128)S(1)}, u32[]{:S(2)}, u32[]{:S(2)}) collective-permute-start(f32[72,512]{1,0:T(8,128)S(1)} %pad_maximum_fusion.3.refs_7_), channel_id=1, source_target_pairs={{0,2},{8,10},{4,6},{12,14},{16,18},{24,26},{20,22},{28,30},{32,34}... | collective-permute-start | bytes 442376 | tf_op jit(solution)/shard_map/ppermute | solution.py:47
  156.4 5.1 %collective-permute-start.35 = (f32[72,512]{1,0:T(8,128)S(1)}, f32[72,512]{1,0:T(8,128)S(1)}, u32[]{:S(2)}, u32[]{:S(2)}) collective-permute-start(f32[72,512]{1,0:T(8,128)S(1)} %pad_maximum_fusion.3.refs_7_), channel_id=1, source_target_pairs={{0,3},{8,11},{4,7},{12,15},{16,19},{24,27},{20,23},{28,31},{32,35}... | collective-permute-start | bytes 442376 | tf_op jit(solution)/shard_map/ppermute | solution.py:47
  156.4 14.0 %collective-permute-start.28 = (bf16[32,4096]{1,0:T(8,128)(2,1)S(1)}, bf16[32,4096]{1,0:T(8,128)(2,1)S(1)}, u32[]{:S(2)}, u32[]{:S(2)}) collective-permute-start(bf16[32,4096]{1,0:T(8,128)(2,1)S(1)} %get-tuple-element.97), channel_id=1, source_target_pairs={{0,4},{8,12},{4,16},{12,24},{16,20},{24,28},{20,0},{28,8},{32,36},... | collective-permute-start | bytes 786440 | tf_op jit(solution)/shard_map/ppermute | solution.py:47
  161.5 12.5 %collective-permute-start.24 = (bf16[32,8192]{1,0:T(8,128)(2,1)S(1)}, bf16[32,8192]{1,0:T(8,128)(2,1)S(1)}, u32[]{:S(2)}, u32[]{:S(2)}) collective-permute-start(bf16[32,8192]{1,0:T(8,128)(2,1)S(1)} %get-tuple-element.71), channel_id=1, source_target_pairs={{0,32},{8,40},{4,36},{12,44},{16,48},{24,56},{20,52},{28,60},{32,6... | collective-permute-start | bytes 1572872 | tf_op jit(solution)/shard_map/ppermute | solution.py:47
  161.6 12.5 %collective-permute-start.25 = (bf16[32,8192]{1,0:T(8,128)(2,1)S(1)}, bf16[32,8192]{1,0:T(8,128)(2,1)S(1)}, u32[]{:S(2)}, u32[]{:S(2)}) collective-permute-start(bf16[32,8192]{1,0:T(8,128)(2,1)S(1)} %get-tuple-element.89), channel_id=1, source_target_pairs={{0,96},{8,104},{4,100},{12,108},{16,112},{24,120},{20,116},{28,124... | collective-permute-start | bytes 1572872 | tf_op jit(solution)/shard_map/ppermute | solution.py:47
  170.4 6.4 %collective-permute-start.31 = (bf16[32,4096]{1,0:T(8,128)(2,1)S(1)}, bf16[32,4096]{1,0:T(8,128)(2,1)S(1)}, u32[]{:S(2)}, u32[]{:S(2)}) collective-permute-start(bf16[32,4096]{1,0:T(8,128)(2,1)S(1)} %collective-permute-done.30), channel_id=1, source_target_pairs={{0,20},{8,28},{4,0},{12,8},{16,4},{24,12},{20,16},{28,24},{32,52},... | collective-permute-start | bytes 786440 | tf_op jit(solution)/shard_map/ppermute | solution.py:47
  172.0 7.6 %collective-permute-start.29 = (bf16[32,4096]{1,0:T(8,128)(2,1)S(1)}, bf16[32,4096]{1,0:T(8,128)(2,1)S(1)}, u32[]{:S(2)}, u32[]{:S(2)}) collective-permute-start(bf16[32,4096]{1,0:T(8,128)(2,1)S(1)} %collective-permute-done.28), channel_id=1, source_target_pairs={{0,4},{8,12},{4,16},{12,24},{16,20},{24,28},{20,0},{28,8},{32,36},... | collective-permute-start | bytes 786440 | tf_op jit(solution)/shard_map/ppermute | solution.py:47
  (7 other events, 13.0 us)

commit v3 on v2

--- a/solution.py
+++ b/solution.py
@@ -60,25 +60,16 @@
     return jnp.stack([stack, other])
 
 
-def gather_y(block, near_blocks, kept):
+def place_blocks(*sides):
     y, _, core, _, _ = places()
-    _, _, tokens, half = block.shape
-
-    def put(whole, part, first, row, at_core):
-        return lax.dynamic_update_slice(whole, part[:, None, :, None], (first, row, 0, at_core, 0, 0))
-
-    whole = jnp.zeros((2, RING, 2, 2, tokens, half), block.dtype)
-    before, after = lax.rem(y + RING - 1, RING), lax.rem(y + 1, RING)
-    far = lax.rem(y + 2, RING)
-    from_before, from_after = near_blocks
-    far_own, far_other = hop(from_before[:1], y=1), hop(from_after[1:], y=-1)
-    far_own, far_other, kept = together(far_own, far_other, kept)
-    for part, first, row in (
-        (block, 0, y), (from_before, 0, before), (from_after, 0, after), (far_own, 0, far), (far_other, 1, far)
-    ):
-        whole = put(whole, part, first, row, core)
-        whole = put(whole, hop(part, core=1), first, row, 1 - core)
-    return whole, kept
+    _, tokens, half = sides[0][0].shape
+    whole = jnp.zeros((2, RING, 2, 2, tokens, half), BF16)
+    for step, blocks in zip((0, RING - 1, 1, 2), zip(*sides)):
+        row = lax.rem(y + step, RING)
+        for side, block in enumerate(blocks):
+            for part, at_core in ((block, core), (hop(block, core=1), 1 - core)):
+                whole = lax.dynamic_update_slice(whole, part[None, None, :, None], (side, row, 0, at_core, 0, 0))
+    return whole
 
 
 def add(*parts):
@@ -358,18 +349,19 @@
     narrow = like((length, channels), BF16)
     table = (modes, channels)
 
-    block = gather_z(cotangent)
+    block, log_first = together(gather_z(cotangent), log_decay)
+    before_own, after_other = hop(block[0], y=1), hop(block[1], y=-1)
     ends, subs, driving = call(
         forward_ends,
-        (key_proj, value_proj, log_decay),
+        (key_proj, value_proj, log_first),
         (like((2 * modes, channels), F32), like((tiles, 2 * SUBS * modes, LANES), F32), wide),
         [table, (SUBS, LANES)],
         0.1,
         "forward_ends",
     )
     ends_pair = jnp.concatenate([ends, hop(ends, pair=1)])
-    block, ends_pair = together(block, ends_pair)
-    near_blocks = [hop(block, y=1), hop(block, y=-1)]
+    before_own, after_other, ends_pair = together(before_own, after_other, ends_pair)
+    before_other, after_own = hop(block[1], y=1), hop(block[0], y=-1)
     earlier = spread_over_x(ends_pair)
     gated, turned, pre_gate, lead = call(
         forward_full,
@@ -379,12 +371,17 @@
         0.1,
         "forward_full",
     )
-    turned, *near_blocks = together(turned, *near_blocks)
+    before_own, after_other, turned = together(before_own, after_other, turned)
+    far_own, far_other = hop(before_own, y=1), hop(after_other, y=-1)
+    before_other, after_own, turned = together(before_other, after_own, turned)
     near_first, near_rest, far_first, far_rest = project(turned, out_weight)
     got_first, got_rest = hop(far_first, core=1), hop(far_rest, core=1)
     gated_pair = jnp.concatenate([gated, hop(gated, pair=1)])
     opposite = add(near_first, got_first).astype(BF16)
-    cot_rows, opposite = gather_y(block, near_blocks, opposite)
+    far_own, far_other, opposite = together(far_own, far_other, opposite)
+    cot_rows = place_blocks(
+        (block[0], before_own, after_own, far_own), (block[1], before_other, after_other, far_other)
+    )
     cot_rows, got_rest = together(cot_rows.reshape(2 * length, -1), got_rest)
 
     half = out_weight.shape[1] // 2
@@ -392,43 +389,50 @@
     weights = {2: weigh(gated_pair, cot_rows, scale, 2)}
     cot_rows, weights[2] = together(cot_rows, weights[2])
     grad_parts = lax.dot_general(cot_rows, low_weight, (((1,), (1,)), ((), ())), preferred_element_type=F32)
-    cot_rows, grad_parts = together(cot_rows, grad_parts)
+    cot_rows, grad_parts, got_rest = together(cot_rows, grad_parts, got_rest)
     theirs = hop(grad_parts[length:].astype(BF16), pair=1)
     part = opposite.shape[0] // 2
     low_sum, high_sum = hop(opposite[:part], y=1), hop(opposite[part:], y=-1)
-    up_low, up_high, down_low, down_high, own_low, own_high = (
-        add(near_rest[i * part : (i + 1) * part], got_rest[i * part : (i + 1) * part]) for i in range(6)
-    )
-    up_low = add(up_low, low_sum).astype(BF16)
-    down_high = add(down_high, high_sum).astype(BF16)
+    above, below, own = (
+        add(near_rest[i * 2 * part : (i + 1) * 2 * part], got_rest[i * 2 * part : (i + 1) * 2 * part]) for i in range(3)
+    )
+    above = jnp.concatenate([add(above[:part], low_sum), above[part:]]).astype(BF16)
+    below = jnp.concatenate([below[:part], add(below[part:], high_sum)]).astype(BF16)
     for r in (1, 3, 0):
         weights[r] = weigh(gated_pair, cot_rows, scale, r)
     cut = channels // 2
     upper, lower = hop(weights[2][:cut], x=1), hop(weights[2][cut:], x=-1)
-    weights_up = jnp.concatenate([add(weights[1][:cut], upper).astype(BF16), weights[1][cut:]])
-    weights_down = jnp.concatenate([weights[3][:cut], add(weights[3][cut:], lower).astype(BF16)])
-    theirs, up_low, down_high, weights_up, weights_down, own_weights = together(
-        theirs, up_low, down_high, weights_up, weights_down, weights[0]
-    )
-    grad_weight = add(own_weights, hop(weights_up, x=1), hop(weights_down, x=-1)).astype(BF16)
+    up_sum = add(weights[1][:cut], upper).astype(BF16)
+    down_sum = add(weights[3][cut:], lower).astype(BF16)
+    up_rest, down_rest = weights[1][cut:], weights[3][:cut]
+    theirs, up_sum, down_sum, up_rest, down_rest = together(theirs, up_sum, down_sum, up_rest, down_rest)
+    up_rest, down_rest = hop(up_rest, x=1), hop(down_rest, x=-1)
     grad_gated = add(grad_parts[:length], theirs)
-    other_high = add(own_high, hop(up_high.astype(BF16), y=1), hop(down_high, y=-1)).astype(BF16)
-    width = other_high.shape[1] // 2
-    crossed = [hop(hop(other_high[:, :width], z=1), z=1), hop(hop(other_high[:, width:], z=-1), z=-1)]
-    mixed = add(own_low, hop(up_low, y=1), hop(down_low.astype(BF16), y=-1), jnp.concatenate(crossed, axis=1)).astype(BF16)
+    own = add(own, hop(above, y=1), hop(below, y=-1))
+    leaving = own[part:].astype(BF16)
+    width = leaving.shape[1] // 2
+    halfway = hop(leaving[:, width:], z=-1)
+    crossed = hop(leaving[:, :width], z=2)
 
     grad_query, back, sums, back_subs = call(
         backward_ends,
         (grad_gated, queries, pre_gate, driving, lead, log_decay),
         (narrow, wide, like((3 * modes + SUBS, channels), F32), like((tiles, SUBS * modes, LANES), F32)),
         [table, (tiles, 2 * SUBS * modes, LANES), (SUBS, LANES)],
-        0.1,
+        2.0,
         "backward_ends",
     )
+    sums, up_rest, down_rest = together(sums, up_rest, down_rest)
+    up_sum, down_sum = hop(up_sum, x=1), hop(down_sum, x=-1)
     others = hop(sums, pair=1)
-    all_sums = spread_over_x(
-        jnp.concatenate([sums[:modes], others[:modes], sums[modes:] + others[modes:]])
-    )
+    sums_pair = jnp.concatenate([sums[:modes], others[:modes], sums[modes:] + others[modes:]])
+    sums_pair, up_sum, down_sum = together(sums_pair, up_sum, down_sum)
+    crossed = jnp.concatenate([crossed, hop(halfway, z=-1)], axis=1)
+    mixed = add(own[:part], crossed).astype(BF16)
+    all_sums = spread_over_x(sums_pair)
+    grad_weight = jnp.concatenate(
+        [add(weights[0][:cut], up_sum, down_rest), add(weights[0][cut:], up_rest, down_sum)]
+    ).astype(BF16)
     grad_key, grad_value, grad_residue, grad_decay, grad_skip = call(
         functools.partial(backward_full, scale=scale),
         (key_proj, value_proj, back, back_subs, log_decay, residue, skip_row, *all_sums),

time: 181 us -> 153 us (0.85)
  waiting for transfers between devices: 60.6 us -> 36.2 us
  local copies, waits for them, and re-layouts: 19.1 us -> 15.6 us
    ppermute x38 -> x42, waiting for transfers between devices: 60.6 us -> 36.2 us  [hop(): return lax.ppermute(value, ('chan', 'seq'), moves)]
    convert_element_type x6 -> x3, other arithmetic: 5.29 us -> 1.3 us  [the longest x1 0.91 us: local(): mixed = add(own[:part], crossed).astype(BF16)]
    slice x5, local copies, waits for them, and re-layouts: 3.84 us -> 0.22 us  [the longest x2 0.07 us: local(): up_rest, down_rest = (weights[1][cut:], weights[3][:cut])]
    another operation x0 -> x4, other arithmetic: none -> 2.58 us
    add x1 -> x2, other arithmetic: 0.15 us -> 2.3 us  [add(): return functools.reduce(jnp.add, [part.astype(F32) for part in parts])]
    unnamed x35 -> x27, local copies, waits for them, and re-layouts: 4.56 us -> 2.52 us
    dynamic_update_slice x10 -> x16, local copies, waits for them, and re-layouts: 5.67 us -> 6.98 us  [place_blocks(): lax.dynamic_update_slice(whole, part[None, None, :, None], (side, row, 0,...]
    ppermute x38 -> x42, starting transfers between devices: 50.6 us -> 51 us  [hop(): return lax.ppermute(value, ('chan', 'seq'), moves)]
  transfers between devices with their start and end apart: 38 -> 42, of which waited for: 12 -> 16; matrix products, arithmetic and copies ran while one was open for 16% -> 19% of each run, Pallas kernels for 17% -> 20%
where the time goes in v3:
time: 153 us
  starting transfers between devices  51 us (33%)
  waiting for transfers between devices  36.2 us (24%)
  Pallas kernels  30 us (20%)
  local copies, waits for them, and re-layouts  15.6 us (10%)
  matrix products  10.6 us (7%)
  other arithmetic  7.95 us (5%)
    ppermute x42, starting transfers between devices, hop(): return lax.ppermute(value, ('chan', 'seq'), moves)  51 us
    ppermute x42, waiting for transfers between devices, hop(): return lax.ppermute(value, ('chan', 'seq'), moves)  36.2 us
    pallas_call x4, Pallas kernels, call(): pl.pallas_call(body, out_shape=[jax.ShapeDtypeStruct(o.shape, o.dtype) fo...  23.1 us
    dynamic_update_slice x16, local copies, waits for them, and re-layouts, place_blocks(): lax.dynamic_update_slice(whole, part[None, None, :, None], (side, row, 0,...  6.98 us
    pallas_call x1, Pallas kernels, project(): pl.pallas_call(project_tile, grid=(width // tile,), out_shape=[jax.ShapeD...  6.86 us
    dot_general x4, matrix products, weigh(): lax.dot_general(gated, columns, (((0,), (0,)), ((), ())), preferred_eleme...  6.09 us
    dot_general x1, matrix products, local(): lax.dot_general(cot_rows, low_weight, (((1,), (1,)), ((), ())), preferred...  4.52 us
  transfers between devices with their start and end apart: 42, of which 16 were waited for; matrix products, arithmetic and copies ran while one was open for 19% of the time, Pallas kernels for 20%

profile of v3, /device:TPU:0, one launch (start us, length us, event | category | flops | bytes accessed | tf_op | source)
XLA Modules:
  0.0 152.6 jit_solution(5154195804211460938)
XLA Ops:
  0.7 1.1 constant_dynamic-slice_fusion.1
  1.8 2.1 %collective-permute-start.1 = (bf16[32,4096]{1,0:T(8,128)(2,1)S(1)}, bf16[32,4096]{1,0:T(8,128)(2,1)S(1)}, u32[]{:S(2)}, u32[]{:S(2)}) collective-permute-start(bf16[32,4096]{1,0:T(8,128)(2,1)S(1)} %get-tuple-element.127), channel_id=1, source_target_pairs={{0,4},{8,12},{4,16},{12,24},{16,20},{24,28},{20,0},{28,8},{32,36},... | collective-permute-start | bytes 786440 | tf_op jit(solution)/shard_map/ppermute | solution.py:47
  3.9 2.2 %collective-permute-start.2 = (bf16[32,4096]{1,0:T(8,128)(2,1)S(1)}, bf16[32,4096]{1,0:T(8,128)(2,1)S(1)}, u32[]{:S(2)}, u32[]{:S(2)}) collective-permute-start(bf16[32,4096]{1,0:T(8,128)(2,1)S(1)} %get-tuple-element.127), channel_id=1, source_target_pairs={{0,20},{8,28},{4,0},{12,8},{16,4},{24,12},{20,16},{28,24},{32,52},... | collective-permute-start | bytes 786440 | tf_op jit(solution)/shard_map/ppermute | solution.py:47
  6.1 1.8 %collective-permute-start = (bf16[32,4096]{1,0:T(8,128)(2,1)S(1)}, bf16[32,4096]{1,0:T(8,128)(2,1)S(1)}, u32[]{:S(2)}, u32[]{:S(2)}) collective-permute-start(bf16[32,4096]{1,0:T(8,128)(2,1)S(1)} %get-tuple-element.126), channel_id=1, source_target_pairs={{0,16},{8,24},{4,20},{12,28},{16,0},{24,8},{20,4},{28,12},{32,48},... | collective-permute-start | bytes 786440 | tf_op jit(solution)/shard_map/ppermute | solution.py:47
  7.9 4.4 %collective-permute-done.1 = bf16[32,4096]{1,0:T(8,128)(2,1)S(1)} collective-permute-done((bf16[32,4096]{1,0:T(8,128)(2,1)S(1)}, bf16[32,4096]{1,0:T(8,128)(2,1)S(1)}, u32[]{:S(2)}, u32[]{:S(2)}) %collective-permute-start.1) | collective-permute-done | bytes 262176 | tf_op jit(solution)/shard_map/ppermute | solution.py:47
  12.3 5.0 %collective-permute-done.2 = bf16[32,4096]{1,0:T(8,128)(2,1)S(1)} collective-permute-done((bf16[32,4096]{1,0:T(8,128)(2,1)S(1)}, bf16[32,4096]{1,0:T(8,128)(2,1)S(1)}, u32[]{:S(2)}, u32[]{:S(2)}) %collective-permute-start.2) | collective-permute-done | bytes 262176 | tf_op jit(solution)/shard_map/ppermute | solution.py:47
  17.5 1.7 %collective-permute-done = bf16[32,4096]{1,0:T(8,128)(2,1)S(1)} collective-permute-done((bf16[32,4096]{1,0:T(8,128)(2,1)S(1)}, bf16[32,4096]{1,0:T(8,128)(2,1)S(1)}, u32[]{:S(2)}, u32[]{:S(2)}) %collective-permute-start) | collective-permute-done | bytes 262176 | tf_op jit(solution)/shard_map/ppermute | solution.py:47
  20.4 1.6 %collective-permute-start.5 = (bf16[2,32,4096]{2,1,0:T(8,128)(2,1)}, bf16[2,32,4096]{2,1,0:T(8,128)(2,1)S(1)}, u32[]{:S(2)}, u32[]{:S(2)}) collective-permute-start(bf16[2,32,4096]{2,1,0:T(8,128)(2,1)} %get-tuple-element.125), channel_id=1, source_target_pairs={{0,32},{8,40},{4,36},{12,44},{16,48},{24,56},{20,52},{28,60},{32,6... | collective-permute-start | bytes 1572872 | tf_op jit(solution)/shard_map/ppermute | solution.py:47
  22.2 1.7 %collective-permute-start.6 = (bf16[2,32,4096]{2,1,0:T(8,128)(2,1)}, bf16[2,32,4096]{2,1,0:T(8,128)(2,1)S(1)}, u32[]{:S(2)}, u32[]{:S(2)}) collective-permute-start(bf16[2,32,4096]{2,1,0:T(8,128)(2,1)} %get-tuple-element.124), channel_id=1, source_target_pairs={{0,96},{8,104},{4,100},{12,108},{16,112},{24,120},{20,116},{28,124... | collective-permute-start | bytes 1572872 | tf_op jit(solution)/shard_map/ppermute | solution.py:47
  23.9 3.6 %forward_ends.1 = (f32[32,512]{1,0:T(8,128)S(1)}, f32[4,256,128]{2,1,0:T(8,128)S(1)}, f32[4,512,128]{2,1,0:T(8,128)S(1)}) custom-call(bf16[512,512]{1,0:T(8,128)(2,1)S(1)} %copy-done, bf16[512,512]{1,0:T(8,128)(2,1)S(1)} %copy-done.1, f32[16,512]{1,0:T(8,128)S(1)} %copy-done.3), custom_call_target="tpu_custom_call" | custom-call | flops 115000000 | tf_op jit(solution)/shard_map/forward_ends/pallas_call | solution.py:317
  27.5 1.2 collective-permute-start.7
  29.9 2.0 %collective-permute-done.7 = f32[32,512]{1,0:T(8,128)S(1)} collective-permute-done((f32[32,512]{1,0:T(8,128)S(1)}, f32[32,512]{1,0:T(8,128)S(1)}, u32[]{:S(2)}, u32[]{:S(2)}) %collective-permute-start.7) | collective-permute-done | bytes 65568 | tf_op jit(solution)/shard_map/ppermute | solution.py:47
  32.2 4.3 %collective-permute-done.5 = bf16[2,32,4096]{2,1,0:T(8,128)(2,1)S(1)} collective-permute-done((bf16[2,32,4096]{2,1,0:T(8,128)(2,1)}, bf16[2,32,4096]{2,1,0:T(8,128)(2,1)S(1)}, u32[]{:S(2)}, u32[]{:S(2)}) %collective-permute-start.5) | collective-permute-done | bytes 524320 | tf_op jit(solution)/shard_map/ppermute | solution.py:47
  36.5 1.8 %collective-permute-start.4 = (bf16[2,32,4096]{2,1,0:T(8,128)(2,1)}, bf16[2,32,4096]{2,1,0:T(8,128)(2,1)S(1)}, u32[]{:S(2)}, u32[]{:S(2)}) collective-permute-start(bf16[2,32,4096]{2,1,0:T(8,128)(2,1)} %get-tuple-element.125), channel_id=1, source_target_pairs={{0,96},{8,104},{4,100},{12,108},{16,112},{24,120},{20,116},{28,124... | collective-permute-start | bytes 1572872 | tf_op jit(solution)/shard_map/ppermute | solution.py:47
  38.3 1.5 collective-permute-start.8
  39.8 2.7 %collective-permute-start.9 = (f32[64,512]{1,0:T(8,128)S(1)}, f32[64,512]{1,0:T(8,128)S(1)}, u32[]{:S(2)}, u32[]{:S(2)}) collective-permute-start(f32[64,512]{1,0:T(8,128)S(1)} %pad_maximum_fusion.5.refs_6_), channel_id=1, source_target_pairs={{0,2},{8,10},{4,6},{12,14},{16,18},{24,26},{20,22},{28,30},{32,34}... | collective-permute-start | bytes 393224 | tf_op jit(solution)/shard_map/ppermute | solution.py:47
  43.7 1.5 collective-permute-start.10
  46.3 1.5 collective-permute-done.9.refs_8_
  48.8 4.0 %forward_full.1 = (bf16[512,512]{1,0:T(8,128)(2,1)S(1)}, bf16[512,512]{1,0:T(8,128)(2,1)S(1)}, f32[4,512,128]{2,1,0:T(8,128)S(1)}, f32[4,256,128]{2,1,0:T(8,128)S(1)}) custom-call(bf16[512,512]{1,0:T(8,128)(2,1)S(1)} %copy-done.2, f32[4,512,128]{2,1,0:T(8,128)S(1)} %get-tuple-element.65.refs_1_.drive_ref, f32[4,256,128]{2,1,0:T(8,128)S(1)} %get-tuple-element.66.refs_2_, ...), custom_call_target="tpu_custom_call" | custom-call | flops 115000000 | tf_op jit(solution)/shard_map/forward_full/pallas_call | solution.py:317
  53.4 3.0 %collective-permute-start.18 = (bf16[2,32,4096]{2,1,0:T(8,128)(2,1)S(1)}, bf16[2,32,4096]{2,1,0:T(8,128)(2,1)S(1)}, u32[]{:S(2)}, u32[]{:S(2)}) collective-permute-start(bf16[2,32,4096]{2,1,0:T(8,128)(2,1)S(1)} %collective-permute-done.6), channel_id=1, source_target_pairs={{0,96},{8,104},{4,100},{12,108},{16,112},{24,120},{20,116},{28,124... | collective-permute-start | bytes 1572872 | tf_op jit(solution)/shard_map/ppermute | solution.py:47
  56.4 1.1 collective-permute-start.23
  58.4 6.9 %project.1 = (bf16[64,8192]{1,0:T(8,128)(2,1)S(1)}, bf16[192,8192]{1,0:T(8,128)(2,1)S(1)}, bf16[64,8192]{1,0:T(8,128)(2,1)S(1)}, bf16[192,8192]{1,0:T(8,128)(2,1)S(1)}) custom-call(bf16[512,512]{1,0:T(8,128)(2,1)S(1)} %get-tuple-element.70.rows_ref, bf16[512,8192]{1,0:T(8,128)(2,1)S(1)} %bitcast.83), custom_call_target="tpu_custom_call" | custom-call | flops 4294967296 | bytes 16777216 | tf_op jit(solution)/shard_map/project/pallas_call | solution.py:92
  66.5 1.1 bitcast_dynamic-update-slice_fusion.8
  70.6 1.9 %constant_dynamic-update-slice_fusion = bf16[1024,512]{1,0:T(8,128)(2,1)} fusion(bf16[1024,512]{1,0:T(8,128)(2,1)} %constant_dynamic-update-slice_fusion.1, bf16[512,512]{1,0:T(8,128)(2,1)} %collective-permute-done.23), kind=kLoop, calls=%fused_computation.61 | loop fusion | bytes 1048576 | tf_op jit(solution)/shard_map/concatenate | solution.py:379
  72.5 1.2 bitcast_dynamic-update-slice_fusion.3
  75.1 1.8 %collective-permute-start.24 = (bf16[32,8192]{1,0:T(8,128)(2,1)S(1)}, bf16[32,8192]{1,0:T(8,128)(2,1)S(1)}, u32[]{:S(2)}, u32[]{:S(2)}) collective-permute-start(bf16[32,8192]{1,0:T(8,128)(2,1)S(1)} %get-tuple-element.122), channel_id=1, source_target_pairs={{0,32},{8,40},{4,36},{12,44},{16,48},{24,56},{20,52},{28,60},{32,6... | collective-permute-start | bytes 1572872 | tf_op jit(solution)/shard_map/ppermute | solution.py:47
  78.6 1.6 %copy-done.6 = bf16[192,8192]{1,0:T(8,128)(2,1)} copy-done((bf16[192,8192]{1,0:T(8,128)(2,1)}, bf16[192,8192]{1,0:T(8,128)(2,1)S(1)}, u32[]{:S(2)}) %copy-start.6) | copy-done | bytes 3145752
  80.2 2.3 %multiply_convert_fusion.3 = bf16[512,1024]{1,0:T(8,128)(2,1)} fusion(bf16[1024,512]{1,0:T(8,128)(2,1)S(1)} %copy-done.9, bf16[1024,4096]{1,0:T(8,128)(2,1)S(1)} %bitcast.84, s32[]{:T(128)S(6)} %select_n.130), kind=kOutput, calls=%fused_computation.14 | convolution fusion | flops 1074790400 | bytes 4194308 | tf_op jit(solution)/shard_map/dot_general | solution.py:110
  82.5 4.5 %fusion = f32[1024,512]{1,0:T(8,128)S(1)} fusion(bf16[1024,4096]{1,0:T(8,128)(2,1)S(1)} %bitcast.85, bf16[512,8192]{1,0:T(8,128)(2,1)S(1)} %bitcast.83, s32[]{:T(128)S(6)} %select_n.116), kind=kOutput, calls=%fused_computation | convolution fusion | flops 4294967296 | bytes 14680068 | tf_op jit(solution)/shard_map/dot_general | solution.py:391
  87.1 2.1 %convert_add_fusion.2 = (f32[64,8192]{1,0:T(8,128)S(1)}, f32[64,8192]{1,0:T(8,128)S(1)}) fusion(bf16[192,8192]{1,0:T(8,128)(2,1)} %copy-done.6, bf16[192,8192]{1,0:T(8,128)(2,1)S(1)} %get-tuple-element.71), kind=kLoop, calls=%fused_computation.13 | loop fusion | flops 3145728 | bytes 8388608 | tf_op jit(solution)/shard_map/add | solution.py:76
  89.4 1.4 collective-permute-start.27
  93.0 1.1 collective-permute-start.32
  94.2 2.2 %collective-permute-start.33 = (bf16[256,1024]{1,0:T(8,128)(2,1)S(1)}, bf16[256,1024]{1,0:T(8,128)(2,1)S(1)}, u32[]{:S(2)}, u32[]{:S(2)}) collective-permute-start(bf16[256,1024]{1,0:T(8,128)(2,1)S(1)} %get-tuple-element.118), channel_id=1, source_target_pairs={{0,3},{8,11},{4,7},{12,15},{16,19},{24,27},{20,23},{28,31},{32,35}... | collective-permute-start | bytes 1572872 | tf_op jit(solution)/shard_map/ppermute | solution.py:47
  96.3 1.3 multiply_convert_fusion.2
  97.6 1.3 multiply_convert_fusion.1
  98.9 8.7 %collective-permute-done.32 = bf16[256,1024]{1,0:T(8,128)(2,1)S(1)} collective-permute-done((bf16[256,1024]{1,0:T(8,128)(2,1)S(1)}, bf16[256,1024]{1,0:T(8,128)(2,1)S(1)}, u32[]{:S(2)}, u32[]{:S(2)}) %collective-permute-start.32) | collective-permute-done | bytes 524320 | tf_op jit(solution)/shard_map/ppermute | solution.py:47
  108.8 2.6 %collective-permute-start.35 = (bf16[256,1024]{1,0:T(8,128)(2,1)S(1)}, bf16[256,1024]{1,0:T(8,128)(2,1)S(1)}, u32[]{:S(2)}, u32[]{:S(2)}) collective-permute-start(bf16[256,1024]{1,0:T(8,128)(2,1)S(1)} %slice.150), channel_id=1, source_target_pairs={{0,3},{8,11},{4,7},{12,15},{16,19},{24,27},{20,23},{28,31},{32,35}... | collective-permute-start | bytes 1572872 | tf_op jit(solution)/shard_map/ppermute | solution.py:47
  111.4 1.3 multiply_convert_fusion
  112.9 10.5 %backward_ends.1 = (bf16[512,512]{1,0:T(8,128)(2,1)}, f32[4,512,128]{2,1,0:T(8,128)S(1)}, f32[56,512]{1,0:T(8,128)S(1)}, f32[4,128,128]{2,1,0:T(8,128)S(1)}) custom-call(f32[512,512]{1,0:T(8,128)S(1)} %convert_add_fusion.3.grad_ref, bf16[512,512]{1,0:T(8,128)(2,1)S(1)} %copy-done.2, f32[4,512,128]{2,1,0:T(8,128)S(1)} %get-tuple-element.91.pre_ref, ...), custom_call_target="tpu_custom_call" | custom-call | flops 2300000000 | tf_op jit(solution)/shard_map/backward_ends/pallas_call | solution.py:317
  124.2 2.4 %collective-permute-start.38 = (bf16[256,1024]{1,0:T(8,128)(2,1)S(1)}, bf16[256,1024]{1,0:T(8,128)(2,1)S(1)}, u32[]{:S(2)}, u32[]{:S(2)}) collective-permute-start(bf16[256,1024]{1,0:T(8,128)(2,1)S(1)} %add_convert_fusion.3), channel_id=1, source_target_pairs={{0,3},{8,11},{4,7},{12,15},{16,19},{24,27},{20,23},{28,31},{32,35}... | collective-permute-start | bytes 1572872 | tf_op jit(solution)/shard_map/ppermute | solution.py:47
  126.6 1.1 collective-permute-start.36
  127.8 1.7 %fusion.26 = (bf16[64,8192]{1,0:T(8,128)(2,1)S(1)}, f32[64,8192]{1,0:T(8,128)S(1)}) fusion(bf16[64,8192]{1,0:T(8,128)(2,1)S(1)} %collective-permute-done.27, bf16[64,8192]{1,0:T(8,128)(2,1)S(1)} %collective-permute-done.25, bf16[192,8192]{1,0:T(8,128)(2,1)} %copy-done.6, bf16[192,8192]{1,0:T(8,128)(2,1)S(1)} %get-tuple-element.71), kind=kLoop, calls=%fused_computation.70 | loop fusion | flops 4194304 | bytes 7340032 | tf_op jit(solution)/shard_map/convert.3
  129.6 1.7 %collective-permute-start.29 = (bf16[32,4096]{1,0:T(8,128)(2,1)S(1)}, bf16[32,4096]{1,0:T(8,128)(2,1)S(1)}, u32[]{:S(2)}, u32[]{:S(2)}) collective-permute-start(bf16[32,4096]{1,0:T(8,128)(2,1)S(1)} %get-tuple-element.121), channel_id=1, source_target_pairs={{0,20},{8,28},{4,0},{12,8},{16,4},{24,12},{20,16},{28,24},{32,52},... | collective-permute-start | bytes 786440 | tf_op jit(solution)/shard_map/ppermute | solution.py:47
  131.3 1.3 collective-permute-start.28
  133.0 2.7 %collective-permute-done.38 = bf16[256,1024]{1,0:T(8,128)(2,1)S(1)} collective-permute-done((bf16[256,1024]{1,0:T(8,128)(2,1)S(1)}, bf16[256,1024]{1,0:T(8,128)(2,1)S(1)}, u32[]{:S(2)}, u32[]{:S(2)}) %collective-permute-start.38) | collective-permute-done | bytes 524320 | tf_op jit(solution)/shard_map/ppermute | solution.py:47
  135.9 5.0 %collective-permute-start.40 = (f32[72,512]{1,0:T(8,128)S(1)}, f32[72,512]{1,0:T(8,128)S(1)}, u32[]{:S(2)}, u32[]{:S(2)}) collective-permute-start(f32[72,512]{1,0:T(8,128)S(1)} %pad_maximum_fusion.4.refs_7_), channel_id=1, source_target_pairs={{0,2},{8,10},{4,6},{12,14},{16,18},{24,26},{20,22},{28,30},{32,34}... | collective-permute-start | bytes 442376 | tf_op jit(solution)/shard_map/ppermute | solution.py:47
  140.9 2.0 %collective-permute-start.30 = (bf16[32,4096]{1,0:T(8,128)(2,1)S(1)}, bf16[32,4096]{1,0:T(8,128)(2,1)S(1)}, u32[]{:S(2)}, u32[]{:S(2)}) collective-permute-start(bf16[32,4096]{1,0:T(8,128)(2,1)S(1)} %collective-permute-done.29), channel_id=1, source_target_pairs={{0,20},{8,28},{4,0},{12,8},{16,4},{24,12},{20,16},{28,24},{32,52},... | collective-permute-start | bytes 786440 | tf_op jit(solution)/shard_map/ppermute | solution.py:47
  146.0 5.1 %backward_full.1 = (bf16[512,512]{1,0:T(8,128)(2,1)}, bf16[512,512]{1,0:T(8,128)(2,1)}, f32[16,512]{1,0:T(8,128)}, f32[16,512]{1,0:T(8,128)}, f32[8,512]{1,0:T(8,128)S(1)}) custom-call(bf16[512,512]{1,0:T(8,128)(2,1)S(1)} %copy-done, bf16[512,512]{1,0:T(8,128)(2,1)S(1)} %copy-done.1, f32[4,512,128]{2,1,0:T(8,128)S(1)} %get-tuple-element.94.refs_2_, ...), custom_call_target="tpu_custom_call" | custom-call | flops 115000000 | tf_op jit(solution)/shard_map/backward_full/pallas_call | solution.py:317
  (125 shorter events, 24.7 us)
Async XLA Ops:
  0.6 23.3 %copy-start.3 = (f32[16,512]{1,0:T(8,128)S(1)}, f32[16,512]{1,0:T(8,128)}, u32[]{:S(2)}) copy-start(f32[16,512]{1,0:T(8,128)} %refs_4_.3) | copy-start | bytes 98308
  1.8 10.5 %collective-permute-start.1 = (bf16[32,4096]{1,0:T(8,128)(2,1)S(1)}, bf16[32,4096]{1,0:T(8,128)(2,1)S(1)}, u32[]{:S(2)}, u32[]{:S(2)}) collective-permute-start(bf16[32,4096]{1,0:T(8,128)(2,1)S(1)} %get-tuple-element.127), channel_id=1, source_target_pairs={{0,4},{8,12},{4,16},{12,24},{16,20},{24,28},{20,0},{28,8},{32,36},... | collective-permute-start | bytes 786440 | tf_op jit(solution)/shard_map/ppermute | solution.py:47
  3.9 13.4 %collective-permute-start.2 = (bf16[32,4096]{1,0:T(8,128)(2,1)S(1)}, bf16[32,4096]{1,0:T(8,128)(2,1)S(1)}, u32[]{:S(2)}, u32[]{:S(2)}) collective-permute-start(bf16[32,4096]{1,0:T(8,128)(2,1)S(1)} %get-tuple-element.127), channel_id=1, source_target_pairs={{0,20},{8,28},{4,0},{12,8},{16,4},{24,12},{20,16},{28,24},{32,52},... | collective-permute-start | bytes 786440 | tf_op jit(solution)/shard_map/ppermute | solution.py:47
  6.1 13.0 %collective-permute-start = (bf16[32,4096]{1,0:T(8,128)(2,1)S(1)}, bf16[32,4096]{1,0:T(8,128)(2,1)S(1)}, u32[]{:S(2)}, u32[]{:S(2)}) collective-permute-start(bf16[32,4096]{1,0:T(8,128)(2,1)S(1)} %get-tuple-element.126), channel_id=1, source_target_pairs={{0,16},{8,24},{4,20},{12,28},{16,0},{24,8},{20,4},{28,12},{32,48},... | collective-permute-start | bytes 786440 | tf_op jit(solution)/shard_map/ppermute | solution.py:47
  19.3 29.4 %copy-start.2 = (bf16[512,512]{1,0:T(8,128)(2,1)S(1)}, bf16[512,512]{1,0:T(8,128)(2,1)}, u32[]{:S(2)}) copy-start(bf16[512,512]{1,0:T(8,128)(2,1)} %query_ref.1) | copy-start | bytes 1572868
  19.3 29.4 %copy-start.4 = (f32[16,512]{1,0:T(8,128)S(1)}, f32[16,512]{1,0:T(8,128)}, u32[]{:S(2)}) copy-start(f32[16,512]{1,0:T(8,128)} %refs_5_.1) | copy-start | bytes 98308
  19.3 29.4 %copy-start.5 = (f32[512]{0:T(512)S(1)}, f32[512]{0:T(512)}, u32[]{:S(2)}) copy-start(f32[512]{0:T(512)} %param.11) | copy-start | bytes 6148
  20.4 19.4 %collective-permute-start.11 = (bf16[2,32,4096]{2,1,0:T(8,128)(2,1)}, bf16[2,32,4096]{2,1,0:T(8,128)(2,1)}, u32[]{:S(2)}, u32[]{:S(2)}) collective-permute-start(bf16[2,32,4096]{2,1,0:T(8,128)(2,1)} %get-tuple-element.125), channel_id=1, source_target_pairs={{0,8},{8,0},{4,12},{12,4},{16,24},{24,16},{20,28},{28,20},{32,40},... | collective-permute-start | bytes 1572872 | tf_op jit(solution)/shard_map/ppermute | solution.py:47
  20.4 16.1 %collective-permute-start.5 = (bf16[2,32,4096]{2,1,0:T(8,128)(2,1)}, bf16[2,32,4096]{2,1,0:T(8,128)(2,1)S(1)}, u32[]{:S(2)}, u32[]{:S(2)}) collective-permute-start(bf16[2,32,4096]{2,1,0:T(8,128)(2,1)} %get-tuple-element.125), channel_id=1, source_target_pairs={{0,32},{8,40},{4,36},{12,44},{16,48},{24,56},{20,52},{28,60},{32,6... | collective-permute-start | bytes 1572872 | tf_op jit(solution)/shard_map/ppermute | solution.py:47
  22.0 21.7 %collective-permute-start.12 = (bf16[2,32,4096]{2,1,0:T(8,128)(2,1)}, bf16[2,32,4096]{2,1,0:T(8,128)(2,1)}, u32[]{:S(2)}, u32[]{:S(2)}) collective-permute-start(bf16[2,32,4096]{2,1,0:T(8,128)(2,1)} %get-tuple-element.124), channel_id=1, source_target_pairs={{0,8},{8,0},{4,12},{12,4},{16,24},{24,16},{20,28},{28,20},{32,40},... | collective-permute-start | bytes 1572872 | tf_op jit(solution)/shard_map/ppermute | solution.py:47
  22.2 16.1 %collective-permute-start.6 = (bf16[2,32,4096]{2,1,0:T(8,128)(2,1)}, bf16[2,32,4096]{2,1,0:T(8,128)(2,1)S(1)}, u32[]{:S(2)}, u32[]{:S(2)}) collective-permute-start(bf16[2,32,4096]{2,1,0:T(8,128)(2,1)} %get-tuple-element.124), channel_id=1, source_target_pairs={{0,96},{8,104},{4,100},{12,108},{16,112},{24,120},{20,116},{28,124... | collective-permute-start | bytes 1572872 | tf_op jit(solution)/shard_map/ppermute | solution.py:47
  27.5 30.9 %slice-start = ((s8[8388608]{0:T(1024)(128)(4,1)}), s8[4194304]{0:T(1024)(128)(4,1)S(1)}, s32[]{:S(2)}) async-start(s8[8388608]{0:T(1024)(128)(4,1)} %bitcast.82), calls=%async_computation | async-start | bytes 8388608
  27.5 4.3 %collective-permute-start.7 = (f32[32,512]{1,0:T(8,128)S(1)}, f32[32,512]{1,0:T(8,128)S(1)}, u32[]{:S(2)}, u32[]{:S(2)}) collective-permute-start(f32[32,512]{1,0:T(8,128)S(1)} %get-tuple-element.62), channel_id=1, source_target_pairs={{0,4},{8,12},{4,0},{12,8},{16,20},{24,28},{20,16},{28,24},{32,36},... | collective-permute-start | bytes 196616 | tf_op jit(solution)/shard_map/ppermute | solution.py:47
  29.8 28.6 %slice-start.1 = ((s8[8388608]{0:T(1024)(128)(4,1)}), s8[4194304]{0:T(1024)(128)(4,1)S(1)}, s32[]{:S(2)}) async-start(s8[8388608]{0:T(1024)(128)(4,1)} %bitcast.82), calls=%async_computation.1 | async-start | bytes 8388608
  31.9 21.5 %collective-permute-start.3 = (bf16[2,32,4096]{2,1,0:T(8,128)(2,1)}, bf16[2,32,4096]{2,1,0:T(8,128)(2,1)}, u32[]{:S(2)}, u32[]{:S(2)}) collective-permute-start(bf16[2,32,4096]{2,1,0:T(8,128)(2,1)} %get-tuple-element.124), channel_id=1, source_target_pairs={{0,32},{8,40},{4,36},{12,44},{16,48},{24,56},{20,52},{28,60},{32,6... | collective-permute-start | bytes 1572872 | tf_op jit(solution)/shard_map/ppermute | solution.py:47
  36.5 19.8 %collective-permute-start.4 = (bf16[2,32,4096]{2,1,0:T(8,128)(2,1)}, bf16[2,32,4096]{2,1,0:T(8,128)(2,1)S(1)}, u32[]{:S(2)}, u32[]{:S(2)}) collective-permute-start(bf16[2,32,4096]{2,1,0:T(8,128)(2,1)} %get-tuple-element.125), channel_id=1, source_target_pairs={{0,96},{8,104},{4,100},{12,108},{16,112},{24,120},{20,116},{28,124... | collective-permute-start | bytes 1572872 | tf_op jit(solution)/shard_map/ppermute | solution.py:47
  38.3 8.0 %collective-permute-start.8 = (f32[64,512]{1,0:T(8,128)S(1)}, f32[64,512]{1,0:T(8,128)S(1)}, u32[]{:S(2)}, u32[]{:S(2)}) collective-permute-start(f32[64,512]{1,0:T(8,128)S(1)} %pad_maximum_fusion.5.refs_6_), channel_id=1, source_target_pairs={{0,1},{8,9},{4,5},{12,13},{16,17},{24,25},{20,21},{28,29},{32,33},... | collective-permute-start | bytes 393224 | tf_op jit(solution)/shard_map/ppermute | solution.py:47
  39.8 8.0 %collective-permute-start.9 = (f32[64,512]{1,0:T(8,128)S(1)}, f32[64,512]{1,0:T(8,128)S(1)}, u32[]{:S(2)}, u32[]{:S(2)}) collective-permute-start(f32[64,512]{1,0:T(8,128)S(1)} %pad_maximum_fusion.5.refs_6_), channel_id=1, source_target_pairs={{0,2},{8,10},{4,6},{12,14},{16,18},{24,26},{20,22},{28,30},{32,34}... | collective-permute-start | bytes 393224 | tf_op jit(solution)/shard_map/ppermute | solution.py:47
  43.7 5.0 %collective-permute-start.10 = (f32[64,512]{1,0:T(8,128)S(1)}, f32[64,512]{1,0:T(8,128)S(1)}, u32[]{:S(2)}, u32[]{:S(2)}) collective-permute-start(f32[64,512]{1,0:T(8,128)S(1)} %pad_maximum_fusion.5.refs_6_), channel_id=1, source_target_pairs={{0,3},{8,11},{4,7},{12,15},{16,19},{24,27},{20,23},{28,31},{32,35}... | collective-permute-start | bytes 393224 | tf_op jit(solution)/shard_map/ppermute | solution.py:47
  52.8 12.5 %collective-permute-start.13 = (bf16[2,32,4096]{2,1,0:T(8,128)(2,1)S(1)}, bf16[2,32,4096]{2,1,0:T(8,128)(2,1)}, u32[]{:S(2)}, u32[]{:S(2)}) collective-permute-start(bf16[2,32,4096]{2,1,0:T(8,128)(2,1)S(1)} %collective-permute-done.5), channel_id=1, source_target_pairs={{0,8},{8,0},{4,12},{12,4},{16,24},{24,16},{20,28},{28,20},{32,40},... | collective-permute-start | bytes 1572872 | tf_op jit(solution)/shard_map/ppermute | solution.py:47
  52.9 21.0 %collective-permute-start.17 = (bf16[2,32,4096]{2,1,0:T(8,128)(2,1)S(1)}, bf16[2,32,4096]{2,1,0:T(8,128)(2,1)S(1)}, u32[]{:S(2)}, u32[]{:S(2)}) collective-permute-start(bf16[2,32,4096]{2,1,0:T(8,128)(2,1)S(1)} %collective-permute-done.5), channel_id=1, source_target_pairs={{0,32},{8,40},{4,36},{12,44},{16,48},{24,56},{20,52},{28,60},{32,6... | collective-permute-start | bytes 1572872 | tf_op jit(solution)/shard_map/ppermute | solution.py:47
  53.2 19.3 %collective-permute-start.16 = (bf16[2,32,4096]{2,1,0:T(8,128)(2,1)S(1)}, bf16[2,32,4096]{2,1,0:T(8,128)(2,1)}, u32[]{:S(2)}, u32[]{:S(2)}) collective-permute-start(bf16[2,32,4096]{2,1,0:T(8,128)(2,1)S(1)} %collective-permute-done.6), channel_id=1, source_target_pairs={{0,8},{8,0},{4,12},{12,4},{16,24},{24,16},{20,28},{28,20},{32,40},... | collective-permute-start | bytes 1572872 | tf_op jit(solution)/shard_map/ppermute | solution.py:47
  53.4 20.5 %collective-permute-start.18 = (bf16[2,32,4096]{2,1,0:T(8,128)(2,1)S(1)}, bf16[2,32,4096]{2,1,0:T(8,128)(2,1)S(1)}, u32[]{:S(2)}, u32[]{:S(2)}) collective-permute-start(bf16[2,32,4096]{2,1,0:T(8,128)(2,1)S(1)} %collective-permute-done.6), channel_id=1, source_target_pairs={{0,96},{8,104},{4,100},{12,108},{16,112},{24,120},{20,116},{28,124... | collective-permute-start | bytes 1572872 | tf_op jit(solution)/shard_map/ppermute | solution.py:47
  56.4 14.0 %collective-permute-start.23 = (bf16[512,512]{1,0:T(8,128)(2,1)S(1)}, bf16[512,512]{1,0:T(8,128)(2,1)}, u32[]{:S(2)}, u32[]{:S(2)}) collective-permute-start(bf16[512,512]{1,0:T(8,128)(2,1)S(1)} %get-tuple-element.82), channel_id=1, source_target_pairs={{0,4},{8,12},{4,0},{12,8},{16,20},{24,28},{20,16},{28,24},{32,36},... | collective-permute-start | bytes 1572872 | tf_op jit(solution)/shard_map/ppermute | solution.py:47
  65.3 2.3 %collective-permute-start.14 = (bf16[2,32,4096]{2,1,0:T(8,128)(2,1)}, bf16[2,32,4096]{2,1,0:T(8,128)(2,1)S(1)}, u32[]{:S(2)}, u32[]{:S(2)}) collective-permute-start(bf16[2,32,4096]{2,1,0:T(8,128)(2,1)} %collective-permute-done.3), channel_id=1, source_target_pairs={{0,8},{8,0},{4,12},{12,4},{16,24},{24,16},{20,28},{28,20},{32,40},... | collective-permute-start | bytes 1572872 | tf_op jit(solution)/shard_map/ppermute | solution.py:47
  67.6 2.3 %collective-permute-start.15 = (bf16[2,32,4096]{2,1,0:T(8,128)(2,1)}, bf16[2,32,4096]{2,1,0:T(8,128)(2,1)S(1)}, u32[]{:S(2)}, u32[]{:S(2)}) collective-permute-start(bf16[2,32,4096]{2,1,0:T(8,128)(2,1)} %copy-done.8), channel_id=1, source_target_pairs={{0,8},{8,0},{4,12},{12,4},{16,24},{24,16},{20,28},{28,20},{32,40},... | collective-permute-start | bytes 1572872 | tf_op jit(solution)/shard_map/ppermute | solution.py:47
  69.9 3.7 %collective-permute-start.19 = (bf16[64,8192]{1,0:T(8,128)(2,1)S(1)}, bf16[64,8192]{1,0:T(8,128)(2,1)S(1)}, u32[]{:S(2)}, u32[]{:S(2)}) collective-permute-start(bf16[64,8192]{1,0:T(8,128)(2,1)S(1)} %get-tuple-element.77), channel_id=1, source_target_pairs={{0,8},{8,0},{4,12},{12,4},{16,24},{24,16},{20,28},{28,20},{32,40},... | collective-permute-start | bytes 3145736 | tf_op jit(solution)/shard_map/ppermute | solution.py:47
  70.4 8.2 %collective-permute-start.22 = (bf16[192,8192]{1,0:T(8,128)(2,1)S(1)}, bf16[192,8192]{1,0:T(8,128)(2,1)S(1)}, u32[]{:S(2)}, u32[]{:S(2)}) collective-permute-start(bf16[192,8192]{1,0:T(8,128)(2,1)S(1)} %get-tuple-element.80), channel_id=1, source_target_pairs={{0,8},{8,0},{4,12},{12,4},{16,24},{24,16},{20,28},{28,20},{32,40},... | collective-permute-start | bytes 9437192 | tf_op jit(solution)/shard_map/ppermute | solution.py:47
  73.9 3.9 %collective-permute-start.20 = (bf16[2,32,4096]{2,1,0:T(8,128)(2,1)S(1)}, bf16[2,32,4096]{2,1,0:T(8,128)(2,1)S(1)}, u32[]{:S(2)}, u32[]{:S(2)}) collective-permute-start(bf16[2,32,4096]{2,1,0:T(8,128)(2,1)S(1)} %collective-permute-done.17), channel_id=1, source_target_pairs={{0,8},{8,0},{4,12},{12,4},{16,24},{24,16},{20,28},{28,20},{32,40},... | collective-permute-start | bytes 1572872 | tf_op jit(solution)/shard_map/ppermute | solution.py:47
  74.4 4.2 %collective-permute-start.21 = (bf16[2,32,4096]{2,1,0:T(8,128)(2,1)S(1)}, bf16[2,32,4096]{2,1,0:T(8,128)(2,1)S(1)}, u32[]{:S(2)}, u32[]{:S(2)}) collective-permute-start(bf16[2,32,4096]{2,1,0:T(8,128)(2,1)S(1)} %collective-permute-done.18), channel_id=1, source_target_pairs={{0,8},{8,0},{4,12},{12,4},{16,24},{24,16},{20,28},{28,20},{32,40},... | collective-permute-start | bytes 1572872 | tf_op jit(solution)/shard_map/ppermute | solution.py:47
  74.6 14.7 %collective-permute-start.26 = (bf16[32,8192]{1,0:T(8,128)(2,1)S(1)}, bf16[32,8192]{1,0:T(8,128)(2,1)S(1)}, u32[]{:S(2)}, u32[]{:S(2)}) collective-permute-start(bf16[32,8192]{1,0:T(8,128)(2,1)S(1)} %get-tuple-element.123), channel_id=1, source_target_pairs={{0,96},{8,104},{4,100},{12,108},{16,112},{24,120},{20,116},{28,124... | collective-permute-start | bytes 1572872 | tf_op jit(solution)/shard_map/ppermute | solution.py:47
  75.1 15.8 %collective-permute-start.24 = (bf16[32,8192]{1,0:T(8,128)(2,1)S(1)}, bf16[32,8192]{1,0:T(8,128)(2,1)S(1)}, u32[]{:S(2)}, u32[]{:S(2)}) collective-permute-start(bf16[32,8192]{1,0:T(8,128)(2,1)S(1)} %get-tuple-element.122), channel_id=1, source_target_pairs={{0,32},{8,40},{4,36},{12,44},{16,48},{24,56},{20,52},{28,60},{32,6... | collective-permute-start | bytes 1572872 | tf_op jit(solution)/shard_map/ppermute | solution.py:47
  89.4 38.3 %collective-permute-start.27 = (bf16[64,8192]{1,0:T(8,128)(2,1)S(1)}, bf16[64,8192]{1,0:T(8,128)(2,1)S(1)}, u32[]{:S(2)}, u32[]{:S(2)}) collective-permute-start(bf16[64,8192]{1,0:T(8,128)(2,1)S(1)} %pad_maximum_fusion.2), channel_id=1, source_target_pairs={{0,96},{8,104},{4,100},{12,108},{16,112},{24,120},{20,116},{28,124... | collective-permute-start | bytes 3145736 | tf_op jit(solution)/shard_map/ppermute | solution.py:47
  91.1 36.7 %collective-permute-start.25 = (bf16[64,8192]{1,0:T(8,128)(2,1)S(1)}, bf16[64,8192]{1,0:T(8,128)(2,1)S(1)}, u32[]{:S(2)}, u32[]{:S(2)}) collective-permute-start(bf16[64,8192]{1,0:T(8,128)(2,1)S(1)} %pad_maximum_fusion.1), channel_id=1, source_target_pairs={{0,32},{8,40},{4,36},{12,44},{16,48},{24,56},{20,52},{28,60},{32,6... | collective-permute-start | bytes 3145736 | tf_op jit(solution)/shard_map/ppermute | solution.py:47
  92.0 16.1 %collective-permute-start.31 = (bf16[512,512]{1,0:T(8,128)(2,1)S(1)}, bf16[512,512]{1,0:T(8,128)(2,1)S(1)}, u32[]{:S(2)}, u32[]{:S(2)}) collective-permute-start(bf16[512,512]{1,0:T(8,128)(2,1)S(1)} %slice.184), channel_id=1, source_target_pairs={{0,4},{8,12},{4,0},{12,8},{16,20},{24,28},{20,16},{28,24},{32,36},... | collective-permute-start | bytes 1572872 | tf_op jit(solution)/shard_map/ppermute | solution.py:47
  93.0 14.6 %collective-permute-start.32 = (bf16[256,1024]{1,0:T(8,128)(2,1)S(1)}, bf16[256,1024]{1,0:T(8,128)(2,1)S(1)}, u32[]{:S(2)}, u32[]{:S(2)}) collective-permute-start(bf16[256,1024]{1,0:T(8,128)(2,1)S(1)} %get-tuple-element.119), channel_id=1, source_target_pairs={{0,1},{8,9},{4,5},{12,13},{16,17},{24,25},{20,21},{28,29},{32,33},... | collective-permute-start | bytes 1572872 | tf_op jit(solution)/shard_map/ppermute | solution.py:47
  94.2 13.7 %collective-permute-start.33 = (bf16[256,1024]{1,0:T(8,128)(2,1)S(1)}, bf16[256,1024]{1,0:T(8,128)(2,1)S(1)}, u32[]{:S(2)}, u32[]{:S(2)}) collective-permute-start(bf16[256,1024]{1,0:T(8,128)(2,1)S(1)} %get-tuple-element.118), channel_id=1, source_target_pairs={{0,3},{8,11},{4,7},{12,15},{16,19},{24,27},{20,23},{28,31},{32,35}... | collective-permute-start | bytes 1572872 | tf_op jit(solution)/shard_map/ppermute | solution.py:47
  108.1 16.1 %collective-permute-start.34 = (bf16[256,1024]{1,0:T(8,128)(2,1)S(1)}, bf16[256,1024]{1,0:T(8,128)(2,1)S(1)}, u32[]{:S(2)}, u32[]{:S(2)}) collective-permute-start(bf16[256,1024]{1,0:T(8,128)(2,1)S(1)} %slice.149), channel_id=1, source_target_pairs={{0,1},{8,9},{4,5},{12,13},{16,17},{24,25},{20,21},{28,29},{32,33},... | collective-permute-start | bytes 1572872 | tf_op jit(solution)/shard_map/ppermute | solution.py:47
  108.8 17.9 %collective-permute-start.35 = (bf16[256,1024]{1,0:T(8,128)(2,1)S(1)}, bf16[256,1024]{1,0:T(8,128)(2,1)S(1)}, u32[]{:S(2)}, u32[]{:S(2)}) collective-permute-start(bf16[256,1024]{1,0:T(8,128)(2,1)S(1)} %slice.150), channel_id=1, source_target_pairs={{0,3},{8,11},{4,7},{12,15},{16,19},{24,27},{20,23},{28,31},{32,35}... | collective-permute-start | bytes 1572872 | tf_op jit(solution)/shard_map/ppermute | solution.py:47
  112.6 20.4 %collective-permute-start.37 = (bf16[256,1024]{1,0:T(8,128)(2,1)S(1)}, bf16[256,1024]{1,0:T(8,128)(2,1)S(1)}, u32[]{:S(2)}, u32[]{:S(2)}) collective-permute-start(bf16[256,1024]{1,0:T(8,128)(2,1)S(1)} %add_convert_fusion.4), channel_id=1, source_target_pairs={{0,1},{8,9},{4,5},{12,13},{16,17},{24,25},{20,21},{28,29},{32,33},... | collective-permute-start | bytes 1572872 | tf_op jit(solution)/shard_map/ppermute | solution.py:47
  124.2 11.5 %collective-permute-start.38 = (bf16[256,1024]{1,0:T(8,128)(2,1)S(1)}, bf16[256,1024]{1,0:T(8,128)(2,1)S(1)}, u32[]{:S(2)}, u32[]{:S(2)}) collective-permute-start(bf16[256,1024]{1,0:T(8,128)(2,1)S(1)} %add_convert_fusion.3), channel_id=1, source_target_pairs={{0,3},{8,11},{4,7},{12,15},{16,19},{24,27},{20,23},{28,31},{32,35}... | collective-permute-start | bytes 1572872 | tf_op jit(solution)/shard_map/ppermute | solution.py:47
  126.6 6.0 %collective-permute-start.36 = (f32[56,512]{1,0:T(8,128)S(1)}, f32[56,512]{1,0:T(8,128)S(1)}, u32[]{:S(2)}, u32[]{:S(2)}) collective-permute-start(f32[56,512]{1,0:T(8,128)S(1)} %get-tuple-element.99), channel_id=1, source_target_pairs={{0,4},{8,12},{4,0},{12,8},{16,20},{24,28},{20,16},{28,24},{32,36},... | collective-permute-start | bytes 344072 | tf_op jit(solution)/shard_map/ppermute | solution.py:47
  129.6 11.3 %collective-permute-start.29 = (bf16[32,4096]{1,0:T(8,128)(2,1)S(1)}, bf16[32,4096]{1,0:T(8,128)(2,1)S(1)}, u32[]{:S(2)}, u32[]{:S(2)}) collective-permute-start(bf16[32,4096]{1,0:T(8,128)(2,1)S(1)} %get-tuple-element.121), channel_id=1, source_target_pairs={{0,20},{8,28},{4,0},{12,8},{16,4},{24,12},{20,16},{28,24},{32,52},... | collective-permute-start | bytes 786440 | tf_op jit(solution)/shard_map/ppermute | solution.py:47
  131.3 20.4 %collective-permute-start.28 = (bf16[32,4096]{1,0:T(8,128)(2,1)S(1)}, bf16[32,4096]{1,0:T(8,128)(2,1)S(1)}, u32[]{:S(2)}, u32[]{:S(2)}) collective-permute-start(bf16[32,4096]{1,0:T(8,128)(2,1)S(1)} %get-tuple-element.120), channel_id=1, source_target_pairs={{0,16},{8,24},{4,20},{12,28},{16,0},{24,8},{20,4},{28,12},{32,48},... | collective-permute-start | bytes 786440 | tf_op jit(solution)/shard_map/ppermute | solution.py:47
  135.7 8.8 %collective-permute-start.39 = (f32[72,512]{1,0:T(8,128)S(1)}, f32[72,512]{1,0:T(8,128)S(1)}, u32[]{:S(2)}, u32[]{:S(2)}) collective-permute-start(f32[72,512]{1,0:T(8,128)S(1)} %pad_maximum_fusion.4.refs_7_), channel_id=1, source_target_pairs={{0,1},{8,9},{4,5},{12,13},{16,17},{24,25},{20,21},{28,29},{32,33},... | collective-permute-start | bytes 442376 | tf_op jit(solution)/shard_map/ppermute | solution.py:47
  135.9 9.7 %collective-permute-start.40 = (f32[72,512]{1,0:T(8,128)S(1)}, f32[72,512]{1,0:T(8,128)S(1)}, u32[]{:S(2)}, u32[]{:S(2)}) collective-permute-start(f32[72,512]{1,0:T(8,128)S(1)} %pad_maximum_fusion.4.refs_7_), channel_id=1, source_target_pairs={{0,2},{8,10},{4,6},{12,14},{16,18},{24,26},{20,22},{28,30},{32,34}... | collective-permute-start | bytes 442376 | tf_op jit(solution)/shard_map/ppermute | solution.py:47
  140.9 5.1 %collective-permute-start.41 = (f32[72,512]{1,0:T(8,128)S(1)}, f32[72,512]{1,0:T(8,128)S(1)}, u32[]{:S(2)}, u32[]{:S(2)}) collective-permute-start(f32[72,512]{1,0:T(8,128)S(1)} %pad_maximum_fusion.4.refs_7_), channel_id=1, source_target_pairs={{0,3},{8,11},{4,7},{12,15},{16,19},{24,27},{20,23},{28,31},{32,35}... | collective-permute-start | bytes 442376 | tf_op jit(solution)/shard_map/ppermute | solution.py:47
  140.9 10.8 %collective-permute-start.30 = (bf16[32,4096]{1,0:T(8,128)(2,1)S(1)}, bf16[32,4096]{1,0:T(8,128)(2,1)S(1)}, u32[]{:S(2)}, u32[]{:S(2)}) collective-permute-start(bf16[32,4096]{1,0:T(8,128)(2,1)S(1)} %collective-permute-done.29), channel_id=1, source_target_pairs={{0,20},{8,28},{4,0},{12,8},{16,4},{24,12},{20,16},{28,24},{32,52},... | collective-permute-start | bytes 786440 | tf_op jit(solution)/shard_map/ppermute | solution.py:47
  (7 other events, 70.2 us)

commit v4 on v3

--- a/solution.py
+++ b/solution.py
@@ -10,6 +10,7 @@
 from jax.sharding import PartitionSpec as P
 
 RING = 4
+MAIN, OTHER = (1, -1), (-1, 1)
 SUBS = 8
 LANES = 128
 F32 = jnp.float32
@@ -42,9 +43,16 @@
 def hop(value, x=0, y=0, z=0, core=0, pair=0):
     moves = []
     for i, j, k, c in itertools.product(range(RING), range(RING), range(RING), range(2)):
-        there = ((i + x) % RING, (j + y) % RING, ((k + z) % RING) ^ pair, c ^ core)
+        dx, dy, dz = (step[c] if isinstance(step, tuple) else step for step in (x, y, z))
+        if None in (dx, dy, dz):
+            continue
+        there = ((i + dx) % RING, (j + dy) % RING, ((k + dz) % RING) ^ pair, c ^ core)
         moves.append(tuple(((b * 2 + d // 2) * 2 + e) * 2 * RING + d % 2 * RING + a for a, b, d, e in ((i, j, k, c), there)))
     return lax.ppermute(value, ("chan", "seq"), moves)
+
+
+def by_core(first, second):
+    return jnp.where(places()[2] == 0, first, second)
 
 
 def gather_z(cotangent):
@@ -60,15 +68,14 @@
     return jnp.stack([stack, other])
 
 
-def place_blocks(*sides):
+def place_blocks(*blocks):
     y, _, core, _, _ = places()
-    _, tokens, half = sides[0][0].shape
+    _, _, tokens, half = blocks[0].shape
     whole = jnp.zeros((2, RING, 2, 2, tokens, half), BF16)
-    for step, blocks in zip((0, RING - 1, 1, 2), zip(*sides)):
-        row = lax.rem(y + step, RING)
-        for side, block in enumerate(blocks):
-            for part, at_core in ((block, core), (hop(block, core=1), 1 - core)):
-                whole = lax.dynamic_update_slice(whole, part[None, None, :, None], (side, row, 0, at_core, 0, 0))
+    for block, steps in zip(blocks, ((0, 0), (RING - 1, 1), (1, RING - 1), (2, 2))):
+        for part, at_core in ((block, core), (hop(block, core=1), 1 - core)):
+            row = lax.rem(y + jnp.where(at_core == 0, *steps), RING)
+            whole = lax.dynamic_update_slice(whole, part[:, None, :, None], (0, row, 0, at_core, 0, 0))
     return whole
 
 
@@ -103,10 +110,9 @@
     )(turned, out_weight)
 
 
-def weigh(gated, cot_rows, scale, r):
+def weigh(gated, cot_rows, scale, block):
     width = cot_rows.shape[1] // RING
-    first = lax.rem(places()[4] + r, RING) * width
-    columns = lax.dynamic_slice(cot_rows, (0, first), (cot_rows.shape[0], width))
+    columns = lax.dynamic_slice(cot_rows, (0, block * width), (cot_rows.shape[0], width))
     product = lax.dot_general(gated, columns, (((0,), (0,)), ((), ())), preferred_element_type=F32)
     return (product * scale).astype(BF16)
 
@@ -199,7 +205,10 @@
     y, high, core, _, _ = places()
     for i in range(RING * 4):
         on = lax.rem(i // 4 + RING - y, RING)
-        there = lax.rem(i % 2 + core, 2) * RING + jnp.where(on == 0, 3, jnp.where(on == 2, 0, (on + 1) // 2))
+        kept = lax.rem(i % 2 + core, 2) == 0
+        first = jnp.where(kept, 1 + 2 * core, 3 - 2 * core)
+        there = jnp.where(on == 0, 3, jnp.where(on == 2, 0, jnp.where(on == first, 1, 2)))
+        there = there + jnp.where(kept, 0, RING)
         there = there * 2 + lax.rem(i // 2 % 2 + high, 2)
         turned_ref[pl.ds(pl.multiple_of(there * part, part), part)] = gated_ref[pl.ds(i * part, part)]
 
@@ -350,7 +359,7 @@
     table = (modes, channels)
 
     block, log_first = together(gather_z(cotangent), log_decay)
-    before_own, after_other = hop(block[0], y=1), hop(block[1], y=-1)
+    main_block, other_block = hop(block, y=MAIN), hop(block, y=OTHER)
     ends, subs, driving = call(
         forward_ends,
         (key_proj, value_proj, log_first),
@@ -360,8 +369,6 @@
         "forward_ends",
     )
     ends_pair = jnp.concatenate([ends, hop(ends, pair=1)])
-    before_own, after_other, ends_pair = together(before_own, after_other, ends_pair)
-    before_other, after_own = hop(block[1], y=1), hop(block[0], y=-1)
     earlier = spread_over_x(ends_pair)
     gated, turned, pre_gate, lead = call(
         forward_full,
@@ -371,48 +378,38 @@
         0.1,
         "forward_full",
     )
-    before_own, after_other, turned = together(before_own, after_other, turned)
-    far_own, far_other = hop(before_own, y=1), hop(after_other, y=-1)
-    before_other, after_own, turned = together(before_other, after_own, turned)
+    main_block, other_block, turned = together(main_block, other_block, turned)
+    far_block = hop(main_block, y=MAIN)
     near_first, near_rest, far_first, far_rest = project(turned, out_weight)
+    far_block, far_first, gated_other = together(far_block, far_first, hop(gated, pair=1))
     got_first, got_rest = hop(far_first, core=1), hop(far_rest, core=1)
-    gated_pair = jnp.concatenate([gated, hop(gated, pair=1)])
+    gated_pair = jnp.concatenate([gated, gated_other])
     opposite = add(near_first, got_first).astype(BF16)
-    far_own, far_other, opposite = together(far_own, far_other, opposite)
-    cot_rows = place_blocks(
-        (block[0], before_own, after_own, far_own), (block[1], before_other, after_other, far_other)
-    )
+    cot_rows = place_blocks(block, main_block, other_block, far_block)
     cot_rows, got_rest = together(cot_rows.reshape(2 * length, -1), got_rest)
 
+    _, _, core, low, x = places()
     half = out_weight.shape[1] // 2
-    low_weight = lax.dynamic_slice(out_weight, (0, places()[3] * half), (channels, half))
-    weights = {2: weigh(gated_pair, cot_rows, scale, 2)}
-    cot_rows, weights[2] = together(cot_rows, weights[2])
+    low_weight = lax.dynamic_slice(out_weight, (0, low * half), (channels, half))
     grad_parts = lax.dot_general(cot_rows, low_weight, (((1,), (1,)), ((), ())), preferred_element_type=F32)
-    cot_rows, grad_parts, got_rest = together(cot_rows, grad_parts, got_rest)
+    cot_rows, grad_parts = together(cot_rows, grad_parts)
     theirs = hop(grad_parts[length:].astype(BF16), pair=1)
-    part = opposite.shape[0] // 2
-    low_sum, high_sum = hop(opposite[:part], y=1), hop(opposite[part:], y=-1)
-    above, below, own = (
-        add(near_rest[i * 2 * part : (i + 1) * 2 * part], got_rest[i * 2 * part : (i + 1) * 2 * part]) for i in range(3)
-    )
-    above = jnp.concatenate([add(above[:part], low_sum), above[part:]]).astype(BF16)
-    below = jnp.concatenate([below[:part], add(below[part:], high_sum)]).astype(BF16)
-    for r in (1, 3, 0):
-        weights[r] = weigh(gated_pair, cot_rows, scale, r)
-    cut = channels // 2
-    upper, lower = hop(weights[2][:cut], x=1), hop(weights[2][cut:], x=-1)
-    up_sum = add(weights[1][:cut], upper).astype(BF16)
-    down_sum = add(weights[3][cut:], lower).astype(BF16)
-    up_rest, down_rest = weights[1][cut:], weights[3][:cut]
-    theirs, up_sum, down_sum, up_rest, down_rest = together(theirs, up_sum, down_sum, up_rest, down_rest)
-    up_rest, down_rest = hop(up_rest, x=1), hop(down_rest, x=-1)
+
+    far_weight = weigh(gated_pair, cot_rows, scale, lax.rem(x + 2, RING))
+    cot_rows, far_weight, got_rest = together(cot_rows, far_weight, got_rest)
+    main_weight, other_weight, own_weight = (
+        weigh(gated_pair, cot_rows, scale, lax.rem(x + r, RING)) for r in (1 + 2 * core, 3 - 2 * core, 0)
+    )
+    main_weight = add(main_weight, hop(far_weight, x=MAIN)).astype(BF16)
+
+    main, other, own = (add(a, b) for a, b in zip(jnp.split(near_rest, 3), jnp.split(got_rest, 3)))
+    main = add(main, hop(opposite, y=MAIN)).astype(BF16)
+    other = other.astype(BF16)
+
+    theirs, main_weight, other_weight, main, other = together(theirs, main_weight, other_weight, main, other)
     grad_gated = add(grad_parts[:length], theirs)
-    own = add(own, hop(above, y=1), hop(below, y=-1))
-    leaving = own[part:].astype(BF16)
-    width = leaving.shape[1] // 2
-    halfway = hop(leaving[:, width:], z=-1)
-    crossed = hop(leaving[:, :width], z=2)
+    main, other = hop(main, y=MAIN), hop(other, y=OTHER)
+    main_weight, other_weight = hop(main_weight, x=MAIN), hop(other_weight, x=OTHER)
 
     grad_query, back, sums, back_subs = call(
         backward_ends,
@@ -422,17 +419,16 @@
         2.0,
         "backward_ends",
     )
-    sums, up_rest, down_rest = together(sums, up_rest, down_rest)
-    up_sum, down_sum = hop(up_sum, x=1), hop(down_sum, x=-1)
     others = hop(sums, pair=1)
+    others, main, other, main_weight, other_weight = together(others, main, other, main_weight, other_weight)
+    own = add(own, main, other)
+    part = own.shape[0] // 2
+    leaving = hop(own[part:].astype(BF16), z=(2, -1))
     sums_pair = jnp.concatenate([sums[:modes], others[:modes], sums[modes:] + others[modes:]])
-    sums_pair, up_sum, down_sum = together(sums_pair, up_sum, down_sum)
-    crossed = jnp.concatenate([crossed, hop(halfway, z=-1)], axis=1)
-    mixed = add(own[:part], crossed).astype(BF16)
     all_sums = spread_over_x(sums_pair)
-    grad_weight = jnp.concatenate(
-        [add(weights[0][:cut], up_sum, down_rest), add(weights[0][cut:], up_rest, down_sum)]
-    ).astype(BF16)
+    leaving, *_ = together(leaving, *all_sums[1:])
+    mixed = add(own[:part], by_core(leaving, hop(leaving, z=(None, -1)))).astype(BF16)
+    grad_weight = add(own_weight, main_weight, other_weight).astype(BF16)
     grad_key, grad_value, grad_residue, grad_decay, grad_skip = call(
         functools.partial(backward_full, scale=scale),
         (key_proj, value_proj, back, back_subs, log_decay, residue, skip_row, *all_sums),

time: 153 us -> 170 us (1.11); the launches traced: 153 us -> 167 us
  waiting for transfers between devices: 36.2 us -> 51.5 us
  starting transfers between devices: 51 us -> 39 us
  matrix products: 10.6 us -> 17.1 us
  local copies, waits for them, and re-layouts: 15.6 us -> 21.5 us
    ppermute x42 -> x30, waiting for transfers between devices: 36.2 us -> 51.5 us  [hop(): return lax.ppermute(value, ('chan', 'seq'), moves)]
    ppermute x42 -> x30, starting transfers between devices: 51 us -> 39 us  [hop(): return lax.ppermute(value, ('chan', 'seq'), moves)]
    dynamic_update_slice x16 -> x8, local copies, waits for them, and re-layouts: 6.98 us -> 12.2 us  [place_blocks(): lax.dynamic_update_slice(whole, part[:, None, :, None], (0, row, 0, at_co...]
    broadcast_in_dim x1, local copies, waits for them, and re-layouts: 1.04 us -> 5.3 us  [place_blocks(): whole = jnp.zeros((2, RING, 2, 2, tokens, half), BF16)]
    dot_general x4, matrix products: 6.09 us -> 10.2 us  [weigh(): lax.dot_general(gated, columns, (((0,), (0,)), ((), ())), preferred_eleme...]
    convert_element_type x3, other arithmetic: 1.3 us -> 4.28 us  [the longest x1 1.99 us: local(): add(own[:part], by_core(leaving, hop(leaving, z=(None, -1)))).astype(BF16)]
    another operation x4 -> x0, other arithmetic: 2.58 us -> none
    dot_general x1, matrix products: 4.52 us -> 6.93 us  [local(): lax.dot_general(cot_rows, low_weight, (((1,), (1,)), ((), ())), preferred...]
  transfers between devices with their start and end apart: 42 -> 30, of which waited for: 16 -> 14; matrix products, arithmetic and copies ran while one was open for 19% -> 23% of each run, Pallas kernels for 20% -> 16%
where the time goes in v4:
time: 170 us; the launch traced here: 167 us
  waiting for transfers between devices  51.5 us (30%)
  starting transfers between devices  39 us (23%)
  Pallas kernels  30 us (18%)
  local copies, waits for them, and re-layouts  21.5 us (13%)
  matrix products  17.1 us (10%)
  other arithmetic  6.46 us (4%)
    ppermute x30, waiting for transfers between devices, hop(): return lax.ppermute(value, ('chan', 'seq'), moves)  51.5 us
    ppermute x30, starting transfers between devices, hop(): return lax.ppermute(value, ('chan', 'seq'), moves)  39 us
    pallas_call x4, Pallas kernels, call(): pl.pallas_call(body, out_shape=[jax.ShapeDtypeStruct(o.shape, o.dtype) fo...  23.1 us
    dynamic_update_slice x8, local copies, waits for them, and re-layouts, place_blocks(): lax.dynamic_update_slice(whole, part[:, None, :, None], (0, row, 0, at_co...  12.2 us
    dot_general x4, matrix products, weigh(): lax.dot_general(gated, columns, (((0,), (0,)), ((), ())), preferred_eleme...  10.2 us
    dot_general x1, matrix products, local(): lax.dot_general(cot_rows, low_weight, (((1,), (1,)), ((), ())), preferred...  6.93 us
    pallas_call x1, Pallas kernels, project(): pl.pallas_call(project_tile, grid=(width // tile,), out_shape=[jax.ShapeD...  6.86 us
    broadcast_in_dim x1, local copies, waits for them, and re-layouts, place_blocks(): whole = jnp.zeros((2, RING, 2, 2, tokens, half), BF16)  5.3 us
  transfers between devices with their start and end apart: 30, of which 14 were waited for; matrix products, arithmetic and copies ran while one was open for 23% of the time, Pallas kernels for 16%

profile of v4, /device:TPU:0, one launch (start us, length us, event | category | flops | bytes accessed | tf_op | source)
XLA Modules:
  0.0 166.6 jit_solution(4396463818949340666)
XLA Ops:
  1.7 2.1 %collective-permute-start.1 = (bf16[32,4096]{1,0:T(8,128)(2,1)S(1)}, bf16[32,4096]{1,0:T(8,128)(2,1)S(1)}, u32[]{:S(2)}, u32[]{:S(2)}) collective-permute-start(bf16[32,4096]{1,0:T(8,128)(2,1)S(1)} %get-tuple-element.103), channel_id=1, source_target_pairs={{0,4},{8,12},{4,16},{12,24},{16,20},{24,28},{20,0},{28,8},{32,36},... | collective-permute-start | bytes 786440 | tf_op jit(solution)/shard_map/ppermute | solution.py:51
  3.8 2.2 %collective-permute-start.2 = (bf16[32,4096]{1,0:T(8,128)(2,1)S(1)}, bf16[32,4096]{1,0:T(8,128)(2,1)S(1)}, u32[]{:S(2)}, u32[]{:S(2)}) collective-permute-start(bf16[32,4096]{1,0:T(8,128)(2,1)S(1)} %get-tuple-element.103), channel_id=1, source_target_pairs={{0,20},{8,28},{4,0},{12,8},{16,4},{24,12},{20,16},{28,24},{32,52},... | collective-permute-start | bytes 786440 | tf_op jit(solution)/shard_map/ppermute | solution.py:51
  6.0 1.8 %collective-permute-start = (bf16[32,4096]{1,0:T(8,128)(2,1)S(1)}, bf16[32,4096]{1,0:T(8,128)(2,1)S(1)}, u32[]{:S(2)}, u32[]{:S(2)}) collective-permute-start(bf16[32,4096]{1,0:T(8,128)(2,1)S(1)} %get-tuple-element.102), channel_id=1, source_target_pairs={{0,16},{8,24},{4,20},{12,28},{16,0},{24,8},{20,4},{28,12},{32,48},... | collective-permute-start | bytes 786440 | tf_op jit(solution)/shard_map/ppermute | solution.py:51
  7.8 4.4 %collective-permute-done.1 = bf16[32,4096]{1,0:T(8,128)(2,1)S(1)} collective-permute-done((bf16[32,4096]{1,0:T(8,128)(2,1)S(1)}, bf16[32,4096]{1,0:T(8,128)(2,1)S(1)}, u32[]{:S(2)}, u32[]{:S(2)}) %collective-permute-start.1) | collective-permute-done | bytes 262176 | tf_op jit(solution)/shard_map/ppermute | solution.py:51
  12.2 5.0 %collective-permute-done.2 = bf16[32,4096]{1,0:T(8,128)(2,1)S(1)} collective-permute-done((bf16[32,4096]{1,0:T(8,128)(2,1)S(1)}, bf16[32,4096]{1,0:T(8,128)(2,1)S(1)}, u32[]{:S(2)}, u32[]{:S(2)}) %collective-permute-start.2) | collective-permute-done | bytes 262176 | tf_op jit(solution)/shard_map/ppermute | solution.py:51
  17.4 1.6 collective-permute-done
  20.2 3.6 %forward_ends.1 = (f32[32,512]{1,0:T(8,128)S(1)}, f32[4,256,128]{2,1,0:T(8,128)S(1)}, f32[4,512,128]{2,1,0:T(8,128)S(1)}) custom-call(bf16[512,512]{1,0:T(8,128)(2,1)S(1)} %copy-done, bf16[512,512]{1,0:T(8,128)(2,1)S(1)} %copy-done.1, f32[16,512]{1,0:T(8,128)S(1)} %copy-done.3), custom_call_target="tpu_custom_call" | custom-call | flops 115000000 | tf_op jit(solution)/shard_map/forward_ends/pallas_call | solution.py:326
  23.8 1.2 collective-permute-start.5
  25.0 3.1 %collective-permute-done.5 = f32[32,512]{1,0:T(8,128)S(1)} collective-permute-done((f32[32,512]{1,0:T(8,128)S(1)}, f32[32,512]{1,0:T(8,128)S(1)}, u32[]{:S(2)}, u32[]{:S(2)}) %collective-permute-start.5) | collective-permute-done | bytes 65568 | tf_op jit(solution)/shard_map/ppermute | solution.py:51
  28.1 1.5 collective-permute-start.6
  29.6 1.6 collective-permute-start.3
  31.2 1.7 collective-permute-start.4
  32.8 2.7 %collective-permute-start.7 = (f32[64,512]{1,0:T(8,128)S(1)}, f32[64,512]{1,0:T(8,128)S(1)}, u32[]{:S(2)}, u32[]{:S(2)}) collective-permute-start(f32[64,512]{1,0:T(8,128)S(1)} %constant_dynamic-update-slice_fusion.refs_6_), channel_id=1, source_target_pairs={{0,2},{8,10},{4,6},{12,14},{16,18},{24,26},{20,22},{28,30},{32,34}... | collective-permute-start | bytes 393224 | tf_op jit(solution)/shard_map/ppermute | solution.py:51
  35.6 1.4 collective-permute-start.8
  37.0 5.3 %broadcast_in_dim.27 = bf16[2,4,2,2,32,4096]{5,4,3,2,1,0:T(8,128)(2,1)} broadcast(bf16[]{:T(256)} %constant.80.clone.1), dimensions={} | broadcast | bytes 8388610 | tf_op jit(solution)/shard_map/broadcast_in_dim | solution.py:74
  43.8 4.0 %forward_full.1 = (bf16[512,512]{1,0:T(8,128)(2,1)S(1)}, bf16[512,512]{1,0:T(8,128)(2,1)S(1)}, f32[4,512,128]{2,1,0:T(8,128)S(1)}, f32[4,256,128]{2,1,0:T(8,128)S(1)}) custom-call(bf16[512,512]{1,0:T(8,128)(2,1)S(1)} %copy-done.2, f32[4,512,128]{2,1,0:T(8,128)S(1)} %get-tuple-element.56.refs_1_.drive_ref, f32[4,256,128]{2,1,0:T(8,128)S(1)} %get-tuple-element.57.refs_2_, ...), custom_call_target="tpu_custom_call" | custom-call | flops 115000000 | tf_op jit(solution)/shard_map/forward_full/pallas_call | solution.py:326
  47.9 1.2 collective-permute-start.13
  49.1 5.7 %collective-permute-done.3 = bf16[2,2,32,4096]{3,2,1,0:T(8,128)(2,1)} collective-permute-done((bf16[2,2,32,4096]{3,2,1,0:T(8,128)(2,1)}, bf16[2,2,32,4096]{3,2,1,0:T(8,128)(2,1)}, u32[]{:S(2)}, u32[]{:S(2)}) %collective-permute-start.3) | collective-permute-done | bytes 1048608 | tf_op jit(solution)/shard_map/ppermute | solution.py:51
  54.8 1.2 collective-permute-done.4
  57.5 2.4 %collective-permute-start.11 = (bf16[2,2,32,4096]{3,2,1,0:T(8,128)(2,1)}, bf16[2,2,32,4096]{3,2,1,0:T(8,128)(2,1)S(1)}, u32[]{:S(2)}, u32[]{:S(2)}) collective-permute-start(bf16[2,2,32,4096]{3,2,1,0:T(8,128)(2,1)} %collective-permute-done.4), channel_id=1, source_target_pairs={{0,8},{8,0},{4,12},{12,4},{16,24},{24,16},{20,28},{28,20},{32,40},... | collective-permute-start | bytes 3145736 | tf_op jit(solution)/shard_map/ppermute | solution.py:51
  60.0 6.9 %project.1 = (bf16[64,8192]{1,0:T(8,128)(2,1)S(1)}, bf16[192,8192]{1,0:T(8,128)(2,1)S(1)}, bf16[64,8192]{1,0:T(8,128)(2,1)S(1)}, bf16[192,8192]{1,0:T(8,128)(2,1)S(1)}) custom-call(bf16[512,512]{1,0:T(8,128)(2,1)S(1)} %get-tuple-element.60.rows_ref, bf16[512,8192]{1,0:T(8,128)(2,1)S(1)} %copy-done.6), custom_call_target="tpu_custom_call" | custom-call | flops 4294967296 | bytes 16777216 | tf_op jit(solution)/shard_map/project/pallas_call | solution.py:99
  66.9 2.3 %bitcast_dynamic-update-slice_fusion.5 = bf16[2,4,2,2,32,4096]{5,4,3,2,1,0:T(8,128)(2,1)} fusion(bf16[2,4,2,2,32,4096]{5,4,3,2,1,0:T(8,128)(2,1)} %bitcast_dynamic-update-slice_fusion.6, s32[]{:T(128)S(6)} %select_n.137, s32[]{:T(128)S(6)} %select_n.139, bf16[2,2,32,4096]{3,2,1,0:T(8,128)(2,1)} %collective-permute-done.9), kind=kLoop, calls=%fused_computation.30 | loop fusion | bytes 2097160 | tf_op jit(solution)/shard_map/dynamic_update_slice | solution.py:78
  69.2 2.3 %bitcast_dynamic-update-slice_fusion.4 = bf16[2,4,2,2,32,4096]{5,4,3,2,1,0:T(8,128)(2,1)} fusion(bf16[2,4,2,2,32,4096]{5,4,3,2,1,0:T(8,128)(2,1)} %bitcast_dynamic-update-slice_fusion.5, s32[]{:T(128)S(6)} %select_n.141, s32[]{:T(128)S(6)} %select_n.138, bf16[2,2,32,4096]{3,2,1,0:T(8,128)(2,1)} %collective-permute-done.3), kind=kLoop, calls=%fused_computation.29 | loop fusion | bytes 2097160 | tf_op jit(solution)/shard_map/dynamic_update_slice | solution.py:78
  71.6 1.6 collective-permute-done.12
  74.8 2.3 %bitcast_dynamic-update-slice_fusion.2 = bf16[2,4,2,2,32,4096]{5,4,3,2,1,0:T(8,128)(2,1)} fusion(bf16[2,4,2,2,32,4096]{5,4,3,2,1,0:T(8,128)(2,1)} %bitcast_dynamic-update-slice_fusion.3, s32[]{:T(128)S(6)} %select_n.145, s32[]{:T(128)S(6)} %select_n.138, bf16[2,2,32,4096]{3,2,1,0:T(8,128)(2,1)} %collective-permute-done.4), kind=kLoop, calls=%fused_computation.27 | loop fusion | bytes 2097160 | tf_op jit(solution)/shard_map/dynamic_update_slice | solution.py:78
  77.1 1.1 bitcast_dynamic-update-slice_fusion.1
  80.8 6.9 %fusion = f32[1024,512]{1,0:T(8,128)S(1)} fusion(bf16[1024,4096]{1,0:T(8,128)(2,1)} %bitcast.46, bf16[512,8192]{1,0:T(8,128)(2,1)S(1)} %copy-done.6, s32[]{:T(128)S(6)} %select_n.129), kind=kOutput, calls=%fused_computation | convolution fusion | flops 4294967296 | bytes 14680068 | tf_op jit(solution)/shard_map/dot_general | solution.py:394
  87.9 1.2 collective-permute-start.16
  89.1 3.5 %multiply_convert_fusion.3 = bf16[512,1024]{1,0:T(8,128)(2,1)S(1)} fusion(bf16[1024,512]{1,0:T(8,128)(2,1)S(1)} %constant_dynamic-update-slice_fusion.2, bf16[1024,4096]{1,0:T(8,128)(2,1)} %bitcast.47, s32[]{:T(128)S(6)} %select_n.149), kind=kOutput, calls=%fused_computation.17 | convolution fusion | flops 1074790400 | bytes 4194308 | tf_op jit(solution)/shard_map/dot_general | solution.py:116
  92.6 1.6 collective-permute-start.17
  94.1 1.7 collective-permute-done.19
  96.5 2.2 %multiply_convert_fusion.1 = bf16[512,1024]{1,0:T(8,128)(2,1)} fusion(bf16[1024,512]{1,0:T(8,128)(2,1)S(1)} %constant_dynamic-update-slice_fusion.2, bf16[1024,4096]{1,0:T(8,128)(2,1)S(1)} %bitcast.51, s32[]{:T(128)S(6)} %select_n.151), kind=kOutput, calls=%fused_computation.10 | convolution fusion | flops 1074790400 | bytes 4194308 | tf_op jit(solution)/shard_map/dot_general | solution.py:116
  98.7 9.9 %collective-permute-done.17 = bf16[512,1024]{1,0:T(8,128)(2,1)S(1)} collective-permute-done((bf16[512,1024]{1,0:T(8,128)(2,1)S(1)}, bf16[512,1024]{1,0:T(8,128)(2,1)S(1)}, u32[]{:S(2)}, u32[]{:S(2)}) %collective-permute-start.17) | collective-permute-done | bytes 1048608 | tf_op jit(solution)/shard_map/ppermute | solution.py:51
  108.6 1.3 add_convert_fusion.4
  110.7 2.6 %collective-permute-start.22 = (bf16[64,8192]{1,0:T(8,128)(2,1)S(1)}, bf16[64,8192]{1,0:T(8,128)(2,1)S(1)}, u32[]{:S(2)}, u32[]{:S(2)}) collective-permute-start(bf16[64,8192]{1,0:T(8,128)(2,1)S(1)} %get-tuple-element.83), channel_id=1, source_target_pairs={{0,96},{8,40},{4,100},{12,44},{16,112},{24,56},{20,116},{28,60},{3... | collective-permute-start | bytes 3145736 | tf_op jit(solution)/shard_map/ppermute | solution.py:51
  113.6 3.0 %collective-permute-start.24 = (bf16[512,1024]{1,0:T(8,128)(2,1)}, bf16[512,1024]{1,0:T(8,128)(2,1)S(1)}, u32[]{:S(2)}, u32[]{:S(2)}) collective-permute-start(bf16[512,1024]{1,0:T(8,128)(2,1)} %multiply_convert_fusion.1), channel_id=1, source_target_pairs={{0,3},{8,9},{4,7},{12,13},{16,19},{24,25},{20,23},{28,29},{32,35},... | collective-permute-start | bytes 3145736 | tf_op jit(solution)/shard_map/ppermute | solution.py:51
  116.7 10.5 %backward_ends.1 = (bf16[512,512]{1,0:T(8,128)(2,1)}, f32[4,512,128]{2,1,0:T(8,128)S(1)}, f32[56,512]{1,0:T(8,128)S(1)}, f32[4,128,128]{2,1,0:T(8,128)S(1)}) custom-call(f32[512,512]{1,0:T(8,128)S(1)} %convert_add_fusion.1.grad_ref, bf16[512,512]{1,0:T(8,128)(2,1)S(1)} %copy-done.2, f32[4,512,128]{2,1,0:T(8,128)S(1)} %get-tuple-element.79.pre_ref, ...), custom_call_target="tpu_custom_call" | custom-call | flops 2300000000 | tf_op jit(solution)/shard_map/backward_ends/pallas_call | solution.py:326
  128.0 4.0 %collective-permute-done.20 = f32[56,512]{1,0:T(8,128)S(1)} collective-permute-done((f32[56,512]{1,0:T(8,128)S(1)}, f32[56,512]{1,0:T(8,128)S(1)}, u32[]{:S(2)}, u32[]{:S(2)}) %collective-permute-start.20) | collective-permute-done | bytes 114720 | tf_op jit(solution)/shard_map/ppermute | solution.py:51
  132.0 3.6 %collective-permute-done.21 = bf16[64,8192]{1,0:T(8,128)(2,1)S(1)} collective-permute-done((bf16[64,8192]{1,0:T(8,128)(2,1)S(1)}, bf16[64,8192]{1,0:T(8,128)(2,1)S(1)}, u32[]{:S(2)}, u32[]{:S(2)}) %collective-permute-start.21) | collective-permute-done | bytes 1048608 | tf_op jit(solution)/shard_map/ppermute | solution.py:51
  135.6 4.0 %collective-permute-done.23 = bf16[512,1024]{1,0:T(8,128)(2,1)S(1)} collective-permute-done((bf16[512,1024]{1,0:T(8,128)(2,1)S(1)}, bf16[512,1024]{1,0:T(8,128)(2,1)S(1)}, u32[]{:S(2)}, u32[]{:S(2)}) %collective-permute-start.23) | collective-permute-done | bytes 1048608 | tf_op jit(solution)/shard_map/ppermute | solution.py:51
  141.8 2.4 %collective-permute-start.25 = (bf16[32,8192]{1,0:T(8,128)(2,1)}, bf16[32,8192]{1,0:T(8,128)(2,1)}, u32[]{:S(2)}, u32[]{:S(2)}) collective-permute-start(bf16[32,8192]{1,0:T(8,128)(2,1)} %slice.49), channel_id=1, source_target_pairs={{0,16},{8,28},{4,20},{12,8},{16,0},{24,12},{20,4},{28,24},{32,48},... | collective-permute-start | bytes 1572872 | tf_op jit(solution)/shard_map/ppermute | solution.py:51
  144.4 1.2 collective-permute-start.27
  145.5 2.1 %collective-permute-start.28 = (f32[72,512]{1,0:T(8,128)S(1)}, f32[72,512]{1,0:T(8,128)S(1)}, u32[]{:S(2)}, u32[]{:S(2)}) collective-permute-start(f32[72,512]{1,0:T(8,128)S(1)} %pad_maximum_fusion.1.refs_7_), channel_id=1, source_target_pairs={{0,3},{8,11},{4,7},{12,15},{16,19},{24,27},{20,23},{28,31},{32,35}... | collective-permute-start | bytes 442376 | tf_op jit(solution)/shard_map/ppermute | solution.py:51
  147.6 4.7 %collective-permute-done.26.refs_8_ = f32[72,512]{1,0:T(8,128)S(1)} collective-permute-done((f32[72,512]{1,0:T(8,128)S(1)}, f32[72,512]{1,0:T(8,128)S(1)}, u32[]{:S(2)}, u32[]{:S(2)}) %collective-permute-start.26) | collective-permute-done | bytes 147488 | tf_op jit(solution)/shard_map/ppermute | solution.py:51
  154.1 3.2 %multiply_convert_fusion = bf16[512,1024]{1,0:T(8,128)(2,1)S(1)} fusion(bf16[1024,512]{1,0:T(8,128)(2,1)} %copy-done.10, bf16[1024,4096]{1,0:T(8,128)(2,1)} %bitcast.48, s32[]{:T(128)S(6)} %select_n.154), kind=kOutput, calls=%fused_computation.3 | convolution fusion | flops 1074790400 | bytes 4194308 | tf_op jit(solution)/shard_map/dot_general | solution.py:116
  157.3 1.6 add_convert_fusion
  158.9 5.0 %backward_full.1 = (bf16[512,512]{1,0:T(8,128)(2,1)}, bf16[512,512]{1,0:T(8,128)(2,1)}, f32[16,512]{1,0:T(8,128)}, f32[16,512]{1,0:T(8,128)}, f32[8,512]{1,0:T(8,128)S(1)}) custom-call(bf16[512,512]{1,0:T(8,128)(2,1)S(1)} %copy-done, bf16[512,512]{1,0:T(8,128)(2,1)S(1)} %copy-done.1, f32[4,512,128]{2,1,0:T(8,128)S(1)} %get-tuple-element.91.refs_2_, ...), custom_call_target="tpu_custom_call" | custom-call | flops 115000000 | tf_op jit(solution)/shard_map/backward_full/pallas_call | solution.py:326
  164.6 2.0 %fusion.20 = bf16[32,8192]{1,0:T(8,128)(2,1)} fusion(f32[64,8192]{1,0:T(8,128)S(1)} %copy-done.8, bf16[32,8192]{1,0:T(8,128)(2,1)} %collective-permute-done.25, bf16[32,8192]{1,0:T(8,128)(2,1)S(1)} %collective-permute-done.29, pred[]{:T(512)S(6)} %eq.10), kind=kLoop, calls=%fused_computation.22 | loop fusion | flops 1048576 | bytes 2621441 | tf_op jit(solution)/shard_map/convert_element_type | solution.py:430
  (88 shorter events, 17.2 us)
Async XLA Ops:
  1.7 10.5 %collective-permute-start.1 = (bf16[32,4096]{1,0:T(8,128)(2,1)S(1)}, bf16[32,4096]{1,0:T(8,128)(2,1)S(1)}, u32[]{:S(2)}, u32[]{:S(2)}) collective-permute-start(bf16[32,4096]{1,0:T(8,128)(2,1)S(1)} %get-tuple-element.103), channel_id=1, source_target_pairs={{0,4},{8,12},{4,16},{12,24},{16,20},{24,28},{20,0},{28,8},{32,36},... | collective-permute-start | bytes 786440 | tf_op jit(solution)/shard_map/ppermute | solution.py:51
  3.8 13.4 %collective-permute-start.2 = (bf16[32,4096]{1,0:T(8,128)(2,1)S(1)}, bf16[32,4096]{1,0:T(8,128)(2,1)S(1)}, u32[]{:S(2)}, u32[]{:S(2)}) collective-permute-start(bf16[32,4096]{1,0:T(8,128)(2,1)S(1)} %get-tuple-element.103), channel_id=1, source_target_pairs={{0,20},{8,28},{4,0},{12,8},{16,4},{24,12},{20,16},{28,24},{32,52},... | collective-permute-start | bytes 786440 | tf_op jit(solution)/shard_map/ppermute | solution.py:51
  6.0 13.0 %collective-permute-start = (bf16[32,4096]{1,0:T(8,128)(2,1)S(1)}, bf16[32,4096]{1,0:T(8,128)(2,1)S(1)}, u32[]{:S(2)}, u32[]{:S(2)}) collective-permute-start(bf16[32,4096]{1,0:T(8,128)(2,1)S(1)} %get-tuple-element.102), channel_id=1, source_target_pairs={{0,16},{8,24},{4,20},{12,28},{16,0},{24,8},{20,4},{28,12},{32,48},... | collective-permute-start | bytes 786440 | tf_op jit(solution)/shard_map/ppermute | solution.py:51
  17.3 2.9 %copy-start = (bf16[512,512]{1,0:T(8,128)(2,1)S(1)}, bf16[512,512]{1,0:T(8,128)(2,1)}, u32[]{:S(2)}) copy-start(bf16[512,512]{1,0:T(8,128)(2,1)} %refs_0_.3) | copy-start | bytes 1572868
  17.3 2.9 %copy-start.1 = (bf16[512,512]{1,0:T(8,128)(2,1)S(1)}, bf16[512,512]{1,0:T(8,128)(2,1)}, u32[]{:S(2)}) copy-start(bf16[512,512]{1,0:T(8,128)(2,1)} %refs_1_.1) | copy-start | bytes 1572868
  17.3 2.9 %copy-start.3 = (f32[16,512]{1,0:T(8,128)S(1)}, f32[16,512]{1,0:T(8,128)}, u32[]{:S(2)}) copy-start(f32[16,512]{1,0:T(8,128)} %refs_4_.3) | copy-start | bytes 98308
  23.8 4.3 %collective-permute-start.5 = (f32[32,512]{1,0:T(8,128)S(1)}, f32[32,512]{1,0:T(8,128)S(1)}, u32[]{:S(2)}, u32[]{:S(2)}) collective-permute-start(f32[32,512]{1,0:T(8,128)S(1)} %get-tuple-element.58), channel_id=1, source_target_pairs={{0,4},{8,12},{4,0},{12,8},{16,20},{24,28},{20,16},{28,24},{32,36},... | collective-permute-start | bytes 196616 | tf_op jit(solution)/shard_map/ppermute | solution.py:51
  28.1 7.5 %collective-permute-start.6 = (f32[64,512]{1,0:T(8,128)S(1)}, f32[64,512]{1,0:T(8,128)S(1)}, u32[]{:S(2)}, u32[]{:S(2)}) collective-permute-start(f32[64,512]{1,0:T(8,128)S(1)} %constant_dynamic-update-slice_fusion.refs_6_), channel_id=1, source_target_pairs={{0,1},{8,9},{4,5},{12,13},{16,17},{24,25},{20,21},{28,29},{32,33},... | collective-permute-start | bytes 393224 | tf_op jit(solution)/shard_map/ppermute | solution.py:51
  29.6 12.7 %copy-start.9 = (bf16[2,2,32,4096]{3,2,1,0:T(8,128)(2,1)S(1)}, bf16[2,2,32,4096]{3,2,1,0:T(8,128)(2,1)}, u32[]{:S(2)}) copy-start(bf16[2,2,32,4096]{3,2,1,0:T(8,128)(2,1)} %pad_maximum_fusion) | copy-start | bytes 3145732
  29.6 37.2 %collective-permute-start.9 = (bf16[2,2,32,4096]{3,2,1,0:T(8,128)(2,1)}, bf16[2,2,32,4096]{3,2,1,0:T(8,128)(2,1)}, u32[]{:S(2)}, u32[]{:S(2)}) collective-permute-start(bf16[2,2,32,4096]{3,2,1,0:T(8,128)(2,1)} %pad_maximum_fusion), channel_id=1, source_target_pairs={{0,8},{8,0},{4,12},{12,4},{16,24},{24,16},{20,28},{28,20},{32,40},... | collective-permute-start | bytes 3145736 | tf_op jit(solution)/shard_map/ppermute | solution.py:51
  29.6 25.2 %collective-permute-start.3 = (bf16[2,2,32,4096]{3,2,1,0:T(8,128)(2,1)}, bf16[2,2,32,4096]{3,2,1,0:T(8,128)(2,1)}, u32[]{:S(2)}, u32[]{:S(2)}) collective-permute-start(bf16[2,2,32,4096]{3,2,1,0:T(8,128)(2,1)} %pad_maximum_fusion), channel_id=1, source_target_pairs={{0,32},{8,104},{4,36},{12,108},{16,48},{24,120},{20,52},{28,124},{... | collective-permute-start | bytes 3145736 | tf_op jit(solution)/shard_map/ppermute | solution.py:51
  31.2 24.8 %collective-permute-start.4 = (bf16[2,2,32,4096]{3,2,1,0:T(8,128)(2,1)}, bf16[2,2,32,4096]{3,2,1,0:T(8,128)(2,1)}, u32[]{:S(2)}, u32[]{:S(2)}) collective-permute-start(bf16[2,2,32,4096]{3,2,1,0:T(8,128)(2,1)} %pad_maximum_fusion), channel_id=1, source_target_pairs={{0,96},{8,40},{4,100},{12,44},{16,112},{24,56},{20,116},{28,60},{3... | collective-permute-start | bytes 3145736 | tf_op jit(solution)/shard_map/ppermute | solution.py:51
  32.8 10.5 %collective-permute-start.7 = (f32[64,512]{1,0:T(8,128)S(1)}, f32[64,512]{1,0:T(8,128)S(1)}, u32[]{:S(2)}, u32[]{:S(2)}) collective-permute-start(f32[64,512]{1,0:T(8,128)S(1)} %constant_dynamic-update-slice_fusion.refs_6_), channel_id=1, source_target_pairs={{0,2},{8,10},{4,6},{12,14},{16,18},{24,26},{20,22},{28,30},{32,34}... | collective-permute-start | bytes 393224 | tf_op jit(solution)/shard_map/ppermute | solution.py:51
  35.6 7.8 %collective-permute-start.8 = (f32[64,512]{1,0:T(8,128)S(1)}, f32[64,512]{1,0:T(8,128)S(1)}, u32[]{:S(2)}, u32[]{:S(2)}) collective-permute-start(f32[64,512]{1,0:T(8,128)S(1)} %constant_dynamic-update-slice_fusion.refs_6_), channel_id=1, source_target_pairs={{0,3},{8,11},{4,7},{12,15},{16,19},{24,27},{20,23},{28,31},{32,35}... | collective-permute-start | bytes 393224 | tf_op jit(solution)/shard_map/ppermute | solution.py:51
  37.0 22.9 %copy-start.6 = (bf16[512,8192]{1,0:T(8,128)(2,1)S(1)}, bf16[512,8192]{1,0:T(8,128)(2,1)}, u32[]{:S(2)}) copy-start(bf16[512,8192]{1,0:T(8,128)(2,1)} %weight_ref.1) | copy-start | bytes 25165828
  42.3 1.5 copy-start.2
  42.3 1.5 copy-start.4
  42.3 1.5 copy-start.5
  47.9 23.7 %collective-permute-start.13 = (bf16[512,512]{1,0:T(8,128)(2,1)S(1)}, bf16[512,512]{1,0:T(8,128)(2,1)S(1)}, u32[]{:S(2)}, u32[]{:S(2)}) collective-permute-start(bf16[512,512]{1,0:T(8,128)(2,1)S(1)} %get-tuple-element.65), channel_id=1, source_target_pairs={{0,4},{8,12},{4,0},{12,8},{16,20},{24,28},{20,16},{28,24},{32,36},... | collective-permute-start | bytes 1572872 | tf_op jit(solution)/shard_map/ppermute | solution.py:51
  56.0 17.7 %collective-permute-start.10 = (bf16[2,2,32,4096]{3,2,1,0:T(8,128)(2,1)}, bf16[2,2,32,4096]{3,2,1,0:T(8,128)(2,1)S(1)}, u32[]{:S(2)}, u32[]{:S(2)}) collective-permute-start(bf16[2,2,32,4096]{3,2,1,0:T(8,128)(2,1)} %collective-permute-done.3), channel_id=1, source_target_pairs={{0,8},{8,0},{4,12},{12,4},{16,24},{24,16},{20,28},{28,20},{32,40},... | collective-permute-start | bytes 3145736 | tf_op jit(solution)/shard_map/ppermute | solution.py:51
  57.0 16.2 %collective-permute-start.12 = (bf16[2,2,32,4096]{3,2,1,0:T(8,128)(2,1)}, bf16[2,2,32,4096]{3,2,1,0:T(8,128)(2,1)S(1)}, u32[]{:S(2)}, u32[]{:S(2)}) collective-permute-start(bf16[2,2,32,4096]{3,2,1,0:T(8,128)(2,1)} %collective-permute-done.3), channel_id=1, source_target_pairs={{0,32},{8,104},{4,36},{12,108},{16,48},{24,120},{20,52},{28,124},{... | collective-permute-start | bytes 3145736 | tf_op jit(solution)/shard_map/ppermute | solution.py:51
  57.5 19.5 %collective-permute-start.11 = (bf16[2,2,32,4096]{3,2,1,0:T(8,128)(2,1)}, bf16[2,2,32,4096]{3,2,1,0:T(8,128)(2,1)S(1)}, u32[]{:S(2)}, u32[]{:S(2)}) collective-permute-start(bf16[2,2,32,4096]{3,2,1,0:T(8,128)(2,1)} %collective-permute-done.4), channel_id=1, source_target_pairs={{0,8},{8,0},{4,12},{12,4},{16,24},{24,16},{20,28},{28,20},{32,40},... | collective-permute-start | bytes 3145736 | tf_op jit(solution)/shard_map/ppermute | solution.py:51
  66.8 14.0 %collective-permute-start.15 = (bf16[192,8192]{1,0:T(8,128)(2,1)S(1)}, bf16[192,8192]{1,0:T(8,128)(2,1)S(1)}, u32[]{:S(2)}, u32[]{:S(2)}) collective-permute-start(bf16[192,8192]{1,0:T(8,128)(2,1)S(1)} %get-tuple-element.67), channel_id=1, source_target_pairs={{0,8},{8,0},{4,12},{12,4},{16,24},{24,16},{20,28},{28,20},{32,40},... | collective-permute-start | bytes 9437192 | tf_op jit(solution)/shard_map/ppermute | solution.py:51
  73.2 6.6 %collective-permute-start.14 = (bf16[2,2,32,4096]{3,2,1,0:T(8,128)(2,1)S(1)}, bf16[2,2,32,4096]{3,2,1,0:T(8,128)(2,1)S(1)}, u32[]{:S(2)}, u32[]{:S(2)}) collective-permute-start(bf16[2,2,32,4096]{3,2,1,0:T(8,128)(2,1)S(1)} %collective-permute-done.12), channel_id=1, source_target_pairs={{0,8},{8,0},{4,12},{12,4},{16,24},{24,16},{20,28},{28,20},{32,40},... | collective-permute-start | bytes 3145736 | tf_op jit(solution)/shard_map/ppermute | solution.py:51
  73.2 6.0 %collective-permute-start.18 = (bf16[64,8192]{1,0:T(8,128)(2,1)S(1)}, bf16[64,8192]{1,0:T(8,128)(2,1)S(1)}, u32[]{:S(2)}, u32[]{:S(2)}) collective-permute-start(bf16[64,8192]{1,0:T(8,128)(2,1)S(1)} %get-tuple-element.77), channel_id=1, source_target_pairs={{0,8},{8,0},{4,12},{12,4},{16,24},{24,16},{20,28},{28,20},{32,40},... | collective-permute-start | bytes 3145736 | tf_op jit(solution)/shard_map/ppermute | solution.py:51
  79.2 29.4 %copy-start.10 = (bf16[1024,512]{1,0:T(8,128)(2,1)}, bf16[1024,512]{1,0:T(8,128)(2,1)S(1)}, u32[]{:S(2)}) copy-start(bf16[1024,512]{1,0:T(8,128)(2,1)S(1)} %constant_dynamic-update-slice_fusion.2) | copy-start | bytes 3145732
  79.5 16.3 %collective-permute-start.19 = (bf16[64,8192]{1,0:T(8,128)(2,1)S(1)}, bf16[64,8192]{1,0:T(8,128)(2,1)S(1)}, u32[]{:S(2)}, u32[]{:S(2)}) collective-permute-start(bf16[64,8192]{1,0:T(8,128)(2,1)S(1)} %add_convert_fusion.3), channel_id=1, source_target_pairs={{0,32},{8,104},{4,36},{12,108},{16,48},{24,120},{20,52},{28,124},{... | collective-permute-start | bytes 3145736 | tf_op jit(solution)/shard_map/ppermute | solution.py:51
  87.8 8.7 %slice-start = ((s8[8388608]{0:T(1024)(128)(4,1)}), s8[4194304]{0:T(1024)(128)(4,1)S(1)}, s32[]{:S(2)}) async-start(s8[8388608]{0:T(1024)(128)(4,1)} %bitcast.49), calls=%async_computation | async-start | bytes 8388608
  87.9 8.6 %slice-start.1 = ((s8[8388608]{0:T(1024)(128)(4,1)}), s8[4194304]{0:T(1024)(128)(4,1)S(1)}, s32[]{:S(2)}) async-start(s8[8388608]{0:T(1024)(128)(4,1)} %bitcast.49), calls=%async_computation.1 | async-start | bytes 8388608
  87.9 22.0 %collective-permute-start.16 = (bf16[512,512]{1,0:T(8,128)(2,1)S(1)}, bf16[512,512]{1,0:T(8,128)(2,1)S(1)}, u32[]{:S(2)}, u32[]{:S(2)}) collective-permute-start(bf16[512,512]{1,0:T(8,128)(2,1)S(1)} %slice.50), channel_id=1, source_target_pairs={{0,4},{8,12},{4,0},{12,8},{16,20},{24,28},{20,16},{28,24},{32,36},... | collective-permute-start | bytes 1572872 | tf_op jit(solution)/shard_map/ppermute | solution.py:51
  92.6 16.1 %collective-permute-start.17 = (bf16[512,1024]{1,0:T(8,128)(2,1)S(1)}, bf16[512,1024]{1,0:T(8,128)(2,1)S(1)}, u32[]{:S(2)}, u32[]{:S(2)}) collective-permute-start(bf16[512,1024]{1,0:T(8,128)(2,1)S(1)} %multiply_convert_fusion.3), channel_id=1, source_target_pairs={{0,1},{8,11},{4,5},{12,15},{16,17},{24,27},{20,21},{28,31},{32,33}... | collective-permute-start | bytes 3145736 | tf_op jit(solution)/shard_map/ppermute | solution.py:51
  109.9 25.7 %collective-permute-start.21 = (bf16[64,8192]{1,0:T(8,128)(2,1)S(1)}, bf16[64,8192]{1,0:T(8,128)(2,1)S(1)}, u32[]{:S(2)}, u32[]{:S(2)}) collective-permute-start(bf16[64,8192]{1,0:T(8,128)(2,1)S(1)} %get-tuple-element.82), channel_id=1, source_target_pairs={{0,32},{8,104},{4,36},{12,108},{16,48},{24,120},{20,52},{28,124},{... | collective-permute-start | bytes 3145736 | tf_op jit(solution)/shard_map/ppermute | solution.py:51
  110.7 24.9 %collective-permute-start.22 = (bf16[64,8192]{1,0:T(8,128)(2,1)S(1)}, bf16[64,8192]{1,0:T(8,128)(2,1)S(1)}, u32[]{:S(2)}, u32[]{:S(2)}) collective-permute-start(bf16[64,8192]{1,0:T(8,128)(2,1)S(1)} %get-tuple-element.83), channel_id=1, source_target_pairs={{0,96},{8,40},{4,100},{12,44},{16,112},{24,56},{20,116},{28,60},{3... | collective-permute-start | bytes 3145736 | tf_op jit(solution)/shard_map/ppermute | solution.py:51
  113.3 26.3 %collective-permute-start.23 = (bf16[512,1024]{1,0:T(8,128)(2,1)S(1)}, bf16[512,1024]{1,0:T(8,128)(2,1)S(1)}, u32[]{:S(2)}, u32[]{:S(2)}) collective-permute-start(bf16[512,1024]{1,0:T(8,128)(2,1)S(1)} %add_convert_fusion.4), channel_id=1, source_target_pairs={{0,1},{8,11},{4,5},{12,15},{16,17},{24,27},{20,21},{28,31},{32,33}... | collective-permute-start | bytes 3145736 | tf_op jit(solution)/shard_map/ppermute | solution.py:51
  113.6 26.0 %collective-permute-start.24 = (bf16[512,1024]{1,0:T(8,128)(2,1)}, bf16[512,1024]{1,0:T(8,128)(2,1)S(1)}, u32[]{:S(2)}, u32[]{:S(2)}) collective-permute-start(bf16[512,1024]{1,0:T(8,128)(2,1)} %multiply_convert_fusion.1), channel_id=1, source_target_pairs={{0,3},{8,9},{4,7},{12,13},{16,19},{24,25},{20,23},{28,29},{32,35},... | collective-permute-start | bytes 3145736 | tf_op jit(solution)/shard_map/ppermute | solution.py:51
  127.2 4.8 %collective-permute-start.20 = (f32[56,512]{1,0:T(8,128)S(1)}, f32[56,512]{1,0:T(8,128)S(1)}, u32[]{:S(2)}, u32[]{:S(2)}) collective-permute-start(f32[56,512]{1,0:T(8,128)S(1)} %get-tuple-element.81), channel_id=1, source_target_pairs={{0,4},{8,12},{4,0},{12,8},{16,20},{24,28},{20,16},{28,24},{32,36},... | collective-permute-start | bytes 344072 | tf_op jit(solution)/shard_map/ppermute | solution.py:51
  139.6 1.0 copy-start.11
  139.6 1.3 copy-start.13
  140.9 3.5 %copy-start.7 = (f32[64,8192]{1,0:T(8,128)}, f32[64,8192]{1,0:T(8,128)S(1)}, u32[]{:S(2)}) copy-start(f32[64,8192]{1,0:T(8,128)S(1)} %convert_add_fusion) | copy-start | bytes 6291460
  141.8 11.4 %collective-permute-start.25 = (bf16[32,8192]{1,0:T(8,128)(2,1)}, bf16[32,8192]{1,0:T(8,128)(2,1)}, u32[]{:S(2)}, u32[]{:S(2)}) collective-permute-start(bf16[32,8192]{1,0:T(8,128)(2,1)} %slice.49), channel_id=1, source_target_pairs={{0,16},{8,28},{4,20},{12,8},{16,0},{24,12},{20,4},{28,24},{32,48},... | collective-permute-start | bytes 1572872 | tf_op jit(solution)/shard_map/ppermute | solution.py:51
  144.3 8.0 %collective-permute-start.26 = (f32[72,512]{1,0:T(8,128)S(1)}, f32[72,512]{1,0:T(8,128)S(1)}, u32[]{:S(2)}, u32[]{:S(2)}) collective-permute-start(f32[72,512]{1,0:T(8,128)S(1)} %pad_maximum_fusion.1.refs_7_), channel_id=1, source_target_pairs={{0,1},{8,9},{4,5},{12,13},{16,17},{24,25},{20,21},{28,29},{32,33},... | collective-permute-start | bytes 442376 | tf_op jit(solution)/shard_map/ppermute | solution.py:51
  144.4 7.9 %collective-permute-start.27 = (f32[72,512]{1,0:T(8,128)S(1)}, f32[72,512]{1,0:T(8,128)S(1)}, u32[]{:S(2)}, u32[]{:S(2)}) collective-permute-start(f32[72,512]{1,0:T(8,128)S(1)} %pad_maximum_fusion.1.refs_7_), channel_id=1, source_target_pairs={{0,2},{8,10},{4,6},{12,14},{16,18},{24,26},{20,22},{28,30},{32,34}... | collective-permute-start | bytes 442376 | tf_op jit(solution)/shard_map/ppermute | solution.py:51
  145.5 7.6 %collective-permute-start.28 = (f32[72,512]{1,0:T(8,128)S(1)}, f32[72,512]{1,0:T(8,128)S(1)}, u32[]{:S(2)}, u32[]{:S(2)}) collective-permute-start(f32[72,512]{1,0:T(8,128)S(1)} %pad_maximum_fusion.1.refs_7_), channel_id=1, source_target_pairs={{0,3},{8,11},{4,7},{12,15},{16,19},{24,27},{20,23},{28,31},{32,35}... | collective-permute-start | bytes 442376 | tf_op jit(solution)/shard_map/ppermute | solution.py:51
  147.6 9.7 %copy-start.12 = (bf16[512,1024]{1,0:T(8,128)(2,1)S(1)}, bf16[512,1024]{1,0:T(8,128)(2,1)}, u32[]{:S(2)}) copy-start(bf16[512,1024]{1,0:T(8,128)(2,1)} %copy-done.11) | copy-start | bytes 3145732
  147.6 9.7 %copy-start.14 = (bf16[512,1024]{1,0:T(8,128)(2,1)S(1)}, bf16[512,1024]{1,0:T(8,128)(2,1)}, u32[]{:S(2)}) copy-start(bf16[512,1024]{1,0:T(8,128)(2,1)} %copy-done.13) | copy-start | bytes 3145732
  153.2 11.4 %collective-permute-start.29 = (bf16[32,8192]{1,0:T(8,128)(2,1)}, bf16[32,8192]{1,0:T(8,128)(2,1)S(1)}, u32[]{:S(2)}, u32[]{:S(2)}) collective-permute-start(bf16[32,8192]{1,0:T(8,128)(2,1)} %collective-permute-done.25), channel_id=1, source_target_pairs={{8,28},{12,8},{24,12},{28,24},{40,60},{44,40},{56,44},{60,56},{72,... | collective-permute-start | bytes 1572872 | tf_op jit(solution)/shard_map/ppermute | solution.py:51
  158.9 5.6 %copy-start.8 = (f32[64,8192]{1,0:T(8,128)S(1)}, f32[64,8192]{1,0:T(8,128)}, u32[]{:S(2)}) copy-start(f32[64,8192]{1,0:T(8,128)} %copy-done.7) | copy-start | bytes 6291460

commit v5 on v4

--- a/solution.py
+++ b/solution.py
@@ -102,7 +102,7 @@
         out_shape=[jax.ShapeDtypeStruct((size, width), BF16) for size in sizes],
         in_specs=[pl.BlockSpec((rows, depth), lambda i: (0, 0)), pl.BlockSpec((depth, tile), lambda i: (0, i))],
         out_specs=[pl.BlockSpec((size, tile), lambda i: (0, i)) for size in sizes],
-        compiler_params=pltpu.CompilerParams(vmem_limit_bytes=32 * 2**20),
+        compiler_params=pltpu.CompilerParams(vmem_limit_bytes=12 * 2**20),
         cost_estimate=pl.CostEstimate(
             flops=2 * rows * depth * width, bytes_accessed=2 * width * (rows + depth), transcendentals=0
         ),
@@ -329,7 +329,7 @@
         in_specs=[whole] * len(args),
         out_specs=[whole] * len(outs),
         scratch_shapes=[pltpu.VMEM(shape, F32) for shape in scratch],
-        compiler_params=pltpu.CompilerParams(vmem_limit_bytes=32 * 2**20),
+        compiler_params=pltpu.CompilerParams(vmem_limit_bytes=6 * 2**20),
         cost_estimate=pl.CostEstimate(flops=int(micros * 1.15e9), bytes_accessed=0, transcendentals=0),
         name=name,
     )(*args)
@@ -358,18 +358,18 @@
     narrow = like((length, channels), BF16)
     table = (modes, channels)
 
-    block, log_first = together(gather_z(cotangent), log_decay)
-    main_block, other_block = hop(block, y=MAIN), hop(block, y=OTHER)
+    block = gather_z(cotangent)
     ends, subs, driving = call(
         forward_ends,
-        (key_proj, value_proj, log_first),
+        (key_proj, value_proj, log_decay),
         (like((2 * modes, channels), F32), like((tiles, 2 * SUBS * modes, LANES), F32), wide),
         [table, (SUBS, LANES)],
         0.1,
         "forward_ends",
     )
     ends_pair = jnp.concatenate([ends, hop(ends, pair=1)])
-    earlier = spread_over_x(ends_pair)
+    block, *earlier = together(block, *spread_over_x(ends_pair))
+    main_block, other_block = hop(block, y=MAIN), hop(block, y=OTHER)
     gated, turned, pre_gate, lead = call(
         forward_full,
         (queries, driving, subs, log_decay, residue, skip_row, *earlier),
@@ -400,16 +400,18 @@
     main_weight, other_weight, own_weight = (
         weigh(gated_pair, cot_rows, scale, lax.rem(x + r, RING)) for r in (1 + 2 * core, 3 - 2 * core, 0)
     )
-    main_weight = add(main_weight, hop(far_weight, x=MAIN)).astype(BF16)
-
     main, other, own = (add(a, b) for a, b in zip(jnp.split(near_rest, 3), jnp.split(got_rest, 3)))
     main = add(main, hop(opposite, y=MAIN)).astype(BF16)
-    other = other.astype(BF16)
-
-    theirs, main_weight, other_weight, main, other = together(theirs, main_weight, other_weight, main, other)
+    main, other, main_weight, other_weight, own_weight = together(
+        main, other.astype(BF16), main_weight, other_weight, own_weight
+    )
+    main, other = hop(main, y=MAIN), hop(other, y=OTHER)
+    other_weight = hop(other_weight, x=OTHER)
+    main_weight = add(main_weight, hop(far_weight, x=MAIN)).astype(BF16)
+
+    theirs, main_weight = together(theirs, main_weight)
     grad_gated = add(grad_parts[:length], theirs)
-    main, other = hop(main, y=MAIN), hop(other, y=OTHER)
-    main_weight, other_weight = hop(main_weight, x=MAIN), hop(other_weight, x=OTHER)
+    main_weight = hop(main_weight, x=MAIN)
 
     grad_query, back, sums, back_subs = call(
         backward_ends,

time: 170 us -> 156 us (0.918)
  the two profiles are of different devices: /device:TPU:0 before, /device:TPU:1 now
where the time goes in v5:
time: 156 us
  starting transfers between devices  46.9 us (30%)
  waiting for transfers between devices  46.5 us (30%)
  Pallas kernels  30 us (19%)
  local copies, waits for them, and re-layouts  15.7 us (10%)
  matrix products  9.58 us (6%)
  other arithmetic  5.85 us (4%)
    ppermute x30, starting transfers between devices, hop(): return lax.ppermute(value, ('chan', 'seq'), moves)  46.9 us
    ppermute x30, waiting for transfers between devices, hop(): return lax.ppermute(value, ('chan', 'seq'), moves)  46.5 us
    pallas_call x4, Pallas kernels, call(): pl.pallas_call(body, out_shape=[jax.ShapeDtypeStruct(o.shape, o.dtype) fo...  23.1 us
    pallas_call x1, Pallas kernels, project(): pl.pallas_call(project_tile, grid=(width // tile,), out_shape=[jax.ShapeD...  6.88 us
    unnamed x36, local copies, waits for them, and re-layouts  6.82 us
    dynamic_update_slice x8, local copies, waits for them, and re-layouts, place_blocks(): lax.dynamic_update_slice(whole, part[:, None, :, None], (0, row, 0, at_co...  6.02 us
    dot_general x4, matrix products, weigh(): lax.dot_general(gated, columns, (((0,), (0,)), ((), ())), preferred_eleme...  5.07 us
    dot_general x1, matrix products, local(): lax.dot_general(cot_rows, low_weight, (((1,), (1,)), ((), ())), preferred...  4.52 us
  transfers between devices with their start and end apart: 30, of which 16 were waited for; matrix products, arithmetic and copies ran while one was open for 15% of the time, Pallas kernels for 19%

profile of v5, /device:TPU:1, one launch (start us, length us, event | category | flops | bytes accessed | tf_op | source)
XLA Modules:
  0.0 155.7 jit_solution(15738579038344547430)
XLA Ops:
  0.7 1.1 constant_dynamic-slice_fusion.1
  1.7 2.5 %collective-permute-start.1 = (bf16[32,4096]{1,0:T(8,128)(2,1)S(1)}, bf16[32,4096]{1,0:T(8,128)(2,1)S(1)}, u32[]{:S(2)}, u32[]{:S(2)}) collective-permute-start(bf16[32,4096]{1,0:T(8,128)(2,1)S(1)} %get-tuple-element.113), channel_id=1, source_target_pairs={{0,4},{8,12},{4,16},{12,24},{16,20},{24,28},{20,0},{28,8},{32,36},... | collective-permute-start | bytes 786440 | tf_op jit(solution)/shard_map/ppermute | solution.py:51
  4.3 2.2 %collective-permute-start.2 = (bf16[32,4096]{1,0:T(8,128)(2,1)S(1)}, bf16[32,4096]{1,0:T(8,128)(2,1)S(1)}, u32[]{:S(2)}, u32[]{:S(2)}) collective-permute-start(bf16[32,4096]{1,0:T(8,128)(2,1)S(1)} %get-tuple-element.113), channel_id=1, source_target_pairs={{0,20},{8,28},{4,0},{12,8},{16,4},{24,12},{20,16},{28,24},{32,52},... | collective-permute-start | bytes 786440 | tf_op jit(solution)/shard_map/ppermute | solution.py:51
  6.5 1.2 collective-permute-start
  10.5 3.6 %forward_ends.1 = (f32[32,512]{1,0:T(8,128)S(1)}, f32[4,256,128]{2,1,0:T(8,128)S(1)}, f32[4,512,128]{2,1,0:T(8,128)S(1)}) custom-call(bf16[512,512]{1,0:T(8,128)(2,1)S(1)} %copy-done, bf16[512,512]{1,0:T(8,128)(2,1)S(1)} %copy-done.2, f32[16,512]{1,0:T(8,128)S(1)} %copy-done.5), custom_call_target="tpu_custom_call" | custom-call | flops 115000000 | tf_op jit(solution)/shard_map/forward_ends/pallas_call | solution.py:326
  14.9 3.6 %collective-permute-done.3 = f32[32,512]{1,0:T(8,128)S(1)} collective-permute-done((f32[32,512]{1,0:T(8,128)S(1)}, f32[32,512]{1,0:T(8,128)S(1)}, u32[]{:S(2)}, u32[]{:S(2)}) %collective-permute-start.3) | collective-permute-done | bytes 65568 | tf_op jit(solution)/shard_map/ppermute | solution.py:51
  18.6 1.2 collective-permute-start.4
  19.8 2.5 %collective-permute-start.5 = (f32[64,512]{1,0:T(8,128)S(1)}, f32[64,512]{1,0:T(8,128)S(1)}, u32[]{:S(2)}, u32[]{:S(2)}) collective-permute-start(f32[64,512]{1,0:T(8,128)S(1)} %constant_dynamic-update-slice_fusion.refs_6_), channel_id=1, source_target_pairs={{0,2},{8,10},{4,6},{12,14},{16,18},{24,26},{20,22},{28,30},{32,34}... | collective-permute-start | bytes 393224 | tf_op jit(solution)/shard_map/ppermute | solution.py:51
  22.2 1.2 collective-permute-start.6
  24.7 1.9 %collective-permute-done.5.refs_8_ = f32[64,512]{1,0:T(8,128)S(1)} collective-permute-done((f32[64,512]{1,0:T(8,128)S(1)}, f32[64,512]{1,0:T(8,128)S(1)}, u32[]{:S(2)}, u32[]{:S(2)}) %collective-permute-start.5) | collective-permute-done | bytes 131104 | tf_op jit(solution)/shard_map/ppermute | solution.py:51
  27.3 2.3 %collective-permute-start.9 = (bf16[2,2,32,4096]{3,2,1,0:T(8,128)(2,1)}, bf16[2,2,32,4096]{3,2,1,0:T(8,128)(2,1)}, u32[]{:S(2)}, u32[]{:S(2)}) collective-permute-start(bf16[2,2,32,4096]{3,2,1,0:T(8,128)(2,1)} %pad_maximum_fusion), channel_id=1, source_target_pairs={{0,8},{8,0},{4,12},{12,4},{16,24},{24,16},{20,28},{28,20},{32,40},... | collective-permute-start | bytes 3145736 | tf_op jit(solution)/shard_map/ppermute | solution.py:51
  29.6 2.7 %collective-permute-start.7 = (bf16[2,2,32,4096]{3,2,1,0:T(8,128)(2,1)}, bf16[2,2,32,4096]{3,2,1,0:T(8,128)(2,1)}, u32[]{:S(2)}, u32[]{:S(2)}) collective-permute-start(bf16[2,2,32,4096]{3,2,1,0:T(8,128)(2,1)} %pad_maximum_fusion), channel_id=1, source_target_pairs={{0,32},{8,104},{4,36},{12,108},{16,48},{24,120},{20,52},{28,124},{... | collective-permute-start | bytes 3145736 | tf_op jit(solution)/shard_map/ppermute | solution.py:51
  32.3 4.0 %forward_full.1 = (bf16[512,512]{1,0:T(8,128)(2,1)S(1)}, bf16[512,512]{1,0:T(8,128)(2,1)S(1)}, f32[4,512,128]{2,1,0:T(8,128)S(1)}, f32[4,256,128]{2,1,0:T(8,128)S(1)}) custom-call(bf16[512,512]{1,0:T(8,128)(2,1)S(1)} %copy-done.4, f32[4,512,128]{2,1,0:T(8,128)S(1)} %get-tuple-element.61.refs_1_.drive_ref, f32[4,256,128]{2,1,0:T(8,128)S(1)} %get-tuple-element.62.refs_2_, ...), custom_call_target="tpu_custom_call" | custom-call | flops 115000000 | tf_op jit(solution)/shard_map/forward_full/pallas_call | solution.py:326
  38.7 1.6 bitcast_dynamic-update-slice_fusion.6
  40.3 14.7 %collective-permute-done.7 = bf16[2,2,32,4096]{3,2,1,0:T(8,128)(2,1)} collective-permute-done((bf16[2,2,32,4096]{3,2,1,0:T(8,128)(2,1)}, bf16[2,2,32,4096]{3,2,1,0:T(8,128)(2,1)}, u32[]{:S(2)}, u32[]{:S(2)}) %collective-permute-start.7) | collective-permute-done | bytes 1048608 | tf_op jit(solution)/shard_map/ppermute | solution.py:51
  54.9 1.5 collective-permute-done.8
  56.4 3.0 %collective-permute-start.12 = (bf16[2,2,32,4096]{3,2,1,0:T(8,128)(2,1)}, bf16[2,2,32,4096]{3,2,1,0:T(8,128)(2,1)S(1)}, u32[]{:S(2)}, u32[]{:S(2)}) collective-permute-start(bf16[2,2,32,4096]{3,2,1,0:T(8,128)(2,1)} %collective-permute-done.7), channel_id=1, source_target_pairs={{0,32},{8,104},{4,36},{12,108},{16,48},{24,120},{20,52},{28,124},{... | collective-permute-start | bytes 3145736 | tf_op jit(solution)/shard_map/ppermute | solution.py:51
  59.4 6.9 %project.1 = (bf16[64,8192]{1,0:T(8,128)(2,1)S(1)}, bf16[192,8192]{1,0:T(8,128)(2,1)S(1)}, bf16[64,8192]{1,0:T(8,128)(2,1)S(1)}, bf16[192,8192]{1,0:T(8,128)(2,1)S(1)}) custom-call(bf16[512,512]{1,0:T(8,128)(2,1)S(1)} %get-tuple-element.68.rows_ref, bf16[512,8192]{1,0:T(8,128)(2,1)S(1)} %bitcast.47), custom_call_target="tpu_custom_call" | custom-call | flops 4294967296 | bytes 16777216 | tf_op jit(solution)/shard_map/project/pallas_call | solution.py:99
  66.9 1.3 bitcast_dynamic-update-slice_fusion.5
  68.2 1.3 bitcast_dynamic-update-slice_fusion.4
  69.6 1.9 %collective-permute-done.12 = bf16[2,2,32,4096]{3,2,1,0:T(8,128)(2,1)S(1)} collective-permute-done((bf16[2,2,32,4096]{3,2,1,0:T(8,128)(2,1)}, bf16[2,2,32,4096]{3,2,1,0:T(8,128)(2,1)S(1)}, u32[]{:S(2)}, u32[]{:S(2)}) %collective-permute-start.12) | collective-permute-done | bytes 1048608 | tf_op jit(solution)/shard_map/ppermute | solution.py:51
  71.4 1.7 %collective-permute-start.14 = (bf16[2,2,32,4096]{3,2,1,0:T(8,128)(2,1)S(1)}, bf16[2,2,32,4096]{3,2,1,0:T(8,128)(2,1)S(1)}, u32[]{:S(2)}, u32[]{:S(2)}) collective-permute-start(bf16[2,2,32,4096]{3,2,1,0:T(8,128)(2,1)S(1)} %collective-permute-done.12), channel_id=1, source_target_pairs={{0,8},{8,0},{4,12},{12,4},{16,24},{24,16},{20,28},{28,20},{32,40},... | collective-permute-start | bytes 3145736 | tf_op jit(solution)/shard_map/ppermute | solution.py:51
  73.3 1.3 bitcast_dynamic-update-slice_fusion.2
  77.2 2.0 %collective-permute-start.18 = (bf16[64,8192]{1,0:T(8,128)(2,1)S(1)}, bf16[64,8192]{1,0:T(8,128)(2,1)S(1)}, u32[]{:S(2)}, u32[]{:S(2)}) collective-permute-start(bf16[64,8192]{1,0:T(8,128)(2,1)S(1)} %add_convert_fusion.4), channel_id=1, source_target_pairs={{0,32},{8,104},{4,36},{12,108},{16,48},{24,120},{20,52},{28,124},{... | collective-permute-start | bytes 3145736 | tf_op jit(solution)/shard_map/ppermute | solution.py:51
  79.3 1.6 %copy-done.9 = bf16[192,8192]{1,0:T(8,128)(2,1)} copy-done((bf16[192,8192]{1,0:T(8,128)(2,1)}, bf16[192,8192]{1,0:T(8,128)(2,1)S(1)}, u32[]{:S(2)}) %copy-start.9) | copy-done | bytes 3145752
  80.9 4.5 %fusion = f32[1024,512]{1,0:T(8,128)S(1)} fusion(bf16[1024,4096]{1,0:T(8,128)(2,1)S(1)} %bitcast.48, bf16[512,8192]{1,0:T(8,128)(2,1)S(1)} %bitcast.47, s32[]{:T(128)S(6)} %select_n.129), kind=kOutput, calls=%fused_computation | convolution fusion | flops 4294967296 | bytes 14680068 | tf_op jit(solution)/shard_map/dot_general | solution.py:394
  86.0 1.3 multiply_convert_fusion.3
  87.3 2.5 %collective-permute-start.19 = (bf16[512,1024]{1,0:T(8,128)(2,1)S(1)}, bf16[512,1024]{1,0:T(8,128)(2,1)S(1)}, u32[]{:S(2)}, u32[]{:S(2)}) collective-permute-start(bf16[512,1024]{1,0:T(8,128)(2,1)S(1)} %multiply_convert_fusion.3), channel_id=1, source_target_pairs={{0,1},{8,11},{4,5},{12,15},{16,17},{24,27},{20,21},{28,31},{32,33}... | collective-permute-start | bytes 3145736 | tf_op jit(solution)/shard_map/ppermute | solution.py:51
  89.8 1.6 %collective-permute-done.18 = bf16[64,8192]{1,0:T(8,128)(2,1)S(1)} collective-permute-done((bf16[64,8192]{1,0:T(8,128)(2,1)S(1)}, bf16[64,8192]{1,0:T(8,128)(2,1)S(1)}, u32[]{:S(2)}, u32[]{:S(2)}) %collective-permute-start.18) | collective-permute-done | bytes 1048608 | tf_op jit(solution)/shard_map/ppermute | solution.py:51
  92.6 1.3 multiply_convert_fusion.2
  93.9 1.3 multiply_convert_fusion.1
  95.2 1.3 multiply_convert_fusion
  96.4 3.0 %collective-permute-start.21 = (bf16[64,8192]{1,0:T(8,128)(2,1)S(1)}, bf16[64,8192]{1,0:T(8,128)(2,1)S(1)}, u32[]{:S(2)}, u32[]{:S(2)}) collective-permute-start(bf16[64,8192]{1,0:T(8,128)(2,1)S(1)} %get-tuple-element.91), channel_id=1, source_target_pairs={{0,32},{8,104},{4,36},{12,108},{16,48},{24,120},{20,52},{28,124},{... | collective-permute-start | bytes 3145736 | tf_op jit(solution)/shard_map/ppermute | solution.py:51
  100.2 1.4 collective-permute-done.19
  101.9 3.4 %collective-permute-start.23 = (bf16[512,1024]{1,0:T(8,128)(2,1)S(1)}, bf16[512,1024]{1,0:T(8,128)(2,1)S(1)}, u32[]{:S(2)}, u32[]{:S(2)}) collective-permute-start(bf16[512,1024]{1,0:T(8,128)(2,1)S(1)} %add_convert_fusion.1), channel_id=1, source_target_pairs={{0,1},{8,11},{4,5},{12,15},{16,17},{24,27},{20,21},{28,31},{32,33}... | collective-permute-start | bytes 3145736 | tf_op jit(solution)/shard_map/ppermute | solution.py:51
  105.5 10.5 %backward_ends.1 = (bf16[512,512]{1,0:T(8,128)(2,1)}, f32[4,512,128]{2,1,0:T(8,128)S(1)}, f32[56,512]{1,0:T(8,128)S(1)}, f32[4,128,128]{2,1,0:T(8,128)S(1)}) custom-call(f32[512,512]{1,0:T(8,128)S(1)} %convert_add_fusion.1.grad_ref, bf16[512,512]{1,0:T(8,128)(2,1)S(1)} %copy-done.4, f32[4,512,128]{2,1,0:T(8,128)S(1)} %get-tuple-element.88.pre_ref, ...), custom_call_target="tpu_custom_call" | custom-call | flops 2300000000 | tf_op jit(solution)/shard_map/backward_ends/pallas_call | solution.py:326
  116.0 1.1 collective-permute-start.20
  117.1 2.3 %collective-permute-done.21 = bf16[64,8192]{1,0:T(8,128)(2,1)S(1)} collective-permute-done((bf16[64,8192]{1,0:T(8,128)(2,1)S(1)}, bf16[64,8192]{1,0:T(8,128)(2,1)S(1)}, u32[]{:S(2)}, u32[]{:S(2)}) %collective-permute-start.21) | collective-permute-done | bytes 1048608 | tf_op jit(solution)/shard_map/ppermute | solution.py:51
  119.4 6.4 %collective-permute-done.22 = bf16[64,8192]{1,0:T(8,128)(2,1)S(1)} collective-permute-done((bf16[64,8192]{1,0:T(8,128)(2,1)S(1)}, bf16[64,8192]{1,0:T(8,128)(2,1)S(1)}, u32[]{:S(2)}, u32[]{:S(2)}) %collective-permute-start.22) | collective-permute-done | bytes 1048608 | tf_op jit(solution)/shard_map/ppermute | solution.py:51
  125.8 2.2 %collective-permute-done.23 = bf16[512,1024]{1,0:T(8,128)(2,1)S(1)} collective-permute-done((bf16[512,1024]{1,0:T(8,128)(2,1)S(1)}, bf16[512,1024]{1,0:T(8,128)(2,1)S(1)}, u32[]{:S(2)}, u32[]{:S(2)}) %collective-permute-start.23) | collective-permute-done | bytes 1048608 | tf_op jit(solution)/shard_map/ppermute | solution.py:51
  128.6 2.1 %collective-permute-start.25 = (bf16[32,8192]{1,0:T(8,128)(2,1)S(1)}, bf16[32,8192]{1,0:T(8,128)(2,1)S(1)}, u32[]{:S(2)}, u32[]{:S(2)}) collective-permute-start(bf16[32,8192]{1,0:T(8,128)(2,1)S(1)} %slice.49), channel_id=1, source_target_pairs={{0,16},{8,28},{4,20},{12,8},{16,0},{24,12},{20,4},{28,24},{32,48},... | collective-permute-start | bytes 1572872 | tf_op jit(solution)/shard_map/ppermute | solution.py:51
  131.4 3.8 %collective-permute-start.27 = (f32[72,512]{1,0:T(8,128)S(1)}, f32[72,512]{1,0:T(8,128)S(1)}, u32[]{:S(2)}, u32[]{:S(2)}) collective-permute-start(f32[72,512]{1,0:T(8,128)S(1)} %pad_maximum_fusion.1.refs_7_), channel_id=1, source_target_pairs={{0,2},{8,10},{4,6},{12,14},{16,18},{24,26},{20,22},{28,30},{32,34}... | collective-permute-start | bytes 442376 | tf_op jit(solution)/shard_map/ppermute | solution.py:51
  135.1 1.6 %collective-permute-done.26.refs_8_ = f32[72,512]{1,0:T(8,128)S(1)} collective-permute-done((f32[72,512]{1,0:T(8,128)S(1)}, f32[72,512]{1,0:T(8,128)S(1)}, u32[]{:S(2)}, u32[]{:S(2)}) %collective-permute-start.26) | collective-permute-done | bytes 147488 | tf_op jit(solution)/shard_map/ppermute | solution.py:51
  136.8 3.3 %collective-permute-done.27.refs_9_ = f32[72,512]{1,0:T(8,128)S(1)} collective-permute-done((f32[72,512]{1,0:T(8,128)S(1)}, f32[72,512]{1,0:T(8,128)S(1)}, u32[]{:S(2)}, u32[]{:S(2)}) %collective-permute-start.27) | collective-permute-done | bytes 147488 | tf_op jit(solution)/shard_map/ppermute | solution.py:51
  140.5 2.0 %collective-permute-done.25 = bf16[32,8192]{1,0:T(8,128)(2,1)S(1)} collective-permute-done((bf16[32,8192]{1,0:T(8,128)(2,1)S(1)}, bf16[32,8192]{1,0:T(8,128)(2,1)S(1)}, u32[]{:S(2)}, u32[]{:S(2)}) %collective-permute-start.25) | collective-permute-done | bytes 524320 | tf_op jit(solution)/shard_map/ppermute | solution.py:51
  142.4 5.0 %collective-permute-start.29 = (bf16[32,8192]{1,0:T(8,128)(2,1)S(1)}, bf16[32,8192]{1,0:T(8,128)(2,1)S(1)}, u32[]{:S(2)}, u32[]{:S(2)}) collective-permute-start(bf16[32,8192]{1,0:T(8,128)(2,1)S(1)} %collective-permute-done.25), channel_id=1, source_target_pairs={{8,28},{12,8},{24,12},{28,24},{40,60},{44,40},{56,44},{60,56},{72,... | collective-permute-start | bytes 1572872 | tf_op jit(solution)/shard_map/ppermute | solution.py:51
  147.5 1.6 %add_convert_fusion = bf16[512,1024]{1,0:T(8,128)(2,1)} fusion(bf16[512,1024]{1,0:T(8,128)(2,1)S(1)} %collective-permute-done.24, bf16[512,1024]{1,0:T(8,128)(2,1)S(1)} %collective-permute-done.23, bf16[512,1024]{1,0:T(8,128)(2,1)S(1)} %multiply_convert_fusion), kind=kLoop, calls=%fused_computation.2 | loop fusion | flops 3145728 | bytes 4194304 | tf_op jit(solution)/shard_map/convert_element_type | solution.py:433
  149.1 5.1 %backward_full.1 = (bf16[512,512]{1,0:T(8,128)(2,1)}, bf16[512,512]{1,0:T(8,128)(2,1)}, f32[16,512]{1,0:T(8,128)}, f32[16,512]{1,0:T(8,128)}, f32[8,512]{1,0:T(8,128)S(1)}) custom-call(bf16[512,512]{1,0:T(8,128)(2,1)S(1)} %copy-done.1, bf16[512,512]{1,0:T(8,128)(2,1)S(1)} %copy-done.3, f32[4,512,128]{2,1,0:T(8,128)S(1)} %get-tuple-element.100.refs_2_, ...), custom_call_target="tpu_custom_call" | custom-call | flops 115000000 | tf_op jit(solution)/shard_map/backward_full/pallas_call | solution.py:326
  (89 shorter events, 17.4 us)
Async XLA Ops:
  1.7 20.5 %collective-permute-start.1 = (bf16[32,4096]{1,0:T(8,128)(2,1)S(1)}, bf16[32,4096]{1,0:T(8,128)(2,1)S(1)}, u32[]{:S(2)}, u32[]{:S(2)}) collective-permute-start(bf16[32,4096]{1,0:T(8,128)(2,1)S(1)} %get-tuple-element.113), channel_id=1, source_target_pairs={{0,4},{8,12},{4,16},{12,24},{16,20},{24,28},{20,0},{28,8},{32,36},... | collective-permute-start | bytes 786440 | tf_op jit(solution)/shard_map/ppermute | solution.py:51
  4.3 19.1 %collective-permute-start.2 = (bf16[32,4096]{1,0:T(8,128)(2,1)S(1)}, bf16[32,4096]{1,0:T(8,128)(2,1)S(1)}, u32[]{:S(2)}, u32[]{:S(2)}) collective-permute-start(bf16[32,4096]{1,0:T(8,128)(2,1)S(1)} %get-tuple-element.113), channel_id=1, source_target_pairs={{0,20},{8,28},{4,0},{12,8},{16,4},{24,12},{20,16},{28,24},{32,52},... | collective-permute-start | bytes 786440 | tf_op jit(solution)/shard_map/ppermute | solution.py:51
  6.5 17.1 %collective-permute-start = (bf16[32,4096]{1,0:T(8,128)(2,1)S(1)}, bf16[32,4096]{1,0:T(8,128)(2,1)S(1)}, u32[]{:S(2)}, u32[]{:S(2)}) collective-permute-start(bf16[32,4096]{1,0:T(8,128)(2,1)S(1)} %get-tuple-element.112), channel_id=1, source_target_pairs={{0,16},{8,24},{4,20},{12,28},{16,0},{24,8},{20,4},{28,12},{32,48},... | collective-permute-start | bytes 786440 | tf_op jit(solution)/shard_map/ppermute | solution.py:51
  7.7 1.0 copy-start
  8.7 1.0 copy-start.2
  9.8 0.8 copy-start.5
  14.1 4.4 %collective-permute-start.3 = (f32[32,512]{1,0:T(8,128)S(1)}, f32[32,512]{1,0:T(8,128)S(1)}, u32[]{:S(2)}, u32[]{:S(2)}) collective-permute-start(f32[32,512]{1,0:T(8,128)S(1)} %get-tuple-element.59), channel_id=1, source_target_pairs={{0,4},{8,12},{4,0},{12,8},{16,20},{24,28},{20,16},{28,24},{32,36},... | collective-permute-start | bytes 196616 | tf_op jit(solution)/shard_map/ppermute | solution.py:51
  18.6 6.2 %collective-permute-start.4 = (f32[64,512]{1,0:T(8,128)S(1)}, f32[64,512]{1,0:T(8,128)S(1)}, u32[]{:S(2)}, u32[]{:S(2)}) collective-permute-start(f32[64,512]{1,0:T(8,128)S(1)} %constant_dynamic-update-slice_fusion.refs_6_), channel_id=1, source_target_pairs={{0,1},{8,9},{4,5},{12,13},{16,17},{24,25},{20,21},{28,29},{32,33},... | collective-permute-start | bytes 393224 | tf_op jit(solution)/shard_map/ppermute | solution.py:51
  19.8 6.8 %collective-permute-start.5 = (f32[64,512]{1,0:T(8,128)S(1)}, f32[64,512]{1,0:T(8,128)S(1)}, u32[]{:S(2)}, u32[]{:S(2)}) collective-permute-start(f32[64,512]{1,0:T(8,128)S(1)} %constant_dynamic-update-slice_fusion.refs_6_), channel_id=1, source_target_pairs={{0,2},{8,10},{4,6},{12,14},{16,18},{24,26},{20,22},{28,30},{32,34}... | collective-permute-start | bytes 393224 | tf_op jit(solution)/shard_map/ppermute | solution.py:51
  22.2 5.0 %collective-permute-start.6 = (f32[64,512]{1,0:T(8,128)S(1)}, f32[64,512]{1,0:T(8,128)S(1)}, u32[]{:S(2)}, u32[]{:S(2)}) collective-permute-start(f32[64,512]{1,0:T(8,128)S(1)} %constant_dynamic-update-slice_fusion.refs_6_), channel_id=1, source_target_pairs={{0,3},{8,11},{4,7},{12,15},{16,19},{24,27},{20,23},{28,31},{32,35}... | collective-permute-start | bytes 393224 | tf_op jit(solution)/shard_map/ppermute | solution.py:51
  23.4 8.9 %copy-start.4 = (bf16[512,512]{1,0:T(8,128)(2,1)S(1)}, bf16[512,512]{1,0:T(8,128)(2,1)}, u32[]{:S(2)}) copy-start(bf16[512,512]{1,0:T(8,128)(2,1)} %query_ref.1) | copy-start | bytes 1572868
  23.4 8.8 %copy-start.6 = (f32[16,512]{1,0:T(8,128)S(1)}, f32[16,512]{1,0:T(8,128)}, u32[]{:S(2)}) copy-start(f32[16,512]{1,0:T(8,128)} %refs_4_.3) | copy-start | bytes 98308
  23.5 8.8 %copy-start.7 = (f32[16,512]{1,0:T(8,128)S(1)}, f32[16,512]{1,0:T(8,128)}, u32[]{:S(2)}) copy-start(f32[16,512]{1,0:T(8,128)} %refs_5_.1) | copy-start | bytes 98308
  23.5 8.8 %copy-start.8 = (f32[512]{0:T(512)S(1)}, f32[512]{0:T(512)}, u32[]{:S(2)}) copy-start(f32[512]{0:T(512)} %param.11) | copy-start | bytes 6148
  23.7 35.7 %slice-start = ((s8[8388608]{0:T(1024)(128)(4,1)}), s8[4194304]{0:T(1024)(128)(4,1)S(1)}, s32[]{:S(2)}) async-start(s8[8388608]{0:T(1024)(128)(4,1)} %bitcast.46), calls=%async_computation | async-start | bytes 8388608
  27.3 39.0 %collective-permute-start.9 = (bf16[2,2,32,4096]{3,2,1,0:T(8,128)(2,1)}, bf16[2,2,32,4096]{3,2,1,0:T(8,128)(2,1)}, u32[]{:S(2)}, u32[]{:S(2)}) collective-permute-start(bf16[2,2,32,4096]{3,2,1,0:T(8,128)(2,1)} %pad_maximum_fusion), channel_id=1, source_target_pairs={{0,8},{8,0},{4,12},{12,4},{16,24},{24,16},{20,28},{28,20},{32,40},... | collective-permute-start | bytes 3145736 | tf_op jit(solution)/shard_map/ppermute | solution.py:51
  29.6 25.4 %collective-permute-start.7 = (bf16[2,2,32,4096]{3,2,1,0:T(8,128)(2,1)}, bf16[2,2,32,4096]{3,2,1,0:T(8,128)(2,1)}, u32[]{:S(2)}, u32[]{:S(2)}) collective-permute-start(bf16[2,2,32,4096]{3,2,1,0:T(8,128)(2,1)} %pad_maximum_fusion), channel_id=1, source_target_pairs={{0,32},{8,104},{4,36},{12,108},{16,48},{24,120},{20,52},{28,124},{... | collective-permute-start | bytes 3145736 | tf_op jit(solution)/shard_map/ppermute | solution.py:51
  32.3 24.1 %collective-permute-start.8 = (bf16[2,2,32,4096]{3,2,1,0:T(8,128)(2,1)}, bf16[2,2,32,4096]{3,2,1,0:T(8,128)(2,1)}, u32[]{:S(2)}, u32[]{:S(2)}) collective-permute-start(bf16[2,2,32,4096]{3,2,1,0:T(8,128)(2,1)} %pad_maximum_fusion), channel_id=1, source_target_pairs={{0,96},{8,40},{4,100},{12,44},{16,112},{24,56},{20,116},{28,60},{3... | collective-permute-start | bytes 3145736 | tf_op jit(solution)/shard_map/ppermute | solution.py:51
  36.3 33.2 %collective-permute-start.13 = (bf16[512,512]{1,0:T(8,128)(2,1)S(1)}, bf16[512,512]{1,0:T(8,128)(2,1)S(1)}, u32[]{:S(2)}, u32[]{:S(2)}) collective-permute-start(bf16[512,512]{1,0:T(8,128)(2,1)S(1)} %get-tuple-element.73), channel_id=1, source_target_pairs={{0,4},{8,12},{4,0},{12,8},{16,20},{24,28},{20,16},{28,24},{32,36},... | collective-permute-start | bytes 1572872 | tf_op jit(solution)/shard_map/ppermute | solution.py:51
  37.6 21.7 %slice-start.1 = ((s8[8388608]{0:T(1024)(128)(4,1)}), s8[4194304]{0:T(1024)(128)(4,1)S(1)}, s32[]{:S(2)}) async-start(s8[8388608]{0:T(1024)(128)(4,1)} %bitcast.46), calls=%async_computation.1 | async-start | bytes 8388608
  56.4 16.7 %collective-permute-start.10 = (bf16[2,2,32,4096]{3,2,1,0:T(8,128)(2,1)}, bf16[2,2,32,4096]{3,2,1,0:T(8,128)(2,1)S(1)}, u32[]{:S(2)}, u32[]{:S(2)}) collective-permute-start(bf16[2,2,32,4096]{3,2,1,0:T(8,128)(2,1)} %collective-permute-done.7), channel_id=1, source_target_pairs={{0,8},{8,0},{4,12},{12,4},{16,24},{24,16},{20,28},{28,20},{32,40},... | collective-permute-start | bytes 3145736 | tf_op jit(solution)/shard_map/ppermute | solution.py:51
  56.4 15.0 %collective-permute-start.12 = (bf16[2,2,32,4096]{3,2,1,0:T(8,128)(2,1)}, bf16[2,2,32,4096]{3,2,1,0:T(8,128)(2,1)S(1)}, u32[]{:S(2)}, u32[]{:S(2)}) collective-permute-start(bf16[2,2,32,4096]{3,2,1,0:T(8,128)(2,1)} %collective-permute-done.7), channel_id=1, source_target_pairs={{0,32},{8,104},{4,36},{12,108},{16,48},{24,120},{20,52},{28,124},{... | collective-permute-start | bytes 3145736 | tf_op jit(solution)/shard_map/ppermute | solution.py:51
  59.4 15.3 %collective-permute-start.11 = (bf16[2,2,32,4096]{3,2,1,0:T(8,128)(2,1)}, bf16[2,2,32,4096]{3,2,1,0:T(8,128)(2,1)S(1)}, u32[]{:S(2)}, u32[]{:S(2)}) collective-permute-start(bf16[2,2,32,4096]{3,2,1,0:T(8,128)(2,1)} %collective-permute-done.8), channel_id=1, source_target_pairs={{0,8},{8,0},{4,12},{12,4},{16,24},{24,16},{20,28},{28,20},{32,40},... | collective-permute-start | bytes 3145736 | tf_op jit(solution)/shard_map/ppermute | solution.py:51
  66.3 13.0 %collective-permute-start.15 = (bf16[192,8192]{1,0:T(8,128)(2,1)S(1)}, bf16[192,8192]{1,0:T(8,128)(2,1)S(1)}, u32[]{:S(2)}, u32[]{:S(2)}) collective-permute-start(bf16[192,8192]{1,0:T(8,128)(2,1)S(1)} %get-tuple-element.75), channel_id=1, source_target_pairs={{0,8},{8,0},{4,12},{12,4},{16,24},{24,16},{20,28},{28,20},{32,40},... | collective-permute-start | bytes 9437192 | tf_op jit(solution)/shard_map/ppermute | solution.py:51
  71.4 7.7 %collective-permute-start.14 = (bf16[2,2,32,4096]{3,2,1,0:T(8,128)(2,1)S(1)}, bf16[2,2,32,4096]{3,2,1,0:T(8,128)(2,1)S(1)}, u32[]{:S(2)}, u32[]{:S(2)}) collective-permute-start(bf16[2,2,32,4096]{3,2,1,0:T(8,128)(2,1)S(1)} %collective-permute-done.12), channel_id=1, source_target_pairs={{0,8},{8,0},{4,12},{12,4},{16,24},{24,16},{20,28},{28,20},{32,40},... | collective-permute-start | bytes 3145736 | tf_op jit(solution)/shard_map/ppermute | solution.py:51
  73.2 3.8 %collective-permute-start.17 = (bf16[64,8192]{1,0:T(8,128)(2,1)S(1)}, bf16[64,8192]{1,0:T(8,128)(2,1)S(1)}, u32[]{:S(2)}, u32[]{:S(2)}) collective-permute-start(bf16[64,8192]{1,0:T(8,128)(2,1)S(1)} %get-tuple-element.83), channel_id=1, source_target_pairs={{0,8},{8,0},{4,12},{12,4},{16,24},{24,16},{20,28},{28,20},{32,40},... | collective-permute-start | bytes 3145736 | tf_op jit(solution)/shard_map/ppermute | solution.py:51
  74.6 1.2 copy-start.11
  75.9 1.0 copy-start.12
  77.2 14.2 %collective-permute-start.18 = (bf16[64,8192]{1,0:T(8,128)(2,1)S(1)}, bf16[64,8192]{1,0:T(8,128)(2,1)S(1)}, u32[]{:S(2)}, u32[]{:S(2)}) collective-permute-start(bf16[64,8192]{1,0:T(8,128)(2,1)S(1)} %add_convert_fusion.4), channel_id=1, source_target_pairs={{0,32},{8,104},{4,36},{12,108},{16,48},{24,120},{20,52},{28,124},{... | collective-permute-start | bytes 3145736 | tf_op jit(solution)/shard_map/ppermute | solution.py:51
  79.3 1.6 %copy-start.9 = (bf16[192,8192]{1,0:T(8,128)(2,1)}, bf16[192,8192]{1,0:T(8,128)(2,1)S(1)}, u32[]{:S(2)}) copy-start(bf16[192,8192]{1,0:T(8,128)(2,1)S(1)} %collective-permute-done.15) | copy-start | bytes 9437188
  80.9 5.1 %copy-start.13 = (bf16[1024,512]{1,0:T(8,128)(2,1)S(1)}, bf16[1024,512]{1,0:T(8,128)(2,1)}, u32[]{:S(2)}) copy-start(bf16[1024,512]{1,0:T(8,128)(2,1)} %copy-done.12) | copy-start | bytes 3145732
  85.5 5.9 %copy-start.10 = (bf16[192,8192]{1,0:T(8,128)(2,1)S(1)}, bf16[192,8192]{1,0:T(8,128)(2,1)}, u32[]{:S(2)}) copy-start(bf16[192,8192]{1,0:T(8,128)(2,1)} %copy-done.9) | copy-start | bytes 9437188
  85.5 16.4 %collective-permute-start.16 = (bf16[512,512]{1,0:T(8,128)(2,1)S(1)}, bf16[512,512]{1,0:T(8,128)(2,1)S(1)}, u32[]{:S(2)}, u32[]{:S(2)}) collective-permute-start(bf16[512,512]{1,0:T(8,128)(2,1)S(1)} %slice.50), channel_id=1, source_target_pairs={{0,4},{8,12},{4,0},{12,8},{16,20},{24,28},{20,16},{28,24},{32,36},... | collective-permute-start | bytes 1572872 | tf_op jit(solution)/shard_map/ppermute | solution.py:51
  87.3 14.2 %collective-permute-start.19 = (bf16[512,1024]{1,0:T(8,128)(2,1)S(1)}, bf16[512,1024]{1,0:T(8,128)(2,1)S(1)}, u32[]{:S(2)}, u32[]{:S(2)}) collective-permute-start(bf16[512,1024]{1,0:T(8,128)(2,1)S(1)} %multiply_convert_fusion.3), channel_id=1, source_target_pairs={{0,1},{8,11},{4,5},{12,15},{16,17},{24,27},{20,21},{28,31},{32,33}... | collective-permute-start | bytes 3145736 | tf_op jit(solution)/shard_map/ppermute | solution.py:51
  91.4 1.2 copy-start.14
  96.4 23.0 %collective-permute-start.21 = (bf16[64,8192]{1,0:T(8,128)(2,1)S(1)}, bf16[64,8192]{1,0:T(8,128)(2,1)S(1)}, u32[]{:S(2)}, u32[]{:S(2)}) collective-permute-start(bf16[64,8192]{1,0:T(8,128)(2,1)S(1)} %get-tuple-element.91), channel_id=1, source_target_pairs={{0,32},{8,104},{4,36},{12,108},{16,48},{24,120},{20,52},{28,124},{... | collective-permute-start | bytes 3145736 | tf_op jit(solution)/shard_map/ppermute | solution.py:51
  99.4 26.4 %collective-permute-start.22 = (bf16[64,8192]{1,0:T(8,128)(2,1)S(1)}, bf16[64,8192]{1,0:T(8,128)(2,1)S(1)}, u32[]{:S(2)}, u32[]{:S(2)}) collective-permute-start(bf16[64,8192]{1,0:T(8,128)(2,1)S(1)} %get-tuple-element.92), channel_id=1, source_target_pairs={{0,96},{8,40},{4,100},{12,44},{16,112},{24,56},{20,116},{28,60},{3... | collective-permute-start | bytes 3145736 | tf_op jit(solution)/shard_map/ppermute | solution.py:51
  99.5 26.4 %collective-permute-start.24 = (bf16[512,1024]{1,0:T(8,128)(2,1)S(1)}, bf16[512,1024]{1,0:T(8,128)(2,1)S(1)}, u32[]{:S(2)}, u32[]{:S(2)}) collective-permute-start(bf16[512,1024]{1,0:T(8,128)(2,1)S(1)} %multiply_convert_fusion.1), channel_id=1, source_target_pairs={{0,3},{8,9},{4,7},{12,13},{16,19},{24,25},{20,23},{28,29},{32,35},... | collective-permute-start | bytes 3145736 | tf_op jit(solution)/shard_map/ppermute | solution.py:51
  101.9 26.1 %collective-permute-start.23 = (bf16[512,1024]{1,0:T(8,128)(2,1)S(1)}, bf16[512,1024]{1,0:T(8,128)(2,1)S(1)}, u32[]{:S(2)}, u32[]{:S(2)}) collective-permute-start(bf16[512,1024]{1,0:T(8,128)(2,1)S(1)} %add_convert_fusion.1), channel_id=1, source_target_pairs={{0,1},{8,11},{4,5},{12,15},{16,17},{24,27},{20,21},{28,31},{32,33}... | collective-permute-start | bytes 3145736 | tf_op jit(solution)/shard_map/ppermute | solution.py:51
  116.0 9.8 %collective-permute-start.20 = (f32[56,512]{1,0:T(8,128)S(1)}, f32[56,512]{1,0:T(8,128)S(1)}, u32[]{:S(2)}, u32[]{:S(2)}) collective-permute-start(f32[56,512]{1,0:T(8,128)S(1)} %get-tuple-element.90), channel_id=1, source_target_pairs={{0,4},{8,12},{4,0},{12,8},{16,20},{24,28},{20,16},{28,24},{32,36},... | collective-permute-start | bytes 344072 | tf_op jit(solution)/shard_map/ppermute | solution.py:51
  128.6 13.8 %collective-permute-start.25 = (bf16[32,8192]{1,0:T(8,128)(2,1)S(1)}, bf16[32,8192]{1,0:T(8,128)(2,1)S(1)}, u32[]{:S(2)}, u32[]{:S(2)}) collective-permute-start(bf16[32,8192]{1,0:T(8,128)(2,1)S(1)} %slice.49), channel_id=1, source_target_pairs={{0,16},{8,28},{4,20},{12,8},{16,0},{24,12},{20,4},{28,24},{32,48},... | collective-permute-start | bytes 1572872 | tf_op jit(solution)/shard_map/ppermute | solution.py:51
  130.7 18.3 %copy-start.1 = (bf16[512,512]{1,0:T(8,128)(2,1)S(1)}, bf16[512,512]{1,0:T(8,128)(2,1)}, u32[]{:S(2)}) copy-start(bf16[512,512]{1,0:T(8,128)(2,1)} %refs_0_.3) | copy-start | bytes 1572868
  130.8 18.3 %copy-start.3 = (bf16[512,512]{1,0:T(8,128)(2,1)S(1)}, bf16[512,512]{1,0:T(8,128)(2,1)}, u32[]{:S(2)}) copy-start(bf16[512,512]{1,0:T(8,128)(2,1)} %refs_1_.1) | copy-start | bytes 1572868
  130.8 6.0 %collective-permute-start.26 = (f32[72,512]{1,0:T(8,128)S(1)}, f32[72,512]{1,0:T(8,128)S(1)}, u32[]{:S(2)}, u32[]{:S(2)}) collective-permute-start(f32[72,512]{1,0:T(8,128)S(1)} %pad_maximum_fusion.1.refs_7_), channel_id=1, source_target_pairs={{0,1},{8,9},{4,5},{12,13},{16,17},{24,25},{20,21},{28,29},{32,33},... | collective-permute-start | bytes 442376 | tf_op jit(solution)/shard_map/ppermute | solution.py:51
  131.4 8.7 %collective-permute-start.27 = (f32[72,512]{1,0:T(8,128)S(1)}, f32[72,512]{1,0:T(8,128)S(1)}, u32[]{:S(2)}, u32[]{:S(2)}) collective-permute-start(f32[72,512]{1,0:T(8,128)S(1)} %pad_maximum_fusion.1.refs_7_), channel_id=1, source_target_pairs={{0,2},{8,10},{4,6},{12,14},{16,18},{24,26},{20,22},{28,30},{32,34}... | collective-permute-start | bytes 442376 | tf_op jit(solution)/shard_map/ppermute | solution.py:51
  135.1 5.3 %collective-permute-start.28 = (f32[72,512]{1,0:T(8,128)S(1)}, f32[72,512]{1,0:T(8,128)S(1)}, u32[]{:S(2)}, u32[]{:S(2)}) collective-permute-start(f32[72,512]{1,0:T(8,128)S(1)} %pad_maximum_fusion.1.refs_7_), channel_id=1, source_target_pairs={{0,3},{8,11},{4,7},{12,15},{16,19},{24,27},{20,23},{28,31},{32,35}... | collective-permute-start | bytes 442376 | tf_op jit(solution)/shard_map/ppermute | solution.py:51
  142.4 12.3 %collective-permute-start.29 = (bf16[32,8192]{1,0:T(8,128)(2,1)S(1)}, bf16[32,8192]{1,0:T(8,128)(2,1)S(1)}, u32[]{:S(2)}, u32[]{:S(2)}) collective-permute-start(bf16[32,8192]{1,0:T(8,128)(2,1)S(1)} %collective-permute-done.25), channel_id=1, source_target_pairs={{8,28},{12,8},{24,12},{28,24},{40,60},{44,40},{56,44},{60,56},{72,... | collective-permute-start | bytes 1572872 | tf_op jit(solution)/shard_map/ppermute | solution.py:51

commit v6 on v5

--- a/solution.py
+++ b/solution.py
@@ -149,7 +149,7 @@
             return now, lag
 
         zero = [zero_ref[...]] * modes
-        now, lag = lax.fori_loop(0, span, step, (zero, zero), unroll=4)
+        now, lag = lax.fori_loop(0, span, step, (zero, zero), unroll=8)
         for m in range(modes):
             sub_ref[tile, strided(m, modes)] = now[m]
             sub_ref[tile, strided(SUBS * modes + m, modes)] = lag[m]
@@ -199,7 +199,7 @@
             return now
 
         first = [lead_ref[tile, strided(m, modes)] for m in range(modes)]
-        lax.fori_loop(0, span, step, first, unroll=4)
+        lax.fori_loop(0, span, step, first, unroll=8)
         gated_ref[:, lanes] = (query_ref[:, lanes].astype(F32) * pre_ref[tile]).astype(BF16)
     part = length // (RING * 4)
     y, high, core, _, _ = places()
@@ -234,7 +234,7 @@
             return [decay[m] * now[m] + g for m in range(modes)]
 
         zero = [zero_ref[...]] * modes
-        now = lax.fori_loop(0, span, back_step, zero, unroll=4)
+        now = lax.fori_loop(0, span, back_step, zero, unroll=8)
         for m in range(modes):
             sub_ref[tile, strided(m, modes)] = now[m]
         for low in range(0, modes, half):
@@ -256,7 +256,7 @@
             lag = [lead_ref[tile, strided(SUBS * modes + m, modes)] for m in group]
             zero = [zero_ref[...]] * half
             state, lag, pair, lag_pair, skip = lax.fori_loop(
-                0, span, pair_step, (state, lag, zero, zero, zero[0]), unroll=4
+                0, span, pair_step, (state, lag, zero, zero, zero[0]), unroll=8
             )
             for m in range(half):
                 part_ref[tile, strided(low + m, modes)] = pair[m]
@@ -315,7 +315,7 @@
             return now
 
         first = [lead_ref[tile, strided(m, modes)] for m in range(modes)]
-        lax.fori_loop(0, span, step, first, unroll=4)
+        lax.fori_loop(0, span, step, first, unroll=8)
         drive_grad = drive_grad_ref[tile]
         grad_key_ref[:, lanes] = (drive_grad * value_ref[:, lanes].astype(F32)).astype(BF16)
         grad_value_ref[:, lanes] = (drive_grad * key_ref[:, lanes].astype(F32)).astype(BF16)
@@ -368,8 +368,9 @@
         "forward_ends",
     )
     ends_pair = jnp.concatenate([ends, hop(ends, pair=1)])
-    block, *earlier = together(block, *spread_over_x(ends_pair))
+    block, ends_pair = together(block, ends_pair)
     main_block, other_block = hop(block, y=MAIN), hop(block, y=OTHER)
+    earlier = spread_over_x(ends_pair)
     gated, turned, pre_gate, lead = call(
         forward_full,
         (queries, driving, subs, log_decay, residue, skip_row, *earlier),
@@ -378,40 +379,38 @@
         0.1,
         "forward_full",
     )
+    block, gated = together(block, gated)
     main_block, other_block, turned = together(main_block, other_block, turned)
     far_block = hop(main_block, y=MAIN)
     near_first, near_rest, far_first, far_rest = project(turned, out_weight)
-    far_block, far_first, gated_other = together(far_block, far_first, hop(gated, pair=1))
+    far_block, far_rest, gated_other = together(far_block, far_rest, hop(gated, pair=1))
     got_first, got_rest = hop(far_first, core=1), hop(far_rest, core=1)
     gated_pair = jnp.concatenate([gated, gated_other])
     opposite = add(near_first, got_first).astype(BF16)
     cot_rows = place_blocks(block, main_block, other_block, far_block)
-    cot_rows, got_rest = together(cot_rows.reshape(2 * length, -1), got_rest)
+    cot_rows = cot_rows.reshape(2 * length, -1)
+    far_weight = weigh(gated_pair, cot_rows, scale, lax.rem(places()[4] + 2, RING))
+    cot_rows, far_weight = together(cot_rows, far_weight)
 
     _, _, core, low, x = places()
     half = out_weight.shape[1] // 2
     low_weight = lax.dynamic_slice(out_weight, (0, low * half), (channels, half))
     grad_parts = lax.dot_general(cot_rows, low_weight, (((1,), (1,)), ((), ())), preferred_element_type=F32)
-    cot_rows, grad_parts = together(cot_rows, grad_parts)
+    grad_parts, got_rest, opposite = together(grad_parts, got_rest, hop(opposite, y=MAIN))
     theirs = hop(grad_parts[length:].astype(BF16), pair=1)
-
-    far_weight = weigh(gated_pair, cot_rows, scale, lax.rem(x + 2, RING))
-    cot_rows, far_weight, got_rest = together(cot_rows, far_weight, got_rest)
+    cot_rows, theirs, far_weight = together(cot_rows, theirs, hop(far_weight, x=MAIN))
     main_weight, other_weight, own_weight = (
         weigh(gated_pair, cot_rows, scale, lax.rem(x + r, RING)) for r in (1 + 2 * core, 3 - 2 * core, 0)
     )
+
     main, other, own = (add(a, b) for a, b in zip(jnp.split(near_rest, 3), jnp.split(got_rest, 3)))
-    main = add(main, hop(opposite, y=MAIN)).astype(BF16)
-    main, other, main_weight, other_weight, own_weight = together(
-        main, other.astype(BF16), main_weight, other_weight, own_weight
-    )
-    main, other = hop(main, y=MAIN), hop(other, y=OTHER)
-    other_weight = hop(other_weight, x=OTHER)
-    main_weight = add(main_weight, hop(far_weight, x=MAIN)).astype(BF16)
-
-    theirs, main_weight = together(theirs, main_weight)
+    main = add(main, opposite).astype(BF16)
+    main, other = hop(main, y=MAIN), hop(other.astype(BF16), y=OTHER)
+    main_weight = add(main_weight, far_weight).astype(BF16)
+
+    theirs, main_weight, other_weight, own_weight = together(theirs, main_weight, other_weight, own_weight)
     grad_gated = add(grad_parts[:length], theirs)
-    main_weight = hop(main_weight, x=MAIN)
+    main_weight, other_weight = hop(main_weight, x=MAIN), hop(other_weight, x=OTHER)
 
     grad_query, back, sums, back_subs = call(
         backward_ends,

time: 156 us -> 163 us (1.045)
  the two profiles are of different devices: /device:TPU:1 before, /device:TPU:27 now
where the time goes in v6:
time: 163 us; the launch traced here: 162 us
  waiting for transfers between devices  55.8 us (34%)
  starting transfers between devices  38.7 us (24%)
  Pallas kernels  28.5 us (17%)
  matrix products  15.9 us (10%)
  local copies, waits for them, and re-layouts  11.6 us (7%)
  other arithmetic  10.8 us (7%)
    ppermute x30, waiting for transfers between devices, hop(): return lax.ppermute(value, ('chan', 'seq'), moves)  55.8 us
    ppermute x30, starting transfers between devices, hop(): return lax.ppermute(value, ('chan', 'seq'), moves)  38.7 us
    pallas_call x4, Pallas kernels, call(): pl.pallas_call(body, out_shape=[jax.ShapeDtypeStruct(o.shape, o.dtype) fo...  21.7 us
    dot_general x4, matrix products, weigh(): lax.dot_general(gated, columns, (((0,), (0,)), ((), ())), preferred_eleme...  11.4 us
    unnamed x27, local copies, waits for them, and re-layouts  7.1 us
    pallas_call x1, Pallas kernels, project(): pl.pallas_call(project_tile, grid=(width // tile,), out_shape=[jax.ShapeD...  6.86 us
    dot_general x1, matrix products, local(): lax.dot_general(cot_rows, low_weight, (((1,), (1,)), ((), ())), preferred...  4.52 us
  transfers between devices with their start and end apart: 30, of which 17 were waited for; matrix products, arithmetic and copies ran while one was open for 16% of the time, Pallas kernels for 18%

profile of v6, /device:TPU:27, one launch (start us, length us, event | category | flops | bytes accessed | tf_op | source)
XLA Modules:
  0.0 162.5 jit_solution(18069721567015190660)
XLA Ops:
  0.7 1.1 constant_dynamic-slice_fusion.1
  1.7 1.7 %collective-permute-start.1 = (bf16[32,4096]{1,0:T(8,128)(2,1)S(1)}, bf16[32,4096]{1,0:T(8,128)(2,1)S(1)}, u32[]{:S(2)}, u32[]{:S(2)}) collective-permute-start(bf16[32,4096]{1,0:T(8,128)(2,1)S(1)} %get-tuple-element.107), channel_id=1, source_target_pairs={{0,4},{8,12},{4,16},{12,24},{16,20},{24,28},{20,0},{28,8},{32,36},... | collective-permute-start | bytes 786440 | tf_op jit(solution)/shard_map/ppermute | solution.py:51
  3.4 2.2 %collective-permute-start.2 = (bf16[32,4096]{1,0:T(8,128)(2,1)S(1)}, bf16[32,4096]{1,0:T(8,128)(2,1)S(1)}, u32[]{:S(2)}, u32[]{:S(2)}) collective-permute-start(bf16[32,4096]{1,0:T(8,128)(2,1)S(1)} %get-tuple-element.107), channel_id=1, source_target_pairs={{0,20},{8,28},{4,0},{12,8},{16,4},{24,12},{20,16},{28,24},{32,52},... | collective-permute-start | bytes 786440 | tf_op jit(solution)/shard_map/ppermute | solution.py:51
  5.6 1.0 copy-done
  6.7 1.0 copy-done.2
  8.5 3.2 %forward_ends.1 = (f32[32,512]{1,0:T(8,128)S(1)}, f32[4,256,128]{2,1,0:T(8,128)S(1)}, f32[4,512,128]{2,1,0:T(8,128)S(1)}) custom-call(bf16[512,512]{1,0:T(8,128)(2,1)S(1)} %copy-done, bf16[512,512]{1,0:T(8,128)(2,1)S(1)} %copy-done.2, f32[16,512]{1,0:T(8,128)S(1)} %copy-done.5), custom_call_target="tpu_custom_call" | custom-call | flops 115000000 | tf_op jit(solution)/shard_map/forward_ends/pallas_call | solution.py:326
  11.8 2.6 %collective-permute-start = (bf16[32,4096]{1,0:T(8,128)(2,1)S(1)}, bf16[32,4096]{1,0:T(8,128)(2,1)}, u32[]{:S(2)}, u32[]{:S(2)}) collective-permute-start(bf16[32,4096]{1,0:T(8,128)(2,1)S(1)} %get-tuple-element.106), channel_id=1, source_target_pairs={{0,16},{8,24},{4,20},{12,28},{16,0},{24,8},{20,4},{28,12},{32,48},... | collective-permute-start | bytes 786440 | tf_op jit(solution)/shard_map/ppermute | solution.py:51
  15.1 5.8 %collective-permute-done = bf16[32,4096]{1,0:T(8,128)(2,1)} collective-permute-done((bf16[32,4096]{1,0:T(8,128)(2,1)S(1)}, bf16[32,4096]{1,0:T(8,128)(2,1)}, u32[]{:S(2)}, u32[]{:S(2)}) %collective-permute-start) | collective-permute-done | bytes 262176 | tf_op jit(solution)/shard_map/ppermute | solution.py:51
  21.0 1.1 maximum_select_fusion
  22.1 1.1 pad_maximum_fusion
  23.2 1.2 collective-permute-start.6
  25.2 1.9 %collective-permute-start.8 = (f32[64,512]{1,0:T(8,128)S(1)}, f32[64,512]{1,0:T(8,128)S(1)}, u32[]{:S(2)}, u32[]{:S(2)}) collective-permute-start(f32[64,512]{1,0:T(8,128)S(1)} %pad_maximum_fusion.2.refs_6_), channel_id=1, source_target_pairs={{0,3},{8,11},{4,7},{12,15},{16,19},{24,27},{20,23},{28,31},{32,35}... | collective-permute-start | bytes 393224 | tf_op jit(solution)/shard_map/ppermute | solution.py:51
  27.5 2.2 %collective-permute-start.5 = (bf16[2,2,32,4096]{3,2,1,0:T(8,128)(2,1)}, bf16[2,2,32,4096]{3,2,1,0:T(8,128)(2,1)S(1)}, u32[]{:S(2)}, u32[]{:S(2)}) collective-permute-start(bf16[2,2,32,4096]{3,2,1,0:T(8,128)(2,1)} %pad_maximum_fusion), channel_id=1, source_target_pairs={{0,96},{8,40},{4,100},{12,44},{16,112},{24,56},{20,116},{28,60},{3... | collective-permute-start | bytes 3145736 | tf_op jit(solution)/shard_map/ppermute | solution.py:51
  30.7 3.8 %forward_full.1 = (bf16[512,512]{1,0:T(8,128)(2,1)S(1)}, bf16[512,512]{1,0:T(8,128)(2,1)S(1)}, f32[4,512,128]{2,1,0:T(8,128)S(1)}, f32[4,256,128]{2,1,0:T(8,128)S(1)}) custom-call(bf16[512,512]{1,0:T(8,128)(2,1)S(1)} %copy-done.4, f32[4,512,128]{2,1,0:T(8,128)S(1)} %get-tuple-element.58.refs_1_.drive_ref, f32[4,256,128]{2,1,0:T(8,128)S(1)} %get-tuple-element.59.refs_2_, ...), custom_call_target="tpu_custom_call" | custom-call | flops 115000000 | tf_op jit(solution)/shard_map/forward_full/pallas_call | solution.py:326
  34.6 3.7 %collective-permute-start.9 = (bf16[2,2,32,4096]{3,2,1,0:T(8,128)(2,1)S(1)}, bf16[2,2,32,4096]{3,2,1,0:T(8,128)(2,1)S(1)}, u32[]{:S(2)}, u32[]{:S(2)}) collective-permute-start(bf16[2,2,32,4096]{3,2,1,0:T(8,128)(2,1)S(1)} %copy-done.10), channel_id=1, source_target_pairs={{0,8},{8,0},{4,12},{12,4},{16,24},{24,16},{20,28},{28,20},{32,40},... | collective-permute-start | bytes 3145736 | tf_op jit(solution)/shard_map/ppermute | solution.py:51
  40.8 9.2 %collective-permute-done.4 = bf16[2,2,32,4096]{3,2,1,0:T(8,128)(2,1)S(1)} collective-permute-done((bf16[2,2,32,4096]{3,2,1,0:T(8,128)(2,1)}, bf16[2,2,32,4096]{3,2,1,0:T(8,128)(2,1)S(1)}, u32[]{:S(2)}, u32[]{:S(2)}) %collective-permute-start.4) | collective-permute-done | bytes 1048608 | tf_op jit(solution)/shard_map/ppermute | solution.py:51
  49.9 2.4 %collective-permute-done.5 = bf16[2,2,32,4096]{3,2,1,0:T(8,128)(2,1)S(1)} collective-permute-done((bf16[2,2,32,4096]{3,2,1,0:T(8,128)(2,1)}, bf16[2,2,32,4096]{3,2,1,0:T(8,128)(2,1)S(1)}, u32[]{:S(2)}, u32[]{:S(2)}) %collective-permute-start.5) | collective-permute-done | bytes 1048608 | tf_op jit(solution)/shard_map/ppermute | solution.py:51
  52.4 1.7 %collective-permute-start.10 = (bf16[2,2,32,4096]{3,2,1,0:T(8,128)(2,1)S(1)}, bf16[2,2,32,4096]{3,2,1,0:T(8,128)(2,1)S(1)}, u32[]{:S(2)}, u32[]{:S(2)}) collective-permute-start(bf16[2,2,32,4096]{3,2,1,0:T(8,128)(2,1)S(1)} %collective-permute-done.4), channel_id=1, source_target_pairs={{0,8},{8,0},{4,12},{12,4},{16,24},{24,16},{20,28},{28,20},{32,40},... | collective-permute-start | bytes 3145736 | tf_op jit(solution)/shard_map/ppermute | solution.py:51
  54.1 3.0 %collective-permute-start.11 = (bf16[2,2,32,4096]{3,2,1,0:T(8,128)(2,1)S(1)}, bf16[2,2,32,4096]{3,2,1,0:T(8,128)(2,1)S(1)}, u32[]{:S(2)}, u32[]{:S(2)}) collective-permute-start(bf16[2,2,32,4096]{3,2,1,0:T(8,128)(2,1)S(1)} %collective-permute-done.5), channel_id=1, source_target_pairs={{0,8},{8,0},{4,12},{12,4},{16,24},{24,16},{20,28},{28,20},{32,40},... | collective-permute-start | bytes 3145736 | tf_op jit(solution)/shard_map/ppermute | solution.py:51
  57.0 3.4 %copy-done.9 = bf16[512,8192]{1,0:T(8,128)(2,1)S(1)} copy-done((bf16[512,8192]{1,0:T(8,128)(2,1)S(1)}, bf16[512,8192]{1,0:T(8,128)(2,1)}, u32[]{:S(2)}) %copy-start.9) | copy-done | bytes 8388632
  60.4 6.9 %project.1 = (bf16[64,8192]{1,0:T(8,128)(2,1)S(1)}, bf16[192,8192]{1,0:T(8,128)(2,1)S(1)}, bf16[64,8192]{1,0:T(8,128)(2,1)S(1)}, bf16[192,8192]{1,0:T(8,128)(2,1)S(1)}) custom-call(bf16[512,512]{1,0:T(8,128)(2,1)S(1)} %get-tuple-element.62.rows_ref, bf16[512,8192]{1,0:T(8,128)(2,1)S(1)} %copy-done.9), custom_call_target="tpu_custom_call" | custom-call | flops 4294967296 | bytes 16777216 | tf_op jit(solution)/shard_map/project/pallas_call | solution.py:99
  67.6 1.3 collective-permute-done.12
  72.3 3.9 %multiply_convert_fusion.3 = bf16[512,1024]{1,0:T(8,128)(2,1)} fusion(bf16[1024,512]{1,0:T(8,128)(2,1)} %constant_dynamic-update-slice_fusion, bf16[1024,4096]{1,0:T(8,128)(2,1)S(1)} %bitcast.48, s32[]{:T(128)S(6)} %select_n.149), kind=kOutput, calls=%fused_computation.17 | convolution fusion | flops 1074790400 | bytes 4194308 | tf_op jit(solution)/shard_map/dot_general | solution.py:116
  76.2 1.2 collective-permute-start.19
  77.4 4.5 %fusion = f32[1024,512]{1,0:T(8,128)S(1)} fusion(bf16[1024,4096]{1,0:T(8,128)(2,1)S(1)} %bitcast.49, bf16[512,8192]{1,0:T(8,128)(2,1)S(1)} %bitcast.47, s32[]{:T(128)S(6)} %select_n.129), kind=kOutput, calls=%fused_computation | convolution fusion | flops 4294967296 | bytes 14680068 | tf_op jit(solution)/shard_map/dot_general | solution.py:398
  81.9 3.4 %collective-permute-done.17 = bf16[64,8192]{1,0:T(8,128)(2,1)S(1)} collective-permute-done((bf16[64,8192]{1,0:T(8,128)(2,1)S(1)}, bf16[64,8192]{1,0:T(8,128)(2,1)S(1)}, u32[]{:S(2)}, u32[]{:S(2)}) %collective-permute-start.17) | collective-permute-done | bytes 1048608 | tf_op jit(solution)/shard_map/ppermute | solution.py:51
  86.0 2.2 %add_convert_fusion.1 = (bf16[64,8192]{1,0:T(8,128)(2,1)S(1)}, bf16[64,8192]{1,0:T(8,128)(2,1)S(1)}) fusion(bf16[192,8192]{1,0:T(8,128)(2,1)} %collective-permute-done.15, bf16[192,8192]{1,0:T(8,128)(2,1)S(1)} %get-tuple-element.63, bf16[64,8192]{1,0:T(8,128)(2,1)S(1)} %collective-permute-done.17), kind=kLoop, calls=%fused_computation.4 | loop fusion | flops 5242880 | bytes 7340032 | tf_op jit(solution)/shard_map/convert_element_type | solution.py:408
  88.2 2.7 %collective-permute-start.22 = (bf16[64,8192]{1,0:T(8,128)(2,1)S(1)}, bf16[64,8192]{1,0:T(8,128)(2,1)S(1)}, u32[]{:S(2)}, u32[]{:S(2)}) collective-permute-start(bf16[64,8192]{1,0:T(8,128)(2,1)S(1)} %get-tuple-element.104), channel_id=1, source_target_pairs={{0,96},{8,40},{4,100},{12,44},{16,112},{24,56},{20,116},{28,60},{3... | collective-permute-start | bytes 3145736 | tf_op jit(solution)/shard_map/ppermute | solution.py:51
  90.9 7.1 %collective-permute-done.18 = bf16[512,512]{1,0:T(8,128)(2,1)S(1)} collective-permute-done((bf16[512,512]{1,0:T(8,128)(2,1)S(1)}, bf16[512,512]{1,0:T(8,128)(2,1)S(1)}, u32[]{:S(2)}, u32[]{:S(2)}) %collective-permute-start.18) | collective-permute-done | bytes 524320 | tf_op jit(solution)/shard_map/ppermute | solution.py:51
  98.0 2.5 %multiply_convert_fusion.2 = bf16[512,1024]{1,0:T(8,128)(2,1)S(1)} fusion(bf16[1024,512]{1,0:T(8,128)(2,1)} %constant_dynamic-update-slice_fusion, bf16[1024,4096]{1,0:T(8,128)(2,1)S(1)} %bitcast.50, s32[]{:T(128)S(6)} %select_n.150), kind=kOutput, calls=%fused_computation.13 | convolution fusion | flops 1074790400 | bytes 4194308 | tf_op jit(solution)/shard_map/dot_general | solution.py:116
  100.4 2.5 %multiply_convert_fusion.1 = bf16[512,1024]{1,0:T(8,128)(2,1)S(1)} fusion(bf16[1024,512]{1,0:T(8,128)(2,1)} %constant_dynamic-update-slice_fusion, bf16[1024,4096]{1,0:T(8,128)(2,1)S(1)} %bitcast.51, s32[]{:T(128)S(6)} %select_n.151), kind=kOutput, calls=%fused_computation.9 | convolution fusion | flops 1074790400 | bytes 4194308 | tf_op jit(solution)/shard_map/dot_general | solution.py:116
  103.0 2.5 %multiply_convert_fusion = bf16[512,1024]{1,0:T(8,128)(2,1)S(1)} fusion(bf16[1024,512]{1,0:T(8,128)(2,1)} %constant_dynamic-update-slice_fusion, bf16[1024,4096]{1,0:T(8,128)(2,1)S(1)} %bitcast.52, s32[]{:T(128)S(6)} %select_n.152), kind=kOutput, calls=%fused_computation.6 | convolution fusion | flops 1074790400 | bytes 4194308 | tf_op jit(solution)/shard_map/dot_general | solution.py:116
  105.5 1.5 add_convert_fusion.3
  107.0 2.1 %collective-permute-start.23 = (bf16[512,1024]{1,0:T(8,128)(2,1)S(1)}, bf16[512,1024]{1,0:T(8,128)(2,1)S(1)}, u32[]{:S(2)}, u32[]{:S(2)}) collective-permute-start(bf16[512,1024]{1,0:T(8,128)(2,1)S(1)} %add_convert_fusion.3), channel_id=1, source_target_pairs={{0,1},{8,11},{4,5},{12,15},{16,17},{24,27},{20,21},{28,31},{32,33}... | collective-permute-start | bytes 3145736 | tf_op jit(solution)/shard_map/ppermute | solution.py:51
  109.2 9.5 %backward_ends.1 = (bf16[512,512]{1,0:T(8,128)(2,1)}, f32[4,512,128]{2,1,0:T(8,128)S(1)}, f32[56,512]{1,0:T(8,128)S(1)}, f32[4,128,128]{2,1,0:T(8,128)S(1)}) custom-call(f32[512,512]{1,0:T(8,128)S(1)} %convert_add_fusion.1.grad_ref, bf16[512,512]{1,0:T(8,128)(2,1)S(1)} %copy-done.4, f32[4,512,128]{2,1,0:T(8,128)S(1)} %get-tuple-element.83.pre_ref, ...), custom_call_target="tpu_custom_call" | custom-call | flops 2300000000 | tf_op jit(solution)/shard_map/backward_ends/pallas_call | solution.py:326
  119.3 3.4 %collective-permute-done.20 = f32[56,512]{1,0:T(8,128)S(1)} collective-permute-done((f32[56,512]{1,0:T(8,128)S(1)}, f32[56,512]{1,0:T(8,128)S(1)}, u32[]{:S(2)}, u32[]{:S(2)}) %collective-permute-start.20) | collective-permute-done | bytes 114720 | tf_op jit(solution)/shard_map/ppermute | solution.py:51
  122.7 7.2 %collective-permute-done.23 = bf16[512,1024]{1,0:T(8,128)(2,1)S(1)} collective-permute-done((bf16[512,1024]{1,0:T(8,128)(2,1)S(1)}, bf16[512,1024]{1,0:T(8,128)(2,1)S(1)}, u32[]{:S(2)}, u32[]{:S(2)}) %collective-permute-start.23) | collective-permute-done | bytes 1048608 | tf_op jit(solution)/shard_map/ppermute | solution.py:51
  130.0 4.0 %collective-permute-done.24 = bf16[512,1024]{1,0:T(8,128)(2,1)S(1)} collective-permute-done((bf16[512,1024]{1,0:T(8,128)(2,1)S(1)}, bf16[512,1024]{1,0:T(8,128)(2,1)S(1)}, u32[]{:S(2)}, u32[]{:S(2)}) %collective-permute-start.24) | collective-permute-done | bytes 1048608 | tf_op jit(solution)/shard_map/ppermute | solution.py:51
  134.0 1.8 %convert_add_fusion = f32[64,8192]{1,0:T(8,128)S(1)} fusion(bf16[64,8192]{1,0:T(8,128)(2,1)S(1)} %collective-permute-done.22, bf16[64,8192]{1,0:T(8,128)(2,1)S(1)} %collective-permute-done.21, bf16[192,8192]{1,0:T(8,128)(2,1)} %collective-permute-done.15, bf16[192,8192]{1,0:T(8,128)(2,1)S(1)} %get-tuple-element.63), kind=kLoop, calls=%fused_computation.3 | loop fusion | flops 3670016 | bytes 6291456 | tf_op jit(solution)/shard_map/add | solution.py:83
  135.8 1.7 %collective-permute-start.25 = (bf16[32,8192]{1,0:T(8,128)(2,1)S(1)}, bf16[32,8192]{1,0:T(8,128)(2,1)S(1)}, u32[]{:S(2)}, u32[]{:S(2)}) collective-permute-start(bf16[32,8192]{1,0:T(8,128)(2,1)S(1)} %slice.49), channel_id=1, source_target_pairs={{0,16},{8,28},{4,20},{12,8},{16,0},{24,12},{20,4},{28,24},{32,48},... | collective-permute-start | bytes 1572872 | tf_op jit(solution)/shard_map/ppermute | solution.py:51
  137.9 1.3 collective-permute-start.27
  139.8 2.5 %collective-permute-done.26.refs_8_ = f32[72,512]{1,0:T(8,128)S(1)} collective-permute-done((f32[72,512]{1,0:T(8,128)S(1)}, f32[72,512]{1,0:T(8,128)S(1)}, u32[]{:S(2)}, u32[]{:S(2)}) %collective-permute-start.26) | collective-permute-done | bytes 147488 | tf_op jit(solution)/shard_map/ppermute | solution.py:51
  142.3 1.9 %collective-permute-done.27.refs_9_ = f32[72,512]{1,0:T(8,128)S(1)} collective-permute-done((f32[72,512]{1,0:T(8,128)S(1)}, f32[72,512]{1,0:T(8,128)S(1)}, u32[]{:S(2)}, u32[]{:S(2)}) %collective-permute-start.27) | collective-permute-done | bytes 147488 | tf_op jit(solution)/shard_map/ppermute | solution.py:51
  144.2 3.2 %collective-permute-done.28.refs_10_ = f32[72,512]{1,0:T(8,128)S(1)} collective-permute-done((f32[72,512]{1,0:T(8,128)S(1)}, f32[72,512]{1,0:T(8,128)S(1)}, u32[]{:S(2)}, u32[]{:S(2)}) %collective-permute-start.28) | collective-permute-done | bytes 147488 | tf_op jit(solution)/shard_map/ppermute | solution.py:51
  147.4 1.8 %collective-permute-done.25 = bf16[32,8192]{1,0:T(8,128)(2,1)S(1)} collective-permute-done((bf16[32,8192]{1,0:T(8,128)(2,1)S(1)}, bf16[32,8192]{1,0:T(8,128)(2,1)S(1)}, u32[]{:S(2)}, u32[]{:S(2)}) %collective-permute-start.25) | collective-permute-done | bytes 524320 | tf_op jit(solution)/shard_map/ppermute | solution.py:51
  149.2 5.0 %collective-permute-start.29 = (bf16[32,8192]{1,0:T(8,128)(2,1)S(1)}, bf16[32,8192]{1,0:T(8,128)(2,1)S(1)}, u32[]{:S(2)}, u32[]{:S(2)}) collective-permute-start(bf16[32,8192]{1,0:T(8,128)(2,1)S(1)} %collective-permute-done.25), channel_id=1, source_target_pairs={{8,28},{12,8},{24,12},{28,24},{40,60},{44,40},{56,44},{60,56},{72,... | collective-permute-start | bytes 1572872 | tf_op jit(solution)/shard_map/ppermute | solution.py:51
  154.2 1.6 add_convert_fusion
  155.9 5.1 %backward_full.1 = (bf16[512,512]{1,0:T(8,128)(2,1)}, bf16[512,512]{1,0:T(8,128)(2,1)}, f32[16,512]{1,0:T(8,128)}, f32[16,512]{1,0:T(8,128)}, f32[8,512]{1,0:T(8,128)S(1)}) custom-call(bf16[512,512]{1,0:T(8,128)(2,1)S(1)} %copy-done.1, bf16[512,512]{1,0:T(8,128)(2,1)S(1)} %copy-done.3, f32[4,512,128]{2,1,0:T(8,128)S(1)} %get-tuple-element.94.refs_2_, ...), custom_call_target="tpu_custom_call" | custom-call | flops 115000000 | tf_op jit(solution)/shard_map/backward_full/pallas_call | solution.py:326
  (80 shorter events, 14.0 us)
Async XLA Ops:
  1.7 13.2 %collective-permute-start.1 = (bf16[32,4096]{1,0:T(8,128)(2,1)S(1)}, bf16[32,4096]{1,0:T(8,128)(2,1)S(1)}, u32[]{:S(2)}, u32[]{:S(2)}) collective-permute-start(bf16[32,4096]{1,0:T(8,128)(2,1)S(1)} %get-tuple-element.107), channel_id=1, source_target_pairs={{0,4},{8,12},{4,16},{12,24},{16,20},{24,28},{20,0},{28,8},{32,36},... | collective-permute-start | bytes 786440 | tf_op jit(solution)/shard_map/ppermute | solution.py:51
  3.4 11.5 %collective-permute-start.2 = (bf16[32,4096]{1,0:T(8,128)(2,1)S(1)}, bf16[32,4096]{1,0:T(8,128)(2,1)S(1)}, u32[]{:S(2)}, u32[]{:S(2)}) collective-permute-start(bf16[32,4096]{1,0:T(8,128)(2,1)S(1)} %get-tuple-element.107), channel_id=1, source_target_pairs={{0,20},{8,28},{4,0},{12,8},{16,4},{24,12},{20,16},{28,24},{32,52},... | collective-permute-start | bytes 786440 | tf_op jit(solution)/shard_map/ppermute | solution.py:51
  5.6 1.0 copy-start
  6.7 1.0 copy-start.2
  7.7 0.8 copy-start.5
  11.7 3.2 %collective-permute-start.3 = (f32[32,512]{1,0:T(8,128)S(1)}, f32[32,512]{1,0:T(8,128)S(1)}, u32[]{:S(2)}, u32[]{:S(2)}) collective-permute-start(f32[32,512]{1,0:T(8,128)S(1)} %get-tuple-element.56), channel_id=1, source_target_pairs={{0,4},{8,12},{4,0},{12,8},{16,20},{24,28},{20,16},{28,24},{32,36},... | collective-permute-start | bytes 196616 | tf_op jit(solution)/shard_map/ppermute | solution.py:51
  11.8 9.2 %collective-permute-start = (bf16[32,4096]{1,0:T(8,128)(2,1)S(1)}, bf16[32,4096]{1,0:T(8,128)(2,1)}, u32[]{:S(2)}, u32[]{:S(2)}) collective-permute-start(bf16[32,4096]{1,0:T(8,128)(2,1)S(1)} %get-tuple-element.106), channel_id=1, source_target_pairs={{0,16},{8,24},{4,20},{12,28},{16,0},{24,8},{20,4},{28,12},{32,48},... | collective-permute-start | bytes 786440 | tf_op jit(solution)/shard_map/ppermute | solution.py:51
  15.0 15.7 %copy-start.4 = (bf16[512,512]{1,0:T(8,128)(2,1)S(1)}, bf16[512,512]{1,0:T(8,128)(2,1)}, u32[]{:S(2)}) copy-start(bf16[512,512]{1,0:T(8,128)(2,1)} %query_ref.1) | copy-start | bytes 1572868
  15.0 15.7 %copy-start.6 = (f32[16,512]{1,0:T(8,128)S(1)}, f32[16,512]{1,0:T(8,128)}, u32[]{:S(2)}) copy-start(f32[16,512]{1,0:T(8,128)} %refs_4_.3) | copy-start | bytes 98308
  15.0 15.7 %copy-start.7 = (f32[16,512]{1,0:T(8,128)S(1)}, f32[16,512]{1,0:T(8,128)}, u32[]{:S(2)}) copy-start(f32[16,512]{1,0:T(8,128)} %refs_5_.1) | copy-start | bytes 98308
  15.0 15.7 %copy-start.8 = (f32[512]{0:T(512)S(1)}, f32[512]{0:T(512)}, u32[]{:S(2)}) copy-start(f32[512]{0:T(512)} %param.11) | copy-start | bytes 6148
  23.2 6.6 %collective-permute-start.6 = (f32[64,512]{1,0:T(8,128)S(1)}, f32[64,512]{1,0:T(8,128)S(1)}, u32[]{:S(2)}, u32[]{:S(2)}) collective-permute-start(f32[64,512]{1,0:T(8,128)S(1)} %pad_maximum_fusion.2.refs_6_), channel_id=1, source_target_pairs={{0,1},{8,9},{4,5},{12,13},{16,17},{24,25},{20,21},{28,29},{32,33},... | collective-permute-start | bytes 393224 | tf_op jit(solution)/shard_map/ppermute | solution.py:51
  24.4 5.4 %collective-permute-start.7 = (f32[64,512]{1,0:T(8,128)S(1)}, f32[64,512]{1,0:T(8,128)S(1)}, u32[]{:S(2)}, u32[]{:S(2)}) collective-permute-start(f32[64,512]{1,0:T(8,128)S(1)} %pad_maximum_fusion.2.refs_6_), channel_id=1, source_target_pairs={{0,2},{8,10},{4,6},{12,14},{16,18},{24,26},{20,22},{28,30},{32,34}... | collective-permute-start | bytes 393224 | tf_op jit(solution)/shard_map/ppermute | solution.py:51
  25.2 5.5 %collective-permute-start.8 = (f32[64,512]{1,0:T(8,128)S(1)}, f32[64,512]{1,0:T(8,128)S(1)}, u32[]{:S(2)}, u32[]{:S(2)}) collective-permute-start(f32[64,512]{1,0:T(8,128)S(1)} %pad_maximum_fusion.2.refs_6_), channel_id=1, source_target_pairs={{0,3},{8,11},{4,7},{12,15},{16,19},{24,27},{20,23},{28,31},{32,35}... | collective-permute-start | bytes 393224 | tf_op jit(solution)/shard_map/ppermute | solution.py:51
  27.1 7.5 %copy-start.10 = (bf16[2,2,32,4096]{3,2,1,0:T(8,128)(2,1)S(1)}, bf16[2,2,32,4096]{3,2,1,0:T(8,128)(2,1)}, u32[]{:S(2)}) copy-start(bf16[2,2,32,4096]{3,2,1,0:T(8,128)(2,1)} %pad_maximum_fusion) | copy-start | bytes 3145732
  27.1 22.8 %collective-permute-start.4 = (bf16[2,2,32,4096]{3,2,1,0:T(8,128)(2,1)}, bf16[2,2,32,4096]{3,2,1,0:T(8,128)(2,1)S(1)}, u32[]{:S(2)}, u32[]{:S(2)}) collective-permute-start(bf16[2,2,32,4096]{3,2,1,0:T(8,128)(2,1)} %pad_maximum_fusion), channel_id=1, source_target_pairs={{0,32},{8,104},{4,36},{12,108},{16,48},{24,120},{20,52},{28,124},{... | collective-permute-start | bytes 3145736 | tf_op jit(solution)/shard_map/ppermute | solution.py:51
  27.5 24.8 %collective-permute-start.5 = (bf16[2,2,32,4096]{3,2,1,0:T(8,128)(2,1)}, bf16[2,2,32,4096]{3,2,1,0:T(8,128)(2,1)S(1)}, u32[]{:S(2)}, u32[]{:S(2)}) collective-permute-start(bf16[2,2,32,4096]{3,2,1,0:T(8,128)(2,1)} %pad_maximum_fusion), channel_id=1, source_target_pairs={{0,96},{8,40},{4,100},{12,44},{16,112},{24,56},{20,116},{28,60},{3... | collective-permute-start | bytes 3145736 | tf_op jit(solution)/shard_map/ppermute | solution.py:51
  34.6 32.7 %collective-permute-start.9 = (bf16[2,2,32,4096]{3,2,1,0:T(8,128)(2,1)S(1)}, bf16[2,2,32,4096]{3,2,1,0:T(8,128)(2,1)S(1)}, u32[]{:S(2)}, u32[]{:S(2)}) collective-permute-start(bf16[2,2,32,4096]{3,2,1,0:T(8,128)(2,1)S(1)} %copy-done.10), channel_id=1, source_target_pairs={{0,8},{8,0},{4,12},{12,4},{16,24},{24,16},{20,28},{28,20},{32,40},... | collective-permute-start | bytes 3145736 | tf_op jit(solution)/shard_map/ppermute | solution.py:51
  38.3 29.4 %collective-permute-start.13 = (bf16[512,512]{1,0:T(8,128)(2,1)S(1)}, bf16[512,512]{1,0:T(8,128)(2,1)S(1)}, u32[]{:S(2)}, u32[]{:S(2)}) collective-permute-start(bf16[512,512]{1,0:T(8,128)(2,1)S(1)} %get-tuple-element.69), channel_id=1, source_target_pairs={{0,4},{8,12},{4,0},{12,8},{16,20},{24,28},{20,16},{28,24},{32,36},... | collective-permute-start | bytes 1572872 | tf_op jit(solution)/shard_map/ppermute | solution.py:51
  52.4 18.0 %collective-permute-start.10 = (bf16[2,2,32,4096]{3,2,1,0:T(8,128)(2,1)S(1)}, bf16[2,2,32,4096]{3,2,1,0:T(8,128)(2,1)S(1)}, u32[]{:S(2)}, u32[]{:S(2)}) collective-permute-start(bf16[2,2,32,4096]{3,2,1,0:T(8,128)(2,1)S(1)} %collective-permute-done.4), channel_id=1, source_target_pairs={{0,8},{8,0},{4,12},{12,4},{16,24},{24,16},{20,28},{28,20},{32,40},... | collective-permute-start | bytes 3145736 | tf_op jit(solution)/shard_map/ppermute | solution.py:51
  54.1 14.9 %collective-permute-start.12 = (bf16[2,2,32,4096]{3,2,1,0:T(8,128)(2,1)S(1)}, bf16[2,2,32,4096]{3,2,1,0:T(8,128)(2,1)S(1)}, u32[]{:S(2)}, u32[]{:S(2)}) collective-permute-start(bf16[2,2,32,4096]{3,2,1,0:T(8,128)(2,1)S(1)} %collective-permute-done.4), channel_id=1, source_target_pairs={{0,32},{8,104},{4,36},{12,108},{16,48},{24,120},{20,52},{28,124},{... | collective-permute-start | bytes 3145736 | tf_op jit(solution)/shard_map/ppermute | solution.py:51
  54.1 16.6 %collective-permute-start.11 = (bf16[2,2,32,4096]{3,2,1,0:T(8,128)(2,1)S(1)}, bf16[2,2,32,4096]{3,2,1,0:T(8,128)(2,1)S(1)}, u32[]{:S(2)}, u32[]{:S(2)}) collective-permute-start(bf16[2,2,32,4096]{3,2,1,0:T(8,128)(2,1)S(1)} %collective-permute-done.5), channel_id=1, source_target_pairs={{0,8},{8,0},{4,12},{12,4},{16,24},{24,16},{20,28},{28,20},{32,40},... | collective-permute-start | bytes 3145736 | tf_op jit(solution)/shard_map/ppermute | solution.py:51
  57.0 3.4 %copy-start.9 = (bf16[512,8192]{1,0:T(8,128)(2,1)S(1)}, bf16[512,8192]{1,0:T(8,128)(2,1)}, u32[]{:S(2)}) copy-start(bf16[512,8192]{1,0:T(8,128)(2,1)} %weight_ref.1) | copy-start | bytes 25165828
  67.3 2.7 %collective-permute-start.16 = (bf16[64,8192]{1,0:T(8,128)(2,1)S(1)}, bf16[64,8192]{1,0:T(8,128)(2,1)S(1)}, u32[]{:S(2)}, u32[]{:S(2)}) collective-permute-start(bf16[64,8192]{1,0:T(8,128)(2,1)S(1)} %get-tuple-element.75), channel_id=1, source_target_pairs={{0,8},{8,0},{4,12},{12,4},{16,24},{24,16},{20,28},{28,20},{32,40},... | collective-permute-start | bytes 3145736 | tf_op jit(solution)/shard_map/ppermute | solution.py:51
  68.9 3.2 %collective-permute-start.14 = (bf16[2,2,32,4096]{3,2,1,0:T(8,128)(2,1)S(1)}, bf16[2,2,32,4096]{3,2,1,0:T(8,128)(2,1)S(1)}, u32[]{:S(2)}, u32[]{:S(2)}) collective-permute-start(bf16[2,2,32,4096]{3,2,1,0:T(8,128)(2,1)S(1)} %collective-permute-done.12), channel_id=1, source_target_pairs={{0,8},{8,0},{4,12},{12,4},{16,24},{24,16},{20,28},{28,20},{32,40},... | collective-permute-start | bytes 3145736 | tf_op jit(solution)/shard_map/ppermute | solution.py:51
  69.4 15.9 %collective-permute-start.15 = (bf16[192,8192]{1,0:T(8,128)(2,1)S(1)}, bf16[192,8192]{1,0:T(8,128)(2,1)}, u32[]{:S(2)}, u32[]{:S(2)}) collective-permute-start(bf16[192,8192]{1,0:T(8,128)(2,1)S(1)} %get-tuple-element.73), channel_id=1, source_target_pairs={{0,8},{8,0},{4,12},{12,4},{16,24},{24,16},{20,28},{28,20},{32,40},... | collective-permute-start | bytes 9437192 | tf_op jit(solution)/shard_map/ppermute | solution.py:51
  70.3 15.0 %collective-permute-start.17 = (bf16[64,8192]{1,0:T(8,128)(2,1)S(1)}, bf16[64,8192]{1,0:T(8,128)(2,1)S(1)}, u32[]{:S(2)}, u32[]{:S(2)}) collective-permute-start(bf16[64,8192]{1,0:T(8,128)(2,1)S(1)} %add_convert_fusion.4), channel_id=1, source_target_pairs={{0,32},{8,104},{4,36},{12,108},{16,48},{24,120},{20,52},{28,124},{... | collective-permute-start | bytes 3145736 | tf_op jit(solution)/shard_map/ppermute | solution.py:51
  70.5 6.9 %slice-start = ((s8[8388608]{0:T(1024)(128)(4,1)}), s8[4194304]{0:T(1024)(128)(4,1)S(1)}, s32[]{:S(2)}) async-start(s8[8388608]{0:T(1024)(128)(4,1)} %bitcast.46), calls=%async_computation | async-start | bytes 8388608
  71.7 5.7 %slice-start.1 = ((s8[8388608]{0:T(1024)(128)(4,1)}), s8[4194304]{0:T(1024)(128)(4,1)S(1)}, s32[]{:S(2)}) async-start(s8[8388608]{0:T(1024)(128)(4,1)} %bitcast.46), calls=%async_computation.1 | async-start | bytes 8388608
  76.2 14.7 %collective-permute-start.19 = (bf16[512,1024]{1,0:T(8,128)(2,1)}, bf16[512,1024]{1,0:T(8,128)(2,1)}, u32[]{:S(2)}, u32[]{:S(2)}) collective-permute-start(bf16[512,1024]{1,0:T(8,128)(2,1)} %multiply_convert_fusion.3), channel_id=1, source_target_pairs={{0,1},{8,11},{4,5},{12,15},{16,17},{24,27},{20,21},{28,31},{32,33}... | collective-permute-start | bytes 3145736 | tf_op jit(solution)/shard_map/ppermute | solution.py:51
  85.4 12.6 %collective-permute-start.18 = (bf16[512,512]{1,0:T(8,128)(2,1)S(1)}, bf16[512,512]{1,0:T(8,128)(2,1)S(1)}, u32[]{:S(2)}, u32[]{:S(2)}) collective-permute-start(bf16[512,512]{1,0:T(8,128)(2,1)S(1)} %slice.50), channel_id=1, source_target_pairs={{0,4},{8,12},{4,0},{12,8},{16,20},{24,28},{20,16},{28,24},{32,36},... | collective-permute-start | bytes 1572872 | tf_op jit(solution)/shard_map/ppermute | solution.py:51
  88.1 34.6 %collective-permute-start.21 = (bf16[64,8192]{1,0:T(8,128)(2,1)S(1)}, bf16[64,8192]{1,0:T(8,128)(2,1)S(1)}, u32[]{:S(2)}, u32[]{:S(2)}) collective-permute-start(bf16[64,8192]{1,0:T(8,128)(2,1)S(1)} %get-tuple-element.105), channel_id=1, source_target_pairs={{0,32},{8,104},{4,36},{12,108},{16,48},{24,120},{20,52},{28,124},{... | collective-permute-start | bytes 3145736 | tf_op jit(solution)/shard_map/ppermute | solution.py:51
  88.2 34.5 %collective-permute-start.22 = (bf16[64,8192]{1,0:T(8,128)(2,1)S(1)}, bf16[64,8192]{1,0:T(8,128)(2,1)S(1)}, u32[]{:S(2)}, u32[]{:S(2)}) collective-permute-start(bf16[64,8192]{1,0:T(8,128)(2,1)S(1)} %get-tuple-element.104), channel_id=1, source_target_pairs={{0,96},{8,40},{4,100},{12,44},{16,112},{24,56},{20,116},{28,60},{3... | collective-permute-start | bytes 3145736 | tf_op jit(solution)/shard_map/ppermute | solution.py:51
  107.0 23.0 %collective-permute-start.23 = (bf16[512,1024]{1,0:T(8,128)(2,1)S(1)}, bf16[512,1024]{1,0:T(8,128)(2,1)S(1)}, u32[]{:S(2)}, u32[]{:S(2)}) collective-permute-start(bf16[512,1024]{1,0:T(8,128)(2,1)S(1)} %add_convert_fusion.3), channel_id=1, source_target_pairs={{0,1},{8,11},{4,5},{12,15},{16,17},{24,27},{20,21},{28,31},{32,33}... | collective-permute-start | bytes 3145736 | tf_op jit(solution)/shard_map/ppermute | solution.py:51
  109.1 24.9 %collective-permute-start.24 = (bf16[512,1024]{1,0:T(8,128)(2,1)S(1)}, bf16[512,1024]{1,0:T(8,128)(2,1)S(1)}, u32[]{:S(2)}, u32[]{:S(2)}) collective-permute-start(bf16[512,1024]{1,0:T(8,128)(2,1)S(1)} %multiply_convert_fusion.1), channel_id=1, source_target_pairs={{0,3},{8,9},{4,7},{12,13},{16,19},{24,25},{20,23},{28,29},{32,35},... | collective-permute-start | bytes 3145736 | tf_op jit(solution)/shard_map/ppermute | solution.py:51
  118.8 3.9 %collective-permute-start.20 = (f32[56,512]{1,0:T(8,128)S(1)}, f32[56,512]{1,0:T(8,128)S(1)}, u32[]{:S(2)}, u32[]{:S(2)}) collective-permute-start(f32[56,512]{1,0:T(8,128)S(1)} %get-tuple-element.85), channel_id=1, source_target_pairs={{0,4},{8,12},{4,0},{12,8},{16,20},{24,28},{20,16},{28,24},{32,36},... | collective-permute-start | bytes 344072 | tf_op jit(solution)/shard_map/ppermute | solution.py:51
  135.8 13.4 %collective-permute-start.25 = (bf16[32,8192]{1,0:T(8,128)(2,1)S(1)}, bf16[32,8192]{1,0:T(8,128)(2,1)S(1)}, u32[]{:S(2)}, u32[]{:S(2)}) collective-permute-start(bf16[32,8192]{1,0:T(8,128)(2,1)S(1)} %slice.49), channel_id=1, source_target_pairs={{0,16},{8,28},{4,20},{12,8},{16,0},{24,12},{20,4},{28,24},{32,48},... | collective-permute-start | bytes 1572872 | tf_op jit(solution)/shard_map/ppermute | solution.py:51
  137.5 18.3 %copy-start.1 = (bf16[512,512]{1,0:T(8,128)(2,1)S(1)}, bf16[512,512]{1,0:T(8,128)(2,1)}, u32[]{:S(2)}) copy-start(bf16[512,512]{1,0:T(8,128)(2,1)} %refs_0_.3) | copy-start | bytes 1572868
  137.5 18.3 %copy-start.3 = (bf16[512,512]{1,0:T(8,128)(2,1)S(1)}, bf16[512,512]{1,0:T(8,128)(2,1)}, u32[]{:S(2)}) copy-start(bf16[512,512]{1,0:T(8,128)(2,1)} %refs_1_.1) | copy-start | bytes 1572868
  137.5 4.7 %collective-permute-start.26 = (f32[72,512]{1,0:T(8,128)S(1)}, f32[72,512]{1,0:T(8,128)S(1)}, u32[]{:S(2)}, u32[]{:S(2)}) collective-permute-start(f32[72,512]{1,0:T(8,128)S(1)} %pad_maximum_fusion.1.refs_7_), channel_id=1, source_target_pairs={{0,1},{8,9},{4,5},{12,13},{16,17},{24,25},{20,21},{28,29},{32,33},... | collective-permute-start | bytes 442376 | tf_op jit(solution)/shard_map/ppermute | solution.py:51
  137.9 6.3 %collective-permute-start.27 = (f32[72,512]{1,0:T(8,128)S(1)}, f32[72,512]{1,0:T(8,128)S(1)}, u32[]{:S(2)}, u32[]{:S(2)}) collective-permute-start(f32[72,512]{1,0:T(8,128)S(1)} %pad_maximum_fusion.1.refs_7_), channel_id=1, source_target_pairs={{0,2},{8,10},{4,6},{12,14},{16,18},{24,26},{20,22},{28,30},{32,34}... | collective-permute-start | bytes 442376 | tf_op jit(solution)/shard_map/ppermute | solution.py:51
  139.2 8.2 %collective-permute-start.28 = (f32[72,512]{1,0:T(8,128)S(1)}, f32[72,512]{1,0:T(8,128)S(1)}, u32[]{:S(2)}, u32[]{:S(2)}) collective-permute-start(f32[72,512]{1,0:T(8,128)S(1)} %pad_maximum_fusion.1.refs_7_), channel_id=1, source_target_pairs={{0,3},{8,11},{4,7},{12,15},{16,19},{24,27},{20,23},{28,31},{32,35}... | collective-permute-start | bytes 442376 | tf_op jit(solution)/shard_map/ppermute | solution.py:51
  149.2 12.3 %collective-permute-start.29 = (bf16[32,8192]{1,0:T(8,128)(2,1)S(1)}, bf16[32,8192]{1,0:T(8,128)(2,1)S(1)}, u32[]{:S(2)}, u32[]{:S(2)}) collective-permute-start(bf16[32,8192]{1,0:T(8,128)(2,1)S(1)} %collective-permute-done.25), channel_id=1, source_target_pairs={{8,28},{12,8},{24,12},{28,24},{40,60},{44,40},{56,44},{60,56},{72,... | collective-permute-start | bytes 1572872 | tf_op jit(solution)/shard_map/ppermute | solution.py:51

commit v7 on v5

--- a/solution.py
+++ b/solution.py
@@ -149,7 +149,7 @@
             return now, lag
 
         zero = [zero_ref[...]] * modes
-        now, lag = lax.fori_loop(0, span, step, (zero, zero), unroll=4)
+        now, lag = lax.fori_loop(0, span, step, (zero, zero), unroll=8)
         for m in range(modes):
             sub_ref[tile, strided(m, modes)] = now[m]
             sub_ref[tile, strided(SUBS * modes + m, modes)] = lag[m]
@@ -199,7 +199,7 @@
             return now
 
         first = [lead_ref[tile, strided(m, modes)] for m in range(modes)]
-        lax.fori_loop(0, span, step, first, unroll=4)
+        lax.fori_loop(0, span, step, first, unroll=8)
         gated_ref[:, lanes] = (query_ref[:, lanes].astype(F32) * pre_ref[tile]).astype(BF16)
     part = length // (RING * 4)
     y, high, core, _, _ = places()
@@ -234,7 +234,7 @@
             return [decay[m] * now[m] + g for m in range(modes)]
 
         zero = [zero_ref[...]] * modes
-        now = lax.fori_loop(0, span, back_step, zero, unroll=4)
+        now = lax.fori_loop(0, span, back_step, zero, unroll=8)
         for m in range(modes):
             sub_ref[tile, strided(m, modes)] = now[m]
         for low in range(0, modes, half):
@@ -256,7 +256,7 @@
             lag = [lead_ref[tile, strided(SUBS * modes + m, modes)] for m in group]
             zero = [zero_ref[...]] * half
             state, lag, pair, lag_pair, skip = lax.fori_loop(
-                0, span, pair_step, (state, lag, zero, zero, zero[0]), unroll=4
+                0, span, pair_step, (state, lag, zero, zero, zero[0]), unroll=8
             )
             for m in range(half):
                 part_ref[tile, strided(low + m, modes)] = pair[m]
@@ -315,7 +315,7 @@
             return now
 
         first = [lead_ref[tile, strided(m, modes)] for m in range(modes)]
-        lax.fori_loop(0, span, step, first, unroll=4)
+        lax.fori_loop(0, span, step, first, unroll=8)
         drive_grad = drive_grad_ref[tile]
         grad_key_ref[:, lanes] = (drive_grad * value_ref[:, lanes].astype(F32)).astype(BF16)
         grad_value_ref[:, lanes] = (drive_grad * key_ref[:, lanes].astype(F32)).astype(BF16)
@@ -368,8 +368,10 @@
         "forward_ends",
     )
     ends_pair = jnp.concatenate([ends, hop(ends, pair=1)])
-    block, *earlier = together(block, *spread_over_x(ends_pair))
     main_block, other_block = hop(block, y=MAIN), hop(block, y=OTHER)
+    main_block, other_block, ends_pair = together(main_block, other_block, ends_pair)
+    far_block = hop(main_block, y=MAIN)
+    earlier = spread_over_x(ends_pair)
     gated, turned, pre_gate, lead = call(
         forward_full,
         (queries, driving, subs, log_decay, residue, skip_row, *earlier),
@@ -378,15 +380,16 @@
         0.1,
         "forward_full",
     )
-    main_block, other_block, turned = together(main_block, other_block, turned)
-    far_block = hop(main_block, y=MAIN)
+    block, gated = together(block, gated)
+    far_block, turned = together(far_block, turned)
     near_first, near_rest, far_first, far_rest = project(turned, out_weight)
-    far_block, far_first, gated_other = together(far_block, far_first, hop(gated, pair=1))
-    got_first, got_rest = hop(far_first, core=1), hop(far_rest, core=1)
+    far_first, gated_other = together(far_first, hop(gated, pair=1))
+    got_first, far_rest = together(hop(far_first, core=1), far_rest)
+    got_rest = hop(far_rest, core=1)
     gated_pair = jnp.concatenate([gated, gated_other])
     opposite = add(near_first, got_first).astype(BF16)
     cot_rows = place_blocks(block, main_block, other_block, far_block)
-    cot_rows, got_rest = together(cot_rows.reshape(2 * length, -1), got_rest)
+    cot_rows, opposite = together(cot_rows.reshape(2 * length, -1), opposite)
 
     _, _, core, low, x = places()
     half = out_weight.shape[1] // 2
@@ -396,7 +399,8 @@
     theirs = hop(grad_parts[length:].astype(BF16), pair=1)
 
     far_weight = weigh(gated_pair, cot_rows, scale, lax.rem(x + 2, RING))
-    cot_rows, far_weight, got_rest = together(cot_rows, far_weight, got_rest)
+    cot_rows, far_weight = together(cot_rows, far_weight)
+    got_rest, _ = together(got_rest, far_weight)
     main_weight, other_weight, own_weight = (
         weigh(gated_pair, cot_rows, scale, lax.rem(x + r, RING)) for r in (1 + 2 * core, 3 - 2 * core, 0)
     )

time: 156 us -> 165 us (1.058)
  the two profiles are of different devices: /device:TPU:1 before, /device:TPU:9 now
where the time goes in v7:
time: 165 us; the launch traced here: 164 us
  waiting for transfers between devices  64.5 us (39%)
  starting transfers between devices  34.6 us (21%)
  Pallas kernels  29.5 us (18%)
  matrix products  15.8 us (10%)
  local copies, waits for them, and re-layouts  13.8 us (8%)
  other arithmetic  4.85 us (3%)
    ppermute x30, waiting for transfers between devices, hop(): return lax.ppermute(value, ('chan', 'seq'), moves)  64.5 us
    ppermute x30, starting transfers between devices, hop(): return lax.ppermute(value, ('chan', 'seq'), moves)  34.6 us
    pallas_call x4, Pallas kernels, call(): pl.pallas_call(body, out_shape=[jax.ShapeDtypeStruct(o.shape, o.dtype) fo...  22.6 us
    dot_general x4, matrix products, weigh(): lax.dot_general(gated, columns, (((0,), (0,)), ((), ())), preferred_eleme...  9.97 us
    pallas_call x1, Pallas kernels, project(): pl.pallas_call(project_tile, grid=(width // tile,), out_shape=[jax.ShapeD...  6.86 us
    dot_general x1, matrix products, local(): lax.dot_general(cot_rows, low_weight, (((1,), (1,)), ((), ())), preferred...  5.87 us
    unnamed x33, local copies, waits for them, and re-layouts  5.23 us
    dynamic_update_slice x8, local copies, waits for them, and re-layouts, place_blocks(): lax.dynamic_update_slice(whole, part[:, None, :, None], (0, row, 0, at_co...  3.76 us
  transfers between devices with their start and end apart: 30, of which 18 were waited for; matrix products, arithmetic and copies ran while one was open for 17% of the time, Pallas kernels for 18%

profile of v7, /device:TPU:9, one launch (start us, length us, event | category | flops | bytes accessed | tf_op | source)
XLA Modules:
  0.0 164.2 jit_solution(4570571273246450698)
XLA Ops:
  0.7 1.1 constant_dynamic-slice_fusion.1
  1.7 1.7 %collective-permute-start.1 = (bf16[32,4096]{1,0:T(8,128)(2,1)S(1)}, bf16[32,4096]{1,0:T(8,128)(2,1)S(1)}, u32[]{:S(2)}, u32[]{:S(2)}) collective-permute-start(bf16[32,4096]{1,0:T(8,128)(2,1)S(1)} %get-tuple-element.113), channel_id=1, source_target_pairs={{0,4},{8,12},{4,16},{12,24},{16,20},{24,28},{20,0},{28,8},{32,36},... | collective-permute-start | bytes 786440 | tf_op jit(solution)/shard_map/ppermute | solution.py:51
  3.4 2.2 %collective-permute-start.2 = (bf16[32,4096]{1,0:T(8,128)(2,1)S(1)}, bf16[32,4096]{1,0:T(8,128)(2,1)S(1)}, u32[]{:S(2)}, u32[]{:S(2)}) collective-permute-start(bf16[32,4096]{1,0:T(8,128)(2,1)S(1)} %get-tuple-element.113), channel_id=1, source_target_pairs={{0,20},{8,28},{4,0},{12,8},{16,4},{24,12},{20,16},{28,24},{32,52},... | collective-permute-start | bytes 786440 | tf_op jit(solution)/shard_map/ppermute | solution.py:51
  5.6 1.2 collective-permute-start
  6.9 4.7 %collective-permute-done.1 = bf16[32,4096]{1,0:T(8,128)(2,1)S(1)} collective-permute-done((bf16[32,4096]{1,0:T(8,128)(2,1)S(1)}, bf16[32,4096]{1,0:T(8,128)(2,1)S(1)}, u32[]{:S(2)}, u32[]{:S(2)}) %collective-permute-start.1) | collective-permute-done | bytes 262176 | tf_op jit(solution)/shard_map/ppermute | solution.py:51
  11.8 6.3 %collective-permute-done = bf16[32,4096]{1,0:T(8,128)(2,1)S(1)} collective-permute-done((bf16[32,4096]{1,0:T(8,128)(2,1)S(1)}, bf16[32,4096]{1,0:T(8,128)(2,1)S(1)}, u32[]{:S(2)}, u32[]{:S(2)}) %collective-permute-start) | collective-permute-done | bytes 262176 | tf_op jit(solution)/shard_map/ppermute | solution.py:51
  18.5 1.3 collective-permute-start.4
  19.8 3.2 %forward_ends.1 = (f32[32,512]{1,0:T(8,128)S(1)}, f32[4,256,128]{2,1,0:T(8,128)S(1)}, f32[4,512,128]{2,1,0:T(8,128)S(1)}) custom-call(bf16[512,512]{1,0:T(8,128)(2,1)S(1)} %copy-done, bf16[512,512]{1,0:T(8,128)(2,1)S(1)} %copy-done.1, f32[16,512]{1,0:T(8,128)S(1)} %copy-done.3), custom_call_target="tpu_custom_call" | custom-call | flops 115000000 | tf_op jit(solution)/shard_map/forward_ends/pallas_call | solution.py:326
  23.7 2.9 %collective-permute-done.5 = f32[32,512]{1,0:T(8,128)S(1)} collective-permute-done((f32[32,512]{1,0:T(8,128)S(1)}, f32[32,512]{1,0:T(8,128)S(1)}, u32[]{:S(2)}, u32[]{:S(2)}) %collective-permute-start.5) | collective-permute-done | bytes 65568 | tf_op jit(solution)/shard_map/ppermute | solution.py:51
  26.6 13.3 %collective-permute-done.3 = bf16[2,2,32,4096]{3,2,1,0:T(8,128)(2,1)S(1)} collective-permute-done((bf16[2,2,32,4096]{3,2,1,0:T(8,128)(2,1)S(1)}, bf16[2,2,32,4096]{3,2,1,0:T(8,128)(2,1)S(1)}, u32[]{:S(2)}, u32[]{:S(2)}) %collective-permute-start.3) | collective-permute-done | bytes 1048608 | tf_op jit(solution)/shard_map/ppermute | solution.py:51
  39.9 4.6 %collective-permute-done.4 = bf16[2,2,32,4096]{3,2,1,0:T(8,128)(2,1)S(1)} collective-permute-done((bf16[2,2,32,4096]{3,2,1,0:T(8,128)(2,1)S(1)}, bf16[2,2,32,4096]{3,2,1,0:T(8,128)(2,1)S(1)}, u32[]{:S(2)}, u32[]{:S(2)}) %collective-permute-start.4) | collective-permute-done | bytes 1048608 | tf_op jit(solution)/shard_map/ppermute | solution.py:51
  44.5 1.2 collective-permute-start.7
  45.7 2.5 %collective-permute-start.8 = (f32[64,512]{1,0:T(8,128)S(1)}, f32[64,512]{1,0:T(8,128)}, u32[]{:S(2)}, u32[]{:S(2)}) collective-permute-start(f32[64,512]{1,0:T(8,128)S(1)} %pad_maximum_fusion.2.refs_6_), channel_id=1, source_target_pairs={{0,2},{8,10},{4,6},{12,14},{16,18},{24,26},{20,22},{28,30},{32,34}... | collective-permute-start | bytes 393224 | tf_op jit(solution)/shard_map/ppermute | solution.py:51
  48.2 1.2 collective-permute-start.9
  49.3 1.8 %collective-permute-start.14 = (bf16[2,2,32,4096]{3,2,1,0:T(8,128)(2,1)}, bf16[2,2,32,4096]{3,2,1,0:T(8,128)(2,1)S(1)}, u32[]{:S(2)}, u32[]{:S(2)}) collective-permute-start(bf16[2,2,32,4096]{3,2,1,0:T(8,128)(2,1)} %copy-done.12), channel_id=1, source_target_pairs={{0,8},{8,0},{4,12},{12,4},{16,24},{24,16},{20,28},{28,20},{32,40},... | collective-permute-start | bytes 3145736 | tf_op jit(solution)/shard_map/ppermute | solution.py:51
  51.1 1.3 collective-permute-start.6
  53.8 4.8 %forward_full.1 = (bf16[512,512]{1,0:T(8,128)(2,1)S(1)}, bf16[512,512]{1,0:T(8,128)(2,1)S(1)}, f32[4,512,128]{2,1,0:T(8,128)S(1)}, f32[4,256,128]{2,1,0:T(8,128)S(1)}) custom-call(bf16[512,512]{1,0:T(8,128)(2,1)S(1)} %copy-done.2, f32[4,512,128]{2,1,0:T(8,128)S(1)} %get-tuple-element.61.refs_1_.drive_ref, f32[4,256,128]{2,1,0:T(8,128)S(1)} %get-tuple-element.62.refs_2_, ...), custom_call_target="tpu_custom_call" | custom-call | flops 115000000 | tf_op jit(solution)/shard_map/forward_full/pallas_call | solution.py:326
  58.6 1.8 %collective-permute-start.13 = (bf16[2,2,32,4096]{3,2,1,0:T(8,128)(2,1)S(1)}, bf16[2,2,32,4096]{3,2,1,0:T(8,128)(2,1)S(1)}, u32[]{:S(2)}, u32[]{:S(2)}) collective-permute-start(bf16[2,2,32,4096]{3,2,1,0:T(8,128)(2,1)S(1)} %copy-done.8), channel_id=1, source_target_pairs={{0,8},{8,0},{4,12},{12,4},{16,24},{24,16},{20,28},{28,20},{32,40},... | collective-permute-start | bytes 3145736 | tf_op jit(solution)/shard_map/ppermute | solution.py:51
  60.7 1.0 broadcast_in_dim.27
  62.7 2.7 %collective-permute-done.6 = bf16[2,2,32,4096]{3,2,1,0:T(8,128)(2,1)} collective-permute-done((bf16[2,2,32,4096]{3,2,1,0:T(8,128)(2,1)}, bf16[2,2,32,4096]{3,2,1,0:T(8,128)(2,1)}, u32[]{:S(2)}, u32[]{:S(2)}) %collective-permute-start.6) | collective-permute-done | bytes 1048608 | tf_op jit(solution)/shard_map/ppermute | solution.py:51
  66.2 3.4 %copy-done.6 = bf16[512,8192]{1,0:T(8,128)(2,1)S(1)} copy-done((bf16[512,8192]{1,0:T(8,128)(2,1)S(1)}, bf16[512,8192]{1,0:T(8,128)(2,1)}, u32[]{:S(2)}) %copy-start.6) | copy-done | bytes 8388632
  69.6 6.9 %project.1 = (bf16[64,8192]{1,0:T(8,128)(2,1)S(1)}, bf16[192,8192]{1,0:T(8,128)(2,1)S(1)}, bf16[64,8192]{1,0:T(8,128)(2,1)S(1)}, bf16[192,8192]{1,0:T(8,128)(2,1)S(1)}) custom-call(bf16[512,512]{1,0:T(8,128)(2,1)S(1)} %get-tuple-element.65.rows_ref, bf16[512,8192]{1,0:T(8,128)(2,1)S(1)} %copy-done.6), custom_call_target="tpu_custom_call" | custom-call | flops 4294967296 | bytes 16777216 | tf_op jit(solution)/shard_map/project/pallas_call | solution.py:99
  78.9 1.6 bitcast_dynamic-update-slice_fusion.1
  80.5 1.5 bitcast_dynamic-update-slice_fusion
  83.0 5.9 %fusion = f32[1024,512]{1,0:T(8,128)} fusion(bf16[1024,4096]{1,0:T(8,128)(2,1)S(1)} %bitcast.48, bf16[512,8192]{1,0:T(8,128)(2,1)S(1)} %bitcast.47, s32[]{:T(128)S(6)} %select_n.129), kind=kOutput, calls=%fused_computation | convolution fusion | flops 4294967296 | bytes 14680068 | tf_op jit(solution)/shard_map/dot_general | solution.py:397
  88.9 1.3 slice.50
  91.0 3.0 %collective-permute-start.18 = (bf16[64,8192]{1,0:T(8,128)(2,1)S(1)}, bf16[64,8192]{1,0:T(8,128)(2,1)S(1)}, u32[]{:S(2)}, u32[]{:S(2)}) collective-permute-start(bf16[64,8192]{1,0:T(8,128)(2,1)S(1)} %add_convert_fusion.4), channel_id=1, source_target_pairs={{0,32},{8,104},{4,36},{12,108},{16,48},{24,120},{20,52},{28,124},{... | collective-permute-start | bytes 3145736 | tf_op jit(solution)/shard_map/ppermute | solution.py:51
  94.0 2.5 %multiply_convert_fusion.3 = bf16[512,1024]{1,0:T(8,128)(2,1)S(1)} fusion(bf16[1024,512]{1,0:T(8,128)(2,1)} %constant_dynamic-update-slice_fusion, bf16[1024,4096]{1,0:T(8,128)(2,1)S(1)} %bitcast.49, s32[]{:T(128)S(6)} %select_n.149), kind=kOutput, calls=%fused_computation.16 | convolution fusion | flops 1074790400 | bytes 4194308 | tf_op jit(solution)/shard_map/dot_general | solution.py:116
  96.6 2.5 %multiply_convert_fusion.2 = bf16[512,1024]{1,0:T(8,128)(2,1)S(1)} fusion(bf16[1024,512]{1,0:T(8,128)(2,1)} %constant_dynamic-update-slice_fusion, bf16[1024,4096]{1,0:T(8,128)(2,1)S(1)} %bitcast.50, s32[]{:T(128)S(6)} %select_n.150), kind=kOutput, calls=%fused_computation.11 | convolution fusion | flops 1074790400 | bytes 4194308 | tf_op jit(solution)/shard_map/dot_general | solution.py:116
  99.1 2.5 %multiply_convert_fusion.1 = bf16[512,1024]{1,0:T(8,128)(2,1)S(1)} fusion(bf16[1024,512]{1,0:T(8,128)(2,1)} %constant_dynamic-update-slice_fusion, bf16[1024,4096]{1,0:T(8,128)(2,1)S(1)} %bitcast.51, s32[]{:T(128)S(6)} %select_n.151), kind=kOutput, calls=%fused_computation.8 | convolution fusion | flops 1074790400 | bytes 4194308 | tf_op jit(solution)/shard_map/dot_general | solution.py:116
  101.6 2.5 %multiply_convert_fusion = bf16[512,1024]{1,0:T(8,128)(2,1)S(1)} fusion(bf16[1024,512]{1,0:T(8,128)(2,1)} %constant_dynamic-update-slice_fusion, bf16[1024,4096]{1,0:T(8,128)(2,1)S(1)} %bitcast.52, s32[]{:T(128)S(6)} %select_n.152), kind=kOutput, calls=%fused_computation.5 | convolution fusion | flops 1074790400 | bytes 4194308 | tf_op jit(solution)/shard_map/dot_general | solution.py:116
  104.1 1.6 collective-permute-done.18
  106.4 3.8 %collective-permute-done.19 = bf16[512,1024]{1,0:T(8,128)(2,1)S(1)} collective-permute-done((bf16[512,1024]{1,0:T(8,128)(2,1)S(1)}, bf16[512,1024]{1,0:T(8,128)(2,1)S(1)}, u32[]{:S(2)}, u32[]{:S(2)}) %collective-permute-start.19) | collective-permute-done | bytes 1048608 | tf_op jit(solution)/shard_map/ppermute | solution.py:51
  111.0 1.2 collective-permute-start.22
  112.1 1.3 collective-permute-start.23
  113.8 9.5 %backward_ends.1 = (bf16[512,512]{1,0:T(8,128)(2,1)}, f32[4,512,128]{2,1,0:T(8,128)S(1)}, f32[56,512]{1,0:T(8,128)S(1)}, f32[4,128,128]{2,1,0:T(8,128)S(1)}) custom-call(f32[512,512]{1,0:T(8,128)S(1)} %convert_add_fusion.1.grad_ref, bf16[512,512]{1,0:T(8,128)(2,1)S(1)} %copy-done.2, f32[4,512,128]{2,1,0:T(8,128)S(1)} %get-tuple-element.88.pre_ref, ...), custom_call_target="tpu_custom_call" | custom-call | flops 2300000000 | tf_op jit(solution)/shard_map/backward_ends/pallas_call | solution.py:326
  123.8 3.5 %collective-permute-done.20 = f32[56,512]{1,0:T(8,128)S(1)} collective-permute-done((f32[56,512]{1,0:T(8,128)S(1)}, f32[56,512]{1,0:T(8,128)S(1)}, u32[]{:S(2)}, u32[]{:S(2)}) %collective-permute-start.20) | collective-permute-done | bytes 114720 | tf_op jit(solution)/shard_map/ppermute | solution.py:51
  127.2 4.4 %collective-permute-done.21 = bf16[64,8192]{1,0:T(8,128)(2,1)S(1)} collective-permute-done((bf16[64,8192]{1,0:T(8,128)(2,1)S(1)}, bf16[64,8192]{1,0:T(8,128)(2,1)S(1)}, u32[]{:S(2)}, u32[]{:S(2)}) %collective-permute-start.21) | collective-permute-done | bytes 1048608 | tf_op jit(solution)/shard_map/ppermute | solution.py:51
  131.6 3.3 %collective-permute-done.22 = bf16[64,8192]{1,0:T(8,128)(2,1)S(1)} collective-permute-done((bf16[64,8192]{1,0:T(8,128)(2,1)S(1)}, bf16[64,8192]{1,0:T(8,128)(2,1)S(1)}, u32[]{:S(2)}, u32[]{:S(2)}) %collective-permute-start.22) | collective-permute-done | bytes 1048608 | tf_op jit(solution)/shard_map/ppermute | solution.py:51
  135.1 3.8 %collective-permute-done.24 = bf16[512,1024]{1,0:T(8,128)(2,1)S(1)} collective-permute-done((bf16[512,1024]{1,0:T(8,128)(2,1)S(1)}, bf16[512,1024]{1,0:T(8,128)(2,1)S(1)}, u32[]{:S(2)}, u32[]{:S(2)}) %collective-permute-start.24) | collective-permute-done | bytes 1048608 | tf_op jit(solution)/shard_map/ppermute | solution.py:51
  139.4 1.3 collective-permute-start.25
  141.3 2.2 %collective-permute-start.28 = (f32[72,512]{1,0:T(8,128)S(1)}, f32[72,512]{1,0:T(8,128)S(1)}, u32[]{:S(2)}, u32[]{:S(2)}) collective-permute-start(f32[72,512]{1,0:T(8,128)S(1)} %pad_maximum_fusion.1.refs_7_), channel_id=1, source_target_pairs={{0,3},{8,11},{4,7},{12,15},{16,19},{24,27},{20,23},{28,31},{32,35}... | collective-permute-start | bytes 442376 | tf_op jit(solution)/shard_map/ppermute | solution.py:51
  143.5 4.7 %collective-permute-done.26.refs_8_ = f32[72,512]{1,0:T(8,128)S(1)} collective-permute-done((f32[72,512]{1,0:T(8,128)S(1)}, f32[72,512]{1,0:T(8,128)S(1)}, u32[]{:S(2)}, u32[]{:S(2)}) %collective-permute-start.26) | collective-permute-done | bytes 147488 | tf_op jit(solution)/shard_map/ppermute | solution.py:51
  148.6 3.0 %collective-permute-done.25 = bf16[32,8192]{1,0:T(8,128)(2,1)S(1)} collective-permute-done((bf16[32,8192]{1,0:T(8,128)(2,1)S(1)}, bf16[32,8192]{1,0:T(8,128)(2,1)S(1)}, u32[]{:S(2)}, u32[]{:S(2)}) %collective-permute-start.25) | collective-permute-done | bytes 524320 | tf_op jit(solution)/shard_map/ppermute | solution.py:51
  151.6 4.4 %collective-permute-start.29 = (bf16[32,8192]{1,0:T(8,128)(2,1)S(1)}, bf16[32,8192]{1,0:T(8,128)(2,1)S(1)}, u32[]{:S(2)}, u32[]{:S(2)}) collective-permute-start(bf16[32,8192]{1,0:T(8,128)(2,1)S(1)} %collective-permute-done.25), channel_id=1, source_target_pairs={{8,28},{12,8},{24,12},{28,24},{40,60},{44,40},{56,44},{60,56},{72,... | collective-permute-start | bytes 1572872 | tf_op jit(solution)/shard_map/ppermute | solution.py:51
  156.0 1.6 add_convert_fusion
  157.6 5.0 %backward_full.1 = (bf16[512,512]{1,0:T(8,128)(2,1)}, bf16[512,512]{1,0:T(8,128)(2,1)}, f32[16,512]{1,0:T(8,128)}, f32[16,512]{1,0:T(8,128)}, f32[8,512]{1,0:T(8,128)S(1)}) custom-call(bf16[512,512]{1,0:T(8,128)(2,1)S(1)} %copy-done, bf16[512,512]{1,0:T(8,128)(2,1)S(1)} %copy-done.1, f32[4,512,128]{2,1,0:T(8,128)S(1)} %get-tuple-element.100.refs_2_, ...), custom_call_target="tpu_custom_call" | custom-call | flops 115000000 | tf_op jit(solution)/shard_map/backward_full/pallas_call | solution.py:326
  163.2 1.0 fusion.18
  (86 shorter events, 13.4 us)
Async XLA Ops:
  1.7 9.9 %collective-permute-start.1 = (bf16[32,4096]{1,0:T(8,128)(2,1)S(1)}, bf16[32,4096]{1,0:T(8,128)(2,1)S(1)}, u32[]{:S(2)}, u32[]{:S(2)}) collective-permute-start(bf16[32,4096]{1,0:T(8,128)(2,1)S(1)} %get-tuple-element.113), channel_id=1, source_target_pairs={{0,4},{8,12},{4,16},{12,24},{16,20},{24,28},{20,0},{28,8},{32,36},... | collective-permute-start | bytes 786440 | tf_op jit(solution)/shard_map/ppermute | solution.py:51
  3.4 8.2 %collective-permute-start.2 = (bf16[32,4096]{1,0:T(8,128)(2,1)S(1)}, bf16[32,4096]{1,0:T(8,128)(2,1)S(1)}, u32[]{:S(2)}, u32[]{:S(2)}) collective-permute-start(bf16[32,4096]{1,0:T(8,128)(2,1)S(1)} %get-tuple-element.113), channel_id=1, source_target_pairs={{0,20},{8,28},{4,0},{12,8},{16,4},{24,12},{20,16},{28,24},{32,52},... | collective-permute-start | bytes 786440 | tf_op jit(solution)/shard_map/ppermute | solution.py:51
  5.6 12.4 %collective-permute-start = (bf16[32,4096]{1,0:T(8,128)(2,1)S(1)}, bf16[32,4096]{1,0:T(8,128)(2,1)S(1)}, u32[]{:S(2)}, u32[]{:S(2)}) collective-permute-start(bf16[32,4096]{1,0:T(8,128)(2,1)S(1)} %get-tuple-element.112), channel_id=1, source_target_pairs={{0,16},{8,24},{4,20},{12,28},{16,0},{24,8},{20,4},{28,12},{32,48},... | collective-permute-start | bytes 786440 | tf_op jit(solution)/shard_map/ppermute | solution.py:51
  11.6 8.2 %copy-start = (bf16[512,512]{1,0:T(8,128)(2,1)S(1)}, bf16[512,512]{1,0:T(8,128)(2,1)}, u32[]{:S(2)}) copy-start(bf16[512,512]{1,0:T(8,128)(2,1)} %refs_0_.3) | copy-start | bytes 1572868
  11.7 8.2 %copy-start.1 = (bf16[512,512]{1,0:T(8,128)(2,1)S(1)}, bf16[512,512]{1,0:T(8,128)(2,1)}, u32[]{:S(2)}) copy-start(bf16[512,512]{1,0:T(8,128)(2,1)} %refs_1_.1) | copy-start | bytes 1572868
  11.7 8.2 %copy-start.3 = (f32[16,512]{1,0:T(8,128)S(1)}, f32[16,512]{1,0:T(8,128)}, u32[]{:S(2)}) copy-start(f32[16,512]{1,0:T(8,128)} %refs_4_.3) | copy-start | bytes 98308
  18.2 35.6 %copy-start.2 = (bf16[512,512]{1,0:T(8,128)(2,1)S(1)}, bf16[512,512]{1,0:T(8,128)(2,1)}, u32[]{:S(2)}) copy-start(bf16[512,512]{1,0:T(8,128)(2,1)} %query_ref.1) | copy-start | bytes 1572868
  18.2 35.6 %copy-start.4 = (f32[16,512]{1,0:T(8,128)S(1)}, f32[16,512]{1,0:T(8,128)}, u32[]{:S(2)}) copy-start(f32[16,512]{1,0:T(8,128)} %refs_5_.1) | copy-start | bytes 98308
  18.2 35.6 %copy-start.5 = (f32[512]{0:T(512)S(1)}, f32[512]{0:T(512)}, u32[]{:S(2)}) copy-start(f32[512]{0:T(512)} %param.11) | copy-start | bytes 6148
  18.3 27.4 %copy-start.7 = (bf16[2,2,32,4096]{3,2,1,0:T(8,128)(2,1)}, bf16[2,2,32,4096]{3,2,1,0:T(8,128)(2,1)S(1)}, u32[]{:S(2)}) copy-start(bf16[2,2,32,4096]{3,2,1,0:T(8,128)(2,1)S(1)} %pad_maximum_fusion) | copy-start | bytes 3145732
  18.3 21.6 %collective-permute-start.3 = (bf16[2,2,32,4096]{3,2,1,0:T(8,128)(2,1)S(1)}, bf16[2,2,32,4096]{3,2,1,0:T(8,128)(2,1)S(1)}, u32[]{:S(2)}, u32[]{:S(2)}) collective-permute-start(bf16[2,2,32,4096]{3,2,1,0:T(8,128)(2,1)S(1)} %pad_maximum_fusion), channel_id=1, source_target_pairs={{0,32},{8,104},{4,36},{12,108},{16,48},{24,120},{20,52},{28,124},{... | collective-permute-start | bytes 3145736 | tf_op jit(solution)/shard_map/ppermute | solution.py:51
  18.5 25.9 %collective-permute-start.4 = (bf16[2,2,32,4096]{3,2,1,0:T(8,128)(2,1)S(1)}, bf16[2,2,32,4096]{3,2,1,0:T(8,128)(2,1)S(1)}, u32[]{:S(2)}, u32[]{:S(2)}) collective-permute-start(bf16[2,2,32,4096]{3,2,1,0:T(8,128)(2,1)S(1)} %pad_maximum_fusion), channel_id=1, source_target_pairs={{0,96},{8,40},{4,100},{12,44},{16,112},{24,56},{20,116},{28,60},{3... | collective-permute-start | bytes 3145736 | tf_op jit(solution)/shard_map/ppermute | solution.py:51
  23.1 3.5 %collective-permute-start.5 = (f32[32,512]{1,0:T(8,128)S(1)}, f32[32,512]{1,0:T(8,128)S(1)}, u32[]{:S(2)}, u32[]{:S(2)}) collective-permute-start(f32[32,512]{1,0:T(8,128)S(1)} %get-tuple-element.59), channel_id=1, source_target_pairs={{0,4},{8,12},{4,0},{12,8},{16,20},{24,28},{20,16},{28,24},{32,36},... | collective-permute-start | bytes 196616 | tf_op jit(solution)/shard_map/ppermute | solution.py:51
  39.9 8.3 %copy-start.12 = (bf16[2,2,32,4096]{3,2,1,0:T(8,128)(2,1)}, bf16[2,2,32,4096]{3,2,1,0:T(8,128)(2,1)S(1)}, u32[]{:S(2)}) copy-start(bf16[2,2,32,4096]{3,2,1,0:T(8,128)(2,1)S(1)} %collective-permute-done.3) | copy-start | bytes 3145732
  44.5 3.7 %copy-start.10 = (bf16[2,2,32,4096]{3,2,1,0:T(8,128)(2,1)}, bf16[2,2,32,4096]{3,2,1,0:T(8,128)(2,1)S(1)}, u32[]{:S(2)}) copy-start(bf16[2,2,32,4096]{3,2,1,0:T(8,128)(2,1)S(1)} %collective-permute-done.4) | copy-start | bytes 3145732
  44.5 7.9 %collective-permute-start.7 = (f32[64,512]{1,0:T(8,128)S(1)}, f32[64,512]{1,0:T(8,128)S(1)}, u32[]{:S(2)}, u32[]{:S(2)}) collective-permute-start(f32[64,512]{1,0:T(8,128)S(1)} %pad_maximum_fusion.2.refs_6_), channel_id=1, source_target_pairs={{0,1},{8,9},{4,5},{12,13},{16,17},{24,25},{20,21},{28,29},{32,33},... | collective-permute-start | bytes 393224 | tf_op jit(solution)/shard_map/ppermute | solution.py:51
  45.7 7.6 %collective-permute-start.8 = (f32[64,512]{1,0:T(8,128)S(1)}, f32[64,512]{1,0:T(8,128)}, u32[]{:S(2)}, u32[]{:S(2)}) collective-permute-start(f32[64,512]{1,0:T(8,128)S(1)} %pad_maximum_fusion.2.refs_6_), channel_id=1, source_target_pairs={{0,2},{8,10},{4,6},{12,14},{16,18},{24,26},{20,22},{28,30},{32,34}... | collective-permute-start | bytes 393224 | tf_op jit(solution)/shard_map/ppermute | solution.py:51
  48.2 5.6 %collective-permute-start.9 = (f32[64,512]{1,0:T(8,128)S(1)}, f32[64,512]{1,0:T(8,128)}, u32[]{:S(2)}, u32[]{:S(2)}) collective-permute-start(f32[64,512]{1,0:T(8,128)S(1)} %pad_maximum_fusion.2.refs_6_), channel_id=1, source_target_pairs={{0,3},{8,11},{4,7},{12,15},{16,19},{24,27},{20,23},{28,31},{32,35}... | collective-permute-start | bytes 393224 | tf_op jit(solution)/shard_map/ppermute | solution.py:51
  49.3 9.3 %copy-start.8 = (bf16[2,2,32,4096]{3,2,1,0:T(8,128)(2,1)S(1)}, bf16[2,2,32,4096]{3,2,1,0:T(8,128)(2,1)}, u32[]{:S(2)}) copy-start(bf16[2,2,32,4096]{3,2,1,0:T(8,128)(2,1)} %copy-done.7) | copy-start | bytes 3145732
  49.3 28.7 %collective-permute-start.14 = (bf16[2,2,32,4096]{3,2,1,0:T(8,128)(2,1)}, bf16[2,2,32,4096]{3,2,1,0:T(8,128)(2,1)S(1)}, u32[]{:S(2)}, u32[]{:S(2)}) collective-permute-start(bf16[2,2,32,4096]{3,2,1,0:T(8,128)(2,1)} %copy-done.12), channel_id=1, source_target_pairs={{0,8},{8,0},{4,12},{12,4},{16,24},{24,16},{20,28},{28,20},{32,40},... | collective-permute-start | bytes 3145736 | tf_op jit(solution)/shard_map/ppermute | solution.py:51
  51.1 14.3 %collective-permute-start.6 = (bf16[2,2,32,4096]{3,2,1,0:T(8,128)(2,1)}, bf16[2,2,32,4096]{3,2,1,0:T(8,128)(2,1)}, u32[]{:S(2)}, u32[]{:S(2)}) collective-permute-start(bf16[2,2,32,4096]{3,2,1,0:T(8,128)(2,1)} %copy-done.12), channel_id=1, source_target_pairs={{0,32},{8,104},{4,36},{12,108},{16,48},{24,120},{20,52},{28,124},{... | collective-permute-start | bytes 3145736 | tf_op jit(solution)/shard_map/ppermute | solution.py:51
  52.4 26.5 %collective-permute-start.15 = (bf16[2,2,32,4096]{3,2,1,0:T(8,128)(2,1)}, bf16[2,2,32,4096]{3,2,1,0:T(8,128)(2,1)}, u32[]{:S(2)}, u32[]{:S(2)}) collective-permute-start(bf16[2,2,32,4096]{3,2,1,0:T(8,128)(2,1)} %copy-done.10), channel_id=1, source_target_pairs={{0,8},{8,0},{4,12},{12,4},{16,24},{24,16},{20,28},{28,20},{32,40},... | collective-permute-start | bytes 3145736 | tf_op jit(solution)/shard_map/ppermute | solution.py:51
  58.6 18.8 %collective-permute-start.13 = (bf16[2,2,32,4096]{3,2,1,0:T(8,128)(2,1)S(1)}, bf16[2,2,32,4096]{3,2,1,0:T(8,128)(2,1)S(1)}, u32[]{:S(2)}, u32[]{:S(2)}) collective-permute-start(bf16[2,2,32,4096]{3,2,1,0:T(8,128)(2,1)S(1)} %copy-done.8), channel_id=1, source_target_pairs={{0,8},{8,0},{4,12},{12,4},{16,24},{24,16},{20,28},{28,20},{32,40},... | collective-permute-start | bytes 3145736 | tf_op jit(solution)/shard_map/ppermute | solution.py:51
  60.5 16.1 %collective-permute-start.10 = (bf16[512,512]{1,0:T(8,128)(2,1)S(1)}, bf16[512,512]{1,0:T(8,128)(2,1)S(1)}, u32[]{:S(2)}, u32[]{:S(2)}) collective-permute-start(bf16[512,512]{1,0:T(8,128)(2,1)S(1)} %get-tuple-element.69), channel_id=1, source_target_pairs={{0,4},{8,12},{4,0},{12,8},{16,20},{24,28},{20,16},{28,24},{32,36},... | collective-permute-start | bytes 1572872 | tf_op jit(solution)/shard_map/ppermute | solution.py:51
  65.4 17.5 %collective-permute-start.16 = (bf16[2,2,32,4096]{3,2,1,0:T(8,128)(2,1)}, bf16[2,2,32,4096]{3,2,1,0:T(8,128)(2,1)S(1)}, u32[]{:S(2)}, u32[]{:S(2)}) collective-permute-start(bf16[2,2,32,4096]{3,2,1,0:T(8,128)(2,1)} %collective-permute-done.6), channel_id=1, source_target_pairs={{0,8},{8,0},{4,12},{12,4},{16,24},{24,16},{20,28},{28,20},{32,40},... | collective-permute-start | bytes 3145736 | tf_op jit(solution)/shard_map/ppermute | solution.py:51
  66.2 3.4 %copy-start.6 = (bf16[512,8192]{1,0:T(8,128)(2,1)S(1)}, bf16[512,8192]{1,0:T(8,128)(2,1)}, u32[]{:S(2)}) copy-start(bf16[512,8192]{1,0:T(8,128)(2,1)} %weight_ref.1) | copy-start | bytes 25165828
  76.5 1.4 copy-start.13
  76.5 5.5 %collective-permute-start.11 = (bf16[64,8192]{1,0:T(8,128)(2,1)S(1)}, bf16[64,8192]{1,0:T(8,128)(2,1)S(1)}, u32[]{:S(2)}, u32[]{:S(2)}) collective-permute-start(bf16[64,8192]{1,0:T(8,128)(2,1)S(1)} %get-tuple-element.70), channel_id=1, source_target_pairs={{0,8},{8,0},{4,12},{12,4},{16,24},{24,16},{20,28},{28,20},{32,40},... | collective-permute-start | bytes 3145736 | tf_op jit(solution)/shard_map/ppermute | solution.py:51
  77.4 1.3 copy-start.11
  77.9 5.1 %slice-start = ((s8[8388608]{0:T(1024)(128)(4,1)}), s8[4194304]{0:T(1024)(128)(4,1)S(1)}, s32[]{:S(2)}) async-start(s8[8388608]{0:T(1024)(128)(4,1)} %bitcast.46), calls=%async_computation | async-start | bytes 8388608
  78.9 4.1 %slice-start.1 = ((s8[8388608]{0:T(1024)(128)(4,1)}), s8[4194304]{0:T(1024)(128)(4,1)S(1)}, s32[]{:S(2)}) async-start(s8[8388608]{0:T(1024)(128)(4,1)} %bitcast.46), calls=%async_computation.1 | async-start | bytes 8388608
  82.0 22.1 %collective-permute-start.12 = (bf16[192,8192]{1,0:T(8,128)(2,1)S(1)}, bf16[192,8192]{1,0:T(8,128)(2,1)S(1)}, u32[]{:S(2)}, u32[]{:S(2)}) collective-permute-start(bf16[192,8192]{1,0:T(8,128)(2,1)S(1)} %get-tuple-element.72), channel_id=1, source_target_pairs={{0,8},{8,0},{4,12},{12,4},{16,24},{24,16},{20,28},{28,20},{32,40},... | collective-permute-start | bytes 9437192 | tf_op jit(solution)/shard_map/ppermute | solution.py:51
  90.2 20.4 %collective-permute-start.17 = (bf16[512,512]{1,0:T(8,128)(2,1)S(1)}, bf16[512,512]{1,0:T(8,128)(2,1)S(1)}, u32[]{:S(2)}, u32[]{:S(2)}) collective-permute-start(bf16[512,512]{1,0:T(8,128)(2,1)S(1)} %slice.50), channel_id=1, source_target_pairs={{0,4},{8,12},{4,0},{12,8},{16,20},{24,28},{20,16},{28,24},{32,36},... | collective-permute-start | bytes 1572872 | tf_op jit(solution)/shard_map/ppermute | solution.py:51
  91.0 14.7 %collective-permute-start.18 = (bf16[64,8192]{1,0:T(8,128)(2,1)S(1)}, bf16[64,8192]{1,0:T(8,128)(2,1)S(1)}, u32[]{:S(2)}, u32[]{:S(2)}) collective-permute-start(bf16[64,8192]{1,0:T(8,128)(2,1)S(1)} %add_convert_fusion.4), channel_id=1, source_target_pairs={{0,32},{8,104},{4,36},{12,108},{16,48},{24,120},{20,52},{28,124},{... | collective-permute-start | bytes 3145736 | tf_op jit(solution)/shard_map/ppermute | solution.py:51
  96.5 13.7 %collective-permute-start.19 = (bf16[512,1024]{1,0:T(8,128)(2,1)S(1)}, bf16[512,1024]{1,0:T(8,128)(2,1)S(1)}, u32[]{:S(2)}, u32[]{:S(2)}) collective-permute-start(bf16[512,1024]{1,0:T(8,128)(2,1)S(1)} %multiply_convert_fusion.3), channel_id=1, source_target_pairs={{0,1},{8,11},{4,5},{12,15},{16,17},{24,27},{20,21},{28,31},{32,33}... | collective-permute-start | bytes 3145736 | tf_op jit(solution)/shard_map/ppermute | solution.py:51
  106.4 7.2 %copy-start.9 = (f32[1024,512]{1,0:T(8,128)S(1)}, f32[1024,512]{1,0:T(8,128)}, u32[]{:S(2)}) copy-start(f32[1024,512]{1,0:T(8,128)} %fusion) | copy-start | bytes 6291460
  110.6 21.0 %collective-permute-start.21 = (bf16[64,8192]{1,0:T(8,128)(2,1)S(1)}, bf16[64,8192]{1,0:T(8,128)(2,1)S(1)}, u32[]{:S(2)}, u32[]{:S(2)}) collective-permute-start(bf16[64,8192]{1,0:T(8,128)(2,1)S(1)} %get-tuple-element.91), channel_id=1, source_target_pairs={{0,32},{8,104},{4,36},{12,108},{16,48},{24,120},{20,52},{28,124},{... | collective-permute-start | bytes 3145736 | tf_op jit(solution)/shard_map/ppermute | solution.py:51
  111.0 23.9 %collective-permute-start.22 = (bf16[64,8192]{1,0:T(8,128)(2,1)S(1)}, bf16[64,8192]{1,0:T(8,128)(2,1)S(1)}, u32[]{:S(2)}, u32[]{:S(2)}) collective-permute-start(bf16[64,8192]{1,0:T(8,128)(2,1)S(1)} %get-tuple-element.92), channel_id=1, source_target_pairs={{0,96},{8,40},{4,100},{12,44},{16,112},{24,56},{20,116},{28,60},{3... | collective-permute-start | bytes 3145736 | tf_op jit(solution)/shard_map/ppermute | solution.py:51
  112.1 22.9 %collective-permute-start.23 = (bf16[512,1024]{1,0:T(8,128)(2,1)S(1)}, bf16[512,1024]{1,0:T(8,128)(2,1)S(1)}, u32[]{:S(2)}, u32[]{:S(2)}) collective-permute-start(bf16[512,1024]{1,0:T(8,128)(2,1)S(1)} %add_convert_fusion.1), channel_id=1, source_target_pairs={{0,1},{8,11},{4,5},{12,15},{16,17},{24,27},{20,21},{28,31},{32,33}... | collective-permute-start | bytes 3145736 | tf_op jit(solution)/shard_map/ppermute | solution.py:51
  113.4 25.5 %collective-permute-start.24 = (bf16[512,1024]{1,0:T(8,128)(2,1)S(1)}, bf16[512,1024]{1,0:T(8,128)(2,1)S(1)}, u32[]{:S(2)}, u32[]{:S(2)}) collective-permute-start(bf16[512,1024]{1,0:T(8,128)(2,1)S(1)} %multiply_convert_fusion.1), channel_id=1, source_target_pairs={{0,3},{8,9},{4,7},{12,13},{16,19},{24,25},{20,23},{28,29},{32,35},... | collective-permute-start | bytes 3145736 | tf_op jit(solution)/shard_map/ppermute | solution.py:51
  123.3 3.9 %collective-permute-start.20 = (f32[56,512]{1,0:T(8,128)S(1)}, f32[56,512]{1,0:T(8,128)S(1)}, u32[]{:S(2)}, u32[]{:S(2)}) collective-permute-start(f32[56,512]{1,0:T(8,128)S(1)} %get-tuple-element.90), channel_id=1, source_target_pairs={{0,4},{8,12},{4,0},{12,8},{16,20},{24,28},{20,16},{28,24},{32,36},... | collective-permute-start | bytes 344072 | tf_op jit(solution)/shard_map/ppermute | solution.py:51
  139.4 12.2 %collective-permute-start.25 = (bf16[32,8192]{1,0:T(8,128)(2,1)S(1)}, bf16[32,8192]{1,0:T(8,128)(2,1)S(1)}, u32[]{:S(2)}, u32[]{:S(2)}) collective-permute-start(bf16[32,8192]{1,0:T(8,128)(2,1)S(1)} %slice.49), channel_id=1, source_target_pairs={{0,16},{8,28},{4,20},{12,8},{16,0},{24,12},{20,4},{28,24},{32,48},... | collective-permute-start | bytes 1572872 | tf_op jit(solution)/shard_map/ppermute | solution.py:51
  140.8 7.4 %collective-permute-start.26 = (f32[72,512]{1,0:T(8,128)S(1)}, f32[72,512]{1,0:T(8,128)S(1)}, u32[]{:S(2)}, u32[]{:S(2)}) collective-permute-start(f32[72,512]{1,0:T(8,128)S(1)} %pad_maximum_fusion.1.refs_7_), channel_id=1, source_target_pairs={{0,1},{8,9},{4,5},{12,13},{16,17},{24,25},{20,21},{28,29},{32,33},... | collective-permute-start | bytes 442376 | tf_op jit(solution)/shard_map/ppermute | solution.py:51
  140.9 7.3 %collective-permute-start.27 = (f32[72,512]{1,0:T(8,128)S(1)}, f32[72,512]{1,0:T(8,128)S(1)}, u32[]{:S(2)}, u32[]{:S(2)}) collective-permute-start(f32[72,512]{1,0:T(8,128)S(1)} %pad_maximum_fusion.1.refs_7_), channel_id=1, source_target_pairs={{0,2},{8,10},{4,6},{12,14},{16,18},{24,26},{20,22},{28,30},{32,34}... | collective-permute-start | bytes 442376 | tf_op jit(solution)/shard_map/ppermute | solution.py:51
  141.3 7.3 %collective-permute-start.28 = (f32[72,512]{1,0:T(8,128)S(1)}, f32[72,512]{1,0:T(8,128)S(1)}, u32[]{:S(2)}, u32[]{:S(2)}) collective-permute-start(f32[72,512]{1,0:T(8,128)S(1)} %pad_maximum_fusion.1.refs_7_), channel_id=1, source_target_pairs={{0,3},{8,11},{4,7},{12,15},{16,19},{24,27},{20,23},{28,31},{32,35}... | collective-permute-start | bytes 442376 | tf_op jit(solution)/shard_map/ppermute | solution.py:51
  151.6 11.6 %collective-permute-start.29 = (bf16[32,8192]{1,0:T(8,128)(2,1)S(1)}, bf16[32,8192]{1,0:T(8,128)(2,1)S(1)}, u32[]{:S(2)}, u32[]{:S(2)}) collective-permute-start(bf16[32,8192]{1,0:T(8,128)(2,1)S(1)} %collective-permute-done.25), channel_id=1, source_target_pairs={{8,28},{12,8},{24,12},{28,24},{40,60},{44,40},{56,44},{60,56},{72,... | collective-permute-start | bytes 1572872 | tf_op jit(solution)/shard_map/ppermute | solution.py:51

commit v8 on v7

--- a/solution.py
+++ b/solution.py
@@ -368,10 +368,8 @@
         "forward_ends",
     )
     ends_pair = jnp.concatenate([ends, hop(ends, pair=1)])
+    block, *earlier = together(block, *spread_over_x(ends_pair))
     main_block, other_block = hop(block, y=MAIN), hop(block, y=OTHER)
-    main_block, other_block, ends_pair = together(main_block, other_block, ends_pair)
-    far_block = hop(main_block, y=MAIN)
-    earlier = spread_over_x(ends_pair)
     gated, turned, pre_gate, lead = call(
         forward_full,
         (queries, driving, subs, log_decay, residue, skip_row, *earlier),
@@ -380,22 +378,22 @@
         0.1,
         "forward_full",
     )
-    block, gated = together(block, gated)
-    far_block, turned = together(far_block, turned)
+    main_block, other_block, turned = together(main_block, other_block, turned)
+    far_block = hop(main_block, y=MAIN)
     near_first, near_rest, far_first, far_rest = project(turned, out_weight)
-    far_first, gated_other = together(far_first, hop(gated, pair=1))
+    far_block, far_rest, gated_other = together(far_block, far_rest, hop(gated, pair=1))
     got_first, far_rest = together(hop(far_first, core=1), far_rest)
     got_rest = hop(far_rest, core=1)
     gated_pair = jnp.concatenate([gated, gated_other])
     opposite = add(near_first, got_first).astype(BF16)
     cot_rows = place_blocks(block, main_block, other_block, far_block)
-    cot_rows, opposite = together(cot_rows.reshape(2 * length, -1), opposite)
+    cot_rows = cot_rows.reshape(2 * length, -1)
 
     _, _, core, low, x = places()
     half = out_weight.shape[1] // 2
     low_weight = lax.dynamic_slice(out_weight, (0, low * half), (channels, half))
     grad_parts = lax.dot_general(cot_rows, low_weight, (((1,), (1,)), ((), ())), preferred_element_type=F32)
-    cot_rows, grad_parts = together(cot_rows, grad_parts)
+    cot_rows, grad_parts, opposite = together(cot_rows, grad_parts, hop(opposite, y=MAIN))
     theirs = hop(grad_parts[length:].astype(BF16), pair=1)
 
     far_weight = weigh(gated_pair, cot_rows, scale, lax.rem(x + 2, RING))
@@ -405,7 +403,7 @@
         weigh(gated_pair, cot_rows, scale, lax.rem(x + r, RING)) for r in (1 + 2 * core, 3 - 2 * core, 0)
     )
     main, other, own = (add(a, b) for a, b in zip(jnp.split(near_rest, 3), jnp.split(got_rest, 3)))
-    main = add(main, hop(opposite, y=MAIN)).astype(BF16)
+    main = add(main, opposite).astype(BF16)
     main, other, main_weight, other_weight, own_weight = together(
         main, other.astype(BF16), main_weight, other_weight, own_weight
     )

time: 165 us -> 164 us (level)
  the two profiles are of different devices: /device:TPU:9 before, /device:TPU:25 now
where the time goes in v8:
time: 164 us
  waiting for transfers between devices  53.3 us (32%)
  starting transfers between devices  40.1 us (24%)
  Pallas kernels  28.5 us (17%)
  matrix products  18.4 us (11%)
  local copies, waits for them, and re-layouts  17.5 us (11%)
  other arithmetic  4.89 us (3%)
    ppermute x30, waiting for transfers between devices, hop(): return lax.ppermute(value, ('chan', 'seq'), moves)  53.3 us
    ppermute x30, starting transfers between devices, hop(): return lax.ppermute(value, ('chan', 'seq'), moves)  40.1 us
    pallas_call x4, Pallas kernels, call(): pl.pallas_call(body, out_shape=[jax.ShapeDtypeStruct(o.shape, o.dtype) fo...  21.6 us
    dot_general x4, matrix products, weigh(): lax.dot_general(gated, columns, (((0,), (0,)), ((), ())), preferred_eleme...  11.4 us
    dynamic_update_slice x8, local copies, waits for them, and re-layouts, place_blocks(): lax.dynamic_update_slice(whole, part[:, None, :, None], (0, row, 0, at_co...  8.42 us
    dot_general x1, matrix products, local(): lax.dot_general(cot_rows, low_weight, (((1,), (1,)), ((), ())), preferred...  6.93 us
    pallas_call x1, Pallas kernels, project(): pl.pallas_call(project_tile, grid=(width // tile,), out_shape=[jax.ShapeD...  6.87 us
    broadcast_in_dim x1, local copies, waits for them, and re-layouts, place_blocks(): whole = jnp.zeros((2, RING, 2, 2, tokens, half), BF16)  4.35 us
  transfers between devices with their start and end apart: 30, of which 14 were waited for; matrix products, arithmetic and copies ran while one was open for 22% of the time, Pallas kernels for 17%

profile of v8, /device:TPU:25, one launch (start us, length us, event | category | flops | bytes accessed | tf_op | source)
XLA Modules:
  0.0 163.6 jit_solution(35726714560904208)
XLA Ops:
  0.7 1.1 constant_dynamic-slice_fusion.1
  1.7 1.7 %collective-permute-start.1 = (bf16[32,4096]{1,0:T(8,128)(2,1)S(1)}, bf16[32,4096]{1,0:T(8,128)(2,1)S(1)}, u32[]{:S(2)}, u32[]{:S(2)}) collective-permute-start(bf16[32,4096]{1,0:T(8,128)(2,1)S(1)} %get-tuple-element.115), channel_id=1, source_target_pairs={{0,4},{8,12},{4,16},{12,24},{16,20},{24,28},{20,0},{28,8},{32,36},... | collective-permute-start | bytes 786440 | tf_op jit(solution)/shard_map/ppermute | solution.py:51
  3.4 2.2 %collective-permute-start.2 = (bf16[32,4096]{1,0:T(8,128)(2,1)S(1)}, bf16[32,4096]{1,0:T(8,128)(2,1)S(1)}, u32[]{:S(2)}, u32[]{:S(2)}) collective-permute-start(bf16[32,4096]{1,0:T(8,128)(2,1)S(1)} %get-tuple-element.115), channel_id=1, source_target_pairs={{0,20},{8,28},{4,0},{12,8},{16,4},{24,12},{20,16},{28,24},{32,52},... | collective-permute-start | bytes 786440 | tf_op jit(solution)/shard_map/ppermute | solution.py:51
  5.6 1.2 collective-permute-start
  6.9 1.0 copy-done
  9.7 3.2 %forward_ends.1 = (f32[32,512]{1,0:T(8,128)S(1)}, f32[4,256,128]{2,1,0:T(8,128)S(1)}, f32[4,512,128]{2,1,0:T(8,128)S(1)}) custom-call(bf16[512,512]{1,0:T(8,128)(2,1)S(1)} %copy-done, bf16[512,512]{1,0:T(8,128)(2,1)S(1)} %copy-done.2, f32[16,512]{1,0:T(8,128)S(1)} %copy-done.5), custom_call_target="tpu_custom_call" | custom-call | flops 115000000 | tf_op jit(solution)/shard_map/forward_ends/pallas_call | solution.py:326
  13.7 4.0 %collective-permute-done.3 = f32[32,512]{1,0:T(8,128)S(1)} collective-permute-done((f32[32,512]{1,0:T(8,128)S(1)}, f32[32,512]{1,0:T(8,128)S(1)}, u32[]{:S(2)}, u32[]{:S(2)}) %collective-permute-start.3) | collective-permute-done | bytes 65568 | tf_op jit(solution)/shard_map/ppermute | solution.py:51
  17.7 1.2 collective-permute-start.4
  19.0 2.5 %collective-permute-start.5 = (f32[64,512]{1,0:T(8,128)S(1)}, f32[64,512]{1,0:T(8,128)S(1)}, u32[]{:S(2)}, u32[]{:S(2)}) collective-permute-start(f32[64,512]{1,0:T(8,128)S(1)} %constant_dynamic-update-slice_fusion.refs_6_), channel_id=1, source_target_pairs={{0,2},{8,10},{4,6},{12,14},{16,18},{24,26},{20,22},{28,30},{32,34}... | collective-permute-start | bytes 393224 | tf_op jit(solution)/shard_map/ppermute | solution.py:51
  21.4 1.2 collective-permute-start.6
  23.0 2.8 %collective-permute-done.5.refs_8_ = f32[64,512]{1,0:T(8,128)S(1)} collective-permute-done((f32[64,512]{1,0:T(8,128)S(1)}, f32[64,512]{1,0:T(8,128)S(1)}, u32[]{:S(2)}, u32[]{:S(2)}) %collective-permute-start.5) | collective-permute-done | bytes 131104 | tf_op jit(solution)/shard_map/ppermute | solution.py:51
  26.5 2.3 %collective-permute-start.13 = (bf16[2,2,32,4096]{3,2,1,0:T(8,128)(2,1)S(1)}, bf16[2,2,32,4096]{3,2,1,0:T(8,128)(2,1)S(1)}, u32[]{:S(2)}, u32[]{:S(2)}) collective-permute-start(bf16[2,2,32,4096]{3,2,1,0:T(8,128)(2,1)S(1)} %pad_maximum_fusion), channel_id=1, source_target_pairs={{0,8},{8,0},{4,12},{12,4},{16,24},{24,16},{20,28},{28,20},{32,40},... | collective-permute-start | bytes 3145736 | tf_op jit(solution)/shard_map/ppermute | solution.py:51
  29.2 2.2 %collective-permute-start.8 = (bf16[2,2,32,4096]{3,2,1,0:T(8,128)(2,1)S(1)}, bf16[2,2,32,4096]{3,2,1,0:T(8,128)(2,1)S(1)}, u32[]{:S(2)}, u32[]{:S(2)}) collective-permute-start(bf16[2,2,32,4096]{3,2,1,0:T(8,128)(2,1)S(1)} %pad_maximum_fusion), channel_id=1, source_target_pairs={{0,96},{8,40},{4,100},{12,44},{16,112},{24,56},{20,116},{28,60},{3... | collective-permute-start | bytes 3145736 | tf_op jit(solution)/shard_map/ppermute | solution.py:51
  31.4 3.8 %forward_full.1 = (bf16[512,512]{1,0:T(8,128)(2,1)S(1)}, bf16[512,512]{1,0:T(8,128)(2,1)S(1)}, f32[4,512,128]{2,1,0:T(8,128)S(1)}, f32[4,256,128]{2,1,0:T(8,128)S(1)}) custom-call(bf16[512,512]{1,0:T(8,128)(2,1)S(1)} %copy-done.4, f32[4,512,128]{2,1,0:T(8,128)S(1)} %get-tuple-element.62.refs_1_.drive_ref, f32[4,256,128]{2,1,0:T(8,128)S(1)} %get-tuple-element.63.refs_2_, ...), custom_call_target="tpu_custom_call" | custom-call | flops 115000000 | tf_op jit(solution)/shard_map/forward_full/pallas_call | solution.py:326
  35.6 4.4 %broadcast_in_dim.27 = bf16[2,4,2,2,32,4096]{5,4,3,2,1,0:T(8,128)(2,1)} broadcast(bf16[]{:T(256)} %constant.80.clone.1), dimensions={} | broadcast | bytes 8388610 | tf_op jit(solution)/shard_map/broadcast_in_dim | solution.py:74
  39.9 1.1 bitcast_dynamic-update-slice_fusion.6
  41.0 13.5 %collective-permute-done.7 = bf16[2,2,32,4096]{3,2,1,0:T(8,128)(2,1)S(1)} collective-permute-done((bf16[2,2,32,4096]{3,2,1,0:T(8,128)(2,1)S(1)}, bf16[2,2,32,4096]{3,2,1,0:T(8,128)(2,1)S(1)}, u32[]{:S(2)}, u32[]{:S(2)}) %collective-permute-start.7) | collective-permute-done | bytes 1048608 | tf_op jit(solution)/shard_map/ppermute | solution.py:51
  56.0 6.9 %project.1 = (bf16[64,8192]{1,0:T(8,128)(2,1)S(1)}, bf16[192,8192]{1,0:T(8,128)(2,1)S(1)}, bf16[64,8192]{1,0:T(8,128)(2,1)S(1)}, bf16[192,8192]{1,0:T(8,128)(2,1)S(1)}) custom-call(bf16[512,512]{1,0:T(8,128)(2,1)S(1)} %get-tuple-element.69.rows_ref, bf16[512,8192]{1,0:T(8,128)(2,1)S(1)} %bitcast.47), custom_call_target="tpu_custom_call" | custom-call | flops 4294967296 | bytes 16777216 | tf_op jit(solution)/shard_map/project/pallas_call | solution.py:99
  63.0 1.0 bitcast_dynamic-update-slice_fusion.5
  65.1 5.3 %collective-permute-done.10 = bf16[2,2,32,4096]{3,2,1,0:T(8,128)(2,1)S(1)} collective-permute-done((bf16[2,2,32,4096]{3,2,1,0:T(8,128)(2,1)S(1)}, bf16[2,2,32,4096]{3,2,1,0:T(8,128)(2,1)S(1)}, u32[]{:S(2)}, u32[]{:S(2)}) %collective-permute-start.10) | collective-permute-done | bytes 1048608 | tf_op jit(solution)/shard_map/ppermute | solution.py:51
  70.7 1.6 %collective-permute-start.12 = (bf16[192,8192]{1,0:T(8,128)(2,1)S(1)}, bf16[192,8192]{1,0:T(8,128)(2,1)S(1)}, u32[]{:S(2)}, u32[]{:S(2)}) collective-permute-start(bf16[192,8192]{1,0:T(8,128)(2,1)S(1)} %get-tuple-element.76), channel_id=1, source_target_pairs={{0,8},{8,0},{4,12},{12,4},{16,24},{24,16},{20,28},{28,20},{32,40},... | collective-permute-start | bytes 9437192 | tf_op jit(solution)/shard_map/ppermute | solution.py:51
  72.4 1.1 bitcast_dynamic-update-slice_fusion.3
  74.4 1.1 bitcast_dynamic-update-slice_fusion.1
  75.6 1.1 bitcast_dynamic-update-slice_fusion
  76.6 1.0 bitcast_dynamic-update-slice_fusion.7
  77.7 6.9 %fusion = f32[1024,512]{1,0:T(8,128)S(1)} fusion(bf16[1024,4096]{1,0:T(8,128)(2,1)} %bitcast.20, bf16[512,8192]{1,0:T(8,128)(2,1)S(1)} %bitcast.47, s32[]{:T(128)S(6)} %select_n.129), kind=kOutput, calls=%fused_computation | convolution fusion | flops 4294967296 | bytes 14680068 | tf_op jit(solution)/shard_map/dot_general | solution.py:395
  85.9 2.9 %multiply_convert_fusion.3 = bf16[512,1024]{1,0:T(8,128)(2,1)S(1)} fusion(bf16[1024,512]{1,0:T(8,128)(2,1)S(1)} %constant_dynamic-update-slice_fusion.2, bf16[1024,4096]{1,0:T(8,128)(2,1)} %bitcast.20, s32[]{:T(128)S(6)} %select_n.149), kind=kOutput, calls=%fused_computation.16 | convolution fusion | flops 1074790400 | bytes 4194308 | tf_op jit(solution)/shard_map/dot_general | solution.py:116
  88.7 2.5 %collective-permute-start.19 = (bf16[512,1024]{1,0:T(8,128)(2,1)S(1)}, bf16[512,1024]{1,0:T(8,128)(2,1)S(1)}, u32[]{:S(2)}, u32[]{:S(2)}) collective-permute-start(bf16[512,1024]{1,0:T(8,128)(2,1)S(1)} %multiply_convert_fusion.3), channel_id=1, source_target_pairs={{0,1},{8,11},{4,5},{12,15},{16,17},{24,27},{20,21},{28,31},{32,33}... | collective-permute-start | bytes 3145736 | tf_op jit(solution)/shard_map/ppermute | solution.py:51
  91.2 2.9 %multiply_convert_fusion.2 = bf16[512,1024]{1,0:T(8,128)(2,1)S(1)} fusion(bf16[1024,512]{1,0:T(8,128)(2,1)S(1)} %constant_dynamic-update-slice_fusion.2, bf16[1024,4096]{1,0:T(8,128)(2,1)} %bitcast.20, s32[]{:T(128)S(6)} %select_n.150), kind=kOutput, calls=%fused_computation.11 | convolution fusion | flops 1074790400 | bytes 4194308 | tf_op jit(solution)/shard_map/dot_general | solution.py:116
  94.1 2.9 %multiply_convert_fusion.1 = bf16[512,1024]{1,0:T(8,128)(2,1)S(1)} fusion(bf16[1024,512]{1,0:T(8,128)(2,1)S(1)} %constant_dynamic-update-slice_fusion.2, bf16[1024,4096]{1,0:T(8,128)(2,1)} %bitcast.20, s32[]{:T(128)S(6)} %select_n.151), kind=kOutput, calls=%fused_computation.8 | convolution fusion | flops 1074790400 | bytes 4194308 | tf_op jit(solution)/shard_map/dot_general | solution.py:116
  96.9 2.9 %multiply_convert_fusion = bf16[512,1024]{1,0:T(8,128)(2,1)S(1)} fusion(bf16[1024,512]{1,0:T(8,128)(2,1)S(1)} %constant_dynamic-update-slice_fusion.2, bf16[1024,4096]{1,0:T(8,128)(2,1)} %bitcast.20, s32[]{:T(128)S(6)} %select_n.152), kind=kOutput, calls=%fused_computation.5 | convolution fusion | flops 1074790400 | bytes 4194308 | tf_op jit(solution)/shard_map/dot_general | solution.py:116
  100.6 2.4 %collective-permute-done.19 = bf16[512,1024]{1,0:T(8,128)(2,1)S(1)} collective-permute-done((bf16[512,1024]{1,0:T(8,128)(2,1)S(1)}, bf16[512,1024]{1,0:T(8,128)(2,1)S(1)}, u32[]{:S(2)}, u32[]{:S(2)}) %collective-permute-start.19) | collective-permute-done | bytes 1048608 | tf_op jit(solution)/shard_map/ppermute | solution.py:51
  103.4 2.7 %collective-permute-start.22 = (bf16[64,8192]{1,0:T(8,128)(2,1)S(1)}, bf16[64,8192]{1,0:T(8,128)(2,1)S(1)}, u32[]{:S(2)}, u32[]{:S(2)}) collective-permute-start(bf16[64,8192]{1,0:T(8,128)(2,1)S(1)} %get-tuple-element.94), channel_id=1, source_target_pairs={{0,96},{8,40},{4,100},{12,44},{16,112},{24,56},{20,116},{28,60},{3... | collective-permute-start | bytes 3145736 | tf_op jit(solution)/shard_map/ppermute | solution.py:51
  106.1 3.1 %collective-permute-start.23 = (bf16[512,1024]{1,0:T(8,128)(2,1)S(1)}, bf16[512,1024]{1,0:T(8,128)(2,1)S(1)}, u32[]{:S(2)}, u32[]{:S(2)}) collective-permute-start(bf16[512,1024]{1,0:T(8,128)(2,1)S(1)} %add_convert_fusion.1), channel_id=1, source_target_pairs={{0,1},{8,11},{4,5},{12,15},{16,17},{24,27},{20,21},{28,31},{32,33}... | collective-permute-start | bytes 3145736 | tf_op jit(solution)/shard_map/ppermute | solution.py:51
  109.4 9.5 %backward_ends.1 = (bf16[512,512]{1,0:T(8,128)(2,1)}, f32[4,512,128]{2,1,0:T(8,128)S(1)}, f32[56,512]{1,0:T(8,128)S(1)}, f32[4,128,128]{2,1,0:T(8,128)S(1)}) custom-call(f32[512,512]{1,0:T(8,128)S(1)} %convert_add_fusion.1.grad_ref, bf16[512,512]{1,0:T(8,128)(2,1)S(1)} %copy-done.4, f32[4,512,128]{2,1,0:T(8,128)S(1)} %get-tuple-element.90.pre_ref, ...), custom_call_target="tpu_custom_call" | custom-call | flops 2300000000 | tf_op jit(solution)/shard_map/backward_ends/pallas_call | solution.py:326
  118.9 1.3 collective-permute-start.20
  120.2 2.7 %collective-permute-done.20 = f32[56,512]{1,0:T(8,128)S(1)} collective-permute-done((f32[56,512]{1,0:T(8,128)S(1)}, f32[56,512]{1,0:T(8,128)S(1)}, u32[]{:S(2)}, u32[]{:S(2)}) %collective-permute-start.20) | collective-permute-done | bytes 114720 | tf_op jit(solution)/shard_map/ppermute | solution.py:51
  122.8 1.5 collective-permute-done.21
  124.3 2.2 %collective-permute-done.22 = bf16[64,8192]{1,0:T(8,128)(2,1)S(1)} collective-permute-done((bf16[64,8192]{1,0:T(8,128)(2,1)S(1)}, bf16[64,8192]{1,0:T(8,128)(2,1)S(1)}, u32[]{:S(2)}, u32[]{:S(2)}) %collective-permute-start.22) | collective-permute-done | bytes 1048608 | tf_op jit(solution)/shard_map/ppermute | solution.py:51
  126.6 3.0 %collective-permute-done.23 = bf16[512,1024]{1,0:T(8,128)(2,1)S(1)} collective-permute-done((bf16[512,1024]{1,0:T(8,128)(2,1)S(1)}, bf16[512,1024]{1,0:T(8,128)(2,1)S(1)}, u32[]{:S(2)}, u32[]{:S(2)}) %collective-permute-start.23) | collective-permute-done | bytes 1048608 | tf_op jit(solution)/shard_map/ppermute | solution.py:51
  129.6 5.4 %collective-permute-done.24 = bf16[512,1024]{1,0:T(8,128)(2,1)S(1)} collective-permute-done((bf16[512,1024]{1,0:T(8,128)(2,1)S(1)}, bf16[512,1024]{1,0:T(8,128)(2,1)S(1)}, u32[]{:S(2)}, u32[]{:S(2)}) %collective-permute-start.24) | collective-permute-done | bytes 1048608 | tf_op jit(solution)/shard_map/ppermute | solution.py:51
  135.5 3.1 %collective-permute-start.25 = (bf16[32,8192]{1,0:T(8,128)(2,1)S(1)}, bf16[32,8192]{1,0:T(8,128)(2,1)S(1)}, u32[]{:S(2)}, u32[]{:S(2)}) collective-permute-start(bf16[32,8192]{1,0:T(8,128)(2,1)S(1)} %slice.49), channel_id=1, source_target_pairs={{0,16},{8,28},{4,20},{12,8},{16,0},{24,12},{20,4},{28,24},{32,48},... | collective-permute-start | bytes 1572872 | tf_op jit(solution)/shard_map/ppermute | solution.py:51
  139.5 1.9 %collective-permute-start.28 = (f32[72,512]{1,0:T(8,128)S(1)}, f32[72,512]{1,0:T(8,128)S(1)}, u32[]{:S(2)}, u32[]{:S(2)}) collective-permute-start(f32[72,512]{1,0:T(8,128)S(1)} %pad_maximum_fusion.1.refs_7_), channel_id=1, source_target_pairs={{0,3},{8,11},{4,7},{12,15},{16,19},{24,27},{20,23},{28,31},{32,35}... | collective-permute-start | bytes 442376 | tf_op jit(solution)/shard_map/ppermute | solution.py:51
  141.4 6.8 %collective-permute-done.26.refs_8_ = f32[72,512]{1,0:T(8,128)S(1)} collective-permute-done((f32[72,512]{1,0:T(8,128)S(1)}, f32[72,512]{1,0:T(8,128)S(1)}, u32[]{:S(2)}, u32[]{:S(2)}) %collective-permute-start.26) | collective-permute-done | bytes 147488 | tf_op jit(solution)/shard_map/ppermute | solution.py:51
  148.2 2.1 %collective-permute-done.25 = bf16[32,8192]{1,0:T(8,128)(2,1)S(1)} collective-permute-done((bf16[32,8192]{1,0:T(8,128)(2,1)S(1)}, bf16[32,8192]{1,0:T(8,128)(2,1)S(1)}, u32[]{:S(2)}, u32[]{:S(2)}) %collective-permute-start.25) | collective-permute-done | bytes 524320 | tf_op jit(solution)/shard_map/ppermute | solution.py:51
  150.4 5.0 %collective-permute-start.29 = (bf16[32,8192]{1,0:T(8,128)(2,1)S(1)}, bf16[32,8192]{1,0:T(8,128)(2,1)S(1)}, u32[]{:S(2)}, u32[]{:S(2)}) collective-permute-start(bf16[32,8192]{1,0:T(8,128)(2,1)S(1)} %collective-permute-done.25), channel_id=1, source_target_pairs={{8,28},{12,8},{24,12},{28,24},{40,60},{44,40},{56,44},{60,56},{72,... | collective-permute-start | bytes 1572872 | tf_op jit(solution)/shard_map/ppermute | solution.py:51
  155.4 1.6 add_convert_fusion
  157.0 5.0 %backward_full.1 = (bf16[512,512]{1,0:T(8,128)(2,1)}, bf16[512,512]{1,0:T(8,128)(2,1)}, f32[16,512]{1,0:T(8,128)}, f32[16,512]{1,0:T(8,128)}, f32[8,512]{1,0:T(8,128)S(1)}) custom-call(bf16[512,512]{1,0:T(8,128)(2,1)S(1)} %copy-done.1, bf16[512,512]{1,0:T(8,128)(2,1)S(1)} %copy-done.3, f32[4,512,128]{2,1,0:T(8,128)S(1)} %get-tuple-element.102.refs_2_, ...), custom_call_target="tpu_custom_call" | custom-call | flops 115000000 | tf_op jit(solution)/shard_map/backward_full/pallas_call | solution.py:326
  (77 shorter events, 14.1 us)
Async XLA Ops:
  1.7 19.7 %collective-permute-start.1 = (bf16[32,4096]{1,0:T(8,128)(2,1)S(1)}, bf16[32,4096]{1,0:T(8,128)(2,1)S(1)}, u32[]{:S(2)}, u32[]{:S(2)}) collective-permute-start(bf16[32,4096]{1,0:T(8,128)(2,1)S(1)} %get-tuple-element.115), channel_id=1, source_target_pairs={{0,4},{8,12},{4,16},{12,24},{16,20},{24,28},{20,0},{28,8},{32,36},... | collective-permute-start | bytes 786440 | tf_op jit(solution)/shard_map/ppermute | solution.py:51
  3.4 19.1 %collective-permute-start.2 = (bf16[32,4096]{1,0:T(8,128)(2,1)S(1)}, bf16[32,4096]{1,0:T(8,128)(2,1)S(1)}, u32[]{:S(2)}, u32[]{:S(2)}) collective-permute-start(bf16[32,4096]{1,0:T(8,128)(2,1)S(1)} %get-tuple-element.115), channel_id=1, source_target_pairs={{0,20},{8,28},{4,0},{12,8},{16,4},{24,12},{20,16},{28,24},{32,52},... | collective-permute-start | bytes 786440 | tf_op jit(solution)/shard_map/ppermute | solution.py:51
  5.6 17.1 %collective-permute-start = (bf16[32,4096]{1,0:T(8,128)(2,1)S(1)}, bf16[32,4096]{1,0:T(8,128)(2,1)S(1)}, u32[]{:S(2)}, u32[]{:S(2)}) collective-permute-start(bf16[32,4096]{1,0:T(8,128)(2,1)S(1)} %get-tuple-element.114), channel_id=1, source_target_pairs={{0,16},{8,24},{4,20},{12,28},{16,0},{24,8},{20,4},{28,12},{32,48},... | collective-permute-start | bytes 786440 | tf_op jit(solution)/shard_map/ppermute | solution.py:51
  6.9 1.0 copy-start
  7.9 1.0 copy-start.2
  8.9 0.8 copy-start.5
  12.9 4.8 %collective-permute-start.3 = (f32[32,512]{1,0:T(8,128)S(1)}, f32[32,512]{1,0:T(8,128)S(1)}, u32[]{:S(2)}, u32[]{:S(2)}) collective-permute-start(f32[32,512]{1,0:T(8,128)S(1)} %get-tuple-element.60), channel_id=1, source_target_pairs={{0,4},{8,12},{4,0},{12,8},{16,20},{24,28},{20,16},{28,24},{32,36},... | collective-permute-start | bytes 196616 | tf_op jit(solution)/shard_map/ppermute | solution.py:51
  17.7 5.2 %collective-permute-start.4 = (f32[64,512]{1,0:T(8,128)S(1)}, f32[64,512]{1,0:T(8,128)S(1)}, u32[]{:S(2)}, u32[]{:S(2)}) collective-permute-start(f32[64,512]{1,0:T(8,128)S(1)} %constant_dynamic-update-slice_fusion.refs_6_), channel_id=1, source_target_pairs={{0,1},{8,9},{4,5},{12,13},{16,17},{24,25},{20,21},{28,29},{32,33},... | collective-permute-start | bytes 393224 | tf_op jit(solution)/shard_map/ppermute | solution.py:51
  19.0 6.8 %collective-permute-start.5 = (f32[64,512]{1,0:T(8,128)S(1)}, f32[64,512]{1,0:T(8,128)S(1)}, u32[]{:S(2)}, u32[]{:S(2)}) collective-permute-start(f32[64,512]{1,0:T(8,128)S(1)} %constant_dynamic-update-slice_fusion.refs_6_), channel_id=1, source_target_pairs={{0,2},{8,10},{4,6},{12,14},{16,18},{24,26},{20,22},{28,30},{32,34}... | collective-permute-start | bytes 393224 | tf_op jit(solution)/shard_map/ppermute | solution.py:51
  21.4 5.0 %collective-permute-start.6 = (f32[64,512]{1,0:T(8,128)S(1)}, f32[64,512]{1,0:T(8,128)S(1)}, u32[]{:S(2)}, u32[]{:S(2)}) collective-permute-start(f32[64,512]{1,0:T(8,128)S(1)} %constant_dynamic-update-slice_fusion.refs_6_), channel_id=1, source_target_pairs={{0,3},{8,11},{4,7},{12,15},{16,19},{24,27},{20,23},{28,31},{32,35}... | collective-permute-start | bytes 393224 | tf_op jit(solution)/shard_map/ppermute | solution.py:51
  22.6 8.8 %copy-start.4 = (bf16[512,512]{1,0:T(8,128)(2,1)S(1)}, bf16[512,512]{1,0:T(8,128)(2,1)}, u32[]{:S(2)}) copy-start(bf16[512,512]{1,0:T(8,128)(2,1)} %query_ref.1) | copy-start | bytes 1572868
  22.6 8.8 %copy-start.6 = (f32[16,512]{1,0:T(8,128)S(1)}, f32[16,512]{1,0:T(8,128)}, u32[]{:S(2)}) copy-start(f32[16,512]{1,0:T(8,128)} %refs_4_.3) | copy-start | bytes 98308
  22.6 8.8 %copy-start.7 = (f32[16,512]{1,0:T(8,128)S(1)}, f32[16,512]{1,0:T(8,128)}, u32[]{:S(2)}) copy-start(f32[16,512]{1,0:T(8,128)} %refs_5_.1) | copy-start | bytes 98308
  22.6 8.8 %copy-start.8 = (f32[512]{0:T(512)S(1)}, f32[512]{0:T(512)}, u32[]{:S(2)}) copy-start(f32[512]{0:T(512)} %param.11) | copy-start | bytes 6148
  22.8 33.2 %slice-start = ((s8[8388608]{0:T(1024)(128)(4,1)}), s8[4194304]{0:T(1024)(128)(4,1)S(1)}, s32[]{:S(2)}) async-start(s8[8388608]{0:T(1024)(128)(4,1)} %bitcast.46), calls=%async_computation | async-start | bytes 8388608
  26.5 36.4 %collective-permute-start.13 = (bf16[2,2,32,4096]{3,2,1,0:T(8,128)(2,1)S(1)}, bf16[2,2,32,4096]{3,2,1,0:T(8,128)(2,1)S(1)}, u32[]{:S(2)}, u32[]{:S(2)}) collective-permute-start(bf16[2,2,32,4096]{3,2,1,0:T(8,128)(2,1)S(1)} %pad_maximum_fusion), channel_id=1, source_target_pairs={{0,8},{8,0},{4,12},{12,4},{16,24},{24,16},{20,28},{28,20},{32,40},... | collective-permute-start | bytes 3145736 | tf_op jit(solution)/shard_map/ppermute | solution.py:51
  28.7 25.7 %collective-permute-start.7 = (bf16[2,2,32,4096]{3,2,1,0:T(8,128)(2,1)S(1)}, bf16[2,2,32,4096]{3,2,1,0:T(8,128)(2,1)S(1)}, u32[]{:S(2)}, u32[]{:S(2)}) collective-permute-start(bf16[2,2,32,4096]{3,2,1,0:T(8,128)(2,1)S(1)} %pad_maximum_fusion), channel_id=1, source_target_pairs={{0,32},{8,104},{4,36},{12,108},{16,48},{24,120},{20,52},{28,124},{... | collective-permute-start | bytes 3145736 | tf_op jit(solution)/shard_map/ppermute | solution.py:51
  29.2 25.3 %collective-permute-start.8 = (bf16[2,2,32,4096]{3,2,1,0:T(8,128)(2,1)S(1)}, bf16[2,2,32,4096]{3,2,1,0:T(8,128)(2,1)S(1)}, u32[]{:S(2)}, u32[]{:S(2)}) collective-permute-start(bf16[2,2,32,4096]{3,2,1,0:T(8,128)(2,1)S(1)} %pad_maximum_fusion), channel_id=1, source_target_pairs={{0,96},{8,40},{4,100},{12,44},{16,112},{24,56},{20,116},{28,60},{3... | collective-permute-start | bytes 3145736 | tf_op jit(solution)/shard_map/ppermute | solution.py:51
  35.3 29.8 %collective-permute-start.11 = (bf16[512,512]{1,0:T(8,128)(2,1)S(1)}, bf16[512,512]{1,0:T(8,128)(2,1)S(1)}, u32[]{:S(2)}, u32[]{:S(2)}) collective-permute-start(bf16[512,512]{1,0:T(8,128)(2,1)S(1)} %get-tuple-element.74), channel_id=1, source_target_pairs={{0,4},{8,12},{4,0},{12,8},{16,20},{24,28},{20,16},{28,24},{32,36},... | collective-permute-start | bytes 1572872 | tf_op jit(solution)/shard_map/ppermute | solution.py:51
  35.6 20.5 %slice-start.1 = ((s8[8388608]{0:T(1024)(128)(4,1)}), s8[4194304]{0:T(1024)(128)(4,1)S(1)}, s32[]{:S(2)}) async-start(s8[8388608]{0:T(1024)(128)(4,1)} %bitcast.46), calls=%async_computation.1 | async-start | bytes 8388608
  54.5 17.9 %collective-permute-start.14 = (bf16[2,2,32,4096]{3,2,1,0:T(8,128)(2,1)S(1)}, bf16[2,2,32,4096]{3,2,1,0:T(8,128)(2,1)S(1)}, u32[]{:S(2)}, u32[]{:S(2)}) collective-permute-start(bf16[2,2,32,4096]{3,2,1,0:T(8,128)(2,1)S(1)} %collective-permute-done.7), channel_id=1, source_target_pairs={{0,8},{8,0},{4,12},{12,4},{16,24},{24,16},{20,28},{28,20},{32,40},... | collective-permute-start | bytes 3145736 | tf_op jit(solution)/shard_map/ppermute | solution.py:51
  55.5 14.9 %collective-permute-start.10 = (bf16[2,2,32,4096]{3,2,1,0:T(8,128)(2,1)S(1)}, bf16[2,2,32,4096]{3,2,1,0:T(8,128)(2,1)S(1)}, u32[]{:S(2)}, u32[]{:S(2)}) collective-permute-start(bf16[2,2,32,4096]{3,2,1,0:T(8,128)(2,1)S(1)} %collective-permute-done.7), channel_id=1, source_target_pairs={{0,32},{8,104},{4,36},{12,108},{16,48},{24,120},{20,52},{28,124},{... | collective-permute-start | bytes 3145736 | tf_op jit(solution)/shard_map/ppermute | solution.py:51
  55.5 18.9 %collective-permute-start.15 = (bf16[2,2,32,4096]{3,2,1,0:T(8,128)(2,1)S(1)}, bf16[2,2,32,4096]{3,2,1,0:T(8,128)(2,1)S(1)}, u32[]{:S(2)}, u32[]{:S(2)}) collective-permute-start(bf16[2,2,32,4096]{3,2,1,0:T(8,128)(2,1)S(1)} %collective-permute-done.8), channel_id=1, source_target_pairs={{0,8},{8,0},{4,12},{12,4},{16,24},{24,16},{20,28},{28,20},{32,40},... | collective-permute-start | bytes 3145736 | tf_op jit(solution)/shard_map/ppermute | solution.py:51
  62.9 7.5 %collective-permute-start.9 = (bf16[64,8192]{1,0:T(8,128)(2,1)S(1)}, bf16[64,8192]{1,0:T(8,128)(2,1)S(1)}, u32[]{:S(2)}, u32[]{:S(2)}) collective-permute-start(bf16[64,8192]{1,0:T(8,128)(2,1)S(1)} %get-tuple-element.71), channel_id=1, source_target_pairs={{0,8},{8,0},{4,12},{12,4},{16,24},{24,16},{20,28},{28,20},{32,40},... | collective-permute-start | bytes 3145736 | tf_op jit(solution)/shard_map/ppermute | solution.py:51
  70.4 6.3 %collective-permute-start.16 = (bf16[2,2,32,4096]{3,2,1,0:T(8,128)(2,1)S(1)}, bf16[2,2,32,4096]{3,2,1,0:T(8,128)(2,1)S(1)}, u32[]{:S(2)}, u32[]{:S(2)}) collective-permute-start(bf16[2,2,32,4096]{3,2,1,0:T(8,128)(2,1)S(1)} %collective-permute-done.10), channel_id=1, source_target_pairs={{0,8},{8,0},{4,12},{12,4},{16,24},{24,16},{20,28},{28,20},{32,40},... | collective-permute-start | bytes 3145736 | tf_op jit(solution)/shard_map/ppermute | solution.py:51
  70.6 14.9 %collective-permute-start.17 = (bf16[64,8192]{1,0:T(8,128)(2,1)S(1)}, bf16[64,8192]{1,0:T(8,128)(2,1)S(1)}, u32[]{:S(2)}, u32[]{:S(2)}) collective-permute-start(bf16[64,8192]{1,0:T(8,128)(2,1)S(1)} %add_convert_fusion.4), channel_id=1, source_target_pairs={{0,32},{8,104},{4,36},{12,108},{16,48},{24,120},{20,52},{28,124},{... | collective-permute-start | bytes 3145736 | tf_op jit(solution)/shard_map/ppermute | solution.py:51
  70.7 29.1 %collective-permute-start.12 = (bf16[192,8192]{1,0:T(8,128)(2,1)S(1)}, bf16[192,8192]{1,0:T(8,128)(2,1)S(1)}, u32[]{:S(2)}, u32[]{:S(2)}) collective-permute-start(bf16[192,8192]{1,0:T(8,128)(2,1)S(1)} %get-tuple-element.76), channel_id=1, source_target_pairs={{0,8},{8,0},{4,12},{12,4},{16,24},{24,16},{20,28},{28,20},{32,40},... | collective-permute-start | bytes 9437192 | tf_op jit(solution)/shard_map/ppermute | solution.py:51
  85.6 17.7 %collective-permute-start.18 = (bf16[512,512]{1,0:T(8,128)(2,1)S(1)}, bf16[512,512]{1,0:T(8,128)(2,1)S(1)}, u32[]{:S(2)}, u32[]{:S(2)}) collective-permute-start(bf16[512,512]{1,0:T(8,128)(2,1)S(1)} %slice.50), channel_id=1, source_target_pairs={{0,4},{8,12},{4,0},{12,8},{16,20},{24,28},{20,16},{28,24},{32,36},... | collective-permute-start | bytes 1572872 | tf_op jit(solution)/shard_map/ppermute | solution.py:51
  88.7 14.2 %collective-permute-start.19 = (bf16[512,1024]{1,0:T(8,128)(2,1)S(1)}, bf16[512,1024]{1,0:T(8,128)(2,1)S(1)}, u32[]{:S(2)}, u32[]{:S(2)}) collective-permute-start(bf16[512,1024]{1,0:T(8,128)(2,1)S(1)} %multiply_convert_fusion.3), channel_id=1, source_target_pairs={{0,1},{8,11},{4,5},{12,15},{16,17},{24,27},{20,21},{28,31},{32,33}... | collective-permute-start | bytes 3145736 | tf_op jit(solution)/shard_map/ppermute | solution.py:51
  103.4 21.0 %collective-permute-start.21 = (bf16[64,8192]{1,0:T(8,128)(2,1)S(1)}, bf16[64,8192]{1,0:T(8,128)(2,1)S(1)}, u32[]{:S(2)}, u32[]{:S(2)}) collective-permute-start(bf16[64,8192]{1,0:T(8,128)(2,1)S(1)} %get-tuple-element.93), channel_id=1, source_target_pairs={{0,32},{8,104},{4,36},{12,108},{16,48},{24,120},{20,52},{28,124},{... | collective-permute-start | bytes 3145736 | tf_op jit(solution)/shard_map/ppermute | solution.py:51
  103.4 23.1 %collective-permute-start.22 = (bf16[64,8192]{1,0:T(8,128)(2,1)S(1)}, bf16[64,8192]{1,0:T(8,128)(2,1)S(1)}, u32[]{:S(2)}, u32[]{:S(2)}) collective-permute-start(bf16[64,8192]{1,0:T(8,128)(2,1)S(1)} %get-tuple-element.94), channel_id=1, source_target_pairs={{0,96},{8,40},{4,100},{12,44},{16,112},{24,56},{20,116},{28,60},{3... | collective-permute-start | bytes 3145736 | tf_op jit(solution)/shard_map/ppermute | solution.py:51
  106.1 23.4 %collective-permute-start.23 = (bf16[512,1024]{1,0:T(8,128)(2,1)S(1)}, bf16[512,1024]{1,0:T(8,128)(2,1)S(1)}, u32[]{:S(2)}, u32[]{:S(2)}) collective-permute-start(bf16[512,1024]{1,0:T(8,128)(2,1)S(1)} %add_convert_fusion.1), channel_id=1, source_target_pairs={{0,1},{8,11},{4,5},{12,15},{16,17},{24,27},{20,21},{28,31},{32,33}... | collective-permute-start | bytes 3145736 | tf_op jit(solution)/shard_map/ppermute | solution.py:51
  109.2 25.7 %collective-permute-start.24 = (bf16[512,1024]{1,0:T(8,128)(2,1)S(1)}, bf16[512,1024]{1,0:T(8,128)(2,1)S(1)}, u32[]{:S(2)}, u32[]{:S(2)}) collective-permute-start(bf16[512,1024]{1,0:T(8,128)(2,1)S(1)} %multiply_convert_fusion.1), channel_id=1, source_target_pairs={{0,3},{8,9},{4,7},{12,13},{16,19},{24,25},{20,23},{28,29},{32,35},... | collective-permute-start | bytes 3145736 | tf_op jit(solution)/shard_map/ppermute | solution.py:51
  118.9 3.9 %collective-permute-start.20 = (f32[56,512]{1,0:T(8,128)S(1)}, f32[56,512]{1,0:T(8,128)S(1)}, u32[]{:S(2)}, u32[]{:S(2)}) collective-permute-start(f32[56,512]{1,0:T(8,128)S(1)} %get-tuple-element.92), channel_id=1, source_target_pairs={{0,4},{8,12},{4,0},{12,8},{16,20},{24,28},{20,16},{28,24},{32,36},... | collective-permute-start | bytes 344072 | tf_op jit(solution)/shard_map/ppermute | solution.py:51
  135.5 14.9 %collective-permute-start.25 = (bf16[32,8192]{1,0:T(8,128)(2,1)S(1)}, bf16[32,8192]{1,0:T(8,128)(2,1)S(1)}, u32[]{:S(2)}, u32[]{:S(2)}) collective-permute-start(bf16[32,8192]{1,0:T(8,128)(2,1)S(1)} %slice.49), channel_id=1, source_target_pairs={{0,16},{8,28},{4,20},{12,8},{16,0},{24,12},{20,4},{28,24},{32,48},... | collective-permute-start | bytes 1572872 | tf_op jit(solution)/shard_map/ppermute | solution.py:51
  138.7 18.3 %copy-start.1 = (bf16[512,512]{1,0:T(8,128)(2,1)S(1)}, bf16[512,512]{1,0:T(8,128)(2,1)}, u32[]{:S(2)}) copy-start(bf16[512,512]{1,0:T(8,128)(2,1)} %refs_0_.3) | copy-start | bytes 1572868
  138.7 18.3 %copy-start.3 = (bf16[512,512]{1,0:T(8,128)(2,1)S(1)}, bf16[512,512]{1,0:T(8,128)(2,1)}, u32[]{:S(2)}) copy-start(bf16[512,512]{1,0:T(8,128)(2,1)} %refs_1_.1) | copy-start | bytes 1572868
  138.7 9.5 %collective-permute-start.26 = (f32[72,512]{1,0:T(8,128)S(1)}, f32[72,512]{1,0:T(8,128)S(1)}, u32[]{:S(2)}, u32[]{:S(2)}) collective-permute-start(f32[72,512]{1,0:T(8,128)S(1)} %pad_maximum_fusion.1.refs_7_), channel_id=1, source_target_pairs={{0,1},{8,9},{4,5},{12,13},{16,17},{24,25},{20,21},{28,29},{32,33},... | collective-permute-start | bytes 442376 | tf_op jit(solution)/shard_map/ppermute | solution.py:51
  138.8 9.5 %collective-permute-start.27 = (f32[72,512]{1,0:T(8,128)S(1)}, f32[72,512]{1,0:T(8,128)S(1)}, u32[]{:S(2)}, u32[]{:S(2)}) collective-permute-start(f32[72,512]{1,0:T(8,128)S(1)} %pad_maximum_fusion.1.refs_7_), channel_id=1, source_target_pairs={{0,2},{8,10},{4,6},{12,14},{16,18},{24,26},{20,22},{28,30},{32,34}... | collective-permute-start | bytes 442376 | tf_op jit(solution)/shard_map/ppermute | solution.py:51
  139.5 8.7 %collective-permute-start.28 = (f32[72,512]{1,0:T(8,128)S(1)}, f32[72,512]{1,0:T(8,128)S(1)}, u32[]{:S(2)}, u32[]{:S(2)}) collective-permute-start(f32[72,512]{1,0:T(8,128)S(1)} %pad_maximum_fusion.1.refs_7_), channel_id=1, source_target_pairs={{0,3},{8,11},{4,7},{12,15},{16,19},{24,27},{20,23},{28,31},{32,35}... | collective-permute-start | bytes 442376 | tf_op jit(solution)/shard_map/ppermute | solution.py:51
  150.4 12.3 %collective-permute-start.29 = (bf16[32,8192]{1,0:T(8,128)(2,1)S(1)}, bf16[32,8192]{1,0:T(8,128)(2,1)S(1)}, u32[]{:S(2)}, u32[]{:S(2)}) collective-permute-start(bf16[32,8192]{1,0:T(8,128)(2,1)S(1)} %collective-permute-done.25), channel_id=1, source_target_pairs={{8,28},{12,8},{24,12},{28,24},{40,60},{44,40},{56,44},{60,56},{72,... | collective-permute-start | bytes 1572872 | tf_op jit(solution)/shard_map/ppermute | solution.py:51

commit v9 on v8

--- a/solution.py
+++ b/solution.py
@@ -68,15 +68,43 @@
     return jnp.stack([stack, other])
 
 
-def place_blocks(*blocks):
+def put_in_place(*refs):
+    gated_ref, gated_other_ref, *block_refs = refs[:-3]
+    whole_ref, pair_ref, sems = refs[-3:]
     y, _, core, _, _ = places()
+    rows = gated_ref.shape[0]
+    copies = [
+        pltpu.make_async_copy(gated_ref, pair_ref.at[pl.ds(0, rows)], sems.at[0]),
+        pltpu.make_async_copy(gated_other_ref, pair_ref.at[pl.ds(rows, rows)], sems.at[1]),
+    ]
+    steps = ((0, 0), (RING - 1, 1), (1, RING - 1), (2, 2))
+    for i, ref in enumerate(block_refs):
+        at_core = core if i % 2 == 0 else 1 - core
+        row = lax.rem(y + jnp.where(at_core == 0, *steps[i // 2]), RING)
+        copies.append(pltpu.make_async_copy(ref, whole_ref.at[:, row, :, at_core], sems.at[2 + i]))
+    for copy in copies:
+        copy.start()
+    for copy in copies:
+        copy.wait()
+
+
+def place_blocks(gated, gated_other, blocks):
     _, _, tokens, half = blocks[0].shape
-    whole = jnp.zeros((2, RING, 2, 2, tokens, half), BF16)
-    for block, steps in zip(blocks, ((0, 0), (RING - 1, 1), (1, RING - 1), (2, 2))):
-        for part, at_core in ((block, core), (hop(block, core=1), 1 - core)):
-            row = lax.rem(y + jnp.where(at_core == 0, *steps), RING)
-            whole = lax.dynamic_update_slice(whole, part[:, None, :, None], (0, row, 0, at_core, 0, 0))
-    return whole
+    parts = [part for block in blocks for part in (block, hop(block, core=1))]
+    rows, channels = gated.shape
+    whole = (2, RING, 2, 2, tokens, half)
+    moved = 4 * math.prod(whole)
+    cot, pair = pl.pallas_call(
+        put_in_place,
+        out_shape=[jax.ShapeDtypeStruct(whole, BF16), jax.ShapeDtypeStruct((2 * rows, channels), BF16)],
+        in_specs=[pl.BlockSpec(memory_space=pl.ANY)] * (2 + len(parts)),
+        out_specs=[pl.BlockSpec(memory_space=pltpu.VMEM)] * 2,
+        scratch_shapes=[pltpu.SemaphoreType.DMA((2 + len(parts),))],
+        compiler_params=pltpu.CompilerParams(vmem_limit_bytes=16 * 2**20),
+        cost_estimate=pl.CostEstimate(flops=0, bytes_accessed=moved, transcendentals=0),
+        name="put_in_place",
+    )(gated, gated_other, *parts)
+    return cot.reshape(-1, half), pair
 
 
 def add(*parts):
@@ -384,10 +412,8 @@
     far_block, far_rest, gated_other = together(far_block, far_rest, hop(gated, pair=1))
     got_first, far_rest = together(hop(far_first, core=1), far_rest)
     got_rest = hop(far_rest, core=1)
-    gated_pair = jnp.concatenate([gated, gated_other])
     opposite = add(near_first, got_first).astype(BF16)
-    cot_rows = place_blocks(block, main_block, other_block, far_block)
-    cot_rows = cot_rows.reshape(2 * length, -1)
+    cot_rows, gated_pair = place_blocks(gated, gated_other, (block, main_block, other_block, far_block))
 
     _, _, core, low, x = places()
     half = out_weight.shape[1] // 2
@@ -420,9 +446,10 @@
         (grad_gated, queries, pre_gate, driving, lead, log_decay),
         (narrow, wide, like((3 * modes + SUBS, channels), F32), like((tiles, SUBS * modes, LANES), F32)),
         [table, (tiles, 2 * SUBS * modes, LANES), (SUBS, LANES)],
-        2.0,
+        0.1,
         "backward_ends",
     )
+    sums, main, other = together(sums, main, other)
     others = hop(sums, pair=1)
     others, main, other, main_weight, other_weight = together(others, main, other, main_weight, other_weight)
     own = add(own, main, other)

time: 164 us -> 182 us (1.11)
  the two profiles are of different devices: /device:TPU:25 before, /device:TPU:1 now
where the time goes in v9:
time: 182 us
  waiting for transfers between devices  73.9 us (41%)
  starting transfers between devices  38.2 us (21%)
  Pallas kernels  31 us (17%)
  local copies, waits for them, and re-layouts  17.5 us (10%)
  matrix products  10.7 us (6%)
  other arithmetic  9.44 us (5%)
    ppermute x30, waiting for transfers between devices, hop(): return lax.ppermute(value, ('chan', 'seq'), moves)  73.9 us
    ppermute x30, starting transfers between devices, hop(): return lax.ppermute(value, ('chan', 'seq'), moves)  38.2 us
    pallas_call x4, Pallas kernels, call(): pl.pallas_call(body, out_shape=[jax.ShapeDtypeStruct(o.shape, o.dtype) fo...  21.6 us
    unnamed x55, local copies, waits for them, and re-layouts  15.7 us
    pallas_call x1, Pallas kernels, project(): pl.pallas_call(project_tile, grid=(width // tile,), out_shape=[jax.ShapeD...  7.45 us
    dot_general x4, matrix products, weigh(): lax.dot_general(gated, columns, (((0,), (0,)), ((), ())), preferred_eleme...  6.14 us
    dot_general x1, matrix products, local(): lax.dot_general(cot_rows, low_weight, (((1,), (1,)), ((), ())), preferred...  4.52 us
  transfers between devices with their start and end apart: 30, of which 15 were waited for; matrix products, arithmetic and copies ran while one was open for 10% of the time, Pallas kernels for 17%

profile of v9, /device:TPU:1, one launch (start us, length us, event | category | flops | bytes accessed | tf_op | source)
XLA Modules:
  0.0 181.8 jit_solution(10514723609163113427)
XLA Ops:
  0.7 1.1 constant_dynamic-slice_fusion.1
  1.7 2.5 %collective-permute-start.1 = (bf16[32,4096]{1,0:T(8,128)(2,1)S(1)}, bf16[32,4096]{1,0:T(8,128)(2,1)S(1)}, u32[]{:S(2)}, u32[]{:S(2)}) collective-permute-start(bf16[32,4096]{1,0:T(8,128)(2,1)S(1)} %get-tuple-element.125), channel_id=1, source_target_pairs={{0,4},{8,12},{4,16},{12,24},{16,20},{24,28},{20,0},{28,8},{32,36},... | collective-permute-start | bytes 786440 | tf_op jit(solution)/shard_map/ppermute | solution.py:51
  4.3 2.2 %collective-permute-start.2 = (bf16[32,4096]{1,0:T(8,128)(2,1)S(1)}, bf16[32,4096]{1,0:T(8,128)(2,1)S(1)}, u32[]{:S(2)}, u32[]{:S(2)}) collective-permute-start(bf16[32,4096]{1,0:T(8,128)(2,1)S(1)} %get-tuple-element.125), channel_id=1, source_target_pairs={{0,20},{8,28},{4,0},{12,8},{16,4},{24,12},{20,16},{28,24},{32,52},... | collective-permute-start | bytes 786440 | tf_op jit(solution)/shard_map/ppermute | solution.py:51
  6.5 1.2 collective-permute-start
  7.7 1.0 copy-done.2
  8.7 1.0 copy-done.4
  10.5 3.2 %forward_ends.1 = (f32[32,512]{1,0:T(8,128)S(1)}, f32[4,256,128]{2,1,0:T(8,128)S(1)}, f32[4,512,128]{2,1,0:T(8,128)S(1)}) custom-call(bf16[512,512]{1,0:T(8,128)(2,1)S(1)} %copy-done.2, bf16[512,512]{1,0:T(8,128)(2,1)S(1)} %copy-done.4, f32[16,512]{1,0:T(8,128)S(1)} %copy-done.12), custom_call_target="tpu_custom_call" | custom-call | flops 115000000 | tf_op jit(solution)/shard_map/forward_ends/pallas_call | solution.py:354
  15.3 3.4 %collective-permute-done.3 = f32[32,512]{1,0:T(8,128)S(1)} collective-permute-done((f32[32,512]{1,0:T(8,128)S(1)}, f32[32,512]{1,0:T(8,128)S(1)}, u32[]{:S(2)}, u32[]{:S(2)}) %collective-permute-start.3) | collective-permute-done | bytes 65568 | tf_op jit(solution)/shard_map/ppermute | solution.py:51
  18.7 1.2 collective-permute-start.4
  20.0 2.5 %collective-permute-start.5 = (f32[64,512]{1,0:T(8,128)S(1)}, f32[64,512]{1,0:T(8,128)S(1)}, u32[]{:S(2)}, u32[]{:S(2)}) collective-permute-start(f32[64,512]{1,0:T(8,128)S(1)} %constant_dynamic-update-slice_fusion.refs_6_), channel_id=1, source_target_pairs={{0,2},{8,10},{4,6},{12,14},{16,18},{24,26},{20,22},{28,30},{32,34}... | collective-permute-start | bytes 393224 | tf_op jit(solution)/shard_map/ppermute | solution.py:51
  22.4 1.2 collective-permute-start.6
  24.0 2.9 %collective-permute-done.5.refs_8_ = f32[64,512]{1,0:T(8,128)S(1)} collective-permute-done((f32[64,512]{1,0:T(8,128)S(1)}, f32[64,512]{1,0:T(8,128)S(1)}, u32[]{:S(2)}, u32[]{:S(2)}) %collective-permute-start.5) | collective-permute-done | bytes 131104 | tf_op jit(solution)/shard_map/ppermute | solution.py:51
  27.5 2.7 %collective-permute-start.7 = (bf16[2,2,32,4096]{3,2,1,0:T(8,128)(2,1)S(1)}, bf16[2,2,32,4096]{3,2,1,0:T(8,128)(2,1)}, u32[]{:S(2)}, u32[]{:S(2)}) collective-permute-start(bf16[2,2,32,4096]{3,2,1,0:T(8,128)(2,1)S(1)} %pad_maximum_fusion.refs_2_), channel_id=1, source_target_pairs={{0,32},{8,104},{4,36},{12,108},{16,48},{24,120},{20,52},{28,124},{... | collective-permute-start | bytes 3145736 | tf_op jit(solution)/shard_map/ppermute | solution.py:51
  30.3 3.8 %forward_full.1 = (bf16[512,512]{1,0:T(8,128)(2,1)S(1)}, bf16[512,512]{1,0:T(8,128)(2,1)S(1)}, f32[4,512,128]{2,1,0:T(8,128)S(1)}, f32[4,256,128]{2,1,0:T(8,128)S(1)}) custom-call(bf16[512,512]{1,0:T(8,128)(2,1)S(1)} %copy-done.6, f32[4,512,128]{2,1,0:T(8,128)S(1)} %get-tuple-element.67.refs_1_.drive_ref, f32[4,256,128]{2,1,0:T(8,128)S(1)} %copy-done.15, ...), custom_call_target="tpu_custom_call" | custom-call | flops 115000000 | tf_op jit(solution)/shard_map/forward_full/pallas_call | solution.py:354
  35.9 14.4 %collective-permute-done.7.refs_4_ = bf16[2,2,32,4096]{3,2,1,0:T(8,128)(2,1)} collective-permute-done((bf16[2,2,32,4096]{3,2,1,0:T(8,128)(2,1)S(1)}, bf16[2,2,32,4096]{3,2,1,0:T(8,128)(2,1)}, u32[]{:S(2)}, u32[]{:S(2)}) %collective-permute-start.7) | collective-permute-done | bytes 1048608 | tf_op jit(solution)/shard_map/ppermute | solution.py:51
  50.3 6.3 %collective-permute-done.8.refs_6_ = bf16[2,2,32,4096]{3,2,1,0:T(8,128)(2,1)S(1)} collective-permute-done((bf16[2,2,32,4096]{3,2,1,0:T(8,128)(2,1)S(1)}, bf16[2,2,32,4096]{3,2,1,0:T(8,128)(2,1)S(1)}, u32[]{:S(2)}, u32[]{:S(2)}) %collective-permute-start.8) | collective-permute-done | bytes 1048608 | tf_op jit(solution)/shard_map/ppermute | solution.py:51
  57.6 3.4 %copy-done.20 = bf16[512,8192]{1,0:T(8,128)(2,1)S(1)} copy-done((bf16[512,8192]{1,0:T(8,128)(2,1)S(1)}, bf16[512,8192]{1,0:T(8,128)(2,1)}, u32[]{:S(2)}) %copy-start.20) | copy-done | bytes 8388632
  61.0 7.4 %project.1 = (bf16[64,8192]{1,0:T(8,128)(2,1)S(1)}, bf16[192,8192]{1,0:T(8,128)(2,1)S(1)}, bf16[64,8192]{1,0:T(8,128)(2,1)}, bf16[192,8192]{1,0:T(8,128)(2,1)S(1)}) custom-call(bf16[512,512]{1,0:T(8,128)(2,1)S(1)} %get-tuple-element.74.rows_ref, bf16[512,8192]{1,0:T(8,128)(2,1)S(1)} %copy-done.20), custom_call_target="tpu_custom_call" | custom-call | flops 4294967296 | bytes 16777216 | tf_op jit(solution)/shard_map/project/pallas_call | solution.py:127
  68.4 1.6 copy-done
  71.0 1.7 copy-done.22
  73.6 13.0 %collective-permute-done.11.refs_1_ = bf16[512,512]{1,0:T(8,128)(2,1)} collective-permute-done((bf16[512,512]{1,0:T(8,128)(2,1)S(1)}, bf16[512,512]{1,0:T(8,128)(2,1)}, u32[]{:S(2)}, u32[]{:S(2)}) %collective-permute-start.11) | collective-permute-done | bytes 524320 | tf_op jit(solution)/shard_map/ppermute | solution.py:51
  88.0 1.8 add_convert_fusion.4
  89.8 3.2 %collective-permute-start.17 = (bf16[64,8192]{1,0:T(8,128)(2,1)S(1)}, bf16[64,8192]{1,0:T(8,128)(2,1)S(1)}, u32[]{:S(2)}, u32[]{:S(2)}) collective-permute-start(bf16[64,8192]{1,0:T(8,128)(2,1)S(1)} %add_convert_fusion.4), channel_id=1, source_target_pairs={{0,32},{8,104},{4,36},{12,108},{16,48},{24,120},{20,52},{28,124},{... | collective-permute-start | bytes 3145736 | tf_op jit(solution)/shard_map/ppermute | solution.py:51
  93.1 1.9 %put_in_place.1 = (bf16[2,4,2,2,32,4096]{5,4,3,2,1,0:T(8,128)(2,1)S(1)}, bf16[1024,512]{1,0:T(8,128)(2,1)S(1)}) custom-call(bf16[512,512]{1,0:T(8,128)(2,1)S(1)} %get-tuple-element.79.refs_0_, bf16[512,512]{1,0:T(8,128)(2,1)} %collective-permute-done.11.refs_1_, bf16[2,2,32,4096]{3,2,1,0:T(8,128)(2,1)S(1)} %pad_maximum_fusion.refs_2_, ...), custom_call_target="tpu_custom_call" | custom-call | bytes 16777216 | tf_op jit(solution)/shard_map/put_in_place/pallas_call | solution.py:97
  95.0 4.5 %fusion = f32[1024,512]{1,0:T(8,128)S(1)} fusion(bf16[1024,4096]{1,0:T(8,128)(2,1)S(1)} %bitcast.16, bf16[512,8192]{1,0:T(8,128)(2,1)S(1)} %copy-done.21, s32[]{:T(128)S(6)} %select_n.77), kind=kOutput, calls=%fused_computation | convolution fusion | flops 4294967296 | bytes 14680068 | tf_op jit(solution)/shard_map/dot_general | solution.py:421
  99.6 5.2 %collective-permute-done.17 = bf16[64,8192]{1,0:T(8,128)(2,1)S(1)} collective-permute-done((bf16[64,8192]{1,0:T(8,128)(2,1)S(1)}, bf16[64,8192]{1,0:T(8,128)(2,1)S(1)}, u32[]{:S(2)}, u32[]{:S(2)}) %collective-permute-start.17) | collective-permute-done | bytes 1048608 | tf_op jit(solution)/shard_map/ppermute | solution.py:51
  104.8 1.3 multiply_convert_fusion.3
  106.1 2.5 %collective-permute-start.19 = (bf16[512,1024]{1,0:T(8,128)(2,1)S(1)}, bf16[512,1024]{1,0:T(8,128)(2,1)S(1)}, u32[]{:S(2)}, u32[]{:S(2)}) collective-permute-start(bf16[512,1024]{1,0:T(8,128)(2,1)S(1)} %multiply_convert_fusion.3), channel_id=1, source_target_pairs={{0,1},{8,11},{4,5},{12,15},{16,17},{24,27},{20,21},{28,31},{32,33}... | collective-permute-start | bytes 3145736 | tf_op jit(solution)/shard_map/ppermute | solution.py:51
  108.8 2.3 %multiply_convert_fusion = bf16[512,1024]{1,0:T(8,128)(2,1)} fusion(bf16[1024,512]{1,0:T(8,128)(2,1)S(1)} %get-tuple-element.89, bf16[1024,4096]{1,0:T(8,128)(2,1)S(1)} %bitcast.18, s32[]{:T(128)S(6)} %select_n.87), kind=kOutput, calls=%fused_computation.5 | convolution fusion | flops 1074790400 | bytes 4194308 | tf_op jit(solution)/shard_map/dot_general | solution.py:144
  111.1 1.3 multiply_convert_fusion.1
  112.4 1.3 multiply_convert_fusion.2
  115.0 3.2 %collective-permute-start.20 = (bf16[64,8192]{1,0:T(8,128)(2,1)S(1)}, bf16[64,8192]{1,0:T(8,128)(2,1)S(1)}, u32[]{:S(2)}, u32[]{:S(2)}) collective-permute-start(bf16[64,8192]{1,0:T(8,128)(2,1)S(1)} %get-tuple-element.100), channel_id=1, source_target_pairs={{0,32},{8,104},{4,36},{12,108},{16,48},{24,120},{20,52},{28,124},{... | collective-permute-start | bytes 3145736 | tf_op jit(solution)/shard_map/ppermute | solution.py:51
  118.2 2.2 %collective-permute-done.19 = bf16[512,1024]{1,0:T(8,128)(2,1)S(1)} collective-permute-done((bf16[512,1024]{1,0:T(8,128)(2,1)S(1)}, bf16[512,1024]{1,0:T(8,128)(2,1)S(1)}, u32[]{:S(2)}, u32[]{:S(2)}) %collective-permute-start.19) | collective-permute-done | bytes 1048608 | tf_op jit(solution)/shard_map/ppermute | solution.py:51
  120.8 1.9 %collective-permute-done.18 = bf16[512,512]{1,0:T(8,128)(2,1)S(1)} collective-permute-done((bf16[512,512]{1,0:T(8,128)(2,1)S(1)}, bf16[512,512]{1,0:T(8,128)(2,1)S(1)}, u32[]{:S(2)}, u32[]{:S(2)}) %collective-permute-start.18) | collective-permute-done | bytes 524320 | tf_op jit(solution)/shard_map/ppermute | solution.py:51
  122.6 1.6 collective-permute-start.23
  124.5 9.5 %backward_ends.1 = (bf16[512,512]{1,0:T(8,128)(2,1)}, f32[4,512,128]{2,1,0:T(8,128)S(1)}, f32[56,512]{1,0:T(8,128)S(1)}, f32[4,128,128]{2,1,0:T(8,128)S(1)}) custom-call(f32[512,512]{1,0:T(8,128)S(1)} %convert_add_fusion.1.grad_ref, bf16[512,512]{1,0:T(8,128)(2,1)S(1)} %copy-done.6, f32[4,512,128]{2,1,0:T(8,128)S(1)} %copy-done.11, ...), custom_call_target="tpu_custom_call" | custom-call | flops 115000000 | tf_op jit(solution)/shard_map/backward_ends/pallas_call | solution.py:354
  134.0 7.0 %collective-permute-done.20 = bf16[64,8192]{1,0:T(8,128)(2,1)S(1)} collective-permute-done((bf16[64,8192]{1,0:T(8,128)(2,1)S(1)}, bf16[64,8192]{1,0:T(8,128)(2,1)S(1)}, u32[]{:S(2)}, u32[]{:S(2)}) %collective-permute-start.20) | collective-permute-done | bytes 1048608 | tf_op jit(solution)/shard_map/ppermute | solution.py:51
  141.8 1.4 collective-permute-start.22
  143.1 2.4 %collective-permute-done.23 = bf16[512,1024]{1,0:T(8,128)(2,1)S(1)} collective-permute-done((bf16[512,1024]{1,0:T(8,128)(2,1)S(1)}, bf16[512,1024]{1,0:T(8,128)(2,1)S(1)}, u32[]{:S(2)}, u32[]{:S(2)}) %collective-permute-start.23) | collective-permute-done | bytes 1048608 | tf_op jit(solution)/shard_map/ppermute | solution.py:51
  145.6 4.8 %collective-permute-done.24 = bf16[512,1024]{1,0:T(8,128)(2,1)S(1)} collective-permute-done((bf16[512,1024]{1,0:T(8,128)(2,1)S(1)}, bf16[512,1024]{1,0:T(8,128)(2,1)S(1)}, u32[]{:S(2)}, u32[]{:S(2)}) %collective-permute-start.24) | collective-permute-done | bytes 1048608 | tf_op jit(solution)/shard_map/ppermute | solution.py:51
  151.9 1.8 collective-permute-start.25
  154.3 2.2 %collective-permute-start.28 = (f32[72,512]{1,0:T(8,128)S(1)}, f32[72,512]{1,0:T(8,128)S(1)}, u32[]{:S(2)}, u32[]{:S(2)}) collective-permute-start(f32[72,512]{1,0:T(8,128)S(1)} %pad_maximum_fusion.1.refs_7_), channel_id=1, source_target_pairs={{0,3},{8,11},{4,7},{12,15},{16,19},{24,27},{20,23},{28,31},{32,35}... | collective-permute-start | bytes 442376 | tf_op jit(solution)/shard_map/ppermute | solution.py:51
  156.5 6.6 %collective-permute-done.26.refs_8_ = f32[72,512]{1,0:T(8,128)S(1)} collective-permute-done((f32[72,512]{1,0:T(8,128)S(1)}, f32[72,512]{1,0:T(8,128)S(1)}, u32[]{:S(2)}, u32[]{:S(2)}) %collective-permute-start.26) | collective-permute-done | bytes 147488 | tf_op jit(solution)/shard_map/ppermute | solution.py:51
  163.1 2.4 %collective-permute-done.25 = bf16[32,8192]{1,0:T(8,128)(2,1)S(1)} collective-permute-done((bf16[32,8192]{1,0:T(8,128)(2,1)S(1)}, bf16[32,8192]{1,0:T(8,128)(2,1)S(1)}, u32[]{:S(2)}, u32[]{:S(2)}) %collective-permute-start.25) | collective-permute-done | bytes 524320 | tf_op jit(solution)/shard_map/ppermute | solution.py:51
  165.5 5.0 %collective-permute-start.29 = (bf16[32,8192]{1,0:T(8,128)(2,1)S(1)}, bf16[32,8192]{1,0:T(8,128)(2,1)}, u32[]{:S(2)}, u32[]{:S(2)}) collective-permute-start(bf16[32,8192]{1,0:T(8,128)(2,1)S(1)} %collective-permute-done.25), channel_id=1, source_target_pairs={{8,28},{12,8},{24,12},{28,24},{40,60},{44,40},{56,44},{60,56},{72,... | collective-permute-start | bytes 1572872 | tf_op jit(solution)/shard_map/ppermute | solution.py:51
  170.5 3.6 %add_convert_fusion = bf16[512,1024]{1,0:T(8,128)(2,1)} fusion(bf16[512,1024]{1,0:T(8,128)(2,1)} %copy-done.26, bf16[512,1024]{1,0:T(8,128)(2,1)} %copy-done.25, bf16[512,1024]{1,0:T(8,128)(2,1)} %multiply_convert_fusion), kind=kLoop, calls=%fused_computation.2 | loop fusion | flops 3145728 | bytes 4194304 | tf_op jit(solution)/shard_map/convert_element_type | solution.py:462
  174.1 5.1 %backward_full.1 = (bf16[512,512]{1,0:T(8,128)(2,1)}, bf16[512,512]{1,0:T(8,128)(2,1)}, f32[16,512]{1,0:T(8,128)}, f32[16,512]{1,0:T(8,128)}, f32[8,512]{1,0:T(8,128)S(1)}) custom-call(bf16[512,512]{1,0:T(8,128)(2,1)S(1)} %copy-done.3, bf16[512,512]{1,0:T(8,128)(2,1)S(1)} %copy-done.5, f32[4,512,128]{2,1,0:T(8,128)S(1)} %get-tuple-element.112.refs_2_, ...), custom_call_target="tpu_custom_call" | custom-call | flops 115000000 | tf_op jit(solution)/shard_map/backward_full/pallas_call | solution.py:354
  179.7 2.0 %fusion.18 = bf16[32,8192]{1,0:T(8,128)(2,1)} fusion(f32[64,8192]{1,0:T(8,128)S(1)} %copy-done.24, bf16[32,8192]{1,0:T(8,128)(2,1)S(1)} %collective-permute-done.25, bf16[32,8192]{1,0:T(8,128)(2,1)} %collective-permute-done.29, pred[]{:T(512)S(6)} %eq.13), kind=kLoop, calls=%fused_computation.22 | loop fusion | flops 1048576 | bytes 2621441 | tf_op jit(solution)/shard_map/convert_element_type | solution.py:461
  (98 shorter events, 14.9 us)
Async XLA Ops:
  1.7 20.7 %collective-permute-start.1 = (bf16[32,4096]{1,0:T(8,128)(2,1)S(1)}, bf16[32,4096]{1,0:T(8,128)(2,1)S(1)}, u32[]{:S(2)}, u32[]{:S(2)}) collective-permute-start(bf16[32,4096]{1,0:T(8,128)(2,1)S(1)} %get-tuple-element.125), channel_id=1, source_target_pairs={{0,4},{8,12},{4,16},{12,24},{16,20},{24,28},{20,0},{28,8},{32,36},... | collective-permute-start | bytes 786440 | tf_op jit(solution)/shard_map/ppermute | solution.py:51
  4.3 19.3 %collective-permute-start.2 = (bf16[32,4096]{1,0:T(8,128)(2,1)S(1)}, bf16[32,4096]{1,0:T(8,128)(2,1)S(1)}, u32[]{:S(2)}, u32[]{:S(2)}) collective-permute-start(bf16[32,4096]{1,0:T(8,128)(2,1)S(1)} %get-tuple-element.125), channel_id=1, source_target_pairs={{0,20},{8,28},{4,0},{12,8},{16,4},{24,12},{20,16},{28,24},{32,52},... | collective-permute-start | bytes 786440 | tf_op jit(solution)/shard_map/ppermute | solution.py:51
  6.5 17.3 %collective-permute-start = (bf16[32,4096]{1,0:T(8,128)(2,1)S(1)}, bf16[32,4096]{1,0:T(8,128)(2,1)S(1)}, u32[]{:S(2)}, u32[]{:S(2)}) collective-permute-start(bf16[32,4096]{1,0:T(8,128)(2,1)S(1)} %get-tuple-element.124), channel_id=1, source_target_pairs={{0,16},{8,24},{4,20},{12,28},{16,0},{24,8},{20,4},{28,12},{32,48},... | collective-permute-start | bytes 786440 | tf_op jit(solution)/shard_map/ppermute | solution.py:51
  14.6 4.2 %collective-permute-start.3 = (f32[32,512]{1,0:T(8,128)S(1)}, f32[32,512]{1,0:T(8,128)S(1)}, u32[]{:S(2)}, u32[]{:S(2)}) collective-permute-start(f32[32,512]{1,0:T(8,128)S(1)} %get-tuple-element.65), channel_id=1, source_target_pairs={{0,4},{8,12},{4,0},{12,8},{16,20},{24,28},{20,16},{28,24},{32,36},... | collective-permute-start | bytes 196616 | tf_op jit(solution)/shard_map/ppermute | solution.py:51
  18.7 5.2 %collective-permute-start.4 = (f32[64,512]{1,0:T(8,128)S(1)}, f32[64,512]{1,0:T(8,128)S(1)}, u32[]{:S(2)}, u32[]{:S(2)}) collective-permute-start(f32[64,512]{1,0:T(8,128)S(1)} %constant_dynamic-update-slice_fusion.refs_6_), channel_id=1, source_target_pairs={{0,1},{8,9},{4,5},{12,13},{16,17},{24,25},{20,21},{28,29},{32,33},... | collective-permute-start | bytes 393224 | tf_op jit(solution)/shard_map/ppermute | solution.py:51
  20.0 6.9 %collective-permute-start.5 = (f32[64,512]{1,0:T(8,128)S(1)}, f32[64,512]{1,0:T(8,128)S(1)}, u32[]{:S(2)}, u32[]{:S(2)}) collective-permute-start(f32[64,512]{1,0:T(8,128)S(1)} %constant_dynamic-update-slice_fusion.refs_6_), channel_id=1, source_target_pairs={{0,2},{8,10},{4,6},{12,14},{16,18},{24,26},{20,22},{28,30},{32,34}... | collective-permute-start | bytes 393224 | tf_op jit(solution)/shard_map/ppermute | solution.py:51
  22.4 5.1 %collective-permute-start.6 = (f32[64,512]{1,0:T(8,128)S(1)}, f32[64,512]{1,0:T(8,128)S(1)}, u32[]{:S(2)}, u32[]{:S(2)}) collective-permute-start(f32[64,512]{1,0:T(8,128)S(1)} %constant_dynamic-update-slice_fusion.refs_6_), channel_id=1, source_target_pairs={{0,3},{8,11},{4,7},{12,15},{16,19},{24,27},{20,23},{28,31},{32,35}... | collective-permute-start | bytes 393224 | tf_op jit(solution)/shard_map/ppermute | solution.py:51
  23.6 6.7 %copy-start.6 = (bf16[512,512]{1,0:T(8,128)(2,1)S(1)}, bf16[512,512]{1,0:T(8,128)(2,1)}, u32[]{:S(2)}) copy-start(bf16[512,512]{1,0:T(8,128)(2,1)} %query_ref.1) | copy-start | bytes 1572868
  23.6 6.7 %copy-start.13 = (f32[16,512]{1,0:T(8,128)S(1)}, f32[16,512]{1,0:T(8,128)}, u32[]{:S(2)}) copy-start(f32[16,512]{1,0:T(8,128)} %refs_4_.3) | copy-start | bytes 98308
  23.6 6.6 %copy-start.15 = (f32[4,256,128]{2,1,0:T(8,128)S(1)}, f32[4,256,128]{2,1,0:T(8,128)}, u32[]{:S(2)}) copy-start(f32[4,256,128]{2,1,0:T(8,128)} %copy-done.14) | copy-start | bytes 1572868
  23.6 6.6 %copy-start.18 = (f32[16,512]{1,0:T(8,128)S(1)}, f32[16,512]{1,0:T(8,128)}, u32[]{:S(2)}) copy-start(f32[16,512]{1,0:T(8,128)} %refs_5_.1) | copy-start | bytes 98308
  23.7 6.6 %copy-start.19 = (f32[512]{0:T(512)S(1)}, f32[512]{0:T(512)}, u32[]{:S(2)}) copy-start(f32[512]{0:T(512)} %param.11) | copy-start | bytes 6148
  27.5 22.8 %collective-permute-start.7 = (bf16[2,2,32,4096]{3,2,1,0:T(8,128)(2,1)S(1)}, bf16[2,2,32,4096]{3,2,1,0:T(8,128)(2,1)}, u32[]{:S(2)}, u32[]{:S(2)}) collective-permute-start(bf16[2,2,32,4096]{3,2,1,0:T(8,128)(2,1)S(1)} %pad_maximum_fusion.refs_2_), channel_id=1, source_target_pairs={{0,32},{8,104},{4,36},{12,108},{16,48},{24,120},{20,52},{28,124},{... | collective-permute-start | bytes 3145736 | tf_op jit(solution)/shard_map/ppermute | solution.py:51
  30.3 26.3 %collective-permute-start.8 = (bf16[2,2,32,4096]{3,2,1,0:T(8,128)(2,1)S(1)}, bf16[2,2,32,4096]{3,2,1,0:T(8,128)(2,1)S(1)}, u32[]{:S(2)}, u32[]{:S(2)}) collective-permute-start(bf16[2,2,32,4096]{3,2,1,0:T(8,128)(2,1)S(1)} %pad_maximum_fusion.refs_2_), channel_id=1, source_target_pairs={{0,96},{8,40},{4,100},{12,44},{16,112},{24,56},{20,116},{28,60},{3... | collective-permute-start | bytes 3145736 | tf_op jit(solution)/shard_map/ppermute | solution.py:51
  57.6 29.9 %collective-permute-start.10 = (bf16[2,2,32,4096]{3,2,1,0:T(8,128)(2,1)}, bf16[2,2,32,4096]{3,2,1,0:T(8,128)(2,1)}, u32[]{:S(2)}, u32[]{:S(2)}) collective-permute-start(bf16[2,2,32,4096]{3,2,1,0:T(8,128)(2,1)} %collective-permute-done.7.refs_4_), channel_id=1, source_target_pairs={{0,32},{8,104},{4,36},{12,108},{16,48},{24,120},{20,52},{28,124},{... | collective-permute-start | bytes 3145736 | tf_op jit(solution)/shard_map/ppermute | solution.py:51
  57.6 3.4 %copy-start.20 = (bf16[512,8192]{1,0:T(8,128)(2,1)S(1)}, bf16[512,8192]{1,0:T(8,128)(2,1)}, u32[]{:S(2)}) copy-start(bf16[512,8192]{1,0:T(8,128)(2,1)} %weight_ref.1) | copy-start | bytes 25165828
  68.4 1.6 copy-start
  71.0 1.7 copy-start.22
  72.7 14.8 %collective-permute-start.9 = (bf16[64,8192]{1,0:T(8,128)(2,1)}, bf16[64,8192]{1,0:T(8,128)(2,1)}, u32[]{:S(2)}, u32[]{:S(2)}) collective-permute-start(bf16[64,8192]{1,0:T(8,128)(2,1)} %get-tuple-element.76), channel_id=1, source_target_pairs={{0,8},{8,0},{4,12},{12,4},{16,24},{24,16},{20,28},{28,20},{32,40},... | collective-permute-start | bytes 3145736 | tf_op jit(solution)/shard_map/ppermute | solution.py:51
  73.1 13.5 %collective-permute-start.11 = (bf16[512,512]{1,0:T(8,128)(2,1)S(1)}, bf16[512,512]{1,0:T(8,128)(2,1)}, u32[]{:S(2)}, u32[]{:S(2)}) collective-permute-start(bf16[512,512]{1,0:T(8,128)(2,1)S(1)} %get-tuple-element.79.refs_0_), channel_id=1, source_target_pairs={{0,4},{8,12},{4,0},{12,8},{16,20},{24,28},{20,16},{28,24},{32,36},... | collective-permute-start | bytes 1572872 | tf_op jit(solution)/shard_map/ppermute | solution.py:51
  73.1 20.0 %copy-start.8 = (bf16[2,2,32,4096]{3,2,1,0:T(8,128)(2,1)S(1)}, bf16[2,2,32,4096]{3,2,1,0:T(8,128)(2,1)}, u32[]{:S(2)}) copy-start(bf16[2,2,32,4096]{3,2,1,0:T(8,128)(2,1)} %copy-done.7) | copy-start | bytes 3145732
  73.1 16.8 %collective-permute-start.13 = (bf16[2,2,32,4096]{3,2,1,0:T(8,128)(2,1)S(1)}, bf16[2,2,32,4096]{3,2,1,0:T(8,128)(2,1)S(1)}, u32[]{:S(2)}, u32[]{:S(2)}) collective-permute-start(bf16[2,2,32,4096]{3,2,1,0:T(8,128)(2,1)S(1)} %pad_maximum_fusion.refs_2_), channel_id=1, source_target_pairs={{0,8},{8,0},{4,12},{12,4},{16,24},{24,16},{20,28},{28,20},{32,40},... | collective-permute-start | bytes 3145736 | tf_op jit(solution)/shard_map/ppermute | solution.py:51
  73.2 19.9 %collective-permute-start.14 = (bf16[2,2,32,4096]{3,2,1,0:T(8,128)(2,1)}, bf16[2,2,32,4096]{3,2,1,0:T(8,128)(2,1)S(1)}, u32[]{:S(2)}, u32[]{:S(2)}) collective-permute-start(bf16[2,2,32,4096]{3,2,1,0:T(8,128)(2,1)} %collective-permute-done.7.refs_4_), channel_id=1, source_target_pairs={{0,8},{8,0},{4,12},{12,4},{16,24},{24,16},{20,28},{28,20},{32,40},... | collective-permute-start | bytes 3145736 | tf_op jit(solution)/shard_map/ppermute | solution.py:51
  86.6 6.5 %collective-permute-start.15 = (bf16[2,2,32,4096]{3,2,1,0:T(8,128)(2,1)}, bf16[2,2,32,4096]{3,2,1,0:T(8,128)(2,1)S(1)}, u32[]{:S(2)}, u32[]{:S(2)}) collective-permute-start(bf16[2,2,32,4096]{3,2,1,0:T(8,128)(2,1)} %copy-done.7), channel_id=1, source_target_pairs={{0,8},{8,0},{4,12},{12,4},{16,24},{24,16},{20,28},{28,20},{32,40},... | collective-permute-start | bytes 3145736 | tf_op jit(solution)/shard_map/ppermute | solution.py:51
  87.5 5.5 %collective-permute-start.16 = (bf16[2,2,32,4096]{3,2,1,0:T(8,128)(2,1)}, bf16[2,2,32,4096]{3,2,1,0:T(8,128)(2,1)S(1)}, u32[]{:S(2)}, u32[]{:S(2)}) collective-permute-start(bf16[2,2,32,4096]{3,2,1,0:T(8,128)(2,1)} %collective-permute-done.10.refs_8_), channel_id=1, source_target_pairs={{0,8},{8,0},{4,12},{12,4},{16,24},{24,16},{20,28},{28,20},{32,40},... | collective-permute-start | bytes 3145736 | tf_op jit(solution)/shard_map/ppermute | solution.py:51
  87.6 26.0 %collective-permute-start.12 = (bf16[192,8192]{1,0:T(8,128)(2,1)}, bf16[192,8192]{1,0:T(8,128)(2,1)S(1)}, u32[]{:S(2)}, u32[]{:S(2)}) collective-permute-start(bf16[192,8192]{1,0:T(8,128)(2,1)} %copy-done.22), channel_id=1, source_target_pairs={{0,8},{8,0},{4,12},{12,4},{16,24},{24,16},{20,28},{28,20},{32,40},... | collective-permute-start | bytes 9437192 | tf_op jit(solution)/shard_map/ppermute | solution.py:51
  89.8 5.2 %copy-start.21 = (bf16[512,8192]{1,0:T(8,128)(2,1)S(1)}, bf16[512,8192]{1,0:T(8,128)(2,1)}, u32[]{:S(2)}) copy-start(bf16[512,8192]{1,0:T(8,128)(2,1)} %weight_ref.1) | copy-start | bytes 25165828
  89.8 14.9 %collective-permute-start.17 = (bf16[64,8192]{1,0:T(8,128)(2,1)S(1)}, bf16[64,8192]{1,0:T(8,128)(2,1)S(1)}, u32[]{:S(2)}, u32[]{:S(2)}) collective-permute-start(bf16[64,8192]{1,0:T(8,128)(2,1)S(1)} %add_convert_fusion.4), channel_id=1, source_target_pairs={{0,32},{8,104},{4,36},{12,108},{16,48},{24,120},{20,52},{28,124},{... | collective-permute-start | bytes 3145736 | tf_op jit(solution)/shard_map/ppermute | solution.py:51
  106.1 14.3 %collective-permute-start.19 = (bf16[512,1024]{1,0:T(8,128)(2,1)S(1)}, bf16[512,1024]{1,0:T(8,128)(2,1)S(1)}, u32[]{:S(2)}, u32[]{:S(2)}) collective-permute-start(bf16[512,1024]{1,0:T(8,128)(2,1)S(1)} %multiply_convert_fusion.3), channel_id=1, source_target_pairs={{0,1},{8,11},{4,5},{12,15},{16,17},{24,27},{20,21},{28,31},{32,33}... | collective-permute-start | bytes 3145736 | tf_op jit(solution)/shard_map/ppermute | solution.py:51
  108.7 14.0 %collective-permute-start.18 = (bf16[512,512]{1,0:T(8,128)(2,1)S(1)}, bf16[512,512]{1,0:T(8,128)(2,1)S(1)}, u32[]{:S(2)}, u32[]{:S(2)}) collective-permute-start(bf16[512,512]{1,0:T(8,128)(2,1)S(1)} %slice.50), channel_id=1, source_target_pairs={{0,4},{8,12},{4,0},{12,8},{16,20},{24,28},{20,16},{28,24},{32,36},... | collective-permute-start | bytes 1572872 | tf_op jit(solution)/shard_map/ppermute | solution.py:51
  112.4 1.9 %copy-start.1 = (bf16[192,8192]{1,0:T(8,128)(2,1)S(1)}, bf16[192,8192]{1,0:T(8,128)(2,1)}, u32[]{:S(2)}) copy-start(bf16[192,8192]{1,0:T(8,128)(2,1)} %copy-done) | copy-start | bytes 9437188
  115.0 26.0 %collective-permute-start.20 = (bf16[64,8192]{1,0:T(8,128)(2,1)S(1)}, bf16[64,8192]{1,0:T(8,128)(2,1)S(1)}, u32[]{:S(2)}, u32[]{:S(2)}) collective-permute-start(bf16[64,8192]{1,0:T(8,128)(2,1)S(1)} %get-tuple-element.100), channel_id=1, source_target_pairs={{0,32},{8,104},{4,36},{12,108},{16,48},{24,120},{20,52},{28,124},{... | collective-permute-start | bytes 3145736 | tf_op jit(solution)/shard_map/ppermute | solution.py:51
  118.2 23.6 %collective-permute-start.21 = (bf16[64,8192]{1,0:T(8,128)(2,1)S(1)}, bf16[64,8192]{1,0:T(8,128)(2,1)S(1)}, u32[]{:S(2)}, u32[]{:S(2)}) collective-permute-start(bf16[64,8192]{1,0:T(8,128)(2,1)S(1)} %get-tuple-element.101), channel_id=1, source_target_pairs={{0,96},{8,40},{4,100},{12,44},{16,112},{24,56},{20,116},{28,60},{3... | collective-permute-start | bytes 3145736 | tf_op jit(solution)/shard_map/ppermute | solution.py:51
  120.8 3.7 %copy-start.11 = (f32[4,512,128]{2,1,0:T(8,128)S(1)}, f32[4,512,128]{2,1,0:T(8,128)}, u32[]{:S(2)}) copy-start(f32[4,512,128]{2,1,0:T(8,128)} %copy-done.10) | copy-start | bytes 3145732
  120.8 3.7 %copy-start.17 = (f32[4,256,128]{2,1,0:T(8,128)S(1)}, f32[4,256,128]{2,1,0:T(8,128)}, u32[]{:S(2)}) copy-start(f32[4,256,128]{2,1,0:T(8,128)} %copy-done.16) | copy-start | bytes 1572868
  122.6 22.9 %collective-permute-start.23 = (bf16[512,1024]{1,0:T(8,128)(2,1)S(1)}, bf16[512,1024]{1,0:T(8,128)(2,1)S(1)}, u32[]{:S(2)}, u32[]{:S(2)}) collective-permute-start(bf16[512,1024]{1,0:T(8,128)(2,1)S(1)} %add_convert_fusion.1), channel_id=1, source_target_pairs={{0,1},{8,11},{4,5},{12,15},{16,17},{24,27},{20,21},{28,31},{32,33}... | collective-permute-start | bytes 3145736 | tf_op jit(solution)/shard_map/ppermute | solution.py:51
  124.3 26.1 %collective-permute-start.24 = (bf16[512,1024]{1,0:T(8,128)(2,1)S(1)}, bf16[512,1024]{1,0:T(8,128)(2,1)S(1)}, u32[]{:S(2)}, u32[]{:S(2)}) collective-permute-start(bf16[512,1024]{1,0:T(8,128)(2,1)S(1)} %multiply_convert_fusion.1), channel_id=1, source_target_pairs={{0,3},{8,9},{4,7},{12,13},{16,19},{24,25},{20,23},{28,29},{32,35},... | collective-permute-start | bytes 3145736 | tf_op jit(solution)/shard_map/ppermute | solution.py:51
  141.8 9.6 %collective-permute-start.22 = (f32[56,512]{1,0:T(8,128)S(1)}, f32[56,512]{1,0:T(8,128)S(1)}, u32[]{:S(2)}, u32[]{:S(2)}) collective-permute-start(f32[56,512]{1,0:T(8,128)S(1)} %get-tuple-element.102), channel_id=1, source_target_pairs={{0,4},{8,12},{4,0},{12,8},{16,20},{24,28},{20,16},{28,24},{32,36},... | collective-permute-start | bytes 344072 | tf_op jit(solution)/shard_map/ppermute | solution.py:51
  145.6 6.3 %copy-start.25 = (bf16[512,1024]{1,0:T(8,128)(2,1)}, bf16[512,1024]{1,0:T(8,128)(2,1)S(1)}, u32[]{:S(2)}) copy-start(bf16[512,1024]{1,0:T(8,128)(2,1)S(1)} %collective-permute-done.23) | copy-start | bytes 3145732
  151.9 11.3 %copy-start.23 = (f32[64,8192]{1,0:T(8,128)}, f32[64,8192]{1,0:T(8,128)S(1)}, u32[]{:S(2)}) copy-start(f32[64,8192]{1,0:T(8,128)S(1)} %convert_add_fusion) | copy-start | bytes 6291460
  151.9 13.5 %collective-permute-start.25 = (bf16[32,8192]{1,0:T(8,128)(2,1)S(1)}, bf16[32,8192]{1,0:T(8,128)(2,1)S(1)}, u32[]{:S(2)}, u32[]{:S(2)}) collective-permute-start(bf16[32,8192]{1,0:T(8,128)(2,1)S(1)} %slice.49), channel_id=1, source_target_pairs={{0,16},{8,28},{4,20},{12,8},{16,0},{24,12},{20,4},{28,24},{32,48},... | collective-permute-start | bytes 1572872 | tf_op jit(solution)/shard_map/ppermute | solution.py:51
  153.8 9.3 %collective-permute-start.26 = (f32[72,512]{1,0:T(8,128)S(1)}, f32[72,512]{1,0:T(8,128)S(1)}, u32[]{:S(2)}, u32[]{:S(2)}) collective-permute-start(f32[72,512]{1,0:T(8,128)S(1)} %pad_maximum_fusion.1.refs_7_), channel_id=1, source_target_pairs={{0,1},{8,9},{4,5},{12,13},{16,17},{24,25},{20,21},{28,29},{32,33},... | collective-permute-start | bytes 442376 | tf_op jit(solution)/shard_map/ppermute | solution.py:51
  153.9 9.3 %collective-permute-start.27 = (f32[72,512]{1,0:T(8,128)S(1)}, f32[72,512]{1,0:T(8,128)S(1)}, u32[]{:S(2)}, u32[]{:S(2)}) collective-permute-start(f32[72,512]{1,0:T(8,128)S(1)} %pad_maximum_fusion.1.refs_7_), channel_id=1, source_target_pairs={{0,2},{8,10},{4,6},{12,14},{16,18},{24,26},{20,22},{28,30},{32,34}... | collective-permute-start | bytes 442376 | tf_op jit(solution)/shard_map/ppermute | solution.py:51
  154.3 8.8 %collective-permute-start.28 = (f32[72,512]{1,0:T(8,128)S(1)}, f32[72,512]{1,0:T(8,128)S(1)}, u32[]{:S(2)}, u32[]{:S(2)}) collective-permute-start(f32[72,512]{1,0:T(8,128)S(1)} %pad_maximum_fusion.1.refs_7_), channel_id=1, source_target_pairs={{0,3},{8,11},{4,7},{12,15},{16,19},{24,27},{20,23},{28,31},{32,35}... | collective-permute-start | bytes 442376 | tf_op jit(solution)/shard_map/ppermute | solution.py:51
  165.5 14.3 %collective-permute-start.29 = (bf16[32,8192]{1,0:T(8,128)(2,1)S(1)}, bf16[32,8192]{1,0:T(8,128)(2,1)}, u32[]{:S(2)}, u32[]{:S(2)}) collective-permute-start(bf16[32,8192]{1,0:T(8,128)(2,1)S(1)} %collective-permute-done.25), channel_id=1, source_target_pairs={{8,28},{12,8},{24,12},{28,24},{40,60},{44,40},{56,44},{60,56},{72,... | collective-permute-start | bytes 1572872 | tf_op jit(solution)/shard_map/ppermute | solution.py:51
  170.5 3.6 %copy-start.3 = (bf16[512,512]{1,0:T(8,128)(2,1)S(1)}, bf16[512,512]{1,0:T(8,128)(2,1)}, u32[]{:S(2)}) copy-start(bf16[512,512]{1,0:T(8,128)(2,1)} %refs_0_.3) | copy-start | bytes 1572868
  170.5 3.6 %copy-start.5 = (bf16[512,512]{1,0:T(8,128)(2,1)S(1)}, bf16[512,512]{1,0:T(8,128)(2,1)}, u32[]{:S(2)}) copy-start(bf16[512,512]{1,0:T(8,128)(2,1)} %refs_1_.1) | copy-start | bytes 1572868
  174.1 5.7 %copy-start.24 = (f32[64,8192]{1,0:T(8,128)S(1)}, f32[64,8192]{1,0:T(8,128)}, u32[]{:S(2)}) copy-start(f32[64,8192]{1,0:T(8,128)} %copy-done.23) | copy-start | bytes 6291460
  (9 other events, 8.3 us)

commit v10 on v9

--- a/solution.py
+++ b/solution.py
@@ -68,7 +68,7 @@
     return jnp.stack([stack, other])
 
 
-def put_in_place(*refs):
+def put_in_place(*refs, spots):
     gated_ref, gated_other_ref, *block_refs = refs[:-3]
     whole_ref, pair_ref, sems = refs[-3:]
     y, _, core, _, _ = places()
@@ -77,30 +77,33 @@
         pltpu.make_async_copy(gated_ref, pair_ref.at[pl.ds(0, rows)], sems.at[0]),
         pltpu.make_async_copy(gated_other_ref, pair_ref.at[pl.ds(rows, rows)], sems.at[1]),
     ]
-    steps = ((0, 0), (RING - 1, 1), (1, RING - 1), (2, 2))
-    for i, ref in enumerate(block_refs):
+    for i, (ref, (first, steps)) in enumerate(zip(block_refs, spots)):
         at_core = core if i % 2 == 0 else 1 - core
-        row = lax.rem(y + jnp.where(at_core == 0, *steps[i // 2]), RING)
-        copies.append(pltpu.make_async_copy(ref, whole_ref.at[:, row, :, at_core], sems.at[2 + i]))
+        row = lax.rem(y + jnp.where(at_core == 0, *steps), RING)
+        spot = whole_ref.at[pl.ds(first, ref.shape[0]), row, :, at_core]
+        copies.append(pltpu.make_async_copy(ref, spot, sems.at[2 + i]))
     for copy in copies:
         copy.start()
     for copy in copies:
         copy.wait()
 
 
-def place_blocks(gated, gated_other, blocks):
-    _, _, tokens, half = blocks[0].shape
-    parts = [part for block in blocks for part in (block, hop(block, core=1))]
+def place_blocks(gated, gated_other, own, main, other, far):
+    _, _, tokens, half = own.shape
+    blocks = [(own, 0, (0, 0)), (main, 0, (RING - 1, 1))]
+    blocks += [(part, i, (1, RING - 1)) for i, part in enumerate(other)] + [(far, 0, (2, 2))]
+    parts = [part for block, _, _ in blocks for part in (block, hop(block, core=1))]
+    spots = [(first, steps) for _, first, steps in blocks for _ in range(2)]
     rows, channels = gated.shape
     whole = (2, RING, 2, 2, tokens, half)
     moved = 4 * math.prod(whole)
     cot, pair = pl.pallas_call(
-        put_in_place,
+        functools.partial(put_in_place, spots=spots),
         out_shape=[jax.ShapeDtypeStruct(whole, BF16), jax.ShapeDtypeStruct((2 * rows, channels), BF16)],
         in_specs=[pl.BlockSpec(memory_space=pl.ANY)] * (2 + len(parts)),
         out_specs=[pl.BlockSpec(memory_space=pltpu.VMEM)] * 2,
         scratch_shapes=[pltpu.SemaphoreType.DMA((2 + len(parts),))],
-        compiler_params=pltpu.CompilerParams(vmem_limit_bytes=16 * 2**20),
+        compiler_params=pltpu.CompilerParams(vmem_limit_bytes=2 * 2**20),
         cost_estimate=pl.CostEstimate(flops=0, bytes_accessed=moved, transcendentals=0),
         name="put_in_place",
     )(gated, gated_other, *parts)
@@ -130,7 +133,7 @@
         out_shape=[jax.ShapeDtypeStruct((size, width), BF16) for size in sizes],
         in_specs=[pl.BlockSpec((rows, depth), lambda i: (0, 0)), pl.BlockSpec((depth, tile), lambda i: (0, i))],
         out_specs=[pl.BlockSpec((size, tile), lambda i: (0, i)) for size in sizes],
-        compiler_params=pltpu.CompilerParams(vmem_limit_bytes=12 * 2**20),
+        compiler_params=pltpu.CompilerParams(vmem_limit_bytes=10 * 2**20),
         cost_estimate=pl.CostEstimate(
             flops=2 * rows * depth * width, bytes_accessed=2 * width * (rows + depth), transcendentals=0
         ),
@@ -396,8 +399,10 @@
         "forward_ends",
     )
     ends_pair = jnp.concatenate([ends, hop(ends, pair=1)])
-    block, *earlier = together(block, *spread_over_x(ends_pair))
-    main_block, other_block = hop(block, y=MAIN), hop(block, y=OTHER)
+    main_block = hop(block, y=MAIN)
+    other_block = [hop(block[:1], y=OTHER), hop(block[1:], y=OTHER)]
+    other_block[0], ends_pair = together(other_block[0], ends_pair)
+    earlier = spread_over_x(ends_pair)
     gated, turned, pre_gate, lead = call(
         forward_full,
         (queries, driving, subs, log_decay, residue, skip_row, *earlier),
@@ -406,14 +411,15 @@
         0.1,
         "forward_full",
     )
-    main_block, other_block, turned = together(main_block, other_block, turned)
+    block, gated = together(block, gated)
+    main_block, other_block, turned, gated_other = together(main_block, other_block, turned, hop(gated, pair=1))
     far_block = hop(main_block, y=MAIN)
     near_first, near_rest, far_first, far_rest = project(turned, out_weight)
-    far_block, far_rest, gated_other = together(far_block, far_rest, hop(gated, pair=1))
+    far_block, far_rest = together(far_block, far_rest)
     got_first, far_rest = together(hop(far_first, core=1), far_rest)
     got_rest = hop(far_rest, core=1)
     opposite = add(near_first, got_first).astype(BF16)
-    cot_rows, gated_pair = place_blocks(gated, gated_other, (block, main_block, other_block, far_block))
+    cot_rows, gated_pair = place_blocks(gated, gated_other, block, main_block, other_block, far_block)
 
     _, _, core, low, x = places()
     half = out_weight.shape[1] // 2

time: 182 us -> 175 us (0.962)
  waiting for transfers between devices: 73.9 us -> 60.3 us
  starting transfers between devices: 38.2 us -> 47.3 us
  local copies, waits for them, and re-layouts: 17.5 us -> 14.5 us
    ppermute x30 -> x32, waiting for transfers between devices: 73.9 us -> 60.3 us  [hop(): return lax.ppermute(value, ('chan', 'seq'), moves)]
    ppermute x30 -> x32, starting transfers between devices: 38.2 us -> 47.3 us  [hop(): return lax.ppermute(value, ('chan', 'seq'), moves)]
    unnamed x55 -> x54, local copies, waits for them, and re-layouts: 15.7 us -> 12.7 us
  transfers between devices with their start and end apart: 30 -> 32, of which waited for: 15 -> 18; matrix products, arithmetic and copies ran while one was open for 10% -> 10% of each run, Pallas kernels for 17% -> 18%
where the time goes in v10:
time: 175 us; the launch traced here: 174 us
  waiting for transfers between devices  60.3 us (34%)
  starting transfers between devices  47.3 us (27%)
  Pallas kernels  31.3 us (18%)
  local copies, waits for them, and re-layouts  14.5 us (8%)
  matrix products  10.7 us (6%)
  other arithmetic  9.36 us (5%)
    ppermute x32, waiting for transfers between devices, hop(): return lax.ppermute(value, ('chan', 'seq'), moves)  60.3 us
    ppermute x32, starting transfers between devices, hop(): return lax.ppermute(value, ('chan', 'seq'), moves)  47.3 us
    pallas_call x4, Pallas kernels, call(): pl.pallas_call(body, out_shape=[jax.ShapeDtypeStruct(o.shape, o.dtype) fo...  21.6 us
    unnamed x54, local copies, waits for them, and re-layouts  12.7 us
    pallas_call x1, Pallas kernels, project(): pl.pallas_call(project_tile, grid=(width // tile,), out_shape=[jax.ShapeD...  7.45 us
    dot_general x4, matrix products, weigh(): lax.dot_general(gated, columns, (((0,), (0,)), ((), ())), preferred_eleme...  6.13 us
    dot_general x1, matrix products, local(): lax.dot_general(cot_rows, low_weight, (((1,), (1,)), ((), ())), preferred...  4.52 us
  transfers between devices with their start and end apart: 32, of which 18 were waited for; matrix products, arithmetic and copies ran while one was open for 10% of the time, Pallas kernels for 18%

profile of v10, /device:TPU:1, one launch (start us, length us, event | category | flops | bytes accessed | tf_op | source)
XLA Modules:
  0.0 174.4 jit_solution(8806193517851380419)
XLA Ops:
  1.7 4.5 %collective-permute-start = (bf16[32,4096]{1,0:T(8,128)(2,1)S(1)}, bf16[32,4096]{1,0:T(8,128)(2,1)S(1)}, u32[]{:S(2)}, u32[]{:S(2)}) collective-permute-start(bf16[32,4096]{1,0:T(8,128)(2,1)S(1)} %get-tuple-element.124), channel_id=1, source_target_pairs={{0,16},{8,24},{4,20},{12,28},{16,0},{24,8},{20,4},{28,12},{32,48},... | collective-permute-start | bytes 786440 | tf_op jit(solution)/shard_map/ppermute | solution.py:51
  7.0 1.9 %collective-permute-start.2 = (bf16[32,4096]{1,0:T(8,128)(2,1)S(1)}, bf16[32,4096]{1,0:T(8,128)(2,1)S(1)}, u32[]{:S(2)}, u32[]{:S(2)}) collective-permute-start(bf16[32,4096]{1,0:T(8,128)(2,1)S(1)} %get-tuple-element.125), channel_id=1, source_target_pairs={{0,20},{8,28},{4,0},{12,8},{16,4},{24,12},{20,16},{28,24},{32,52},... | collective-permute-start | bytes 786440 | tf_op jit(solution)/shard_map/ppermute | solution.py:51
  8.9 3.4 %collective-permute-done = bf16[32,4096]{1,0:T(8,128)(2,1)S(1)} collective-permute-done((bf16[32,4096]{1,0:T(8,128)(2,1)S(1)}, bf16[32,4096]{1,0:T(8,128)(2,1)S(1)}, u32[]{:S(2)}, u32[]{:S(2)}) %collective-permute-start) | collective-permute-done | bytes 262176 | tf_op jit(solution)/shard_map/ppermute | solution.py:51
  12.4 1.4 collective-permute-start.4
  13.8 4.8 %collective-permute-done.1 = bf16[32,4096]{1,0:T(8,128)(2,1)S(1)} collective-permute-done((bf16[32,4096]{1,0:T(8,128)(2,1)S(1)}, bf16[32,4096]{1,0:T(8,128)(2,1)S(1)}, u32[]{:S(2)}, u32[]{:S(2)}) %collective-permute-start.1) | collective-permute-done | bytes 262176 | tf_op jit(solution)/shard_map/ppermute | solution.py:51
  18.9 2.8 %collective-permute-start.3 = (bf16[2,2,32,4096]{3,2,1,0:T(8,128)(2,1)S(1)}, bf16[2,2,32,4096]{3,2,1,0:T(8,128)(2,1)}, u32[]{:S(2)}, u32[]{:S(2)}) collective-permute-start(bf16[2,2,32,4096]{3,2,1,0:T(8,128)(2,1)S(1)} %pad_maximum_fusion.refs_2_), channel_id=1, source_target_pairs={{0,32},{8,104},{4,36},{12,108},{16,48},{24,120},{20,52},{28,124},{... | collective-permute-start | bytes 3145736 | tf_op jit(solution)/shard_map/ppermute | solution.py:51
  21.7 3.2 %forward_ends.1 = (f32[32,512]{1,0:T(8,128)S(1)}, f32[4,256,128]{2,1,0:T(8,128)S(1)}, f32[4,512,128]{2,1,0:T(8,128)S(1)}) custom-call(bf16[512,512]{1,0:T(8,128)(2,1)S(1)} %copy-done.2, bf16[512,512]{1,0:T(8,128)(2,1)S(1)} %copy-done.3, f32[16,512]{1,0:T(8,128)S(1)} %copy-done.9), custom_call_target="tpu_custom_call" | custom-call | flops 115000000 | tf_op jit(solution)/shard_map/forward_ends/pallas_call | solution.py:357
  24.9 1.1 collective-permute-start.5
  26.0 2.8 %collective-permute-done.5 = f32[32,512]{1,0:T(8,128)S(1)} collective-permute-done((f32[32,512]{1,0:T(8,128)S(1)}, f32[32,512]{1,0:T(8,128)S(1)}, u32[]{:S(2)}, u32[]{:S(2)}) %collective-permute-start.5) | collective-permute-done | bytes 65568 | tf_op jit(solution)/shard_map/ppermute | solution.py:51
  28.8 1.3 collective-permute-start.7
  30.1 2.5 %collective-permute-start.8 = (f32[64,512]{1,0:T(8,128)S(1)}, f32[64,512]{1,0:T(8,128)S(1)}, u32[]{:S(2)}, u32[]{:S(2)}) collective-permute-start(f32[64,512]{1,0:T(8,128)S(1)} %pad_maximum_fusion.2.refs_6_), channel_id=1, source_target_pairs={{0,2},{8,10},{4,6},{12,14},{16,18},{24,26},{20,22},{28,30},{32,34}... | collective-permute-start | bytes 393224 | tf_op jit(solution)/shard_map/ppermute | solution.py:51
  32.5 1.2 collective-permute-start.9
  34.5 3.7 %collective-permute-done.8.refs_8_ = f32[64,512]{1,0:T(8,128)S(1)} collective-permute-done((f32[64,512]{1,0:T(8,128)S(1)}, f32[64,512]{1,0:T(8,128)S(1)}, u32[]{:S(2)}, u32[]{:S(2)}) %collective-permute-start.8) | collective-permute-done | bytes 131104 | tf_op jit(solution)/shard_map/ppermute | solution.py:51
  38.2 3.8 %forward_full.1 = (bf16[512,512]{1,0:T(8,128)(2,1)S(1)}, bf16[512,512]{1,0:T(8,128)(2,1)S(1)}, f32[4,512,128]{2,1,0:T(8,128)S(1)}, f32[4,256,128]{2,1,0:T(8,128)S(1)}) custom-call(bf16[512,512]{1,0:T(8,128)(2,1)S(1)} %copy-done.4, f32[4,512,128]{2,1,0:T(8,128)S(1)} %get-tuple-element.67.refs_1_.drive_ref, f32[4,256,128]{2,1,0:T(8,128)S(1)} %get-tuple-element.68.refs_2_, ...), custom_call_target="tpu_custom_call" | custom-call | flops 115000000 | tf_op jit(solution)/shard_map/forward_full/pallas_call | solution.py:357
  43.8 1.3 collective-permute-start.10
  45.9 9.6 %collective-permute-done.10.refs_1_ = bf16[512,512]{1,0:T(8,128)(2,1)S(1)} collective-permute-done((bf16[512,512]{1,0:T(8,128)(2,1)S(1)}, bf16[512,512]{1,0:T(8,128)(2,1)S(1)}, u32[]{:S(2)}, u32[]{:S(2)}) %collective-permute-start.10) | collective-permute-done | bytes 524320 | tf_op jit(solution)/shard_map/ppermute | solution.py:51
  56.4 3.4 %copy-done.20 = bf16[512,8192]{1,0:T(8,128)(2,1)S(1)} copy-done((bf16[512,8192]{1,0:T(8,128)(2,1)S(1)}, bf16[512,8192]{1,0:T(8,128)(2,1)}, u32[]{:S(2)}) %copy-start.20) | copy-done | bytes 8388632
  59.7 7.5 %project.1 = (bf16[64,8192]{1,0:T(8,128)(2,1)S(1)}, bf16[192,8192]{1,0:T(8,128)(2,1)S(1)}, bf16[64,8192]{1,0:T(8,128)(2,1)}, bf16[192,8192]{1,0:T(8,128)(2,1)S(1)}) custom-call(bf16[512,512]{1,0:T(8,128)(2,1)S(1)} %get-tuple-element.73.rows_ref, bf16[512,8192]{1,0:T(8,128)(2,1)S(1)} %copy-done.20), custom_call_target="tpu_custom_call" | custom-call | flops 4294967296 | bytes 16777216 | tf_op jit(solution)/shard_map/project/pallas_call | solution.py:130
  67.2 1.6 copy-done
  69.8 1.7 copy-done.22
  71.5 2.6 %collective-permute-start.11 = (bf16[64,8192]{1,0:T(8,128)(2,1)}, bf16[64,8192]{1,0:T(8,128)(2,1)}, u32[]{:S(2)}, u32[]{:S(2)}) collective-permute-start(bf16[64,8192]{1,0:T(8,128)(2,1)} %get-tuple-element.75), channel_id=1, source_target_pairs={{0,8},{8,0},{4,12},{12,4},{16,24},{24,16},{20,28},{28,20},{32,40},... | collective-permute-start | bytes 3145736 | tf_op jit(solution)/shard_map/ppermute | solution.py:51
  75.3 1.4 collective-permute-done.11
  77.1 1.9 %collective-permute-done.16.refs_7_ = bf16[1,2,32,4096]{3,2,1,0:T(8,128)(2,1)} collective-permute-done((bf16[1,2,32,4096]{3,2,1,0:T(8,128)(2,1)}, bf16[1,2,32,4096]{3,2,1,0:T(8,128)(2,1)}, u32[]{:S(2)}, u32[]{:S(2)}) %collective-permute-start.16) | collective-permute-done | bytes 524320 | tf_op jit(solution)/shard_map/ppermute | solution.py:51
  79.3 1.8 %add_convert_fusion.4 = bf16[64,8192]{1,0:T(8,128)(2,1)S(1)} fusion(bf16[64,8192]{1,0:T(8,128)(2,1)} %collective-permute-done.11, bf16[64,8192]{1,0:T(8,128)(2,1)} %copy-done.6), kind=kLoop, calls=%fused_computation.19 | loop fusion | flops 2097152 | bytes 3145728 | tf_op jit(solution)/shard_map/convert_element_type | solution.py:421
  81.1 3.2 %collective-permute-start.19 = (bf16[64,8192]{1,0:T(8,128)(2,1)S(1)}, bf16[64,8192]{1,0:T(8,128)(2,1)S(1)}, u32[]{:S(2)}, u32[]{:S(2)}) collective-permute-start(bf16[64,8192]{1,0:T(8,128)(2,1)S(1)} %add_convert_fusion.4), channel_id=1, source_target_pairs={{0,32},{8,104},{4,36},{12,108},{16,48},{24,120},{20,52},{28,124},{... | collective-permute-start | bytes 3145736 | tf_op jit(solution)/shard_map/ppermute | solution.py:51
  84.3 2.3 %put_in_place.1 = (bf16[2,4,2,2,32,4096]{5,4,3,2,1,0:T(8,128)(2,1)S(1)}, bf16[1024,512]{1,0:T(8,128)(2,1)S(1)}) custom-call(bf16[512,512]{1,0:T(8,128)(2,1)S(1)} %copy-done.13, bf16[512,512]{1,0:T(8,128)(2,1)S(1)} %copy-done.15, bf16[2,2,32,4096]{3,2,1,0:T(8,128)(2,1)S(1)} %pad_maximum_fusion.refs_2_, ...), custom_call_target="tpu_custom_call" | custom-call | bytes 16777216 | tf_op jit(solution)/shard_map/put_in_place/pallas_call | solution.py:100
  86.6 4.5 %fusion = f32[1024,512]{1,0:T(8,128)S(1)} fusion(bf16[1024,4096]{1,0:T(8,128)(2,1)S(1)} %bitcast.16, bf16[512,8192]{1,0:T(8,128)(2,1)S(1)} %copy-done.21, s32[]{:T(128)S(6)} %select_n.77), kind=kOutput, calls=%fused_computation | convolution fusion | flops 4294967296 | bytes 14680068 | tf_op jit(solution)/shard_map/dot_general | solution.py:427
  91.2 4.9 %collective-permute-done.19 = bf16[64,8192]{1,0:T(8,128)(2,1)S(1)} collective-permute-done((bf16[64,8192]{1,0:T(8,128)(2,1)S(1)}, bf16[64,8192]{1,0:T(8,128)(2,1)S(1)}, u32[]{:S(2)}, u32[]{:S(2)}) %collective-permute-start.19) | collective-permute-done | bytes 1048608 | tf_op jit(solution)/shard_map/ppermute | solution.py:51
  96.1 1.3 multiply_convert_fusion.3
  97.3 2.4 %collective-permute-start.21 = (bf16[512,1024]{1,0:T(8,128)(2,1)S(1)}, bf16[512,1024]{1,0:T(8,128)(2,1)S(1)}, u32[]{:S(2)}, u32[]{:S(2)}) collective-permute-start(bf16[512,1024]{1,0:T(8,128)(2,1)S(1)} %multiply_convert_fusion.3), channel_id=1, source_target_pairs={{0,1},{8,11},{4,5},{12,15},{16,17},{24,27},{20,21},{28,31},{32,33}... | collective-permute-start | bytes 3145736 | tf_op jit(solution)/shard_map/ppermute | solution.py:51
  99.8 1.2 collective-permute-start.20
  101.0 2.3 %multiply_convert_fusion = bf16[512,1024]{1,0:T(8,128)(2,1)} fusion(bf16[1024,512]{1,0:T(8,128)(2,1)S(1)} %get-tuple-element.89, bf16[1024,4096]{1,0:T(8,128)(2,1)S(1)} %bitcast.18, s32[]{:T(128)S(6)} %select_n.87), kind=kOutput, calls=%fused_computation.5 | convolution fusion | flops 1074790400 | bytes 4194308 | tf_op jit(solution)/shard_map/dot_general | solution.py:147
  103.4 1.3 multiply_convert_fusion.1
  104.6 1.3 multiply_convert_fusion.2
  107.2 3.2 %collective-permute-start.22 = (bf16[64,8192]{1,0:T(8,128)(2,1)S(1)}, bf16[64,8192]{1,0:T(8,128)(2,1)S(1)}, u32[]{:S(2)}, u32[]{:S(2)}) collective-permute-start(bf16[64,8192]{1,0:T(8,128)(2,1)S(1)} %get-tuple-element.100), channel_id=1, source_target_pairs={{0,32},{8,104},{4,36},{12,108},{16,48},{24,120},{20,52},{28,124},{... | collective-permute-start | bytes 3145736 | tf_op jit(solution)/shard_map/ppermute | solution.py:51
  112.8 2.6 %collective-permute-start.25 = (bf16[512,1024]{1,0:T(8,128)(2,1)S(1)}, bf16[512,1024]{1,0:T(8,128)(2,1)S(1)}, u32[]{:S(2)}, u32[]{:S(2)}) collective-permute-start(bf16[512,1024]{1,0:T(8,128)(2,1)S(1)} %add_convert_fusion.1), channel_id=1, source_target_pairs={{0,1},{8,11},{4,5},{12,15},{16,17},{24,27},{20,21},{28,31},{32,33}... | collective-permute-start | bytes 3145736 | tf_op jit(solution)/shard_map/ppermute | solution.py:51
  115.6 9.5 %backward_ends.1 = (bf16[512,512]{1,0:T(8,128)(2,1)}, f32[4,512,128]{2,1,0:T(8,128)S(1)}, f32[56,512]{1,0:T(8,128)S(1)}, f32[4,128,128]{2,1,0:T(8,128)S(1)}) custom-call(f32[512,512]{1,0:T(8,128)S(1)} %convert_add_fusion.1.grad_ref, bf16[512,512]{1,0:T(8,128)(2,1)S(1)} %copy-done.5, f32[4,512,128]{2,1,0:T(8,128)S(1)} %copy-done.8, ...), custom_call_target="tpu_custom_call" | custom-call | flops 115000000 | tf_op jit(solution)/shard_map/backward_ends/pallas_call | solution.py:357
  125.1 6.9 %collective-permute-done.22 = bf16[64,8192]{1,0:T(8,128)(2,1)S(1)} collective-permute-done((bf16[64,8192]{1,0:T(8,128)(2,1)S(1)}, bf16[64,8192]{1,0:T(8,128)(2,1)S(1)}, u32[]{:S(2)}, u32[]{:S(2)}) %collective-permute-start.22) | collective-permute-done | bytes 1048608 | tf_op jit(solution)/shard_map/ppermute | solution.py:51
  132.0 3.2 %collective-permute-done.23 = bf16[64,8192]{1,0:T(8,128)(2,1)S(1)} collective-permute-done((bf16[64,8192]{1,0:T(8,128)(2,1)S(1)}, bf16[64,8192]{1,0:T(8,128)(2,1)S(1)}, u32[]{:S(2)}, u32[]{:S(2)}) %collective-permute-start.23) | collective-permute-done | bytes 1048608 | tf_op jit(solution)/shard_map/ppermute | solution.py:51
  135.4 6.1 %collective-permute-done.26 = bf16[512,1024]{1,0:T(8,128)(2,1)S(1)} collective-permute-done((bf16[512,1024]{1,0:T(8,128)(2,1)S(1)}, bf16[512,1024]{1,0:T(8,128)(2,1)S(1)}, u32[]{:S(2)}, u32[]{:S(2)}) %collective-permute-start.26) | collective-permute-done | bytes 1048608 | tf_op jit(solution)/shard_map/ppermute | solution.py:51
  143.0 3.5 %collective-permute-start.27 = (bf16[32,8192]{1,0:T(8,128)(2,1)S(1)}, bf16[32,8192]{1,0:T(8,128)(2,1)}, u32[]{:S(2)}, u32[]{:S(2)}) collective-permute-start(bf16[32,8192]{1,0:T(8,128)(2,1)S(1)} %slice.49), channel_id=1, source_target_pairs={{0,16},{8,28},{4,20},{12,8},{16,0},{24,12},{20,4},{28,24},{32,48},... | collective-permute-start | bytes 1572872 | tf_op jit(solution)/shard_map/ppermute | solution.py:51
  147.0 2.2 %collective-permute-start.30 = (f32[72,512]{1,0:T(8,128)S(1)}, f32[72,512]{1,0:T(8,128)S(1)}, u32[]{:S(2)}, u32[]{:S(2)}) collective-permute-start(f32[72,512]{1,0:T(8,128)S(1)} %pad_maximum_fusion.1.refs_7_), channel_id=1, source_target_pairs={{0,3},{8,11},{4,7},{12,15},{16,19},{24,27},{20,23},{28,31},{32,35}... | collective-permute-start | bytes 442376 | tf_op jit(solution)/shard_map/ppermute | solution.py:51
  149.2 4.1 %collective-permute-done.28.refs_8_ = f32[72,512]{1,0:T(8,128)S(1)} collective-permute-done((f32[72,512]{1,0:T(8,128)S(1)}, f32[72,512]{1,0:T(8,128)S(1)}, u32[]{:S(2)}, u32[]{:S(2)}) %collective-permute-start.28) | collective-permute-done | bytes 147488 | tf_op jit(solution)/shard_map/ppermute | solution.py:51
  154.6 3.6 %collective-permute-done.27 = bf16[32,8192]{1,0:T(8,128)(2,1)} collective-permute-done((bf16[32,8192]{1,0:T(8,128)(2,1)S(1)}, bf16[32,8192]{1,0:T(8,128)(2,1)}, u32[]{:S(2)}, u32[]{:S(2)}) %collective-permute-start.27) | collective-permute-done | bytes 524320 | tf_op jit(solution)/shard_map/ppermute | solution.py:51
  158.2 5.1 %collective-permute-start.31 = (bf16[32,8192]{1,0:T(8,128)(2,1)}, bf16[32,8192]{1,0:T(8,128)(2,1)}, u32[]{:S(2)}, u32[]{:S(2)}) collective-permute-start(bf16[32,8192]{1,0:T(8,128)(2,1)} %collective-permute-done.27), channel_id=1, source_target_pairs={{8,28},{12,8},{24,12},{28,24},{40,60},{44,40},{56,44},{60,56},{72,... | collective-permute-start | bytes 1572872 | tf_op jit(solution)/shard_map/ppermute | solution.py:51
  163.3 3.5 %add_convert_fusion = bf16[512,1024]{1,0:T(8,128)(2,1)} fusion(bf16[512,1024]{1,0:T(8,128)(2,1)} %copy-done.26, bf16[512,1024]{1,0:T(8,128)(2,1)} %copy-done.25, bf16[512,1024]{1,0:T(8,128)(2,1)} %multiply_convert_fusion), kind=kLoop, calls=%fused_computation.2 | loop fusion | flops 3145728 | bytes 4194304 | tf_op jit(solution)/shard_map/convert_element_type | solution.py:468
  166.8 5.0 %backward_full.1 = (bf16[512,512]{1,0:T(8,128)(2,1)}, bf16[512,512]{1,0:T(8,128)(2,1)}, f32[16,512]{1,0:T(8,128)}, f32[16,512]{1,0:T(8,128)}, f32[8,512]{1,0:T(8,128)S(1)}) custom-call(bf16[512,512]{1,0:T(8,128)(2,1)S(1)} %copy-done.2, bf16[512,512]{1,0:T(8,128)(2,1)S(1)} %copy-done.3, f32[4,512,128]{2,1,0:T(8,128)S(1)} %get-tuple-element.112.refs_2_, ...), custom_call_target="tpu_custom_call" | custom-call | flops 115000000 | tf_op jit(solution)/shard_map/backward_full/pallas_call | solution.py:357
  172.4 2.0 %fusion.18 = bf16[32,8192]{1,0:T(8,128)(2,1)} fusion(f32[64,8192]{1,0:T(8,128)S(1)} %copy-done.24, bf16[32,8192]{1,0:T(8,128)(2,1)} %collective-permute-done.27, bf16[32,8192]{1,0:T(8,128)(2,1)} %collective-permute-done.31, pred[]{:T(512)S(6)} %eq.13), kind=kLoop, calls=%fused_computation.22 | loop fusion | flops 1048576 | bytes 2621441 | tf_op jit(solution)/shard_map/convert_element_type | solution.py:467
  (101 shorter events, 17.1 us)
Async XLA Ops:
  1.7 10.6 %collective-permute-start = (bf16[32,4096]{1,0:T(8,128)(2,1)S(1)}, bf16[32,4096]{1,0:T(8,128)(2,1)S(1)}, u32[]{:S(2)}, u32[]{:S(2)}) collective-permute-start(bf16[32,4096]{1,0:T(8,128)(2,1)S(1)} %get-tuple-element.124), channel_id=1, source_target_pairs={{0,16},{8,24},{4,20},{12,28},{16,0},{24,8},{20,4},{28,12},{32,48},... | collective-permute-start | bytes 786440 | tf_op jit(solution)/shard_map/ppermute | solution.py:51
  6.2 12.4 %collective-permute-start.1 = (bf16[32,4096]{1,0:T(8,128)(2,1)S(1)}, bf16[32,4096]{1,0:T(8,128)(2,1)S(1)}, u32[]{:S(2)}, u32[]{:S(2)}) collective-permute-start(bf16[32,4096]{1,0:T(8,128)(2,1)S(1)} %get-tuple-element.125), channel_id=1, source_target_pairs={{0,4},{8,12},{4,16},{12,24},{16,20},{24,28},{20,0},{28,8},{32,36},... | collective-permute-start | bytes 786440 | tf_op jit(solution)/shard_map/ppermute | solution.py:51
  7.0 11.6 %collective-permute-start.2 = (bf16[32,4096]{1,0:T(8,128)(2,1)S(1)}, bf16[32,4096]{1,0:T(8,128)(2,1)S(1)}, u32[]{:S(2)}, u32[]{:S(2)}) collective-permute-start(bf16[32,4096]{1,0:T(8,128)(2,1)S(1)} %get-tuple-element.125), channel_id=1, source_target_pairs={{0,20},{8,28},{4,0},{12,8},{16,4},{24,12},{20,16},{28,24},{32,52},... | collective-permute-start | bytes 786440 | tf_op jit(solution)/shard_map/ppermute | solution.py:51
  12.4 9.3 %copy-start.2 = (bf16[512,512]{1,0:T(8,128)(2,1)S(1)}, bf16[512,512]{1,0:T(8,128)(2,1)}, u32[]{:S(2)}) copy-start(bf16[512,512]{1,0:T(8,128)(2,1)} %refs_0_.3) | copy-start | bytes 1572868
  12.4 9.3 %copy-start.3 = (bf16[512,512]{1,0:T(8,128)(2,1)S(1)}, bf16[512,512]{1,0:T(8,128)(2,1)}, u32[]{:S(2)}) copy-start(bf16[512,512]{1,0:T(8,128)(2,1)} %refs_1_.1) | copy-start | bytes 1572868
  12.4 9.3 %copy-start.9 = (f32[16,512]{1,0:T(8,128)S(1)}, f32[16,512]{1,0:T(8,128)}, u32[]{:S(2)}) copy-start(f32[16,512]{1,0:T(8,128)} %refs_4_.3) | copy-start | bytes 98308
  12.4 16.4 %collective-permute-start.4 = (bf16[1,2,32,4096]{3,2,1,0:T(8,128)(2,1)S(1)}, bf16[1,2,32,4096]{3,2,1,0:T(8,128)(2,1)}, u32[]{:S(2)}, u32[]{:S(2)}) collective-permute-start(bf16[1,2,32,4096]{3,2,1,0:T(8,128)(2,1)S(1)} %maximum_select_fusion), channel_id=1, source_target_pairs={{0,96},{8,40},{4,100},{12,44},{16,112},{24,56},{20,116},{28,60},{3... | collective-permute-start | bytes 1572872 | tf_op jit(solution)/shard_map/ppermute | solution.py:51
  18.7 19.5 %copy-start.4 = (bf16[512,512]{1,0:T(8,128)(2,1)S(1)}, bf16[512,512]{1,0:T(8,128)(2,1)}, u32[]{:S(2)}) copy-start(bf16[512,512]{1,0:T(8,128)(2,1)} %query_ref.1) | copy-start | bytes 1572868
  18.7 19.5 %copy-start.18 = (f32[16,512]{1,0:T(8,128)S(1)}, f32[16,512]{1,0:T(8,128)}, u32[]{:S(2)}) copy-start(f32[16,512]{1,0:T(8,128)} %refs_5_.1) | copy-start | bytes 98308
  18.7 19.5 %copy-start.19 = (f32[512]{0:T(512)S(1)}, f32[512]{0:T(512)}, u32[]{:S(2)}) copy-start(f32[512]{0:T(512)} %param.11) | copy-start | bytes 6148
  18.9 27.0 %collective-permute-start.3 = (bf16[2,2,32,4096]{3,2,1,0:T(8,128)(2,1)S(1)}, bf16[2,2,32,4096]{3,2,1,0:T(8,128)(2,1)}, u32[]{:S(2)}, u32[]{:S(2)}) collective-permute-start(bf16[2,2,32,4096]{3,2,1,0:T(8,128)(2,1)S(1)} %pad_maximum_fusion.refs_2_), channel_id=1, source_target_pairs={{0,32},{8,104},{4,36},{12,108},{16,48},{24,120},{20,52},{28,124},{... | collective-permute-start | bytes 3145736 | tf_op jit(solution)/shard_map/ppermute | solution.py:51
  24.9 3.8 %collective-permute-start.5 = (f32[32,512]{1,0:T(8,128)S(1)}, f32[32,512]{1,0:T(8,128)S(1)}, u32[]{:S(2)}, u32[]{:S(2)}) collective-permute-start(f32[32,512]{1,0:T(8,128)S(1)} %get-tuple-element.65), channel_id=1, source_target_pairs={{0,4},{8,12},{4,0},{12,8},{16,20},{24,28},{20,16},{28,24},{32,36},... | collective-permute-start | bytes 196616 | tf_op jit(solution)/shard_map/ppermute | solution.py:51
  28.8 5.6 %collective-permute-start.7 = (f32[64,512]{1,0:T(8,128)S(1)}, f32[64,512]{1,0:T(8,128)S(1)}, u32[]{:S(2)}, u32[]{:S(2)}) collective-permute-start(f32[64,512]{1,0:T(8,128)S(1)} %pad_maximum_fusion.2.refs_6_), channel_id=1, source_target_pairs={{0,1},{8,9},{4,5},{12,13},{16,17},{24,25},{20,21},{28,29},{32,33},... | collective-permute-start | bytes 393224 | tf_op jit(solution)/shard_map/ppermute | solution.py:51
  30.1 8.1 %collective-permute-start.8 = (f32[64,512]{1,0:T(8,128)S(1)}, f32[64,512]{1,0:T(8,128)S(1)}, u32[]{:S(2)}, u32[]{:S(2)}) collective-permute-start(f32[64,512]{1,0:T(8,128)S(1)} %pad_maximum_fusion.2.refs_6_), channel_id=1, source_target_pairs={{0,2},{8,10},{4,6},{12,14},{16,18},{24,26},{20,22},{28,30},{32,34}... | collective-permute-start | bytes 393224 | tf_op jit(solution)/shard_map/ppermute | solution.py:51
  32.5 5.6 %collective-permute-start.9 = (f32[64,512]{1,0:T(8,128)S(1)}, f32[64,512]{1,0:T(8,128)S(1)}, u32[]{:S(2)}, u32[]{:S(2)}) collective-permute-start(f32[64,512]{1,0:T(8,128)S(1)} %pad_maximum_fusion.2.refs_6_), channel_id=1, source_target_pairs={{0,3},{8,11},{4,7},{12,15},{16,19},{24,27},{20,23},{28,31},{32,35}... | collective-permute-start | bytes 393224 | tf_op jit(solution)/shard_map/ppermute | solution.py:51
  33.7 12.2 %collective-permute-start.6 = (bf16[1,2,32,4096]{3,2,1,0:T(8,128)(2,1)S(1)}, bf16[1,2,32,4096]{3,2,1,0:T(8,128)(2,1)S(1)}, u32[]{:S(2)}, u32[]{:S(2)}) collective-permute-start(bf16[1,2,32,4096]{3,2,1,0:T(8,128)(2,1)S(1)} %maximum_select_fusion.1), channel_id=1, source_target_pairs={{0,96},{8,40},{4,100},{12,44},{16,112},{24,56},{20,116},{28,60},{3... | collective-permute-start | bytes 1572872 | tf_op jit(solution)/shard_map/ppermute | solution.py:51
  43.8 11.8 %collective-permute-start.10 = (bf16[512,512]{1,0:T(8,128)(2,1)S(1)}, bf16[512,512]{1,0:T(8,128)(2,1)S(1)}, u32[]{:S(2)}, u32[]{:S(2)}) collective-permute-start(bf16[512,512]{1,0:T(8,128)(2,1)S(1)} %get-tuple-element.72.refs_0_), channel_id=1, source_target_pairs={{0,4},{8,12},{4,0},{12,8},{16,20},{24,28},{20,16},{28,24},{32,36},... | collective-permute-start | bytes 1572872 | tf_op jit(solution)/shard_map/ppermute | solution.py:51
  45.9 10.4 %copy-start.10 = (bf16[1,2,32,4096]{3,2,1,0:T(8,128)(2,1)}, bf16[1,2,32,4096]{3,2,1,0:T(8,128)(2,1)S(1)}, u32[]{:S(2)}) copy-start(bf16[1,2,32,4096]{3,2,1,0:T(8,128)(2,1)S(1)} %collective-permute-done.6.refs_8_) | copy-start | bytes 1572868
  56.4 18.3 %collective-permute-start.12 = (bf16[2,2,32,4096]{3,2,1,0:T(8,128)(2,1)}, bf16[2,2,32,4096]{3,2,1,0:T(8,128)(2,1)}, u32[]{:S(2)}, u32[]{:S(2)}) collective-permute-start(bf16[2,2,32,4096]{3,2,1,0:T(8,128)(2,1)} %collective-permute-done.3.refs_4_), channel_id=1, source_target_pairs={{0,32},{8,104},{4,36},{12,108},{16,48},{24,120},{20,52},{28,124},{... | collective-permute-start | bytes 3145736 | tf_op jit(solution)/shard_map/ppermute | solution.py:51
  71.5 5.2 %collective-permute-start.11 = (bf16[64,8192]{1,0:T(8,128)(2,1)}, bf16[64,8192]{1,0:T(8,128)(2,1)}, u32[]{:S(2)}, u32[]{:S(2)}) collective-permute-start(bf16[64,8192]{1,0:T(8,128)(2,1)} %get-tuple-element.75), channel_id=1, source_target_pairs={{0,8},{8,0},{4,12},{12,4},{16,24},{24,16},{20,28},{28,20},{32,40},... | collective-permute-start | bytes 3145736 | tf_op jit(solution)/shard_map/ppermute | solution.py:51
  74.1 4.9 %collective-permute-start.16 = (bf16[1,2,32,4096]{3,2,1,0:T(8,128)(2,1)}, bf16[1,2,32,4096]{3,2,1,0:T(8,128)(2,1)}, u32[]{:S(2)}, u32[]{:S(2)}) collective-permute-start(bf16[1,2,32,4096]{3,2,1,0:T(8,128)(2,1)} %collective-permute-done.4.refs_6_), channel_id=1, source_target_pairs={{0,8},{8,0},{4,12},{12,4},{16,24},{24,16},{20,28},{28,20},{32,40},... | collective-permute-start | bytes 1572872 | tf_op jit(solution)/shard_map/ppermute | solution.py:51
  74.1 10.3 %copy-start.11 = (bf16[1,2,32,4096]{3,2,1,0:T(8,128)(2,1)S(1)}, bf16[1,2,32,4096]{3,2,1,0:T(8,128)(2,1)}, u32[]{:S(2)}) copy-start(bf16[1,2,32,4096]{3,2,1,0:T(8,128)(2,1)} %copy-done.10) | copy-start | bytes 1572868
  74.1 10.3 %copy-start.13 = (bf16[512,512]{1,0:T(8,128)(2,1)S(1)}, bf16[512,512]{1,0:T(8,128)(2,1)}, u32[]{:S(2)}) copy-start(bf16[512,512]{1,0:T(8,128)(2,1)} %copy-done.12) | copy-start | bytes 1572868
  74.1 10.3 %copy-start.15 = (bf16[512,512]{1,0:T(8,128)(2,1)S(1)}, bf16[512,512]{1,0:T(8,128)(2,1)}, u32[]{:S(2)}) copy-start(bf16[512,512]{1,0:T(8,128)(2,1)} %copy-done.14) | copy-start | bytes 1572868
  74.1 10.2 %collective-permute-start.14 = (bf16[2,2,32,4096]{3,2,1,0:T(8,128)(2,1)S(1)}, bf16[2,2,32,4096]{3,2,1,0:T(8,128)(2,1)S(1)}, u32[]{:S(2)}, u32[]{:S(2)}) collective-permute-start(bf16[2,2,32,4096]{3,2,1,0:T(8,128)(2,1)S(1)} %pad_maximum_fusion.refs_2_), channel_id=1, source_target_pairs={{0,8},{8,0},{4,12},{12,4},{16,24},{24,16},{20,28},{28,20},{32,40},... | collective-permute-start | bytes 3145736 | tf_op jit(solution)/shard_map/ppermute | solution.py:51
  74.6 9.7 %collective-permute-start.15 = (bf16[2,2,32,4096]{3,2,1,0:T(8,128)(2,1)}, bf16[2,2,32,4096]{3,2,1,0:T(8,128)(2,1)S(1)}, u32[]{:S(2)}, u32[]{:S(2)}) collective-permute-start(bf16[2,2,32,4096]{3,2,1,0:T(8,128)(2,1)} %collective-permute-done.3.refs_4_), channel_id=1, source_target_pairs={{0,8},{8,0},{4,12},{12,4},{16,24},{24,16},{20,28},{28,20},{32,40},... | collective-permute-start | bytes 3145736 | tf_op jit(solution)/shard_map/ppermute | solution.py:51
  74.7 6.4 %collective-permute-start.17 = (bf16[1,2,32,4096]{3,2,1,0:T(8,128)(2,1)}, bf16[1,2,32,4096]{3,2,1,0:T(8,128)(2,1)S(1)}, u32[]{:S(2)}, u32[]{:S(2)}) collective-permute-start(bf16[1,2,32,4096]{3,2,1,0:T(8,128)(2,1)} %copy-done.10), channel_id=1, source_target_pairs={{0,8},{8,0},{4,12},{12,4},{16,24},{24,16},{20,28},{28,20},{32,40},... | collective-permute-start | bytes 1572872 | tf_op jit(solution)/shard_map/ppermute | solution.py:51
  76.7 7.6 %collective-permute-start.18 = (bf16[2,2,32,4096]{3,2,1,0:T(8,128)(2,1)}, bf16[2,2,32,4096]{3,2,1,0:T(8,128)(2,1)S(1)}, u32[]{:S(2)}, u32[]{:S(2)}) collective-permute-start(bf16[2,2,32,4096]{3,2,1,0:T(8,128)(2,1)} %collective-permute-done.12.refs_10_), channel_id=1, source_target_pairs={{0,8},{8,0},{4,12},{12,4},{16,24},{24,16},{20,28},{28,20},{32,40},... | collective-permute-start | bytes 3145736 | tf_op jit(solution)/shard_map/ppermute | solution.py:51
  78.9 27.0 %collective-permute-start.13 = (bf16[192,8192]{1,0:T(8,128)(2,1)}, bf16[192,8192]{1,0:T(8,128)(2,1)S(1)}, u32[]{:S(2)}, u32[]{:S(2)}) collective-permute-start(bf16[192,8192]{1,0:T(8,128)(2,1)} %copy-done.22), channel_id=1, source_target_pairs={{0,8},{8,0},{4,12},{12,4},{16,24},{24,16},{20,28},{28,20},{32,40},... | collective-permute-start | bytes 9437192 | tf_op jit(solution)/shard_map/ppermute | solution.py:51
  81.1 5.5 %copy-start.21 = (bf16[512,8192]{1,0:T(8,128)(2,1)S(1)}, bf16[512,8192]{1,0:T(8,128)(2,1)}, u32[]{:S(2)}) copy-start(bf16[512,8192]{1,0:T(8,128)(2,1)} %weight_ref.1) | copy-start | bytes 25165828
  81.1 14.9 %collective-permute-start.19 = (bf16[64,8192]{1,0:T(8,128)(2,1)S(1)}, bf16[64,8192]{1,0:T(8,128)(2,1)S(1)}, u32[]{:S(2)}, u32[]{:S(2)}) collective-permute-start(bf16[64,8192]{1,0:T(8,128)(2,1)S(1)} %add_convert_fusion.4), channel_id=1, source_target_pairs={{0,32},{8,104},{4,36},{12,108},{16,48},{24,120},{20,52},{28,124},{... | collective-permute-start | bytes 3145736 | tf_op jit(solution)/shard_map/ppermute | solution.py:51
  97.3 14.2 %collective-permute-start.21 = (bf16[512,1024]{1,0:T(8,128)(2,1)S(1)}, bf16[512,1024]{1,0:T(8,128)(2,1)S(1)}, u32[]{:S(2)}, u32[]{:S(2)}) collective-permute-start(bf16[512,1024]{1,0:T(8,128)(2,1)S(1)} %multiply_convert_fusion.3), channel_id=1, source_target_pairs={{0,1},{8,11},{4,5},{12,15},{16,17},{24,27},{20,21},{28,31},{32,33}... | collective-permute-start | bytes 3145736 | tf_op jit(solution)/shard_map/ppermute | solution.py:51
  99.8 13.0 %collective-permute-start.20 = (bf16[512,512]{1,0:T(8,128)(2,1)S(1)}, bf16[512,512]{1,0:T(8,128)(2,1)S(1)}, u32[]{:S(2)}, u32[]{:S(2)}) collective-permute-start(bf16[512,512]{1,0:T(8,128)(2,1)S(1)} %slice.50), channel_id=1, source_target_pairs={{0,4},{8,12},{4,0},{12,8},{16,20},{24,28},{20,16},{28,24},{32,36},... | collective-permute-start | bytes 1572872 | tf_op jit(solution)/shard_map/ppermute | solution.py:51
  107.2 24.8 %collective-permute-start.22 = (bf16[64,8192]{1,0:T(8,128)(2,1)S(1)}, bf16[64,8192]{1,0:T(8,128)(2,1)S(1)}, u32[]{:S(2)}, u32[]{:S(2)}) collective-permute-start(bf16[64,8192]{1,0:T(8,128)(2,1)S(1)} %get-tuple-element.100), channel_id=1, source_target_pairs={{0,32},{8,104},{4,36},{12,108},{16,48},{24,120},{20,52},{28,124},{... | collective-permute-start | bytes 3145736 | tf_op jit(solution)/shard_map/ppermute | solution.py:51
  110.4 24.8 %collective-permute-start.23 = (bf16[64,8192]{1,0:T(8,128)(2,1)S(1)}, bf16[64,8192]{1,0:T(8,128)(2,1)S(1)}, u32[]{:S(2)}, u32[]{:S(2)}) collective-permute-start(bf16[64,8192]{1,0:T(8,128)(2,1)S(1)} %get-tuple-element.101), channel_id=1, source_target_pairs={{0,96},{8,40},{4,100},{12,44},{16,112},{24,56},{20,116},{28,60},{3... | collective-permute-start | bytes 3145736 | tf_op jit(solution)/shard_map/ppermute | solution.py:51
  111.9 3.7 %copy-start.5 = (bf16[512,512]{1,0:T(8,128)(2,1)S(1)}, bf16[512,512]{1,0:T(8,128)(2,1)}, u32[]{:S(2)}) copy-start(bf16[512,512]{1,0:T(8,128)(2,1)} %query_ref.1) | copy-start | bytes 1572868
  111.9 3.7 %copy-start.8 = (f32[4,512,128]{2,1,0:T(8,128)S(1)}, f32[4,512,128]{2,1,0:T(8,128)}, u32[]{:S(2)}) copy-start(f32[4,512,128]{2,1,0:T(8,128)} %copy-done.7) | copy-start | bytes 3145732
  112.8 22.6 %collective-permute-start.25 = (bf16[512,1024]{1,0:T(8,128)(2,1)S(1)}, bf16[512,1024]{1,0:T(8,128)(2,1)S(1)}, u32[]{:S(2)}, u32[]{:S(2)}) collective-permute-start(bf16[512,1024]{1,0:T(8,128)(2,1)S(1)} %add_convert_fusion.1), channel_id=1, source_target_pairs={{0,1},{8,11},{4,5},{12,15},{16,17},{24,27},{20,21},{28,31},{32,33}... | collective-permute-start | bytes 3145736 | tf_op jit(solution)/shard_map/ppermute | solution.py:51
  115.4 26.0 %collective-permute-start.26 = (bf16[512,1024]{1,0:T(8,128)(2,1)S(1)}, bf16[512,1024]{1,0:T(8,128)(2,1)S(1)}, u32[]{:S(2)}, u32[]{:S(2)}) collective-permute-start(bf16[512,1024]{1,0:T(8,128)(2,1)S(1)} %multiply_convert_fusion.1), channel_id=1, source_target_pairs={{0,3},{8,9},{4,7},{12,13},{16,19},{24,25},{20,23},{28,29},{32,35},... | collective-permute-start | bytes 3145736 | tf_op jit(solution)/shard_map/ppermute | solution.py:51
  135.2 7.2 %collective-permute-start.24 = (f32[56,512]{1,0:T(8,128)S(1)}, f32[56,512]{1,0:T(8,128)S(1)}, u32[]{:S(2)}, u32[]{:S(2)}) collective-permute-start(f32[56,512]{1,0:T(8,128)S(1)} %get-tuple-element.102), channel_id=1, source_target_pairs={{0,4},{8,12},{4,0},{12,8},{16,20},{24,28},{20,16},{28,24},{32,36},... | collective-permute-start | bytes 344072 | tf_op jit(solution)/shard_map/ppermute | solution.py:51
  135.4 6.1 %copy-start.25 = (bf16[512,1024]{1,0:T(8,128)(2,1)}, bf16[512,1024]{1,0:T(8,128)(2,1)S(1)}, u32[]{:S(2)}) copy-start(bf16[512,1024]{1,0:T(8,128)(2,1)S(1)} %collective-permute-done.25) | copy-start | bytes 3145732
  142.9 11.7 %copy-start.23 = (f32[64,8192]{1,0:T(8,128)}, f32[64,8192]{1,0:T(8,128)S(1)}, u32[]{:S(2)}) copy-start(f32[64,8192]{1,0:T(8,128)S(1)} %convert_add_fusion) | copy-start | bytes 6291460
  143.0 15.2 %collective-permute-start.27 = (bf16[32,8192]{1,0:T(8,128)(2,1)S(1)}, bf16[32,8192]{1,0:T(8,128)(2,1)}, u32[]{:S(2)}, u32[]{:S(2)}) collective-permute-start(bf16[32,8192]{1,0:T(8,128)(2,1)S(1)} %slice.49), channel_id=1, source_target_pairs={{0,16},{8,28},{4,20},{12,8},{16,0},{24,12},{20,4},{28,24},{32,48},... | collective-permute-start | bytes 1572872 | tf_op jit(solution)/shard_map/ppermute | solution.py:51
  146.5 6.9 %collective-permute-start.28 = (f32[72,512]{1,0:T(8,128)S(1)}, f32[72,512]{1,0:T(8,128)S(1)}, u32[]{:S(2)}, u32[]{:S(2)}) collective-permute-start(f32[72,512]{1,0:T(8,128)S(1)} %pad_maximum_fusion.1.refs_7_), channel_id=1, source_target_pairs={{0,1},{8,9},{4,5},{12,13},{16,17},{24,25},{20,21},{28,29},{32,33},... | collective-permute-start | bytes 442376 | tf_op jit(solution)/shard_map/ppermute | solution.py:51
  146.6 7.6 %collective-permute-start.29 = (f32[72,512]{1,0:T(8,128)S(1)}, f32[72,512]{1,0:T(8,128)S(1)}, u32[]{:S(2)}, u32[]{:S(2)}) collective-permute-start(f32[72,512]{1,0:T(8,128)S(1)} %pad_maximum_fusion.1.refs_7_), channel_id=1, source_target_pairs={{0,2},{8,10},{4,6},{12,14},{16,18},{24,26},{20,22},{28,30},{32,34}... | collective-permute-start | bytes 442376 | tf_op jit(solution)/shard_map/ppermute | solution.py:51
  147.0 7.6 %collective-permute-start.30 = (f32[72,512]{1,0:T(8,128)S(1)}, f32[72,512]{1,0:T(8,128)S(1)}, u32[]{:S(2)}, u32[]{:S(2)}) collective-permute-start(f32[72,512]{1,0:T(8,128)S(1)} %pad_maximum_fusion.1.refs_7_), channel_id=1, source_target_pairs={{0,3},{8,11},{4,7},{12,15},{16,19},{24,27},{20,23},{28,31},{32,35}... | collective-permute-start | bytes 442376 | tf_op jit(solution)/shard_map/ppermute | solution.py:51
  158.2 14.2 %collective-permute-start.31 = (bf16[32,8192]{1,0:T(8,128)(2,1)}, bf16[32,8192]{1,0:T(8,128)(2,1)}, u32[]{:S(2)}, u32[]{:S(2)}) collective-permute-start(bf16[32,8192]{1,0:T(8,128)(2,1)} %collective-permute-done.27), channel_id=1, source_target_pairs={{8,28},{12,8},{24,12},{28,24},{40,60},{44,40},{56,44},{60,56},{72,... | collective-permute-start | bytes 1572872 | tf_op jit(solution)/shard_map/ppermute | solution.py:51
  166.8 5.6 %copy-start.24 = (f32[64,8192]{1,0:T(8,128)S(1)}, f32[64,8192]{1,0:T(8,128)}, u32[]{:S(2)}) copy-start(f32[64,8192]{1,0:T(8,128)} %copy-done.23) | copy-start | bytes 6291460
  (11 other events, 17.6 us)

commit v11 on v3

--- a/solution.py
+++ b/solution.py
@@ -143,7 +143,7 @@
             return now, lag
 
         zero = [zero_ref[...]] * modes
-        now, lag = lax.fori_loop(0, span, step, (zero, zero), unroll=4)
+        now, lag = lax.fori_loop(0, span, step, (zero, zero), unroll=8)
         for m in range(modes):
             sub_ref[tile, strided(m, modes)] = now[m]
             sub_ref[tile, strided(SUBS * modes + m, modes)] = lag[m]
@@ -193,7 +193,7 @@
             return now
 
         first = [lead_ref[tile, strided(m, modes)] for m in range(modes)]
-        lax.fori_loop(0, span, step, first, unroll=4)
+        lax.fori_loop(0, span, step, first, unroll=8)
         gated_ref[:, lanes] = (query_ref[:, lanes].astype(F32) * pre_ref[tile]).astype(BF16)
     part = length // (RING * 4)
     y, high, core, _, _ = places()
@@ -225,7 +225,7 @@
             return [decay[m] * now[m] + g for m in range(modes)]
 
         zero = [zero_ref[...]] * modes
-        now = lax.fori_loop(0, span, back_step, zero, unroll=4)
+        now = lax.fori_loop(0, span, back_step, zero, unroll=8)
         for m in range(modes):
             sub_ref[tile, strided(m, modes)] = now[m]
         for low in range(0, modes, half):
@@ -247,7 +247,7 @@
             lag = [lead_ref[tile, strided(SUBS * modes + m, modes)] for m in group]
             zero = [zero_ref[...]] * half
             state, lag, pair, lag_pair, skip = lax.fori_loop(
-                0, span, pair_step, (state, lag, zero, zero, zero[0]), unroll=4
+                0, span, pair_step, (state, lag, zero, zero, zero[0]), unroll=8
             )
             for m in range(half):
                 part_ref[tile, strided(low + m, modes)] = pair[m]
@@ -306,7 +306,7 @@
             return now
 
         first = [lead_ref[tile, strided(m, modes)] for m in range(modes)]
-        lax.fori_loop(0, span, step, first, unroll=4)
+        lax.fori_loop(0, span, step, first, unroll=8)
         drive_grad = drive_grad_ref[tile]
         grad_key_ref[:, lanes] = (drive_grad * value_ref[:, lanes].astype(F32)).astype(BF16)
         grad_value_ref[:, lanes] = (drive_grad * key_ref[:, lanes].astype(F32)).astype(BF16)
@@ -389,8 +389,11 @@
     weights = {2: weigh(gated_pair, cot_rows, scale, 2)}
     cot_rows, weights[2] = together(cot_rows, weights[2])
     grad_parts = lax.dot_general(cot_rows, low_weight, (((1,), (1,)), ((), ())), preferred_element_type=F32)
-    cot_rows, grad_parts, got_rest = together(cot_rows, grad_parts, got_rest)
+    cot_rows, grad_parts = together(cot_rows, grad_parts)
     theirs = hop(grad_parts[length:].astype(BF16), pair=1)
+    for r in (1, 3, 0):
+        weights[r] = weigh(gated_pair, cot_rows, scale, r)
+    got_rest, _ = together(got_rest, theirs)
     part = opposite.shape[0] // 2
     low_sum, high_sum = hop(opposite[:part], y=1), hop(opposite[part:], y=-1)
     above, below, own = (
@@ -398,8 +401,6 @@
     )
     above = jnp.concatenate([add(above[:part], low_sum), above[part:]]).astype(BF16)
     below = jnp.concatenate([below[:part], add(below[part:], high_sum)]).astype(BF16)
-    for r in (1, 3, 0):
-        weights[r] = weigh(gated_pair, cot_rows, scale, r)
     cut = channels // 2
     upper, lower = hop(weights[2][:cut], x=1), hop(weights[2][cut:], x=-1)
     up_sum = add(weights[1][:cut], upper).astype(BF16)

time: 153 us -> 168 us (1.098)
  local copies, waits for them, and re-layouts: 15.6 us -> 28.4 us
  waiting for transfers between devices: 36.2 us -> 27.8 us
  matrix products: 10.6 us -> 16.5 us
  other arithmetic: 7.95 us -> 13.2 us
    ppermute x42, waiting for transfers between devices: 36.2 us -> 27.8 us  [hop(): return lax.ppermute(value, ('chan', 'seq'), moves)]
    dynamic_update_slice x16, local copies, waits for them, and re-layouts: 6.98 us -> 14.7 us  [place_blocks(): lax.dynamic_update_slice(whole, part[None, None, :, None], (side, row, 0,...]
    broadcast_in_dim x1, local copies, waits for them, and re-layouts: 1.04 us -> 4.41 us  [place_blocks(): whole = jnp.zeros((2, RING, 2, 2, tokens, half), BF16)]
    dot_general x4, matrix products: 6.09 us -> 9.43 us  [weigh(): lax.dot_general(gated, columns, (((0,), (0,)), ((), ())), preferred_eleme...]
    unnamed x27 -> x55, local copies, waits for them, and re-layouts: 2.52 us -> 5.45 us
    dot_general x1, matrix products: 4.52 us -> 7.1 us  [local(): lax.dot_general(cot_rows, low_weight, (((1,), (1,)), ((), ())), preferred...]
    another operation x4, other arithmetic: 2.58 us -> 4.44 us
    concatenate x1, local copies, waits for them, and re-layouts: 1.87 us -> 0.03 us  [local(): gated_pair = jnp.concatenate([gated, hop(gated, pair=1)])]
  transfers between devices with their start and end apart: 42 -> 42, of which waited for: 16 -> 10; matrix products, arithmetic and copies ran while one was open for 19% -> 30% of each run, Pallas kernels for 20% -> 17%
where the time goes in v11:
time: 168 us; the launch traced here: 167 us
  starting transfers between devices  51.3 us (31%)
  Pallas kernels  28.5 us (17%)
  local copies, waits for them, and re-layouts  28.4 us (17%)
  waiting for transfers between devices  27.8 us (17%)
  matrix products  16.5 us (10%)
  other arithmetic  13.2 us (8%)
    ppermute x42, starting transfers between devices, hop(): return lax.ppermute(value, ('chan', 'seq'), moves)  51.3 us
    ppermute x42, waiting for transfers between devices, hop(): return lax.ppermute(value, ('chan', 'seq'), moves)  27.8 us
    pallas_call x4, Pallas kernels, call(): pl.pallas_call(body, out_shape=[jax.ShapeDtypeStruct(o.shape, o.dtype) fo...  21.6 us
    dynamic_update_slice x16, local copies, waits for them, and re-layouts, place_blocks(): lax.dynamic_update_slice(whole, part[None, None, :, None], (side, row, 0,...  14.7 us
    dot_general x4, matrix products, weigh(): lax.dot_general(gated, columns, (((0,), (0,)), ((), ())), preferred_eleme...  9.43 us
    dot_general x1, matrix products, local(): lax.dot_general(cot_rows, low_weight, (((1,), (1,)), ((), ())), preferred...  7.1 us
    pallas_call x1, Pallas kernels, project(): pl.pallas_call(project_tile, grid=(width // tile,), out_shape=[jax.ShapeD...  6.9 us
    unnamed x55, local copies, waits for them, and re-layouts  5.45 us
  transfers between devices with their start and end apart: 42, of which 10 were waited for; matrix products, arithmetic and copies ran while one was open for 30% of the time, Pallas kernels for 17%

profile of v11, /device:TPU:0, one launch (start us, length us, event | category | flops | bytes accessed | tf_op | source)
XLA Modules:
  0.0 167.0 jit_solution(5769080459060939476)
XLA Ops:
  0.7 1.1 constant_dynamic-slice_fusion.1
  1.8 2.1 %collective-permute-start.1 = (bf16[32,4096]{1,0:T(8,128)(2,1)S(1)}, bf16[32,4096]{1,0:T(8,128)(2,1)S(1)}, u32[]{:S(2)}, u32[]{:S(2)}) collective-permute-start(bf16[32,4096]{1,0:T(8,128)(2,1)S(1)} %get-tuple-element.127), channel_id=1, source_target_pairs={{0,4},{8,12},{4,16},{12,24},{16,20},{24,28},{20,0},{28,8},{32,36},... | collective-permute-start | bytes 786440 | tf_op jit(solution)/shard_map/ppermute | solution.py:47
  3.9 2.2 %collective-permute-start.2 = (bf16[32,4096]{1,0:T(8,128)(2,1)S(1)}, bf16[32,4096]{1,0:T(8,128)(2,1)S(1)}, u32[]{:S(2)}, u32[]{:S(2)}) collective-permute-start(bf16[32,4096]{1,0:T(8,128)(2,1)S(1)} %get-tuple-element.127), channel_id=1, source_target_pairs={{0,20},{8,28},{4,0},{12,8},{16,4},{24,12},{20,16},{28,24},{32,52},... | collective-permute-start | bytes 786440 | tf_op jit(solution)/shard_map/ppermute | solution.py:47
  6.1 1.8 %collective-permute-start = (bf16[32,4096]{1,0:T(8,128)(2,1)S(1)}, bf16[32,4096]{1,0:T(8,128)(2,1)S(1)}, u32[]{:S(2)}, u32[]{:S(2)}) collective-permute-start(bf16[32,4096]{1,0:T(8,128)(2,1)S(1)} %get-tuple-element.126), channel_id=1, source_target_pairs={{0,16},{8,24},{4,20},{12,28},{16,0},{24,8},{20,4},{28,12},{32,48},... | collective-permute-start | bytes 786440 | tf_op jit(solution)/shard_map/ppermute | solution.py:47
  7.9 4.4 %collective-permute-done.1 = bf16[32,4096]{1,0:T(8,128)(2,1)S(1)} collective-permute-done((bf16[32,4096]{1,0:T(8,128)(2,1)S(1)}, bf16[32,4096]{1,0:T(8,128)(2,1)S(1)}, u32[]{:S(2)}, u32[]{:S(2)}) %collective-permute-start.1) | collective-permute-done | bytes 262176 | tf_op jit(solution)/shard_map/ppermute | solution.py:47
  12.3 5.0 %collective-permute-done.2 = bf16[32,4096]{1,0:T(8,128)(2,1)S(1)} collective-permute-done((bf16[32,4096]{1,0:T(8,128)(2,1)S(1)}, bf16[32,4096]{1,0:T(8,128)(2,1)S(1)}, u32[]{:S(2)}, u32[]{:S(2)}) %collective-permute-start.2) | collective-permute-done | bytes 262176 | tf_op jit(solution)/shard_map/ppermute | solution.py:47
  17.5 1.7 %collective-permute-done = bf16[32,4096]{1,0:T(8,128)(2,1)S(1)} collective-permute-done((bf16[32,4096]{1,0:T(8,128)(2,1)S(1)}, bf16[32,4096]{1,0:T(8,128)(2,1)S(1)}, u32[]{:S(2)}, u32[]{:S(2)}) %collective-permute-start) | collective-permute-done | bytes 262176 | tf_op jit(solution)/shard_map/ppermute | solution.py:47
  19.5 1.6 collective-permute-start.5
  21.3 1.7 %collective-permute-start.6 = (bf16[2,32,4096]{2,1,0:T(8,128)(2,1)S(1)}, bf16[2,32,4096]{2,1,0:T(8,128)(2,1)}, u32[]{:S(2)}, u32[]{:S(2)}) collective-permute-start(bf16[2,32,4096]{2,1,0:T(8,128)(2,1)S(1)} %get-tuple-element.124), channel_id=1, source_target_pairs={{0,96},{8,104},{4,100},{12,108},{16,112},{24,120},{20,116},{28,124... | collective-permute-start | bytes 1572872 | tf_op jit(solution)/shard_map/ppermute | solution.py:47
  23.1 3.2 %forward_ends.1 = (f32[32,512]{1,0:T(8,128)S(1)}, f32[4,256,128]{2,1,0:T(8,128)S(1)}, f32[4,512,128]{2,1,0:T(8,128)S(1)}) custom-call(bf16[512,512]{1,0:T(8,128)(2,1)S(1)} %copy-done, bf16[512,512]{1,0:T(8,128)(2,1)S(1)} %copy-done.2, f32[16,512]{1,0:T(8,128)S(1)} %copy-done.8), custom_call_target="tpu_custom_call" | custom-call | flops 115000000 | tf_op jit(solution)/shard_map/forward_ends/pallas_call | solution.py:317
  26.3 1.2 collective-permute-start.7
  27.5 4.4 %broadcast_in_dim.45 = bf16[2,4,2,2,32,4096]{5,4,3,2,1,0:T(8,128)(2,1)} broadcast(bf16[]{:T(256)} %constant.72.clone.1), dimensions={} | broadcast | bytes 8388610 | tf_op jit(solution)/shard_map/broadcast_in_dim | solution.py:66
  33.1 2.0 %collective-permute-done.5 = bf16[2,32,4096]{2,1,0:T(8,128)(2,1)S(1)} collective-permute-done((bf16[2,32,4096]{2,1,0:T(8,128)(2,1)S(1)}, bf16[2,32,4096]{2,1,0:T(8,128)(2,1)S(1)}, u32[]{:S(2)}, u32[]{:S(2)}) %collective-permute-start.5) | collective-permute-done | bytes 524320 | tf_op jit(solution)/shard_map/ppermute | solution.py:47
  35.1 1.8 %collective-permute-start.4 = (bf16[2,32,4096]{2,1,0:T(8,128)(2,1)S(1)}, bf16[2,32,4096]{2,1,0:T(8,128)(2,1)S(1)}, u32[]{:S(2)}, u32[]{:S(2)}) collective-permute-start(bf16[2,32,4096]{2,1,0:T(8,128)(2,1)S(1)} %get-tuple-element.125), channel_id=1, source_target_pairs={{0,96},{8,104},{4,100},{12,108},{16,112},{24,120},{20,116},{28,124... | collective-permute-start | bytes 1572872 | tf_op jit(solution)/shard_map/ppermute | solution.py:47
  36.9 1.5 collective-permute-start.8
  38.4 2.7 %collective-permute-start.9 = (f32[64,512]{1,0:T(8,128)S(1)}, f32[64,512]{1,0:T(8,128)S(1)}, u32[]{:S(2)}, u32[]{:S(2)}) collective-permute-start(f32[64,512]{1,0:T(8,128)S(1)} %pad_maximum_fusion.5.refs_6_), channel_id=1, source_target_pairs={{0,2},{8,10},{4,6},{12,14},{16,18},{24,26},{20,22},{28,30},{32,34}... | collective-permute-start | bytes 393224 | tf_op jit(solution)/shard_map/ppermute | solution.py:47
  42.8 1.4 collective-permute-start.10
  45.1 1.7 %collective-permute-done.9.refs_8_ = f32[64,512]{1,0:T(8,128)S(1)} collective-permute-done((f32[64,512]{1,0:T(8,128)S(1)}, f32[64,512]{1,0:T(8,128)S(1)}, u32[]{:S(2)}, u32[]{:S(2)}) %collective-permute-start.9) | collective-permute-done | bytes 131104 | tf_op jit(solution)/shard_map/ppermute | solution.py:47
  47.8 3.8 %forward_full.1 = (bf16[512,512]{1,0:T(8,128)(2,1)S(1)}, bf16[512,512]{1,0:T(8,128)(2,1)S(1)}, f32[4,512,128]{2,1,0:T(8,128)S(1)}, f32[4,256,128]{2,1,0:T(8,128)S(1)}) custom-call(bf16[512,512]{1,0:T(8,128)(2,1)S(1)} %copy-done.6, f32[4,512,128]{2,1,0:T(8,128)S(1)} %get-tuple-element.65.refs_1_.drive_ref, f32[4,256,128]{2,1,0:T(8,128)S(1)} %get-tuple-element.66.refs_2_, ...), custom_call_target="tpu_custom_call" | custom-call | flops 115000000 | tf_op jit(solution)/shard_map/forward_full/pallas_call | solution.py:317
  53.0 2.9 %collective-permute-start.18 = (bf16[2,32,4096]{2,1,0:T(8,128)(2,1)}, bf16[2,32,4096]{2,1,0:T(8,128)(2,1)S(1)}, u32[]{:S(2)}, u32[]{:S(2)}) collective-permute-start(bf16[2,32,4096]{2,1,0:T(8,128)(2,1)} %collective-permute-done.6), channel_id=1, source_target_pairs={{0,96},{8,104},{4,100},{12,108},{16,112},{24,120},{20,116},{28,124... | collective-permute-start | bytes 1572872 | tf_op jit(solution)/shard_map/ppermute | solution.py:47
  55.9 1.3 collective-permute-start.23
  58.1 6.9 %project.1 = (bf16[64,8192]{1,0:T(8,128)(2,1)S(1)}, bf16[192,8192]{1,0:T(8,128)(2,1)S(1)}, bf16[64,8192]{1,0:T(8,128)(2,1)S(1)}, bf16[192,8192]{1,0:T(8,128)(2,1)S(1)}) custom-call(bf16[512,512]{1,0:T(8,128)(2,1)S(1)} %get-tuple-element.70.rows_ref, bf16[512,8192]{1,0:T(8,128)(2,1)S(1)} %bitcast.83), custom_call_target="tpu_custom_call" | custom-call | flops 4294967296 | bytes 16777216 | tf_op jit(solution)/shard_map/project/pallas_call | solution.py:92
  70.0 1.9 %bitcast_dynamic-update-slice_fusion.4 = bf16[2,4,2,2,32,4096]{5,4,3,2,1,0:T(8,128)(2,1)} fusion(bf16[2,4,2,2,32,4096]{5,4,3,2,1,0:T(8,128)(2,1)} %bitcast_dynamic-update-slice_fusion.5, s32[]{:T(128)S(6)} %select_n.128, s32[]{:T(128)S(6)} %select_n.125, bf16[2,32,4096]{2,1,0:T(8,128)(2,1)} %collective-permute-done.6), kind=kLoop, calls=%fused_computation.42 | loop fusion | bytes 1048584 | tf_op jit(solution)/shard_map/dynamic_update_slice | solution.py:71
  74.5 1.7 %collective-permute-start.25 = (bf16[32,8192]{1,0:T(8,128)(2,1)S(1)}, bf16[32,8192]{1,0:T(8,128)(2,1)S(1)}, u32[]{:S(2)}, u32[]{:S(2)}) collective-permute-start(bf16[32,8192]{1,0:T(8,128)(2,1)S(1)} %get-tuple-element.122), channel_id=1, source_target_pairs={{0,32},{8,40},{4,36},{12,44},{16,48},{24,56},{20,52},{28,60},{32,6... | collective-permute-start | bytes 1572872 | tf_op jit(solution)/shard_map/ppermute | solution.py:47
  77.1 1.3 collective-permute-done.20
  81.0 4.0 %multiply_convert_fusion.3 = bf16[512,1024]{1,0:T(8,128)(2,1)S(1)} fusion(bf16[1024,512]{1,0:T(8,128)(2,1)S(1)} %constant_dynamic-update-slice_fusion, bf16[1024,4096]{1,0:T(8,128)(2,1)} %bitcast.84, s32[]{:T(128)S(6)} %select_n.130), kind=kOutput, calls=%fused_computation.14 | convolution fusion | flops 1074790400 | bytes 4194308 | tf_op jit(solution)/shard_map/dot_general | solution.py:110
  85.0 7.1 %fusion = f32[1024,512]{1,0:T(8,128)S(1)} fusion(bf16[1024,4096]{1,0:T(8,128)(2,1)} %bitcast.85, bf16[512,8192]{1,0:T(8,128)(2,1)S(1)} %bitcast.83, s32[]{:T(128)S(6)} %select_n.116), kind=kOutput, calls=%fused_computation | convolution fusion | flops 4294967296 | bytes 14680068 | tf_op jit(solution)/shard_map/dot_general | solution.py:391
  93.2 1.1 collective-permute-start.32
  94.3 2.2 %collective-permute-start.33 = (bf16[256,1024]{1,0:T(8,128)(2,1)S(1)}, bf16[256,1024]{1,0:T(8,128)(2,1)S(1)}, u32[]{:S(2)}, u32[]{:S(2)}) collective-permute-start(bf16[256,1024]{1,0:T(8,128)(2,1)S(1)} %get-tuple-element.118), channel_id=1, source_target_pairs={{0,3},{8,11},{4,7},{12,15},{16,19},{24,27},{20,23},{28,31},{32,35}... | collective-permute-start | bytes 1572872 | tf_op jit(solution)/shard_map/ppermute | solution.py:47
  96.5 1.3 multiply_convert_fusion.2
  98.6 1.3 multiply_convert_fusion.1
  100.7 5.7 %collective-permute-done.24 = bf16[512,512]{1,0:T(8,128)(2,1)S(1)} collective-permute-done((bf16[512,512]{1,0:T(8,128)(2,1)S(1)}, bf16[512,512]{1,0:T(8,128)(2,1)S(1)}, u32[]{:S(2)}, u32[]{:S(2)}) %collective-permute-start.24) | collective-permute-done | bytes 524320 | tf_op jit(solution)/shard_map/ppermute | solution.py:47
  109.7 1.7 %collective-permute-start.26 = (bf16[64,8192]{1,0:T(8,128)(2,1)}, bf16[64,8192]{1,0:T(8,128)(2,1)}, u32[]{:S(2)}, u32[]{:S(2)}) collective-permute-start(bf16[64,8192]{1,0:T(8,128)(2,1)} %pad_maximum_fusion.1), channel_id=1, source_target_pairs={{0,32},{8,40},{4,36},{12,44},{16,48},{24,56},{20,52},{28,60},{32,6... | collective-permute-start | bytes 3145736 | tf_op jit(solution)/shard_map/ppermute | solution.py:47
  114.4 2.3 %collective-permute-start.35 = (bf16[256,1024]{1,0:T(8,128)(2,1)}, bf16[256,1024]{1,0:T(8,128)(2,1)}, u32[]{:S(2)}, u32[]{:S(2)}) collective-permute-start(bf16[256,1024]{1,0:T(8,128)(2,1)} %slice.150), channel_id=1, source_target_pairs={{0,3},{8,11},{4,7},{12,15},{16,19},{24,27},{20,23},{28,31},{32,35}... | collective-permute-start | bytes 1572872 | tf_op jit(solution)/shard_map/ppermute | solution.py:47
  116.7 1.7 %convert_add_fusion.3.grad_ref = f32[512,512]{1,0:T(8,128)S(1)} fusion(bf16[512,512]{1,0:T(8,128)(2,1)} %copy-done.19, f32[1024,512]{1,0:T(8,128)} %copy-done.16), kind=kLoop, calls=%fused_computation.33 | loop fusion | flops 524288 | bytes 2621440 | tf_op jit(solution)/shard_map/add | solution.py:76
  118.4 1.2 copy-done.5
  120.7 1.2 copy-done.12
  122.9 9.5 %backward_ends.1 = (bf16[512,512]{1,0:T(8,128)(2,1)}, f32[4,512,128]{2,1,0:T(8,128)S(1)}, f32[56,512]{1,0:T(8,128)S(1)}, f32[4,128,128]{2,1,0:T(8,128)S(1)}) custom-call(f32[512,512]{1,0:T(8,128)S(1)} %convert_add_fusion.3.grad_ref, bf16[512,512]{1,0:T(8,128)(2,1)S(1)} %copy-done.7, f32[4,512,128]{2,1,0:T(8,128)S(1)} %copy-done.12, ...), custom_call_target="tpu_custom_call" | custom-call | flops 2300000000 | tf_op jit(solution)/shard_map/backward_ends/pallas_call | solution.py:317
  133.2 2.9 %multiply_convert_fusion = bf16[512,1024]{1,0:T(8,128)(2,1)S(1)} fusion(bf16[1024,512]{1,0:T(8,128)(2,1)S(1)} %copy-done.22, bf16[1024,4096]{1,0:T(8,128)(2,1)} %bitcast.86, s32[]{:T(128)S(6)} %select_n.133), kind=kOutput, calls=%fused_computation.2 | convolution fusion | flops 1074790400 | bytes 4194308 | tf_op jit(solution)/shard_map/dot_general | solution.py:110
  136.2 3.2 %collective-permute-start.38 = (bf16[256,1024]{1,0:T(8,128)(2,1)S(1)}, bf16[256,1024]{1,0:T(8,128)(2,1)S(1)}, u32[]{:S(2)}, u32[]{:S(2)}) collective-permute-start(bf16[256,1024]{1,0:T(8,128)(2,1)S(1)} %copy-done.18), channel_id=1, source_target_pairs={{0,3},{8,11},{4,7},{12,15},{16,19},{24,27},{20,23},{28,31},{32,35}... | collective-permute-start | bytes 1572872 | tf_op jit(solution)/shard_map/ppermute | solution.py:47
  139.4 2.4 %fusion.26 = (bf16[64,8192]{1,0:T(8,128)(2,1)S(1)}, f32[64,8192]{1,0:T(8,128)S(1)}) fusion(bf16[64,8192]{1,0:T(8,128)(2,1)} %collective-permute-done.28, bf16[64,8192]{1,0:T(8,128)(2,1)} %collective-permute-done.26, bf16[192,8192]{1,0:T(8,128)(2,1)} %copy-done.15, bf16[192,8192]{1,0:T(8,128)(2,1)S(1)} %get-tuple-element.71), kind=kLoop, calls=%fused_computation.70 | loop fusion | flops 4194304 | bytes 7340032 | tf_op jit(solution)/shard_map/convert.2
  141.9 2.5 %collective-permute-start.30 = (bf16[32,4096]{1,0:T(8,128)(2,1)S(1)}, bf16[32,4096]{1,0:T(8,128)(2,1)S(1)}, u32[]{:S(2)}, u32[]{:S(2)}) collective-permute-start(bf16[32,4096]{1,0:T(8,128)(2,1)S(1)} %get-tuple-element.121), channel_id=1, source_target_pairs={{0,20},{8,28},{4,0},{12,8},{16,4},{24,12},{20,16},{28,24},{32,52},... | collective-permute-start | bytes 786440 | tf_op jit(solution)/shard_map/ppermute | solution.py:47
  144.4 4.8 %collective-permute-done.37 = bf16[256,1024]{1,0:T(8,128)(2,1)S(1)} collective-permute-done((bf16[256,1024]{1,0:T(8,128)(2,1)S(1)}, bf16[256,1024]{1,0:T(8,128)(2,1)S(1)}, u32[]{:S(2)}, u32[]{:S(2)}) %collective-permute-start.37) | collective-permute-done | bytes 524320 | tf_op jit(solution)/shard_map/ppermute | solution.py:47
  149.3 4.4 %collective-permute-start.40 = (f32[72,512]{1,0:T(8,128)S(1)}, f32[72,512]{1,0:T(8,128)S(1)}, u32[]{:S(2)}, u32[]{:S(2)}) collective-permute-start(f32[72,512]{1,0:T(8,128)S(1)} %pad_maximum_fusion.4.refs_7_), channel_id=1, source_target_pairs={{0,2},{8,10},{4,6},{12,14},{16,18},{24,26},{20,22},{28,30},{32,34}... | collective-permute-start | bytes 442376 | tf_op jit(solution)/shard_map/ppermute | solution.py:47
  153.7 2.5 %collective-permute-start.29 = (bf16[32,4096]{1,0:T(8,128)(2,1)S(1)}, bf16[32,4096]{1,0:T(8,128)(2,1)S(1)}, u32[]{:S(2)}, u32[]{:S(2)}) collective-permute-start(bf16[32,4096]{1,0:T(8,128)(2,1)S(1)} %get-tuple-element.120), channel_id=1, source_target_pairs={{0,16},{8,24},{4,20},{12,28},{16,0},{24,8},{20,4},{28,12},{32,48},... | collective-permute-start | bytes 786440 | tf_op jit(solution)/shard_map/ppermute | solution.py:47
  156.2 1.4 collective-permute-start.31
  157.6 1.8 %add_convert_fusion.2 = (bf16[256,1024]{1,0:T(8,128)(2,1)S(1)}, bf16[256,1024]{1,0:T(8,128)(2,1)S(1)}) fusion(bf16[256,1024]{1,0:T(8,128)(2,1)} %collective-permute-done.35, bf16[256,1024]{1,0:T(8,128)(2,1)S(1)} %collective-permute-done.37, bf16[512,1024]{1,0:T(8,128)(2,1)S(1)} %multiply_convert_fusion, bf16[256,1024]{1,0:T(8,128)(2,1)S(1)} %collective-permute-done.38, ...), kind=kLoop, calls=%fused_computation.32 | loop fusion | flops 3145728 | bytes 4194304 | tf_op jit(solution)/shard_map/convert
  160.5 5.0 %backward_full.1 = (bf16[512,512]{1,0:T(8,128)(2,1)}, bf16[512,512]{1,0:T(8,128)(2,1)}, f32[16,512]{1,0:T(8,128)}, f32[16,512]{1,0:T(8,128)}, f32[8,512]{1,0:T(8,128)S(1)}) custom-call(bf16[512,512]{1,0:T(8,128)(2,1)S(1)} %copy-done.1, bf16[512,512]{1,0:T(8,128)(2,1)S(1)} %copy-done.3, f32[4,512,128]{2,1,0:T(8,128)S(1)} %get-tuple-element.94.refs_2_, ...), custom_call_target="tpu_custom_call" | custom-call | flops 115000000 | tf_op jit(solution)/shard_map/backward_full/pallas_call | solution.py:317
  (154 shorter events, 33.1 us)
Async XLA Ops:
  1.8 10.5 %collective-permute-start.1 = (bf16[32,4096]{1,0:T(8,128)(2,1)S(1)}, bf16[32,4096]{1,0:T(8,128)(2,1)S(1)}, u32[]{:S(2)}, u32[]{:S(2)}) collective-permute-start(bf16[32,4096]{1,0:T(8,128)(2,1)S(1)} %get-tuple-element.127), channel_id=1, source_target_pairs={{0,4},{8,12},{4,16},{12,24},{16,20},{24,28},{20,0},{28,8},{32,36},... | collective-permute-start | bytes 786440 | tf_op jit(solution)/shard_map/ppermute | solution.py:47
  3.9 13.4 %collective-permute-start.2 = (bf16[32,4096]{1,0:T(8,128)(2,1)S(1)}, bf16[32,4096]{1,0:T(8,128)(2,1)S(1)}, u32[]{:S(2)}, u32[]{:S(2)}) collective-permute-start(bf16[32,4096]{1,0:T(8,128)(2,1)S(1)} %get-tuple-element.127), channel_id=1, source_target_pairs={{0,20},{8,28},{4,0},{12,8},{16,4},{24,12},{20,16},{28,24},{32,52},... | collective-permute-start | bytes 786440 | tf_op jit(solution)/shard_map/ppermute | solution.py:47
  6.1 13.0 %collective-permute-start = (bf16[32,4096]{1,0:T(8,128)(2,1)S(1)}, bf16[32,4096]{1,0:T(8,128)(2,1)S(1)}, u32[]{:S(2)}, u32[]{:S(2)}) collective-permute-start(bf16[32,4096]{1,0:T(8,128)(2,1)S(1)} %get-tuple-element.126), channel_id=1, source_target_pairs={{0,16},{8,24},{4,20},{12,28},{16,0},{24,8},{20,4},{28,12},{32,48},... | collective-permute-start | bytes 786440 | tf_op jit(solution)/shard_map/ppermute | solution.py:47
  19.3 28.4 %copy-start.6 = (bf16[512,512]{1,0:T(8,128)(2,1)S(1)}, bf16[512,512]{1,0:T(8,128)(2,1)}, u32[]{:S(2)}) copy-start(bf16[512,512]{1,0:T(8,128)(2,1)} %query_ref.1) | copy-start | bytes 1572868
  19.3 28.4 %copy-start.9 = (f32[16,512]{1,0:T(8,128)S(1)}, f32[16,512]{1,0:T(8,128)}, u32[]{:S(2)}) copy-start(f32[16,512]{1,0:T(8,128)} %refs_5_.1) | copy-start | bytes 98308
  19.3 28.4 %copy-start.10 = (f32[512]{0:T(512)S(1)}, f32[512]{0:T(512)}, u32[]{:S(2)}) copy-start(f32[512]{0:T(512)} %param.11) | copy-start | bytes 6148
  19.4 18.9 %collective-permute-start.11 = (bf16[2,32,4096]{2,1,0:T(8,128)(2,1)S(1)}, bf16[2,32,4096]{2,1,0:T(8,128)(2,1)S(1)}, u32[]{:S(2)}, u32[]{:S(2)}) collective-permute-start(bf16[2,32,4096]{2,1,0:T(8,128)(2,1)S(1)} %get-tuple-element.125), channel_id=1, source_target_pairs={{0,8},{8,0},{4,12},{12,4},{16,24},{24,16},{20,28},{28,20},{32,40},... | collective-permute-start | bytes 1572872 | tf_op jit(solution)/shard_map/ppermute | solution.py:47
  19.5 15.6 %collective-permute-start.5 = (bf16[2,32,4096]{2,1,0:T(8,128)(2,1)S(1)}, bf16[2,32,4096]{2,1,0:T(8,128)(2,1)S(1)}, u32[]{:S(2)}, u32[]{:S(2)}) collective-permute-start(bf16[2,32,4096]{2,1,0:T(8,128)(2,1)S(1)} %get-tuple-element.125), channel_id=1, source_target_pairs={{0,32},{8,40},{4,36},{12,44},{16,48},{24,56},{20,52},{28,60},{32,6... | collective-permute-start | bytes 1572872 | tf_op jit(solution)/shard_map/ppermute | solution.py:47
  21.2 21.6 %collective-permute-start.12 = (bf16[2,32,4096]{2,1,0:T(8,128)(2,1)S(1)}, bf16[2,32,4096]{2,1,0:T(8,128)(2,1)S(1)}, u32[]{:S(2)}, u32[]{:S(2)}) collective-permute-start(bf16[2,32,4096]{2,1,0:T(8,128)(2,1)S(1)} %get-tuple-element.124), channel_id=1, source_target_pairs={{0,8},{8,0},{4,12},{12,4},{16,24},{24,16},{20,28},{28,20},{32,40},... | collective-permute-start | bytes 1572872 | tf_op jit(solution)/shard_map/ppermute | solution.py:47
  21.3 15.5 %collective-permute-start.6 = (bf16[2,32,4096]{2,1,0:T(8,128)(2,1)S(1)}, bf16[2,32,4096]{2,1,0:T(8,128)(2,1)}, u32[]{:S(2)}, u32[]{:S(2)}) collective-permute-start(bf16[2,32,4096]{2,1,0:T(8,128)(2,1)S(1)} %get-tuple-element.124), channel_id=1, source_target_pairs={{0,96},{8,104},{4,100},{12,108},{16,112},{24,120},{20,116},{28,124... | collective-permute-start | bytes 1572872 | tf_op jit(solution)/shard_map/ppermute | solution.py:47
  26.3 31.7 %copy-start.4 = (f32[4,512,128]{2,1,0:T(8,128)}, f32[4,512,128]{2,1,0:T(8,128)S(1)}, u32[]{:S(2)}) copy-start(f32[4,512,128]{2,1,0:T(8,128)S(1)} %get-tuple-element.65.refs_1_.drive_ref) | copy-start | bytes 3145732
  26.3 31.7 %slice-start = ((s8[8388608]{0:T(1024)(128)(4,1)}), s8[4194304]{0:T(1024)(128)(4,1)S(1)}, s32[]{:S(2)}) async-start(s8[8388608]{0:T(1024)(128)(4,1)} %bitcast.82), calls=%async_computation | async-start | bytes 8388608
  26.3 6.5 %collective-permute-start.7 = (f32[32,512]{1,0:T(8,128)S(1)}, f32[32,512]{1,0:T(8,128)S(1)}, u32[]{:S(2)}, u32[]{:S(2)}) collective-permute-start(f32[32,512]{1,0:T(8,128)S(1)} %get-tuple-element.62), channel_id=1, source_target_pairs={{0,4},{8,12},{4,0},{12,8},{16,20},{24,28},{20,16},{28,24},{32,36},... | collective-permute-start | bytes 196616 | tf_op jit(solution)/shard_map/ppermute | solution.py:47
  32.0 26.1 %slice-start.1 = ((s8[8388608]{0:T(1024)(128)(4,1)}), s8[4194304]{0:T(1024)(128)(4,1)S(1)}, s32[]{:S(2)}) async-start(s8[8388608]{0:T(1024)(128)(4,1)} %bitcast.82), calls=%async_computation.1 | async-start | bytes 8388608
  32.8 20.2 %collective-permute-start.3 = (bf16[2,32,4096]{2,1,0:T(8,128)(2,1)S(1)}, bf16[2,32,4096]{2,1,0:T(8,128)(2,1)S(1)}, u32[]{:S(2)}, u32[]{:S(2)}) collective-permute-start(bf16[2,32,4096]{2,1,0:T(8,128)(2,1)S(1)} %get-tuple-element.124), channel_id=1, source_target_pairs={{0,32},{8,40},{4,36},{12,44},{16,48},{24,56},{20,52},{28,60},{32,6... | collective-permute-start | bytes 1572872 | tf_op jit(solution)/shard_map/ppermute | solution.py:47
  35.1 20.8 %collective-permute-start.4 = (bf16[2,32,4096]{2,1,0:T(8,128)(2,1)S(1)}, bf16[2,32,4096]{2,1,0:T(8,128)(2,1)S(1)}, u32[]{:S(2)}, u32[]{:S(2)}) collective-permute-start(bf16[2,32,4096]{2,1,0:T(8,128)(2,1)S(1)} %get-tuple-element.125), channel_id=1, source_target_pairs={{0,96},{8,104},{4,100},{12,108},{16,112},{24,120},{20,116},{28,124... | collective-permute-start | bytes 1572872 | tf_op jit(solution)/shard_map/ppermute | solution.py:47
  36.9 8.2 %collective-permute-start.8 = (f32[64,512]{1,0:T(8,128)S(1)}, f32[64,512]{1,0:T(8,128)S(1)}, u32[]{:S(2)}, u32[]{:S(2)}) collective-permute-start(f32[64,512]{1,0:T(8,128)S(1)} %pad_maximum_fusion.5.refs_6_), channel_id=1, source_target_pairs={{0,1},{8,9},{4,5},{12,13},{16,17},{24,25},{20,21},{28,29},{32,33},... | collective-permute-start | bytes 393224 | tf_op jit(solution)/shard_map/ppermute | solution.py:47
  38.4 8.4 %collective-permute-start.9 = (f32[64,512]{1,0:T(8,128)S(1)}, f32[64,512]{1,0:T(8,128)S(1)}, u32[]{:S(2)}, u32[]{:S(2)}) collective-permute-start(f32[64,512]{1,0:T(8,128)S(1)} %pad_maximum_fusion.5.refs_6_), channel_id=1, source_target_pairs={{0,2},{8,10},{4,6},{12,14},{16,18},{24,26},{20,22},{28,30},{32,34}... | collective-permute-start | bytes 393224 | tf_op jit(solution)/shard_map/ppermute | solution.py:47
  42.8 5.0 %collective-permute-start.10 = (f32[64,512]{1,0:T(8,128)S(1)}, f32[64,512]{1,0:T(8,128)S(1)}, u32[]{:S(2)}, u32[]{:S(2)}) collective-permute-start(f32[64,512]{1,0:T(8,128)S(1)} %pad_maximum_fusion.5.refs_6_), channel_id=1, source_target_pairs={{0,3},{8,11},{4,7},{12,15},{16,19},{24,27},{20,23},{28,31},{32,35}... | collective-permute-start | bytes 393224 | tf_op jit(solution)/shard_map/ppermute | solution.py:47
  52.4 12.6 %collective-permute-start.13 = (bf16[2,32,4096]{2,1,0:T(8,128)(2,1)S(1)}, bf16[2,32,4096]{2,1,0:T(8,128)(2,1)S(1)}, u32[]{:S(2)}, u32[]{:S(2)}) collective-permute-start(bf16[2,32,4096]{2,1,0:T(8,128)(2,1)S(1)} %collective-permute-done.5), channel_id=1, source_target_pairs={{0,8},{8,0},{4,12},{12,4},{16,24},{24,16},{20,28},{28,20},{32,40},... | collective-permute-start | bytes 1572872 | tf_op jit(solution)/shard_map/ppermute | solution.py:47
  52.4 21.0 %collective-permute-start.17 = (bf16[2,32,4096]{2,1,0:T(8,128)(2,1)S(1)}, bf16[2,32,4096]{2,1,0:T(8,128)(2,1)S(1)}, u32[]{:S(2)}, u32[]{:S(2)}) collective-permute-start(bf16[2,32,4096]{2,1,0:T(8,128)(2,1)S(1)} %collective-permute-done.5), channel_id=1, source_target_pairs={{0,32},{8,40},{4,36},{12,44},{16,48},{24,56},{20,52},{28,60},{32,6... | collective-permute-start | bytes 1572872 | tf_op jit(solution)/shard_map/ppermute | solution.py:47
  52.8 19.5 %collective-permute-start.16 = (bf16[2,32,4096]{2,1,0:T(8,128)(2,1)}, bf16[2,32,4096]{2,1,0:T(8,128)(2,1)S(1)}, u32[]{:S(2)}, u32[]{:S(2)}) collective-permute-start(bf16[2,32,4096]{2,1,0:T(8,128)(2,1)} %collective-permute-done.6), channel_id=1, source_target_pairs={{0,8},{8,0},{4,12},{12,4},{16,24},{24,16},{20,28},{28,20},{32,40},... | collective-permute-start | bytes 1572872 | tf_op jit(solution)/shard_map/ppermute | solution.py:47
  53.0 20.4 %collective-permute-start.18 = (bf16[2,32,4096]{2,1,0:T(8,128)(2,1)}, bf16[2,32,4096]{2,1,0:T(8,128)(2,1)S(1)}, u32[]{:S(2)}, u32[]{:S(2)}) collective-permute-start(bf16[2,32,4096]{2,1,0:T(8,128)(2,1)} %collective-permute-done.6), channel_id=1, source_target_pairs={{0,96},{8,104},{4,100},{12,108},{16,112},{24,120},{20,116},{28,124... | collective-permute-start | bytes 1572872 | tf_op jit(solution)/shard_map/ppermute | solution.py:47
  55.9 16.1 %collective-permute-start.23 = (bf16[512,512]{1,0:T(8,128)(2,1)S(1)}, bf16[512,512]{1,0:T(8,128)(2,1)S(1)}, u32[]{:S(2)}, u32[]{:S(2)}) collective-permute-start(bf16[512,512]{1,0:T(8,128)(2,1)S(1)} %get-tuple-element.83), channel_id=1, source_target_pairs={{0,4},{8,12},{4,0},{12,8},{16,20},{24,28},{20,16},{28,24},{32,36},... | collective-permute-start | bytes 1572872 | tf_op jit(solution)/shard_map/ppermute | solution.py:47
  65.0 2.0 %collective-permute-start.14 = (bf16[2,32,4096]{2,1,0:T(8,128)(2,1)S(1)}, bf16[2,32,4096]{2,1,0:T(8,128)(2,1)S(1)}, u32[]{:S(2)}, u32[]{:S(2)}) collective-permute-start(bf16[2,32,4096]{2,1,0:T(8,128)(2,1)S(1)} %collective-permute-done.3), channel_id=1, source_target_pairs={{0,8},{8,0},{4,12},{12,4},{16,24},{24,16},{20,28},{28,20},{32,40},... | collective-permute-start | bytes 1572872 | tf_op jit(solution)/shard_map/ppermute | solution.py:47
  67.0 2.0 %collective-permute-start.15 = (bf16[2,32,4096]{2,1,0:T(8,128)(2,1)S(1)}, bf16[2,32,4096]{2,1,0:T(8,128)(2,1)S(1)}, u32[]{:S(2)}, u32[]{:S(2)}) collective-permute-start(bf16[2,32,4096]{2,1,0:T(8,128)(2,1)S(1)} %collective-permute-done.4), channel_id=1, source_target_pairs={{0,8},{8,0},{4,12},{12,4},{16,24},{24,16},{20,28},{28,20},{32,40},... | collective-permute-start | bytes 1572872 | tf_op jit(solution)/shard_map/ppermute | solution.py:47
  69.0 4.2 %collective-permute-start.19 = (bf16[64,8192]{1,0:T(8,128)(2,1)S(1)}, bf16[64,8192]{1,0:T(8,128)(2,1)S(1)}, u32[]{:S(2)}, u32[]{:S(2)}) collective-permute-start(bf16[64,8192]{1,0:T(8,128)(2,1)S(1)} %get-tuple-element.77), channel_id=1, source_target_pairs={{0,8},{8,0},{4,12},{12,4},{16,24},{24,16},{20,28},{28,20},{32,40},... | collective-permute-start | bytes 3145736 | tf_op jit(solution)/shard_map/ppermute | solution.py:47
  72.0 9.0 %collective-permute-start.22 = (bf16[192,8192]{1,0:T(8,128)(2,1)S(1)}, bf16[192,8192]{1,0:T(8,128)(2,1)S(1)}, u32[]{:S(2)}, u32[]{:S(2)}) collective-permute-start(bf16[192,8192]{1,0:T(8,128)(2,1)S(1)} %get-tuple-element.80), channel_id=1, source_target_pairs={{0,8},{8,0},{4,12},{12,4},{16,24},{24,16},{20,28},{28,20},{32,40},... | collective-permute-start | bytes 9437192 | tf_op jit(solution)/shard_map/ppermute | solution.py:47
  73.4 4.9 %collective-permute-start.20 = (bf16[2,32,4096]{2,1,0:T(8,128)(2,1)S(1)}, bf16[2,32,4096]{2,1,0:T(8,128)(2,1)S(1)}, u32[]{:S(2)}, u32[]{:S(2)}) collective-permute-start(bf16[2,32,4096]{2,1,0:T(8,128)(2,1)S(1)} %collective-permute-done.17), channel_id=1, source_target_pairs={{0,8},{8,0},{4,12},{12,4},{16,24},{24,16},{20,28},{28,20},{32,40},... | collective-permute-start | bytes 1572872 | tf_op jit(solution)/shard_map/ppermute | solution.py:47
  73.8 6.2 %collective-permute-start.21 = (bf16[2,32,4096]{2,1,0:T(8,128)(2,1)S(1)}, bf16[2,32,4096]{2,1,0:T(8,128)(2,1)S(1)}, u32[]{:S(2)}, u32[]{:S(2)}) collective-permute-start(bf16[2,32,4096]{2,1,0:T(8,128)(2,1)S(1)} %collective-permute-done.18), channel_id=1, source_target_pairs={{0,8},{8,0},{4,12},{12,4},{16,24},{24,16},{20,28},{28,20},{32,40},... | collective-permute-start | bytes 1572872 | tf_op jit(solution)/shard_map/ppermute | solution.py:47
  74.2 32.8 %collective-permute-start.27 = (bf16[32,8192]{1,0:T(8,128)(2,1)S(1)}, bf16[32,8192]{1,0:T(8,128)(2,1)S(1)}, u32[]{:S(2)}, u32[]{:S(2)}) collective-permute-start(bf16[32,8192]{1,0:T(8,128)(2,1)S(1)} %get-tuple-element.123), channel_id=1, source_target_pairs={{0,96},{8,104},{4,100},{12,108},{16,112},{24,120},{20,116},{28,124... | collective-permute-start | bytes 1572872 | tf_op jit(solution)/shard_map/ppermute | solution.py:47
  74.5 34.0 %collective-permute-start.25 = (bf16[32,8192]{1,0:T(8,128)(2,1)S(1)}, bf16[32,8192]{1,0:T(8,128)(2,1)S(1)}, u32[]{:S(2)}, u32[]{:S(2)}) collective-permute-start(bf16[32,8192]{1,0:T(8,128)(2,1)S(1)} %get-tuple-element.122), channel_id=1, source_target_pairs={{0,32},{8,40},{4,36},{12,44},{16,48},{24,56},{20,52},{28,60},{32,6... | collective-permute-start | bytes 1572872 | tf_op jit(solution)/shard_map/ppermute | solution.py:47
  92.2 14.2 %collective-permute-start.24 = (bf16[512,512]{1,0:T(8,128)(2,1)S(1)}, bf16[512,512]{1,0:T(8,128)(2,1)S(1)}, u32[]{:S(2)}, u32[]{:S(2)}) collective-permute-start(bf16[512,512]{1,0:T(8,128)(2,1)S(1)} %slice.186), channel_id=1, source_target_pairs={{0,4},{8,12},{4,0},{12,8},{16,20},{24,28},{20,16},{28,24},{32,36},... | collective-permute-start | bytes 1572872 | tf_op jit(solution)/shard_map/ppermute | solution.py:47
  93.2 18.3 %collective-permute-start.32 = (bf16[256,1024]{1,0:T(8,128)(2,1)S(1)}, bf16[256,1024]{1,0:T(8,128)(2,1)S(1)}, u32[]{:S(2)}, u32[]{:S(2)}) collective-permute-start(bf16[256,1024]{1,0:T(8,128)(2,1)S(1)} %get-tuple-element.119), channel_id=1, source_target_pairs={{0,1},{8,9},{4,5},{12,13},{16,17},{24,25},{20,21},{28,29},{32,33},... | collective-permute-start | bytes 1572872 | tf_op jit(solution)/shard_map/ppermute | solution.py:47
  94.3 18.2 %collective-permute-start.33 = (bf16[256,1024]{1,0:T(8,128)(2,1)S(1)}, bf16[256,1024]{1,0:T(8,128)(2,1)S(1)}, u32[]{:S(2)}, u32[]{:S(2)}) collective-permute-start(bf16[256,1024]{1,0:T(8,128)(2,1)S(1)} %get-tuple-element.118), channel_id=1, source_target_pairs={{0,3},{8,11},{4,7},{12,15},{16,19},{24,27},{20,23},{28,31},{32,35}... | collective-permute-start | bytes 1572872 | tf_op jit(solution)/shard_map/ppermute | solution.py:47
  108.2 31.3 %collective-permute-start.28 = (bf16[64,8192]{1,0:T(8,128)(2,1)}, bf16[64,8192]{1,0:T(8,128)(2,1)}, u32[]{:S(2)}, u32[]{:S(2)}) collective-permute-start(bf16[64,8192]{1,0:T(8,128)(2,1)} %pad_maximum_fusion.2), channel_id=1, source_target_pairs={{0,96},{8,104},{4,100},{12,108},{16,112},{24,120},{20,116},{28,124... | collective-permute-start | bytes 3145736 | tf_op jit(solution)/shard_map/ppermute | solution.py:47
  109.7 29.7 %collective-permute-start.26 = (bf16[64,8192]{1,0:T(8,128)(2,1)}, bf16[64,8192]{1,0:T(8,128)(2,1)}, u32[]{:S(2)}, u32[]{:S(2)}) collective-permute-start(bf16[64,8192]{1,0:T(8,128)(2,1)} %pad_maximum_fusion.1), channel_id=1, source_target_pairs={{0,32},{8,40},{4,36},{12,44},{16,48},{24,56},{20,52},{28,60},{32,6... | collective-permute-start | bytes 3145736 | tf_op jit(solution)/shard_map/ppermute | solution.py:47
  113.5 19.0 %collective-permute-start.34 = (bf16[256,1024]{1,0:T(8,128)(2,1)}, bf16[256,1024]{1,0:T(8,128)(2,1)}, u32[]{:S(2)}, u32[]{:S(2)}) collective-permute-start(bf16[256,1024]{1,0:T(8,128)(2,1)} %slice.149), channel_id=1, source_target_pairs={{0,1},{8,9},{4,5},{12,13},{16,17},{24,25},{20,21},{28,29},{32,33},... | collective-permute-start | bytes 1572872 | tf_op jit(solution)/shard_map/ppermute | solution.py:47
  114.4 18.0 %collective-permute-start.35 = (bf16[256,1024]{1,0:T(8,128)(2,1)}, bf16[256,1024]{1,0:T(8,128)(2,1)}, u32[]{:S(2)}, u32[]{:S(2)}) collective-permute-start(bf16[256,1024]{1,0:T(8,128)(2,1)} %slice.150), channel_id=1, source_target_pairs={{0,3},{8,11},{4,7},{12,15},{16,19},{24,27},{20,23},{28,31},{32,35}... | collective-permute-start | bytes 1572872 | tf_op jit(solution)/shard_map/ppermute | solution.py:47
  132.4 7.0 %collective-permute-start.36 = (f32[56,512]{1,0:T(8,128)S(1)}, f32[56,512]{1,0:T(8,128)S(1)}, u32[]{:S(2)}, u32[]{:S(2)}) collective-permute-start(f32[56,512]{1,0:T(8,128)S(1)} %get-tuple-element.99), channel_id=1, source_target_pairs={{0,4},{8,12},{4,0},{12,8},{16,20},{24,28},{20,16},{28,24},{32,36},... | collective-permute-start | bytes 344072 | tf_op jit(solution)/shard_map/ppermute | solution.py:47
  136.1 13.2 %collective-permute-start.37 = (bf16[256,1024]{1,0:T(8,128)(2,1)S(1)}, bf16[256,1024]{1,0:T(8,128)(2,1)S(1)}, u32[]{:S(2)}, u32[]{:S(2)}) collective-permute-start(bf16[256,1024]{1,0:T(8,128)(2,1)S(1)} %copy-done.17), channel_id=1, source_target_pairs={{0,1},{8,9},{4,5},{12,13},{16,17},{24,25},{20,21},{28,29},{32,33},... | collective-permute-start | bytes 1572872 | tf_op jit(solution)/shard_map/ppermute | solution.py:47
  136.2 13.1 %collective-permute-start.38 = (bf16[256,1024]{1,0:T(8,128)(2,1)S(1)}, bf16[256,1024]{1,0:T(8,128)(2,1)S(1)}, u32[]{:S(2)}, u32[]{:S(2)}) collective-permute-start(bf16[256,1024]{1,0:T(8,128)(2,1)S(1)} %copy-done.18), channel_id=1, source_target_pairs={{0,3},{8,11},{4,7},{12,15},{16,19},{24,27},{20,23},{28,31},{32,35}... | collective-permute-start | bytes 1572872 | tf_op jit(solution)/shard_map/ppermute | solution.py:47
  141.9 14.3 %collective-permute-start.30 = (bf16[32,4096]{1,0:T(8,128)(2,1)S(1)}, bf16[32,4096]{1,0:T(8,128)(2,1)S(1)}, u32[]{:S(2)}, u32[]{:S(2)}) collective-permute-start(bf16[32,4096]{1,0:T(8,128)(2,1)S(1)} %get-tuple-element.121), channel_id=1, source_target_pairs={{0,20},{8,28},{4,0},{12,8},{16,4},{24,12},{20,16},{28,24},{32,52},... | collective-permute-start | bytes 786440 | tf_op jit(solution)/shard_map/ppermute | solution.py:47
  149.3 11.2 %collective-permute-start.39 = (f32[72,512]{1,0:T(8,128)S(1)}, f32[72,512]{1,0:T(8,128)S(1)}, u32[]{:S(2)}, u32[]{:S(2)}) collective-permute-start(f32[72,512]{1,0:T(8,128)S(1)} %pad_maximum_fusion.4.refs_7_), channel_id=1, source_target_pairs={{0,1},{8,9},{4,5},{12,13},{16,17},{24,25},{20,21},{28,29},{32,33},... | collective-permute-start | bytes 442376 | tf_op jit(solution)/shard_map/ppermute | solution.py:47
  149.3 11.2 %collective-permute-start.40 = (f32[72,512]{1,0:T(8,128)S(1)}, f32[72,512]{1,0:T(8,128)S(1)}, u32[]{:S(2)}, u32[]{:S(2)}) collective-permute-start(f32[72,512]{1,0:T(8,128)S(1)} %pad_maximum_fusion.4.refs_7_), channel_id=1, source_target_pairs={{0,2},{8,10},{4,6},{12,14},{16,18},{24,26},{20,22},{28,30},{32,34}... | collective-permute-start | bytes 442376 | tf_op jit(solution)/shard_map/ppermute | solution.py:47
  153.7 6.8 %collective-permute-start.41 = (f32[72,512]{1,0:T(8,128)S(1)}, f32[72,512]{1,0:T(8,128)S(1)}, u32[]{:S(2)}, u32[]{:S(2)}) collective-permute-start(f32[72,512]{1,0:T(8,128)S(1)} %pad_maximum_fusion.4.refs_7_), channel_id=1, source_target_pairs={{0,3},{8,11},{4,7},{12,15},{16,19},{24,27},{20,23},{28,31},{32,35}... | collective-permute-start | bytes 442376 | tf_op jit(solution)/shard_map/ppermute | solution.py:47
  153.7 12.4 %collective-permute-start.29 = (bf16[32,4096]{1,0:T(8,128)(2,1)S(1)}, bf16[32,4096]{1,0:T(8,128)(2,1)S(1)}, u32[]{:S(2)}, u32[]{:S(2)}) collective-permute-start(bf16[32,4096]{1,0:T(8,128)(2,1)S(1)} %get-tuple-element.120), channel_id=1, source_target_pairs={{0,16},{8,24},{4,20},{12,28},{16,0},{24,8},{20,4},{28,12},{32,48},... | collective-permute-start | bytes 786440 | tf_op jit(solution)/shard_map/ppermute | solution.py:47
  156.2 10.0 %collective-permute-start.31 = (bf16[32,4096]{1,0:T(8,128)(2,1)S(1)}, bf16[32,4096]{1,0:T(8,128)(2,1)S(1)}, u32[]{:S(2)}, u32[]{:S(2)}) collective-permute-start(bf16[32,4096]{1,0:T(8,128)(2,1)S(1)} %collective-permute-done.30), channel_id=1, source_target_pairs={{0,20},{8,28},{4,0},{12,8},{16,4},{24,12},{20,16},{28,24},{32,52},... | collective-permute-start | bytes 786440 | tf_op jit(solution)/shard_map/ppermute | solution.py:47
  (21 other events, 286.5 us)

commit v12 on v3

--- a/solution.py
+++ b/solution.py
@@ -143,7 +143,7 @@
             return now, lag
 
         zero = [zero_ref[...]] * modes
-        now, lag = lax.fori_loop(0, span, step, (zero, zero), unroll=4)
+        now, lag = lax.fori_loop(0, span, step, (zero, zero), unroll=8)
         for m in range(modes):
             sub_ref[tile, strided(m, modes)] = now[m]
             sub_ref[tile, strided(SUBS * modes + m, modes)] = lag[m]
@@ -193,7 +193,7 @@
             return now
 
         first = [lead_ref[tile, strided(m, modes)] for m in range(modes)]
-        lax.fori_loop(0, span, step, first, unroll=4)
+        lax.fori_loop(0, span, step, first, unroll=8)
         gated_ref[:, lanes] = (query_ref[:, lanes].astype(F32) * pre_ref[tile]).astype(BF16)
     part = length // (RING * 4)
     y, high, core, _, _ = places()
@@ -218,40 +218,34 @@
         grad = grad_ref[:, lanes].astype(F32)
         grad_query_ref[:, lanes] = (grad * pre_ref[tile]).astype(BF16)
         back_ref[tile] = grad * query_ref[:, lanes].astype(F32)
-        decay = [spread(decay_ref, m, lanes) for m in range(modes)]
-
-        def back_step(i, now):
-            g = back_ref[tile, strided(span - 1 - i, span)]
-            return [decay[m] * now[m] + g for m in range(modes)]
-
-        zero = [zero_ref[...]] * modes
-        now = lax.fori_loop(0, span, back_step, zero, unroll=4)
-        for m in range(modes):
-            sub_ref[tile, strided(m, modes)] = now[m]
+        skip = zero_ref[...]
         for low in range(0, modes, half):
             group = range(low, low + half)
             decay = [spread(decay_ref, m, lanes) for m in group]
 
-            def pair_step(i, carry):
-                state, lag, pair, lag_pair, skip = carry
-                place = strided(i, span)
+            def back_step(i, carry):
+                start, lag, pair, lag_pair, skip = carry
+                place = strided(span - 1 - i, span)
                 u = drive_ref[tile, place]
                 g = back_ref[tile, place]
-                lag = [decay[m] * (lag[m] + state[m]) for m in range(half)]
-                state = [decay[m] * state[m] + u for m in range(half)]
-                pair = [pair[m] + g * state[m] for m in range(half)]
-                lag_pair = [lag_pair[m] + g * lag[m] for m in range(half)]
-                return state, lag, pair, lag_pair, skip + g * u
-
-            state = [lead_ref[tile, strided(m, modes)] for m in group]
-            lag = [lead_ref[tile, strided(SUBS * modes + m, modes)] for m in group]
+                lag = [decay[m] * (lag[m] + start[m]) for m in range(half)]
+                start = [decay[m] * start[m] + g for m in range(half)]
+                pair = [pair[m] + u * start[m] for m in range(half)]
+                lag_pair = [lag_pair[m] + u * lag[m] for m in range(half)]
+                return start, lag, pair, lag_pair, (skip + g * u if low == 0 else skip)
+
             zero = [zero_ref[...]] * half
-            state, lag, pair, lag_pair, skip = lax.fori_loop(
-                0, span, pair_step, (state, lag, zero, zero, zero[0]), unroll=4
+            start, lag, pair, lag_pair, skip = lax.fori_loop(
+                0, span, back_step, (zero, zero, zero, zero, skip), unroll=8
             )
             for m in range(half):
-                part_ref[tile, strided(low + m, modes)] = pair[m]
-                part_ref[tile, strided(SUBS * modes + low + m, modes)] = lag_pair[m]
+                state = lead_ref[tile, strided(low + m, modes)]
+                lagged = lead_ref[tile, strided(SUBS * modes + low + m, modes)]
+                once = decay[m] * start[m]
+                twice = decay[m] * (lag[m] + start[m])
+                sub_ref[tile, strided(low + m, modes)] = start[m]
+                part_ref[tile, strided(low + m, modes)] = pair[m] + state * once
+                part_ref[tile, strided(SUBS * modes + low + m, modes)] = lag_pair[m] + state * twice + lagged * once
         total = jnp.sum(skip, axis=0, keepdims=True)
         sums_ref[pl.ds(3 * modes, SUBS), lanes] = jnp.broadcast_to(total, (SUBS, LANES))
         power = jnp.exp(-span * jnp.exp(log_ref[:, lanes]))
@@ -306,7 +300,7 @@
             return now
 
         first = [lead_ref[tile, strided(m, modes)] for m in range(modes)]
-        lax.fori_loop(0, span, step, first, unroll=4)
+        lax.fori_loop(0, span, step, first, unroll=8)
         drive_grad = drive_grad_ref[tile]
         grad_key_ref[:, lanes] = (drive_grad * value_ref[:, lanes].astype(F32)).astype(BF16)
         grad_value_ref[:, lanes] = (drive_grad * key_ref[:, lanes].astype(F32)).astype(BF16)

time: 153 us -> 151 us (0.987)
  Pallas kernels: 30 us -> 27.2 us
    pallas_call x4, Pallas kernels: 23.1 us -> 20.4 us  [call(): pl.pallas_call(body, out_shape=[jax.ShapeDtypeStruct(o.shape, o.dtype) fo...]
  transfers between devices with their start and end apart: 42 -> 42, of which waited for: 16 -> 17; matrix products, arithmetic and copies ran while one was open for 19% -> 19% of each run, Pallas kernels for 20% -> 18%
where the time goes in v12:
time: 151 us; the launch traced here: 150 us
  starting transfers between devices  50.1 us (33%)
  waiting for transfers between devices  37.5 us (25%)
  Pallas kernels  27.2 us (18%)
  local copies, waits for them, and re-layouts  15.6 us (10%)
  matrix products  10.6 us (7%)
  other arithmetic  7.95 us (5%)
    ppermute x42, starting transfers between devices, hop(): return lax.ppermute(value, ('chan', 'seq'), moves)  50.1 us
    ppermute x42, waiting for transfers between devices, hop(): return lax.ppermute(value, ('chan', 'seq'), moves)  37.5 us
    pallas_call x4, Pallas kernels, call(): pl.pallas_call(body, out_shape=[jax.ShapeDtypeStruct(o.shape, o.dtype) fo...  20.4 us
    dynamic_update_slice x16, local copies, waits for them, and re-layouts, place_blocks(): lax.dynamic_update_slice(whole, part[None, None, :, None], (side, row, 0,...  6.98 us
    pallas_call x1, Pallas kernels, project(): pl.pallas_call(project_tile, grid=(width // tile,), out_shape=[jax.ShapeD...  6.86 us
    dot_general x4, matrix products, weigh(): lax.dot_general(gated, columns, (((0,), (0,)), ((), ())), preferred_eleme...  6.1 us
    dot_general x1, matrix products, local(): lax.dot_general(cot_rows, low_weight, (((1,), (1,)), ((), ())), preferred...  4.52 us
  transfers between devices with their start and end apart: 42, of which 17 were waited for; matrix products, arithmetic and copies ran while one was open for 19% of the time, Pallas kernels for 18%

profile of v12, /device:TPU:0, one launch (start us, length us, event | category | flops | bytes accessed | tf_op | source)
XLA Modules:
  0.0 150.2 jit_solution(8885107978017431831)
XLA Ops:
  0.7 1.1 constant_dynamic-slice_fusion.1
  1.8 2.1 %collective-permute-start.1 = (bf16[32,4096]{1,0:T(8,128)(2,1)S(1)}, bf16[32,4096]{1,0:T(8,128)(2,1)S(1)}, u32[]{:S(2)}, u32[]{:S(2)}) collective-permute-start(bf16[32,4096]{1,0:T(8,128)(2,1)S(1)} %get-tuple-element.127), channel_id=1, source_target_pairs={{0,4},{8,12},{4,16},{12,24},{16,20},{24,28},{20,0},{28,8},{32,36},... | collective-permute-start | bytes 786440 | tf_op jit(solution)/shard_map/ppermute | solution.py:47
  3.9 2.2 %collective-permute-start.2 = (bf16[32,4096]{1,0:T(8,128)(2,1)S(1)}, bf16[32,4096]{1,0:T(8,128)(2,1)S(1)}, u32[]{:S(2)}, u32[]{:S(2)}) collective-permute-start(bf16[32,4096]{1,0:T(8,128)(2,1)S(1)} %get-tuple-element.127), channel_id=1, source_target_pairs={{0,20},{8,28},{4,0},{12,8},{16,4},{24,12},{20,16},{28,24},{32,52},... | collective-permute-start | bytes 786440 | tf_op jit(solution)/shard_map/ppermute | solution.py:47
  6.1 1.8 %collective-permute-start = (bf16[32,4096]{1,0:T(8,128)(2,1)S(1)}, bf16[32,4096]{1,0:T(8,128)(2,1)S(1)}, u32[]{:S(2)}, u32[]{:S(2)}) collective-permute-start(bf16[32,4096]{1,0:T(8,128)(2,1)S(1)} %get-tuple-element.126), channel_id=1, source_target_pairs={{0,16},{8,24},{4,20},{12,28},{16,0},{24,8},{20,4},{28,12},{32,48},... | collective-permute-start | bytes 786440 | tf_op jit(solution)/shard_map/ppermute | solution.py:47
  7.9 4.4 %collective-permute-done.1 = bf16[32,4096]{1,0:T(8,128)(2,1)S(1)} collective-permute-done((bf16[32,4096]{1,0:T(8,128)(2,1)S(1)}, bf16[32,4096]{1,0:T(8,128)(2,1)S(1)}, u32[]{:S(2)}, u32[]{:S(2)}) %collective-permute-start.1) | collective-permute-done | bytes 262176 | tf_op jit(solution)/shard_map/ppermute | solution.py:47
  12.3 5.0 %collective-permute-done.2 = bf16[32,4096]{1,0:T(8,128)(2,1)S(1)} collective-permute-done((bf16[32,4096]{1,0:T(8,128)(2,1)S(1)}, bf16[32,4096]{1,0:T(8,128)(2,1)S(1)}, u32[]{:S(2)}, u32[]{:S(2)}) %collective-permute-start.2) | collective-permute-done | bytes 262176 | tf_op jit(solution)/shard_map/ppermute | solution.py:47
  17.5 1.7 %collective-permute-done = bf16[32,4096]{1,0:T(8,128)(2,1)S(1)} collective-permute-done((bf16[32,4096]{1,0:T(8,128)(2,1)S(1)}, bf16[32,4096]{1,0:T(8,128)(2,1)S(1)}, u32[]{:S(2)}, u32[]{:S(2)}) %collective-permute-start) | collective-permute-done | bytes 262176 | tf_op jit(solution)/shard_map/ppermute | solution.py:47
  20.4 1.6 %collective-permute-start.5 = (bf16[2,32,4096]{2,1,0:T(8,128)(2,1)}, bf16[2,32,4096]{2,1,0:T(8,128)(2,1)S(1)}, u32[]{:S(2)}, u32[]{:S(2)}) collective-permute-start(bf16[2,32,4096]{2,1,0:T(8,128)(2,1)} %get-tuple-element.125), channel_id=1, source_target_pairs={{0,32},{8,40},{4,36},{12,44},{16,48},{24,56},{20,52},{28,60},{32,6... | collective-permute-start | bytes 1572872 | tf_op jit(solution)/shard_map/ppermute | solution.py:47
  22.2 1.7 %collective-permute-start.6 = (bf16[2,32,4096]{2,1,0:T(8,128)(2,1)}, bf16[2,32,4096]{2,1,0:T(8,128)(2,1)S(1)}, u32[]{:S(2)}, u32[]{:S(2)}) collective-permute-start(bf16[2,32,4096]{2,1,0:T(8,128)(2,1)} %get-tuple-element.124), channel_id=1, source_target_pairs={{0,96},{8,104},{4,100},{12,108},{16,112},{24,120},{20,116},{28,124... | collective-permute-start | bytes 1572872 | tf_op jit(solution)/shard_map/ppermute | solution.py:47
  23.9 3.2 %forward_ends.1 = (f32[32,512]{1,0:T(8,128)S(1)}, f32[4,256,128]{2,1,0:T(8,128)S(1)}, f32[4,512,128]{2,1,0:T(8,128)S(1)}) custom-call(bf16[512,512]{1,0:T(8,128)(2,1)S(1)} %copy-done, bf16[512,512]{1,0:T(8,128)(2,1)S(1)} %copy-done.1, f32[16,512]{1,0:T(8,128)S(1)} %copy-done.3), custom_call_target="tpu_custom_call" | custom-call | flops 115000000 | tf_op jit(solution)/shard_map/forward_ends/pallas_call | solution.py:311
  27.2 1.2 collective-permute-start.7
  29.5 2.0 %collective-permute-done.7 = f32[32,512]{1,0:T(8,128)S(1)} collective-permute-done((f32[32,512]{1,0:T(8,128)S(1)}, f32[32,512]{1,0:T(8,128)S(1)}, u32[]{:S(2)}, u32[]{:S(2)}) %collective-permute-start.7) | collective-permute-done | bytes 65568 | tf_op jit(solution)/shard_map/ppermute | solution.py:47
  31.8 4.7 %collective-permute-done.5 = bf16[2,32,4096]{2,1,0:T(8,128)(2,1)S(1)} collective-permute-done((bf16[2,32,4096]{2,1,0:T(8,128)(2,1)}, bf16[2,32,4096]{2,1,0:T(8,128)(2,1)S(1)}, u32[]{:S(2)}, u32[]{:S(2)}) %collective-permute-start.5) | collective-permute-done | bytes 524320 | tf_op jit(solution)/shard_map/ppermute | solution.py:47
  36.5 1.8 %collective-permute-start.4 = (bf16[2,32,4096]{2,1,0:T(8,128)(2,1)}, bf16[2,32,4096]{2,1,0:T(8,128)(2,1)S(1)}, u32[]{:S(2)}, u32[]{:S(2)}) collective-permute-start(bf16[2,32,4096]{2,1,0:T(8,128)(2,1)} %get-tuple-element.125), channel_id=1, source_target_pairs={{0,96},{8,104},{4,100},{12,108},{16,112},{24,120},{20,116},{28,124... | collective-permute-start | bytes 1572872 | tf_op jit(solution)/shard_map/ppermute | solution.py:47
  38.3 1.5 collective-permute-start.8
  39.8 2.7 %collective-permute-start.9 = (f32[64,512]{1,0:T(8,128)S(1)}, f32[64,512]{1,0:T(8,128)S(1)}, u32[]{:S(2)}, u32[]{:S(2)}) collective-permute-start(f32[64,512]{1,0:T(8,128)S(1)} %pad_maximum_fusion.5.refs_6_), channel_id=1, source_target_pairs={{0,2},{8,10},{4,6},{12,14},{16,18},{24,26},{20,22},{28,30},{32,34}... | collective-permute-start | bytes 393224 | tf_op jit(solution)/shard_map/ppermute | solution.py:47
  43.7 1.5 %collective-permute-start.10 = (f32[64,512]{1,0:T(8,128)S(1)}, f32[64,512]{1,0:T(8,128)S(1)}, u32[]{:S(2)}, u32[]{:S(2)}) collective-permute-start(f32[64,512]{1,0:T(8,128)S(1)} %pad_maximum_fusion.5.refs_6_), channel_id=1, source_target_pairs={{0,3},{8,11},{4,7},{12,15},{16,19},{24,27},{20,23},{28,31},{32,35}... | collective-permute-start | bytes 393224 | tf_op jit(solution)/shard_map/ppermute | solution.py:47
  46.3 1.5 collective-permute-done.9.refs_8_
  48.8 3.8 %forward_full.1 = (bf16[512,512]{1,0:T(8,128)(2,1)S(1)}, bf16[512,512]{1,0:T(8,128)(2,1)S(1)}, f32[4,512,128]{2,1,0:T(8,128)S(1)}, f32[4,256,128]{2,1,0:T(8,128)S(1)}) custom-call(bf16[512,512]{1,0:T(8,128)(2,1)S(1)} %copy-done.2, f32[4,512,128]{2,1,0:T(8,128)S(1)} %get-tuple-element.65.refs_1_.drive_ref, f32[4,256,128]{2,1,0:T(8,128)S(1)} %get-tuple-element.66.refs_2_, ...), custom_call_target="tpu_custom_call" | custom-call | flops 115000000 | tf_op jit(solution)/shard_map/forward_full/pallas_call | solution.py:311
  53.2 3.0 %collective-permute-start.18 = (bf16[2,32,4096]{2,1,0:T(8,128)(2,1)S(1)}, bf16[2,32,4096]{2,1,0:T(8,128)(2,1)S(1)}, u32[]{:S(2)}, u32[]{:S(2)}) collective-permute-start(bf16[2,32,4096]{2,1,0:T(8,128)(2,1)S(1)} %collective-permute-done.6), channel_id=1, source_target_pairs={{0,96},{8,104},{4,100},{12,108},{16,112},{24,120},{20,116},{28,124... | collective-permute-start | bytes 1572872 | tf_op jit(solution)/shard_map/ppermute | solution.py:47
  56.2 1.1 collective-permute-start.23
  58.2 6.9 %project.1 = (bf16[64,8192]{1,0:T(8,128)(2,1)S(1)}, bf16[192,8192]{1,0:T(8,128)(2,1)S(1)}, bf16[64,8192]{1,0:T(8,128)(2,1)S(1)}, bf16[192,8192]{1,0:T(8,128)(2,1)S(1)}) custom-call(bf16[512,512]{1,0:T(8,128)(2,1)S(1)} %get-tuple-element.70.rows_ref, bf16[512,8192]{1,0:T(8,128)(2,1)S(1)} %bitcast.83), custom_call_target="tpu_custom_call" | custom-call | flops 4294967296 | bytes 16777216 | tf_op jit(solution)/shard_map/project/pallas_call | solution.py:92
  70.4 1.9 %constant_dynamic-update-slice_fusion = bf16[1024,512]{1,0:T(8,128)(2,1)} fusion(bf16[1024,512]{1,0:T(8,128)(2,1)} %constant_dynamic-update-slice_fusion.1, bf16[512,512]{1,0:T(8,128)(2,1)} %collective-permute-done.23), kind=kLoop, calls=%fused_computation.61 | loop fusion | bytes 1048576 | tf_op jit(solution)/shard_map/concatenate | solution.py:373
  72.3 1.2 bitcast_dynamic-update-slice_fusion.3
  74.9 1.7 %collective-permute-start.24 = (bf16[32,8192]{1,0:T(8,128)(2,1)S(1)}, bf16[32,8192]{1,0:T(8,128)(2,1)S(1)}, u32[]{:S(2)}, u32[]{:S(2)}) collective-permute-start(bf16[32,8192]{1,0:T(8,128)(2,1)S(1)} %get-tuple-element.122), channel_id=1, source_target_pairs={{0,32},{8,40},{4,36},{12,44},{16,48},{24,56},{20,52},{28,60},{32,6... | collective-permute-start | bytes 1572872 | tf_op jit(solution)/shard_map/ppermute | solution.py:47
  78.4 1.6 %copy-done.6 = bf16[192,8192]{1,0:T(8,128)(2,1)} copy-done((bf16[192,8192]{1,0:T(8,128)(2,1)}, bf16[192,8192]{1,0:T(8,128)(2,1)S(1)}, u32[]{:S(2)}) %copy-start.6) | copy-done | bytes 3145752
  80.0 2.3 %multiply_convert_fusion.3 = bf16[512,1024]{1,0:T(8,128)(2,1)} fusion(bf16[1024,512]{1,0:T(8,128)(2,1)S(1)} %copy-done.9, bf16[1024,4096]{1,0:T(8,128)(2,1)S(1)} %bitcast.84, s32[]{:T(128)S(6)} %select_n.130), kind=kOutput, calls=%fused_computation.14 | convolution fusion | flops 1074790400 | bytes 4194308 | tf_op jit(solution)/shard_map/dot_general | solution.py:110
  82.3 4.5 %fusion = f32[1024,512]{1,0:T(8,128)S(1)} fusion(bf16[1024,4096]{1,0:T(8,128)(2,1)S(1)} %bitcast.85, bf16[512,8192]{1,0:T(8,128)(2,1)S(1)} %bitcast.83, s32[]{:T(128)S(6)} %select_n.116), kind=kOutput, calls=%fused_computation | convolution fusion | flops 4294967296 | bytes 14680068 | tf_op jit(solution)/shard_map/dot_general | solution.py:385
  86.9 2.1 %convert_add_fusion.2 = (f32[64,8192]{1,0:T(8,128)S(1)}, f32[64,8192]{1,0:T(8,128)S(1)}) fusion(bf16[192,8192]{1,0:T(8,128)(2,1)} %copy-done.6, bf16[192,8192]{1,0:T(8,128)(2,1)S(1)} %get-tuple-element.71), kind=kLoop, calls=%fused_computation.13 | loop fusion | flops 3145728 | bytes 8388608 | tf_op jit(solution)/shard_map/add | solution.py:76
  89.2 1.2 collective-permute-start.27
  92.8 1.1 collective-permute-start.32
  94.0 2.2 %collective-permute-start.33 = (bf16[256,1024]{1,0:T(8,128)(2,1)S(1)}, bf16[256,1024]{1,0:T(8,128)(2,1)S(1)}, u32[]{:S(2)}, u32[]{:S(2)}) collective-permute-start(bf16[256,1024]{1,0:T(8,128)(2,1)S(1)} %get-tuple-element.118), channel_id=1, source_target_pairs={{0,3},{8,11},{4,7},{12,15},{16,19},{24,27},{20,23},{28,31},{32,35}... | collective-permute-start | bytes 1572872 | tf_op jit(solution)/shard_map/ppermute | solution.py:47
  96.1 1.3 multiply_convert_fusion.2
  97.4 1.3 multiply_convert_fusion.1
  98.8 8.7 %collective-permute-done.32 = bf16[256,1024]{1,0:T(8,128)(2,1)S(1)} collective-permute-done((bf16[256,1024]{1,0:T(8,128)(2,1)S(1)}, bf16[256,1024]{1,0:T(8,128)(2,1)S(1)}, u32[]{:S(2)}, u32[]{:S(2)}) %collective-permute-start.32) | collective-permute-done | bytes 524320 | tf_op jit(solution)/shard_map/ppermute | solution.py:47
  108.6 2.6 %collective-permute-start.35 = (bf16[256,1024]{1,0:T(8,128)(2,1)S(1)}, bf16[256,1024]{1,0:T(8,128)(2,1)S(1)}, u32[]{:S(2)}, u32[]{:S(2)}) collective-permute-start(bf16[256,1024]{1,0:T(8,128)(2,1)S(1)} %slice.150), channel_id=1, source_target_pairs={{0,3},{8,11},{4,7},{12,15},{16,19},{24,27},{20,23},{28,31},{32,35}... | collective-permute-start | bytes 1572872 | tf_op jit(solution)/shard_map/ppermute | solution.py:47
  111.2 1.3 multiply_convert_fusion
  112.7 8.3 %backward_ends.1 = (bf16[512,512]{1,0:T(8,128)(2,1)}, f32[4,512,128]{2,1,0:T(8,128)S(1)}, f32[56,512]{1,0:T(8,128)S(1)}, f32[4,128,128]{2,1,0:T(8,128)S(1)}) custom-call(f32[512,512]{1,0:T(8,128)S(1)} %convert_add_fusion.3.grad_ref, bf16[512,512]{1,0:T(8,128)(2,1)S(1)} %copy-done.2, f32[4,512,128]{2,1,0:T(8,128)S(1)} %get-tuple-element.91.pre_ref, ...), custom_call_target="tpu_custom_call" | custom-call | flops 2300000000 | tf_op jit(solution)/shard_map/backward_ends/pallas_call | solution.py:311
  121.0 3.0 %collective-permute-done.34 = bf16[256,1024]{1,0:T(8,128)(2,1)S(1)} collective-permute-done((bf16[256,1024]{1,0:T(8,128)(2,1)S(1)}, bf16[256,1024]{1,0:T(8,128)(2,1)S(1)}, u32[]{:S(2)}, u32[]{:S(2)}) %collective-permute-start.34) | collective-permute-done | bytes 524320 | tf_op jit(solution)/shard_map/ppermute | solution.py:47
  124.0 1.5 %collective-permute-start.38 = (bf16[256,1024]{1,0:T(8,128)(2,1)S(1)}, bf16[256,1024]{1,0:T(8,128)(2,1)S(1)}, u32[]{:S(2)}, u32[]{:S(2)}) collective-permute-start(bf16[256,1024]{1,0:T(8,128)(2,1)S(1)} %add_convert_fusion.3), channel_id=1, source_target_pairs={{0,3},{8,11},{4,7},{12,15},{16,19},{24,27},{20,23},{28,31},{32,35}... | collective-permute-start | bytes 1572872 | tf_op jit(solution)/shard_map/ppermute | solution.py:47
  125.5 1.1 collective-permute-start.36
  126.7 1.7 %fusion.26 = (bf16[64,8192]{1,0:T(8,128)(2,1)S(1)}, f32[64,8192]{1,0:T(8,128)S(1)}) fusion(bf16[64,8192]{1,0:T(8,128)(2,1)S(1)} %collective-permute-done.27, bf16[64,8192]{1,0:T(8,128)(2,1)S(1)} %collective-permute-done.25, bf16[192,8192]{1,0:T(8,128)(2,1)} %copy-done.6, bf16[192,8192]{1,0:T(8,128)(2,1)S(1)} %get-tuple-element.71), kind=kLoop, calls=%fused_computation.70 | loop fusion | flops 4194304 | bytes 7340032 | tf_op jit(solution)/shard_map/convert.3
  128.5 1.7 %collective-permute-start.29 = (bf16[32,4096]{1,0:T(8,128)(2,1)S(1)}, bf16[32,4096]{1,0:T(8,128)(2,1)S(1)}, u32[]{:S(2)}, u32[]{:S(2)}) collective-permute-start(bf16[32,4096]{1,0:T(8,128)(2,1)S(1)} %get-tuple-element.121), channel_id=1, source_target_pairs={{0,20},{8,28},{4,0},{12,8},{16,4},{24,12},{20,16},{28,24},{32,52},... | collective-permute-start | bytes 786440 | tf_op jit(solution)/shard_map/ppermute | solution.py:47
  130.1 1.4 collective-permute-start.28
  131.7 1.1 collective-permute-done.37
  133.5 5.0 %collective-permute-start.40 = (f32[72,512]{1,0:T(8,128)S(1)}, f32[72,512]{1,0:T(8,128)S(1)}, u32[]{:S(2)}, u32[]{:S(2)}) collective-permute-start(f32[72,512]{1,0:T(8,128)S(1)} %pad_maximum_fusion.4.refs_7_), channel_id=1, source_target_pairs={{0,2},{8,10},{4,6},{12,14},{16,18},{24,26},{20,22},{28,30},{32,34}... | collective-permute-start | bytes 442376 | tf_op jit(solution)/shard_map/ppermute | solution.py:47
  138.5 2.0 %collective-permute-start.30 = (bf16[32,4096]{1,0:T(8,128)(2,1)S(1)}, bf16[32,4096]{1,0:T(8,128)(2,1)S(1)}, u32[]{:S(2)}, u32[]{:S(2)}) collective-permute-start(bf16[32,4096]{1,0:T(8,128)(2,1)S(1)} %collective-permute-done.29), channel_id=1, source_target_pairs={{0,20},{8,28},{4,0},{12,8},{16,4},{24,12},{20,16},{28,24},{32,52},... | collective-permute-start | bytes 786440 | tf_op jit(solution)/shard_map/ppermute | solution.py:47
  143.7 5.0 %backward_full.1 = (bf16[512,512]{1,0:T(8,128)(2,1)}, bf16[512,512]{1,0:T(8,128)(2,1)}, f32[16,512]{1,0:T(8,128)}, f32[16,512]{1,0:T(8,128)}, f32[8,512]{1,0:T(8,128)S(1)}) custom-call(bf16[512,512]{1,0:T(8,128)(2,1)S(1)} %copy-done, bf16[512,512]{1,0:T(8,128)(2,1)S(1)} %copy-done.1, f32[4,512,128]{2,1,0:T(8,128)S(1)} %get-tuple-element.94.refs_2_, ...), custom_call_target="tpu_custom_call" | custom-call | flops 115000000 | tf_op jit(solution)/shard_map/backward_full/pallas_call | solution.py:311
  (125 shorter events, 25.6 us)
Async XLA Ops:
  0.6 23.3 %copy-start.3 = (f32[16,512]{1,0:T(8,128)S(1)}, f32[16,512]{1,0:T(8,128)}, u32[]{:S(2)}) copy-start(f32[16,512]{1,0:T(8,128)} %refs_4_.3) | copy-start | bytes 98308
  1.8 10.5 %collective-permute-start.1 = (bf16[32,4096]{1,0:T(8,128)(2,1)S(1)}, bf16[32,4096]{1,0:T(8,128)(2,1)S(1)}, u32[]{:S(2)}, u32[]{:S(2)}) collective-permute-start(bf16[32,4096]{1,0:T(8,128)(2,1)S(1)} %get-tuple-element.127), channel_id=1, source_target_pairs={{0,4},{8,12},{4,16},{12,24},{16,20},{24,28},{20,0},{28,8},{32,36},... | collective-permute-start | bytes 786440 | tf_op jit(solution)/shard_map/ppermute | solution.py:47
  3.9 13.4 %collective-permute-start.2 = (bf16[32,4096]{1,0:T(8,128)(2,1)S(1)}, bf16[32,4096]{1,0:T(8,128)(2,1)S(1)}, u32[]{:S(2)}, u32[]{:S(2)}) collective-permute-start(bf16[32,4096]{1,0:T(8,128)(2,1)S(1)} %get-tuple-element.127), channel_id=1, source_target_pairs={{0,20},{8,28},{4,0},{12,8},{16,4},{24,12},{20,16},{28,24},{32,52},... | collective-permute-start | bytes 786440 | tf_op jit(solution)/shard_map/ppermute | solution.py:47
  6.1 13.0 %collective-permute-start = (bf16[32,4096]{1,0:T(8,128)(2,1)S(1)}, bf16[32,4096]{1,0:T(8,128)(2,1)S(1)}, u32[]{:S(2)}, u32[]{:S(2)}) collective-permute-start(bf16[32,4096]{1,0:T(8,128)(2,1)S(1)} %get-tuple-element.126), channel_id=1, source_target_pairs={{0,16},{8,24},{4,20},{12,28},{16,0},{24,8},{20,4},{28,12},{32,48},... | collective-permute-start | bytes 786440 | tf_op jit(solution)/shard_map/ppermute | solution.py:47
  19.3 29.4 %copy-start.2 = (bf16[512,512]{1,0:T(8,128)(2,1)S(1)}, bf16[512,512]{1,0:T(8,128)(2,1)}, u32[]{:S(2)}) copy-start(bf16[512,512]{1,0:T(8,128)(2,1)} %query_ref.1) | copy-start | bytes 1572868
  19.3 29.4 %copy-start.4 = (f32[16,512]{1,0:T(8,128)S(1)}, f32[16,512]{1,0:T(8,128)}, u32[]{:S(2)}) copy-start(f32[16,512]{1,0:T(8,128)} %refs_5_.1) | copy-start | bytes 98308
  19.3 29.4 %copy-start.5 = (f32[512]{0:T(512)S(1)}, f32[512]{0:T(512)}, u32[]{:S(2)}) copy-start(f32[512]{0:T(512)} %param.11) | copy-start | bytes 6148
  20.4 19.4 %collective-permute-start.11 = (bf16[2,32,4096]{2,1,0:T(8,128)(2,1)}, bf16[2,32,4096]{2,1,0:T(8,128)(2,1)}, u32[]{:S(2)}, u32[]{:S(2)}) collective-permute-start(bf16[2,32,4096]{2,1,0:T(8,128)(2,1)} %get-tuple-element.125), channel_id=1, source_target_pairs={{0,8},{8,0},{4,12},{12,4},{16,24},{24,16},{20,28},{28,20},{32,40},... | collective-permute-start | bytes 1572872 | tf_op jit(solution)/shard_map/ppermute | solution.py:47
  20.4 16.1 %collective-permute-start.5 = (bf16[2,32,4096]{2,1,0:T(8,128)(2,1)}, bf16[2,32,4096]{2,1,0:T(8,128)(2,1)S(1)}, u32[]{:S(2)}, u32[]{:S(2)}) collective-permute-start(bf16[2,32,4096]{2,1,0:T(8,128)(2,1)} %get-tuple-element.125), channel_id=1, source_target_pairs={{0,32},{8,40},{4,36},{12,44},{16,48},{24,56},{20,52},{28,60},{32,6... | collective-permute-start | bytes 1572872 | tf_op jit(solution)/shard_map/ppermute | solution.py:47
  22.0 21.7 %collective-permute-start.12 = (bf16[2,32,4096]{2,1,0:T(8,128)(2,1)}, bf16[2,32,4096]{2,1,0:T(8,128)(2,1)}, u32[]{:S(2)}, u32[]{:S(2)}) collective-permute-start(bf16[2,32,4096]{2,1,0:T(8,128)(2,1)} %get-tuple-element.124), channel_id=1, source_target_pairs={{0,8},{8,0},{4,12},{12,4},{16,24},{24,16},{20,28},{28,20},{32,40},... | collective-permute-start | bytes 1572872 | tf_op jit(solution)/shard_map/ppermute | solution.py:47
  22.2 16.1 %collective-permute-start.6 = (bf16[2,32,4096]{2,1,0:T(8,128)(2,1)}, bf16[2,32,4096]{2,1,0:T(8,128)(2,1)S(1)}, u32[]{:S(2)}, u32[]{:S(2)}) collective-permute-start(bf16[2,32,4096]{2,1,0:T(8,128)(2,1)} %get-tuple-element.124), channel_id=1, source_target_pairs={{0,96},{8,104},{4,100},{12,108},{16,112},{24,120},{20,116},{28,124... | collective-permute-start | bytes 1572872 | tf_op jit(solution)/shard_map/ppermute | solution.py:47
  27.1 31.0 %slice-start = ((s8[8388608]{0:T(1024)(128)(4,1)}), s8[4194304]{0:T(1024)(128)(4,1)S(1)}, s32[]{:S(2)}) async-start(s8[8388608]{0:T(1024)(128)(4,1)} %bitcast.82), calls=%async_computation | async-start | bytes 8388608
  27.2 4.3 %collective-permute-start.7 = (f32[32,512]{1,0:T(8,128)S(1)}, f32[32,512]{1,0:T(8,128)S(1)}, u32[]{:S(2)}, u32[]{:S(2)}) collective-permute-start(f32[32,512]{1,0:T(8,128)S(1)} %get-tuple-element.62), channel_id=1, source_target_pairs={{0,4},{8,12},{4,0},{12,8},{16,20},{24,28},{20,16},{28,24},{32,36},... | collective-permute-start | bytes 196616 | tf_op jit(solution)/shard_map/ppermute | solution.py:47
  29.4 28.8 %slice-start.1 = ((s8[8388608]{0:T(1024)(128)(4,1)}), s8[4194304]{0:T(1024)(128)(4,1)S(1)}, s32[]{:S(2)}) async-start(s8[8388608]{0:T(1024)(128)(4,1)} %bitcast.82), calls=%async_computation.1 | async-start | bytes 8388608
  31.5 21.7 %collective-permute-start.3 = (bf16[2,32,4096]{2,1,0:T(8,128)(2,1)}, bf16[2,32,4096]{2,1,0:T(8,128)(2,1)}, u32[]{:S(2)}, u32[]{:S(2)}) collective-permute-start(bf16[2,32,4096]{2,1,0:T(8,128)(2,1)} %get-tuple-element.124), channel_id=1, source_target_pairs={{0,32},{8,40},{4,36},{12,44},{16,48},{24,56},{20,52},{28,60},{32,6... | collective-permute-start | bytes 1572872 | tf_op jit(solution)/shard_map/ppermute | solution.py:47
  36.5 19.6 %collective-permute-start.4 = (bf16[2,32,4096]{2,1,0:T(8,128)(2,1)}, bf16[2,32,4096]{2,1,0:T(8,128)(2,1)S(1)}, u32[]{:S(2)}, u32[]{:S(2)}) collective-permute-start(bf16[2,32,4096]{2,1,0:T(8,128)(2,1)} %get-tuple-element.125), channel_id=1, source_target_pairs={{0,96},{8,104},{4,100},{12,108},{16,112},{24,120},{20,116},{28,124... | collective-permute-start | bytes 1572872 | tf_op jit(solution)/shard_map/ppermute | solution.py:47
  38.3 8.0 %collective-permute-start.8 = (f32[64,512]{1,0:T(8,128)S(1)}, f32[64,512]{1,0:T(8,128)S(1)}, u32[]{:S(2)}, u32[]{:S(2)}) collective-permute-start(f32[64,512]{1,0:T(8,128)S(1)} %pad_maximum_fusion.5.refs_6_), channel_id=1, source_target_pairs={{0,1},{8,9},{4,5},{12,13},{16,17},{24,25},{20,21},{28,29},{32,33},... | collective-permute-start | bytes 393224 | tf_op jit(solution)/shard_map/ppermute | solution.py:47
  39.8 8.0 %collective-permute-start.9 = (f32[64,512]{1,0:T(8,128)S(1)}, f32[64,512]{1,0:T(8,128)S(1)}, u32[]{:S(2)}, u32[]{:S(2)}) collective-permute-start(f32[64,512]{1,0:T(8,128)S(1)} %pad_maximum_fusion.5.refs_6_), channel_id=1, source_target_pairs={{0,2},{8,10},{4,6},{12,14},{16,18},{24,26},{20,22},{28,30},{32,34}... | collective-permute-start | bytes 393224 | tf_op jit(solution)/shard_map/ppermute | solution.py:47
  43.7 5.0 %collective-permute-start.10 = (f32[64,512]{1,0:T(8,128)S(1)}, f32[64,512]{1,0:T(8,128)S(1)}, u32[]{:S(2)}, u32[]{:S(2)}) collective-permute-start(f32[64,512]{1,0:T(8,128)S(1)} %pad_maximum_fusion.5.refs_6_), channel_id=1, source_target_pairs={{0,3},{8,11},{4,7},{12,15},{16,19},{24,27},{20,23},{28,31},{32,35}... | collective-permute-start | bytes 393224 | tf_op jit(solution)/shard_map/ppermute | solution.py:47
  52.6 12.5 %collective-permute-start.13 = (bf16[2,32,4096]{2,1,0:T(8,128)(2,1)S(1)}, bf16[2,32,4096]{2,1,0:T(8,128)(2,1)}, u32[]{:S(2)}, u32[]{:S(2)}) collective-permute-start(bf16[2,32,4096]{2,1,0:T(8,128)(2,1)S(1)} %collective-permute-done.5), channel_id=1, source_target_pairs={{0,8},{8,0},{4,12},{12,4},{16,24},{24,16},{20,28},{28,20},{32,40},... | collective-permute-start | bytes 1572872 | tf_op jit(solution)/shard_map/ppermute | solution.py:47
  52.7 21.0 %collective-permute-start.17 = (bf16[2,32,4096]{2,1,0:T(8,128)(2,1)S(1)}, bf16[2,32,4096]{2,1,0:T(8,128)(2,1)S(1)}, u32[]{:S(2)}, u32[]{:S(2)}) collective-permute-start(bf16[2,32,4096]{2,1,0:T(8,128)(2,1)S(1)} %collective-permute-done.5), channel_id=1, source_target_pairs={{0,32},{8,40},{4,36},{12,44},{16,48},{24,56},{20,52},{28,60},{32,6... | collective-permute-start | bytes 1572872 | tf_op jit(solution)/shard_map/ppermute | solution.py:47
  53.0 19.3 %collective-permute-start.16 = (bf16[2,32,4096]{2,1,0:T(8,128)(2,1)S(1)}, bf16[2,32,4096]{2,1,0:T(8,128)(2,1)}, u32[]{:S(2)}, u32[]{:S(2)}) collective-permute-start(bf16[2,32,4096]{2,1,0:T(8,128)(2,1)S(1)} %collective-permute-done.6), channel_id=1, source_target_pairs={{0,8},{8,0},{4,12},{12,4},{16,24},{24,16},{20,28},{28,20},{32,40},... | collective-permute-start | bytes 1572872 | tf_op jit(solution)/shard_map/ppermute | solution.py:47
  53.2 20.5 %collective-permute-start.18 = (bf16[2,32,4096]{2,1,0:T(8,128)(2,1)S(1)}, bf16[2,32,4096]{2,1,0:T(8,128)(2,1)S(1)}, u32[]{:S(2)}, u32[]{:S(2)}) collective-permute-start(bf16[2,32,4096]{2,1,0:T(8,128)(2,1)S(1)} %collective-permute-done.6), channel_id=1, source_target_pairs={{0,96},{8,104},{4,100},{12,108},{16,112},{24,120},{20,116},{28,124... | collective-permute-start | bytes 1572872 | tf_op jit(solution)/shard_map/ppermute | solution.py:47
  56.2 14.0 %collective-permute-start.23 = (bf16[512,512]{1,0:T(8,128)(2,1)S(1)}, bf16[512,512]{1,0:T(8,128)(2,1)}, u32[]{:S(2)}, u32[]{:S(2)}) collective-permute-start(bf16[512,512]{1,0:T(8,128)(2,1)S(1)} %get-tuple-element.82), channel_id=1, source_target_pairs={{0,4},{8,12},{4,0},{12,8},{16,20},{24,28},{20,16},{28,24},{32,36},... | collective-permute-start | bytes 1572872 | tf_op jit(solution)/shard_map/ppermute | solution.py:47
  65.1 2.3 %collective-permute-start.14 = (bf16[2,32,4096]{2,1,0:T(8,128)(2,1)}, bf16[2,32,4096]{2,1,0:T(8,128)(2,1)S(1)}, u32[]{:S(2)}, u32[]{:S(2)}) collective-permute-start(bf16[2,32,4096]{2,1,0:T(8,128)(2,1)} %collective-permute-done.3), channel_id=1, source_target_pairs={{0,8},{8,0},{4,12},{12,4},{16,24},{24,16},{20,28},{28,20},{32,40},... | collective-permute-start | bytes 1572872 | tf_op jit(solution)/shard_map/ppermute | solution.py:47
  67.4 2.3 %collective-permute-start.15 = (bf16[2,32,4096]{2,1,0:T(8,128)(2,1)}, bf16[2,32,4096]{2,1,0:T(8,128)(2,1)S(1)}, u32[]{:S(2)}, u32[]{:S(2)}) collective-permute-start(bf16[2,32,4096]{2,1,0:T(8,128)(2,1)} %copy-done.8), channel_id=1, source_target_pairs={{0,8},{8,0},{4,12},{12,4},{16,24},{24,16},{20,28},{28,20},{32,40},... | collective-permute-start | bytes 1572872 | tf_op jit(solution)/shard_map/ppermute | solution.py:47
  69.7 3.7 %collective-permute-start.19 = (bf16[64,8192]{1,0:T(8,128)(2,1)S(1)}, bf16[64,8192]{1,0:T(8,128)(2,1)S(1)}, u32[]{:S(2)}, u32[]{:S(2)}) collective-permute-start(bf16[64,8192]{1,0:T(8,128)(2,1)S(1)} %get-tuple-element.77), channel_id=1, source_target_pairs={{0,8},{8,0},{4,12},{12,4},{16,24},{24,16},{20,28},{28,20},{32,40},... | collective-permute-start | bytes 3145736 | tf_op jit(solution)/shard_map/ppermute | solution.py:47
  70.2 8.2 %collective-permute-start.22 = (bf16[192,8192]{1,0:T(8,128)(2,1)S(1)}, bf16[192,8192]{1,0:T(8,128)(2,1)S(1)}, u32[]{:S(2)}, u32[]{:S(2)}) collective-permute-start(bf16[192,8192]{1,0:T(8,128)(2,1)S(1)} %get-tuple-element.80), channel_id=1, source_target_pairs={{0,8},{8,0},{4,12},{12,4},{16,24},{24,16},{20,28},{28,20},{32,40},... | collective-permute-start | bytes 9437192 | tf_op jit(solution)/shard_map/ppermute | solution.py:47
  73.7 3.9 %collective-permute-start.20 = (bf16[2,32,4096]{2,1,0:T(8,128)(2,1)S(1)}, bf16[2,32,4096]{2,1,0:T(8,128)(2,1)S(1)}, u32[]{:S(2)}, u32[]{:S(2)}) collective-permute-start(bf16[2,32,4096]{2,1,0:T(8,128)(2,1)S(1)} %collective-permute-done.17), channel_id=1, source_target_pairs={{0,8},{8,0},{4,12},{12,4},{16,24},{24,16},{20,28},{28,20},{32,40},... | collective-permute-start | bytes 1572872 | tf_op jit(solution)/shard_map/ppermute | solution.py:47
  74.2 4.2 %collective-permute-start.21 = (bf16[2,32,4096]{2,1,0:T(8,128)(2,1)S(1)}, bf16[2,32,4096]{2,1,0:T(8,128)(2,1)S(1)}, u32[]{:S(2)}, u32[]{:S(2)}) collective-permute-start(bf16[2,32,4096]{2,1,0:T(8,128)(2,1)S(1)} %collective-permute-done.18), channel_id=1, source_target_pairs={{0,8},{8,0},{4,12},{12,4},{16,24},{24,16},{20,28},{28,20},{32,40},... | collective-permute-start | bytes 1572872 | tf_op jit(solution)/shard_map/ppermute | solution.py:47
  74.5 14.5 %collective-permute-start.26 = (bf16[32,8192]{1,0:T(8,128)(2,1)S(1)}, bf16[32,8192]{1,0:T(8,128)(2,1)S(1)}, u32[]{:S(2)}, u32[]{:S(2)}) collective-permute-start(bf16[32,8192]{1,0:T(8,128)(2,1)S(1)} %get-tuple-element.123), channel_id=1, source_target_pairs={{0,96},{8,104},{4,100},{12,108},{16,112},{24,120},{20,116},{28,124... | collective-permute-start | bytes 1572872 | tf_op jit(solution)/shard_map/ppermute | solution.py:47
  74.9 15.6 %collective-permute-start.24 = (bf16[32,8192]{1,0:T(8,128)(2,1)S(1)}, bf16[32,8192]{1,0:T(8,128)(2,1)S(1)}, u32[]{:S(2)}, u32[]{:S(2)}) collective-permute-start(bf16[32,8192]{1,0:T(8,128)(2,1)S(1)} %get-tuple-element.122), channel_id=1, source_target_pairs={{0,32},{8,40},{4,36},{12,44},{16,48},{24,56},{20,52},{28,60},{32,6... | collective-permute-start | bytes 1572872 | tf_op jit(solution)/shard_map/ppermute | solution.py:47
  89.2 37.4 %collective-permute-start.27 = (bf16[64,8192]{1,0:T(8,128)(2,1)S(1)}, bf16[64,8192]{1,0:T(8,128)(2,1)S(1)}, u32[]{:S(2)}, u32[]{:S(2)}) collective-permute-start(bf16[64,8192]{1,0:T(8,128)(2,1)S(1)} %pad_maximum_fusion.2), channel_id=1, source_target_pairs={{0,96},{8,104},{4,100},{12,108},{16,112},{24,120},{20,116},{28,124... | collective-permute-start | bytes 3145736 | tf_op jit(solution)/shard_map/ppermute | solution.py:47
  90.7 36.0 %collective-permute-start.25 = (bf16[64,8192]{1,0:T(8,128)(2,1)S(1)}, bf16[64,8192]{1,0:T(8,128)(2,1)S(1)}, u32[]{:S(2)}, u32[]{:S(2)}) collective-permute-start(bf16[64,8192]{1,0:T(8,128)(2,1)S(1)} %pad_maximum_fusion.1), channel_id=1, source_target_pairs={{0,32},{8,40},{4,36},{12,44},{16,48},{24,56},{20,52},{28,60},{32,6... | collective-permute-start | bytes 3145736 | tf_op jit(solution)/shard_map/ppermute | solution.py:47
  91.8 16.1 %collective-permute-start.31 = (bf16[512,512]{1,0:T(8,128)(2,1)S(1)}, bf16[512,512]{1,0:T(8,128)(2,1)S(1)}, u32[]{:S(2)}, u32[]{:S(2)}) collective-permute-start(bf16[512,512]{1,0:T(8,128)(2,1)S(1)} %slice.184), channel_id=1, source_target_pairs={{0,4},{8,12},{4,0},{12,8},{16,20},{24,28},{20,16},{28,24},{32,36},... | collective-permute-start | bytes 1572872 | tf_op jit(solution)/shard_map/ppermute | solution.py:47
  92.8 14.6 %collective-permute-start.32 = (bf16[256,1024]{1,0:T(8,128)(2,1)S(1)}, bf16[256,1024]{1,0:T(8,128)(2,1)S(1)}, u32[]{:S(2)}, u32[]{:S(2)}) collective-permute-start(bf16[256,1024]{1,0:T(8,128)(2,1)S(1)} %get-tuple-element.119), channel_id=1, source_target_pairs={{0,1},{8,9},{4,5},{12,13},{16,17},{24,25},{20,21},{28,29},{32,33},... | collective-permute-start | bytes 1572872 | tf_op jit(solution)/shard_map/ppermute | solution.py:47
  94.0 13.7 %collective-permute-start.33 = (bf16[256,1024]{1,0:T(8,128)(2,1)S(1)}, bf16[256,1024]{1,0:T(8,128)(2,1)S(1)}, u32[]{:S(2)}, u32[]{:S(2)}) collective-permute-start(bf16[256,1024]{1,0:T(8,128)(2,1)S(1)} %get-tuple-element.118), channel_id=1, source_target_pairs={{0,3},{8,11},{4,7},{12,15},{16,19},{24,27},{20,23},{28,31},{32,35}... | collective-permute-start | bytes 1572872 | tf_op jit(solution)/shard_map/ppermute | solution.py:47
  107.9 16.1 %collective-permute-start.34 = (bf16[256,1024]{1,0:T(8,128)(2,1)S(1)}, bf16[256,1024]{1,0:T(8,128)(2,1)S(1)}, u32[]{:S(2)}, u32[]{:S(2)}) collective-permute-start(bf16[256,1024]{1,0:T(8,128)(2,1)S(1)} %slice.149), channel_id=1, source_target_pairs={{0,1},{8,9},{4,5},{12,13},{16,17},{24,25},{20,21},{28,29},{32,33},... | collective-permute-start | bytes 1572872 | tf_op jit(solution)/shard_map/ppermute | solution.py:47
  108.6 17.0 %collective-permute-start.35 = (bf16[256,1024]{1,0:T(8,128)(2,1)S(1)}, bf16[256,1024]{1,0:T(8,128)(2,1)S(1)}, u32[]{:S(2)}, u32[]{:S(2)}) collective-permute-start(bf16[256,1024]{1,0:T(8,128)(2,1)S(1)} %slice.150), channel_id=1, source_target_pairs={{0,3},{8,11},{4,7},{12,15},{16,19},{24,27},{20,23},{28,31},{32,35}... | collective-permute-start | bytes 1572872 | tf_op jit(solution)/shard_map/ppermute | solution.py:47
  112.4 20.4 %collective-permute-start.37 = (bf16[256,1024]{1,0:T(8,128)(2,1)S(1)}, bf16[256,1024]{1,0:T(8,128)(2,1)S(1)}, u32[]{:S(2)}, u32[]{:S(2)}) collective-permute-start(bf16[256,1024]{1,0:T(8,128)(2,1)S(1)} %add_convert_fusion.4), channel_id=1, source_target_pairs={{0,1},{8,9},{4,5},{12,13},{16,17},{24,25},{20,21},{28,29},{32,33},... | collective-permute-start | bytes 1572872 | tf_op jit(solution)/shard_map/ppermute | solution.py:47
  124.0 9.4 %collective-permute-start.38 = (bf16[256,1024]{1,0:T(8,128)(2,1)S(1)}, bf16[256,1024]{1,0:T(8,128)(2,1)S(1)}, u32[]{:S(2)}, u32[]{:S(2)}) collective-permute-start(bf16[256,1024]{1,0:T(8,128)(2,1)S(1)} %add_convert_fusion.3), channel_id=1, source_target_pairs={{0,3},{8,11},{4,7},{12,15},{16,19},{24,27},{20,23},{28,31},{32,35}... | collective-permute-start | bytes 1572872 | tf_op jit(solution)/shard_map/ppermute | solution.py:47
  125.5 6.1 %collective-permute-start.36 = (f32[56,512]{1,0:T(8,128)S(1)}, f32[56,512]{1,0:T(8,128)S(1)}, u32[]{:S(2)}, u32[]{:S(2)}) collective-permute-start(f32[56,512]{1,0:T(8,128)S(1)} %get-tuple-element.99), channel_id=1, source_target_pairs={{0,4},{8,12},{4,0},{12,8},{16,20},{24,28},{20,16},{28,24},{32,36},... | collective-permute-start | bytes 344072 | tf_op jit(solution)/shard_map/ppermute | solution.py:47
  128.5 10.0 %collective-permute-start.29 = (bf16[32,4096]{1,0:T(8,128)(2,1)S(1)}, bf16[32,4096]{1,0:T(8,128)(2,1)S(1)}, u32[]{:S(2)}, u32[]{:S(2)}) collective-permute-start(bf16[32,4096]{1,0:T(8,128)(2,1)S(1)} %get-tuple-element.121), channel_id=1, source_target_pairs={{0,20},{8,28},{4,0},{12,8},{16,4},{24,12},{20,16},{28,24},{32,52},... | collective-permute-start | bytes 786440 | tf_op jit(solution)/shard_map/ppermute | solution.py:47
  130.1 19.1 %collective-permute-start.28 = (bf16[32,4096]{1,0:T(8,128)(2,1)S(1)}, bf16[32,4096]{1,0:T(8,128)(2,1)S(1)}, u32[]{:S(2)}, u32[]{:S(2)}) collective-permute-start(bf16[32,4096]{1,0:T(8,128)(2,1)S(1)} %get-tuple-element.120), channel_id=1, source_target_pairs={{0,16},{8,24},{4,20},{12,28},{16,0},{24,8},{20,4},{28,12},{32,48},... | collective-permute-start | bytes 786440 | tf_op jit(solution)/shard_map/ppermute | solution.py:47
  133.4 8.8 %collective-permute-start.39 = (f32[72,512]{1,0:T(8,128)S(1)}, f32[72,512]{1,0:T(8,128)S(1)}, u32[]{:S(2)}, u32[]{:S(2)}) collective-permute-start(f32[72,512]{1,0:T(8,128)S(1)} %pad_maximum_fusion.4.refs_7_), channel_id=1, source_target_pairs={{0,1},{8,9},{4,5},{12,13},{16,17},{24,25},{20,21},{28,29},{32,33},... | collective-permute-start | bytes 442376 | tf_op jit(solution)/shard_map/ppermute | solution.py:47
  133.5 9.7 %collective-permute-start.40 = (f32[72,512]{1,0:T(8,128)S(1)}, f32[72,512]{1,0:T(8,128)S(1)}, u32[]{:S(2)}, u32[]{:S(2)}) collective-permute-start(f32[72,512]{1,0:T(8,128)S(1)} %pad_maximum_fusion.4.refs_7_), channel_id=1, source_target_pairs={{0,2},{8,10},{4,6},{12,14},{16,18},{24,26},{20,22},{28,30},{32,34}... | collective-permute-start | bytes 442376 | tf_op jit(solution)/shard_map/ppermute | solution.py:47
  138.5 5.1 %collective-permute-start.41 = (f32[72,512]{1,0:T(8,128)S(1)}, f32[72,512]{1,0:T(8,128)S(1)}, u32[]{:S(2)}, u32[]{:S(2)}) collective-permute-start(f32[72,512]{1,0:T(8,128)S(1)} %pad_maximum_fusion.4.refs_7_), channel_id=1, source_target_pairs={{0,3},{8,11},{4,7},{12,15},{16,19},{24,27},{20,23},{28,31},{32,35}... | collective-permute-start | bytes 442376 | tf_op jit(solution)/shard_map/ppermute | solution.py:47
  138.5 10.8 %collective-permute-start.30 = (bf16[32,4096]{1,0:T(8,128)(2,1)S(1)}, bf16[32,4096]{1,0:T(8,128)(2,1)S(1)}, u32[]{:S(2)}, u32[]{:S(2)}) collective-permute-start(bf16[32,4096]{1,0:T(8,128)(2,1)S(1)} %collective-permute-done.29), channel_id=1, source_target_pairs={{0,20},{8,28},{4,0},{12,8},{16,4},{24,12},{20,16},{28,24},{32,52},... | collective-permute-start | bytes 786440 | tf_op jit(solution)/shard_map/ppermute | solution.py:47
  (7 other events, 70.2 us)

commit v13 on v12

--- a/solution.py
+++ b/solution.py
@@ -76,25 +76,29 @@
     return functools.reduce(jnp.add, [part.astype(F32) for part in parts])
 
 
-def project_tile(rows_ref, weight_ref, *out_refs):
-    product = jnp.dot(rows_ref[...], weight_ref[...], preferred_element_type=F32).astype(BF16)
-    first = 0
-    for ref in out_refs:
-        ref[...] = product[first : first + ref.shape[0]]
-        first += ref.shape[0]
+def project_tiles(rows_ref, weight_ref, *out_refs, tile):
+    def one(i, carry):
+        columns = pl.ds(pl.multiple_of(i * tile, tile), tile)
+        product = jnp.dot(rows_ref[...], weight_ref[:, columns], preferred_element_type=F32).astype(BF16)
+        first = 0
+        for ref in out_refs:
+            ref[:, columns] = product[first : first + ref.shape[0]]
+            first += ref.shape[0]
+        return carry
+
+    lax.fori_loop(0, weight_ref.shape[1] // tile, one, 0)
 
 
 def project(turned, out_weight):
     rows, depth = turned.shape
     width = out_weight.shape[1]
-    tile = 1024
     sizes = [rows // 8, 3 * rows // 8] * 2
+    whole = pl.BlockSpec(memory_space=pltpu.VMEM)
     return pl.pallas_call(
-        project_tile,
-        grid=(width // tile,),
+        functools.partial(project_tiles, tile=512),
         out_shape=[jax.ShapeDtypeStruct((size, width), BF16) for size in sizes],
-        in_specs=[pl.BlockSpec((rows, depth), lambda i: (0, 0)), pl.BlockSpec((depth, tile), lambda i: (0, i))],
-        out_specs=[pl.BlockSpec((size, tile), lambda i: (0, i)) for size in sizes],
+        in_specs=[whole] * 2,
+        out_specs=[whole] * len(sizes),
         compiler_params=pltpu.CompilerParams(vmem_limit_bytes=32 * 2**20),
         cost_estimate=pl.CostEstimate(
             flops=2 * rows * depth * width, bytes_accessed=2 * width * (rows + depth), transcendentals=0

time: 151 us -> 151 us (level)
  no operation moved by 1% of the time
where the time goes in v13:
time: 151 us; the launch traced here: 150 us
  starting transfers between devices  50.1 us (33%)
  waiting for transfers between devices  37.4 us (25%)
  Pallas kernels  27.5 us (18%)
  local copies, waits for them, and re-layouts  15.6 us (10%)
  matrix products  10.6 us (7%)
  other arithmetic  7.95 us (5%)
    ppermute x42, starting transfers between devices, hop(): return lax.ppermute(value, ('chan', 'seq'), moves)  50.1 us
    ppermute x42, waiting for transfers between devices, hop(): return lax.ppermute(value, ('chan', 'seq'), moves)  37.4 us
    pallas_call x4, Pallas kernels, call(): pl.pallas_call(body, out_shape=[jax.ShapeDtypeStruct(o.shape, o.dtype) fo...  20.4 us
    pallas_call x1, Pallas kernels, project(): pl.pallas_call(functools.partial(project_tiles, tile=512), out_shape=[jax...  7.07 us
    dynamic_update_slice x16, local copies, waits for them, and re-layouts, place_blocks(): lax.dynamic_update_slice(whole, part[None, None, :, None], (side, row, 0,...  6.98 us
    dot_general x4, matrix products, weigh(): lax.dot_general(gated, columns, (((0,), (0,)), ((), ())), preferred_eleme...  6.09 us
    dot_general x1, matrix products, local(): lax.dot_general(cot_rows, low_weight, (((1,), (1,)), ((), ())), preferred...  4.52 us
  transfers between devices with their start and end apart: 42, of which 17 were waited for; matrix products, arithmetic and copies ran while one was open for 19% of the time, Pallas kernels for 18%

profile of v13, /device:TPU:0, one launch (start us, length us, event | category | flops | bytes accessed | tf_op | source)
XLA Modules:
  0.0 150.4 jit_solution(845433332816660891)
XLA Ops:
  0.7 1.1 constant_dynamic-slice_fusion.1
  1.8 2.1 %collective-permute-start.1 = (bf16[32,4096]{1,0:T(8,128)(2,1)S(1)}, bf16[32,4096]{1,0:T(8,128)(2,1)S(1)}, u32[]{:S(2)}, u32[]{:S(2)}) collective-permute-start(bf16[32,4096]{1,0:T(8,128)(2,1)S(1)} %get-tuple-element.127), channel_id=1, source_target_pairs={{0,4},{8,12},{4,16},{12,24},{16,20},{24,28},{20,0},{28,8},{32,36},... | collective-permute-start | bytes 786440 | tf_op jit(solution)/shard_map/ppermute | solution.py:47
  3.9 2.2 %collective-permute-start.2 = (bf16[32,4096]{1,0:T(8,128)(2,1)S(1)}, bf16[32,4096]{1,0:T(8,128)(2,1)S(1)}, u32[]{:S(2)}, u32[]{:S(2)}) collective-permute-start(bf16[32,4096]{1,0:T(8,128)(2,1)S(1)} %get-tuple-element.127), channel_id=1, source_target_pairs={{0,20},{8,28},{4,0},{12,8},{16,4},{24,12},{20,16},{28,24},{32,52},... | collective-permute-start | bytes 786440 | tf_op jit(solution)/shard_map/ppermute | solution.py:47
  6.1 1.8 %collective-permute-start = (bf16[32,4096]{1,0:T(8,128)(2,1)S(1)}, bf16[32,4096]{1,0:T(8,128)(2,1)S(1)}, u32[]{:S(2)}, u32[]{:S(2)}) collective-permute-start(bf16[32,4096]{1,0:T(8,128)(2,1)S(1)} %get-tuple-element.126), channel_id=1, source_target_pairs={{0,16},{8,24},{4,20},{12,28},{16,0},{24,8},{20,4},{28,12},{32,48},... | collective-permute-start | bytes 786440 | tf_op jit(solution)/shard_map/ppermute | solution.py:47
  7.9 4.4 %collective-permute-done.1 = bf16[32,4096]{1,0:T(8,128)(2,1)S(1)} collective-permute-done((bf16[32,4096]{1,0:T(8,128)(2,1)S(1)}, bf16[32,4096]{1,0:T(8,128)(2,1)S(1)}, u32[]{:S(2)}, u32[]{:S(2)}) %collective-permute-start.1) | collective-permute-done | bytes 262176 | tf_op jit(solution)/shard_map/ppermute | solution.py:47
  12.3 5.0 %collective-permute-done.2 = bf16[32,4096]{1,0:T(8,128)(2,1)S(1)} collective-permute-done((bf16[32,4096]{1,0:T(8,128)(2,1)S(1)}, bf16[32,4096]{1,0:T(8,128)(2,1)S(1)}, u32[]{:S(2)}, u32[]{:S(2)}) %collective-permute-start.2) | collective-permute-done | bytes 262176 | tf_op jit(solution)/shard_map/ppermute | solution.py:47
  17.5 1.7 %collective-permute-done = bf16[32,4096]{1,0:T(8,128)(2,1)S(1)} collective-permute-done((bf16[32,4096]{1,0:T(8,128)(2,1)S(1)}, bf16[32,4096]{1,0:T(8,128)(2,1)S(1)}, u32[]{:S(2)}, u32[]{:S(2)}) %collective-permute-start) | collective-permute-done | bytes 262176 | tf_op jit(solution)/shard_map/ppermute | solution.py:47
  20.4 1.6 %collective-permute-start.5 = (bf16[2,32,4096]{2,1,0:T(8,128)(2,1)}, bf16[2,32,4096]{2,1,0:T(8,128)(2,1)S(1)}, u32[]{:S(2)}, u32[]{:S(2)}) collective-permute-start(bf16[2,32,4096]{2,1,0:T(8,128)(2,1)} %get-tuple-element.125), channel_id=1, source_target_pairs={{0,32},{8,40},{4,36},{12,44},{16,48},{24,56},{20,52},{28,60},{32,6... | collective-permute-start | bytes 1572872 | tf_op jit(solution)/shard_map/ppermute | solution.py:47
  22.2 1.7 %collective-permute-start.6 = (bf16[2,32,4096]{2,1,0:T(8,128)(2,1)}, bf16[2,32,4096]{2,1,0:T(8,128)(2,1)S(1)}, u32[]{:S(2)}, u32[]{:S(2)}) collective-permute-start(bf16[2,32,4096]{2,1,0:T(8,128)(2,1)} %get-tuple-element.124), channel_id=1, source_target_pairs={{0,96},{8,104},{4,100},{12,108},{16,112},{24,120},{20,116},{28,124... | collective-permute-start | bytes 1572872 | tf_op jit(solution)/shard_map/ppermute | solution.py:47
  23.9 3.2 %forward_ends.1 = (f32[32,512]{1,0:T(8,128)S(1)}, f32[4,256,128]{2,1,0:T(8,128)S(1)}, f32[4,512,128]{2,1,0:T(8,128)S(1)}) custom-call(bf16[512,512]{1,0:T(8,128)(2,1)S(1)} %copy-done, bf16[512,512]{1,0:T(8,128)(2,1)S(1)} %copy-done.1, f32[16,512]{1,0:T(8,128)S(1)} %copy-done.3), custom_call_target="tpu_custom_call" | custom-call | flops 115000000 | tf_op jit(solution)/shard_map/forward_ends/pallas_call | solution.py:315
  27.2 1.2 collective-permute-start.7
  29.5 2.0 %collective-permute-done.7 = f32[32,512]{1,0:T(8,128)S(1)} collective-permute-done((f32[32,512]{1,0:T(8,128)S(1)}, f32[32,512]{1,0:T(8,128)S(1)}, u32[]{:S(2)}, u32[]{:S(2)}) %collective-permute-start.7) | collective-permute-done | bytes 65568 | tf_op jit(solution)/shard_map/ppermute | solution.py:47
  31.8 4.7 %collective-permute-done.5 = bf16[2,32,4096]{2,1,0:T(8,128)(2,1)S(1)} collective-permute-done((bf16[2,32,4096]{2,1,0:T(8,128)(2,1)}, bf16[2,32,4096]{2,1,0:T(8,128)(2,1)S(1)}, u32[]{:S(2)}, u32[]{:S(2)}) %collective-permute-start.5) | collective-permute-done | bytes 524320 | tf_op jit(solution)/shard_map/ppermute | solution.py:47
  36.5 1.8 %collective-permute-start.4 = (bf16[2,32,4096]{2,1,0:T(8,128)(2,1)}, bf16[2,32,4096]{2,1,0:T(8,128)(2,1)S(1)}, u32[]{:S(2)}, u32[]{:S(2)}) collective-permute-start(bf16[2,32,4096]{2,1,0:T(8,128)(2,1)} %get-tuple-element.125), channel_id=1, source_target_pairs={{0,96},{8,104},{4,100},{12,108},{16,112},{24,120},{20,116},{28,124... | collective-permute-start | bytes 1572872 | tf_op jit(solution)/shard_map/ppermute | solution.py:47
  38.3 1.5 collective-permute-start.8
  39.8 2.7 %collective-permute-start.9 = (f32[64,512]{1,0:T(8,128)S(1)}, f32[64,512]{1,0:T(8,128)S(1)}, u32[]{:S(2)}, u32[]{:S(2)}) collective-permute-start(f32[64,512]{1,0:T(8,128)S(1)} %pad_maximum_fusion.5.refs_6_), channel_id=1, source_target_pairs={{0,2},{8,10},{4,6},{12,14},{16,18},{24,26},{20,22},{28,30},{32,34}... | collective-permute-start | bytes 393224 | tf_op jit(solution)/shard_map/ppermute | solution.py:47
  43.7 1.5 collective-permute-start.10
  46.3 1.5 collective-permute-done.9.refs_8_
  48.8 3.8 %forward_full.1 = (bf16[512,512]{1,0:T(8,128)(2,1)S(1)}, bf16[512,512]{1,0:T(8,128)(2,1)S(1)}, f32[4,512,128]{2,1,0:T(8,128)S(1)}, f32[4,256,128]{2,1,0:T(8,128)S(1)}) custom-call(bf16[512,512]{1,0:T(8,128)(2,1)S(1)} %copy-done.2, f32[4,512,128]{2,1,0:T(8,128)S(1)} %get-tuple-element.65.refs_1_.drive_ref, f32[4,256,128]{2,1,0:T(8,128)S(1)} %get-tuple-element.66.refs_2_, ...), custom_call_target="tpu_custom_call" | custom-call | flops 115000000 | tf_op jit(solution)/shard_map/forward_full/pallas_call | solution.py:315
  53.2 3.0 %collective-permute-start.18 = (bf16[2,32,4096]{2,1,0:T(8,128)(2,1)S(1)}, bf16[2,32,4096]{2,1,0:T(8,128)(2,1)S(1)}, u32[]{:S(2)}, u32[]{:S(2)}) collective-permute-start(bf16[2,32,4096]{2,1,0:T(8,128)(2,1)S(1)} %collective-permute-done.6), channel_id=1, source_target_pairs={{0,96},{8,104},{4,100},{12,108},{16,112},{24,120},{20,116},{28,124... | collective-permute-start | bytes 1572872 | tf_op jit(solution)/shard_map/ppermute | solution.py:47
  56.2 1.1 collective-permute-start.23
  58.2 7.1 %project.1 = (bf16[64,8192]{1,0:T(8,128)(2,1)S(1)}, bf16[192,8192]{1,0:T(8,128)(2,1)S(1)}, bf16[64,8192]{1,0:T(8,128)(2,1)S(1)}, bf16[192,8192]{1,0:T(8,128)(2,1)S(1)}) custom-call(bf16[512,512]{1,0:T(8,128)(2,1)S(1)} %get-tuple-element.70.rows_ref, bf16[512,8192]{1,0:T(8,128)(2,1)S(1)} %bitcast.83), custom_call_target="tpu_custom_call" | custom-call | flops 4294967296 | bytes 16777216 | tf_op jit(solution)/shard_map/project/pallas_call | solution.py:97
  70.6 1.9 %constant_dynamic-update-slice_fusion = bf16[1024,512]{1,0:T(8,128)(2,1)} fusion(bf16[1024,512]{1,0:T(8,128)(2,1)} %constant_dynamic-update-slice_fusion.1, bf16[512,512]{1,0:T(8,128)(2,1)} %collective-permute-done.23), kind=kLoop, calls=%fused_computation.61 | loop fusion | bytes 1048576 | tf_op jit(solution)/shard_map/concatenate | solution.py:377
  72.5 1.2 bitcast_dynamic-update-slice_fusion.3
  75.0 1.9 %collective-permute-start.24 = (bf16[32,8192]{1,0:T(8,128)(2,1)S(1)}, bf16[32,8192]{1,0:T(8,128)(2,1)S(1)}, u32[]{:S(2)}, u32[]{:S(2)}) collective-permute-start(bf16[32,8192]{1,0:T(8,128)(2,1)S(1)} %get-tuple-element.122), channel_id=1, source_target_pairs={{0,32},{8,40},{4,36},{12,44},{16,48},{24,56},{20,52},{28,60},{32,6... | collective-permute-start | bytes 1572872 | tf_op jit(solution)/shard_map/ppermute | solution.py:47
  78.6 1.6 %copy-done.6 = bf16[192,8192]{1,0:T(8,128)(2,1)} copy-done((bf16[192,8192]{1,0:T(8,128)(2,1)}, bf16[192,8192]{1,0:T(8,128)(2,1)S(1)}, u32[]{:S(2)}) %copy-start.6) | copy-done | bytes 3145752
  80.2 2.3 %multiply_convert_fusion.3 = bf16[512,1024]{1,0:T(8,128)(2,1)} fusion(bf16[1024,512]{1,0:T(8,128)(2,1)S(1)} %copy-done.9, bf16[1024,4096]{1,0:T(8,128)(2,1)S(1)} %bitcast.84, s32[]{:T(128)S(6)} %select_n.130), kind=kOutput, calls=%fused_computation.14 | convolution fusion | flops 1074790400 | bytes 4194308 | tf_op jit(solution)/shard_map/dot_general | solution.py:114
  82.5 4.5 %fusion = f32[1024,512]{1,0:T(8,128)S(1)} fusion(bf16[1024,4096]{1,0:T(8,128)(2,1)S(1)} %bitcast.85, bf16[512,8192]{1,0:T(8,128)(2,1)S(1)} %bitcast.83, s32[]{:T(128)S(6)} %select_n.116), kind=kOutput, calls=%fused_computation | convolution fusion | flops 4294967296 | bytes 14680068 | tf_op jit(solution)/shard_map/dot_general | solution.py:389
  87.1 2.1 %convert_add_fusion.2 = (f32[64,8192]{1,0:T(8,128)S(1)}, f32[64,8192]{1,0:T(8,128)S(1)}) fusion(bf16[192,8192]{1,0:T(8,128)(2,1)} %copy-done.6, bf16[192,8192]{1,0:T(8,128)(2,1)S(1)} %get-tuple-element.71), kind=kLoop, calls=%fused_computation.13 | loop fusion | flops 3145728 | bytes 8388608 | tf_op jit(solution)/shard_map/add | solution.py:76
  89.5 1.3 collective-permute-start.27
  93.0 1.1 collective-permute-start.32
  94.2 2.2 %collective-permute-start.33 = (bf16[256,1024]{1,0:T(8,128)(2,1)S(1)}, bf16[256,1024]{1,0:T(8,128)(2,1)S(1)}, u32[]{:S(2)}, u32[]{:S(2)}) collective-permute-start(bf16[256,1024]{1,0:T(8,128)(2,1)S(1)} %get-tuple-element.118), channel_id=1, source_target_pairs={{0,3},{8,11},{4,7},{12,15},{16,19},{24,27},{20,23},{28,31},{32,35}... | collective-permute-start | bytes 1572872 | tf_op jit(solution)/shard_map/ppermute | solution.py:47
  96.3 1.3 multiply_convert_fusion.2
  97.6 1.3 multiply_convert_fusion.1
  99.0 8.7 %collective-permute-done.32 = bf16[256,1024]{1,0:T(8,128)(2,1)S(1)} collective-permute-done((bf16[256,1024]{1,0:T(8,128)(2,1)S(1)}, bf16[256,1024]{1,0:T(8,128)(2,1)S(1)}, u32[]{:S(2)}, u32[]{:S(2)}) %collective-permute-start.32) | collective-permute-done | bytes 524320 | tf_op jit(solution)/shard_map/ppermute | solution.py:47
  108.8 2.6 %collective-permute-start.35 = (bf16[256,1024]{1,0:T(8,128)(2,1)S(1)}, bf16[256,1024]{1,0:T(8,128)(2,1)S(1)}, u32[]{:S(2)}, u32[]{:S(2)}) collective-permute-start(bf16[256,1024]{1,0:T(8,128)(2,1)S(1)} %slice.150), channel_id=1, source_target_pairs={{0,3},{8,11},{4,7},{12,15},{16,19},{24,27},{20,23},{28,31},{32,35}... | collective-permute-start | bytes 1572872 | tf_op jit(solution)/shard_map/ppermute | solution.py:47
  111.4 1.3 multiply_convert_fusion
  112.9 8.3 %backward_ends.1 = (bf16[512,512]{1,0:T(8,128)(2,1)}, f32[4,512,128]{2,1,0:T(8,128)S(1)}, f32[56,512]{1,0:T(8,128)S(1)}, f32[4,128,128]{2,1,0:T(8,128)S(1)}) custom-call(f32[512,512]{1,0:T(8,128)S(1)} %convert_add_fusion.3.grad_ref, bf16[512,512]{1,0:T(8,128)(2,1)S(1)} %copy-done.2, f32[4,512,128]{2,1,0:T(8,128)S(1)} %get-tuple-element.91.pre_ref, ...), custom_call_target="tpu_custom_call" | custom-call | flops 2300000000 | tf_op jit(solution)/shard_map/backward_ends/pallas_call | solution.py:315
  121.2 3.0 %collective-permute-done.34 = bf16[256,1024]{1,0:T(8,128)(2,1)S(1)} collective-permute-done((bf16[256,1024]{1,0:T(8,128)(2,1)S(1)}, bf16[256,1024]{1,0:T(8,128)(2,1)S(1)}, u32[]{:S(2)}, u32[]{:S(2)}) %collective-permute-start.34) | collective-permute-done | bytes 524320 | tf_op jit(solution)/shard_map/ppermute | solution.py:47
  124.2 1.5 %collective-permute-start.38 = (bf16[256,1024]{1,0:T(8,128)(2,1)S(1)}, bf16[256,1024]{1,0:T(8,128)(2,1)S(1)}, u32[]{:S(2)}, u32[]{:S(2)}) collective-permute-start(bf16[256,1024]{1,0:T(8,128)(2,1)S(1)} %add_convert_fusion.3), channel_id=1, source_target_pairs={{0,3},{8,11},{4,7},{12,15},{16,19},{24,27},{20,23},{28,31},{32,35}... | collective-permute-start | bytes 1572872 | tf_op jit(solution)/shard_map/ppermute | solution.py:47
  125.7 1.1 collective-permute-start.36
  126.9 1.7 %fusion.26 = (bf16[64,8192]{1,0:T(8,128)(2,1)S(1)}, f32[64,8192]{1,0:T(8,128)S(1)}) fusion(bf16[64,8192]{1,0:T(8,128)(2,1)S(1)} %collective-permute-done.27, bf16[64,8192]{1,0:T(8,128)(2,1)S(1)} %collective-permute-done.25, bf16[192,8192]{1,0:T(8,128)(2,1)} %copy-done.6, bf16[192,8192]{1,0:T(8,128)(2,1)S(1)} %get-tuple-element.71), kind=kLoop, calls=%fused_computation.70 | loop fusion | flops 4194304 | bytes 7340032 | tf_op jit(solution)/shard_map/convert.3
  128.7 1.7 %collective-permute-start.29 = (bf16[32,4096]{1,0:T(8,128)(2,1)S(1)}, bf16[32,4096]{1,0:T(8,128)(2,1)S(1)}, u32[]{:S(2)}, u32[]{:S(2)}) collective-permute-start(bf16[32,4096]{1,0:T(8,128)(2,1)S(1)} %get-tuple-element.121), channel_id=1, source_target_pairs={{0,20},{8,28},{4,0},{12,8},{16,4},{24,12},{20,16},{28,24},{32,52},... | collective-permute-start | bytes 786440 | tf_op jit(solution)/shard_map/ppermute | solution.py:47
  130.4 1.4 collective-permute-start.28
  131.9 1.1 collective-permute-done.37
  133.7 5.0 %collective-permute-start.40 = (f32[72,512]{1,0:T(8,128)S(1)}, f32[72,512]{1,0:T(8,128)S(1)}, u32[]{:S(2)}, u32[]{:S(2)}) collective-permute-start(f32[72,512]{1,0:T(8,128)S(1)} %pad_maximum_fusion.4.refs_7_), channel_id=1, source_target_pairs={{0,2},{8,10},{4,6},{12,14},{16,18},{24,26},{20,22},{28,30},{32,34}... | collective-permute-start | bytes 442376 | tf_op jit(solution)/shard_map/ppermute | solution.py:47
  138.7 2.0 %collective-permute-start.30 = (bf16[32,4096]{1,0:T(8,128)(2,1)S(1)}, bf16[32,4096]{1,0:T(8,128)(2,1)S(1)}, u32[]{:S(2)}, u32[]{:S(2)}) collective-permute-start(bf16[32,4096]{1,0:T(8,128)(2,1)S(1)} %collective-permute-done.29), channel_id=1, source_target_pairs={{0,20},{8,28},{4,0},{12,8},{16,4},{24,12},{20,16},{28,24},{32,52},... | collective-permute-start | bytes 786440 | tf_op jit(solution)/shard_map/ppermute | solution.py:47
  143.9 5.0 %backward_full.1 = (bf16[512,512]{1,0:T(8,128)(2,1)}, bf16[512,512]{1,0:T(8,128)(2,1)}, f32[16,512]{1,0:T(8,128)}, f32[16,512]{1,0:T(8,128)}, f32[8,512]{1,0:T(8,128)S(1)}) custom-call(bf16[512,512]{1,0:T(8,128)(2,1)S(1)} %copy-done, bf16[512,512]{1,0:T(8,128)(2,1)S(1)} %copy-done.1, f32[4,512,128]{2,1,0:T(8,128)S(1)} %get-tuple-element.94.refs_2_, ...), custom_call_target="tpu_custom_call" | custom-call | flops 115000000 | tf_op jit(solution)/shard_map/backward_full/pallas_call | solution.py:315
  (125 shorter events, 25.2 us)
Async XLA Ops:
  0.6 23.3 %copy-start.3 = (f32[16,512]{1,0:T(8,128)S(1)}, f32[16,512]{1,0:T(8,128)}, u32[]{:S(2)}) copy-start(f32[16,512]{1,0:T(8,128)} %refs_4_.3) | copy-start | bytes 98308
  1.8 10.5 %collective-permute-start.1 = (bf16[32,4096]{1,0:T(8,128)(2,1)S(1)}, bf16[32,4096]{1,0:T(8,128)(2,1)S(1)}, u32[]{:S(2)}, u32[]{:S(2)}) collective-permute-start(bf16[32,4096]{1,0:T(8,128)(2,1)S(1)} %get-tuple-element.127), channel_id=1, source_target_pairs={{0,4},{8,12},{4,16},{12,24},{16,20},{24,28},{20,0},{28,8},{32,36},... | collective-permute-start | bytes 786440 | tf_op jit(solution)/shard_map/ppermute | solution.py:47
  3.9 13.4 %collective-permute-start.2 = (bf16[32,4096]{1,0:T(8,128)(2,1)S(1)}, bf16[32,4096]{1,0:T(8,128)(2,1)S(1)}, u32[]{:S(2)}, u32[]{:S(2)}) collective-permute-start(bf16[32,4096]{1,0:T(8,128)(2,1)S(1)} %get-tuple-element.127), channel_id=1, source_target_pairs={{0,20},{8,28},{4,0},{12,8},{16,4},{24,12},{20,16},{28,24},{32,52},... | collective-permute-start | bytes 786440 | tf_op jit(solution)/shard_map/ppermute | solution.py:47
  6.1 13.0 %collective-permute-start = (bf16[32,4096]{1,0:T(8,128)(2,1)S(1)}, bf16[32,4096]{1,0:T(8,128)(2,1)S(1)}, u32[]{:S(2)}, u32[]{:S(2)}) collective-permute-start(bf16[32,4096]{1,0:T(8,128)(2,1)S(1)} %get-tuple-element.126), channel_id=1, source_target_pairs={{0,16},{8,24},{4,20},{12,28},{16,0},{24,8},{20,4},{28,12},{32,48},... | collective-permute-start | bytes 786440 | tf_op jit(solution)/shard_map/ppermute | solution.py:47
  19.3 29.4 %copy-start.2 = (bf16[512,512]{1,0:T(8,128)(2,1)S(1)}, bf16[512,512]{1,0:T(8,128)(2,1)}, u32[]{:S(2)}) copy-start(bf16[512,512]{1,0:T(8,128)(2,1)} %query_ref.1) | copy-start | bytes 1572868
  19.3 29.4 %copy-start.4 = (f32[16,512]{1,0:T(8,128)S(1)}, f32[16,512]{1,0:T(8,128)}, u32[]{:S(2)}) copy-start(f32[16,512]{1,0:T(8,128)} %refs_5_.1) | copy-start | bytes 98308
  19.3 29.4 %copy-start.5 = (f32[512]{0:T(512)S(1)}, f32[512]{0:T(512)}, u32[]{:S(2)}) copy-start(f32[512]{0:T(512)} %param.11) | copy-start | bytes 6148
  20.4 19.4 %collective-permute-start.11 = (bf16[2,32,4096]{2,1,0:T(8,128)(2,1)}, bf16[2,32,4096]{2,1,0:T(8,128)(2,1)}, u32[]{:S(2)}, u32[]{:S(2)}) collective-permute-start(bf16[2,32,4096]{2,1,0:T(8,128)(2,1)} %get-tuple-element.125), channel_id=1, source_target_pairs={{0,8},{8,0},{4,12},{12,4},{16,24},{24,16},{20,28},{28,20},{32,40},... | collective-permute-start | bytes 1572872 | tf_op jit(solution)/shard_map/ppermute | solution.py:47
  20.4 16.1 %collective-permute-start.5 = (bf16[2,32,4096]{2,1,0:T(8,128)(2,1)}, bf16[2,32,4096]{2,1,0:T(8,128)(2,1)S(1)}, u32[]{:S(2)}, u32[]{:S(2)}) collective-permute-start(bf16[2,32,4096]{2,1,0:T(8,128)(2,1)} %get-tuple-element.125), channel_id=1, source_target_pairs={{0,32},{8,40},{4,36},{12,44},{16,48},{24,56},{20,52},{28,60},{32,6... | collective-permute-start | bytes 1572872 | tf_op jit(solution)/shard_map/ppermute | solution.py:47
  22.0 21.7 %collective-permute-start.12 = (bf16[2,32,4096]{2,1,0:T(8,128)(2,1)}, bf16[2,32,4096]{2,1,0:T(8,128)(2,1)}, u32[]{:S(2)}, u32[]{:S(2)}) collective-permute-start(bf16[2,32,4096]{2,1,0:T(8,128)(2,1)} %get-tuple-element.124), channel_id=1, source_target_pairs={{0,8},{8,0},{4,12},{12,4},{16,24},{24,16},{20,28},{28,20},{32,40},... | collective-permute-start | bytes 1572872 | tf_op jit(solution)/shard_map/ppermute | solution.py:47
  22.2 16.1 %collective-permute-start.6 = (bf16[2,32,4096]{2,1,0:T(8,128)(2,1)}, bf16[2,32,4096]{2,1,0:T(8,128)(2,1)S(1)}, u32[]{:S(2)}, u32[]{:S(2)}) collective-permute-start(bf16[2,32,4096]{2,1,0:T(8,128)(2,1)} %get-tuple-element.124), channel_id=1, source_target_pairs={{0,96},{8,104},{4,100},{12,108},{16,112},{24,120},{20,116},{28,124... | collective-permute-start | bytes 1572872 | tf_op jit(solution)/shard_map/ppermute | solution.py:47
  27.1 31.0 %slice-start = ((s8[8388608]{0:T(1024)(128)(4,1)}), s8[4194304]{0:T(1024)(128)(4,1)S(1)}, s32[]{:S(2)}) async-start(s8[8388608]{0:T(1024)(128)(4,1)} %bitcast.82), calls=%async_computation | async-start | bytes 8388608
  27.2 4.3 %collective-permute-start.7 = (f32[32,512]{1,0:T(8,128)S(1)}, f32[32,512]{1,0:T(8,128)S(1)}, u32[]{:S(2)}, u32[]{:S(2)}) collective-permute-start(f32[32,512]{1,0:T(8,128)S(1)} %get-tuple-element.62), channel_id=1, source_target_pairs={{0,4},{8,12},{4,0},{12,8},{16,20},{24,28},{20,16},{28,24},{32,36},... | collective-permute-start | bytes 196616 | tf_op jit(solution)/shard_map/ppermute | solution.py:47
  29.4 28.8 %slice-start.1 = ((s8[8388608]{0:T(1024)(128)(4,1)}), s8[4194304]{0:T(1024)(128)(4,1)S(1)}, s32[]{:S(2)}) async-start(s8[8388608]{0:T(1024)(128)(4,1)} %bitcast.82), calls=%async_computation.1 | async-start | bytes 8388608
  31.5 21.7 %collective-permute-start.3 = (bf16[2,32,4096]{2,1,0:T(8,128)(2,1)}, bf16[2,32,4096]{2,1,0:T(8,128)(2,1)}, u32[]{:S(2)}, u32[]{:S(2)}) collective-permute-start(bf16[2,32,4096]{2,1,0:T(8,128)(2,1)} %get-tuple-element.124), channel_id=1, source_target_pairs={{0,32},{8,40},{4,36},{12,44},{16,48},{24,56},{20,52},{28,60},{32,6... | collective-permute-start | bytes 1572872 | tf_op jit(solution)/shard_map/ppermute | solution.py:47
  36.5 19.6 %collective-permute-start.4 = (bf16[2,32,4096]{2,1,0:T(8,128)(2,1)}, bf16[2,32,4096]{2,1,0:T(8,128)(2,1)S(1)}, u32[]{:S(2)}, u32[]{:S(2)}) collective-permute-start(bf16[2,32,4096]{2,1,0:T(8,128)(2,1)} %get-tuple-element.125), channel_id=1, source_target_pairs={{0,96},{8,104},{4,100},{12,108},{16,112},{24,120},{20,116},{28,124... | collective-permute-start | bytes 1572872 | tf_op jit(solution)/shard_map/ppermute | solution.py:47
  38.3 8.0 %collective-permute-start.8 = (f32[64,512]{1,0:T(8,128)S(1)}, f32[64,512]{1,0:T(8,128)S(1)}, u32[]{:S(2)}, u32[]{:S(2)}) collective-permute-start(f32[64,512]{1,0:T(8,128)S(1)} %pad_maximum_fusion.5.refs_6_), channel_id=1, source_target_pairs={{0,1},{8,9},{4,5},{12,13},{16,17},{24,25},{20,21},{28,29},{32,33},... | collective-permute-start | bytes 393224 | tf_op jit(solution)/shard_map/ppermute | solution.py:47
  39.8 8.0 %collective-permute-start.9 = (f32[64,512]{1,0:T(8,128)S(1)}, f32[64,512]{1,0:T(8,128)S(1)}, u32[]{:S(2)}, u32[]{:S(2)}) collective-permute-start(f32[64,512]{1,0:T(8,128)S(1)} %pad_maximum_fusion.5.refs_6_), channel_id=1, source_target_pairs={{0,2},{8,10},{4,6},{12,14},{16,18},{24,26},{20,22},{28,30},{32,34}... | collective-permute-start | bytes 393224 | tf_op jit(solution)/shard_map/ppermute | solution.py:47
  43.7 5.0 %collective-permute-start.10 = (f32[64,512]{1,0:T(8,128)S(1)}, f32[64,512]{1,0:T(8,128)S(1)}, u32[]{:S(2)}, u32[]{:S(2)}) collective-permute-start(f32[64,512]{1,0:T(8,128)S(1)} %pad_maximum_fusion.5.refs_6_), channel_id=1, source_target_pairs={{0,3},{8,11},{4,7},{12,15},{16,19},{24,27},{20,23},{28,31},{32,35}... | collective-permute-start | bytes 393224 | tf_op jit(solution)/shard_map/ppermute | solution.py:47
  52.6 12.7 %collective-permute-start.13 = (bf16[2,32,4096]{2,1,0:T(8,128)(2,1)S(1)}, bf16[2,32,4096]{2,1,0:T(8,128)(2,1)}, u32[]{:S(2)}, u32[]{:S(2)}) collective-permute-start(bf16[2,32,4096]{2,1,0:T(8,128)(2,1)S(1)} %collective-permute-done.5), channel_id=1, source_target_pairs={{0,8},{8,0},{4,12},{12,4},{16,24},{24,16},{20,28},{28,20},{32,40},... | collective-permute-start | bytes 1572872 | tf_op jit(solution)/shard_map/ppermute | solution.py:47
  52.7 21.2 %collective-permute-start.17 = (bf16[2,32,4096]{2,1,0:T(8,128)(2,1)S(1)}, bf16[2,32,4096]{2,1,0:T(8,128)(2,1)S(1)}, u32[]{:S(2)}, u32[]{:S(2)}) collective-permute-start(bf16[2,32,4096]{2,1,0:T(8,128)(2,1)S(1)} %collective-permute-done.5), channel_id=1, source_target_pairs={{0,32},{8,40},{4,36},{12,44},{16,48},{24,56},{20,52},{28,60},{32,6... | collective-permute-start | bytes 1572872 | tf_op jit(solution)/shard_map/ppermute | solution.py:47
  53.0 19.5 %collective-permute-start.16 = (bf16[2,32,4096]{2,1,0:T(8,128)(2,1)S(1)}, bf16[2,32,4096]{2,1,0:T(8,128)(2,1)}, u32[]{:S(2)}, u32[]{:S(2)}) collective-permute-start(bf16[2,32,4096]{2,1,0:T(8,128)(2,1)S(1)} %collective-permute-done.6), channel_id=1, source_target_pairs={{0,8},{8,0},{4,12},{12,4},{16,24},{24,16},{20,28},{28,20},{32,40},... | collective-permute-start | bytes 1572872 | tf_op jit(solution)/shard_map/ppermute | solution.py:47
  53.2 20.7 %collective-permute-start.18 = (bf16[2,32,4096]{2,1,0:T(8,128)(2,1)S(1)}, bf16[2,32,4096]{2,1,0:T(8,128)(2,1)S(1)}, u32[]{:S(2)}, u32[]{:S(2)}) collective-permute-start(bf16[2,32,4096]{2,1,0:T(8,128)(2,1)S(1)} %collective-permute-done.6), channel_id=1, source_target_pairs={{0,96},{8,104},{4,100},{12,108},{16,112},{24,120},{20,116},{28,124... | collective-permute-start | bytes 1572872 | tf_op jit(solution)/shard_map/ppermute | solution.py:47
  56.2 14.2 %collective-permute-start.23 = (bf16[512,512]{1,0:T(8,128)(2,1)S(1)}, bf16[512,512]{1,0:T(8,128)(2,1)}, u32[]{:S(2)}, u32[]{:S(2)}) collective-permute-start(bf16[512,512]{1,0:T(8,128)(2,1)S(1)} %get-tuple-element.82), channel_id=1, source_target_pairs={{0,4},{8,12},{4,0},{12,8},{16,20},{24,28},{20,16},{28,24},{32,36},... | collective-permute-start | bytes 1572872 | tf_op jit(solution)/shard_map/ppermute | solution.py:47
  65.3 2.3 %collective-permute-start.14 = (bf16[2,32,4096]{2,1,0:T(8,128)(2,1)}, bf16[2,32,4096]{2,1,0:T(8,128)(2,1)S(1)}, u32[]{:S(2)}, u32[]{:S(2)}) collective-permute-start(bf16[2,32,4096]{2,1,0:T(8,128)(2,1)} %collective-permute-done.3), channel_id=1, source_target_pairs={{0,8},{8,0},{4,12},{12,4},{16,24},{24,16},{20,28},{28,20},{32,40},... | collective-permute-start | bytes 1572872 | tf_op jit(solution)/shard_map/ppermute | solution.py:47
  67.6 2.3 %collective-permute-start.15 = (bf16[2,32,4096]{2,1,0:T(8,128)(2,1)}, bf16[2,32,4096]{2,1,0:T(8,128)(2,1)S(1)}, u32[]{:S(2)}, u32[]{:S(2)}) collective-permute-start(bf16[2,32,4096]{2,1,0:T(8,128)(2,1)} %copy-done.8), channel_id=1, source_target_pairs={{0,8},{8,0},{4,12},{12,4},{16,24},{24,16},{20,28},{28,20},{32,40},... | collective-permute-start | bytes 1572872 | tf_op jit(solution)/shard_map/ppermute | solution.py:47
  69.9 3.7 %collective-permute-start.19 = (bf16[64,8192]{1,0:T(8,128)(2,1)S(1)}, bf16[64,8192]{1,0:T(8,128)(2,1)S(1)}, u32[]{:S(2)}, u32[]{:S(2)}) collective-permute-start(bf16[64,8192]{1,0:T(8,128)(2,1)S(1)} %get-tuple-element.77), channel_id=1, source_target_pairs={{0,8},{8,0},{4,12},{12,4},{16,24},{24,16},{20,28},{28,20},{32,40},... | collective-permute-start | bytes 3145736 | tf_op jit(solution)/shard_map/ppermute | solution.py:47
  70.4 8.2 %collective-permute-start.22 = (bf16[192,8192]{1,0:T(8,128)(2,1)S(1)}, bf16[192,8192]{1,0:T(8,128)(2,1)S(1)}, u32[]{:S(2)}, u32[]{:S(2)}) collective-permute-start(bf16[192,8192]{1,0:T(8,128)(2,1)S(1)} %get-tuple-element.80), channel_id=1, source_target_pairs={{0,8},{8,0},{4,12},{12,4},{16,24},{24,16},{20,28},{28,20},{32,40},... | collective-permute-start | bytes 9437192 | tf_op jit(solution)/shard_map/ppermute | solution.py:47
  73.9 3.9 %collective-permute-start.20 = (bf16[2,32,4096]{2,1,0:T(8,128)(2,1)S(1)}, bf16[2,32,4096]{2,1,0:T(8,128)(2,1)S(1)}, u32[]{:S(2)}, u32[]{:S(2)}) collective-permute-start(bf16[2,32,4096]{2,1,0:T(8,128)(2,1)S(1)} %collective-permute-done.17), channel_id=1, source_target_pairs={{0,8},{8,0},{4,12},{12,4},{16,24},{24,16},{20,28},{28,20},{32,40},... | collective-permute-start | bytes 1572872 | tf_op jit(solution)/shard_map/ppermute | solution.py:47
  74.4 4.2 %collective-permute-start.21 = (bf16[2,32,4096]{2,1,0:T(8,128)(2,1)S(1)}, bf16[2,32,4096]{2,1,0:T(8,128)(2,1)S(1)}, u32[]{:S(2)}, u32[]{:S(2)}) collective-permute-start(bf16[2,32,4096]{2,1,0:T(8,128)(2,1)S(1)} %collective-permute-done.18), channel_id=1, source_target_pairs={{0,8},{8,0},{4,12},{12,4},{16,24},{24,16},{20,28},{28,20},{32,40},... | collective-permute-start | bytes 1572872 | tf_op jit(solution)/shard_map/ppermute | solution.py:47
  74.6 14.7 %collective-permute-start.26 = (bf16[32,8192]{1,0:T(8,128)(2,1)S(1)}, bf16[32,8192]{1,0:T(8,128)(2,1)S(1)}, u32[]{:S(2)}, u32[]{:S(2)}) collective-permute-start(bf16[32,8192]{1,0:T(8,128)(2,1)S(1)} %get-tuple-element.123), channel_id=1, source_target_pairs={{0,96},{8,104},{4,100},{12,108},{16,112},{24,120},{20,116},{28,124... | collective-permute-start | bytes 1572872 | tf_op jit(solution)/shard_map/ppermute | solution.py:47
  75.0 15.9 %collective-permute-start.24 = (bf16[32,8192]{1,0:T(8,128)(2,1)S(1)}, bf16[32,8192]{1,0:T(8,128)(2,1)S(1)}, u32[]{:S(2)}, u32[]{:S(2)}) collective-permute-start(bf16[32,8192]{1,0:T(8,128)(2,1)S(1)} %get-tuple-element.122), channel_id=1, source_target_pairs={{0,32},{8,40},{4,36},{12,44},{16,48},{24,56},{20,52},{28,60},{32,6... | collective-permute-start | bytes 1572872 | tf_op jit(solution)/shard_map/ppermute | solution.py:47
  89.5 37.4 %collective-permute-start.27 = (bf16[64,8192]{1,0:T(8,128)(2,1)S(1)}, bf16[64,8192]{1,0:T(8,128)(2,1)S(1)}, u32[]{:S(2)}, u32[]{:S(2)}) collective-permute-start(bf16[64,8192]{1,0:T(8,128)(2,1)S(1)} %pad_maximum_fusion.2), channel_id=1, source_target_pairs={{0,96},{8,104},{4,100},{12,108},{16,112},{24,120},{20,116},{28,124... | collective-permute-start | bytes 3145736 | tf_op jit(solution)/shard_map/ppermute | solution.py:47
  91.1 35.8 %collective-permute-start.25 = (bf16[64,8192]{1,0:T(8,128)(2,1)S(1)}, bf16[64,8192]{1,0:T(8,128)(2,1)S(1)}, u32[]{:S(2)}, u32[]{:S(2)}) collective-permute-start(bf16[64,8192]{1,0:T(8,128)(2,1)S(1)} %pad_maximum_fusion.1), channel_id=1, source_target_pairs={{0,32},{8,40},{4,36},{12,44},{16,48},{24,56},{20,52},{28,60},{32,6... | collective-permute-start | bytes 3145736 | tf_op jit(solution)/shard_map/ppermute | solution.py:47
  92.0 16.1 %collective-permute-start.31 = (bf16[512,512]{1,0:T(8,128)(2,1)S(1)}, bf16[512,512]{1,0:T(8,128)(2,1)S(1)}, u32[]{:S(2)}, u32[]{:S(2)}) collective-permute-start(bf16[512,512]{1,0:T(8,128)(2,1)S(1)} %slice.184), channel_id=1, source_target_pairs={{0,4},{8,12},{4,0},{12,8},{16,20},{24,28},{20,16},{28,24},{32,36},... | collective-permute-start | bytes 1572872 | tf_op jit(solution)/shard_map/ppermute | solution.py:47
  93.0 14.6 %collective-permute-start.32 = (bf16[256,1024]{1,0:T(8,128)(2,1)S(1)}, bf16[256,1024]{1,0:T(8,128)(2,1)S(1)}, u32[]{:S(2)}, u32[]{:S(2)}) collective-permute-start(bf16[256,1024]{1,0:T(8,128)(2,1)S(1)} %get-tuple-element.119), channel_id=1, source_target_pairs={{0,1},{8,9},{4,5},{12,13},{16,17},{24,25},{20,21},{28,29},{32,33},... | collective-permute-start | bytes 1572872 | tf_op jit(solution)/shard_map/ppermute | solution.py:47
  94.2 13.7 %collective-permute-start.33 = (bf16[256,1024]{1,0:T(8,128)(2,1)S(1)}, bf16[256,1024]{1,0:T(8,128)(2,1)S(1)}, u32[]{:S(2)}, u32[]{:S(2)}) collective-permute-start(bf16[256,1024]{1,0:T(8,128)(2,1)S(1)} %get-tuple-element.118), channel_id=1, source_target_pairs={{0,3},{8,11},{4,7},{12,15},{16,19},{24,27},{20,23},{28,31},{32,35}... | collective-permute-start | bytes 1572872 | tf_op jit(solution)/shard_map/ppermute | solution.py:47
  108.1 16.1 %collective-permute-start.34 = (bf16[256,1024]{1,0:T(8,128)(2,1)S(1)}, bf16[256,1024]{1,0:T(8,128)(2,1)S(1)}, u32[]{:S(2)}, u32[]{:S(2)}) collective-permute-start(bf16[256,1024]{1,0:T(8,128)(2,1)S(1)} %slice.149), channel_id=1, source_target_pairs={{0,1},{8,9},{4,5},{12,13},{16,17},{24,25},{20,21},{28,29},{32,33},... | collective-permute-start | bytes 1572872 | tf_op jit(solution)/shard_map/ppermute | solution.py:47
  108.8 17.0 %collective-permute-start.35 = (bf16[256,1024]{1,0:T(8,128)(2,1)S(1)}, bf16[256,1024]{1,0:T(8,128)(2,1)S(1)}, u32[]{:S(2)}, u32[]{:S(2)}) collective-permute-start(bf16[256,1024]{1,0:T(8,128)(2,1)S(1)} %slice.150), channel_id=1, source_target_pairs={{0,3},{8,11},{4,7},{12,15},{16,19},{24,27},{20,23},{28,31},{32,35}... | collective-permute-start | bytes 1572872 | tf_op jit(solution)/shard_map/ppermute | solution.py:47
  112.6 20.4 %collective-permute-start.37 = (bf16[256,1024]{1,0:T(8,128)(2,1)S(1)}, bf16[256,1024]{1,0:T(8,128)(2,1)S(1)}, u32[]{:S(2)}, u32[]{:S(2)}) collective-permute-start(bf16[256,1024]{1,0:T(8,128)(2,1)S(1)} %add_convert_fusion.4), channel_id=1, source_target_pairs={{0,1},{8,9},{4,5},{12,13},{16,17},{24,25},{20,21},{28,29},{32,33},... | collective-permute-start | bytes 1572872 | tf_op jit(solution)/shard_map/ppermute | solution.py:47
  124.2 9.4 %collective-permute-start.38 = (bf16[256,1024]{1,0:T(8,128)(2,1)S(1)}, bf16[256,1024]{1,0:T(8,128)(2,1)S(1)}, u32[]{:S(2)}, u32[]{:S(2)}) collective-permute-start(bf16[256,1024]{1,0:T(8,128)(2,1)S(1)} %add_convert_fusion.3), channel_id=1, source_target_pairs={{0,3},{8,11},{4,7},{12,15},{16,19},{24,27},{20,23},{28,31},{32,35}... | collective-permute-start | bytes 1572872 | tf_op jit(solution)/shard_map/ppermute | solution.py:47
  125.7 6.1 %collective-permute-start.36 = (f32[56,512]{1,0:T(8,128)S(1)}, f32[56,512]{1,0:T(8,128)S(1)}, u32[]{:S(2)}, u32[]{:S(2)}) collective-permute-start(f32[56,512]{1,0:T(8,128)S(1)} %get-tuple-element.99), channel_id=1, source_target_pairs={{0,4},{8,12},{4,0},{12,8},{16,20},{24,28},{20,16},{28,24},{32,36},... | collective-permute-start | bytes 344072 | tf_op jit(solution)/shard_map/ppermute | solution.py:47
  128.7 10.0 %collective-permute-start.29 = (bf16[32,4096]{1,0:T(8,128)(2,1)S(1)}, bf16[32,4096]{1,0:T(8,128)(2,1)S(1)}, u32[]{:S(2)}, u32[]{:S(2)}) collective-permute-start(bf16[32,4096]{1,0:T(8,128)(2,1)S(1)} %get-tuple-element.121), channel_id=1, source_target_pairs={{0,20},{8,28},{4,0},{12,8},{16,4},{24,12},{20,16},{28,24},{32,52},... | collective-permute-start | bytes 786440 | tf_op jit(solution)/shard_map/ppermute | solution.py:47
  130.4 19.1 %collective-permute-start.28 = (bf16[32,4096]{1,0:T(8,128)(2,1)S(1)}, bf16[32,4096]{1,0:T(8,128)(2,1)S(1)}, u32[]{:S(2)}, u32[]{:S(2)}) collective-permute-start(bf16[32,4096]{1,0:T(8,128)(2,1)S(1)} %get-tuple-element.120), channel_id=1, source_target_pairs={{0,16},{8,24},{4,20},{12,28},{16,0},{24,8},{20,4},{28,12},{32,48},... | collective-permute-start | bytes 786440 | tf_op jit(solution)/shard_map/ppermute | solution.py:47
  133.6 8.8 %collective-permute-start.39 = (f32[72,512]{1,0:T(8,128)S(1)}, f32[72,512]{1,0:T(8,128)S(1)}, u32[]{:S(2)}, u32[]{:S(2)}) collective-permute-start(f32[72,512]{1,0:T(8,128)S(1)} %pad_maximum_fusion.4.refs_7_), channel_id=1, source_target_pairs={{0,1},{8,9},{4,5},{12,13},{16,17},{24,25},{20,21},{28,29},{32,33},... | collective-permute-start | bytes 442376 | tf_op jit(solution)/shard_map/ppermute | solution.py:47
  133.7 9.7 %collective-permute-start.40 = (f32[72,512]{1,0:T(8,128)S(1)}, f32[72,512]{1,0:T(8,128)S(1)}, u32[]{:S(2)}, u32[]{:S(2)}) collective-permute-start(f32[72,512]{1,0:T(8,128)S(1)} %pad_maximum_fusion.4.refs_7_), channel_id=1, source_target_pairs={{0,2},{8,10},{4,6},{12,14},{16,18},{24,26},{20,22},{28,30},{32,34}... | collective-permute-start | bytes 442376 | tf_op jit(solution)/shard_map/ppermute | solution.py:47
  138.7 5.1 %collective-permute-start.41 = (f32[72,512]{1,0:T(8,128)S(1)}, f32[72,512]{1,0:T(8,128)S(1)}, u32[]{:S(2)}, u32[]{:S(2)}) collective-permute-start(f32[72,512]{1,0:T(8,128)S(1)} %pad_maximum_fusion.4.refs_7_), channel_id=1, source_target_pairs={{0,3},{8,11},{4,7},{12,15},{16,19},{24,27},{20,23},{28,31},{32,35}... | collective-permute-start | bytes 442376 | tf_op jit(solution)/shard_map/ppermute | solution.py:47
  138.7 10.8 %collective-permute-start.30 = (bf16[32,4096]{1,0:T(8,128)(2,1)S(1)}, bf16[32,4096]{1,0:T(8,128)(2,1)S(1)}, u32[]{:S(2)}, u32[]{:S(2)}) collective-permute-start(bf16[32,4096]{1,0:T(8,128)(2,1)S(1)} %collective-permute-done.29), channel_id=1, source_target_pairs={{0,20},{8,28},{4,0},{12,8},{16,4},{24,12},{20,16},{28,24},{32,52},... | collective-permute-start | bytes 786440 | tf_op jit(solution)/shard_map/ppermute | solution.py:47
  (7 other events, 70.2 us)

commit v14 on v12

--- a/solution.py
+++ b/solution.py
@@ -420,10 +420,10 @@
     up_sum, down_sum = hop(up_sum, x=1), hop(down_sum, x=-1)
     others = hop(sums, pair=1)
     sums_pair = jnp.concatenate([sums[:modes], others[:modes], sums[modes:] + others[modes:]])
-    sums_pair, up_sum, down_sum = together(sums_pair, up_sum, down_sum)
     crossed = jnp.concatenate([crossed, hop(halfway, z=-1)], axis=1)
     mixed = add(own[:part], crossed).astype(BF16)
     all_sums = spread_over_x(sums_pair)
+    all_sums[0], up_sum, down_sum = together(all_sums[0], up_sum, down_sum)
     grad_weight = jnp.concatenate(
         [add(weights[0][:cut], up_sum, down_rest), add(weights[0][cut:], up_rest, down_sum)]
     ).astype(BF16)

time: 151 us -> 150 us (level)
  transfers between devices with their start and end apart: 42 -> 42, of which waited for: 17 -> 15; matrix products, arithmetic and copies ran while one was open for 19% -> 19% of each run, Pallas kernels for 18% -> 18%
where the time goes in v14:
time: 150 us
  starting transfers between devices  50.1 us (33%)
  waiting for transfers between devices  37.1 us (25%)
  Pallas kernels  27.3 us (18%)
  local copies, waits for them, and re-layouts  15.6 us (10%)
  matrix products  10.6 us (7%)
  other arithmetic  7.95 us (5%)
    ppermute x42, starting transfers between devices, hop(): return lax.ppermute(value, ('chan', 'seq'), moves)  50.1 us
    ppermute x42, waiting for transfers between devices, hop(): return lax.ppermute(value, ('chan', 'seq'), moves)  37.1 us
    pallas_call x4, Pallas kernels, call(): pl.pallas_call(body, out_shape=[jax.ShapeDtypeStruct(o.shape, o.dtype) fo...  20.4 us
    dynamic_update_slice x16, local copies, waits for them, and re-layouts, place_blocks(): lax.dynamic_update_slice(whole, part[None, None, :, None], (side, row, 0,...  6.98 us
    pallas_call x1, Pallas kernels, project(): pl.pallas_call(project_tile, grid=(width // tile,), out_shape=[jax.ShapeD...  6.86 us
    dot_general x4, matrix products, weigh(): lax.dot_general(gated, columns, (((0,), (0,)), ((), ())), preferred_eleme...  6.1 us
    dot_general x1, matrix products, local(): lax.dot_general(cot_rows, low_weight, (((1,), (1,)), ((), ())), preferred...  4.52 us
  transfers between devices with their start and end apart: 42, of which 15 were waited for; matrix products, arithmetic and copies ran while one was open for 19% of the time, Pallas kernels for 18%

profile of v14, /device:TPU:0, one launch (start us, length us, event | category | flops | bytes accessed | tf_op | source)
XLA Modules:
  0.0 149.9 jit_solution(15181024671646308370)
XLA Ops:
  0.7 1.1 constant_dynamic-slice_fusion.1
  1.8 2.1 %collective-permute-start.1 = (bf16[32,4096]{1,0:T(8,128)(2,1)S(1)}, bf16[32,4096]{1,0:T(8,128)(2,1)S(1)}, u32[]{:S(2)}, u32[]{:S(2)}) collective-permute-start(bf16[32,4096]{1,0:T(8,128)(2,1)S(1)} %get-tuple-element.127), channel_id=1, source_target_pairs={{0,4},{8,12},{4,16},{12,24},{16,20},{24,28},{20,0},{28,8},{32,36},... | collective-permute-start | bytes 786440 | tf_op jit(solution)/shard_map/ppermute | solution.py:47
  3.9 2.2 %collective-permute-start.2 = (bf16[32,4096]{1,0:T(8,128)(2,1)S(1)}, bf16[32,4096]{1,0:T(8,128)(2,1)S(1)}, u32[]{:S(2)}, u32[]{:S(2)}) collective-permute-start(bf16[32,4096]{1,0:T(8,128)(2,1)S(1)} %get-tuple-element.127), channel_id=1, source_target_pairs={{0,20},{8,28},{4,0},{12,8},{16,4},{24,12},{20,16},{28,24},{32,52},... | collective-permute-start | bytes 786440 | tf_op jit(solution)/shard_map/ppermute | solution.py:47
  6.1 1.8 %collective-permute-start = (bf16[32,4096]{1,0:T(8,128)(2,1)S(1)}, bf16[32,4096]{1,0:T(8,128)(2,1)S(1)}, u32[]{:S(2)}, u32[]{:S(2)}) collective-permute-start(bf16[32,4096]{1,0:T(8,128)(2,1)S(1)} %get-tuple-element.126), channel_id=1, source_target_pairs={{0,16},{8,24},{4,20},{12,28},{16,0},{24,8},{20,4},{28,12},{32,48},... | collective-permute-start | bytes 786440 | tf_op jit(solution)/shard_map/ppermute | solution.py:47
  7.9 4.4 %collective-permute-done.1 = bf16[32,4096]{1,0:T(8,128)(2,1)S(1)} collective-permute-done((bf16[32,4096]{1,0:T(8,128)(2,1)S(1)}, bf16[32,4096]{1,0:T(8,128)(2,1)S(1)}, u32[]{:S(2)}, u32[]{:S(2)}) %collective-permute-start.1) | collective-permute-done | bytes 262176 | tf_op jit(solution)/shard_map/ppermute | solution.py:47
  12.3 5.0 %collective-permute-done.2 = bf16[32,4096]{1,0:T(8,128)(2,1)S(1)} collective-permute-done((bf16[32,4096]{1,0:T(8,128)(2,1)S(1)}, bf16[32,4096]{1,0:T(8,128)(2,1)S(1)}, u32[]{:S(2)}, u32[]{:S(2)}) %collective-permute-start.2) | collective-permute-done | bytes 262176 | tf_op jit(solution)/shard_map/ppermute | solution.py:47
  17.5 1.7 %collective-permute-done = bf16[32,4096]{1,0:T(8,128)(2,1)S(1)} collective-permute-done((bf16[32,4096]{1,0:T(8,128)(2,1)S(1)}, bf16[32,4096]{1,0:T(8,128)(2,1)S(1)}, u32[]{:S(2)}, u32[]{:S(2)}) %collective-permute-start) | collective-permute-done | bytes 262176 | tf_op jit(solution)/shard_map/ppermute | solution.py:47
  20.4 1.6 %collective-permute-start.5 = (bf16[2,32,4096]{2,1,0:T(8,128)(2,1)}, bf16[2,32,4096]{2,1,0:T(8,128)(2,1)S(1)}, u32[]{:S(2)}, u32[]{:S(2)}) collective-permute-start(bf16[2,32,4096]{2,1,0:T(8,128)(2,1)} %get-tuple-element.125), channel_id=1, source_target_pairs={{0,32},{8,40},{4,36},{12,44},{16,48},{24,56},{20,52},{28,60},{32,6... | collective-permute-start | bytes 1572872 | tf_op jit(solution)/shard_map/ppermute | solution.py:47
  22.2 1.7 %collective-permute-start.6 = (bf16[2,32,4096]{2,1,0:T(8,128)(2,1)}, bf16[2,32,4096]{2,1,0:T(8,128)(2,1)S(1)}, u32[]{:S(2)}, u32[]{:S(2)}) collective-permute-start(bf16[2,32,4096]{2,1,0:T(8,128)(2,1)} %get-tuple-element.124), channel_id=1, source_target_pairs={{0,96},{8,104},{4,100},{12,108},{16,112},{24,120},{20,116},{28,124... | collective-permute-start | bytes 1572872 | tf_op jit(solution)/shard_map/ppermute | solution.py:47
  23.9 3.2 %forward_ends.1 = (f32[32,512]{1,0:T(8,128)S(1)}, f32[4,256,128]{2,1,0:T(8,128)S(1)}, f32[4,512,128]{2,1,0:T(8,128)S(1)}) custom-call(bf16[512,512]{1,0:T(8,128)(2,1)S(1)} %copy-done, bf16[512,512]{1,0:T(8,128)(2,1)S(1)} %copy-done.1, f32[16,512]{1,0:T(8,128)S(1)} %copy-done.3), custom_call_target="tpu_custom_call" | custom-call | flops 115000000 | tf_op jit(solution)/shard_map/forward_ends/pallas_call | solution.py:311
  27.2 1.2 collective-permute-start.7
  29.5 2.0 %collective-permute-done.7 = f32[32,512]{1,0:T(8,128)S(1)} collective-permute-done((f32[32,512]{1,0:T(8,128)S(1)}, f32[32,512]{1,0:T(8,128)S(1)}, u32[]{:S(2)}, u32[]{:S(2)}) %collective-permute-start.7) | collective-permute-done | bytes 65568 | tf_op jit(solution)/shard_map/ppermute | solution.py:47
  31.8 4.7 %collective-permute-done.5 = bf16[2,32,4096]{2,1,0:T(8,128)(2,1)S(1)} collective-permute-done((bf16[2,32,4096]{2,1,0:T(8,128)(2,1)}, bf16[2,32,4096]{2,1,0:T(8,128)(2,1)S(1)}, u32[]{:S(2)}, u32[]{:S(2)}) %collective-permute-start.5) | collective-permute-done | bytes 524320 | tf_op jit(solution)/shard_map/ppermute | solution.py:47
  36.5 1.8 %collective-permute-start.4 = (bf16[2,32,4096]{2,1,0:T(8,128)(2,1)}, bf16[2,32,4096]{2,1,0:T(8,128)(2,1)S(1)}, u32[]{:S(2)}, u32[]{:S(2)}) collective-permute-start(bf16[2,32,4096]{2,1,0:T(8,128)(2,1)} %get-tuple-element.125), channel_id=1, source_target_pairs={{0,96},{8,104},{4,100},{12,108},{16,112},{24,120},{20,116},{28,124... | collective-permute-start | bytes 1572872 | tf_op jit(solution)/shard_map/ppermute | solution.py:47
  38.3 1.5 collective-permute-start.8
  39.8 2.7 %collective-permute-start.9 = (f32[64,512]{1,0:T(8,128)S(1)}, f32[64,512]{1,0:T(8,128)S(1)}, u32[]{:S(2)}, u32[]{:S(2)}) collective-permute-start(f32[64,512]{1,0:T(8,128)S(1)} %pad_maximum_fusion.5.refs_6_), channel_id=1, source_target_pairs={{0,2},{8,10},{4,6},{12,14},{16,18},{24,26},{20,22},{28,30},{32,34}... | collective-permute-start | bytes 393224 | tf_op jit(solution)/shard_map/ppermute | solution.py:47
  43.7 1.5 %collective-permute-start.10 = (f32[64,512]{1,0:T(8,128)S(1)}, f32[64,512]{1,0:T(8,128)S(1)}, u32[]{:S(2)}, u32[]{:S(2)}) collective-permute-start(f32[64,512]{1,0:T(8,128)S(1)} %pad_maximum_fusion.5.refs_6_), channel_id=1, source_target_pairs={{0,3},{8,11},{4,7},{12,15},{16,19},{24,27},{20,23},{28,31},{32,35}... | collective-permute-start | bytes 393224 | tf_op jit(solution)/shard_map/ppermute | solution.py:47
  46.3 1.5 %collective-permute-done.9.refs_8_ = f32[64,512]{1,0:T(8,128)S(1)} collective-permute-done((f32[64,512]{1,0:T(8,128)S(1)}, f32[64,512]{1,0:T(8,128)S(1)}, u32[]{:S(2)}, u32[]{:S(2)}) %collective-permute-start.9) | collective-permute-done | bytes 131104 | tf_op jit(solution)/shard_map/ppermute | solution.py:47
  48.8 3.8 %forward_full.1 = (bf16[512,512]{1,0:T(8,128)(2,1)S(1)}, bf16[512,512]{1,0:T(8,128)(2,1)S(1)}, f32[4,512,128]{2,1,0:T(8,128)S(1)}, f32[4,256,128]{2,1,0:T(8,128)S(1)}) custom-call(bf16[512,512]{1,0:T(8,128)(2,1)S(1)} %copy-done.2, f32[4,512,128]{2,1,0:T(8,128)S(1)} %get-tuple-element.65.refs_1_.drive_ref, f32[4,256,128]{2,1,0:T(8,128)S(1)} %get-tuple-element.66.refs_2_, ...), custom_call_target="tpu_custom_call" | custom-call | flops 115000000 | tf_op jit(solution)/shard_map/forward_full/pallas_call | solution.py:311
  53.2 3.0 %collective-permute-start.18 = (bf16[2,32,4096]{2,1,0:T(8,128)(2,1)S(1)}, bf16[2,32,4096]{2,1,0:T(8,128)(2,1)S(1)}, u32[]{:S(2)}, u32[]{:S(2)}) collective-permute-start(bf16[2,32,4096]{2,1,0:T(8,128)(2,1)S(1)} %collective-permute-done.6), channel_id=1, source_target_pairs={{0,96},{8,104},{4,100},{12,108},{16,112},{24,120},{20,116},{28,124... | collective-permute-start | bytes 1572872 | tf_op jit(solution)/shard_map/ppermute | solution.py:47
  56.2 1.1 collective-permute-start.23
  58.2 6.9 %project.1 = (bf16[64,8192]{1,0:T(8,128)(2,1)S(1)}, bf16[192,8192]{1,0:T(8,128)(2,1)S(1)}, bf16[64,8192]{1,0:T(8,128)(2,1)S(1)}, bf16[192,8192]{1,0:T(8,128)(2,1)S(1)}) custom-call(bf16[512,512]{1,0:T(8,128)(2,1)S(1)} %get-tuple-element.70.rows_ref, bf16[512,8192]{1,0:T(8,128)(2,1)S(1)} %bitcast.83), custom_call_target="tpu_custom_call" | custom-call | flops 4294967296 | bytes 16777216 | tf_op jit(solution)/shard_map/project/pallas_call | solution.py:92
  70.4 1.9 %constant_dynamic-update-slice_fusion = bf16[1024,512]{1,0:T(8,128)(2,1)} fusion(bf16[1024,512]{1,0:T(8,128)(2,1)} %constant_dynamic-update-slice_fusion.1, bf16[512,512]{1,0:T(8,128)(2,1)} %collective-permute-done.23), kind=kLoop, calls=%fused_computation.61 | loop fusion | bytes 1048576 | tf_op jit(solution)/shard_map/concatenate | solution.py:373
  72.3 1.2 bitcast_dynamic-update-slice_fusion.3
  74.9 1.7 %collective-permute-start.24 = (bf16[32,8192]{1,0:T(8,128)(2,1)S(1)}, bf16[32,8192]{1,0:T(8,128)(2,1)S(1)}, u32[]{:S(2)}, u32[]{:S(2)}) collective-permute-start(bf16[32,8192]{1,0:T(8,128)(2,1)S(1)} %get-tuple-element.122), channel_id=1, source_target_pairs={{0,32},{8,40},{4,36},{12,44},{16,48},{24,56},{20,52},{28,60},{32,6... | collective-permute-start | bytes 1572872 | tf_op jit(solution)/shard_map/ppermute | solution.py:47
  78.4 1.6 %copy-done.6 = bf16[192,8192]{1,0:T(8,128)(2,1)} copy-done((bf16[192,8192]{1,0:T(8,128)(2,1)}, bf16[192,8192]{1,0:T(8,128)(2,1)S(1)}, u32[]{:S(2)}) %copy-start.6) | copy-done | bytes 3145752
  80.0 2.3 %multiply_convert_fusion.3 = bf16[512,1024]{1,0:T(8,128)(2,1)} fusion(bf16[1024,512]{1,0:T(8,128)(2,1)S(1)} %copy-done.9, bf16[1024,4096]{1,0:T(8,128)(2,1)S(1)} %bitcast.84, s32[]{:T(128)S(6)} %select_n.130), kind=kOutput, calls=%fused_computation.14 | convolution fusion | flops 1074790400 | bytes 4194308 | tf_op jit(solution)/shard_map/dot_general | solution.py:110
  82.3 4.5 %fusion = f32[1024,512]{1,0:T(8,128)S(1)} fusion(bf16[1024,4096]{1,0:T(8,128)(2,1)S(1)} %bitcast.85, bf16[512,8192]{1,0:T(8,128)(2,1)S(1)} %bitcast.83, s32[]{:T(128)S(6)} %select_n.116), kind=kOutput, calls=%fused_computation | convolution fusion | flops 4294967296 | bytes 14680068 | tf_op jit(solution)/shard_map/dot_general | solution.py:385
  86.9 2.1 %convert_add_fusion.2 = (f32[64,8192]{1,0:T(8,128)S(1)}, f32[64,8192]{1,0:T(8,128)S(1)}) fusion(bf16[192,8192]{1,0:T(8,128)(2,1)} %copy-done.6, bf16[192,8192]{1,0:T(8,128)(2,1)S(1)} %get-tuple-element.71), kind=kLoop, calls=%fused_computation.13 | loop fusion | flops 3145728 | bytes 8388608 | tf_op jit(solution)/shard_map/add | solution.py:76
  89.2 1.2 collective-permute-start.27
  92.8 1.1 collective-permute-start.32
  94.0 2.2 %collective-permute-start.33 = (bf16[256,1024]{1,0:T(8,128)(2,1)S(1)}, bf16[256,1024]{1,0:T(8,128)(2,1)S(1)}, u32[]{:S(2)}, u32[]{:S(2)}) collective-permute-start(bf16[256,1024]{1,0:T(8,128)(2,1)S(1)} %get-tuple-element.118), channel_id=1, source_target_pairs={{0,3},{8,11},{4,7},{12,15},{16,19},{24,27},{20,23},{28,31},{32,35}... | collective-permute-start | bytes 1572872 | tf_op jit(solution)/shard_map/ppermute | solution.py:47
  96.1 1.3 multiply_convert_fusion.2
  97.4 1.3 multiply_convert_fusion.1
  98.8 8.7 %collective-permute-done.32 = bf16[256,1024]{1,0:T(8,128)(2,1)S(1)} collective-permute-done((bf16[256,1024]{1,0:T(8,128)(2,1)S(1)}, bf16[256,1024]{1,0:T(8,128)(2,1)S(1)}, u32[]{:S(2)}, u32[]{:S(2)}) %collective-permute-start.32) | collective-permute-done | bytes 524320 | tf_op jit(solution)/shard_map/ppermute | solution.py:47
  108.6 2.6 %collective-permute-start.35 = (bf16[256,1024]{1,0:T(8,128)(2,1)S(1)}, bf16[256,1024]{1,0:T(8,128)(2,1)S(1)}, u32[]{:S(2)}, u32[]{:S(2)}) collective-permute-start(bf16[256,1024]{1,0:T(8,128)(2,1)S(1)} %slice.150), channel_id=1, source_target_pairs={{0,3},{8,11},{4,7},{12,15},{16,19},{24,27},{20,23},{28,31},{32,35}... | collective-permute-start | bytes 1572872 | tf_op jit(solution)/shard_map/ppermute | solution.py:47
  111.2 1.3 multiply_convert_fusion
  112.7 8.3 %backward_ends.1 = (bf16[512,512]{1,0:T(8,128)(2,1)}, f32[4,512,128]{2,1,0:T(8,128)S(1)}, f32[56,512]{1,0:T(8,128)S(1)}, f32[4,128,128]{2,1,0:T(8,128)S(1)}) custom-call(f32[512,512]{1,0:T(8,128)S(1)} %convert_add_fusion.3.grad_ref, bf16[512,512]{1,0:T(8,128)(2,1)S(1)} %copy-done.2, f32[4,512,128]{2,1,0:T(8,128)S(1)} %get-tuple-element.91.pre_ref, ...), custom_call_target="tpu_custom_call" | custom-call | flops 2300000000 | tf_op jit(solution)/shard_map/backward_ends/pallas_call | solution.py:311
  121.0 3.0 %collective-permute-done.34 = bf16[256,1024]{1,0:T(8,128)(2,1)S(1)} collective-permute-done((bf16[256,1024]{1,0:T(8,128)(2,1)S(1)}, bf16[256,1024]{1,0:T(8,128)(2,1)S(1)}, u32[]{:S(2)}, u32[]{:S(2)}) %collective-permute-start.34) | collective-permute-done | bytes 524320 | tf_op jit(solution)/shard_map/ppermute | solution.py:47
  124.0 1.5 %collective-permute-start.38 = (bf16[256,1024]{1,0:T(8,128)(2,1)S(1)}, bf16[256,1024]{1,0:T(8,128)(2,1)S(1)}, u32[]{:S(2)}, u32[]{:S(2)}) collective-permute-start(bf16[256,1024]{1,0:T(8,128)(2,1)S(1)} %add_convert_fusion.3), channel_id=1, source_target_pairs={{0,3},{8,11},{4,7},{12,15},{16,19},{24,27},{20,23},{28,31},{32,35}... | collective-permute-start | bytes 1572872 | tf_op jit(solution)/shard_map/ppermute | solution.py:47
  125.5 1.1 collective-permute-start.36
  126.7 1.7 %fusion.26 = (bf16[64,8192]{1,0:T(8,128)(2,1)S(1)}, f32[64,8192]{1,0:T(8,128)S(1)}) fusion(bf16[64,8192]{1,0:T(8,128)(2,1)S(1)} %collective-permute-done.27, bf16[64,8192]{1,0:T(8,128)(2,1)S(1)} %collective-permute-done.25, bf16[192,8192]{1,0:T(8,128)(2,1)} %copy-done.6, bf16[192,8192]{1,0:T(8,128)(2,1)S(1)} %get-tuple-element.71), kind=kLoop, calls=%fused_computation.70 | loop fusion | flops 4194304 | bytes 7340032 | tf_op jit(solution)/shard_map/convert.3
  128.5 1.7 %collective-permute-start.29 = (bf16[32,4096]{1,0:T(8,128)(2,1)S(1)}, bf16[32,4096]{1,0:T(8,128)(2,1)S(1)}, u32[]{:S(2)}, u32[]{:S(2)}) collective-permute-start(bf16[32,4096]{1,0:T(8,128)(2,1)S(1)} %get-tuple-element.121), channel_id=1, source_target_pairs={{0,20},{8,28},{4,0},{12,8},{16,4},{24,12},{20,16},{28,24},{32,52},... | collective-permute-start | bytes 786440 | tf_op jit(solution)/shard_map/ppermute | solution.py:47
  130.1 1.4 collective-permute-start.28
  132.2 2.2 %collective-permute-done.37 = bf16[256,1024]{1,0:T(8,128)(2,1)S(1)} collective-permute-done((bf16[256,1024]{1,0:T(8,128)(2,1)S(1)}, bf16[256,1024]{1,0:T(8,128)(2,1)S(1)}, u32[]{:S(2)}, u32[]{:S(2)}) %collective-permute-start.37) | collective-permute-done | bytes 524320 | tf_op jit(solution)/shard_map/ppermute | solution.py:47
  136.0 3.7 %collective-permute-start.41 = (f32[72,512]{1,0:T(8,128)S(1)}, f32[72,512]{1,0:T(8,128)S(1)}, u32[]{:S(2)}, u32[]{:S(2)}) collective-permute-start(f32[72,512]{1,0:T(8,128)S(1)} %pad_maximum_fusion.4.refs_7_), channel_id=1, source_target_pairs={{0,3},{8,11},{4,7},{12,15},{16,19},{24,27},{20,23},{28,31},{32,35}... | collective-permute-start | bytes 442376 | tf_op jit(solution)/shard_map/ppermute | solution.py:47
  139.7 2.0 %collective-permute-start.30 = (bf16[32,4096]{1,0:T(8,128)(2,1)S(1)}, bf16[32,4096]{1,0:T(8,128)(2,1)S(1)}, u32[]{:S(2)}, u32[]{:S(2)}) collective-permute-start(bf16[32,4096]{1,0:T(8,128)(2,1)S(1)} %collective-permute-done.29), channel_id=1, source_target_pairs={{0,20},{8,28},{4,0},{12,8},{16,4},{24,12},{20,16},{28,24},{32,52},... | collective-permute-start | bytes 786440 | tf_op jit(solution)/shard_map/ppermute | solution.py:47
  143.3 5.0 %backward_full.1 = (bf16[512,512]{1,0:T(8,128)(2,1)}, bf16[512,512]{1,0:T(8,128)(2,1)}, f32[16,512]{1,0:T(8,128)}, f32[16,512]{1,0:T(8,128)}, f32[8,512]{1,0:T(8,128)S(1)}) custom-call(bf16[512,512]{1,0:T(8,128)(2,1)S(1)} %copy-done, bf16[512,512]{1,0:T(8,128)(2,1)S(1)} %copy-done.1, f32[4,512,128]{2,1,0:T(8,128)S(1)} %get-tuple-element.94.refs_2_, ...), custom_call_target="tpu_custom_call" | custom-call | flops 115000000 | tf_op jit(solution)/shard_map/backward_full/pallas_call | solution.py:311
  (125 shorter events, 25.5 us)
Async XLA Ops:
  0.6 23.3 %copy-start.3 = (f32[16,512]{1,0:T(8,128)S(1)}, f32[16,512]{1,0:T(8,128)}, u32[]{:S(2)}) copy-start(f32[16,512]{1,0:T(8,128)} %refs_4_.3) | copy-start | bytes 98308
  1.8 10.5 %collective-permute-start.1 = (bf16[32,4096]{1,0:T(8,128)(2,1)S(1)}, bf16[32,4096]{1,0:T(8,128)(2,1)S(1)}, u32[]{:S(2)}, u32[]{:S(2)}) collective-permute-start(bf16[32,4096]{1,0:T(8,128)(2,1)S(1)} %get-tuple-element.127), channel_id=1, source_target_pairs={{0,4},{8,12},{4,16},{12,24},{16,20},{24,28},{20,0},{28,8},{32,36},... | collective-permute-start | bytes 786440 | tf_op jit(solution)/shard_map/ppermute | solution.py:47
  3.9 13.4 %collective-permute-start.2 = (bf16[32,4096]{1,0:T(8,128)(2,1)S(1)}, bf16[32,4096]{1,0:T(8,128)(2,1)S(1)}, u32[]{:S(2)}, u32[]{:S(2)}) collective-permute-start(bf16[32,4096]{1,0:T(8,128)(2,1)S(1)} %get-tuple-element.127), channel_id=1, source_target_pairs={{0,20},{8,28},{4,0},{12,8},{16,4},{24,12},{20,16},{28,24},{32,52},... | collective-permute-start | bytes 786440 | tf_op jit(solution)/shard_map/ppermute | solution.py:47
  6.1 13.0 %collective-permute-start = (bf16[32,4096]{1,0:T(8,128)(2,1)S(1)}, bf16[32,4096]{1,0:T(8,128)(2,1)S(1)}, u32[]{:S(2)}, u32[]{:S(2)}) collective-permute-start(bf16[32,4096]{1,0:T(8,128)(2,1)S(1)} %get-tuple-element.126), channel_id=1, source_target_pairs={{0,16},{8,24},{4,20},{12,28},{16,0},{24,8},{20,4},{28,12},{32,48},... | collective-permute-start | bytes 786440 | tf_op jit(solution)/shard_map/ppermute | solution.py:47
  19.3 29.4 %copy-start.2 = (bf16[512,512]{1,0:T(8,128)(2,1)S(1)}, bf16[512,512]{1,0:T(8,128)(2,1)}, u32[]{:S(2)}) copy-start(bf16[512,512]{1,0:T(8,128)(2,1)} %query_ref.1) | copy-start | bytes 1572868
  19.3 29.4 %copy-start.4 = (f32[16,512]{1,0:T(8,128)S(1)}, f32[16,512]{1,0:T(8,128)}, u32[]{:S(2)}) copy-start(f32[16,512]{1,0:T(8,128)} %refs_5_.1) | copy-start | bytes 98308
  19.3 29.4 %copy-start.5 = (f32[512]{0:T(512)S(1)}, f32[512]{0:T(512)}, u32[]{:S(2)}) copy-start(f32[512]{0:T(512)} %param.11) | copy-start | bytes 6148
  20.4 19.4 %collective-permute-start.11 = (bf16[2,32,4096]{2,1,0:T(8,128)(2,1)}, bf16[2,32,4096]{2,1,0:T(8,128)(2,1)}, u32[]{:S(2)}, u32[]{:S(2)}) collective-permute-start(bf16[2,32,4096]{2,1,0:T(8,128)(2,1)} %get-tuple-element.125), channel_id=1, source_target_pairs={{0,8},{8,0},{4,12},{12,4},{16,24},{24,16},{20,28},{28,20},{32,40},... | collective-permute-start | bytes 1572872 | tf_op jit(solution)/shard_map/ppermute | solution.py:47
  20.4 16.1 %collective-permute-start.5 = (bf16[2,32,4096]{2,1,0:T(8,128)(2,1)}, bf16[2,32,4096]{2,1,0:T(8,128)(2,1)S(1)}, u32[]{:S(2)}, u32[]{:S(2)}) collective-permute-start(bf16[2,32,4096]{2,1,0:T(8,128)(2,1)} %get-tuple-element.125), channel_id=1, source_target_pairs={{0,32},{8,40},{4,36},{12,44},{16,48},{24,56},{20,52},{28,60},{32,6... | collective-permute-start | bytes 1572872 | tf_op jit(solution)/shard_map/ppermute | solution.py:47
  22.0 21.7 %collective-permute-start.12 = (bf16[2,32,4096]{2,1,0:T(8,128)(2,1)}, bf16[2,32,4096]{2,1,0:T(8,128)(2,1)}, u32[]{:S(2)}, u32[]{:S(2)}) collective-permute-start(bf16[2,32,4096]{2,1,0:T(8,128)(2,1)} %get-tuple-element.124), channel_id=1, source_target_pairs={{0,8},{8,0},{4,12},{12,4},{16,24},{24,16},{20,28},{28,20},{32,40},... | collective-permute-start | bytes 1572872 | tf_op jit(solution)/shard_map/ppermute | solution.py:47
  22.2 16.1 %collective-permute-start.6 = (bf16[2,32,4096]{2,1,0:T(8,128)(2,1)}, bf16[2,32,4096]{2,1,0:T(8,128)(2,1)S(1)}, u32[]{:S(2)}, u32[]{:S(2)}) collective-permute-start(bf16[2,32,4096]{2,1,0:T(8,128)(2,1)} %get-tuple-element.124), channel_id=1, source_target_pairs={{0,96},{8,104},{4,100},{12,108},{16,112},{24,120},{20,116},{28,124... | collective-permute-start | bytes 1572872 | tf_op jit(solution)/shard_map/ppermute | solution.py:47
  27.1 31.0 %slice-start = ((s8[8388608]{0:T(1024)(128)(4,1)}), s8[4194304]{0:T(1024)(128)(4,1)S(1)}, s32[]{:S(2)}) async-start(s8[8388608]{0:T(1024)(128)(4,1)} %bitcast.82), calls=%async_computation | async-start | bytes 8388608
  27.2 4.3 %collective-permute-start.7 = (f32[32,512]{1,0:T(8,128)S(1)}, f32[32,512]{1,0:T(8,128)S(1)}, u32[]{:S(2)}, u32[]{:S(2)}) collective-permute-start(f32[32,512]{1,0:T(8,128)S(1)} %get-tuple-element.62), channel_id=1, source_target_pairs={{0,4},{8,12},{4,0},{12,8},{16,20},{24,28},{20,16},{28,24},{32,36},... | collective-permute-start | bytes 196616 | tf_op jit(solution)/shard_map/ppermute | solution.py:47
  29.4 28.8 %slice-start.1 = ((s8[8388608]{0:T(1024)(128)(4,1)}), s8[4194304]{0:T(1024)(128)(4,1)S(1)}, s32[]{:S(2)}) async-start(s8[8388608]{0:T(1024)(128)(4,1)} %bitcast.82), calls=%async_computation.1 | async-start | bytes 8388608
  31.5 21.7 %collective-permute-start.3 = (bf16[2,32,4096]{2,1,0:T(8,128)(2,1)}, bf16[2,32,4096]{2,1,0:T(8,128)(2,1)}, u32[]{:S(2)}, u32[]{:S(2)}) collective-permute-start(bf16[2,32,4096]{2,1,0:T(8,128)(2,1)} %get-tuple-element.124), channel_id=1, source_target_pairs={{0,32},{8,40},{4,36},{12,44},{16,48},{24,56},{20,52},{28,60},{32,6... | collective-permute-start | bytes 1572872 | tf_op jit(solution)/shard_map/ppermute | solution.py:47
  36.5 19.6 %collective-permute-start.4 = (bf16[2,32,4096]{2,1,0:T(8,128)(2,1)}, bf16[2,32,4096]{2,1,0:T(8,128)(2,1)S(1)}, u32[]{:S(2)}, u32[]{:S(2)}) collective-permute-start(bf16[2,32,4096]{2,1,0:T(8,128)(2,1)} %get-tuple-element.125), channel_id=1, source_target_pairs={{0,96},{8,104},{4,100},{12,108},{16,112},{24,120},{20,116},{28,124... | collective-permute-start | bytes 1572872 | tf_op jit(solution)/shard_map/ppermute | solution.py:47
  38.3 8.0 %collective-permute-start.8 = (f32[64,512]{1,0:T(8,128)S(1)}, f32[64,512]{1,0:T(8,128)S(1)}, u32[]{:S(2)}, u32[]{:S(2)}) collective-permute-start(f32[64,512]{1,0:T(8,128)S(1)} %pad_maximum_fusion.5.refs_6_), channel_id=1, source_target_pairs={{0,1},{8,9},{4,5},{12,13},{16,17},{24,25},{20,21},{28,29},{32,33},... | collective-permute-start | bytes 393224 | tf_op jit(solution)/shard_map/ppermute | solution.py:47
  39.8 8.0 %collective-permute-start.9 = (f32[64,512]{1,0:T(8,128)S(1)}, f32[64,512]{1,0:T(8,128)S(1)}, u32[]{:S(2)}, u32[]{:S(2)}) collective-permute-start(f32[64,512]{1,0:T(8,128)S(1)} %pad_maximum_fusion.5.refs_6_), channel_id=1, source_target_pairs={{0,2},{8,10},{4,6},{12,14},{16,18},{24,26},{20,22},{28,30},{32,34}... | collective-permute-start | bytes 393224 | tf_op jit(solution)/shard_map/ppermute | solution.py:47
  43.7 5.0 %collective-permute-start.10 = (f32[64,512]{1,0:T(8,128)S(1)}, f32[64,512]{1,0:T(8,128)S(1)}, u32[]{:S(2)}, u32[]{:S(2)}) collective-permute-start(f32[64,512]{1,0:T(8,128)S(1)} %pad_maximum_fusion.5.refs_6_), channel_id=1, source_target_pairs={{0,3},{8,11},{4,7},{12,15},{16,19},{24,27},{20,23},{28,31},{32,35}... | collective-permute-start | bytes 393224 | tf_op jit(solution)/shard_map/ppermute | solution.py:47
  52.6 12.5 %collective-permute-start.13 = (bf16[2,32,4096]{2,1,0:T(8,128)(2,1)S(1)}, bf16[2,32,4096]{2,1,0:T(8,128)(2,1)}, u32[]{:S(2)}, u32[]{:S(2)}) collective-permute-start(bf16[2,32,4096]{2,1,0:T(8,128)(2,1)S(1)} %collective-permute-done.5), channel_id=1, source_target_pairs={{0,8},{8,0},{4,12},{12,4},{16,24},{24,16},{20,28},{28,20},{32,40},... | collective-permute-start | bytes 1572872 | tf_op jit(solution)/shard_map/ppermute | solution.py:47
  52.7 21.0 %collective-permute-start.17 = (bf16[2,32,4096]{2,1,0:T(8,128)(2,1)S(1)}, bf16[2,32,4096]{2,1,0:T(8,128)(2,1)S(1)}, u32[]{:S(2)}, u32[]{:S(2)}) collective-permute-start(bf16[2,32,4096]{2,1,0:T(8,128)(2,1)S(1)} %collective-permute-done.5), channel_id=1, source_target_pairs={{0,32},{8,40},{4,36},{12,44},{16,48},{24,56},{20,52},{28,60},{32,6... | collective-permute-start | bytes 1572872 | tf_op jit(solution)/shard_map/ppermute | solution.py:47
  53.0 19.3 %collective-permute-start.16 = (bf16[2,32,4096]{2,1,0:T(8,128)(2,1)S(1)}, bf16[2,32,4096]{2,1,0:T(8,128)(2,1)}, u32[]{:S(2)}, u32[]{:S(2)}) collective-permute-start(bf16[2,32,4096]{2,1,0:T(8,128)(2,1)S(1)} %collective-permute-done.6), channel_id=1, source_target_pairs={{0,8},{8,0},{4,12},{12,4},{16,24},{24,16},{20,28},{28,20},{32,40},... | collective-permute-start | bytes 1572872 | tf_op jit(solution)/shard_map/ppermute | solution.py:47
  53.2 20.5 %collective-permute-start.18 = (bf16[2,32,4096]{2,1,0:T(8,128)(2,1)S(1)}, bf16[2,32,4096]{2,1,0:T(8,128)(2,1)S(1)}, u32[]{:S(2)}, u32[]{:S(2)}) collective-permute-start(bf16[2,32,4096]{2,1,0:T(8,128)(2,1)S(1)} %collective-permute-done.6), channel_id=1, source_target_pairs={{0,96},{8,104},{4,100},{12,108},{16,112},{24,120},{20,116},{28,124... | collective-permute-start | bytes 1572872 | tf_op jit(solution)/shard_map/ppermute | solution.py:47
  56.2 14.0 %collective-permute-start.23 = (bf16[512,512]{1,0:T(8,128)(2,1)S(1)}, bf16[512,512]{1,0:T(8,128)(2,1)}, u32[]{:S(2)}, u32[]{:S(2)}) collective-permute-start(bf16[512,512]{1,0:T(8,128)(2,1)S(1)} %get-tuple-element.82), channel_id=1, source_target_pairs={{0,4},{8,12},{4,0},{12,8},{16,20},{24,28},{20,16},{28,24},{32,36},... | collective-permute-start | bytes 1572872 | tf_op jit(solution)/shard_map/ppermute | solution.py:47
  65.1 2.3 %collective-permute-start.14 = (bf16[2,32,4096]{2,1,0:T(8,128)(2,1)}, bf16[2,32,4096]{2,1,0:T(8,128)(2,1)S(1)}, u32[]{:S(2)}, u32[]{:S(2)}) collective-permute-start(bf16[2,32,4096]{2,1,0:T(8,128)(2,1)} %collective-permute-done.3), channel_id=1, source_target_pairs={{0,8},{8,0},{4,12},{12,4},{16,24},{24,16},{20,28},{28,20},{32,40},... | collective-permute-start | bytes 1572872 | tf_op jit(solution)/shard_map/ppermute | solution.py:47
  67.4 2.3 %collective-permute-start.15 = (bf16[2,32,4096]{2,1,0:T(8,128)(2,1)}, bf16[2,32,4096]{2,1,0:T(8,128)(2,1)S(1)}, u32[]{:S(2)}, u32[]{:S(2)}) collective-permute-start(bf16[2,32,4096]{2,1,0:T(8,128)(2,1)} %copy-done.8), channel_id=1, source_target_pairs={{0,8},{8,0},{4,12},{12,4},{16,24},{24,16},{20,28},{28,20},{32,40},... | collective-permute-start | bytes 1572872 | tf_op jit(solution)/shard_map/ppermute | solution.py:47
  69.7 3.7 %collective-permute-start.19 = (bf16[64,8192]{1,0:T(8,128)(2,1)S(1)}, bf16[64,8192]{1,0:T(8,128)(2,1)S(1)}, u32[]{:S(2)}, u32[]{:S(2)}) collective-permute-start(bf16[64,8192]{1,0:T(8,128)(2,1)S(1)} %get-tuple-element.77), channel_id=1, source_target_pairs={{0,8},{8,0},{4,12},{12,4},{16,24},{24,16},{20,28},{28,20},{32,40},... | collective-permute-start | bytes 3145736 | tf_op jit(solution)/shard_map/ppermute | solution.py:47
  70.2 8.2 %collective-permute-start.22 = (bf16[192,8192]{1,0:T(8,128)(2,1)S(1)}, bf16[192,8192]{1,0:T(8,128)(2,1)S(1)}, u32[]{:S(2)}, u32[]{:S(2)}) collective-permute-start(bf16[192,8192]{1,0:T(8,128)(2,1)S(1)} %get-tuple-element.80), channel_id=1, source_target_pairs={{0,8},{8,0},{4,12},{12,4},{16,24},{24,16},{20,28},{28,20},{32,40},... | collective-permute-start | bytes 9437192 | tf_op jit(solution)/shard_map/ppermute | solution.py:47
  73.7 3.9 %collective-permute-start.20 = (bf16[2,32,4096]{2,1,0:T(8,128)(2,1)S(1)}, bf16[2,32,4096]{2,1,0:T(8,128)(2,1)S(1)}, u32[]{:S(2)}, u32[]{:S(2)}) collective-permute-start(bf16[2,32,4096]{2,1,0:T(8,128)(2,1)S(1)} %collective-permute-done.17), channel_id=1, source_target_pairs={{0,8},{8,0},{4,12},{12,4},{16,24},{24,16},{20,28},{28,20},{32,40},... | collective-permute-start | bytes 1572872 | tf_op jit(solution)/shard_map/ppermute | solution.py:47
  74.2 4.2 %collective-permute-start.21 = (bf16[2,32,4096]{2,1,0:T(8,128)(2,1)S(1)}, bf16[2,32,4096]{2,1,0:T(8,128)(2,1)S(1)}, u32[]{:S(2)}, u32[]{:S(2)}) collective-permute-start(bf16[2,32,4096]{2,1,0:T(8,128)(2,1)S(1)} %collective-permute-done.18), channel_id=1, source_target_pairs={{0,8},{8,0},{4,12},{12,4},{16,24},{24,16},{20,28},{28,20},{32,40},... | collective-permute-start | bytes 1572872 | tf_op jit(solution)/shard_map/ppermute | solution.py:47
  74.5 14.5 %collective-permute-start.26 = (bf16[32,8192]{1,0:T(8,128)(2,1)S(1)}, bf16[32,8192]{1,0:T(8,128)(2,1)S(1)}, u32[]{:S(2)}, u32[]{:S(2)}) collective-permute-start(bf16[32,8192]{1,0:T(8,128)(2,1)S(1)} %get-tuple-element.123), channel_id=1, source_target_pairs={{0,96},{8,104},{4,100},{12,108},{16,112},{24,120},{20,116},{28,124... | collective-permute-start | bytes 1572872 | tf_op jit(solution)/shard_map/ppermute | solution.py:47
  74.9 15.6 %collective-permute-start.24 = (bf16[32,8192]{1,0:T(8,128)(2,1)S(1)}, bf16[32,8192]{1,0:T(8,128)(2,1)S(1)}, u32[]{:S(2)}, u32[]{:S(2)}) collective-permute-start(bf16[32,8192]{1,0:T(8,128)(2,1)S(1)} %get-tuple-element.122), channel_id=1, source_target_pairs={{0,32},{8,40},{4,36},{12,44},{16,48},{24,56},{20,52},{28,60},{32,6... | collective-permute-start | bytes 1572872 | tf_op jit(solution)/shard_map/ppermute | solution.py:47
  89.2 37.4 %collective-permute-start.27 = (bf16[64,8192]{1,0:T(8,128)(2,1)S(1)}, bf16[64,8192]{1,0:T(8,128)(2,1)S(1)}, u32[]{:S(2)}, u32[]{:S(2)}) collective-permute-start(bf16[64,8192]{1,0:T(8,128)(2,1)S(1)} %pad_maximum_fusion.2), channel_id=1, source_target_pairs={{0,96},{8,104},{4,100},{12,108},{16,112},{24,120},{20,116},{28,124... | collective-permute-start | bytes 3145736 | tf_op jit(solution)/shard_map/ppermute | solution.py:47
  90.7 36.0 %collective-permute-start.25 = (bf16[64,8192]{1,0:T(8,128)(2,1)S(1)}, bf16[64,8192]{1,0:T(8,128)(2,1)S(1)}, u32[]{:S(2)}, u32[]{:S(2)}) collective-permute-start(bf16[64,8192]{1,0:T(8,128)(2,1)S(1)} %pad_maximum_fusion.1), channel_id=1, source_target_pairs={{0,32},{8,40},{4,36},{12,44},{16,48},{24,56},{20,52},{28,60},{32,6... | collective-permute-start | bytes 3145736 | tf_op jit(solution)/shard_map/ppermute | solution.py:47
  91.8 16.1 %collective-permute-start.31 = (bf16[512,512]{1,0:T(8,128)(2,1)S(1)}, bf16[512,512]{1,0:T(8,128)(2,1)S(1)}, u32[]{:S(2)}, u32[]{:S(2)}) collective-permute-start(bf16[512,512]{1,0:T(8,128)(2,1)S(1)} %slice.184), channel_id=1, source_target_pairs={{0,4},{8,12},{4,0},{12,8},{16,20},{24,28},{20,16},{28,24},{32,36},... | collective-permute-start | bytes 1572872 | tf_op jit(solution)/shard_map/ppermute | solution.py:47
  92.8 14.6 %collective-permute-start.32 = (bf16[256,1024]{1,0:T(8,128)(2,1)S(1)}, bf16[256,1024]{1,0:T(8,128)(2,1)S(1)}, u32[]{:S(2)}, u32[]{:S(2)}) collective-permute-start(bf16[256,1024]{1,0:T(8,128)(2,1)S(1)} %get-tuple-element.119), channel_id=1, source_target_pairs={{0,1},{8,9},{4,5},{12,13},{16,17},{24,25},{20,21},{28,29},{32,33},... | collective-permute-start | bytes 1572872 | tf_op jit(solution)/shard_map/ppermute | solution.py:47
  94.0 13.7 %collective-permute-start.33 = (bf16[256,1024]{1,0:T(8,128)(2,1)S(1)}, bf16[256,1024]{1,0:T(8,128)(2,1)S(1)}, u32[]{:S(2)}, u32[]{:S(2)}) collective-permute-start(bf16[256,1024]{1,0:T(8,128)(2,1)S(1)} %get-tuple-element.118), channel_id=1, source_target_pairs={{0,3},{8,11},{4,7},{12,15},{16,19},{24,27},{20,23},{28,31},{32,35}... | collective-permute-start | bytes 1572872 | tf_op jit(solution)/shard_map/ppermute | solution.py:47
  107.9 16.1 %collective-permute-start.34 = (bf16[256,1024]{1,0:T(8,128)(2,1)S(1)}, bf16[256,1024]{1,0:T(8,128)(2,1)S(1)}, u32[]{:S(2)}, u32[]{:S(2)}) collective-permute-start(bf16[256,1024]{1,0:T(8,128)(2,1)S(1)} %slice.149), channel_id=1, source_target_pairs={{0,1},{8,9},{4,5},{12,13},{16,17},{24,25},{20,21},{28,29},{32,33},... | collective-permute-start | bytes 1572872 | tf_op jit(solution)/shard_map/ppermute | solution.py:47
  108.6 17.0 %collective-permute-start.35 = (bf16[256,1024]{1,0:T(8,128)(2,1)S(1)}, bf16[256,1024]{1,0:T(8,128)(2,1)S(1)}, u32[]{:S(2)}, u32[]{:S(2)}) collective-permute-start(bf16[256,1024]{1,0:T(8,128)(2,1)S(1)} %slice.150), channel_id=1, source_target_pairs={{0,3},{8,11},{4,7},{12,15},{16,19},{24,27},{20,23},{28,31},{32,35}... | collective-permute-start | bytes 1572872 | tf_op jit(solution)/shard_map/ppermute | solution.py:47
  112.4 21.9 %collective-permute-start.37 = (bf16[256,1024]{1,0:T(8,128)(2,1)S(1)}, bf16[256,1024]{1,0:T(8,128)(2,1)S(1)}, u32[]{:S(2)}, u32[]{:S(2)}) collective-permute-start(bf16[256,1024]{1,0:T(8,128)(2,1)S(1)} %add_convert_fusion.4), channel_id=1, source_target_pairs={{0,1},{8,9},{4,5},{12,13},{16,17},{24,25},{20,21},{28,29},{32,33},... | collective-permute-start | bytes 1572872 | tf_op jit(solution)/shard_map/ppermute | solution.py:47
  124.0 12.0 %collective-permute-start.38 = (bf16[256,1024]{1,0:T(8,128)(2,1)S(1)}, bf16[256,1024]{1,0:T(8,128)(2,1)S(1)}, u32[]{:S(2)}, u32[]{:S(2)}) collective-permute-start(bf16[256,1024]{1,0:T(8,128)(2,1)S(1)} %add_convert_fusion.3), channel_id=1, source_target_pairs={{0,3},{8,11},{4,7},{12,15},{16,19},{24,27},{20,23},{28,31},{32,35}... | collective-permute-start | bytes 1572872 | tf_op jit(solution)/shard_map/ppermute | solution.py:47
  125.5 6.1 %collective-permute-start.36 = (f32[56,512]{1,0:T(8,128)S(1)}, f32[56,512]{1,0:T(8,128)S(1)}, u32[]{:S(2)}, u32[]{:S(2)}) collective-permute-start(f32[56,512]{1,0:T(8,128)S(1)} %get-tuple-element.99), channel_id=1, source_target_pairs={{0,4},{8,12},{4,0},{12,8},{16,20},{24,28},{20,16},{28,24},{32,36},... | collective-permute-start | bytes 344072 | tf_op jit(solution)/shard_map/ppermute | solution.py:47
  128.5 11.2 %collective-permute-start.29 = (bf16[32,4096]{1,0:T(8,128)(2,1)S(1)}, bf16[32,4096]{1,0:T(8,128)(2,1)S(1)}, u32[]{:S(2)}, u32[]{:S(2)}) collective-permute-start(bf16[32,4096]{1,0:T(8,128)(2,1)S(1)} %get-tuple-element.121), channel_id=1, source_target_pairs={{0,20},{8,28},{4,0},{12,8},{16,4},{24,12},{20,16},{28,24},{32,52},... | collective-permute-start | bytes 786440 | tf_op jit(solution)/shard_map/ppermute | solution.py:47
  130.1 18.8 %collective-permute-start.28 = (bf16[32,4096]{1,0:T(8,128)(2,1)S(1)}, bf16[32,4096]{1,0:T(8,128)(2,1)S(1)}, u32[]{:S(2)}, u32[]{:S(2)}) collective-permute-start(bf16[32,4096]{1,0:T(8,128)(2,1)S(1)} %get-tuple-element.120), channel_id=1, source_target_pairs={{0,16},{8,24},{4,20},{12,28},{16,0},{24,8},{20,4},{28,12},{32,48},... | collective-permute-start | bytes 786440 | tf_op jit(solution)/shard_map/ppermute | solution.py:47
  131.7 11.7 %collective-permute-start.39 = (f32[72,512]{1,0:T(8,128)S(1)}, f32[72,512]{1,0:T(8,128)S(1)}, u32[]{:S(2)}, u32[]{:S(2)}) collective-permute-start(f32[72,512]{1,0:T(8,128)S(1)} %pad_maximum_fusion.4.refs_7_), channel_id=1, source_target_pairs={{0,1},{8,9},{4,5},{12,13},{16,17},{24,25},{20,21},{28,29},{32,33},... | collective-permute-start | bytes 442376 | tf_op jit(solution)/shard_map/ppermute | solution.py:47
  134.4 8.9 %collective-permute-start.40 = (f32[72,512]{1,0:T(8,128)S(1)}, f32[72,512]{1,0:T(8,128)S(1)}, u32[]{:S(2)}, u32[]{:S(2)}) collective-permute-start(f32[72,512]{1,0:T(8,128)S(1)} %pad_maximum_fusion.4.refs_7_), channel_id=1, source_target_pairs={{0,2},{8,10},{4,6},{12,14},{16,18},{24,26},{20,22},{28,30},{32,34}... | collective-permute-start | bytes 442376 | tf_op jit(solution)/shard_map/ppermute | solution.py:47
  136.0 7.4 %collective-permute-start.41 = (f32[72,512]{1,0:T(8,128)S(1)}, f32[72,512]{1,0:T(8,128)S(1)}, u32[]{:S(2)}, u32[]{:S(2)}) collective-permute-start(f32[72,512]{1,0:T(8,128)S(1)} %pad_maximum_fusion.4.refs_7_), channel_id=1, source_target_pairs={{0,3},{8,11},{4,7},{12,15},{16,19},{24,27},{20,23},{28,31},{32,35}... | collective-permute-start | bytes 442376 | tf_op jit(solution)/shard_map/ppermute | solution.py:47
  139.7 9.3 %collective-permute-start.30 = (bf16[32,4096]{1,0:T(8,128)(2,1)S(1)}, bf16[32,4096]{1,0:T(8,128)(2,1)S(1)}, u32[]{:S(2)}, u32[]{:S(2)}) collective-permute-start(bf16[32,4096]{1,0:T(8,128)(2,1)S(1)} %collective-permute-done.29), channel_id=1, source_target_pairs={{0,20},{8,28},{4,0},{12,8},{16,4},{24,12},{20,16},{28,24},{32,52},... | collective-permute-start | bytes 786440 | tf_op jit(solution)/shard_map/ppermute | solution.py:47
  (7 other events, 70.2 us)

commit v15 on v14

--- a/solution.py
+++ b/solution.py
@@ -143,7 +143,7 @@
             return now, lag
 
         zero = [zero_ref[...]] * modes
-        now, lag = lax.fori_loop(0, span, step, (zero, zero), unroll=8)
+        now, lag = lax.fori_loop(0, span, step, (zero, zero), unroll=16)
         for m in range(modes):
             sub_ref[tile, strided(m, modes)] = now[m]
             sub_ref[tile, strided(SUBS * modes + m, modes)] = lag[m]
@@ -193,7 +193,7 @@
             return now
 
         first = [lead_ref[tile, strided(m, modes)] for m in range(modes)]
-        lax.fori_loop(0, span, step, first, unroll=8)
+        lax.fori_loop(0, span, step, first, unroll=16)
         gated_ref[:, lanes] = (query_ref[:, lanes].astype(F32) * pre_ref[tile]).astype(BF16)
     part = length // (RING * 4)
     y, high, core, _, _ = places()
@@ -236,7 +236,7 @@
 
             zero = [zero_ref[...]] * half
             start, lag, pair, lag_pair, skip = lax.fori_loop(
-                0, span, back_step, (zero, zero, zero, zero, skip), unroll=8
+                0, span, back_step, (zero, zero, zero, zero, skip), unroll=16
             )
             for m in range(half):
                 state = lead_ref[tile, strided(low + m, modes)]
@@ -300,7 +300,7 @@
             return now
 
         first = [lead_ref[tile, strided(m, modes)] for m in range(modes)]
-        lax.fori_loop(0, span, step, first, unroll=8)
+        lax.fori_loop(0, span, step, first, unroll=16)
         drive_grad = drive_grad_ref[tile]
         grad_key_ref[:, lanes] = (drive_grad * value_ref[:, lanes].astype(F32)).astype(BF16)
         grad_value_ref[:, lanes] = (drive_grad * key_ref[:, lanes].astype(F32)).astype(BF16)
@@ -376,7 +376,7 @@
     cot_rows = place_blocks(
         (block[0], before_own, after_own, far_own), (block[1], before_other, after_other, far_other)
     )
-    cot_rows, got_rest = together(cot_rows.reshape(2 * length, -1), got_rest)
+    cot_rows = cot_rows.reshape(2 * length, -1)
 
     half = out_weight.shape[1] // 2
     low_weight = lax.dynamic_slice(out_weight, (0, places()[3] * half), (channels, half))

time: 150 us -> 150 us (level)
  local copies, waits for them, and re-layouts: 15.6 us -> 14 us
    unnamed x27 -> x25, local copies, waits for them, and re-layouts: 2.52 us -> 0.89 us
  transfers between devices with their start and end apart: 42 -> 42, of which waited for: 15 -> 15; matrix products, arithmetic and copies ran while one was open for 19% -> 21% of each run, Pallas kernels for 18% -> 18%
where the time goes in v15:
time: 150 us; the launch traced here: 149 us
  starting transfers between devices  49.1 us (33%)
  waiting for transfers between devices  37.9 us (25%)
  Pallas kernels  26.7 us (18%)
  local copies, waits for them, and re-layouts  14 us (9%)
  matrix products  10.9 us (7%)
  other arithmetic  8.97 us (6%)
    ppermute x42, starting transfers between devices, hop(): return lax.ppermute(value, ('chan', 'seq'), moves)  49.1 us
    ppermute x42, waiting for transfers between devices, hop(): return lax.ppermute(value, ('chan', 'seq'), moves)  37.9 us
    pallas_call x4, Pallas kernels, call(): pl.pallas_call(body, out_shape=[jax.ShapeDtypeStruct(o.shape, o.dtype) fo...  19.8 us
    dynamic_update_slice x16, local copies, waits for them, and re-layouts, place_blocks(): lax.dynamic_update_slice(whole, part[None, None, :, None], (side, row, 0,...  6.98 us
    pallas_call x1, Pallas kernels, project(): pl.pallas_call(project_tile, grid=(width // tile,), out_shape=[jax.ShapeD...  6.86 us
    dot_general x1, matrix products, local(): lax.dot_general(cot_rows, low_weight, (((1,), (1,)), ((), ())), preferred...  5.84 us
    dot_general x4, matrix products, weigh(): lax.dot_general(gated, columns, (((0,), (0,)), ((), ())), preferred_eleme...  5.11 us
    another operation x4, other arithmetic  3.65 us
  transfers between devices with their start and end apart: 42, of which 15 were waited for; matrix products, arithmetic and copies ran while one was open for 21% of the time, Pallas kernels for 18%

profile of v15, /device:TPU:0, one launch (start us, length us, event | category | flops | bytes accessed | tf_op | source)
XLA Modules:
  0.0 148.8 jit_solution(18363723776495455738)
XLA Ops:
  0.7 1.1 constant_dynamic-slice_fusion.1
  1.8 2.1 %collective-permute-start.1 = (bf16[32,4096]{1,0:T(8,128)(2,1)S(1)}, bf16[32,4096]{1,0:T(8,128)(2,1)S(1)}, u32[]{:S(2)}, u32[]{:S(2)}) collective-permute-start(bf16[32,4096]{1,0:T(8,128)(2,1)S(1)} %get-tuple-element.123), channel_id=1, source_target_pairs={{0,4},{8,12},{4,16},{12,24},{16,20},{24,28},{20,0},{28,8},{32,36},... | collective-permute-start | bytes 786440 | tf_op jit(solution)/shard_map/ppermute | solution.py:47
  3.9 2.2 %collective-permute-start.2 = (bf16[32,4096]{1,0:T(8,128)(2,1)S(1)}, bf16[32,4096]{1,0:T(8,128)(2,1)S(1)}, u32[]{:S(2)}, u32[]{:S(2)}) collective-permute-start(bf16[32,4096]{1,0:T(8,128)(2,1)S(1)} %get-tuple-element.123), channel_id=1, source_target_pairs={{0,20},{8,28},{4,0},{12,8},{16,4},{24,12},{20,16},{28,24},{32,52},... | collective-permute-start | bytes 786440 | tf_op jit(solution)/shard_map/ppermute | solution.py:47
  6.1 1.8 %collective-permute-start = (bf16[32,4096]{1,0:T(8,128)(2,1)S(1)}, bf16[32,4096]{1,0:T(8,128)(2,1)S(1)}, u32[]{:S(2)}, u32[]{:S(2)}) collective-permute-start(bf16[32,4096]{1,0:T(8,128)(2,1)S(1)} %get-tuple-element.122), channel_id=1, source_target_pairs={{0,16},{8,24},{4,20},{12,28},{16,0},{24,8},{20,4},{28,12},{32,48},... | collective-permute-start | bytes 786440 | tf_op jit(solution)/shard_map/ppermute | solution.py:47
  7.9 4.4 %collective-permute-done.1 = bf16[32,4096]{1,0:T(8,128)(2,1)S(1)} collective-permute-done((bf16[32,4096]{1,0:T(8,128)(2,1)S(1)}, bf16[32,4096]{1,0:T(8,128)(2,1)S(1)}, u32[]{:S(2)}, u32[]{:S(2)}) %collective-permute-start.1) | collective-permute-done | bytes 262176 | tf_op jit(solution)/shard_map/ppermute | solution.py:47
  12.3 5.0 %collective-permute-done.2 = bf16[32,4096]{1,0:T(8,128)(2,1)S(1)} collective-permute-done((bf16[32,4096]{1,0:T(8,128)(2,1)S(1)}, bf16[32,4096]{1,0:T(8,128)(2,1)S(1)}, u32[]{:S(2)}, u32[]{:S(2)}) %collective-permute-start.2) | collective-permute-done | bytes 262176 | tf_op jit(solution)/shard_map/ppermute | solution.py:47
  17.5 1.7 %collective-permute-done = bf16[32,4096]{1,0:T(8,128)(2,1)S(1)} collective-permute-done((bf16[32,4096]{1,0:T(8,128)(2,1)S(1)}, bf16[32,4096]{1,0:T(8,128)(2,1)S(1)}, u32[]{:S(2)}, u32[]{:S(2)}) %collective-permute-start) | collective-permute-done | bytes 262176 | tf_op jit(solution)/shard_map/ppermute | solution.py:47
  20.4 1.6 %collective-permute-start.5 = (bf16[2,32,4096]{2,1,0:T(8,128)(2,1)}, bf16[2,32,4096]{2,1,0:T(8,128)(2,1)S(1)}, u32[]{:S(2)}, u32[]{:S(2)}) collective-permute-start(bf16[2,32,4096]{2,1,0:T(8,128)(2,1)} %get-tuple-element.121), channel_id=1, source_target_pairs={{0,32},{8,40},{4,36},{12,44},{16,48},{24,56},{20,52},{28,60},{32,6... | collective-permute-start | bytes 1572872 | tf_op jit(solution)/shard_map/ppermute | solution.py:47
  22.2 1.7 %collective-permute-start.6 = (bf16[2,32,4096]{2,1,0:T(8,128)(2,1)}, bf16[2,32,4096]{2,1,0:T(8,128)(2,1)S(1)}, u32[]{:S(2)}, u32[]{:S(2)}) collective-permute-start(bf16[2,32,4096]{2,1,0:T(8,128)(2,1)} %get-tuple-element.120), channel_id=1, source_target_pairs={{0,96},{8,104},{4,100},{12,108},{16,112},{24,120},{20,116},{28,124... | collective-permute-start | bytes 1572872 | tf_op jit(solution)/shard_map/ppermute | solution.py:47
  23.9 3.0 %forward_ends.1 = (f32[32,512]{1,0:T(8,128)S(1)}, f32[4,256,128]{2,1,0:T(8,128)S(1)}, f32[4,512,128]{2,1,0:T(8,128)S(1)}) custom-call(bf16[512,512]{1,0:T(8,128)(2,1)S(1)} %copy-done, bf16[512,512]{1,0:T(8,128)(2,1)S(1)} %copy-done.1, f32[16,512]{1,0:T(8,128)S(1)} %copy-done.3), custom_call_target="tpu_custom_call" | custom-call | flops 115000000 | tf_op jit(solution)/shard_map/forward_ends/pallas_call | solution.py:311
  27.0 1.2 collective-permute-start.7
  29.3 2.0 %collective-permute-done.7 = f32[32,512]{1,0:T(8,128)S(1)} collective-permute-done((f32[32,512]{1,0:T(8,128)S(1)}, f32[32,512]{1,0:T(8,128)S(1)}, u32[]{:S(2)}, u32[]{:S(2)}) %collective-permute-start.7) | collective-permute-done | bytes 65568 | tf_op jit(solution)/shard_map/ppermute | solution.py:47
  31.6 4.9 %collective-permute-done.5 = bf16[2,32,4096]{2,1,0:T(8,128)(2,1)S(1)} collective-permute-done((bf16[2,32,4096]{2,1,0:T(8,128)(2,1)}, bf16[2,32,4096]{2,1,0:T(8,128)(2,1)S(1)}, u32[]{:S(2)}, u32[]{:S(2)}) %collective-permute-start.5) | collective-permute-done | bytes 524320 | tf_op jit(solution)/shard_map/ppermute | solution.py:47
  36.5 1.8 %collective-permute-start.4 = (bf16[2,32,4096]{2,1,0:T(8,128)(2,1)}, bf16[2,32,4096]{2,1,0:T(8,128)(2,1)S(1)}, u32[]{:S(2)}, u32[]{:S(2)}) collective-permute-start(bf16[2,32,4096]{2,1,0:T(8,128)(2,1)} %get-tuple-element.121), channel_id=1, source_target_pairs={{0,96},{8,104},{4,100},{12,108},{16,112},{24,120},{20,116},{28,124... | collective-permute-start | bytes 1572872 | tf_op jit(solution)/shard_map/ppermute | solution.py:47
  38.3 1.5 %collective-permute-start.8 = (f32[64,512]{1,0:T(8,128)S(1)}, f32[64,512]{1,0:T(8,128)S(1)}, u32[]{:S(2)}, u32[]{:S(2)}) collective-permute-start(f32[64,512]{1,0:T(8,128)S(1)} %pad_maximum_fusion.5.refs_6_), channel_id=1, source_target_pairs={{0,1},{8,9},{4,5},{12,13},{16,17},{24,25},{20,21},{28,29},{32,33},... | collective-permute-start | bytes 393224 | tf_op jit(solution)/shard_map/ppermute | solution.py:47
  39.8 2.7 %collective-permute-start.9 = (f32[64,512]{1,0:T(8,128)S(1)}, f32[64,512]{1,0:T(8,128)S(1)}, u32[]{:S(2)}, u32[]{:S(2)}) collective-permute-start(f32[64,512]{1,0:T(8,128)S(1)} %pad_maximum_fusion.5.refs_6_), channel_id=1, source_target_pairs={{0,2},{8,10},{4,6},{12,14},{16,18},{24,26},{20,22},{28,30},{32,34}... | collective-permute-start | bytes 393224 | tf_op jit(solution)/shard_map/ppermute | solution.py:47
  43.7 1.5 %collective-permute-start.10 = (f32[64,512]{1,0:T(8,128)S(1)}, f32[64,512]{1,0:T(8,128)S(1)}, u32[]{:S(2)}, u32[]{:S(2)}) collective-permute-start(f32[64,512]{1,0:T(8,128)S(1)} %pad_maximum_fusion.5.refs_6_), channel_id=1, source_target_pairs={{0,3},{8,11},{4,7},{12,15},{16,19},{24,27},{20,23},{28,31},{32,35}... | collective-permute-start | bytes 393224 | tf_op jit(solution)/shard_map/ppermute | solution.py:47
  46.3 1.5 %collective-permute-done.9.refs_8_ = f32[64,512]{1,0:T(8,128)S(1)} collective-permute-done((f32[64,512]{1,0:T(8,128)S(1)}, f32[64,512]{1,0:T(8,128)S(1)}, u32[]{:S(2)}, u32[]{:S(2)}) %collective-permute-start.9) | collective-permute-done | bytes 131104 | tf_op jit(solution)/shard_map/ppermute | solution.py:47
  48.8 3.8 %forward_full.1 = (bf16[512,512]{1,0:T(8,128)(2,1)S(1)}, bf16[512,512]{1,0:T(8,128)(2,1)S(1)}, f32[4,512,128]{2,1,0:T(8,128)S(1)}, f32[4,256,128]{2,1,0:T(8,128)S(1)}) custom-call(bf16[512,512]{1,0:T(8,128)(2,1)S(1)} %copy-done.2, f32[4,512,128]{2,1,0:T(8,128)S(1)} %get-tuple-element.63.refs_1_.drive_ref, f32[4,256,128]{2,1,0:T(8,128)S(1)} %get-tuple-element.64.refs_2_, ...), custom_call_target="tpu_custom_call" | custom-call | flops 115000000 | tf_op jit(solution)/shard_map/forward_full/pallas_call | solution.py:311
  53.2 3.0 %collective-permute-start.18 = (bf16[2,32,4096]{2,1,0:T(8,128)(2,1)S(1)}, bf16[2,32,4096]{2,1,0:T(8,128)(2,1)S(1)}, u32[]{:S(2)}, u32[]{:S(2)}) collective-permute-start(bf16[2,32,4096]{2,1,0:T(8,128)(2,1)S(1)} %collective-permute-done.6), channel_id=1, source_target_pairs={{0,96},{8,104},{4,100},{12,108},{16,112},{24,120},{20,116},{28,124... | collective-permute-start | bytes 1572872 | tf_op jit(solution)/shard_map/ppermute | solution.py:47
  56.2 1.1 collective-permute-start.22
  58.2 6.9 %project.1 = (bf16[64,8192]{1,0:T(8,128)(2,1)S(1)}, bf16[192,8192]{1,0:T(8,128)(2,1)S(1)}, bf16[64,8192]{1,0:T(8,128)(2,1)S(1)}, bf16[192,8192]{1,0:T(8,128)(2,1)S(1)}) custom-call(bf16[512,512]{1,0:T(8,128)(2,1)S(1)} %get-tuple-element.68.rows_ref, bf16[512,8192]{1,0:T(8,128)(2,1)S(1)} %bitcast.83), custom_call_target="tpu_custom_call" | custom-call | flops 4294967296 | bytes 16777216 | tf_op jit(solution)/shard_map/project/pallas_call | solution.py:92
  65.2 1.1 bitcast_dynamic-update-slice_fusion.9
  70.6 1.9 %constant_dynamic-update-slice_fusion = bf16[1024,512]{1,0:T(8,128)(2,1)} fusion(bf16[1024,512]{1,0:T(8,128)(2,1)} %constant_dynamic-update-slice_fusion.1, bf16[512,512]{1,0:T(8,128)(2,1)} %collective-permute-done.22), kind=kLoop, calls=%fused_computation.61 | loop fusion | bytes 1048576 | tf_op jit(solution)/shard_map/concatenate | solution.py:373
  72.4 1.2 bitcast_dynamic-update-slice_fusion.3
  74.7 1.9 %collective-permute-start.24 = (bf16[32,8192]{1,0:T(8,128)(2,1)S(1)}, bf16[32,8192]{1,0:T(8,128)(2,1)S(1)}, u32[]{:S(2)}, u32[]{:S(2)}) collective-permute-start(bf16[32,8192]{1,0:T(8,128)(2,1)S(1)} %get-tuple-element.118), channel_id=1, source_target_pairs={{0,32},{8,40},{4,36},{12,44},{16,48},{24,56},{20,52},{28,60},{32,6... | collective-permute-start | bytes 1572872 | tf_op jit(solution)/shard_map/ppermute | solution.py:47
  78.4 1.3 multiply_convert_fusion.3
  79.8 1.2 collective-permute-start.32
  81.0 2.2 %collective-permute-start.33 = (bf16[256,1024]{1,0:T(8,128)(2,1)S(1)}, bf16[256,1024]{1,0:T(8,128)(2,1)S(1)}, u32[]{:S(2)}, u32[]{:S(2)}) collective-permute-start(bf16[256,1024]{1,0:T(8,128)(2,1)S(1)} %get-tuple-element.114), channel_id=1, source_target_pairs={{0,3},{8,11},{4,7},{12,15},{16,19},{24,27},{20,23},{28,31},{32,35}... | collective-permute-start | bytes 1572872 | tf_op jit(solution)/shard_map/ppermute | solution.py:47
  83.1 5.8 %fusion = f32[1024,512]{1,0:T(8,128)} fusion(bf16[1024,4096]{1,0:T(8,128)(2,1)S(1)} %bitcast.85, bf16[512,8192]{1,0:T(8,128)(2,1)S(1)} %bitcast.83, s32[]{:T(128)S(6)} %select_n.116), kind=kOutput, calls=%fused_computation | convolution fusion | flops 4294967296 | bytes 14680068 | tf_op jit(solution)/shard_map/dot_general | solution.py:385
  89.0 2.1 %convert_add_fusion.2 = (f32[64,8192]{1,0:T(8,128)S(1)}, f32[64,8192]{1,0:T(8,128)S(1)}) fusion(bf16[192,8192]{1,0:T(8,128)(2,1)} %collective-permute-done.23, bf16[192,8192]{1,0:T(8,128)(2,1)S(1)} %get-tuple-element.69), kind=kLoop, calls=%fused_computation.13 | loop fusion | flops 3145728 | bytes 8388608 | tf_op jit(solution)/shard_map/add | solution.py:76
  91.1 1.2 fusion.19
  92.8 2.0 %collective-permute-start.25 = (bf16[64,8192]{1,0:T(8,128)(2,1)S(1)}, bf16[64,8192]{1,0:T(8,128)(2,1)S(1)}, u32[]{:S(2)}, u32[]{:S(2)}) collective-permute-start(bf16[64,8192]{1,0:T(8,128)(2,1)S(1)} %pad_maximum_fusion.1), channel_id=1, source_target_pairs={{0,32},{8,40},{4,36},{12,44},{16,48},{24,56},{20,52},{28,60},{32,6... | collective-permute-start | bytes 3145736 | tf_op jit(solution)/shard_map/ppermute | solution.py:47
  95.9 1.3 multiply_convert_fusion.2
  97.2 1.3 multiply_convert_fusion.1
  98.9 9.1 %collective-permute-done.31 = bf16[512,512]{1,0:T(8,128)(2,1)S(1)} collective-permute-done((bf16[512,512]{1,0:T(8,128)(2,1)S(1)}, bf16[512,512]{1,0:T(8,128)(2,1)S(1)}, u32[]{:S(2)}, u32[]{:S(2)}) %collective-permute-start.31) | collective-permute-done | bytes 524320 | tf_op jit(solution)/shard_map/ppermute | solution.py:47
  108.1 3.2 %collective-permute-start.35 = (bf16[256,1024]{1,0:T(8,128)(2,1)S(1)}, bf16[256,1024]{1,0:T(8,128)(2,1)S(1)}, u32[]{:S(2)}, u32[]{:S(2)}) collective-permute-start(bf16[256,1024]{1,0:T(8,128)(2,1)S(1)} %slice.150), channel_id=1, source_target_pairs={{0,3},{8,11},{4,7},{12,15},{16,19},{24,27},{20,23},{28,31},{32,35}... | collective-permute-start | bytes 1572872 | tf_op jit(solution)/shard_map/ppermute | solution.py:47
  111.3 1.3 multiply_convert_fusion
  112.8 7.9 %backward_ends.1 = (bf16[512,512]{1,0:T(8,128)(2,1)}, f32[4,512,128]{2,1,0:T(8,128)S(1)}, f32[56,512]{1,0:T(8,128)S(1)}, f32[4,128,128]{2,1,0:T(8,128)S(1)}) custom-call(f32[512,512]{1,0:T(8,128)S(1)} %convert_add_fusion.3.grad_ref, bf16[512,512]{1,0:T(8,128)(2,1)S(1)} %copy-done.2, f32[4,512,128]{2,1,0:T(8,128)S(1)} %get-tuple-element.87.pre_ref, ...), custom_call_target="tpu_custom_call" | custom-call | flops 2300000000 | tf_op jit(solution)/shard_map/backward_ends/pallas_call | solution.py:311
  120.7 3.5 %collective-permute-done.34 = bf16[256,1024]{1,0:T(8,128)(2,1)S(1)} collective-permute-done((bf16[256,1024]{1,0:T(8,128)(2,1)S(1)}, bf16[256,1024]{1,0:T(8,128)(2,1)S(1)}, u32[]{:S(2)}, u32[]{:S(2)}) %collective-permute-start.34) | collective-permute-done | bytes 524320 | tf_op jit(solution)/shard_map/ppermute | solution.py:47
  125.2 1.7 %fusion.26 = (bf16[64,8192]{1,0:T(8,128)(2,1)S(1)}, f32[64,8192]{1,0:T(8,128)S(1)}) fusion(bf16[64,8192]{1,0:T(8,128)(2,1)S(1)} %collective-permute-done.27, bf16[64,8192]{1,0:T(8,128)(2,1)S(1)} %collective-permute-done.25, bf16[192,8192]{1,0:T(8,128)(2,1)} %collective-permute-done.23, bf16[192,8192]{1,0:T(8,128)(2,1)S(1)} %get-tuple-element.69), kind=kLoop, calls=%fused_computation.70 | loop fusion | flops 4194304 | bytes 7340032 | tf_op jit(solution)/shard_map/convert.3
  127.0 2.1 %collective-permute-start.29 = (bf16[32,4096]{1,0:T(8,128)(2,1)S(1)}, bf16[32,4096]{1,0:T(8,128)(2,1)S(1)}, u32[]{:S(2)}, u32[]{:S(2)}) collective-permute-start(bf16[32,4096]{1,0:T(8,128)(2,1)S(1)} %get-tuple-element.117), channel_id=1, source_target_pairs={{0,20},{8,28},{4,0},{12,8},{16,4},{24,12},{20,16},{28,24},{32,52},... | collective-permute-start | bytes 786440 | tf_op jit(solution)/shard_map/ppermute | solution.py:47
  129.1 1.2 collective-permute-start.28
  130.5 1.9 %collective-permute-start.39 = (f32[72,512]{1,0:T(8,128)S(1)}, f32[72,512]{1,0:T(8,128)S(1)}, u32[]{:S(2)}, u32[]{:S(2)}) collective-permute-start(f32[72,512]{1,0:T(8,128)S(1)} %pad_maximum_fusion.4.refs_7_), channel_id=1, source_target_pairs={{0,1},{8,9},{4,5},{12,13},{16,17},{24,25},{20,21},{28,29},{32,33},... | collective-permute-start | bytes 442376 | tf_op jit(solution)/shard_map/ppermute | solution.py:47
  132.3 1.9 %collective-permute-done.37 = bf16[256,1024]{1,0:T(8,128)(2,1)S(1)} collective-permute-done((bf16[256,1024]{1,0:T(8,128)(2,1)S(1)}, bf16[256,1024]{1,0:T(8,128)(2,1)S(1)}, u32[]{:S(2)}, u32[]{:S(2)}) %collective-permute-start.37) | collective-permute-done | bytes 524320 | tf_op jit(solution)/shard_map/ppermute | solution.py:47
  135.1 3.8 %collective-permute-start.41 = (f32[72,512]{1,0:T(8,128)S(1)}, f32[72,512]{1,0:T(8,128)S(1)}, u32[]{:S(2)}, u32[]{:S(2)}) collective-permute-start(f32[72,512]{1,0:T(8,128)S(1)} %pad_maximum_fusion.4.refs_7_), channel_id=1, source_target_pairs={{0,3},{8,11},{4,7},{12,15},{16,19},{24,27},{20,23},{28,31},{32,35}... | collective-permute-start | bytes 442376 | tf_op jit(solution)/shard_map/ppermute | solution.py:47
  139.0 1.6 %collective-permute-start.30 = (bf16[32,4096]{1,0:T(8,128)(2,1)S(1)}, bf16[32,4096]{1,0:T(8,128)(2,1)S(1)}, u32[]{:S(2)}, u32[]{:S(2)}) collective-permute-start(bf16[32,4096]{1,0:T(8,128)(2,1)S(1)} %collective-permute-done.29), channel_id=1, source_target_pairs={{0,20},{8,28},{4,0},{12,8},{16,4},{24,12},{20,16},{28,24},{32,52},... | collective-permute-start | bytes 786440 | tf_op jit(solution)/shard_map/ppermute | solution.py:47
  142.2 5.1 %backward_full.1 = (bf16[512,512]{1,0:T(8,128)(2,1)}, bf16[512,512]{1,0:T(8,128)(2,1)}, f32[16,512]{1,0:T(8,128)}, f32[16,512]{1,0:T(8,128)}, f32[8,512]{1,0:T(8,128)S(1)}) custom-call(bf16[512,512]{1,0:T(8,128)(2,1)S(1)} %copy-done, bf16[512,512]{1,0:T(8,128)(2,1)S(1)} %copy-done.1, f32[4,512,128]{2,1,0:T(8,128)S(1)} %get-tuple-element.90.refs_2_, ...), custom_call_target="tpu_custom_call" | custom-call | flops 115000000 | tf_op jit(solution)/shard_map/backward_full/pallas_call | solution.py:311
  (123 shorter events, 22.4 us)
Async XLA Ops:
  0.6 23.3 %copy-start.3 = (f32[16,512]{1,0:T(8,128)S(1)}, f32[16,512]{1,0:T(8,128)}, u32[]{:S(2)}) copy-start(f32[16,512]{1,0:T(8,128)} %refs_4_.3) | copy-start | bytes 98308
  1.8 10.5 %collective-permute-start.1 = (bf16[32,4096]{1,0:T(8,128)(2,1)S(1)}, bf16[32,4096]{1,0:T(8,128)(2,1)S(1)}, u32[]{:S(2)}, u32[]{:S(2)}) collective-permute-start(bf16[32,4096]{1,0:T(8,128)(2,1)S(1)} %get-tuple-element.123), channel_id=1, source_target_pairs={{0,4},{8,12},{4,16},{12,24},{16,20},{24,28},{20,0},{28,8},{32,36},... | collective-permute-start | bytes 786440 | tf_op jit(solution)/shard_map/ppermute | solution.py:47
  3.9 13.4 %collective-permute-start.2 = (bf16[32,4096]{1,0:T(8,128)(2,1)S(1)}, bf16[32,4096]{1,0:T(8,128)(2,1)S(1)}, u32[]{:S(2)}, u32[]{:S(2)}) collective-permute-start(bf16[32,4096]{1,0:T(8,128)(2,1)S(1)} %get-tuple-element.123), channel_id=1, source_target_pairs={{0,20},{8,28},{4,0},{12,8},{16,4},{24,12},{20,16},{28,24},{32,52},... | collective-permute-start | bytes 786440 | tf_op jit(solution)/shard_map/ppermute | solution.py:47
  6.1 13.0 %collective-permute-start = (bf16[32,4096]{1,0:T(8,128)(2,1)S(1)}, bf16[32,4096]{1,0:T(8,128)(2,1)S(1)}, u32[]{:S(2)}, u32[]{:S(2)}) collective-permute-start(bf16[32,4096]{1,0:T(8,128)(2,1)S(1)} %get-tuple-element.122), channel_id=1, source_target_pairs={{0,16},{8,24},{4,20},{12,28},{16,0},{24,8},{20,4},{28,12},{32,48},... | collective-permute-start | bytes 786440 | tf_op jit(solution)/shard_map/ppermute | solution.py:47
  19.3 29.4 %copy-start.2 = (bf16[512,512]{1,0:T(8,128)(2,1)S(1)}, bf16[512,512]{1,0:T(8,128)(2,1)}, u32[]{:S(2)}) copy-start(bf16[512,512]{1,0:T(8,128)(2,1)} %query_ref.1) | copy-start | bytes 1572868
  19.3 29.4 %copy-start.4 = (f32[16,512]{1,0:T(8,128)S(1)}, f32[16,512]{1,0:T(8,128)}, u32[]{:S(2)}) copy-start(f32[16,512]{1,0:T(8,128)} %refs_5_.1) | copy-start | bytes 98308
  19.3 29.4 %copy-start.5 = (f32[512]{0:T(512)S(1)}, f32[512]{0:T(512)}, u32[]{:S(2)}) copy-start(f32[512]{0:T(512)} %param.11) | copy-start | bytes 6148
  20.4 19.4 %collective-permute-start.11 = (bf16[2,32,4096]{2,1,0:T(8,128)(2,1)}, bf16[2,32,4096]{2,1,0:T(8,128)(2,1)}, u32[]{:S(2)}, u32[]{:S(2)}) collective-permute-start(bf16[2,32,4096]{2,1,0:T(8,128)(2,1)} %get-tuple-element.121), channel_id=1, source_target_pairs={{0,8},{8,0},{4,12},{12,4},{16,24},{24,16},{20,28},{28,20},{32,40},... | collective-permute-start | bytes 1572872 | tf_op jit(solution)/shard_map/ppermute | solution.py:47
  20.4 16.1 %collective-permute-start.5 = (bf16[2,32,4096]{2,1,0:T(8,128)(2,1)}, bf16[2,32,4096]{2,1,0:T(8,128)(2,1)S(1)}, u32[]{:S(2)}, u32[]{:S(2)}) collective-permute-start(bf16[2,32,4096]{2,1,0:T(8,128)(2,1)} %get-tuple-element.121), channel_id=1, source_target_pairs={{0,32},{8,40},{4,36},{12,44},{16,48},{24,56},{20,52},{28,60},{32,6... | collective-permute-start | bytes 1572872 | tf_op jit(solution)/shard_map/ppermute | solution.py:47
  22.0 21.7 %collective-permute-start.12 = (bf16[2,32,4096]{2,1,0:T(8,128)(2,1)}, bf16[2,32,4096]{2,1,0:T(8,128)(2,1)}, u32[]{:S(2)}, u32[]{:S(2)}) collective-permute-start(bf16[2,32,4096]{2,1,0:T(8,128)(2,1)} %get-tuple-element.120), channel_id=1, source_target_pairs={{0,8},{8,0},{4,12},{12,4},{16,24},{24,16},{20,28},{28,20},{32,40},... | collective-permute-start | bytes 1572872 | tf_op jit(solution)/shard_map/ppermute | solution.py:47
  22.2 16.1 %collective-permute-start.6 = (bf16[2,32,4096]{2,1,0:T(8,128)(2,1)}, bf16[2,32,4096]{2,1,0:T(8,128)(2,1)S(1)}, u32[]{:S(2)}, u32[]{:S(2)}) collective-permute-start(bf16[2,32,4096]{2,1,0:T(8,128)(2,1)} %get-tuple-element.120), channel_id=1, source_target_pairs={{0,96},{8,104},{4,100},{12,108},{16,112},{24,120},{20,116},{28,124... | collective-permute-start | bytes 1572872 | tf_op jit(solution)/shard_map/ppermute | solution.py:47
  27.0 31.2 %slice-start = ((s8[8388608]{0:T(1024)(128)(4,1)}), s8[4194304]{0:T(1024)(128)(4,1)S(1)}, s32[]{:S(2)}) async-start(s8[8388608]{0:T(1024)(128)(4,1)} %bitcast.82), calls=%async_computation | async-start | bytes 8388608
  27.0 4.3 %collective-permute-start.7 = (f32[32,512]{1,0:T(8,128)S(1)}, f32[32,512]{1,0:T(8,128)S(1)}, u32[]{:S(2)}, u32[]{:S(2)}) collective-permute-start(f32[32,512]{1,0:T(8,128)S(1)} %get-tuple-element.60), channel_id=1, source_target_pairs={{0,4},{8,12},{4,0},{12,8},{16,20},{24,28},{20,16},{28,24},{32,36},... | collective-permute-start | bytes 196616 | tf_op jit(solution)/shard_map/ppermute | solution.py:47
  29.2 29.0 %slice-start.1 = ((s8[8388608]{0:T(1024)(128)(4,1)}), s8[4194304]{0:T(1024)(128)(4,1)S(1)}, s32[]{:S(2)}) async-start(s8[8388608]{0:T(1024)(128)(4,1)} %bitcast.82), calls=%async_computation.1 | async-start | bytes 8388608
  31.3 21.9 %collective-permute-start.3 = (bf16[2,32,4096]{2,1,0:T(8,128)(2,1)}, bf16[2,32,4096]{2,1,0:T(8,128)(2,1)}, u32[]{:S(2)}, u32[]{:S(2)}) collective-permute-start(bf16[2,32,4096]{2,1,0:T(8,128)(2,1)} %get-tuple-element.120), channel_id=1, source_target_pairs={{0,32},{8,40},{4,36},{12,44},{16,48},{24,56},{20,52},{28,60},{32,6... | collective-permute-start | bytes 1572872 | tf_op jit(solution)/shard_map/ppermute | solution.py:47
  36.5 19.6 %collective-permute-start.4 = (bf16[2,32,4096]{2,1,0:T(8,128)(2,1)}, bf16[2,32,4096]{2,1,0:T(8,128)(2,1)S(1)}, u32[]{:S(2)}, u32[]{:S(2)}) collective-permute-start(bf16[2,32,4096]{2,1,0:T(8,128)(2,1)} %get-tuple-element.121), channel_id=1, source_target_pairs={{0,96},{8,104},{4,100},{12,108},{16,112},{24,120},{20,116},{28,124... | collective-permute-start | bytes 1572872 | tf_op jit(solution)/shard_map/ppermute | solution.py:47
  38.3 8.0 %collective-permute-start.8 = (f32[64,512]{1,0:T(8,128)S(1)}, f32[64,512]{1,0:T(8,128)S(1)}, u32[]{:S(2)}, u32[]{:S(2)}) collective-permute-start(f32[64,512]{1,0:T(8,128)S(1)} %pad_maximum_fusion.5.refs_6_), channel_id=1, source_target_pairs={{0,1},{8,9},{4,5},{12,13},{16,17},{24,25},{20,21},{28,29},{32,33},... | collective-permute-start | bytes 393224 | tf_op jit(solution)/shard_map/ppermute | solution.py:47
  39.8 8.0 %collective-permute-start.9 = (f32[64,512]{1,0:T(8,128)S(1)}, f32[64,512]{1,0:T(8,128)S(1)}, u32[]{:S(2)}, u32[]{:S(2)}) collective-permute-start(f32[64,512]{1,0:T(8,128)S(1)} %pad_maximum_fusion.5.refs_6_), channel_id=1, source_target_pairs={{0,2},{8,10},{4,6},{12,14},{16,18},{24,26},{20,22},{28,30},{32,34}... | collective-permute-start | bytes 393224 | tf_op jit(solution)/shard_map/ppermute | solution.py:47
  43.7 5.0 %collective-permute-start.10 = (f32[64,512]{1,0:T(8,128)S(1)}, f32[64,512]{1,0:T(8,128)S(1)}, u32[]{:S(2)}, u32[]{:S(2)}) collective-permute-start(f32[64,512]{1,0:T(8,128)S(1)} %pad_maximum_fusion.5.refs_6_), channel_id=1, source_target_pairs={{0,3},{8,11},{4,7},{12,15},{16,19},{24,27},{20,23},{28,31},{32,35}... | collective-permute-start | bytes 393224 | tf_op jit(solution)/shard_map/ppermute | solution.py:47
  52.6 12.5 %collective-permute-start.13 = (bf16[2,32,4096]{2,1,0:T(8,128)(2,1)S(1)}, bf16[2,32,4096]{2,1,0:T(8,128)(2,1)}, u32[]{:S(2)}, u32[]{:S(2)}) collective-permute-start(bf16[2,32,4096]{2,1,0:T(8,128)(2,1)S(1)} %collective-permute-done.5), channel_id=1, source_target_pairs={{0,8},{8,0},{4,12},{12,4},{16,24},{24,16},{20,28},{28,20},{32,40},... | collective-permute-start | bytes 1572872 | tf_op jit(solution)/shard_map/ppermute | solution.py:47
  52.7 21.2 %collective-permute-start.17 = (bf16[2,32,4096]{2,1,0:T(8,128)(2,1)S(1)}, bf16[2,32,4096]{2,1,0:T(8,128)(2,1)S(1)}, u32[]{:S(2)}, u32[]{:S(2)}) collective-permute-start(bf16[2,32,4096]{2,1,0:T(8,128)(2,1)S(1)} %collective-permute-done.5), channel_id=1, source_target_pairs={{0,32},{8,40},{4,36},{12,44},{16,48},{24,56},{20,52},{28,60},{32,6... | collective-permute-start | bytes 1572872 | tf_op jit(solution)/shard_map/ppermute | solution.py:47
  53.0 19.5 %collective-permute-start.16 = (bf16[2,32,4096]{2,1,0:T(8,128)(2,1)S(1)}, bf16[2,32,4096]{2,1,0:T(8,128)(2,1)}, u32[]{:S(2)}, u32[]{:S(2)}) collective-permute-start(bf16[2,32,4096]{2,1,0:T(8,128)(2,1)S(1)} %collective-permute-done.6), channel_id=1, source_target_pairs={{0,8},{8,0},{4,12},{12,4},{16,24},{24,16},{20,28},{28,20},{32,40},... | collective-permute-start | bytes 1572872 | tf_op jit(solution)/shard_map/ppermute | solution.py:47
  53.2 20.7 %collective-permute-start.18 = (bf16[2,32,4096]{2,1,0:T(8,128)(2,1)S(1)}, bf16[2,32,4096]{2,1,0:T(8,128)(2,1)S(1)}, u32[]{:S(2)}, u32[]{:S(2)}) collective-permute-start(bf16[2,32,4096]{2,1,0:T(8,128)(2,1)S(1)} %collective-permute-done.6), channel_id=1, source_target_pairs={{0,96},{8,104},{4,100},{12,108},{16,112},{24,120},{20,116},{28,124... | collective-permute-start | bytes 1572872 | tf_op jit(solution)/shard_map/ppermute | solution.py:47
  56.2 14.0 %collective-permute-start.22 = (bf16[512,512]{1,0:T(8,128)(2,1)S(1)}, bf16[512,512]{1,0:T(8,128)(2,1)}, u32[]{:S(2)}, u32[]{:S(2)}) collective-permute-start(bf16[512,512]{1,0:T(8,128)(2,1)S(1)} %get-tuple-element.78), channel_id=1, source_target_pairs={{0,4},{8,12},{4,0},{12,8},{16,20},{24,28},{20,16},{28,24},{32,36},... | collective-permute-start | bytes 1572872 | tf_op jit(solution)/shard_map/ppermute | solution.py:47
  65.1 2.3 %collective-permute-start.14 = (bf16[2,32,4096]{2,1,0:T(8,128)(2,1)}, bf16[2,32,4096]{2,1,0:T(8,128)(2,1)S(1)}, u32[]{:S(2)}, u32[]{:S(2)}) collective-permute-start(bf16[2,32,4096]{2,1,0:T(8,128)(2,1)} %collective-permute-done.3), channel_id=1, source_target_pairs={{0,8},{8,0},{4,12},{12,4},{16,24},{24,16},{20,28},{28,20},{32,40},... | collective-permute-start | bytes 1572872 | tf_op jit(solution)/shard_map/ppermute | solution.py:47
  67.4 2.3 %collective-permute-start.15 = (bf16[2,32,4096]{2,1,0:T(8,128)(2,1)}, bf16[2,32,4096]{2,1,0:T(8,128)(2,1)S(1)}, u32[]{:S(2)}, u32[]{:S(2)}) collective-permute-start(bf16[2,32,4096]{2,1,0:T(8,128)(2,1)} %copy-done.7), channel_id=1, source_target_pairs={{0,8},{8,0},{4,12},{12,4},{16,24},{24,16},{20,28},{28,20},{32,40},... | collective-permute-start | bytes 1572872 | tf_op jit(solution)/shard_map/ppermute | solution.py:47
  69.7 3.9 %collective-permute-start.19 = (bf16[64,8192]{1,0:T(8,128)(2,1)S(1)}, bf16[64,8192]{1,0:T(8,128)(2,1)S(1)}, u32[]{:S(2)}, u32[]{:S(2)}) collective-permute-start(bf16[64,8192]{1,0:T(8,128)(2,1)S(1)} %get-tuple-element.75), channel_id=1, source_target_pairs={{0,8},{8,0},{4,12},{12,4},{16,24},{24,16},{20,28},{28,20},{32,40},... | collective-permute-start | bytes 3145736 | tf_op jit(solution)/shard_map/ppermute | solution.py:47
  70.2 18.8 %collective-permute-start.23 = (bf16[192,8192]{1,0:T(8,128)(2,1)S(1)}, bf16[192,8192]{1,0:T(8,128)(2,1)}, u32[]{:S(2)}, u32[]{:S(2)}) collective-permute-start(bf16[192,8192]{1,0:T(8,128)(2,1)S(1)} %get-tuple-element.80), channel_id=1, source_target_pairs={{0,8},{8,0},{4,12},{12,4},{16,24},{24,16},{20,28},{28,20},{32,40},... | collective-permute-start | bytes 9437192 | tf_op jit(solution)/shard_map/ppermute | solution.py:47
  73.9 3.7 %collective-permute-start.20 = (bf16[2,32,4096]{2,1,0:T(8,128)(2,1)S(1)}, bf16[2,32,4096]{2,1,0:T(8,128)(2,1)S(1)}, u32[]{:S(2)}, u32[]{:S(2)}) collective-permute-start(bf16[2,32,4096]{2,1,0:T(8,128)(2,1)S(1)} %collective-permute-done.17), channel_id=1, source_target_pairs={{0,8},{8,0},{4,12},{12,4},{16,24},{24,16},{20,28},{28,20},{32,40},... | collective-permute-start | bytes 1572872 | tf_op jit(solution)/shard_map/ppermute | solution.py:47
  74.4 4.0 %collective-permute-start.21 = (bf16[2,32,4096]{2,1,0:T(8,128)(2,1)S(1)}, bf16[2,32,4096]{2,1,0:T(8,128)(2,1)S(1)}, u32[]{:S(2)}, u32[]{:S(2)}) collective-permute-start(bf16[2,32,4096]{2,1,0:T(8,128)(2,1)S(1)} %collective-permute-done.18), channel_id=1, source_target_pairs={{0,8},{8,0},{4,12},{12,4},{16,24},{24,16},{20,28},{28,20},{32,40},... | collective-permute-start | bytes 1572872 | tf_op jit(solution)/shard_map/ppermute | solution.py:47
  74.6 16.6 %collective-permute-start.26 = (bf16[32,8192]{1,0:T(8,128)(2,1)S(1)}, bf16[32,8192]{1,0:T(8,128)(2,1)}, u32[]{:S(2)}, u32[]{:S(2)}) collective-permute-start(bf16[32,8192]{1,0:T(8,128)(2,1)S(1)} %get-tuple-element.119), channel_id=1, source_target_pairs={{0,96},{8,104},{4,100},{12,108},{16,112},{24,120},{20,116},{28,124... | collective-permute-start | bytes 1572872 | tf_op jit(solution)/shard_map/ppermute | solution.py:47
  74.7 17.9 %collective-permute-start.24 = (bf16[32,8192]{1,0:T(8,128)(2,1)S(1)}, bf16[32,8192]{1,0:T(8,128)(2,1)S(1)}, u32[]{:S(2)}, u32[]{:S(2)}) collective-permute-start(bf16[32,8192]{1,0:T(8,128)(2,1)S(1)} %get-tuple-element.118), channel_id=1, source_target_pairs={{0,32},{8,40},{4,36},{12,44},{16,48},{24,56},{20,52},{28,60},{32,6... | collective-permute-start | bytes 1572872 | tf_op jit(solution)/shard_map/ppermute | solution.py:47
  79.8 18.7 %collective-permute-start.32 = (bf16[256,1024]{1,0:T(8,128)(2,1)S(1)}, bf16[256,1024]{1,0:T(8,128)(2,1)S(1)}, u32[]{:S(2)}, u32[]{:S(2)}) collective-permute-start(bf16[256,1024]{1,0:T(8,128)(2,1)S(1)} %get-tuple-element.115), channel_id=1, source_target_pairs={{0,1},{8,9},{4,5},{12,13},{16,17},{24,25},{20,21},{28,29},{32,33},... | collective-permute-start | bytes 1572872 | tf_op jit(solution)/shard_map/ppermute | solution.py:47
  81.0 17.7 %collective-permute-start.33 = (bf16[256,1024]{1,0:T(8,128)(2,1)S(1)}, bf16[256,1024]{1,0:T(8,128)(2,1)S(1)}, u32[]{:S(2)}, u32[]{:S(2)}) collective-permute-start(bf16[256,1024]{1,0:T(8,128)(2,1)S(1)} %get-tuple-element.114), channel_id=1, source_target_pairs={{0,3},{8,11},{4,7},{12,15},{16,19},{24,27},{20,23},{28,31},{32,35}... | collective-permute-start | bytes 1572872 | tf_op jit(solution)/shard_map/ppermute | solution.py:47
  92.4 32.8 %collective-permute-start.27 = (bf16[64,8192]{1,0:T(8,128)(2,1)S(1)}, bf16[64,8192]{1,0:T(8,128)(2,1)S(1)}, u32[]{:S(2)}, u32[]{:S(2)}) collective-permute-start(bf16[64,8192]{1,0:T(8,128)(2,1)S(1)} %pad_maximum_fusion.2), channel_id=1, source_target_pairs={{0,96},{8,104},{4,100},{12,108},{16,112},{24,120},{20,116},{28,124... | collective-permute-start | bytes 3145736 | tf_op jit(solution)/shard_map/ppermute | solution.py:47
  92.8 32.4 %collective-permute-start.25 = (bf16[64,8192]{1,0:T(8,128)(2,1)S(1)}, bf16[64,8192]{1,0:T(8,128)(2,1)S(1)}, u32[]{:S(2)}, u32[]{:S(2)}) collective-permute-start(bf16[64,8192]{1,0:T(8,128)(2,1)S(1)} %pad_maximum_fusion.1), channel_id=1, source_target_pairs={{0,32},{8,40},{4,36},{12,44},{16,48},{24,56},{20,52},{28,60},{32,6... | collective-permute-start | bytes 3145736 | tf_op jit(solution)/shard_map/ppermute | solution.py:47
  94.9 13.1 %collective-permute-start.31 = (bf16[512,512]{1,0:T(8,128)(2,1)S(1)}, bf16[512,512]{1,0:T(8,128)(2,1)S(1)}, u32[]{:S(2)}, u32[]{:S(2)}) collective-permute-start(bf16[512,512]{1,0:T(8,128)(2,1)S(1)} %slice.184), channel_id=1, source_target_pairs={{0,4},{8,12},{4,0},{12,8},{16,20},{24,28},{20,16},{28,24},{32,36},... | collective-permute-start | bytes 1572872 | tf_op jit(solution)/shard_map/ppermute | solution.py:47
  108.1 16.1 %collective-permute-start.34 = (bf16[256,1024]{1,0:T(8,128)(2,1)S(1)}, bf16[256,1024]{1,0:T(8,128)(2,1)S(1)}, u32[]{:S(2)}, u32[]{:S(2)}) collective-permute-start(bf16[256,1024]{1,0:T(8,128)(2,1)S(1)} %slice.149), channel_id=1, source_target_pairs={{0,1},{8,9},{4,5},{12,13},{16,17},{24,25},{20,21},{28,29},{32,33},... | collective-permute-start | bytes 1572872 | tf_op jit(solution)/shard_map/ppermute | solution.py:47
  108.1 16.3 %collective-permute-start.35 = (bf16[256,1024]{1,0:T(8,128)(2,1)S(1)}, bf16[256,1024]{1,0:T(8,128)(2,1)S(1)}, u32[]{:S(2)}, u32[]{:S(2)}) collective-permute-start(bf16[256,1024]{1,0:T(8,128)(2,1)S(1)} %slice.150), channel_id=1, source_target_pairs={{0,3},{8,11},{4,7},{12,15},{16,19},{24,27},{20,23},{28,31},{32,35}... | collective-permute-start | bytes 1572872 | tf_op jit(solution)/shard_map/ppermute | solution.py:47
  112.6 21.7 %collective-permute-start.37 = (bf16[256,1024]{1,0:T(8,128)(2,1)S(1)}, bf16[256,1024]{1,0:T(8,128)(2,1)S(1)}, u32[]{:S(2)}, u32[]{:S(2)}) collective-permute-start(bf16[256,1024]{1,0:T(8,128)(2,1)S(1)} %add_convert_fusion.4), channel_id=1, source_target_pairs={{0,1},{8,9},{4,5},{12,13},{16,17},{24,25},{20,21},{28,29},{32,33},... | collective-permute-start | bytes 1572872 | tf_op jit(solution)/shard_map/ppermute | solution.py:47
  124.1 11.0 %collective-permute-start.38 = (bf16[256,1024]{1,0:T(8,128)(2,1)S(1)}, bf16[256,1024]{1,0:T(8,128)(2,1)S(1)}, u32[]{:S(2)}, u32[]{:S(2)}) collective-permute-start(bf16[256,1024]{1,0:T(8,128)(2,1)S(1)} %add_convert_fusion.3), channel_id=1, source_target_pairs={{0,3},{8,11},{4,7},{12,15},{16,19},{24,27},{20,23},{28,31},{32,35}... | collective-permute-start | bytes 1572872 | tf_op jit(solution)/shard_map/ppermute | solution.py:47
  124.4 6.1 %collective-permute-start.36 = (f32[56,512]{1,0:T(8,128)S(1)}, f32[56,512]{1,0:T(8,128)S(1)}, u32[]{:S(2)}, u32[]{:S(2)}) collective-permute-start(f32[56,512]{1,0:T(8,128)S(1)} %get-tuple-element.95), channel_id=1, source_target_pairs={{0,4},{8,12},{4,0},{12,8},{16,20},{24,28},{20,16},{28,24},{32,36},... | collective-permute-start | bytes 344072 | tf_op jit(solution)/shard_map/ppermute | solution.py:47
  127.0 11.9 %collective-permute-start.29 = (bf16[32,4096]{1,0:T(8,128)(2,1)S(1)}, bf16[32,4096]{1,0:T(8,128)(2,1)S(1)}, u32[]{:S(2)}, u32[]{:S(2)}) collective-permute-start(bf16[32,4096]{1,0:T(8,128)(2,1)S(1)} %get-tuple-element.117), channel_id=1, source_target_pairs={{0,20},{8,28},{4,0},{12,8},{16,4},{24,12},{20,16},{28,24},{32,52},... | collective-permute-start | bytes 786440 | tf_op jit(solution)/shard_map/ppermute | solution.py:47
  129.1 18.8 %collective-permute-start.28 = (bf16[32,4096]{1,0:T(8,128)(2,1)S(1)}, bf16[32,4096]{1,0:T(8,128)(2,1)S(1)}, u32[]{:S(2)}, u32[]{:S(2)}) collective-permute-start(bf16[32,4096]{1,0:T(8,128)(2,1)S(1)} %get-tuple-element.116), channel_id=1, source_target_pairs={{0,16},{8,24},{4,20},{12,28},{16,0},{24,8},{20,4},{28,12},{32,48},... | collective-permute-start | bytes 786440 | tf_op jit(solution)/shard_map/ppermute | solution.py:47
  130.5 11.7 %collective-permute-start.39 = (f32[72,512]{1,0:T(8,128)S(1)}, f32[72,512]{1,0:T(8,128)S(1)}, u32[]{:S(2)}, u32[]{:S(2)}) collective-permute-start(f32[72,512]{1,0:T(8,128)S(1)} %pad_maximum_fusion.4.refs_7_), channel_id=1, source_target_pairs={{0,1},{8,9},{4,5},{12,13},{16,17},{24,25},{20,21},{28,29},{32,33},... | collective-permute-start | bytes 442376 | tf_op jit(solution)/shard_map/ppermute | solution.py:47
  134.2 8.0 %collective-permute-start.40 = (f32[72,512]{1,0:T(8,128)S(1)}, f32[72,512]{1,0:T(8,128)S(1)}, u32[]{:S(2)}, u32[]{:S(2)}) collective-permute-start(f32[72,512]{1,0:T(8,128)S(1)} %pad_maximum_fusion.4.refs_7_), channel_id=1, source_target_pairs={{0,2},{8,10},{4,6},{12,14},{16,18},{24,26},{20,22},{28,30},{32,34}... | collective-permute-start | bytes 442376 | tf_op jit(solution)/shard_map/ppermute | solution.py:47
  135.1 7.1 %collective-permute-start.41 = (f32[72,512]{1,0:T(8,128)S(1)}, f32[72,512]{1,0:T(8,128)S(1)}, u32[]{:S(2)}, u32[]{:S(2)}) collective-permute-start(f32[72,512]{1,0:T(8,128)S(1)} %pad_maximum_fusion.4.refs_7_), channel_id=1, source_target_pairs={{0,3},{8,11},{4,7},{12,15},{16,19},{24,27},{20,23},{28,31},{32,35}... | collective-permute-start | bytes 442376 | tf_op jit(solution)/shard_map/ppermute | solution.py:47
  139.0 8.9 %collective-permute-start.30 = (bf16[32,4096]{1,0:T(8,128)(2,1)S(1)}, bf16[32,4096]{1,0:T(8,128)(2,1)S(1)}, u32[]{:S(2)}, u32[]{:S(2)}) collective-permute-start(bf16[32,4096]{1,0:T(8,128)(2,1)S(1)} %collective-permute-done.29), channel_id=1, source_target_pairs={{0,20},{8,28},{4,0},{12,8},{16,4},{24,12},{20,16},{28,24},{32,52},... | collective-permute-start | bytes 786440 | tf_op jit(solution)/shard_map/ppermute | solution.py:47
  (6 other events, 66.5 us)
